TPU v7x, 32 devices: a whole 2x2x4 slice. The times are simulated.
32 devices in a mesh: rep: 4 (over y, core), shard: 8 (over z, x).
Axes of the slice: x: 2, y: 2, z: 4, core: 2. Of those that a mesh axis runs over, the one named last changes fastest.
Arguments:
- inputs: bfloat16 [32768, 768], P(('rep', 'shard')), may hold values from -6 to 6
- cotangent: bfloat16 [32768, 768], P(('rep', 'shard')), may hold values from -6 to 6
- segment: int32 [32768], P(('rep', 'shard')), may hold values from 0 to 12, as said below
- parent: int32 [32, 13], P(('rep', 'shard')), may hold values from 0 to 4, as said below
- clusters: int32 [12, 32768], P(None, ('rep', 'shard')), may hold values from 0 to 7, as said below
- qkv_weight: bfloat16 [2, 768, 2304], P(None, 'shard'), may hold values from -0.21875 to 0.21875
- qv_bias: bfloat16 [2, 1536], P(None, 'shard'), may hold values from -2 to 2
- out_weight: bfloat16 [2, 768, 768], P(None, 'shard'), may hold values from -1.75 to 1.75
- out_bias: bfloat16 [2, 768], P(None, 'shard'), may hold values from -2 to 2
- attn_gain: bfloat16 [2, 768], P(None, 'shard'), may hold values from 0.5 to 1.5
- attn_shift: bfloat16 [2, 768], P(None, 'shard'), may hold values from -2 to 2
- ffin_weight: bfloat16 [2, 768, 3072], P(None, 'shard'), may hold values from -0.21875 to 0.21875
- ffin_bias: bfloat16 [2, 3072], P(None, 'shard'), may hold values from -2 to 2
- ffout_weight: bfloat16 [2, 3072, 768], P(None, 'shard'), may hold values from -0.109375 to 0.109375
- ffout_bias: bfloat16 [2, 768], P(None, 'shard'), may hold values from -2 to 2
- ffn_gain: bfloat16 [2, 768], P(None, 'shard'), may hold values from 0.5 to 1.5
- ffn_shift: bfloat16 [2, 768], P(None, 'shard'), may hold values from -2 to 2
Outputs:
- out: bfloat16 [32768, 768], P(('rep', 'shard'))
- grad_input: float32 [32768, 768], P(('rep', 'shard'))
- qkv_weight_grad: float32 [2, 768, 2304], P(None, 'shard')
- qv_bias_grad: float32 [2, 1536], P(None, 'shard')
- out_weight_grad: float32 [2, 768, 768], P(None, 'shard')
- out_bias_grad: float32 [2, 768], P(None, 'shard')
- attn_gain_grad: float32 [2, 768], P(None, 'shard')
- attn_shift_grad: float32 [2, 768], P(None, 'shard')
- ffin_weight_grad: float32 [2, 768, 3072], P(None, 'shard')
- ffin_bias_grad: float32 [2, 3072], P(None, 'shard')
- ffout_weight_grad: float32 [2, 3072, 768], P(None, 'shard')
- ffout_bias_grad: float32 [2, 768], P(None, 'shard')
- ffn_gain_grad: float32 [2, 768], P(None, 'shard')
- ffn_shift_grad: float32 [2, 768], P(None, 'shard')
Inputs may be any that keep to these rules, and one draw needn't show every extreme that they name: In each tree the first 512 tokens have segment 0; each of segments 1 to 4 covers 64 consecutive tokens and each of segments 5 to 12 covers 32 consecutive tokens after the trunk, the order of these twelve blocks differing between trees. For every tree, segments 0 to 4 have parent 0 and each of segments 1 to 4 is the parent of exactly two of segments 5 to 12. For every head and tree, each of the 8 clusters holds exactly 128 tokens.
All inputs are finite; a program needn't handle non-finite values.
Results may differ from a plain program's by a relative error of at most 0.02.
Values may be sent and summed in bfloat16 or wider, within the bound.
A program may use at most 320 MiB of HBM per device.

v0:
```python
import jax
import jax.numpy as jnp
from jax import lax
from jax.sharding import PartitionSpec as P

D = 768
HEADS = 12
HEAD_DIM = 64
LAYERS = 2
CLUSTER = 128
TREE_LEN = 1024


norm_eps = 1e-06


def layer_norm(values, norm_gain, norm_shift):
    average = jnp.mean(values, axis=-1, keepdims=True)
    centred = values - average
    variance = jnp.mean(centred * centred, axis=-1, keepdims=True)
    return centred * lax.rsqrt(variance + norm_eps) * norm_gain + norm_shift


def gelu_exact(values):
    return jax.nn.gelu(values, approximate=False)


def dot_first(left_side, right_side):
    return lax.dot_general(
        left_side, right_side, (((0,), (0,)), ((), ())), preferred_element_type=jnp.float32
    )


def dot_last(left_side, right_side):
    return lax.dot_general(
        left_side, right_side, (((1,), (1,)), ((), ())), preferred_element_type=jnp.float32
    )


def lookup_small(index, table):
    match = index[:, None] == jnp.arange(table.shape[0], dtype=jnp.int32)[None, :]
    return jnp.sum(jnp.where(match, table[None, :], 0), axis=1)


def slot_table(cluster_ids):
    length = cluster_ids.shape[0]
    count = length // CLUSTER
    member = (cluster_ids[None, :] == jnp.arange(count, dtype=jnp.int32)[:, None]).astype(jnp.int32)
    rank = jnp.sum(jnp.cumsum(member, axis=1) * member, axis=0) - 1
    slot = cluster_ids * CLUSTER + rank
    return (slot[None, :] == jnp.arange(length, dtype=jnp.int32)[:, None]).astype(jnp.bfloat16)


def to_slots(table, rows):
    return jnp.dot(table, rows, preferred_element_type=jnp.float32).astype(jnp.bfloat16)


def from_slots(table, rows):
    return dot_first(table, rows).astype(jnp.bfloat16)


def block_scores(query_slots, key_slots, slot_ids):
    segs = slot_ids[:, :, 0]
    pars = slot_ids[:, :, 1]
    grands = slot_ids[:, :, 2]
    allowed = (
        (segs[:, None, :] == segs[:, :, None])
        | (segs[:, None, :] == pars[:, :, None])
        | (segs[:, None, :] == grands[:, :, None])
    )
    scaling = query_slots.shape[-1] ** (-0.5)
    scores = (
        jnp.einsum("nqd,nkd->nqk", query_slots, key_slots, preferred_element_type=jnp.float32)
        * scaling
    )
    return jnp.where(allowed, scores, -1e30)


def head_forward(head_inputs):
    query_rows, key_rows, value_rows, segments, parents, grands, cluster_ids = head_inputs
    length, head_size = query_rows.shape
    count = length // CLUSTER
    table = slot_table(cluster_ids)
    joined = jnp.concatenate([query_rows, key_rows, value_rows], axis=1)
    slot_qkv = to_slots(table, joined).reshape(count, CLUSTER, 3 * head_size)
    ids_low = jnp.stack([segments, parents, grands], axis=1).astype(jnp.bfloat16)
    slot_ids = (
        jnp.dot(table, ids_low, preferred_element_type=jnp.float32)
        .astype(jnp.int32)
        .reshape(count, CLUSTER, 3)
    )
    query_slots = slot_qkv[:, :, :head_size]
    key_slots = slot_qkv[:, :, head_size : 2 * head_size]
    value_slots = slot_qkv[:, :, 2 * head_size :]
    masked = block_scores(query_slots, key_slots, slot_ids)
    maxima = jnp.max(masked, axis=2, keepdims=True)
    numerator = jnp.exp(masked - maxima)
    row_total = jnp.sum(numerator, axis=2, keepdims=True)
    softmax_rows = numerator / row_total
    context_slots = jnp.einsum(
        "nqk,nkd->nqd",
        softmax_rows.astype(jnp.bfloat16),
        value_slots,
        preferred_element_type=jnp.float32,
    ).astype(jnp.bfloat16)
    context = from_slots(table, context_slots.reshape(length, head_size))
    return (context, (maxima + jnp.log(row_total))[:, :, 0], slot_qkv, slot_ids)


def head_backward(head_inputs):
    slot_qkv, slot_ids, cluster_ids, grad_context, log_total = head_inputs
    length, head_size = grad_context.shape
    count = length // CLUSTER
    table = slot_table(cluster_ids)
    grad_slots = to_slots(table, grad_context).reshape(count, CLUSTER, head_size)
    query_slots = slot_qkv[:, :, :head_size]
    key_slots = slot_qkv[:, :, head_size : 2 * head_size]
    value_slots = slot_qkv[:, :, 2 * head_size :]
    masked = block_scores(query_slots, key_slots, slot_ids)
    softmax_rows = jnp.exp(masked - log_total[:, :, None])
    grad_value = jnp.einsum(
        "nqk,nqd->nkd",
        softmax_rows.astype(jnp.bfloat16),
        grad_slots,
        preferred_element_type=jnp.float32,
    )
    grad_soft = jnp.einsum(
        "nqd,nkd->nqk", grad_slots, value_slots, preferred_element_type=jnp.float32
    )
    delta = jnp.sum(softmax_rows * grad_soft, axis=2, keepdims=True)
    grad_scores = (softmax_rows * (grad_soft - delta)).astype(jnp.bfloat16)
    scaling = head_size ** (-0.5)
    grad_query = (
        jnp.einsum("nqk,nkd->nqd", grad_scores, key_slots, preferred_element_type=jnp.float32)
        * scaling
    )
    grad_key = (
        jnp.einsum("nqk,nqd->nkd", grad_scores, query_slots, preferred_element_type=jnp.float32)
        * scaling
    )
    joined = jnp.concatenate([grad_query, grad_key, grad_value], axis=2).astype(jnp.bfloat16)
    return from_slots(table, joined.reshape(length, 3 * head_size))


def split_heads(projected, tree_count):
    heads_all = projected.reshape(tree_count, TREE_LEN, 3, HEADS, HEAD_DIM).transpose(2, 0, 3, 1, 4)
    return heads_all.reshape(3, tree_count * HEADS, TREE_LEN, HEAD_DIM)


def layer_forward(layer_in, weights, path_info):
    (
        qkv_weight,
        qv_bias,
        out_weight,
        out_bias,
        attn_gain,
        attn_shift,
        ffin_weight,
        ffin_bias,
        ffout_weight,
        ffout_bias,
        ffn_gain,
        ffn_shift,
    ) = weights
    row_count = layer_in.shape[0]
    tree_count = row_count // TREE_LEN
    layer_low = layer_in.astype(jnp.bfloat16)
    bias_float = qv_bias.astype(jnp.float32)
    full_bias = jnp.concatenate([bias_float[:D], jnp.zeros((D,), jnp.float32), bias_float[D:]])
    projected = (
        jnp.dot(layer_low, qkv_weight, preferred_element_type=jnp.float32) + full_bias
    ).astype(jnp.bfloat16)
    heads_all = split_heads(projected, tree_count)
    context_heads, log_total, slot_qkv, slot_ids = lax.map(
        head_forward, (heads_all[0], heads_all[1], heads_all[2]) + path_info
    )
    context = (
        context_heads.reshape(tree_count, HEADS, TREE_LEN, HEAD_DIM)
        .transpose(0, 2, 1, 3)
        .reshape(row_count, D)
    )
    attn_sum = (
        layer_in
        + jnp.dot(context, out_weight, preferred_element_type=jnp.float32)
        + out_bias.astype(jnp.float32)
    )
    hidden_one = layer_norm(attn_sum, attn_gain.astype(jnp.float32), attn_shift.astype(jnp.float32))
    hidden_low = hidden_one.astype(jnp.bfloat16)
    pre_act = jnp.dot(
        hidden_low, ffin_weight, preferred_element_type=jnp.float32
    ) + ffin_bias.astype(jnp.float32)
    act_low = gelu_exact(pre_act).astype(jnp.bfloat16)
    ffn_sum = (
        hidden_one
        + jnp.dot(act_low, ffout_weight, preferred_element_type=jnp.float32)
        + ffout_bias.astype(jnp.float32)
    )
    result = layer_norm(ffn_sum, ffn_gain.astype(jnp.float32), ffn_shift.astype(jnp.float32))
    saved = (
        layer_low,
        slot_qkv,
        slot_ids,
        context,
        log_total,
        attn_sum,
        hidden_low,
        pre_act,
        act_low,
        ffn_sum,
    )
    return (result, saved)


def layer_backward(grad_out, weights, saved, path_info):
    (
        qkv_weight,
        qv_bias,
        out_weight,
        out_bias,
        attn_gain,
        attn_shift,
        ffin_weight,
        ffin_bias,
        ffout_weight,
        ffout_bias,
        ffn_gain,
        ffn_shift,
    ) = weights
    (
        layer_low,
        slot_qkv,
        slot_ids,
        context,
        log_total,
        attn_sum,
        hidden_low,
        pre_act,
        act_low,
        ffn_sum,
    ) = saved
    row_count = layer_low.shape[0]
    tree_count = row_count // TREE_LEN
    ignored, norm_pull = jax.vjp(
        layer_norm, ffn_sum, ffn_gain.astype(jnp.float32), ffn_shift.astype(jnp.float32)
    )
    grad_ffn_sum, grad_ffn_gain, grad_ffn_shift = norm_pull(grad_out)
    grad_down = grad_ffn_sum.astype(jnp.bfloat16)
    grad_ffout_weight = dot_first(act_low, grad_down)
    grad_ffout_bias = jnp.sum(grad_down.astype(jnp.float32), axis=0)
    grad_act = dot_last(grad_down, ffout_weight)
    ignored, gelu_pull = jax.vjp(gelu_exact, pre_act)
    grad_pre = gelu_pull(grad_act)[0].astype(jnp.bfloat16)
    grad_ffin_weight = dot_first(hidden_low, grad_pre)
    grad_ffin_bias = jnp.sum(grad_pre.astype(jnp.float32), axis=0)
    grad_hidden = grad_ffn_sum + dot_last(grad_pre, ffin_weight)
    ignored, first_pull = jax.vjp(
        layer_norm, attn_sum, attn_gain.astype(jnp.float32), attn_shift.astype(jnp.float32)
    )
    grad_attn_sum, grad_attn_gain, grad_attn_shift = first_pull(grad_hidden)
    grad_attn_low = grad_attn_sum.astype(jnp.bfloat16)
    grad_out_weight = dot_first(context, grad_attn_low)
    grad_out_bias = jnp.sum(grad_attn_low.astype(jnp.float32), axis=0)
    grad_context = dot_last(grad_attn_low, out_weight).astype(jnp.bfloat16)
    grad_heads = grad_context.reshape(tree_count, TREE_LEN, HEADS, HEAD_DIM).transpose(0, 2, 1, 3)
    grad_heads = grad_heads.reshape(tree_count * HEADS, TREE_LEN, HEAD_DIM)
    grad_joined = lax.map(head_backward, (slot_qkv, slot_ids, path_info[3], grad_heads, log_total))
    grad_proj = grad_joined.reshape(tree_count, HEADS, TREE_LEN, 3, HEAD_DIM)
    grad_proj = grad_proj.transpose(0, 2, 3, 1, 4).reshape(row_count, 3 * D)
    grad_qkv_weight = dot_first(layer_low, grad_proj)
    column_sums = jnp.sum(grad_proj.astype(jnp.float32), axis=0)
    grad_qv_bias = jnp.concatenate([column_sums[:D], column_sums[2 * D :]])
    grad_in = grad_attn_sum + dot_last(grad_proj, qkv_weight)
    grads = (
        grad_qkv_weight,
        grad_qv_bias,
        grad_out_weight,
        grad_out_bias,
        grad_attn_gain,
        grad_attn_shift,
        grad_ffin_weight,
        grad_ffin_bias,
        grad_ffout_weight,
        grad_ffout_bias,
        grad_ffn_gain,
        grad_ffn_shift,
    )
    return (grad_in, grads)


def assemble(matrices, vectors):
    return (
        matrices[0],
        vectors[0],
        matrices[1],
        vectors[1],
        vectors[2],
        vectors[3],
        matrices[2],
        vectors[4],
        matrices[3],
        vectors[5],
        vectors[6],
        vectors[7],
    )


def local(
    inputs,
    cotangent,
    segment,
    parent,
    clusters,
    qkv_weight,
    qv_bias,
    out_weight,
    out_bias,
    attn_gain,
    attn_shift,
    ffin_weight,
    ffin_bias,
    ffout_weight,
    ffout_bias,
    ffn_gain,
    ffn_shift,
):
    tree_count = parent.shape[0]
    segments = segment.reshape(tree_count, TREE_LEN)
    parents = jax.vmap(lookup_small)(segments, parent)
    grands = jax.vmap(lookup_small)(parents, parent)
    cluster_ids = (
        clusters.reshape(HEADS, tree_count, TREE_LEN)
        .transpose(1, 0, 2)
        .reshape(tree_count * HEADS, TREE_LEN)
    )
    path_info = (
        jnp.repeat(segments, HEADS, axis=0),
        jnp.repeat(parents, HEADS, axis=0),
        jnp.repeat(grands, HEADS, axis=0),
        cluster_ids,
    )
    hidden = inputs.astype(jnp.float32)
    kept_saved = []
    for layer_index in range(LAYERS):
        weights = (
            lax.all_gather(qkv_weight[layer_index], "shard", axis=0, tiled=True),
            lax.all_gather(qv_bias[layer_index], "shard", axis=0, tiled=True),
            lax.all_gather(out_weight[layer_index], "shard", axis=0, tiled=True),
            lax.all_gather(out_bias[layer_index], "shard", axis=0, tiled=True),
            lax.all_gather(attn_gain[layer_index], "shard", axis=0, tiled=True),
            lax.all_gather(attn_shift[layer_index], "shard", axis=0, tiled=True),
            lax.all_gather(ffin_weight[layer_index], "shard", axis=0, tiled=True),
            lax.all_gather(ffin_bias[layer_index], "shard", axis=0, tiled=True),
            lax.all_gather(ffout_weight[layer_index], "shard", axis=0, tiled=True),
            lax.all_gather(ffout_bias[layer_index], "shard", axis=0, tiled=True),
            lax.all_gather(ffn_gain[layer_index], "shard", axis=0, tiled=True),
            lax.all_gather(ffn_shift[layer_index], "shard", axis=0, tiled=True),
        )
        hidden, saved = layer_forward(hidden, weights, path_info)
        kept_saved.append(saved)
    result = hidden.astype(jnp.bfloat16)
    grad_rows = cotangent.astype(jnp.float32)
    per_layer = [None] * LAYERS
    for layer_index in reversed(range(LAYERS)):
        weights = (
            lax.all_gather(qkv_weight[layer_index], "shard", axis=0, tiled=True),
            lax.all_gather(qv_bias[layer_index], "shard", axis=0, tiled=True),
            lax.all_gather(out_weight[layer_index], "shard", axis=0, tiled=True),
            lax.all_gather(out_bias[layer_index], "shard", axis=0, tiled=True),
            lax.all_gather(attn_gain[layer_index], "shard", axis=0, tiled=True),
            lax.all_gather(attn_shift[layer_index], "shard", axis=0, tiled=True),
            lax.all_gather(ffin_weight[layer_index], "shard", axis=0, tiled=True),
            lax.all_gather(ffin_bias[layer_index], "shard", axis=0, tiled=True),
            lax.all_gather(ffout_weight[layer_index], "shard", axis=0, tiled=True),
            lax.all_gather(ffout_bias[layer_index], "shard", axis=0, tiled=True),
            lax.all_gather(ffn_gain[layer_index], "shard", axis=0, tiled=True),
            lax.all_gather(ffn_shift[layer_index], "shard", axis=0, tiled=True),
        )
        grad_rows, grads = layer_backward(grad_rows, weights, kept_saved[layer_index], path_info)
        owned = (
            lax.psum_scatter(grads[0], "shard", scatter_dimension=0, tiled=True),
            lax.psum_scatter(grads[1], "shard", scatter_dimension=0, tiled=True),
            lax.psum_scatter(grads[2], "shard", scatter_dimension=0, tiled=True),
            lax.psum_scatter(grads[3], "shard", scatter_dimension=0, tiled=True),
            lax.psum_scatter(grads[4], "shard", scatter_dimension=0, tiled=True),
            lax.psum_scatter(grads[5], "shard", scatter_dimension=0, tiled=True),
            lax.psum_scatter(grads[6], "shard", scatter_dimension=0, tiled=True),
            lax.psum_scatter(grads[7], "shard", scatter_dimension=0, tiled=True),
            lax.psum_scatter(grads[8], "shard", scatter_dimension=0, tiled=True),
            lax.psum_scatter(grads[9], "shard", scatter_dimension=0, tiled=True),
            lax.psum_scatter(grads[10], "shard", scatter_dimension=0, tiled=True),
            lax.psum_scatter(grads[11], "shard", scatter_dimension=0, tiled=True),
        )
        vectors = lax.psum(
            (owned[1], owned[3], owned[4], owned[5], owned[7], owned[9], owned[10], owned[11]),
            "rep",
        )
        matrices = (
            lax.all_gather(
                lax.psum_scatter(
                    owned[0].astype(jnp.bfloat16), "rep", scatter_dimension=1, tiled=True
                ),
                "rep",
                axis=1,
                tiled=True,
            ).astype(jnp.float32),
            lax.all_gather(
                lax.psum_scatter(
                    owned[2].astype(jnp.bfloat16), "rep", scatter_dimension=1, tiled=True
                ),
                "rep",
                axis=1,
                tiled=True,
            ).astype(jnp.float32),
            lax.all_gather(
                lax.psum_scatter(
                    owned[6].astype(jnp.bfloat16), "rep", scatter_dimension=1, tiled=True
                ),
                "rep",
                axis=1,
                tiled=True,
            ).astype(jnp.float32),
            lax.all_gather(
                lax.psum_scatter(
                    owned[8].astype(jnp.bfloat16), "rep", scatter_dimension=1, tiled=True
                ),
                "rep",
                axis=1,
                tiled=True,
            ).astype(jnp.float32),
        )
        owned = assemble(matrices, vectors)
        per_layer[layer_index] = owned
    stacked = tuple(
        (
            jnp.stack([per_layer[layer_index][member] for layer_index in range(LAYERS)])
            for member in range(12)
        )
    )
    return (
        result,
        grad_rows,
        stacked[0],
        stacked[1],
        stacked[2],
        stacked[3],
        stacked[4],
        stacked[5],
        stacked[6],
        stacked[7],
        stacked[8],
        stacked[9],
        stacked[10],
        stacked[11],
    )


def solution(mesh):
    in_specs = (
        P(("rep", "shard"), None),
        P(("rep", "shard"), None),
        P(("rep", "shard")),
        P(("rep", "shard"), None),
        P(None, ("rep", "shard")),
        P(None, "shard", None),
        P(None, "shard"),
        P(None, "shard", None),
        P(None, "shard"),
        P(None, "shard"),
        P(None, "shard"),
        P(None, "shard", None),
        P(None, "shard"),
        P(None, "shard", None),
        P(None, "shard"),
        P(None, "shard"),
        P(None, "shard"),
    )
    out_specs = (
        P(("rep", "shard"), None),
        P(("rep", "shard"), None),
        P(None, "shard", None),
        P(None, "shard"),
        P(None, "shard", None),
        P(None, "shard"),
        P(None, "shard"),
        P(None, "shard"),
        P(None, "shard", None),
        P(None, "shard"),
        P(None, "shard", None),
        P(None, "shard"),
        P(None, "shard"),
        P(None, "shard"),
    )
    return jax.shard_map(local, mesh=mesh, in_specs=in_specs, out_specs=out_specs, check_vma=False)
```

profile of v0, /device:TPU:17, one launch (start us, length us, event | category | flops | bytes accessed | tf_op | source)
XLA Modules:
  0.0 2203.3 jit_solution(15207280294058404020)
XLA Ops:
  22.8 26.1 %all-reduce.32 = (bf16[1536]{0:T(1024)(128)(2,1)S(1)}, bf16[1536]{0:T(1024)(128)(2,1)S(1)}, bf16[768]{0:T(1024)(128)(2,1)S(1)}, bf16[768]{0:T(1024)(128)(2,1)S(1...) all-reduce(bf16[1536]{0:T(1024)(128)(2,1)S(1)} %dynamic-update-slic, ...), channel_id=3, replica_groups=mesh['rep'=4,'shard'=8] {'shard'}, use_global_device_ids=true, to_apply=%add | all-reduce | flops 12288 | bytes 49152
  50.9 23.6 %all-gather.7 = bf16[1,3072]{1,0:T(2,128)(2,1)S(1)} all-gather(bf16[1,384]{1,0:T(2,128)(2,1)S(1)} %get-tuple-element.968), channel_id=9, replica_groups=mesh['rep'=4,'shard'=8] {'shard'}, dimensions={1}, use_global_device_ids=true | all-gather | bytes 6912 | tf_op jit(solution)/shard_map/all_gather | solution.py:352
  76.4 22.1 %all-gather.19 = bf16[1,3072]{1,0:T(2,128)(2,1)S(1)} all-gather(bf16[1,384]{1,0:T(2,128)(2,1)S(1)} %get-tuple-element.967), channel_id=21, replica_groups=mesh['rep'=4,'shard'=8] {'shard'}, dimensions={1}, use_global_device_ids=true | all-gather | bytes 6912 | tf_op jit(solution)/shard_map/all_gather | solution.py:352
  102.6 7.4 add_convert_fusion.3
  110.0 6.7 copy.250
  116.7 4.8 slice_bitcast_fusion.15
  126.0 137.5 %while.60 = (s32[]{:T(128)}, bf16[12,1024,64]{1,2,0:T(8,128)(2,1)}, f32[12,8,128]{2,1,0:T(8,128)S(1)}, bf16[12,8,128,192]{2,1,3,0:T(8,128)(2,1)}, s32[12,8,128,3...) while((s32[]{:T(128)}, bf16[12,1024,64]{1,2,0:T(8,128)(2,1)}, ...), condition=%wide.region_8.9_spmd, body=%wide.region_2.8_spmd.sunk | while | flops 584189440 | bytes 7424453 | solution.py:174
  264.1 3.9 fusion.232
  269.4 38.1 %multiply_convert_fusion.3 = (bf16[1024,3072]{1,0:T(8,128)(2,1)}, f32[1024,3072]{1,0:T(8,128)}, f32[1024,3072]{1,0:T(8,128)}) fusion(f32[3072]{0:T(1024)S(1)} %bitcast.671, bf16[1,768,3072]{2,1,0:T(8,128)(2,1)} %all-gather.39.cloned.1.call-done, f32[1024,768]{0,1:T(8,128)S(1)} %get-tuple-element.984, f32[768]{0:T(1024)S(1)} %convert_element_type.392, ...), kind=kOutput, calls=%fused_computation.259 | convolution fusion | flops 5043388416 | bytes 39348224 | tf_op jit(solution)/shard_map/dot_general | solution.py:189
  307.5 9.1 fusion.233
  319.3 26.1 %all-gather.43.cloned.1.call-done = bf16[1,768,2304]{2,1,0:T(8,128)(2,1)} async-done(((bf16[1,96,2304]{2,1,0:T(8,128)(2,1)}), bf16[1,768,2304]{2,1,0:T(8,128)(2,1)}) %all-gather.43.cloned.1.call-update) | async-done | bytes 3538960 | tf_op jit(solution)/shard_map/all_gather | solution.py:345
  345.4 9.2 add_convert_fusion.2
  354.6 6.7 copy.254
  361.3 4.8 slice_bitcast_fusion.12
  370.6 137.5 %while.61 = (s32[]{:T(128)}, bf16[12,1024,64]{1,2,0:T(8,128)(2,1)}, f32[12,8,128]{2,1,0:T(8,128)S(1)}, bf16[12,8,128,192]{2,1,3,0:T(8,128)(2,1)}, s32[12,8,128,3...) while((s32[]{:T(128)}, bf16[12,1024,64]{1,2,0:T(8,128)(2,1)}, ...), condition=%wide.region_19.20_spmd, body=%wide.region_13.19_spmd.sunk | while | flops 584189440 | bytes 7424453 | solution.py:174
  508.8 4.6 fusion.234
  514.3 38.0 %multiply_convert_fusion.2 = (bf16[1024,3072]{1,0:T(8,128)(2,1)}, f32[1024,3072]{1,0:T(8,128)}, f32[1024,3072]{1,0:T(8,128)}) fusion(f32[3072]{0:T(1024)S(1)} %bitcast.673, bf16[1,768,3072]{2,1,0:T(8,128)(2,1)} %all-gather.47.cloned.1.call-done, f32[1024,768]{0,1:T(8,128)S(1)} %get-tuple-element.989, f32[768]{0:T(1024)S(1)} %copy-done.55, ...), kind=kOutput, calls=%fused_computation.246 | convolution fusion | flops 5043388416 | bytes 39348224 | tf_op jit(solution)/shard_map/dot_general | solution.py:189
  552.4 9.7 fusion.235
  566.0 3.3 convert_reduce_fusion.5
  569.3 18.0 convert_reduce_fusion
  587.3 11.9 multiply_reduce_fusion.3
  602.1 4.2 fusion.237
  606.3 4.3 convolution_convert_fusion.5
  610.6 4.1 copy.261
  617.5 146.7 %while.62 = (s32[]{:T(128)}, bf16[12,1024,192]{1,2,0:T(8,128)(2,1)}, s32[12,1024]{1,0:T(8,128)}, s32[12,8,128,3]{2,1,3,0:T(8,128)}, bf16[12,8,128,192]{2,1,3,0:T...) while((s32[]{:T(128)}, ...), condition=%wide.region_33.34_spmd, body=%wide.region_28.33_spmd.sunk | while | flops 627549696 | bytes 9050521 | solution.py:266
  769.4 5.4 multiply_reduce_fusion.2
  778.0 19.6 convert_reduce_fusion.1
  797.6 10.4 multiply_reduce_fusion.4
  813.5 4.2 copy.266
  817.7 4.7 fusion.236
  825.3 147.0 %while.63 = (s32[]{:T(128)}, bf16[12,1024,192]{1,2,0:T(8,128)(2,1)}, s32[12,1024]{1,0:T(8,128)}, s32[12,8,128,3]{2,1,3,0:T(8,128)}, bf16[12,8,128,192]{2,1,3,0:T...) while((s32[]{:T(128)}, ...), condition=%wide.region_43.44_spmd, body=%wide.region_38.43_spmd.sunk | while | flops 627549696 | bytes 9050521 | solution.py:266
  977.5 5.8 convolution_bitcast_fusion
  983.3 8.0 copy.294
  992.0 10.2 fusion.210
  1002.2 9.9 fusion.239
  1020.4 9.9 fusion.238
  1031.0 10.5 fusion.213
  1045.6 73.9 %reduce-scatter.49.cloned.1.call-done = f32[96,2304]{1,0:T(8,128)} async-done(((f32[768,2304]{1,0:T(8,128)}), f32[96,2304]{1,0:T(8,128)}) %reduce-scatter.49.cloned.1.call-update) | async-done | bytes 884752
  1121.7 129.8 %reduce-scatter.31.cloned.1.call-done = f32[96,2304]{1,0:T(8,128)} async-done(((f32[768,2304]{1,0:T(8,128)}), f32[96,2304]{1,0:T(8,128)}) %reduce-scatter.31.cloned.1.call-update) | async-done | bytes 884752 | tf_op jit(solution)/shard_map/reduce_scatter | solution.py:380
  1255.7 10.6 fusion.207
  1268.6 149.0 %reduce-scatter.47.cloned.1.call-done = f32[384,768]{1,0:T(8,128)} async-done(((f32[3072,768]{1,0:T(8,128)}), f32[384,768]{1,0:T(8,128)}) %reduce-scatter.47.cloned.1.call-update) | async-done | bytes 1179664 | tf_op jit(solution)/shard_map/reduce_scatter | solution.py:388
  1422.1 9.0 add_add_fusion.8
  1431.1 3.7 copy.278
  1436.3 57.0 %all-reduce.35.cloned.1.call-done = (f32[1536]{0:T(1024)}, f32[1536]{0:T(1024)}, f32[768]{0:T(1024)}, f32[768]{0:T(1024)}, f32[768]{0:T(1024)}, /*index=5*/f32[7...) async-done(((f32[1536]{0:T(1024)}, f32[1536]{0:T(1024)}, ...) | async-done | bytes 73744
  1498.6 162.6 %reduce-scatter.45.cloned.1.call-done = f32[384,768]{1,0:T(8,128)} async-done(((f32[3072,768]{1,0:T(8,128)}), f32[384,768]{1,0:T(8,128)}) %reduce-scatter.45.cloned.1.call-update) | async-done | bytes 1179664 | tf_op jit(solution)/shard_map/reduce_scatter | solution.py:388
  1670.4 10.3 all-reduce.31
  1681.9 145.4 %reduce-scatter.37.cloned.1.call-done = f32[96,3072]{1,0:T(8,128)} async-done(((f32[768,3072]{1,0:T(8,128)}), f32[96,3072]{1,0:T(8,128)}) %reduce-scatter.37.cloned.1.call-update) | async-done | bytes 1179664 | tf_op jit(solution)/shard_map/reduce_scatter | solution.py:386
  1832.9 16.2 reduce-scatter.55.cloned.1.call-done
  1849.1 6.4 all_gather.135
  1855.6 16.2 reduce-scatter.53.cloned.1.call-done
  1871.8 6.4 all_gather.134
  1879.4 17.7 reduce-scatter.29.cloned.1.call-done
  1898.1 7.1 all-gather.24
  1905.9 16.2 reduce-scatter.51.cloned.1.call-done
  1923.2 7.1 all-gather.25
  1930.9 157.5 %reduce-scatter.41.cloned.1.call-done = f32[96,3072]{1,0:T(8,128)} async-done(((f32[768,3072]{1,0:T(8,128)}), f32[96,3072]{1,0:T(8,128)}) %reduce-scatter.41.cloned.1.call-update) | async-done | bytes 1179664 | tf_op jit(solution)/shard_map/reduce_scatter | solution.py:386
  2091.9 21.0 reduce-scatter.59.cloned.1.call-done
  2112.9 7.8 all_gather.139
  2120.8 16.8 reduce-scatter.57.cloned.1.call-done
  2137.6 7.8 all_gather.138
  2147.5 14.5 reduce-scatter.39.cloned.1.call-done
  2162.0 7.8 all_gather.136
  2169.9 17.3 reduce-scatter.43.cloned.1.call-done
  2187.2 7.8 all_gather.137
  (1575 shorter events, 691.0 us)
Async XLA Ops:
  7.2 95.4 %all-gather.35.cloned.1.call-start = ((), (), s32[]{:S(2)}) async-start(), calls=%async_computation.26 | async-start | bytes 3981312 | tf_op jit(solution)/shard_map/all_gather | solution.py:345
  9.5 254.0 %all-gather.37.cloned.1.call-start = ((), (), s32[]{:S(2)}) async-start(), calls=%async_computation.27 | async-start | bytes 1327104 | tf_op jit(solution)/shard_map/all_gather | solution.py:347
  11.2 258.2 %all-gather.39.cloned.1.call-start = ((), (), s32[]{:S(2)}) async-start(), calls=%async_computation.28 | async-start | bytes 5308416 | tf_op jit(solution)/shard_map/all_gather | solution.py:351
  12.4 5.5 copy-start.65
  12.4 7.4 copy-start.63
  12.5 36.5 %copy-start.50 = (s32[1024]{0:T(1024)S(1)}, s32[1024]{0:T(1024)}, u32[]{:S(2)}) copy-start(s32[1024]{0:T(1024)} %param.27) | copy-start | bytes 12292
  12.5 36.5 %copy-start.64 = (s32[1,13]{1,0:T(1,128)S(1)}, s32[1,13]{1,0:T(1,128)}, u32[]{:S(2)}) copy-start(s32[1,13]{1,0:T(1,128)} %param.28) | copy-start | bytes 160
  12.5 36.8 %copy-start.16 = (bf16[1024,768]{1,0:T(8,128)(2,1)S(1)}, bf16[1024,768]{1,0:T(8,128)(2,1)}, u32[]{:S(2)}) copy-start(bf16[1024,768]{1,0:T(8,128)(2,1)} %param.25) | copy-start | bytes 4718596
  12.5 295.0 %all-gather.41.cloned.1.call-start = ((), (), s32[]{:S(2)}) async-start(), calls=%async_computation.29 | async-start | bytes 5308416 | tf_op jit(solution)/shard_map/all_gather | solution.py:353
  15.1 35.8 %copy-start.54 = (bf16[2,384]{1,0:T(2,128)(2,1)S(1)}, bf16[2,384]{1,0:T(2,128)(2,1)}, u32[]{:S(2)}) copy-start(bf16[2,384]{1,0:T(2,128)(2,1)} %param.37) | copy-start | bytes 4612
  15.1 85.2 %copy-start.15 = (bf16[1024,768]{1,0:T(8,128)(2,1)S(1)}, bf16[1024,768]{1,0:T(8,128)(2,1)}, u32[]{:S(2)}) copy-start(bf16[1024,768]{1,0:T(8,128)(2,1)} %param.26) | copy-start | bytes 4718596
  15.1 330.3 %all-gather.43.cloned.1.call-start = ((), (), s32[]{:S(2)}) async-start(), calls=%async_computation.30 | async-start | bytes 3981312 | tf_op jit(solution)/shard_map/all_gather | solution.py:345
  15.7 492.5 %all-gather.45.cloned.1.call-start = ((), (), s32[]{:S(2)}) async-start(), calls=%async_computation.31 | async-start | bytes 1327104 | tf_op jit(solution)/shard_map/all_gather | solution.py:347
  16.2 497.7 %all-gather.47.cloned.1.call-start = ((), (), s32[]{:S(2)}) async-start(), calls=%async_computation.32 | async-start | bytes 5308416 | tf_op jit(solution)/shard_map/all_gather | solution.py:351
  17.0 535.3 %all-gather.49.cloned.1.call-start = ((), (), s32[]{:S(2)}) async-start(), calls=%async_computation.33 | async-start | bytes 5308416 | tf_op jit(solution)/shard_map/all_gather | solution.py:353
  17.7 1023.8 %reduce-scatter.35.cloned.1.call-start = ((), (), s32[]{:S(2)}) async-start(), calls=%async_computation.19 | async-start | bytes 2654208 | tf_op jit(solution)/shard_map/reduce_scatter | solution.py:382
  50.9 256.6 %copy-start.39 = (f32[768]{0:T(1024)}, f32[768]{0:T(1024)S(1)}, u32[]{:S(2)}) copy-start(f32[768]{0:T(1024)S(1)} %convert_element_type.391) | copy-start | bytes 9220
  50.9 256.6 %copy-start.57 = (f32[768]{0:T(1024)}, f32[768]{0:T(1024)S(1)}, u32[]{:S(2)}) copy-start(f32[768]{0:T(1024)S(1)} %convert_element_type.392) | copy-start | bytes 9220
  74.5 194.9 %copy-start.51 = (f32[1,3072]{1,0:T(1,128)}, f32[1,3072]{1,0:T(1,128)S(1)}, u32[]{:S(2)}) copy-start(f32[1,3072]{1,0:T(1,128)S(1)} %convert_element_type.377) | copy-start | bytes 36868
  74.6 434.2 %copy-start.41 = (f32[768]{0:T(1024)}, f32[768]{0:T(1024)S(1)}, u32[]{:S(2)}) copy-start(f32[768]{0:T(1024)S(1)} %convert_element_type.394) | copy-start | bytes 9220
  74.6 434.2 %copy-start.59 = (f32[768]{0:T(1024)}, f32[768]{0:T(1024)S(1)}, u32[]{:S(2)}) copy-start(f32[768]{0:T(1024)S(1)} %convert_element_type.395) | copy-start | bytes 9220
  268.1 39.4 %copy-start.1 = (f32[1024,768]{0,1:T(8,128)}, f32[1024,768]{0,1:T(8,128)S(1)}, u32[]{:S(2)}) copy-start(f32[1024,768]{0,1:T(8,128)S(1)} %get-tuple-element.984) | copy-start | bytes 9437188
  268.1 39.4 %copy-start.27 = (f32[1024]{0:T(1024)}, f32[1024]{0:T(1024)S(1)}, u32[]{:S(2)}) copy-start(f32[1024]{0:T(1024)S(1)} %broadcast_multiply_fusion.3) | copy-start | bytes 12292
  269.4 38.1 %copy-start.43 = (f32[1024]{0:T(1024)}, f32[1024]{0:T(1024)S(1)}, u32[]{:S(2)}) copy-start(f32[1024]{0:T(1024)S(1)} %fusion.203) | copy-start | bytes 12292
  316.7 192.1 %copy-start.31 = (f32[1024]{0:T(1024)}, f32[1024]{0:T(1024)S(1)}, u32[]{:S(2)}) copy-start(f32[1024]{0:T(1024)S(1)} %broadcast_multiply_fusion.2) | copy-start | bytes 12292
  319.3 189.5 %copy-start.47 = (f32[1024]{0:T(1024)}, f32[1024]{0:T(1024)S(1)}, u32[]{:S(2)}) copy-start(f32[1024]{0:T(1024)S(1)} %fusion.204) | copy-start | bytes 12292
  370.6 138.2 %copy-start.62 = (f32[768]{0:T(1024)S(1)}, f32[768]{0:T(1024)}, u32[]{:S(2)}) copy-start(f32[768]{0:T(1024)} %convert_element_type.397) | copy-start | bytes 9220
  513.5 38.8 %copy-start.3 = (f32[1024,768]{0,1:T(8,128)}, f32[1024,768]{0,1:T(8,128)S(1)}, u32[]{:S(2)}) copy-start(f32[1024,768]{0,1:T(8,128)S(1)} %get-tuple-element.989) | copy-start | bytes 9437188
  513.5 85.6 %copy-start.29 = (f32[1024]{0:T(1024)}, f32[1024]{0:T(1024)S(1)}, u32[]{:S(2)}) copy-start(f32[1024]{0:T(1024)S(1)} %broadcast_multiply_fusion.1) | copy-start | bytes 12292
  514.0 85.2 %copy-start.45 = (f32[1024]{0:T(1024)}, f32[1024]{0:T(1024)S(1)}, u32[]{:S(2)}) copy-start(f32[1024]{0:T(1024)S(1)} %fusion.205) | copy-start | bytes 12292
  514.3 38.1 %copy-start.61 = (f32[768]{0:T(1024)S(1)}, f32[768]{0:T(1024)}, u32[]{:S(2)}) copy-start(f32[768]{0:T(1024)} %convert_element_type.400) | copy-start | bytes 9220
  552.3 9.7 copy-start
  552.3 9.7 copy-start.26
  569.3 18.0 copy-start.18
  587.2 11.9 copy-start.4
  767.2 7.6 copy-start.14
  775.7 267.8 %reduce-scatter.33.cloned.1.call-start = ((), (), s32[]{:S(2)}) async-start(), calls=%async_computation.18 | async-start | bytes 2654208 | tf_op jit(solution)/shard_map/reduce_scatter | solution.py:382
  777.9 19.6 copy-start.2
  777.9 19.6 copy-start.11
  778.0 19.6 copy-start.28
  778.0 19.6 copy-start.40
  778.0 19.6 copy-start.44
  797.6 10.4 copy-start.34
  822.4 297.0 %reduce-scatter.49.cloned.1.call-start = ((), (), s32[]{:S(2)}) async-start(), calls=%async_computation.34 | async-start | bytes 7962624
  991.3 260.2 %reduce-scatter.31.cloned.1.call-start = ((), (), s32[]{:S(2)}) async-start(), calls=%async_computation.17 | async-start | bytes 7962624 | tf_op jit(solution)/shard_map/reduce_scatter | solution.py:380
  1002.2 415.4 %reduce-scatter.47.cloned.1.call-start = ((), (), s32[]{:S(2)}) async-start(), calls=%async_computation.25 | async-start | bytes 10616832 | tf_op jit(solution)/shard_map/reduce_scatter | solution.py:388
  1012.2 481.0 %all-reduce.35.cloned.1.call-start = ((), (), s32[]{:S(2)}) async-start(), calls=%async_computation.40 | async-start | bytes 180224
  1020.4 640.8 %reduce-scatter.45.cloned.1.call-start = ((), (), s32[]{:S(2)}) async-start(), calls=%async_computation.24 | async-start | bytes 10616832 | tf_op jit(solution)/shard_map/reduce_scatter | solution.py:388
  1030.3 797.0 %reduce-scatter.37.cloned.1.call-start = ((), (), s32[]{:S(2)}) async-start(), calls=%async_computation.20 | async-start | bytes 10616832 | tf_op jit(solution)/shard_map/reduce_scatter | solution.py:386
  1041.5 807.6 %reduce-scatter.55.cloned.1.call-start = ((), (), s32[]{:S(2)}) async-start(), calls=%async_computation.37 | async-start | bytes 245760
  1043.4 212.2 %copy-start.5 = (f32[1024,768]{0,1:T(8,128)S(1)}, f32[1024,768]{0,1:T(8,128)}, u32[]{:S(2)}) copy-start(f32[1024,768]{0,1:T(8,128)} %copy-done.3) | copy-start | bytes 9437188
  1043.4 212.3 %copy-start.30 = (f32[1024]{0:T(1024)S(1)}, f32[1024]{0:T(1024)}, u32[]{:S(2)}) copy-start(f32[1024]{0:T(1024)} %copy-done.29) | copy-start | bytes 12292
  1043.4 212.3 %copy-start.38 = (f32[768]{0:T(1024)S(1)}, f32[768]{0:T(1024)}, u32[]{:S(2)}) copy-start(f32[768]{0:T(1024)} %convert_element_type.398) | copy-start | bytes 9220
  1043.4 212.3 %copy-start.46 = (f32[1024]{0:T(1024)S(1)}, f32[1024]{0:T(1024)}, u32[]{:S(2)}) copy-start(f32[1024]{0:T(1024)} %copy-done.45) | copy-start | bytes 12292
  1043.4 212.3 %copy-start.56 = (f32[768]{0:T(1024)S(1)}, f32[768]{0:T(1024)}, u32[]{:S(2)}) copy-start(f32[768]{0:T(1024)} %convert_element_type.399) | copy-start | bytes 9220
  1043.4 828.3 %reduce-scatter.53.cloned.1.call-start = ((), (), s32[]{:S(2)}) async-start(), calls=%async_computation.36 | async-start | bytes 245760
  1045.5 851.6 %reduce-scatter.29.cloned.1.call-start = ((), (), s32[]{:S(2)}) async-start(), calls=%async_computation.16 | async-start | bytes 737280 | tf_op jit(solution)/shard_map/reduce_scatter | solution.py:399
  1121.7 800.4 %reduce-scatter.51.cloned.1.call-start = ((), (), s32[]{:S(2)}) async-start(), calls=%async_computation.35 | async-start | bytes 737280
  1255.6 832.8 %reduce-scatter.41.cloned.1.call-start = ((), (), s32[]{:S(2)}) async-start(), calls=%async_computation.22 | async-start | bytes 10616832 | tf_op jit(solution)/shard_map/reduce_scatter | solution.py:386
  1266.3 155.8 %copy-start.9 = (f32[1024,768]{0,1:T(8,128)S(1)}, f32[1024,768]{0,1:T(8,128)}, u32[]{:S(2)}) copy-start(f32[1024,768]{0,1:T(8,128)} %copy-done.8) | copy-start | bytes 9437188
  1266.3 846.6 %reduce-scatter.59.cloned.1.call-start = ((), (), s32[]{:S(2)}) async-start(), calls=%async_computation.39 | async-start | bytes 737280
  1421.8 715.7 %reduce-scatter.57.cloned.1.call-start = ((), (), s32[]{:S(2)}) async-start(), calls=%async_computation.38 | async-start | bytes 737280
  1663.6 498.4 %reduce-scatter.39.cloned.1.call-start = ((), (), s32[]{:S(2)}) async-start(), calls=%async_computation.21 | async-start | bytes 737280 | tf_op jit(solution)/shard_map/reduce_scatter | solution.py:415
  1829.4 357.8 %reduce-scatter.43.cloned.1.call-start = ((), (), s32[]{:S(2)}) async-start(), calls=%async_computation.23 | async-start | bytes 737280 | tf_op jit(solution)/shard_map/reduce_scatter | solution.py:415
  (35 other events, 99.8 us)
Sparse Core Ops, SparseCore 0:
  10.8 65.5 all-gather.34
  78.6 39.2 all-gather.36
  120.6 79.4 all-gather.38
  202.1 77.8 all-gather.40
  282.0 63.3 all-gather.42
  347.4 39.0 all-gather.44
  389.3 79.1 all-gather.46
  470.7 78.0 all-gather.48
  775.8 66.3 reduce-scatter.34
  846.1 68.1 reduce-scatter.32
  991.5 127.9 reduce-scatter.48
  1123.4 128.0 reduce-scatter.30
  1255.1 162.4 reduce-scatter.46
  1422.6 70.5 all-reduce.34
  1496.7 164.4 reduce-scatter.44
  1664.7 162.5 reduce-scatter.36
  1829.6 19.5 reduce-scatter.54
  1852.0 19.7 reduce-scatter.52
  1874.9 22.1 reduce-scatter.28
  1900.0 22.0 reduce-scatter.50
  1925.7 162.6 reduce-scatter.40
  2090.9 21.9 reduce-scatter.58
  2115.4 22.0 reduce-scatter.56
  2139.9 22.0 reduce-scatter.38
  2165.1 22.0 reduce-scatter.42
where the time goes:
time: 2220 us; the launch traced here: 2200 us
  waiting for transfers between devices  1040 us (47%)
  matrix products  497 us (22%)
  local copies, waits for them, and re-layouts  291 us (13%)
  other arithmetic  209 us (9%)
  blocking collectives  141 us (6%)
    reduce_scatter x2, waiting for transfers between devices, local(): lax.psum_scatter(grads[8], 'shard', scatter_dimension=0, tiled=True)  312 us
    reduce_scatter x2, waiting for transfers between devices, local(): lax.psum_scatter(grads[6], 'shard', scatter_dimension=0, tiled=True)  303 us
    unnamed x32, waiting for transfers between devices  220 us
    dot_general x56, matrix products, dot_first(): lax.dot_general(left_side, right_side, (((0,), (0,)), ((), ())), preferre...  140 us
    reduce_scatter x1, waiting for transfers between devices, local(): lax.psum_scatter(grads[0], 'shard', scatter_dimension=0, tiled=True)  130 us
    another operation x96, other arithmetic  117 us
    dot_general x8, matrix products, dot_last(): lax.dot_general(left_side, right_side, (((1,), (1,)), ((), ())), preferre...  81 us
    dot_general x48, matrix products, to_slots(): jnp.dot(table, rows, preferred_element_type=jnp.float32)  77.2 us
  transfers between devices with their start and end apart: 25, of which 16 were waited for; matrix products, arithmetic and copies ran while one was open for 35% of the time, Pallas kernels for 0%

commit v1 on v0

v1 whole, which is shorter than its diff:
```python
import functools

import jax
import jax.numpy as jnp
from jax import lax
from jax.experimental import pallas as pl
from jax.experimental.pallas import tpu as pltpu
from jax.sharding import PartitionSpec as P

D = 768
HEADS = 12
HEAD_DIM = 64
LAYERS = 2
CLUSTER = 128
TREE_LEN = 1024


norm_eps = 1e-06


def layer_norm(values, norm_gain, norm_shift):
    average = jnp.mean(values, axis=-1, keepdims=True)
    centred = values - average
    variance = jnp.mean(centred * centred, axis=-1, keepdims=True)
    return centred * lax.rsqrt(variance + norm_eps) * norm_gain + norm_shift


def gelu_exact(values):
    return jax.nn.gelu(values, approximate=False)


def dot_first(left_side, right_side):
    return lax.dot_general(
        left_side, right_side, (((0,), (0,)), ((), ())), preferred_element_type=jnp.float32
    )


def dot_last(left_side, right_side):
    return lax.dot_general(
        left_side, right_side, (((1,), (1,)), ((), ())), preferred_element_type=jnp.float32
    )


def lookup_small(index, table):
    match = index[:, None] == jnp.arange(table.shape[0], dtype=jnp.int32)[None, :]
    return jnp.sum(jnp.where(match, table[None, :], 0), axis=1)


PAIRS = HEADS // 2
LANES = 2 * HEAD_DIM
KERNEL_VMEM = 60 * 2**20


def slot_ranks(cluster_ids):
    length = cluster_ids.shape[-1]
    count = length // CLUSTER
    order = jnp.arange(count, dtype=jnp.int32)
    member = cluster_ids[..., None, :] == order[:, None]
    upto = jnp.arange(length, dtype=jnp.int32)
    triangle = (upto[:, None] <= upto[None, :]).astype(jnp.bfloat16)
    ranks = jnp.dot(
        member.astype(jnp.bfloat16), triangle, preferred_element_type=jnp.float32
    ).astype(jnp.int32)
    return jnp.sum(jnp.where(member, ranks - 1 + CLUSTER * order[:, None], 0), axis=-2)


def one_hot_rows(slot_row):
    length = slot_row.shape[-1]
    rows = lax.broadcasted_iota(jnp.int32, (length, length), 0)
    return jnp.where(rows == slot_row, 1.0, 0.0).astype(jnp.bfloat16)


def first_lanes(length):
    return lax.broadcasted_iota(jnp.int32, (length, LANES), 1) < HEAD_DIM


def contract_last(left_side, right_side):
    return lax.dot_general(
        left_side, right_side, (((1,), (1,)), ((), ())), preferred_element_type=jnp.float32
    )


def contract_first(left_side, right_side):
    return lax.dot_general(
        left_side, right_side, (((0,), (0,)), ((), ())), preferred_element_type=jnp.float32
    )


def cluster_blocks(values):
    return [values[at : at + CLUSTER] for at in range(0, values.shape[0], CLUSTER)]


def mask_kernel(slot_ref, ids_ref, bias_ref):
    for head in range(2):
        table = one_hot_rows(slot_ref[0, 0, head : head + 1, :])
        ids = jnp.dot(table, ids_ref[0], preferred_element_type=jnp.float32)
        turned = ids.T
        for at in range(0, TREE_LEN, CLUSTER):
            segs = turned[0:1, at : at + CLUSTER]
            block = ids[at : at + CLUSTER]
            allowed = (
                (segs == block[:, 0:1]) | (segs == block[:, 1:2]) | (segs == block[:, 2:3])
            )
            bias_ref[0, head, at : at + CLUSTER, :] = jnp.where(allowed, 0.0, -1e30).astype(
                jnp.bfloat16
            )


def attend_kernel(slot_ref, query_ref, key_ref, value_ref, bias_ref, ctx_ref, qk_ref, val_ref, p_ref):
    low = first_lanes(TREE_LEN)
    query = query_ref[...] * jnp.bfloat16(HEAD_DIM**-0.5)
    key = key_ref[...]
    value = value_ref[...]
    packed = (
        jnp.where(low, query, pltpu.roll(key, HEAD_DIM, 1)),
        jnp.where(low, pltpu.roll(query, HEAD_DIM, 1), key),
    )
    context = []
    for head in range(2):
        table = one_hot_rows(slot_ref[0, 0, head : head + 1, :])
        joined = jnp.concatenate([packed[head], value], axis=1)
        slots = jnp.dot(table, joined, preferred_element_type=jnp.float32).astype(jnp.bfloat16)
        both, values = slots[:, :LANES], slots[:, LANES:]
        qk_ref[0, head] = both
        val_ref[0, head] = values
        queries = jnp.where(low, both, jnp.bfloat16(0))
        keys = pltpu.roll(both, HEAD_DIM, 1)
        scores = jnp.concatenate(
            [contract_last(q, k) for q, k in zip(cluster_blocks(queries), cluster_blocks(keys))],
            axis=0,
        )
        scores = scores + bias_ref[0, head].astype(jnp.float32)
        numerator = jnp.exp(scores - jnp.max(scores, axis=1, keepdims=True))
        total = jnp.sum(numerator, axis=1, keepdims=True)
        soft = (numerator * (1.0 / total)).astype(jnp.bfloat16)
        p_ref[0, head] = soft
        out = jnp.concatenate(
            [
                jnp.dot(p, v, preferred_element_type=jnp.float32)
                for p, v in zip(cluster_blocks(soft), cluster_blocks(values))
            ],
            axis=0,
        ).astype(jnp.bfloat16)
        context.append(contract_first(table, out))
    ctx_ref[...] = jnp.where(low, context[0], context[1]).astype(jnp.bfloat16)


def attend_back_kernel(slot_ref, grad_ref, qk_ref, val_ref, p_ref, out_ref):
    low = first_lanes(TREE_LEN)
    grads = grad_ref[...]
    placed = []
    for head in range(2):
        table = one_hot_rows(slot_ref[0, 0, head : head + 1, :])
        slots = jnp.dot(table, grads, preferred_element_type=jnp.float32)
        slots = jnp.where(low == (head == 0), slots, 0.0).astype(jnp.bfloat16)
        both, values, soft = qk_ref[0, head], val_ref[0, head], p_ref[0, head]
        grad_soft = jnp.concatenate(
            [contract_last(g, v) for g, v in zip(cluster_blocks(slots), cluster_blocks(values))],
            axis=0,
        )
        grad_value = jnp.concatenate(
            [contract_first(p, g) for p, g in zip(cluster_blocks(soft), cluster_blocks(slots))],
            axis=0,
        ).astype(jnp.bfloat16)
        weights = soft.astype(jnp.float32)
        delta = jnp.sum(weights * grad_soft, axis=1, keepdims=True)
        grad_scores = (weights * (grad_soft - delta)).astype(jnp.bfloat16)
        pairs = list(zip(cluster_blocks(grad_scores), cluster_blocks(both)))
        by_key = jnp.concatenate([contract_first(s, b) for s, b in pairs], axis=0)
        by_query = jnp.concatenate(
            [jnp.dot(s, b, preferred_element_type=jnp.float32) for s, b in pairs], axis=0
        )
        mixed = jnp.where(low, by_key, by_query * HEAD_DIM**-0.5).astype(jnp.bfloat16)
        joined = jnp.concatenate([mixed, grad_value], axis=1)
        placed.append(contract_first(table, joined))
    first, second = placed
    out_ref[0] = jnp.where(
        low, pltpu.roll(first[:, :LANES], HEAD_DIM, 1), second[:, :LANES]
    ).astype(jnp.bfloat16)
    out_ref[1] = jnp.where(
        low, first[:, :LANES], pltpu.roll(second[:, :LANES], HEAD_DIM, 1)
    ).astype(jnp.bfloat16)
    out_ref[2] = jnp.where(low, first[:, LANES:], second[:, LANES:]).astype(jnp.bfloat16)


def slot_spec():
    return pl.BlockSpec((1, 1, 2, TREE_LEN), lambda tree, pair: (tree, pair, 0, 0))


def head_spec():
    return pl.BlockSpec((1, 2, TREE_LEN, LANES), lambda tree, pair: (tree, pair, 0, 0))


def column_spec(offset):
    return pl.BlockSpec((TREE_LEN, LANES), lambda tree, pair: (tree, offset + pair))


def kernel_params():
    return pltpu.CompilerParams(vmem_limit_bytes=KERNEL_VMEM)


def mask_bias(slots, ids):
    trees = slots.shape[0]
    return pl.pallas_call(
        mask_kernel,
        grid=(trees, PAIRS),
        in_specs=[
            slot_spec(),
            pl.BlockSpec((1, TREE_LEN, LANES), lambda tree, pair: (tree, 0, 0)),
        ],
        out_specs=head_spec(),
        out_shape=jax.ShapeDtypeStruct((trees, HEADS, TREE_LEN, LANES), jnp.bfloat16),
        compiler_params=kernel_params(),
        cost_estimate=pl.CostEstimate(
            flops=trees * 12_000_000_000, bytes_accessed=trees * 4_000_000, transcendentals=0
        ),
    )(slots, ids)


def attend(projected, slots, bias):
    trees = slots.shape[0]
    stored = jax.ShapeDtypeStruct((trees, HEADS, TREE_LEN, LANES), jnp.bfloat16)
    return pl.pallas_call(
        attend_kernel,
        grid=(trees, PAIRS),
        in_specs=[
            slot_spec(),
            column_spec(0),
            column_spec(PAIRS),
            column_spec(2 * PAIRS),
            head_spec(),
        ],
        out_specs=[column_spec(0), head_spec(), head_spec(), head_spec()],
        out_shape=[
            jax.ShapeDtypeStruct((trees * TREE_LEN, D), jnp.bfloat16),
            stored,
            stored,
            stored,
        ],
        compiler_params=kernel_params(),
        cost_estimate=pl.CostEstimate(
            flops=trees * 30_000_000_000, bytes_accessed=trees * 20_000_000, transcendentals=0
        ),
    )(slots, projected, projected, projected, bias)


def attend_back(grad_context, slots, kept):
    trees = slots.shape[0]
    return pl.pallas_call(
        attend_back_kernel,
        grid=(trees, PAIRS),
        in_specs=[slot_spec(), column_spec(0), head_spec(), head_spec(), head_spec()],
        out_specs=pl.BlockSpec((3, TREE_LEN, LANES), lambda tree, pair: (0, tree, pair)),
        out_shape=jax.ShapeDtypeStruct((3, trees * TREE_LEN, D), jnp.bfloat16),
        compiler_params=kernel_params(),
        cost_estimate=pl.CostEstimate(
            flops=trees * 40_000_000_000, bytes_accessed=trees * 20_000_000, transcendentals=0
        ),
    )(slots, grad_context, *kept)


def layer_forward(layer_in, weights, path_info):
    (
        qkv_weight,
        qv_bias,
        out_weight,
        out_bias,
        attn_gain,
        attn_shift,
        ffin_weight,
        ffin_bias,
        ffout_weight,
        ffout_bias,
        ffn_gain,
        ffn_shift,
    ) = weights
    layer_low = layer_in.astype(jnp.bfloat16)
    bias_float = qv_bias.astype(jnp.float32)
    full_bias = jnp.concatenate([bias_float[:D], jnp.zeros((D,), jnp.float32), bias_float[D:]])
    projected = (
        jnp.dot(layer_low, qkv_weight, preferred_element_type=jnp.float32) + full_bias
    ).astype(jnp.bfloat16)
    slots, bias = path_info
    context, *kept_heads = attend(projected, slots, bias)
    attn_sum = (
        layer_in
        + jnp.dot(context, out_weight, preferred_element_type=jnp.float32)
        + out_bias.astype(jnp.float32)
    )
    hidden_one = layer_norm(attn_sum, attn_gain.astype(jnp.float32), attn_shift.astype(jnp.float32))
    hidden_low = hidden_one.astype(jnp.bfloat16)
    pre_act = jnp.dot(
        hidden_low, ffin_weight, preferred_element_type=jnp.float32
    ) + ffin_bias.astype(jnp.float32)
    act_low = gelu_exact(pre_act).astype(jnp.bfloat16)
    ffn_sum = (
        hidden_one
        + jnp.dot(act_low, ffout_weight, preferred_element_type=jnp.float32)
        + ffout_bias.astype(jnp.float32)
    )
    result = layer_norm(ffn_sum, ffn_gain.astype(jnp.float32), ffn_shift.astype(jnp.float32))
    saved = (
        layer_low,
        kept_heads,
        context,
        attn_sum,
        hidden_low,
        pre_act,
        act_low,
        ffn_sum,
    )
    return (result, saved)


def layer_backward(grad_out, weights, saved, path_info, reduce):
    (
        qkv_weight,
        qv_bias,
        out_weight,
        out_bias,
        attn_gain,
        attn_shift,
        ffin_weight,
        ffin_bias,
        ffout_weight,
        ffout_bias,
        ffn_gain,
        ffn_shift,
    ) = weights
    (
        layer_low,
        kept_heads,
        context,
        attn_sum,
        hidden_low,
        pre_act,
        act_low,
        ffn_sum,
    ) = saved
    ignored, norm_pull = jax.vjp(
        layer_norm, ffn_sum, ffn_gain.astype(jnp.float32), ffn_shift.astype(jnp.float32)
    )
    grad_ffn_sum, grad_ffn_gain, grad_ffn_shift = norm_pull(grad_out)
    grad_down = grad_ffn_sum.astype(jnp.bfloat16)
    grad_ffout_weight = reduce(act_low, grad_down[None], False)
    grad_ffout_bias = jnp.sum(grad_down.astype(jnp.float32), axis=0)
    grad_act = dot_last(grad_down, ffout_weight)
    ignored, gelu_pull = jax.vjp(gelu_exact, pre_act)
    grad_pre = gelu_pull(grad_act)[0].astype(jnp.bfloat16)
    grad_ffin_weight = reduce(hidden_low, grad_pre[None], True)
    grad_ffin_bias = jnp.sum(grad_pre.astype(jnp.float32), axis=0)
    grad_hidden = grad_ffn_sum + dot_last(grad_pre, ffin_weight)
    ignored, first_pull = jax.vjp(
        layer_norm, attn_sum, attn_gain.astype(jnp.float32), attn_shift.astype(jnp.float32)
    )
    grad_attn_sum, grad_attn_gain, grad_attn_shift = first_pull(grad_hidden)
    grad_attn_low = grad_attn_sum.astype(jnp.bfloat16)
    grad_out_weight = reduce(context, grad_attn_low[None], False)
    grad_out_bias = jnp.sum(grad_attn_low.astype(jnp.float32), axis=0)
    grad_context = dot_last(grad_attn_low, out_weight).astype(jnp.bfloat16)
    grad_proj = attend_back(grad_context, path_info[0], kept_heads)
    grad_qkv_weight = reduce(layer_low, grad_proj, True)
    column_sums = jnp.sum(grad_proj.astype(jnp.float32), axis=1)
    grad_qv_bias = jnp.concatenate([column_sums[0], column_sums[2]])
    grad_in = grad_attn_sum
    for part in range(3):
        grad_in = grad_in + dot_last(grad_proj[part], qkv_weight[:, part * D : (part + 1) * D])
    grads = (
        grad_qkv_weight,
        grad_qv_bias,
        grad_out_weight,
        grad_out_bias,
        grad_attn_gain,
        grad_attn_shift,
        grad_ffin_weight,
        grad_ffin_bias,
        grad_ffout_weight,
        grad_ffout_bias,
        grad_ffn_gain,
        grad_ffn_shift,
    )
    return (grad_in, grads)


MATRICES = (0, 2, 6, 8)
VECTORS = (1, 3, 4, 5, 7, 9, 10, 11)
AXES = ("rep", "shard")
CHIPS_Z, CHIPS_X, CHIPS_Y, CORES = 4, 2, 2, 2


class Place:
    def __init__(self):
        rep = lax.axis_index("rep")
        shard = lax.axis_index("shard")
        self.y, self.core = rep // CORES, rep % CORES
        self.z, self.x = shard // CHIPS_X, shard % CHIPS_X


def hop(value, dz=0, dx=0, dy=0, dc=0):
    pairs = []
    for y in range(CHIPS_Y):
        for c in range(CORES):
            for z in range(CHIPS_Z):
                for x in range(CHIPS_X):
                    source = ((y * CORES + c) * CHIPS_Z + z) * CHIPS_X + x
                    y2, c2 = (y + dy) % CHIPS_Y, (c + dc) % CORES
                    z2, x2 = (z + dz) % CHIPS_Z, (x + dx) % CHIPS_X
                    pairs.append((source, ((y2 * CORES + c2) * CHIPS_Z + z2) * CHIPS_X + x2))
    return lax.ppermute(value, AXES, pairs)


def pick(array, index, axis):
    return lax.dynamic_index_in_dim(array, index, axis, keepdims=False)


def ordered(first, own, other, axis):
    return jnp.where(
        first, jnp.concatenate([own, other], axis), jnp.concatenate([other, own], axis)
    )


def place_kernel(split_y, half, count, *refs):
    pieces, out, sems = refs[:count], refs[count], refs[count + 1]
    rep = lax.axis_index("rep")
    shard = lax.axis_index("shard")
    y, core = rep // CORES, rep % CORES
    z, x = shard // CHIPS_X, shard % CHIPS_X
    copies = []
    for number, piece in enumerate(pieces):
        dc = number % CORES
        dx = number // CORES % CHIPS_X
        dy = number // (CORES * CHIPS_X)
        column = pl.multiple_of((core + dc) % CORES * half, 128)
        for dz in range(CHIPS_Z):
            owner = (z + CHIPS_Z - dz) % CHIPS_Z * CHIPS_X + (x + dx) % CHIPS_X
            row = (y + dy) % CHIPS_Y if split_y else 0
            copies.append(
                pltpu.make_async_copy(
                    piece.at[dz],
                    out.at[owner, row, :, pl.ds(column, half)],
                    sems.at[number * CHIPS_Z + dz],
                )
            )
    for copy in copies:
        copy.start()
    for copy in copies:
        copy.wait()


def gather_start(block):
    return [block] + [hop(block, dz=k) for k in range(1, CHIPS_Z)]


def gather_finish(parts, split_y):
    _, rows, half = parts[0].shape[0], parts[0].shape[0], parts[0].shape[1]
    stack = jnp.stack(parts)
    pieces = [stack, hop(stack, dx=1)]
    if split_y:
        pieces = pieces + [hop(piece, dy=1) for piece in pieces]
    pieces = [item for piece in pieces for item in (piece, hop(piece, dc=1))]
    splits = CHIPS_Y if split_y else 1
    count = len(pieces)
    whole = pl.pallas_call(
        lambda *refs: place_kernel(split_y, half, count, *refs),
        in_specs=[pl.BlockSpec(memory_space=pl.ANY)] * count,
        out_specs=pl.BlockSpec(memory_space=pl.ANY),
        out_shape=jax.ShapeDtypeStruct(
            (CHIPS_Z * CHIPS_X, splits, rows, 2 * half), jnp.bfloat16
        ),
        scratch_shapes=[pltpu.SemaphoreType.DMA((count * CHIPS_Z,))],
        cost_estimate=pl.CostEstimate(
            flops=0, bytes_accessed=4 * CHIPS_Z * count * rows * half, transcendentals=0
        ),
    )(*pieces)
    return whole.reshape(CHIPS_Z * CHIPS_X * splits * rows, 2 * half)


def gather_vectors(vectors, place):
    sizes = [vector.shape[1] for vector in vectors]
    own = jnp.concatenate(vectors, axis=1)
    layers, width = own.shape
    count = CHIPS_Z * CHIPS_X
    rounds = [
        hop(own, dz=dz, dx=dx) if dz or dx else own
        for dz in range(CHIPS_Z)
        for dx in range(CHIPS_X)
    ]
    stack = jnp.stack(rounds).astype(jnp.float32)
    wanted = jnp.arange(count, dtype=jnp.int32)
    behind = (place.z - wanted // CHIPS_X) % CHIPS_Z * CHIPS_X + (
        place.x - wanted % CHIPS_X
    ) % CHIPS_X
    turn = (behind[:, None] == wanted[None, :]).astype(jnp.float32)
    stack = jnp.sum(turn[:, :, None, None] * stack[None], axis=1)
    out, at = [], 0
    for size in sizes:
        out.append(
            stack[:, :, at : at + size].transpose(1, 0, 2).reshape(layers, count * size)
        )
        at += size
    return out


def gather_all(weights, place):
    vectors = gather_vectors([weights[number] for number in VECTORS], place)
    gathered = [[None] * 12 for _ in range(LAYERS)]
    previous = None
    for layer in range(LAYERS):
        for number in MATRICES:
            shard = weights[number][layer]
            rows, columns = shard.shape
            split_y = number in (6, 8)
            tall = rows // CHIPS_Y if split_y else rows
            block = lax.dynamic_slice(
                shard,
                (place.y * tall if split_y else 0, place.core * (columns // 2)),
                (tall, columns // 2),
            )
            if previous is not None:
                block, *_ = lax.optimization_barrier((block, *previous))
            parts = gather_start(block)
            previous = parts[1:]
            gathered[layer][number] = gather_finish(parts, split_y)
        for number, vector in zip(VECTORS, vectors):
            gathered[layer][number] = vector[layer]
    return gathered


def low_sum(*terms):
    total = terms[0].astype(jnp.float32)
    for term in terms[1:]:
        total = total + term.astype(jnp.float32)
    return total


def reduce_matrix(left, right, place, y_first):
    parts, _, columns = right.shape
    half = columns // 2
    depth = left.shape[1]

    def product(core):
        cut = lax.dynamic_slice_in_dim(right, core * half, half, axis=2)
        grads = [dot_first(left, cut[part]).astype(jnp.bfloat16) for part in range(parts)]
        return [
            grad.reshape(CHIPS_Z, CHIPS_X, CHIPS_Y, depth // 16, half) for grad in grads
        ]

    away = product(1 - place.core)
    arrived = [hop(part, dc=1) for part in away]
    kept = product(place.core)
    total = jnp.stack([low_sum(mine, other) for mine, other in zip(kept, arrived)], axis=0)

    def swap(values, index, axis, **step):
        sent = pick(values, 1 - index, axis).astype(jnp.bfloat16)
        return low_sum(pick(values, index, axis), hop(sent, **step))

    if y_first:
        total = swap(total, place.y, 3, dy=1)
    total = swap(total, place.x, 2, dx=1)
    landed = []
    for k in range(1, CHIPS_Z):
        sent = pick(total, (place.z + k) % CHIPS_Z, 1).astype(jnp.bfloat16)
        landed.append(hop(sent, dz=k))
    total = low_sum(pick(total, place.z, 1), *landed).astype(jnp.bfloat16)
    if y_first:
        rows = total[:, None]
        rows = ordered(place.y == 0, rows, hop(rows, dy=1), 1)
    else:
        rows = low_sum(total, hop(total, dy=1)).astype(jnp.bfloat16)
    rows = rows.reshape(parts, depth // 8, half)
    rows = ordered(place.core == 0, rows, hop(rows, dc=1), 2).astype(jnp.float32)
    return rows.transpose(1, 0, 2).reshape(depth // 8, parts * columns)


def reduce_vectors(vectors, place):
    sizes = [vector.shape[0] for vector in vectors]
    total = jnp.concatenate(vectors)
    for step in (dict(dc=1), dict(dy=1), dict(dx=1), dict(dz=2)):
        total = total + hop(total, **step)
    up, down = hop(total, dz=1), hop(total, dz=3)
    total = total + jnp.where(place.z % 2 == 0, down, up)
    count = CHIPS_Z * CHIPS_X
    shard = place.z * CHIPS_X + place.x
    out, at = [], 0
    for size in sizes:
        share = size // count
        out.append(lax.dynamic_slice_in_dim(total, at + shard * share, share))
        at += size
    return out


def local(
    fast,
    inputs,
    cotangent,
    segment,
    parent,
    clusters,
    qkv_weight,
    qv_bias,
    out_weight,
    out_bias,
    attn_gain,
    attn_shift,
    ffin_weight,
    ffin_bias,
    ffout_weight,
    ffout_bias,
    ffn_gain,
    ffn_shift,
):
    tree_count = parent.shape[0]
    segments = segment.reshape(tree_count, TREE_LEN)
    parents = jax.vmap(lookup_small)(segments, parent)
    grands = jax.vmap(lookup_small)(parents, parent)
    cluster_ids = clusters.reshape(HEADS, tree_count, TREE_LEN).transpose(1, 0, 2)
    slots = slot_ranks(cluster_ids).reshape(tree_count, PAIRS, 2, TREE_LEN)
    ids = jnp.stack([segments, parents, grands], axis=-1).astype(jnp.bfloat16)
    ids = jnp.pad(ids, ((0, 0), (0, 0), (0, LANES - 3)))
    path_info = (slots, mask_bias(slots, ids))
    weights = (
        qkv_weight,
        qv_bias,
        out_weight,
        out_bias,
        attn_gain,
        attn_shift,
        ffin_weight,
        ffin_bias,
        ffout_weight,
        ffout_bias,
        ffn_gain,
        ffn_shift,
    )
    if fast:
        place = Place()
        gathered = gather_all(weights, place)

        def reduce(left, right, y_first):
            return reduce_matrix(left, right, place, y_first)

    else:
        gathered = [
            [lax.all_gather(weight[layer], "shard", axis=0, tiled=True) for weight in weights]
            for layer in range(LAYERS)
        ]

        def reduce(left, right, y_first):
            grads = jnp.concatenate([dot_first(left, part) for part in right], axis=1)
            grads = lax.psum_scatter(grads, "shard", scatter_dimension=0, tiled=True)
            return lax.psum(grads.astype(jnp.bfloat16), "rep").astype(jnp.float32)

    hidden = inputs.astype(jnp.float32)
    kept_saved = []
    for layer_index in range(LAYERS):
        hidden, saved = layer_forward(hidden, gathered[layer_index], path_info)
        kept_saved.append(saved)
    result = hidden.astype(jnp.bfloat16)
    grad_rows = cotangent.astype(jnp.float32)
    per_layer = [None] * LAYERS
    for layer_index in reversed(range(LAYERS)):
        grad_rows, grads = layer_backward(
            grad_rows, gathered[layer_index], kept_saved[layer_index], path_info, reduce
        )
        per_layer[layer_index] = list(grads)
    order = [(layer, number) for layer in reversed(range(LAYERS)) for number in VECTORS]
    early = [item for item in order if item != (0, 1)]
    for items in (early, [(0, 1)]):
        vectors = [per_layer[layer][number] for layer, number in items]
        if fast:
            vectors = reduce_vectors(vectors, place)
        else:
            vectors = [
                lax.psum(lax.psum_scatter(vector, "shard", tiled=True), "rep")
                for vector in vectors
            ]
        for (layer, number), vector in zip(items, vectors):
            per_layer[layer][number] = vector
    stacked = tuple(
        (
            jnp.stack([per_layer[layer_index][member] for layer_index in range(LAYERS)])
            for member in range(12)
        )
    )
    return (
        result,
        grad_rows,
        stacked[0],
        stacked[1],
        stacked[2],
        stacked[3],
        stacked[4],
        stacked[5],
        stacked[6],
        stacked[7],
        stacked[8],
        stacked[9],
        stacked[10],
        stacked[11],
    )


def solution(mesh):
    in_specs = (
        P(("rep", "shard"), None),
        P(("rep", "shard"), None),
        P(("rep", "shard")),
        P(("rep", "shard"), None),
        P(None, ("rep", "shard")),
        P(None, "shard", None),
        P(None, "shard"),
        P(None, "shard", None),
        P(None, "shard"),
        P(None, "shard"),
        P(None, "shard"),
        P(None, "shard", None),
        P(None, "shard"),
        P(None, "shard", None),
        P(None, "shard"),
        P(None, "shard"),
        P(None, "shard"),
    )
    out_specs = (
        P(("rep", "shard"), None),
        P(("rep", "shard"), None),
        P(None, "shard", None),
        P(None, "shard"),
        P(None, "shard", None),
        P(None, "shard"),
        P(None, "shard"),
        P(None, "shard"),
        P(None, "shard", None),
        P(None, "shard"),
        P(None, "shard", None),
        P(None, "shard"),
        P(None, "shard"),
        P(None, "shard"),
    )
    fast = mesh.shape["rep"] == CHIPS_Y * CORES and mesh.shape["shard"] == CHIPS_Z * CHIPS_X
    return jax.shard_map(
        functools.partial(local, fast),
        mesh=mesh,
        in_specs=in_specs,
        out_specs=out_specs,
        check_vma=False,
    )
```

time: 2220 us -> 1840 us (0.83)
  Pallas kernels: 0 us -> 1020 us
  waiting for transfers between devices: 1040 us -> 216 us
  matrix products: 497 us -> 257 us
  local copies, waits for them, and re-layouts: 291 us -> 81.5 us
  starting transfers between devices: 1.6 us -> 170 us
  blocking collectives: 141 us -> 0 us
  other arithmetic: 209 us -> 73.7 us
    pallas_call x0 -> x13, Pallas kernels: none -> 1020 us  [the longest x8 868 us: gather_finish(): pl.pallas_call(lambda *refs: place_kernel(split_y, half, count, *refs), i...]
    reduce_scatter x10 -> x0, waiting for transfers between devices: 794 us -> none  [the longest x2 312 us: local(): lax.psum_scatter(grads[8], 'shard', scatter_dimension=0, tiled=True)]
    unnamed x32 -> x0, waiting for transfers between devices: 220 us -> none
    ppermute x0 -> x147, waiting for transfers between devices: none -> 216 us  [hop(): return lax.ppermute(value, AXES, pairs)]
    ppermute x0 -> x147, starting transfers between devices: none -> 170 us  [hop(): return lax.ppermute(value, AXES, pairs)]
    dot_general x240 -> x1, matrix products: 155 us -> 0.48 us  [slot_ranks(): jnp.dot(member.astype(jnp.bfloat16), triangle, preferred_element_type=jnp...]
    another operation x144 -> x20, other arithmetic: 136 us -> 16.6 us  [the longest x8 13.4 us: gather_finish(): stack = jnp.stack(parts)]
    all_gather x10 -> x0, blocking collectives: 104 us -> none  [the longest x2 45.7 us: local(): lax.all_gather(ffin_bias[layer_index], 'shard', axis=0, tiled=True)]
  transfers between devices with their start and end apart: 25 -> 147, of which waited for: 16 -> 51; matrix products, arithmetic and copies ran while one was open for 35% -> 13% of each run, Pallas kernels for 0% -> 44%
where the time goes in v1:
time: 1840 us; the launch traced here: 1820 us
  Pallas kernels  1020 us (55%)
  matrix products  257 us (14%)
  waiting for transfers between devices  216 us (12%)
  starting transfers between devices  170 us (9%)
  local copies, waits for them, and re-layouts  81.5 us (4%)
  other arithmetic  73.7 us (4%)
    pallas_call x8, Pallas kernels, gather_finish(): pl.pallas_call(lambda *refs: place_kernel(split_y, half, count, *refs), i...  868 us
    ppermute x147, waiting for transfers between devices, hop(): return lax.ppermute(value, AXES, pairs)  216 us
    ppermute x147, starting transfers between devices, hop(): return lax.ppermute(value, AXES, pairs)  170 us
    dot_general x12, matrix products, dot_last(): lax.dot_general(left_side, right_side, (((1,), (1,)), ((), ())), preferre...  75.9 us
    dot_general x2, matrix products, layer_forward(): jnp.dot(hidden_low, ffin_weight, preferred_element_type=jnp.float32)  72.7 us
    pallas_call x2, Pallas kernels, attend_back(): pl.pallas_call(attend_back_kernel, grid=(trees, PAIRS), in_specs=[slot_sp...  67.5 us
    pallas_call x2, Pallas kernels, attend(): pl.pallas_call(attend_kernel, grid=(trees, PAIRS), in_specs=[slot_spec(),...  66.9 us
    dot_general x24, matrix products, dot_first(): lax.dot_general(left_side, right_side, (((0,), (0,)), ((), ())), preferre...  65.9 us
  transfers between devices with their start and end apart: 147, of which 51 were waited for; matrix products, arithmetic and copies ran while one was open for 13% of the time, Pallas kernels for 44%

profile of v1, /device:TPU:17, one launch (start us, length us, event | category | flops | bytes accessed | tf_op | source)
XLA Modules:
  0.0 1821.7 jit_solution(1357791325165791059)
XLA Ops:
  26.3 16.9 shard_map.273.bias_ref
  56.8 10.6 collective-permute-done.1
  67.4 4.8 collective-permute-done.2
  72.1 4.0 collective-permute-start.14
  87.3 6.3 collective-permute-done.20
  103.1 4.6 collective-permute-done.30
  118.5 9.9 collective-permute-done.40
  128.5 4.7 collective-permute-done.41
  172.1 4.0 collective-permute-done.62
  178.6 37.0 %shard_map.275 = bf16[8,1,96,768]{3,2,1,0:T(8,128)(2,1)} custom-call(bf16[4,96,384]{2,1,0:T(8,128)(2,1)} %copy-done.43, bf16[4,96,384]{2,1,0:T(8,128)(2,1)} %collective-permute-done.16.refs_1_, bf16[4,96,384]{2,1,0:T(8,128)(2,1)} %copy-done.70, bf16[4,96,384]{2,1,0:T(8,128)(2,1)} %copy-done.71), custom_call_target="tpu_custom_call" | custom-call | bytes 2359296 | tf_op jit(solution)/shard_map/pallas_call | solution.py:463
  222.8 37.0 %shard_map.280 = bf16[8,1,96,768]{3,2,1,0:T(8,128)(2,1)} custom-call(bf16[4,96,384]{2,1,0:T(8,128)(2,1)} %pad_maximum_fusion.9.refs_0_, bf16[4,96,384]{2,1,0:T(8,128)(2,1)} %copy-done.72, bf16[4,96,384]{2,1,0:T(8,128)(2,1)} %collective-permute-done.49.refs_2_, bf16[4,96,384]{2,1,0:T(8,128)(2,1)} %collective-permute-done.50.refs_3_), custom_call_target="tpu_custom_call" | custom-call | bytes 2359296 | tf_op jit(solution)/shard_map/pallas_call | solution.py:463
  262.6 108.5 %shard_map.272 = bf16[8,1,96,2304]{3,2,1,0:T(8,128)(2,1)} custom-call(bf16[4,96,1152]{2,1,0:T(8,128)(2,1)} %copy-done.23, bf16[4,96,1152]{2,1,0:T(8,128)(2,1)} %collective-permute-done.3.refs_1_, bf16[4,96,1152]{2,1,0:T(8,128)(2,1)} %collective-permute-done.4.refs_2_, bf16[4,96,1152]{2,1,0:T(8,128)(2,1)} %collective-permute-done.5.refs_3_), custom_call_target="tpu_custom_call" | custom-call | bytes 7077888 | tf_op jit(solution)/shard_map/pallas_call | solution.py:463
  371.0 7.4 fusion.12.query_ref.key_ref.value_ref
  378.4 33.5 %shard_map.274 = (bf16[1024,768]{1,0:T(8,128)(2,1)}, bf16[1,12,1024,128]{3,2,1,0:T(8,128)(2,1)}, bf16[1,12,1024,128]{3,2,1,0:T(8,128)(2,1)}, bf16[1,12,1024,128]{3,2,1,0:T(8,128)(2,1)}) custom-call(s32[1,6,2,1024]{3,2,1,0:T(2,128)} %reshape.1519.slot_ref, bf16[1024,2304]{1,0:T(8,128)(2,1)} %fusion.12.query_ref.key_ref.value_ref, ...), custom_call_target="tpu_custom_call" | custom-call | flops 30000001024 | bytes 20000000 | tf_op jit(solution)/shard_map/pallas_call | solution.py:223
  419.4 11.5 collective-permute-done.37.refs_6_
  433.1 144.3 %shard_map.276 = bf16[8,2,48,3072]{3,2,1,0:T(8,128)(2,1)} custom-call(bf16[4,48,1536]{2,1,0:T(8,128)(2,1)} %pad_maximum_fusion.4.refs_0_, bf16[4,48,1536]{2,1,0:T(8,128)(2,1)} %collective-permute-done.22.refs_1_, bf16[4,48,1536]{2,1,0:T(8,128)(2,1)} %collective-permute-done.23.refs_2_, bf16[4,48,1536]{2,1,0:T(8,128)(2,1)} %copy-done.50, ...), custom_call_target="tpu_custom_call" | custom-call | bytes 9437184 | tf_op jit(solution)/shard_map/pallas_call | solution.py:463
  577.5 36.5 %multiply_convert_fusion.1 = (bf16[1024,3072]{1,0:T(8,128)(2,1)}, f32[1024,3072]{1,0:T(8,128)}, f32[1024,3072]{1,0:T(8,128)}) fusion(f32[3072]{0:T(1024)S(1)} %bitcast.574, bf16[1024,768]{0,1:T(8,128)(2,1)S(1)} %fusion.24, bf16[768,3072]{1,0:T(8,128)(2,1)} %bitcast.500), kind=kOutput, calls=%fused_computation.21 | convolution fusion | flops 5039456256 | bytes 37761024 | tf_op jit(solution)/shard_map/dot_general | solution.py:292
  615.9 144.3 %shard_map.277 = bf16[8,2,192,768]{3,2,1,0:T(8,128)(2,1)} custom-call(bf16[4,192,384]{2,1,0:T(8,128)(2,1)} %copy-done.24, bf16[4,192,384]{2,1,0:T(8,128)(2,1)} %collective-permute-done.32.refs_1_, bf16[4,192,384]{2,1,0:T(8,128)(2,1)} %collective-permute-done.33.refs_2_, bf16[4,192,384]{2,1,0:T(8,128)(2,1)} %collective-permute-done.34.refs_3_, ...), custom_call_target="tpu_custom_call" | custom-call | bytes 9437184 | tf_op jit(solution)/shard_map/pallas_call | solution.py:463
  760.3 9.8 fusion.198
  775.5 108.5 %shard_map.278 = bf16[8,1,96,2304]{3,2,1,0:T(8,128)(2,1)} custom-call(bf16[4,96,1152]{2,1,0:T(8,128)(2,1)} %pad_maximum_fusion.3.refs_0_, bf16[4,96,1152]{2,1,0:T(8,128)(2,1)} %collective-permute-done.42.refs_1_, bf16[4,96,1152]{2,1,0:T(8,128)(2,1)} %collective-permute-done.43.refs_2_, bf16[4,96,1152]{2,1,0:T(8,128)(2,1)} %collective-permute-done.44.refs_3_), custom_call_target="tpu_custom_call" | custom-call | bytes 7077888 | tf_op jit(solution)/shard_map/pallas_call | solution.py:463
  884.0 8.6 add_convert_fusion.2.query_ref.key_ref.value_ref
  892.6 33.4 %shard_map.279 = (bf16[1024,768]{1,0:T(8,128)(2,1)}, bf16[1,12,1024,128]{3,2,1,0:T(8,128)(2,1)}, bf16[1,12,1024,128]{3,2,1,0:T(8,128)(2,1)}, bf16[1,12,1024,128]{3,2,1,0:T(8,128)(2,1)}) custom-call(s32[1,6,2,1024]{3,2,1,0:T(2,128)} %reshape.1519.slot_ref, bf16[1024,2304]{1,0:T(8,128)(2,1)} %add_convert_fusion.2.query_ref.key_ref.value_ref, ...), custom_call_target="tpu_custom_call" | custom-call | flops 30000001024 | bytes 20000000 | tf_op jit(solution)/shard_map/pallas_call | solution.py:223
  926.0 3.9 fusion.199
  935.4 10.8 collective-permute-done.69.refs_6_
  948.4 144.3 %shard_map.281 = bf16[8,2,48,3072]{3,2,1,0:T(8,128)(2,1)} custom-call(bf16[4,48,1536]{2,1,0:T(8,128)(2,1)} %pad_maximum_fusion.6.refs_0_, bf16[4,48,1536]{2,1,0:T(8,128)(2,1)} %collective-permute-done.54.refs_1_, bf16[4,48,1536]{2,1,0:T(8,128)(2,1)} %collective-permute-done.55.refs_2_, bf16[4,48,1536]{2,1,0:T(8,128)(2,1)} %copy-done.51, ...), custom_call_target="tpu_custom_call" | custom-call | bytes 9437184 | tf_op jit(solution)/shard_map/pallas_call | solution.py:463
  1092.7 36.3 %multiply_convert_fusion = (bf16[1024,3072]{1,0:T(8,128)(2,1)}, f32[1024,3072]{1,0:T(8,128)}, f32[1024,3072]{1,0:T(8,128)}) fusion(f32[3072]{0:T(1024)S(1)} %bitcast.576, bf16[1024,768]{0,1:T(8,128)(2,1)S(1)} %fusion.26, bf16[768,3072]{1,0:T(8,128)(2,1)} %bitcast.504), kind=kOutput, calls=%fused_computation.8 | convolution fusion | flops 5039456256 | bytes 37761024 | tf_op jit(solution)/shard_map/dot_general | solution.py:292
  1129.0 144.4 %shard_map.282 = bf16[8,2,192,768]{3,2,1,0:T(8,128)(2,1)} custom-call(bf16[4,192,384]{2,1,0:T(8,128)(2,1)} %pad_maximum_fusion.7.refs_0_, bf16[4,192,384]{2,1,0:T(8,128)(2,1)} %collective-permute-done.64.refs_1_, bf16[4,192,384]{2,1,0:T(8,128)(2,1)} %collective-permute-done.65.refs_2_, bf16[4,192,384]{2,1,0:T(8,128)(2,1)} %collective-permute-done.66.refs_3_, ...), custom_call_target="tpu_custom_call" | custom-call | bytes 9437184 | tf_op jit(solution)/shard_map/pallas_call | solution.py:463
  1273.4 9.0 fusion.200
  1286.5 3.8 convert_reduce_fusion.7
  1290.3 19.0 %convert_reduce_fusion.1 = (f32[3072]{0:T(1024)}, bf16[1024,3072]{1,0:T(8,128)(2,1)}) fusion(f32[1024,3072]{1,0:T(8,128)} %get-tuple-element.275, bf16[1024,768]{0,1:T(8,128)(2,1)} %get-tuple-element.265, bf16[3072,768]{1,0:T(8,128)(2,1)} %bitcast.507, f32[1024,3072]{1,0:T(8,128)} %get-tuple-element.344, f32[3072]{0:T(1024)S(1)} %bitcast.577), kind=kOutput, calls=%fused_computation.5 | convolution fusion | flops 4885312512 | bytes 37773312 | tf_op jit(solution)/shard_map/dot_general | solution.py:39
  1309.3 11.0 multiply_reduce_fusion.2
  1325.9 34.0 %shard_map.283 = bf16[3,1024,768]{2,1,0:T(8,128)(2,1)} custom-call(s32[1,6,2,1024]{3,2,1,0:T(2,128)} %reshape.1519.slot_ref, bf16[1024,768]{1,0:T(8,128)(2,1)} %convolution_convert_fusion.9.grad_ref, bf16[1,12,1024,128]{3,2,1,0:T(8,128)(2,1)} %get-tuple-element.38.qk_ref, bf16[1,12,1024,128]{3,2,1,0:T(8,128)(2,1)} %get-tuple-element.39.val_ref, ...), custom_call_target="tpu_custom_call" | custom-call | flops 40000000000 | bytes 20000000 | tf_op jit(solution)/shard_map/pallas_call | solution.py:249
  1359.9 3.8 convert_reduce_fusion.2
  1374.3 5.0 convolution_convert_fusion.3
  1379.2 4.8 convolution_convert_fusion.2
  1384.1 4.8 convolution_convert_fusion
  1388.9 4.8 convolution_convert_fusion.1
  1393.7 18.7 %convert_reduce_fusion = (f32[3072]{0:T(1024)S(1)}, bf16[1024,3072]{1,0:T(8,128)(2,1)}) fusion(f32[1024,3072]{1,0:T(8,128)} %get-tuple-element.277, bf16[1024,768]{0,1:T(8,128)(2,1)} %copy-done.42, bf16[3072,768]{1,0:T(8,128)(2,1)} %bitcast.503, f32[1024,3072]{1,0:T(8,128)} %get-tuple-element.339, f32[3072]{0:T(1024)S(1)} %bitcast.575), kind=kOutput, calls=%fused_computation.4 | convolution fusion | flops 4885312512 | bytes 37773312 | tf_op jit(solution)/shard_map/dot_general | solution.py:39
  1412.5 9.9 multiply_reduce_fusion.1
  1422.4 4.0 convolution_convert_fusion.7
  1426.4 3.9 convolution_convert_fusion.6
  1430.4 3.9 convolution_convert_fusion.4
  1434.2 4.2 convolution_convert_fusion.5
  1450.8 33.5 %shard_map.284 = bf16[3,1024,768]{2,1,0:T(8,128)(2,1)} custom-call(s32[1,6,2,1024]{3,2,1,0:T(2,128)} %reshape.1519.slot_ref, bf16[1024,768]{1,0:T(8,128)(2,1)} %convolution_convert_fusion.8.grad_ref, bf16[1,12,1024,128]{3,2,1,0:T(8,128)(2,1)} %get-tuple-element.41.qk_ref, bf16[1,12,1024,128]{3,2,1,0:T(8,128)(2,1)} %get-tuple-element.42.val_ref, ...), custom_call_target="tpu_custom_call" | custom-call | flops 40000000000 | bytes 20000000 | tf_op jit(solution)/shard_map/pallas_call | solution.py:249
  1519.5 3.7 collective-permute-start.94
  1575.7 4.1 collective-permute-done.104
  1581.8 4.3 collective-permute-done.111
  1596.8 17.9 collective-permute-done.108
  1617.9 4.0 collective-permute-start.109
  1629.0 6.3 collective-permute-done.75
  1638.9 5.9 collective-permute-done.85
  1644.8 3.5 collective-permute-start.77
  1653.0 4.6 collective-permute-start.86
  1660.1 4.9 collective-permute-done.87
  1677.7 4.4 convert_add_fusion.1
  1702.0 10.5 collective-permute-done.134
  1714.9 3.9 collective-permute-start.135
  1718.8 19.0 %collective-permute-done.141 = bf16[1,4,2,192,384]{4,3,2,1,0:T(8,128)(2,1)} collective-permute-done((bf16[1,4,2,192,384]{4,3,2,1,0:T(8,128)(2,1)}, bf16[1,4,2,192,384]{4,3,2,1,0:T(8,128)(2,1)}, u32[]{:S(2)}, u32[]{:S(2)}) %collective-permute-start.141) | collective-permute-done | bytes 1179680 | tf_op jit(solution)/shard_map/ppermute | solution.py:409
  1753.9 3.5 collective-permute-done.142
  1757.5 8.2 collective-permute-done.143
  1765.7 6.3 collective-permute-done.144
  1782.0 4.9 collective-permute-start.120
  1796.9 3.6 collective-permute-start.129
  1800.5 5.5 collective-permute-done.122
  (854 shorter events, 384.9 us)
Async XLA Ops:
  1.7 44.8 %collective-permute-start.6 = (bf16[2,1152]{1,0:T(2,128)(2,1)S(1)}, bf16[2,1152]{1,0:T(2,128)(2,1)}, u32[]{:S(2)}, u32[]{:S(2)}) collective-permute-start(bf16[2,1152]{1,0:T(2,128)(2,1)S(1)} %concatenate.220), channel_id=1, source_target_pairs={{0,1},{1,0},{2,3},{3,2},{4,5},{5,4},{6,7},{7,6},{8,9},{9,8},{10,11... | collective-permute-start | bytes 13832 | tf_op jit(solution)/shard_map/ppermute | solution.py:409
  3.0 45.0 %collective-permute-start.7 = (bf16[2,1152]{1,0:T(2,128)(2,1)S(1)}, bf16[2,1152]{1,0:T(2,128)(2,1)}, u32[]{:S(2)}, u32[]{:S(2)}) collective-permute-start(bf16[2,1152]{1,0:T(2,128)(2,1)S(1)} %concatenate.220), channel_id=1, source_target_pairs={{0,2},{1,3},{2,4},{3,5},{4,6},{5,7},{6,0},{7,1},{8,10},{9,11},{10,... | collective-permute-start | bytes 13832 | tf_op jit(solution)/shard_map/ppermute | solution.py:409
  4.3 45.3 %collective-permute-start.8 = (bf16[2,1152]{1,0:T(2,128)(2,1)S(1)}, bf16[2,1152]{1,0:T(2,128)(2,1)}, u32[]{:S(2)}, u32[]{:S(2)}) collective-permute-start(bf16[2,1152]{1,0:T(2,128)(2,1)S(1)} %concatenate.220), channel_id=1, source_target_pairs={{0,3},{1,2},{2,5},{3,4},{4,7},{5,6},{6,1},{7,0},{8,11},{9,10},{10,... | collective-permute-start | bytes 13832 | tf_op jit(solution)/shard_map/ppermute | solution.py:409
  4.3 47.3 %collective-permute-start.9 = (bf16[2,1152]{1,0:T(2,128)(2,1)S(1)}, bf16[2,1152]{1,0:T(2,128)(2,1)}, u32[]{:S(2)}, u32[]{:S(2)}) collective-permute-start(bf16[2,1152]{1,0:T(2,128)(2,1)S(1)} %concatenate.220), channel_id=1, source_target_pairs={{0,4},{1,5},{2,6},{3,7},{4,0},{5,1},{6,2},{7,3},{8,12},{9,13},{10,... | collective-permute-start | bytes 13832 | tf_op jit(solution)/shard_map/ppermute | solution.py:409
  5.6 48.6 %collective-permute-start.10 = (bf16[2,1152]{1,0:T(2,128)(2,1)S(1)}, bf16[2,1152]{1,0:T(2,128)(2,1)}, u32[]{:S(2)}, u32[]{:S(2)}) collective-permute-start(bf16[2,1152]{1,0:T(2,128)(2,1)S(1)} %concatenate.220), channel_id=1, source_target_pairs={{0,5},{1,4},{2,7},{3,6},{4,1},{5,0},{6,3},{7,2},{8,13},{9,12},{10,... | collective-permute-start | bytes 13832 | tf_op jit(solution)/shard_map/ppermute | solution.py:409
  54.2 17.9 collective-permute-start.2
  86.0 73.9 %collective-permute-start.4 = (bf16[4,96,1152]{2,1,0:T(8,128)(2,1)S(1)}, bf16[4,96,1152]{2,1,0:T(8,128)(2,1)}, u32[]{:S(2)}, u32[]{:S(2)}) collective-permute-start(bf16[4,96,1152]{2,1,0:T(8,128)(2,1)S(1)} %pad_maximum_fusion.2.refs_0_), channel_id=1, source_target_pairs={{0,1},{1,0},{2,3},{3,2},{4,5},{5,4},{6,7},{7,6},{8,9},{9,8},{10,11... | collective-permute-start | bytes 2654216 | tf_op jit(solution)/shard_map/ppermute | solution.py:409
  114.2 19.0 %collective-permute-start.41 = (bf16[96,1152]{1,0:T(8,128)(2,1)}, bf16[96,1152]{1,0:T(8,128)(2,1)S(1)}, u32[]{:S(2)}, u32[]{:S(2)}) collective-permute-start(bf16[96,1152]{1,0:T(8,128)(2,1)} %dynamic-slice_bitcast_fusion.24), channel_id=1, source_target_pairs={{0,6},{1,7},{2,0},{3,1},{4,2},{5,3},{6,4},{7,5},{8,14},{9,15},{10,... | collective-permute-start | bytes 663560 | tf_op jit(solution)/shard_map/ppermute | solution.py:409
  116.6 41.9 %collective-permute-start.17 = (bf16[4,96,384]{2,1,0:T(8,128)(2,1)S(1)}, bf16[4,96,384]{2,1,0:T(8,128)(2,1)S(1)}, u32[]{:S(2)}, u32[]{:S(2)}) collective-permute-start(bf16[4,96,384]{2,1,0:T(8,128)(2,1)S(1)} %pad_maximum_fusion.8.refs_0_), channel_id=1, source_target_pairs={{0,1},{1,0},{2,3},{3,2},{4,5},{5,4},{6,7},{7,6},{8,9},{9,8},{10,11... | collective-permute-start | bytes 884744 | tf_op jit(solution)/shard_map/ppermute | solution.py:409
  145.1 20.9 %collective-permute-start.16 = (bf16[4,96,384]{2,1,0:T(8,128)(2,1)S(1)}, bf16[4,96,384]{2,1,0:T(8,128)(2,1)}, u32[]{:S(2)}, u32[]{:S(2)}) collective-permute-start(bf16[4,96,384]{2,1,0:T(8,128)(2,1)S(1)} %pad_maximum_fusion.8.refs_0_), channel_id=1, source_target_pairs={{0,8},{1,9},{2,10},{3,11},{4,12},{5,13},{6,14},{7,15},{8,0},{9,1},... | collective-permute-start | bytes 884744 | tf_op jit(solution)/shard_map/ppermute | solution.py:409
  158.5 102.6 %collective-permute-start.3 = (bf16[4,96,1152]{2,1,0:T(8,128)(2,1)S(1)}, bf16[4,96,1152]{2,1,0:T(8,128)(2,1)}, u32[]{:S(2)}, u32[]{:S(2)}) collective-permute-start(bf16[4,96,1152]{2,1,0:T(8,128)(2,1)S(1)} %pad_maximum_fusion.2.refs_0_), channel_id=1, source_target_pairs={{0,8},{1,9},{2,10},{3,11},{4,12},{5,13},{6,14},{7,15},{8,0},{9,1},... | collective-permute-start | bytes 2654216 | tf_op jit(solution)/shard_map/ppermute | solution.py:409
  159.9 101.4 %collective-permute-start.5 = (bf16[4,96,1152]{2,1,0:T(8,128)(2,1)}, bf16[4,96,1152]{2,1,0:T(8,128)(2,1)}, u32[]{:S(2)}, u32[]{:S(2)}) collective-permute-start(bf16[4,96,1152]{2,1,0:T(8,128)(2,1)} %collective-permute-done.4.refs_2_), channel_id=1, source_target_pairs={{0,8},{1,9},{2,10},{3,11},{4,12},{5,13},{6,14},{7,15},{8,0},{9,1},... | collective-permute-start | bytes 2654216 | tf_op jit(solution)/shard_map/ppermute | solution.py:409
  168.2 48.5 %collective-permute-start.49 = (bf16[4,96,384]{2,1,0:T(8,128)(2,1)}, bf16[4,96,384]{2,1,0:T(8,128)(2,1)}, u32[]{:S(2)}, u32[]{:S(2)}) collective-permute-start(bf16[4,96,384]{2,1,0:T(8,128)(2,1)} %pad_maximum_fusion.9.refs_0_), channel_id=1, source_target_pairs={{0,1},{1,0},{2,3},{3,2},{4,5},{5,4},{6,7},{7,6},{8,9},{9,8},{10,11... | collective-permute-start | bytes 884744 | tf_op jit(solution)/shard_map/ppermute | solution.py:409
  171.4 88.4 %collective-permute-start.23 = (bf16[4,48,1536]{2,1,0:T(8,128)(2,1)}, bf16[4,48,1536]{2,1,0:T(8,128)(2,1)}, u32[]{:S(2)}, u32[]{:S(2)}) collective-permute-start(bf16[4,48,1536]{2,1,0:T(8,128)(2,1)} %pad_maximum_fusion.4.refs_0_), channel_id=1, source_target_pairs={{0,1},{1,0},{2,3},{3,2},{4,5},{5,4},{6,7},{7,6},{8,9},{9,8},{10,11... | collective-permute-start | bytes 1769480 | tf_op jit(solution)/shard_map/ppermute | solution.py:409
  176.1 39.5 %collective-permute-start.63 = (bf16[192,384]{1,0:T(8,128)(2,1)}, bf16[192,384]{1,0:T(8,128)(2,1)}, u32[]{:S(2)}, u32[]{:S(2)}) collective-permute-start(bf16[192,384]{1,0:T(8,128)(2,1)} %dynamic-slice_bitcast_fusion.25), channel_id=1, source_target_pairs={{0,6},{1,7},{2,0},{3,1},{4,2},{5,3},{6,4},{7,5},{8,14},{9,15},{10,... | collective-permute-start | bytes 442376 | tf_op jit(solution)/shard_map/ppermute | solution.py:409
  220.8 194.2 %collective-permute-start.25 = (bf16[4,48,1536]{2,1,0:T(8,128)(2,1)}, bf16[4,48,1536]{2,1,0:T(8,128)(2,1)}, u32[]{:S(2)}, u32[]{:S(2)}) collective-permute-start(bf16[4,48,1536]{2,1,0:T(8,128)(2,1)} %pad_maximum_fusion.4.refs_0_), channel_id=1, source_target_pairs={{0,16},{1,17},{2,18},{3,19},{4,20},{5,21},{6,22},{7,23},{8,24},{9,... | collective-permute-start | bytes 1769480 | tf_op jit(solution)/shard_map/ppermute | solution.py:409
  222.1 193.9 %collective-permute-start.22 = (bf16[4,48,1536]{2,1,0:T(8,128)(2,1)}, bf16[4,48,1536]{2,1,0:T(8,128)(2,1)}, u32[]{:S(2)}, u32[]{:S(2)}) collective-permute-start(bf16[4,48,1536]{2,1,0:T(8,128)(2,1)} %pad_maximum_fusion.4.refs_0_), channel_id=1, source_target_pairs={{0,8},{1,9},{2,10},{3,11},{4,12},{5,13},{6,14},{7,15},{8,0},{9,1},... | collective-permute-start | bytes 1769480 | tf_op jit(solution)/shard_map/ppermute | solution.py:409
  259.8 156.3 %collective-permute-start.33 = (bf16[4,192,384]{2,1,0:T(8,128)(2,1)S(1)}, bf16[4,192,384]{2,1,0:T(8,128)(2,1)}, u32[]{:S(2)}, u32[]{:S(2)}) collective-permute-start(bf16[4,192,384]{2,1,0:T(8,128)(2,1)S(1)} %pad_maximum_fusion.5.refs_0_), channel_id=1, source_target_pairs={{0,1},{1,0},{2,3},{3,2},{4,5},{5,4},{6,7},{7,6},{8,9},{9,8},{10,11... | collective-permute-start | bytes 1769480 | tf_op jit(solution)/shard_map/ppermute | solution.py:409
  261.1 157.1 %collective-permute-start.35 = (bf16[4,192,384]{2,1,0:T(8,128)(2,1)S(1)}, bf16[4,192,384]{2,1,0:T(8,128)(2,1)}, u32[]{:S(2)}, u32[]{:S(2)}) collective-permute-start(bf16[4,192,384]{2,1,0:T(8,128)(2,1)S(1)} %pad_maximum_fusion.5.refs_0_), channel_id=1, source_target_pairs={{0,16},{1,17},{2,18},{3,19},{4,20},{5,21},{6,22},{7,23},{8,24},{9,... | collective-permute-start | bytes 1769480 | tf_op jit(solution)/shard_map/ppermute | solution.py:409
  261.3 155.2 %collective-permute-start.27 = (bf16[4,48,1536]{2,1,0:T(8,128)(2,1)}, bf16[4,48,1536]{2,1,0:T(8,128)(2,1)}, u32[]{:S(2)}, u32[]{:S(2)}) collective-permute-start(bf16[4,48,1536]{2,1,0:T(8,128)(2,1)} %collective-permute-done.23.refs_2_), channel_id=1, source_target_pairs={{0,16},{1,17},{2,18},{3,19},{4,20},{5,21},{6,22},{7,23},{8,24},{9,... | collective-permute-start | bytes 1769480 | tf_op jit(solution)/shard_map/ppermute | solution.py:409
  418.2 195.8 %collective-permute-start.32 = (bf16[4,192,384]{2,1,0:T(8,128)(2,1)S(1)}, bf16[4,192,384]{2,1,0:T(8,128)(2,1)}, u32[]{:S(2)}, u32[]{:S(2)}) collective-permute-start(bf16[4,192,384]{2,1,0:T(8,128)(2,1)S(1)} %pad_maximum_fusion.5.refs_0_), channel_id=1, source_target_pairs={{0,8},{1,9},{2,10},{3,11},{4,12},{5,13},{6,14},{7,15},{8,0},{9,1},... | collective-permute-start | bytes 1769480 | tf_op jit(solution)/shard_map/ppermute | solution.py:409
  418.3 196.0 %collective-permute-start.43 = (bf16[4,96,1152]{2,1,0:T(8,128)(2,1)}, bf16[4,96,1152]{2,1,0:T(8,128)(2,1)}, u32[]{:S(2)}, u32[]{:S(2)}) collective-permute-start(bf16[4,96,1152]{2,1,0:T(8,128)(2,1)} %pad_maximum_fusion.3.refs_0_), channel_id=1, source_target_pairs={{0,1},{1,0},{2,3},{3,2},{4,5},{5,4},{6,7},{7,6},{8,9},{9,8},{10,11... | collective-permute-start | bytes 2654216 | tf_op jit(solution)/shard_map/ppermute | solution.py:409
  418.7 195.9 %collective-permute-start.34 = (bf16[4,192,384]{2,1,0:T(8,128)(2,1)}, bf16[4,192,384]{2,1,0:T(8,128)(2,1)}, u32[]{:S(2)}, u32[]{:S(2)}) collective-permute-start(bf16[4,192,384]{2,1,0:T(8,128)(2,1)} %collective-permute-done.33.refs_2_), channel_id=1, source_target_pairs={{0,8},{1,9},{2,10},{3,11},{4,12},{5,13},{6,14},{7,15},{8,0},{9,1},... | collective-permute-start | bytes 1769480 | tf_op jit(solution)/shard_map/ppermute | solution.py:409
  430.9 184.1 %collective-permute-start.36 = (bf16[4,192,384]{2,1,0:T(8,128)(2,1)}, bf16[4,192,384]{2,1,0:T(8,128)(2,1)}, u32[]{:S(2)}, u32[]{:S(2)}) collective-permute-start(bf16[4,192,384]{2,1,0:T(8,128)(2,1)} %collective-permute-done.35.refs_4_), channel_id=1, source_target_pairs={{0,8},{1,9},{2,10},{3,11},{4,12},{5,13},{6,14},{7,15},{8,0},{9,1},... | collective-permute-start | bytes 1769480 | tf_op jit(solution)/shard_map/ppermute | solution.py:409
  432.9 182.9 %collective-permute-start.38 = (bf16[4,192,384]{2,1,0:T(8,128)(2,1)S(1)}, bf16[4,192,384]{2,1,0:T(8,128)(2,1)}, u32[]{:S(2)}, u32[]{:S(2)}) collective-permute-start(bf16[4,192,384]{2,1,0:T(8,128)(2,1)S(1)} %collective-permute-done.37.refs_6_), channel_id=1, source_target_pairs={{0,8},{1,9},{2,10},{3,11},{4,12},{5,13},{6,14},{7,15},{8,0},{9,1},... | collective-permute-start | bytes 1769480 | tf_op jit(solution)/shard_map/ppermute | solution.py:409
  614.0 160.0 %collective-permute-start.42 = (bf16[4,96,1152]{2,1,0:T(8,128)(2,1)}, bf16[4,96,1152]{2,1,0:T(8,128)(2,1)}, u32[]{:S(2)}, u32[]{:S(2)}) collective-permute-start(bf16[4,96,1152]{2,1,0:T(8,128)(2,1)} %pad_maximum_fusion.3.refs_0_), channel_id=1, source_target_pairs={{0,8},{1,9},{2,10},{3,11},{4,12},{5,13},{6,14},{7,15},{8,0},{9,1},... | collective-permute-start | bytes 2654216 | tf_op jit(solution)/shard_map/ppermute | solution.py:409
  614.3 158.5 %collective-permute-start.55 = (bf16[4,48,1536]{2,1,0:T(8,128)(2,1)}, bf16[4,48,1536]{2,1,0:T(8,128)(2,1)}, u32[]{:S(2)}, u32[]{:S(2)}) collective-permute-start(bf16[4,48,1536]{2,1,0:T(8,128)(2,1)} %pad_maximum_fusion.6.refs_0_), channel_id=1, source_target_pairs={{0,1},{1,0},{2,3},{3,2},{4,5},{5,4},{6,7},{7,6},{8,9},{9,8},{10,11... | collective-permute-start | bytes 1769480 | tf_op jit(solution)/shard_map/ppermute | solution.py:409
  614.6 315.4 %collective-permute-start.57 = (bf16[4,48,1536]{2,1,0:T(8,128)(2,1)}, bf16[4,48,1536]{2,1,0:T(8,128)(2,1)}, u32[]{:S(2)}, u32[]{:S(2)}) collective-permute-start(bf16[4,48,1536]{2,1,0:T(8,128)(2,1)} %pad_maximum_fusion.6.refs_0_), channel_id=1, source_target_pairs={{0,16},{1,17},{2,18},{3,19},{4,20},{5,21},{6,22},{7,23},{8,24},{9,... | collective-permute-start | bytes 1769480 | tf_op jit(solution)/shard_map/ppermute | solution.py:409
  615.0 316.3 %collective-permute-start.54 = (bf16[4,48,1536]{2,1,0:T(8,128)(2,1)}, bf16[4,48,1536]{2,1,0:T(8,128)(2,1)}, u32[]{:S(2)}, u32[]{:S(2)}) collective-permute-start(bf16[4,48,1536]{2,1,0:T(8,128)(2,1)} %pad_maximum_fusion.6.refs_0_), channel_id=1, source_target_pairs={{0,8},{1,9},{2,10},{3,11},{4,12},{5,13},{6,14},{7,15},{8,0},{9,1},... | collective-permute-start | bytes 1769480 | tf_op jit(solution)/shard_map/ppermute | solution.py:409
  615.8 159.2 %collective-permute-start.44 = (bf16[4,96,1152]{2,1,0:T(8,128)(2,1)}, bf16[4,96,1152]{2,1,0:T(8,128)(2,1)}, u32[]{:S(2)}, u32[]{:S(2)}) collective-permute-start(bf16[4,96,1152]{2,1,0:T(8,128)(2,1)} %collective-permute-done.43.refs_2_), channel_id=1, source_target_pairs={{0,8},{1,9},{2,10},{3,11},{4,12},{5,13},{6,14},{7,15},{8,0},{9,1},... | collective-permute-start | bytes 2654216 | tf_op jit(solution)/shard_map/ppermute | solution.py:409
  772.8 158.6 %collective-permute-start.65 = (bf16[4,192,384]{2,1,0:T(8,128)(2,1)}, bf16[4,192,384]{2,1,0:T(8,128)(2,1)}, u32[]{:S(2)}, u32[]{:S(2)}) collective-permute-start(bf16[4,192,384]{2,1,0:T(8,128)(2,1)} %pad_maximum_fusion.7.refs_0_), channel_id=1, source_target_pairs={{0,1},{1,0},{2,3},{3,2},{4,5},{5,4},{6,7},{7,6},{8,9},{9,8},{10,11... | collective-permute-start | bytes 1769480 | tf_op jit(solution)/shard_map/ppermute | solution.py:409
  774.0 160.7 %collective-permute-start.67 = (bf16[4,192,384]{2,1,0:T(8,128)(2,1)}, bf16[4,192,384]{2,1,0:T(8,128)(2,1)}, u32[]{:S(2)}, u32[]{:S(2)}) collective-permute-start(bf16[4,192,384]{2,1,0:T(8,128)(2,1)} %pad_maximum_fusion.7.refs_0_), channel_id=1, source_target_pairs={{0,16},{1,17},{2,18},{3,19},{4,20},{5,21},{6,22},{7,23},{8,24},{9,... | collective-permute-start | bytes 1769480 | tf_op jit(solution)/shard_map/ppermute | solution.py:409
  775.1 157.4 %collective-permute-start.59 = (bf16[4,48,1536]{2,1,0:T(8,128)(2,1)}, bf16[4,48,1536]{2,1,0:T(8,128)(2,1)}, u32[]{:S(2)}, u32[]{:S(2)}) collective-permute-start(bf16[4,48,1536]{2,1,0:T(8,128)(2,1)} %collective-permute-done.55.refs_2_), channel_id=1, source_target_pairs={{0,16},{1,17},{2,18},{3,19},{4,20},{5,21},{6,22},{7,23},{8,24},{9,... | collective-permute-start | bytes 1769480 | tf_op jit(solution)/shard_map/ppermute | solution.py:409
  934.7 194.3 %collective-permute-start.64 = (bf16[4,192,384]{2,1,0:T(8,128)(2,1)}, bf16[4,192,384]{2,1,0:T(8,128)(2,1)}, u32[]{:S(2)}, u32[]{:S(2)}) collective-permute-start(bf16[4,192,384]{2,1,0:T(8,128)(2,1)} %pad_maximum_fusion.7.refs_0_), channel_id=1, source_target_pairs={{0,8},{1,9},{2,10},{3,11},{4,12},{5,13},{6,14},{7,15},{8,0},{9,1},... | collective-permute-start | bytes 1769480 | tf_op jit(solution)/shard_map/ppermute | solution.py:409
  934.8 194.2 %collective-permute-start.66 = (bf16[4,192,384]{2,1,0:T(8,128)(2,1)}, bf16[4,192,384]{2,1,0:T(8,128)(2,1)}, u32[]{:S(2)}, u32[]{:S(2)}) collective-permute-start(bf16[4,192,384]{2,1,0:T(8,128)(2,1)} %collective-permute-done.65.refs_2_), channel_id=1, source_target_pairs={{0,8},{1,9},{2,10},{3,11},{4,12},{5,13},{6,14},{7,15},{8,0},{9,1},... | collective-permute-start | bytes 1769480 | tf_op jit(solution)/shard_map/ppermute | solution.py:409
  935.3 193.7 %collective-permute-start.68 = (bf16[4,192,384]{2,1,0:T(8,128)(2,1)}, bf16[4,192,384]{2,1,0:T(8,128)(2,1)}, u32[]{:S(2)}, u32[]{:S(2)}) collective-permute-start(bf16[4,192,384]{2,1,0:T(8,128)(2,1)} %collective-permute-done.67.refs_4_), channel_id=1, source_target_pairs={{0,8},{1,9},{2,10},{3,11},{4,12},{5,13},{6,14},{7,15},{8,0},{9,1},... | collective-permute-start | bytes 1769480 | tf_op jit(solution)/shard_map/ppermute | solution.py:409
  946.2 182.8 %collective-permute-start.70 = (bf16[4,192,384]{2,1,0:T(8,128)(2,1)}, bf16[4,192,384]{2,1,0:T(8,128)(2,1)}, u32[]{:S(2)}, u32[]{:S(2)}) collective-permute-start(bf16[4,192,384]{2,1,0:T(8,128)(2,1)} %collective-permute-done.69.refs_6_), channel_id=1, source_target_pairs={{0,8},{1,9},{2,10},{3,11},{4,12},{5,13},{6,14},{7,15},{8,0},{9,1},... | collective-permute-start | bytes 1769480 | tf_op jit(solution)/shard_map/ppermute | solution.py:409
  1513.3 164.3 %collective-permute-start.133 = (bf16[4,2,2,192,384]{4,3,2,1,0:T(8,128)(2,1)}, bf16[4,2,2,192,384]{4,3,2,1,0:T(8,128)(2,1)}, u32[]{:S(2)}, u32[]{:S(2)}) collective-permute-start(bf16[4,2,2,192,384]{4,3,2,1,0:T(8,128)(2,1)} %bitcast.183), channel_id=1, source_target_pairs={{0,8},{1,9},{2,10},{3,11},{4,12},{5,13},{6,14},{7,15},{8,0},{9,1},... | collective-permute-start | bytes 7077896 | tf_op jit(solution)/shard_map/ppermute | solution.py:409
  1515.3 52.9 %collective-permute-start.103 = (bf16[4,2,2,48,384]{4,3,2,1,0:T(8,128)(2,1)}, bf16[4,2,2,48,384]{4,3,2,1,0:T(8,128)(2,1)}, u32[]{:S(2)}, u32[]{:S(2)}) collective-permute-start(bf16[4,2,2,48,384]{4,3,2,1,0:T(8,128)(2,1)} %bitcast.135), channel_id=1, source_target_pairs={{0,8},{1,9},{2,10},{3,11},{4,12},{5,13},{6,14},{7,15},{8,0},{9,1},... | collective-permute-start | bytes 1769480 | tf_op jit(solution)/shard_map/ppermute | solution.py:409
  1525.5 29.8 %collective-permute-start.95 = (f32[1536]{0:T(1024)S(1)}, f32[1536]{0:T(1024)S(1)}, u32[]{:S(2)}, u32[]{:S(2)}) collective-permute-start(f32[1536]{0:T(1024)S(1)} %add.819), channel_id=1, source_target_pairs={{0,6},{1,7},{2,0},{3,1},{4,2},{5,3},{6,4},{7,5},{8,14},{9,15},{10,... | collective-permute-start | bytes 18440 | tf_op jit(solution)/shard_map/ppermute | solution.py:409
  1526.6 31.4 %collective-permute-start.96 = (f32[1536]{0:T(1024)S(1)}, f32[1536]{0:T(1024)}, u32[]{:S(2)}, u32[]{:S(2)}) collective-permute-start(f32[1536]{0:T(1024)S(1)} %add.819), channel_id=1, source_target_pairs={{0,2},{1,3},{2,4},{3,5},{4,6},{5,7},{6,0},{7,1},{8,10},{9,11},{10,... | collective-permute-start | bytes 18440 | tf_op jit(solution)/shard_map/ppermute | solution.py:409
  1527.7 24.5 %collective-permute-start.100 = (f32[16896]{0:T(1024)}, f32[16896]{0:T(1024)}, u32[]{:S(2)}, u32[]{:S(2)}) collective-permute-start(f32[16896]{0:T(1024)} %add.826), channel_id=1, source_target_pairs={{0,4},{1,5},{2,6},{3,7},{4,0},{5,1},{6,2},{7,3},{8,12},{9,13},{10,... | collective-permute-start | bytes 202760 | tf_op jit(solution)/shard_map/ppermute | solution.py:409
  1552.2 19.2 %collective-permute-start.110 = (bf16[4,2,2,48,384]{4,3,2,1,0:T(8,128)(2,1)}, bf16[4,2,2,48,384]{4,3,2,1,0:T(8,128)(2,1)S(1)}, u32[]{:S(2)}, u32[]{:S(2)}) collective-permute-start(bf16[4,2,2,48,384]{4,3,2,1,0:T(8,128)(2,1)} %bitcast.586), channel_id=1, source_target_pairs={{0,8},{1,9},{2,10},{3,11},{4,12},{5,13},{6,14},{7,15},{8,0},{9,1},... | collective-permute-start | bytes 1769480 | tf_op jit(solution)/shard_map/ppermute | solution.py:409
  1573.8 49.4 %collective-permute-start.74 = (bf16[3,4,2,48,384]{4,3,2,1,0:T(8,128)(2,1)S(1)}, bf16[3,4,2,48,384]{4,3,2,1,0:T(8,128)(2,1)S(1)}, u32[]{:S(2)}, u32[]{:S(2)}) collective-permute-start(bf16[3,4,2,48,384]{4,3,2,1,0:T(8,128)(2,1)S(1)} %fusion.74), channel_id=1, source_target_pairs={{0,16},{1,17},{2,18},{3,19},{4,20},{5,21},{6,22},{7,23},{8,24},{9,... | collective-permute-start | bytes 2654216 | tf_op jit(solution)/shard_map/ppermute | solution.py:409
  1591.5 93.6 %collective-permute-start.140 = (bf16[4,2,2,192,384]{4,3,2,1,0:T(8,128)(2,1)S(1)}, bf16[4,2,2,192,384]{4,3,2,1,0:T(8,128)(2,1)S(1)}, u32[]{:S(2)}, u32[]{:S(2)}) collective-permute-start(bf16[4,2,2,192,384]{4,3,2,1,0:T(8,128)(2,1)S(1)} %bitcast.584), channel_id=1, source_target_pairs={{0,8},{1,9},{2,10},{3,11},{4,12},{5,13},{6,14},{7,15},{8,0},{9,1},... | collective-permute-start | bytes 7077896 | tf_op jit(solution)/shard_map/ppermute | solution.py:409
  1593.9 29.9 %collective-permute-start.84 = (bf16[3,4,2,48,384]{4,3,0,1,2:T(8,128)(2,1)S(1)}, bf16[3,4,2,48,384]{4,3,0,1,2:T(8,128)(2,1)S(1)}, u32[]{:S(2)}, u32[]{:S(2)}) collective-permute-start(bf16[3,4,2,48,384]{4,3,0,1,2:T(8,128)(2,1)S(1)} %fusion.75), channel_id=1, source_target_pairs={{0,16},{1,17},{2,18},{3,19},{4,20},{5,21},{6,22},{7,23},{8,24},{9,... | collective-permute-start | bytes 2654216 | tf_op jit(solution)/shard_map/ppermute | solution.py:409
  1595.6 19.1 %collective-permute-start.108 = (bf16[1,2,48,384]{3,2,1,0:T(8,128)(2,1)S(1)}, bf16[1,2,48,384]{3,2,1,0:T(8,128)(2,1)S(1)}, u32[]{:S(2)}, u32[]{:S(2)}) collective-permute-start(bf16[1,2,48,384]{3,2,1,0:T(8,128)(2,1)S(1)} %fusion.130), channel_id=1, source_target_pairs={{0,16},{1,17},{2,18},{3,19},{4,20},{5,21},{6,22},{7,23},{8,24},{9,... | collective-permute-start | bytes 221192 | tf_op jit(solution)/shard_map/ppermute | solution.py:409
  1622.8 65.3 %collective-permute-start.117 = (bf16[4,2,2,48,1536]{4,3,2,1,0:T(8,128)(2,1)S(1)}, bf16[4,2,2,48,1536]{4,3,2,1,0:T(8,128)(2,1)S(1)}, u32[]{:S(2)}, u32[]{:S(2)}) collective-permute-start(bf16[4,2,2,48,1536]{4,3,2,1,0:T(8,128)(2,1)S(1)} %bitcast.585), channel_id=1, source_target_pairs={{0,8},{1,9},{2,10},{3,11},{4,12},{5,13},{6,14},{7,15},{8,0},{9,1},... | collective-permute-start | bytes 7077896 | tf_op jit(solution)/shard_map/ppermute | solution.py:409
  1664.9 26.2 %collective-permute-start.125 = (bf16[4,2,2,48,1536]{4,3,0,1,2:T(8,128)(2,1)S(1)}, bf16[4,2,2,48,1536]{4,3,0,1,2:T(8,128)(2,1)S(1)}, u32[]{:S(2)}, u32[]{:S(2)}) collective-permute-start(bf16[4,2,2,48,1536]{4,3,0,1,2:T(8,128)(2,1)S(1)} %copy-done.25), channel_id=1, source_target_pairs={{0,8},{1,9},{2,10},{3,11},{4,12},{5,13},{6,14},{7,15},{8,0},{9,1},... | collective-permute-start | bytes 7077896 | tf_op jit(solution)/shard_map/ppermute | solution.py:409
  1675.0 22.5 %collective-permute-start.80 = (bf16[3,96,384]{2,1,0:T(8,128)(2,1)S(1)}, bf16[3,96,384]{2,1,0:T(8,128)(2,1)S(1)}, u32[]{:S(2)}, u32[]{:S(2)}) collective-permute-start(bf16[3,96,384]{2,1,0:T(8,128)(2,1)S(1)} %bitcast.528), channel_id=1, source_target_pairs={{0,8},{1,9},{2,10},{3,11},{4,12},{5,13},{6,14},{7,15},{8,0},{9,1},... | collective-permute-start | bytes 663560 | tf_op jit(solution)/shard_map/ppermute | solution.py:409
  1677.6 22.0 %collective-permute-start.90 = (bf16[3,96,384]{2,1,0:T(8,128)(2,1)S(1)}, bf16[3,96,384]{2,1,0:T(8,128)(2,1)S(1)}, u32[]{:S(2)}, u32[]{:S(2)}) collective-permute-start(bf16[3,96,384]{2,1,0:T(8,128)(2,1)S(1)} %bitcast.530), channel_id=1, source_target_pairs={{0,8},{1,9},{2,10},{3,11},{4,12},{5,13},{6,14},{7,15},{8,0},{9,1},... | collective-permute-start | bytes 663560 | tf_op jit(solution)/shard_map/ppermute | solution.py:409
  1685.1 27.4 %collective-permute-start.134 = (bf16[1,4,2,192,384]{4,3,2,1,0:T(8,128)(2,1)}, bf16[1,4,2,192,384]{4,3,2,1,0:T(8,128)(2,1)}, u32[]{:S(2)}, u32[]{:S(2)}) collective-permute-start(bf16[1,4,2,192,384]{4,3,2,1,0:T(8,128)(2,1)} %fusion.56), channel_id=1, source_target_pairs={{0,1},{1,0},{2,3},{3,2},{4,5},{5,4},{6,7},{7,6},{8,9},{9,8},{10,11... | collective-permute-start | bytes 3538952 | tf_op jit(solution)/shard_map/ppermute | solution.py:409
  1688.1 49.7 %collective-permute-start.141 = (bf16[1,4,2,192,384]{4,3,2,1,0:T(8,128)(2,1)}, bf16[1,4,2,192,384]{4,3,2,1,0:T(8,128)(2,1)}, u32[]{:S(2)}, u32[]{:S(2)}) collective-permute-start(bf16[1,4,2,192,384]{4,3,2,1,0:T(8,128)(2,1)} %fusion.57), channel_id=1, source_target_pairs={{0,1},{1,0},{2,3},{3,2},{4,5},{5,4},{6,7},{7,6},{8,9},{9,8},{10,11... | collective-permute-start | bytes 3538952 | tf_op jit(solution)/shard_map/ppermute | solution.py:409
  1691.1 50.7 %collective-permute-start.118 = (bf16[1,4,2,48,1536]{4,3,2,1,0:T(8,128)(2,1)S(1)}, bf16[1,4,2,48,1536]{4,3,2,1,0:T(8,128)(2,1)}, u32[]{:S(2)}, u32[]{:S(2)}) collective-permute-start(bf16[1,4,2,48,1536]{4,3,2,1,0:T(8,128)(2,1)S(1)} %fusion.54), channel_id=1, source_target_pairs={{0,16},{1,17},{2,18},{3,19},{4,20},{5,21},{6,22},{7,23},{8,24},{9,... | collective-permute-start | bytes 3538952 | tf_op jit(solution)/shard_map/ppermute | solution.py:409
  1697.5 47.7 %collective-permute-start.126 = (bf16[1,4,2,48,1536]{4,3,1,2,0:T(8,128)(2,1)}, bf16[1,4,2,48,1536]{4,3,1,2,0:T(8,128)(2,1)}, u32[]{:S(2)}, u32[]{:S(2)}) collective-permute-start(bf16[1,4,2,48,1536]{4,3,1,2,0:T(8,128)(2,1)} %fusion.55), channel_id=1, source_target_pairs={{0,16},{1,17},{2,18},{3,19},{4,20},{5,21},{6,22},{7,23},{8,24},{9,... | collective-permute-start | bytes 3538952 | tf_op jit(solution)/shard_map/ppermute | solution.py:409
  1714.9 34.2 %collective-permute-start.135 = (bf16[1,2,192,384]{3,2,1,0:T(8,128)(2,1)S(1)}, bf16[1,2,192,384]{3,2,1,0:T(8,128)(2,1)S(1)}, u32[]{:S(2)}, u32[]{:S(2)}) collective-permute-start(bf16[1,2,192,384]{3,2,1,0:T(8,128)(2,1)S(1)} %get-tuple-element.279), channel_id=1, source_target_pairs={{0,2},{1,3},{2,4},{3,5},{4,6},{5,7},{6,0},{7,1},{8,10},{9,11},{10,... | collective-permute-start | bytes 884744 | tf_op jit(solution)/shard_map/ppermute | solution.py:409
  1718.8 32.8 %collective-permute-start.136 = (bf16[1,2,192,384]{3,2,1,0:T(8,128)(2,1)S(1)}, bf16[1,2,192,384]{3,2,1,0:T(8,128)(2,1)S(1)}, u32[]{:S(2)}, u32[]{:S(2)}) collective-permute-start(bf16[1,2,192,384]{3,2,1,0:T(8,128)(2,1)S(1)} %get-tuple-element.281), channel_id=1, source_target_pairs={{0,4},{1,5},{2,6},{3,7},{4,0},{5,1},{6,2},{7,3},{8,12},{9,13},{10,... | collective-permute-start | bytes 884744 | tf_op jit(solution)/shard_map/ppermute | solution.py:409
  1745.3 20.4 %collective-permute-start.143 = (bf16[1,2,192,384]{3,2,1,0:T(8,128)(2,1)S(1)}, bf16[1,2,192,384]{3,2,1,0:T(8,128)(2,1)S(1)}, u32[]{:S(2)}, u32[]{:S(2)}) collective-permute-start(bf16[1,2,192,384]{3,2,1,0:T(8,128)(2,1)S(1)} %get-tuple-element.284), channel_id=1, source_target_pairs={{0,4},{1,5},{2,6},{3,7},{4,0},{5,1},{6,2},{7,3},{8,12},{9,13},{10,... | collective-permute-start | bytes 884744 | tf_op jit(solution)/shard_map/ppermute | solution.py:409
  1749.1 22.9 %collective-permute-start.144 = (bf16[1,2,192,384]{3,2,1,0:T(8,128)(2,1)S(1)}, bf16[1,2,192,384]{3,2,1,0:T(8,128)(2,1)S(1)}, u32[]{:S(2)}, u32[]{:S(2)}) collective-permute-start(bf16[1,2,192,384]{3,2,1,0:T(8,128)(2,1)S(1)} %get-tuple-element.283), channel_id=1, source_target_pairs={{0,6},{1,7},{2,0},{3,1},{4,2},{5,3},{6,4},{7,5},{8,14},{9,15},{10,... | collective-permute-start | bytes 884744 | tf_op jit(solution)/shard_map/ppermute | solution.py:409
  1751.6 30.2 %collective-permute-start.119 = (bf16[1,4,48,1536]{3,2,1,0:T(8,128)(2,1)S(1)}, bf16[1,4,48,1536]{3,2,1,0:T(8,128)(2,1)S(1)}, u32[]{:S(2)}, u32[]{:S(2)}) collective-permute-start(bf16[1,4,48,1536]{3,2,1,0:T(8,128)(2,1)S(1)} %fusion.84), channel_id=1, source_target_pairs={{0,1},{1,0},{2,3},{3,2},{4,5},{5,4},{6,7},{7,6},{8,9},{9,8},{10,11... | collective-permute-start | bytes 1769480 | tf_op jit(solution)/shard_map/ppermute | solution.py:409
  1752.8 21.6 %collective-permute-start.138 = (bf16[1,2,192,384]{3,2,1,0:T(8,128)(2,1)S(1)}, bf16[1,2,192,384]{3,2,1,0:T(8,128)(2,1)S(1)}, u32[]{:S(2)}, u32[]{:S(2)}) collective-permute-start(bf16[1,2,192,384]{3,2,1,0:T(8,128)(2,1)S(1)} %fusion.91), channel_id=1, source_target_pairs={{0,16},{1,17},{2,18},{3,19},{4,20},{5,21},{6,22},{7,23},{8,24},{9,... | collective-permute-start | bytes 884744 | tf_op jit(solution)/shard_map/ppermute | solution.py:409
  1774.5 38.6 %collective-permute-start.139 = (bf16[1,384,384]{2,1,0:T(8,128)(2,1)S(1)}, bf16[1,384,384]{2,1,0:T(8,128)(2,1)S(1)}, u32[]{:S(2)}, u32[]{:S(2)}) collective-permute-start(bf16[1,384,384]{2,1,0:T(8,128)(2,1)S(1)} %bitcast.520), channel_id=1, source_target_pairs={{0,8},{1,9},{2,10},{3,11},{4,12},{5,13},{6,14},{7,15},{8,0},{9,1},... | collective-permute-start | bytes 884744 | tf_op jit(solution)/shard_map/ppermute | solution.py:409
  1779.5 33.7 %collective-permute-start.146 = (bf16[1,384,384]{2,1,0:T(8,128)(2,1)S(1)}, bf16[1,384,384]{2,1,0:T(8,128)(2,1)S(1)}, u32[]{:S(2)}, u32[]{:S(2)}) collective-permute-start(bf16[1,384,384]{2,1,0:T(8,128)(2,1)S(1)} %bitcast.522), channel_id=1, source_target_pairs={{0,8},{1,9},{2,10},{3,11},{4,12},{5,13},{6,14},{7,15},{8,0},{9,1},... | collective-permute-start | bytes 884744 | tf_op jit(solution)/shard_map/ppermute | solution.py:409
  1786.9 19.1 %collective-permute-start.122 = (bf16[1,48,1536]{2,1,0:T(8,128)(2,1)S(1)}, bf16[1,48,1536]{2,1,0:T(8,128)(2,1)S(1)}, u32[]{:S(2)}, u32[]{:S(2)}) collective-permute-start(bf16[1,48,1536]{2,1,0:T(8,128)(2,1)S(1)} %get-tuple-element.286), channel_id=1, source_target_pairs={{0,6},{1,7},{2,0},{3,1},{4,2},{5,3},{6,4},{7,5},{8,14},{9,15},{10,... | collective-permute-start | bytes 442376 | tf_op jit(solution)/shard_map/ppermute | solution.py:409
  (241 other events, 6082.9 us)

commit v2 on v1

--- a/solution.py
+++ b/solution.py
@@ -259,46 +259,40 @@
     )(slots, grad_context, *kept)
 
 
-def layer_forward(layer_in, weights, path_info):
-    (
-        qkv_weight,
-        qv_bias,
-        out_weight,
-        out_bias,
-        attn_gain,
-        attn_shift,
-        ffin_weight,
-        ffin_bias,
-        ffout_weight,
-        ffout_bias,
-        ffn_gain,
-        ffn_shift,
-    ) = weights
+def layer_forward(layer_in, get, path_info, tick):
+    qv_bias, out_bias, attn_gain, attn_shift, ffin_bias, ffout_bias, ffn_gain, ffn_shift = (
+        get(number) for number in VECTORS
+    )
     layer_low = layer_in.astype(jnp.bfloat16)
     bias_float = qv_bias.astype(jnp.float32)
     full_bias = jnp.concatenate([bias_float[:D], jnp.zeros((D,), jnp.float32), bias_float[D:]])
     projected = (
-        jnp.dot(layer_low, qkv_weight, preferred_element_type=jnp.float32) + full_bias
+        jnp.dot(layer_low, get(0), preferred_element_type=jnp.float32) + full_bias
     ).astype(jnp.bfloat16)
+    projected = tick("projected", projected)
     slots, bias = path_info
     context, *kept_heads = attend(projected, slots, bias)
+    context = tick("context", context)
     attn_sum = (
         layer_in
-        + jnp.dot(context, out_weight, preferred_element_type=jnp.float32)
+        + jnp.dot(context, get(2), preferred_element_type=jnp.float32)
         + out_bias.astype(jnp.float32)
     )
     hidden_one = layer_norm(attn_sum, attn_gain.astype(jnp.float32), attn_shift.astype(jnp.float32))
     hidden_low = hidden_one.astype(jnp.bfloat16)
+    hidden_low = tick("hidden", hidden_low)
     pre_act = jnp.dot(
-        hidden_low, ffin_weight, preferred_element_type=jnp.float32
+        hidden_low, get(6), preferred_element_type=jnp.float32
     ) + ffin_bias.astype(jnp.float32)
     act_low = gelu_exact(pre_act).astype(jnp.bfloat16)
+    act_low = tick("act", act_low)
     ffn_sum = (
         hidden_one
-        + jnp.dot(act_low, ffout_weight, preferred_element_type=jnp.float32)
+        + jnp.dot(act_low, get(8), preferred_element_type=jnp.float32)
         + ffout_bias.astype(jnp.float32)
     )
     result = layer_norm(ffn_sum, ffn_gain.astype(jnp.float32), ffn_shift.astype(jnp.float32))
+    result = tick("result", result)
     saved = (
         layer_low,
         kept_heads,
@@ -312,7 +306,7 @@
     return (result, saved)
 
 
-def layer_backward(grad_out, weights, saved, path_info, reduce):
+def layer_backward(grad_out, weights, saved, path_info, reduce, tick):
     (
         qkv_weight,
         qv_bias,
@@ -342,12 +336,14 @@
     )
     grad_ffn_sum, grad_ffn_gain, grad_ffn_shift = norm_pull(grad_out)
     grad_down = grad_ffn_sum.astype(jnp.bfloat16)
-    grad_ffout_weight = reduce(act_low, grad_down[None], False)
+    grad_down = tick("down", grad_down)
+    grad_ffout_weight = reduce(8, act_low, grad_down[None])
     grad_ffout_bias = jnp.sum(grad_down.astype(jnp.float32), axis=0)
     grad_act = dot_last(grad_down, ffout_weight)
     ignored, gelu_pull = jax.vjp(gelu_exact, pre_act)
     grad_pre = gelu_pull(grad_act)[0].astype(jnp.bfloat16)
-    grad_ffin_weight = reduce(hidden_low, grad_pre[None], True)
+    grad_pre = tick("pre", grad_pre)
+    grad_ffin_weight = reduce(6, hidden_low, grad_pre[None])
     grad_ffin_bias = jnp.sum(grad_pre.astype(jnp.float32), axis=0)
     grad_hidden = grad_ffn_sum + dot_last(grad_pre, ffin_weight)
     ignored, first_pull = jax.vjp(
@@ -355,11 +351,14 @@
     )
     grad_attn_sum, grad_attn_gain, grad_attn_shift = first_pull(grad_hidden)
     grad_attn_low = grad_attn_sum.astype(jnp.bfloat16)
-    grad_out_weight = reduce(context, grad_attn_low[None], False)
+    grad_attn_low = tick("attn", grad_attn_low)
+    grad_out_weight = reduce(2, context, grad_attn_low[None])
     grad_out_bias = jnp.sum(grad_attn_low.astype(jnp.float32), axis=0)
     grad_context = dot_last(grad_attn_low, out_weight).astype(jnp.bfloat16)
+    grad_context = tick("context", grad_context)
     grad_proj = attend_back(grad_context, path_info[0], kept_heads)
-    grad_qkv_weight = reduce(layer_low, grad_proj, True)
+    grad_proj = tick("proj", grad_proj)
+    grad_qkv_weight = reduce(0, layer_low, grad_proj)
     column_sums = jnp.sum(grad_proj.astype(jnp.float32), axis=1)
     grad_qv_bias = jnp.concatenate([column_sums[0], column_sums[2]])
     grad_in = grad_attn_sum
@@ -388,12 +387,32 @@
 CHIPS_Z, CHIPS_X, CHIPS_Y, CORES = 4, 2, 2, 2
 
 
+FORWARD = {
+    "begin": ((), ((0, 0),)),
+    "slots": (((0, 0),), ((0, 2), (0, 6))),
+    "mask": (((0, 0),), ()),
+    "ready": (((0, 0), (0, 2), (0, 6)), ((0, 8),)),
+    (0, "projected"): (((0, 2), (0, 6), (0, 8)), ((1, 0),)),
+    (0, "context"): (((0, 2), (0, 6), (0, 8), (1, 0)), ((1, 2), (1, 6))),
+    (0, "hidden"): (((0, 6),), ()),
+    (0, "act"): (((0, 8), (1, 0), (1, 2), (1, 6)), ((1, 8),)),
+    (0, "result"): (((1, 0), (1, 2)), ()),
+    (1, "projected"): (((1, 2), (1, 6), (1, 8)), ()),
+    (1, "context"): (((1, 6), (1, 8)), ()),
+    (1, "hidden"): (((1, 6), (1, 8)), ()),
+    (1, "act"): (((1, 8),), ()),
+}
+
+
 class Place:
     def __init__(self):
         rep = lax.axis_index("rep")
         shard = lax.axis_index("shard")
         self.y, self.core = rep // CORES, rep % CORES
         self.z, self.x = shard // CHIPS_X, shard % CHIPS_X
+
+    def vector(self):
+        return jnp.stack([self.z, self.x, self.y, self.core]).astype(jnp.int32)
 
 
 def hop(value, dz=0, dx=0, dy=0, dc=0):
@@ -419,60 +438,81 @@
     )
 
 
-def place_kernel(split_y, half, count, *refs):
-    pieces, out, sems = refs[:count], refs[count], refs[count + 1]
-    rep = lax.axis_index("rep")
-    shard = lax.axis_index("shard")
-    y, core = rep // CORES, rep % CORES
-    z, x = shard // CHIPS_X, shard % CHIPS_X
-    copies = []
+def place_kernel(split_y, half, at_ref, *refs):
+    pieces, out_ref = refs[:-1], refs[-1]
     for number, piece in enumerate(pieces):
-        dc = number % CORES
-        dx = number // CORES % CHIPS_X
-        dy = number // (CORES * CHIPS_X)
-        column = pl.multiple_of((core + dc) % CORES * half, 128)
-        for dz in range(CHIPS_Z):
-            owner = (z + CHIPS_Z - dz) % CHIPS_Z * CHIPS_X + (x + dx) % CHIPS_X
-            row = (y + dy) % CHIPS_Y if split_y else 0
-            copies.append(
-                pltpu.make_async_copy(
-                    piece.at[dz],
-                    out.at[owner, row, :, pl.ds(column, half)],
-                    sems.at[number * CHIPS_Z + dz],
-                )
-            )
-    for copy in copies:
-        copy.start()
-    for copy in copies:
-        copy.wait()
-
-
-def gather_start(block):
-    return [block] + [hop(block, dz=k) for k in range(1, CHIPS_Z)]
-
-
-def gather_finish(parts, split_y):
-    _, rows, half = parts[0].shape[0], parts[0].shape[0], parts[0].shape[1]
-    stack = jnp.stack(parts)
-    pieces = [stack, hop(stack, dx=1)]
-    if split_y:
-        pieces = pieces + [hop(piece, dy=1) for piece in pieces]
-    pieces = [item for piece in pieces for item in (piece, hop(piece, dc=1))]
+        core = (at_ref[3] + number % CORES) % CORES
+        x = (at_ref[1] + number // CORES % CHIPS_X) % CHIPS_X
+        row = (at_ref[2] + number // (CORES * CHIPS_X)) % CHIPS_Y if split_y else 0
+        out_ref[x, row, :, pl.ds(pl.multiple_of(core * half, 128), half)] = piece[0]
+
+
+def place_pieces(pieces, split_y, place):
+    _, rows, half = pieces[0].shape
     splits = CHIPS_Y if split_y else 1
-    count = len(pieces)
     whole = pl.pallas_call(
-        lambda *refs: place_kernel(split_y, half, count, *refs),
-        in_specs=[pl.BlockSpec(memory_space=pl.ANY)] * count,
-        out_specs=pl.BlockSpec(memory_space=pl.ANY),
+        functools.partial(place_kernel, split_y, half),
+        grid_spec=pltpu.PrefetchScalarGridSpec(
+            num_scalar_prefetch=1,
+            grid=(CHIPS_Z,),
+            in_specs=[pl.BlockSpec((1, rows, half), lambda k, at: (k, 0, 0))] * len(pieces),
+            out_specs=pl.BlockSpec(
+                (CHIPS_X, splits, rows, 2 * half),
+                lambda k, at: (lax.rem(at[0] + CHIPS_Z - k, CHIPS_Z), 0, 0, 0),
+            ),
+        ),
         out_shape=jax.ShapeDtypeStruct(
             (CHIPS_Z * CHIPS_X, splits, rows, 2 * half), jnp.bfloat16
         ),
-        scratch_shapes=[pltpu.SemaphoreType.DMA((count * CHIPS_Z,))],
+        compiler_params=kernel_params(),
         cost_estimate=pl.CostEstimate(
-            flops=0, bytes_accessed=4 * CHIPS_Z * count * rows * half, transcendentals=0
+            flops=0,
+            bytes_accessed=4 * CHIPS_Z * len(pieces) * rows * half,
+            transcendentals=0,
         ),
-    )(*pieces)
+    )(place.vector(), *pieces)
     return whole.reshape(CHIPS_Z * CHIPS_X * splits * rows, 2 * half)
+
+
+def gather_chain(block, split_y, place):
+    parts = yield [hop(block, dz=k) for k in range(1, CHIPS_Z)]
+    stack = jnp.stack([block, *parts])
+    (across,) = yield [hop(stack, dx=1)]
+    pieces = [stack, across]
+    if split_y:
+        pieces = pieces + (yield [hop(piece, dy=1) for piece in pieces])
+    others = yield [hop(piece, dc=1) for piece in pieces]
+    return place_pieces(
+        [item for pair in zip(pieces, others) for item in pair], split_y, place
+    )
+
+
+class Flow:
+    def __init__(self):
+        self.running, self.done = {}, {}
+
+    def start(self, name, chain):
+        self.running[name] = (chain, next(chain))
+
+    def advance(self, name, arrived):
+        chain, _ = self.running.pop(name)
+        try:
+            self.running[name] = (chain, chain.send(list(arrived)))
+        except StopIteration as end:
+            self.done[name] = end.value
+
+    def tick(self, main, *names):
+        names = [name for name in names if name in self.running]
+        pending = [self.running[name][1] for name in names]
+        main, pending = lax.optimization_barrier((main, pending))
+        for name, arrived in zip(names, pending):
+            self.advance(name, arrived)
+        return main
+
+    def finish(self, name):
+        while name in self.running:
+            self.advance(name, self.running[name][1])
+        return self.done[name]
 
 
 def gather_vectors(vectors, place):
@@ -501,29 +541,13 @@
     return out
 
 
-def gather_all(weights, place):
-    vectors = gather_vectors([weights[number] for number in VECTORS], place)
-    gathered = [[None] * 12 for _ in range(LAYERS)]
-    previous = None
-    for layer in range(LAYERS):
-        for number in MATRICES:
-            shard = weights[number][layer]
-            rows, columns = shard.shape
-            split_y = number in (6, 8)
-            tall = rows // CHIPS_Y if split_y else rows
-            block = lax.dynamic_slice(
-                shard,
-                (place.y * tall if split_y else 0, place.core * (columns // 2)),
-                (tall, columns // 2),
-            )
-            if previous is not None:
-                block, *_ = lax.optimization_barrier((block, *previous))
-            parts = gather_start(block)
-            previous = parts[1:]
-            gathered[layer][number] = gather_finish(parts, split_y)
-        for number, vector in zip(VECTORS, vectors):
-            gathered[layer][number] = vector[layer]
-    return gathered
+def gather_block(weights, layer, number, place):
+    shard = weights[number][layer]
+    rows, columns = shard.shape
+    split_y = number in (6, 8)
+    tall = rows // CHIPS_Y if split_y else rows
+    start = (place.y * tall if split_y else 0, place.core * (columns // 2))
+    return lax.dynamic_slice(shard, start, (tall, columns // 2)), split_y
 
 
 def low_sum(*terms):
@@ -533,7 +557,7 @@
     return total
 
 
-def reduce_matrix(left, right, place, y_first):
+def reduce_chain(left, right, place, y_first):
     parts, _, columns = right.shape
     half = columns // 2
     depth = left.shape[1]
@@ -546,29 +570,32 @@
         ]
 
     away = product(1 - place.core)
-    arrived = [hop(part, dc=1) for part in away]
+    hops = [hop(part, dc=1) for part in away]
     kept = product(place.core)
+    arrived = yield hops
     total = jnp.stack([low_sum(mine, other) for mine, other in zip(kept, arrived)], axis=0)
 
-    def swap(values, index, axis, **step):
+    def swap(values, index, axis, step):
         sent = pick(values, 1 - index, axis).astype(jnp.bfloat16)
-        return low_sum(pick(values, index, axis), hop(sent, **step))
+        (other,) = yield [hop(sent, **step)]
+        return low_sum(pick(values, index, axis), other)
 
     if y_first:
-        total = swap(total, place.y, 3, dy=1)
-    total = swap(total, place.x, 2, dx=1)
-    landed = []
-    for k in range(1, CHIPS_Z):
-        sent = pick(total, (place.z + k) % CHIPS_Z, 1).astype(jnp.bfloat16)
-        landed.append(hop(sent, dz=k))
+        total = yield from swap(total, place.y, 3, dict(dy=1))
+    total = yield from swap(total, place.x, 2, dict(dx=1))
+    landed = yield [
+        hop(pick(total, (place.z + k) % CHIPS_Z, 1).astype(jnp.bfloat16), dz=k)
+        for k in range(1, CHIPS_Z)
+    ]
     total = low_sum(pick(total, place.z, 1), *landed).astype(jnp.bfloat16)
+    (other,) = yield [hop(total, dy=1)]
     if y_first:
-        rows = total[:, None]
-        rows = ordered(place.y == 0, rows, hop(rows, dy=1), 1)
+        rows = ordered(place.y == 0, total[:, None], other[:, None], 1)
     else:
-        rows = low_sum(total, hop(total, dy=1)).astype(jnp.bfloat16)
+        rows = low_sum(total, other).astype(jnp.bfloat16)
     rows = rows.reshape(parts, depth // 8, half)
-    rows = ordered(place.core == 0, rows, hop(rows, dc=1), 2).astype(jnp.float32)
+    (other,) = yield [hop(rows, dc=1)]
+    rows = ordered(place.core == 0, rows, other, 2).astype(jnp.float32)
     return rows.transpose(1, 0, 2).reshape(depth // 8, parts * columns)
 
 
@@ -576,8 +603,9 @@
     sizes = [vector.shape[0] for vector in vectors]
     total = jnp.concatenate(vectors)
     for step in (dict(dc=1), dict(dy=1), dict(dx=1), dict(dz=2)):
-        total = total + hop(total, **step)
-    up, down = hop(total, dz=1), hop(total, dz=3)
+        (other,) = yield [hop(total, **step)]
+        total = total + other
+    up, down = yield [hop(total, dz=1), hop(total, dz=3)]
     total = total + jnp.where(place.z % 2 == 0, down, up)
     count = CHIPS_Z * CHIPS_X
     shard = place.z * CHIPS_X + place.x
@@ -617,7 +645,6 @@
     slots = slot_ranks(cluster_ids).reshape(tree_count, PAIRS, 2, TREE_LEN)
     ids = jnp.stack([segments, parents, grands], axis=-1).astype(jnp.bfloat16)
     ids = jnp.pad(ids, ((0, 0), (0, 0), (0, LANES - 3)))
-    path_info = (slots, mask_bias(slots, ids))
     weights = (
         qkv_weight,
         qv_bias,
@@ -632,50 +659,93 @@
         ffn_gain,
         ffn_shift,
     )
+    flow = Flow()
     if fast:
         place = Place()
-        gathered = gather_all(weights, place)
-
-        def reduce(left, right, y_first):
-            return reduce_matrix(left, right, place, y_first)
+        vectors = gather_vectors([weights[number] for number in VECTORS], place)
+
+        def begin(layer, number):
+            flow.start((layer, number), gather_chain(*gather_block(weights, layer, number, place), place))
+
+        def get(layer, number):
+            if number in VECTORS:
+                return vectors[VECTORS.index(number)][layer]
+            return flow.finish((layer, number))
+
+        def step(point, main):
+            advanced, started = FORWARD.get(point, ((), ()))
+            main = flow.tick(main, *advanced)
+            for name in started:
+                begin(*name)
+            return main
+
+        def reduce(layer, number, left, right):
+            flow.start(
+                ("grad", layer, number), reduce_chain(left, right, place, number in (0, 6))
+            )
+
+        def back_step(point, main):
+            return flow.tick(main, *[name for name in flow.running if name[0] == "grad"])
 
     else:
-        gathered = [
-            [lax.all_gather(weight[layer], "shard", axis=0, tiled=True) for weight in weights]
-            for layer in range(LAYERS)
-        ]
-
-        def reduce(left, right, y_first):
+
+        def get(layer, number):
+            return lax.all_gather(weights[number][layer], "shard", axis=0, tiled=True)
+
+        def step(point, main):
+            return main
+
+        def reduce(layer, number, left, right):
             grads = jnp.concatenate([dot_first(left, part) for part in right], axis=1)
             grads = lax.psum_scatter(grads, "shard", scatter_dimension=0, tiled=True)
-            return lax.psum(grads.astype(jnp.bfloat16), "rep").astype(jnp.float32)
-
-    hidden = inputs.astype(jnp.float32)
+            grads = lax.psum(grads.astype(jnp.bfloat16), "rep").astype(jnp.float32)
+            flow.done[("grad", layer, number)] = grads
+
+        back_step = step
+
+    step("begin", ())
+    slots = step("slots", slots)
+    path_info = (slots, step("mask", mask_bias(slots, ids)))
+    hidden = step("ready", inputs.astype(jnp.float32))
     kept_saved = []
     for layer_index in range(LAYERS):
-        hidden, saved = layer_forward(hidden, gathered[layer_index], path_info)
+        hidden, saved = layer_forward(
+            hidden,
+            functools.partial(get, layer_index),
+            path_info,
+            lambda point, main: step((layer_index, point), main),
+        )
         kept_saved.append(saved)
     result = hidden.astype(jnp.bfloat16)
     grad_rows = cotangent.astype(jnp.float32)
     per_layer = [None] * LAYERS
+    vector_items = [(1, number) for number in VECTORS] + [(0, number) for number in VECTORS[1:]]
     for layer_index in reversed(range(LAYERS)):
         grad_rows, grads = layer_backward(
-            grad_rows, gathered[layer_index], kept_saved[layer_index], path_info, reduce
+            grad_rows,
+            [get(layer_index, number) for number in range(12)],
+            kept_saved[layer_index],
+            path_info,
+            functools.partial(reduce, layer_index),
+            lambda point, main: back_step((layer_index, point), main),
         )
         per_layer[layer_index] = list(grads)
-    order = [(layer, number) for layer in reversed(range(LAYERS)) for number in VECTORS]
-    early = [item for item in order if item != (0, 1)]
-    for items in (early, [(0, 1)]):
-        vectors = [per_layer[layer][number] for layer, number in items]
+        grad_rows = back_step((layer_index, "end"), grad_rows)
+    for tag, items in (("early", vector_items), ("late", [(0, 1)])):
+        vectors_in = [per_layer[layer][number] for layer, number in items]
         if fast:
-            vectors = reduce_vectors(vectors, place)
+            flow.start(tag, reduce_vectors(vectors_in, place))
+            vectors_out = flow.finish(tag)
         else:
-            vectors = [
+            vectors_out = [
                 lax.psum(lax.psum_scatter(vector, "shard", tiled=True), "rep")
-                for vector in vectors
+                for vector in vectors_in
             ]
-        for (layer, number), vector in zip(items, vectors):
+        for (layer, number), vector in zip(items, vectors_out):
             per_layer[layer][number] = vector
+    for layer_index in range(LAYERS):
+        for number in MATRICES:
+            per_layer[layer_index][number] = flow.finish(("grad", layer_index, number))
     stacked = tuple(
         (
             jnp.stack([per_layer[layer_index][member] for layer_index in range(LAYERS)])

time: 1840 us -> 1000 us (0.54)
  Pallas kernels: 1020 us -> 193 us
    pallas_call x8, Pallas kernels: 868 us -> 42.4 us  [place_pieces(): pl.pallas_call(functools.partial(place_kernel, split_y, half), grid_spec=...]
  transfers between devices with their start and end apart: 147 -> 147, of which waited for: 51 -> 33; matrix products, arithmetic and copies ran while one was open for 13% -> 30% of each run, Pallas kernels for 44% -> 19%
where the time goes in v2:
time: 1000 us; the launch traced here: 990 us
  matrix products  247 us (25%)
  waiting for transfers between devices  202 us (20%)
  Pallas kernels  193 us (19%)
  starting transfers between devices  170 us (17%)
  local copies, waits for them, and re-layouts  88.2 us (9%)
  other arithmetic  86.1 us (9%)
    ppermute x147, waiting for transfers between devices, hop(): return lax.ppermute(value, AXES, pairs)  202 us
    ppermute x147, starting transfers between devices, hop(): return lax.ppermute(value, AXES, pairs)  170 us
    dot_general x12, matrix products, dot_last(): lax.dot_general(left_side, right_side, (((1,), (1,)), ((), ())), preferre...  77.7 us
    dot_general x2, matrix products, layer_forward(): jnp.dot(hidden_low, get(6), preferred_element_type=jnp.float32)  73.3 us
    pallas_call x2, Pallas kernels, attend_back(): pl.pallas_call(attend_back_kernel, grid=(trees, PAIRS), in_specs=[slot_sp...  67.1 us
    pallas_call x2, Pallas kernels, attend(): pl.pallas_call(attend_kernel, grid=(trees, PAIRS), in_specs=[slot_spec(),...  66.8 us
    dot_general x24, matrix products, dot_first(): lax.dot_general(left_side, right_side, (((0,), (0,)), ((), ())), preferre...  52.6 us
    pallas_call x8, Pallas kernels, place_pieces(): pl.pallas_call(functools.partial(place_kernel, split_y, half), grid_spec=...  42.4 us
  transfers between devices with their start and end apart: 147, of which 33 were waited for; matrix products, arithmetic and copies ran while one was open for 30% of the time, Pallas kernels for 19%

profile of v2, /device:TPU:17, one launch (start us, length us, event | category | flops | bytes accessed | tf_op | source)
XLA Modules:
  0.0 990.3 jit_solution(7927963231016373862)
XLA Ops:
  57.4 5.5 collective-permute-done.1
  62.9 6.3 collective-permute-done.2
  73.3 16.8 %shard_map.272.bias_ref = bf16[1,12,1024,128]{3,2,1,0:T(8,128)(2,1)} custom-call(s32[1,6,2,1024]{3,2,1,0:T(2,128)} %reshape.1536.slot_ref, bf16[1,1024,128]{2,1,0:T(8,128)(2,1)} %pad.4.ids_ref), custom_call_target="tpu_custom_call" | custom-call | flops 12000000000 | bytes 4000000 | tf_op jit(solution)/shard_map/pallas_call | solution.py:204
  90.1 3.6 collective-permute-done.4.refs_2_
  109.4 3.2 collective-permute-start.22
  112.6 6.3 collective-permute-done.11
  125.7 5.3 shard_map.273
  134.0 7.6 add_convert_fusion.3.query_ref.key_ref.value_ref
  141.6 3.6 collective-permute-start.24
  145.2 7.2 collective-permute-done.20.refs_2_
  159.7 33.4 %shard_map.274 = (bf16[1024,768]{1,0:T(8,128)(2,1)}, bf16[1,12,1024,128]{3,2,1,0:T(8,128)(2,1)}, bf16[1,12,1024,128]{3,2,1,0:T(8,128)(2,1)}, bf16[1,12,1024,128]{3,2,1,0:T(8,128)(2,1)}) custom-call(s32[1,6,2,1024]{3,2,1,0:T(2,128)} %reshape.1536.slot_ref, bf16[1024,2304]{1,0:T(8,128)(2,1)} %add_convert_fusion.3.query_ref.key_ref.value_ref, ...), custom_call_target="tpu_custom_call" | custom-call | flops 30000001024 | bytes 20000000 | tf_op jit(solution)/shard_map/pallas_call | solution.py:223
  196.0 4.2 shard_map.275
  200.2 4.3 fusion.191
  215.9 5.8 shard_map.276
  225.8 37.1 %multiply_convert_fusion.1 = (bf16[1024,3072]{1,0:T(8,128)(2,1)}, f32[1024,3072]{1,0:T(8,128)}, f32[1024,3072]{1,0:T(8,128)}) fusion(f32[3072]{0:T(1024)S(1)} %bitcast.522, bf16[1024,768]{0,1:T(8,128)(2,1)} %fusion.23, bf16[768,3072]{1,0:T(8,128)(2,1)} %bitcast.462), kind=kOutput, calls=%fused_computation.21 | convolution fusion | flops 5039456256 | bytes 37761024 | tf_op jit(solution)/shard_map/dot_general | solution.py:284
  277.4 5.8 shard_map.277
  283.3 8.9 fusion.192
  299.6 5.3 shard_map.278
  305.2 8.6 add_convert_fusion.2.query_ref.key_ref.value_ref
  319.3 33.4 %shard_map.279 = (bf16[1024,768]{1,0:T(8,128)(2,1)}, bf16[1,12,1024,128]{3,2,1,0:T(8,128)(2,1)}, bf16[1,12,1024,128]{3,2,1,0:T(8,128)(2,1)}, bf16[1,12,1024,128]{3,2,1,0:T(8,128)(2,1)}) custom-call(s32[1,6,2,1024]{3,2,1,0:T(2,128)} %reshape.1536.slot_ref, bf16[1024,2304]{1,0:T(8,128)(2,1)} %add_convert_fusion.2.query_ref.key_ref.value_ref, ...), custom_call_target="tpu_custom_call" | custom-call | flops 30000001024 | bytes 20000000 | tf_op jit(solution)/shard_map/pallas_call | solution.py:223
  352.7 4.4 shard_map.280
  359.2 3.3 fusion.193
  364.7 7.3 collective-permute-done.65.refs_4_
  374.1 10.3 %collective-permute-done.66.refs_6_ = bf16[4,192,384]{2,1,0:T(8,128)(2,1)S(1)} collective-permute-done((bf16[4,192,384]{2,1,0:T(8,128)(2,1)}, bf16[4,192,384]{2,1,0:T(8,128)(2,1)S(1)}, u32[]{:S(2)}, u32[]{:S(2)}) %collective-permute-start.66) | collective-permute-done | bytes 589856 | tf_op jit(solution)/shard_map/ppermute | solution.py:428
  385.8 5.8 shard_map.281
  391.7 36.3 %multiply_convert_fusion = (bf16[1024,3072]{1,0:T(8,128)(2,1)}, f32[1024,3072]{1,0:T(8,128)}, f32[1024,3072]{1,0:T(8,128)}) fusion(f32[3072]{0:T(1024)S(1)} %bitcast.524, bf16[1024,768]{0,1:T(8,128)(2,1)S(1)} %fusion.24, bf16[768,3072]{1,0:T(8,128)(2,1)} %bitcast.466), kind=kOutput, calls=%fused_computation.8 | convolution fusion | flops 5039456256 | bytes 37761024 | tf_op jit(solution)/shard_map/dot_general | solution.py:284
  429.1 6.0 shard_map.282
  435.1 9.7 fusion.194
  449.8 4.8 convolution_convert_fusion.2
  459.1 7.8 convolution_convert_fusion.3
  467.4 19.1 %add_convert_fusion.1 = bf16[1024,3072]{1,0:T(8,128)(2,1)} fusion(f32[1024,3072]{1,0:T(8,128)} %get-tuple-element.525, f32[1024,3072]{1,0:T(8,128)} %get-tuple-element.593, f32[3072]{0:T(1024)S(1)} %bitcast.525, bf16[1024,768]{0,1:T(8,128)(2,1)} %copy-done.19, bf16[3072,768]{1,0:T(8,128)(2,1)} %bitcast.469), kind=kOutput, calls=%fused_computation.7 | convolution fusion | flops 4879024128 | bytes 37761024 | tf_op jit(solution)/shard_map/dot_general | solution.py:39
  486.5 10.5 %multiply_reduce_fusion.2 = (f32[768]{0:T(1024)S(1)}, f32[1024]{0:T(1024)S(1)}, f32[768]{0:T(1024)S(1)}, f32[1024,768]{0,1:T(8,128)S(1)}) fusion(f32[1024,768]{0,1:T(8,128)S(1)} %copy-done.5, f32[1024]{0:T(1024)S(1)} %fusion.170, f32[1024]{0:T(1024)S(1)} %broadcast_multiply_fusion.1, f32[768]{0:T(1024)S(1)} %mul.423, ...), kind=kOutput, calls=%fused_computation.73 | convolution fusion | flops 4845204480 | bytes 22061056 | tf_op jit(solution)/shard_map/dot_general | solution.py:39
  505.1 3.1 convolution_convert_fusion.6
  508.1 21.6 %collective-permute-done.72 = bf16[1,4,2,192,384]{4,3,2,1,0:T(8,128)(2,1)S(1)} collective-permute-done((bf16[1,4,2,192,384]{4,3,2,1,0:T(8,128)(2,1)S(1)}, bf16[1,4,2,192,384]{4,3,2,1,0:T(8,128)(2,1)S(1)}, u32[]{:S(2)}, u32[]{:S(2)}) %collective-permute-start.72) | collective-permute-done | bytes 1179680 | tf_op jit(solution)/shard_map/ppermute | solution.py:428
  541.9 3.8 collective-permute-done.74
  545.7 11.4 %collective-permute-done.75 = bf16[1,2,192,384]{3,2,1,0:T(8,128)(2,1)S(1)} collective-permute-done((bf16[1,2,192,384]{3,2,1,0:T(8,128)(2,1)S(1)}, bf16[1,2,192,384]{3,2,1,0:T(8,128)(2,1)S(1)}, u32[]{:S(2)}, u32[]{:S(2)}) %collective-permute-start.75) | collective-permute-done | bytes 294944 | tf_op jit(solution)/shard_map/ppermute | solution.py:428
  557.1 6.3 collective-permute-done.76
  569.9 33.8 %shard_map.283 = bf16[3,1024,768]{2,1,0:T(8,128)(2,1)} custom-call(s32[1,6,2,1024]{3,2,1,0:T(2,128)} %reshape.1536.slot_ref, bf16[1024,768]{1,0:T(8,128)(2,1)} %convolution_convert_fusion.9.grad_ref, bf16[1,12,1024,128]{3,2,1,0:T(8,128)(2,1)} %get-tuple-element.238.qk_ref, bf16[1,12,1024,128]{3,2,1,0:T(8,128)(2,1)} %get-tuple-element.239.val_ref, ...), custom_call_target="tpu_custom_call" | custom-call | flops 40000000000 | bytes 20000000 | tf_op jit(solution)/shard_map/pallas_call | solution.py:249
  603.7 3.3 fusion.31
  636.2 5.5 collective-permute-done.88
  659.5 18.5 %collective-permute-done.93 = bf16[1,2,48,384]{3,2,1,0:T(8,128)(2,1)S(1)} collective-permute-done((bf16[1,2,48,384]{3,2,1,0:T(8,128)(2,1)S(1)}, bf16[1,2,48,384]{3,2,1,0:T(8,128)(2,1)S(1)}, u32[]{:S(2)}, u32[]{:S(2)}) %collective-permute-start.93) | collective-permute-done | bytes 73760 | tf_op jit(solution)/shard_map/ppermute | solution.py:428
  678.0 4.8 convolution_convert_fusion.1
  682.8 4.7 convolution_convert_fusion
  687.5 3.6 collective-permute-start.95
  693.4 18.6 %add_convert_fusion = bf16[1024,3072]{1,0:T(8,128)(2,1)} fusion(f32[1024,3072]{1,0:T(8,128)} %get-tuple-element.527, f32[1024,3072]{1,0:T(8,128)} %get-tuple-element.588, f32[3072]{0:T(1024)S(1)} %bitcast.523, bf16[1024,768]{0,1:T(8,128)(2,1)} %copy-done.18, bf16[3072,768]{1,0:T(8,128)(2,1)} %bitcast.465), kind=kOutput, calls=%fused_computation.6 | convolution fusion | flops 4879024128 | bytes 37761024 | tf_op jit(solution)/shard_map/dot_general | solution.py:39
  714.0 9.9 multiply_reduce_fusion.1
  723.9 3.3 convolution_convert_fusion.5
  729.3 3.3 collective-permute-start.99
  749.1 15.4 %collective-permute-done.102 = bf16[1,4,2,192,384]{4,3,2,1,0:T(8,128)(2,1)} collective-permute-done((bf16[1,4,2,192,384]{4,3,2,1,0:T(8,128)(2,1)S(1)}, bf16[1,4,2,192,384]{4,3,2,1,0:T(8,128)(2,1)}, u32[]{:S(2)}, u32[]{:S(2)}) %collective-permute-start.102) | collective-permute-done | bytes 1179680 | tf_op jit(solution)/shard_map/ppermute | solution.py:428
  783.1 12.3 %collective-permute-done.140 = f32[16896]{0:T(1024)S(1)} collective-permute-done((f32[16896]{0:T(1024)S(1)}, f32[16896]{0:T(1024)S(1)}, u32[]{:S(2)}, u32[]{:S(2)}) %collective-permute-start.140) | collective-permute-done | bytes 67616 | tf_op jit(solution)/shard_map/ppermute | solution.py:428
  809.4 6.5 collective-permute-done.107
  815.9 9.5 collective-permute-done.108
  834.7 33.4 %shard_map.284 = bf16[3,1024,768]{2,1,0:T(8,128)(2,1)} custom-call(s32[1,6,2,1024]{3,2,1,0:T(2,128)} %reshape.1536.slot_ref, bf16[1024,768]{1,0:T(8,128)(2,1)} %convolution_convert_fusion.8.grad_ref, bf16[1,12,1024,128]{3,2,1,0:T(8,128)(2,1)} %get-tuple-element.274.qk_ref, bf16[1,12,1024,128]{3,2,1,0:T(8,128)(2,1)} %get-tuple-element.275.val_ref, ...), custom_call_target="tpu_custom_call" | custom-call | flops 40000000000 | bytes 20000000 | tf_op jit(solution)/shard_map/pallas_call | solution.py:249
  868.2 3.3 fusion.26
  881.7 3.6 collective-permute-start.118
  886.6 3.3 add_add_fusion.4
  909.0 4.3 collective-permute-start.121
  915.3 3.5 collective-permute-start.114
  924.0 5.0 collective-permute-done.117
  944.1 12.9 %collective-permute-done.124 = bf16[3,4,2,48,384]{4,3,0,1,2:T(8,128)(2,1)S(1)} collective-permute-done((bf16[3,4,2,48,384]{4,3,0,1,2:T(8,128)(2,1)S(1)}, bf16[3,4,2,48,384]{4,3,0,1,2:T(8,128)(2,1)S(1)}, u32[]{:S(2)}, u32[]{:S(2)}) %collective-permute-start.124) | collective-permute-done | bytes 884768 | tf_op jit(solution)/shard_map/ppermute | solution.py:428
  958.6 3.3 collective-permute-start.144
  967.1 3.8 collective-permute-start.127
  974.7 4.3 collective-permute-done.126
  982.7 3.5 collective-permute-start.130
  (814 shorter events, 366.2 us)
Async XLA Ops:
  2.1 37.6 %collective-permute-start.12 = (bf16[2,1152]{1,0:T(2,128)(2,1)}, bf16[2,1152]{1,0:T(2,128)(2,1)}, u32[]{:S(2)}, u32[]{:S(2)}) collective-permute-start(bf16[2,1152]{1,0:T(2,128)(2,1)} %concatenate.216), channel_id=1, source_target_pairs={{0,1},{1,0},{2,3},{3,2},{4,5},{5,4},{6,7},{7,6},{8,9},{9,8},{10,11... | collective-permute-start | bytes 13832 | tf_op jit(solution)/shard_map/ppermute | solution.py:428
  3.3 37.8 %collective-permute-start.13 = (bf16[2,1152]{1,0:T(2,128)(2,1)}, bf16[2,1152]{1,0:T(2,128)(2,1)}, u32[]{:S(2)}, u32[]{:S(2)}) collective-permute-start(bf16[2,1152]{1,0:T(2,128)(2,1)} %concatenate.216), channel_id=1, source_target_pairs={{0,2},{1,3},{2,4},{3,5},{4,6},{5,7},{6,0},{7,1},{8,10},{9,11},{10,... | collective-permute-start | bytes 13832 | tf_op jit(solution)/shard_map/ppermute | solution.py:428
  4.6 38.8 %collective-permute-start.14 = (bf16[2,1152]{1,0:T(2,128)(2,1)}, bf16[2,1152]{1,0:T(2,128)(2,1)}, u32[]{:S(2)}, u32[]{:S(2)}) collective-permute-start(bf16[2,1152]{1,0:T(2,128)(2,1)} %concatenate.216), channel_id=1, source_target_pairs={{0,3},{1,2},{2,5},{3,4},{4,7},{5,6},{6,1},{7,0},{8,11},{9,10},{10,... | collective-permute-start | bytes 13832 | tf_op jit(solution)/shard_map/ppermute | solution.py:428
  4.6 40.9 %collective-permute-start.15 = (bf16[2,1152]{1,0:T(2,128)(2,1)}, bf16[2,1152]{1,0:T(2,128)(2,1)}, u32[]{:S(2)}, u32[]{:S(2)}) collective-permute-start(bf16[2,1152]{1,0:T(2,128)(2,1)} %concatenate.216), channel_id=1, source_target_pairs={{0,4},{1,5},{2,6},{3,7},{4,0},{5,1},{6,2},{7,3},{8,12},{9,13},{10,... | collective-permute-start | bytes 13832 | tf_op jit(solution)/shard_map/ppermute | solution.py:428
  5.9 42.2 %collective-permute-start.16 = (bf16[2,1152]{1,0:T(2,128)(2,1)}, bf16[2,1152]{1,0:T(2,128)(2,1)}, u32[]{:S(2)}, u32[]{:S(2)}) collective-permute-start(bf16[2,1152]{1,0:T(2,128)(2,1)} %concatenate.216), channel_id=1, source_target_pairs={{0,5},{1,4},{2,7},{3,6},{4,1},{5,0},{6,3},{7,2},{8,13},{9,12},{10,... | collective-permute-start | bytes 13832 | tf_op jit(solution)/shard_map/ppermute | solution.py:428
  50.0 46.4 %collective-permute-start.6 = (bf16[96,384]{1,0:T(8,128)(2,1)}, bf16[96,384]{1,0:T(8,128)(2,1)}, u32[]{:S(2)}, u32[]{:S(2)}) collective-permute-start(bf16[96,384]{1,0:T(8,128)(2,1)} %fusion.253), channel_id=1, source_target_pairs={{0,2},{1,3},{2,4},{3,5},{4,6},{5,7},{6,0},{7,1},{8,10},{9,11},{10,... | collective-permute-start | bytes 221192 | tf_op jit(solution)/shard_map/ppermute | solution.py:428
  51.1 48.4 %collective-permute-start.7 = (bf16[96,384]{1,0:T(8,128)(2,1)}, bf16[96,384]{1,0:T(8,128)(2,1)}, u32[]{:S(2)}, u32[]{:S(2)}) collective-permute-start(bf16[96,384]{1,0:T(8,128)(2,1)} %fusion.253), channel_id=1, source_target_pairs={{0,4},{1,5},{2,6},{3,7},{4,0},{5,1},{6,2},{7,3},{8,12},{9,13},{10,... | collective-permute-start | bytes 221192 | tf_op jit(solution)/shard_map/ppermute | solution.py:428
  55.2 44.6 %collective-permute-start.8 = (bf16[96,384]{1,0:T(8,128)(2,1)}, bf16[96,384]{1,0:T(8,128)(2,1)}, u32[]{:S(2)}, u32[]{:S(2)}) collective-permute-start(bf16[96,384]{1,0:T(8,128)(2,1)} %fusion.253), channel_id=1, source_target_pairs={{0,6},{1,7},{2,0},{3,1},{4,2},{5,3},{6,4},{7,5},{8,14},{9,15},{10,... | collective-permute-start | bytes 221192 | tf_op jit(solution)/shard_map/ppermute | solution.py:428
  71.5 49.6 %collective-permute-start.3 = (bf16[4,96,1152]{2,1,0:T(8,128)(2,1)}, bf16[4,96,1152]{2,1,0:T(8,128)(2,1)}, u32[]{:S(2)}, u32[]{:S(2)}) collective-permute-start(bf16[4,96,1152]{2,1,0:T(8,128)(2,1)} %pad_maximum_fusion.2.refs_0_), channel_id=1, source_target_pairs={{0,8},{1,9},{2,10},{3,11},{4,12},{5,13},{6,14},{7,15},{8,0},{9,1},... | collective-permute-start | bytes 2654216 | tf_op jit(solution)/shard_map/ppermute | solution.py:428
  93.7 27.4 %collective-permute-start.5 = (bf16[4,96,1152]{2,1,0:T(8,128)(2,1)}, bf16[4,96,1152]{2,1,0:T(8,128)(2,1)}, u32[]{:S(2)}, u32[]{:S(2)}) collective-permute-start(bf16[4,96,1152]{2,1,0:T(8,128)(2,1)} %collective-permute-done.4.refs_2_), channel_id=1, source_target_pairs={{0,8},{1,9},{2,10},{3,11},{4,12},{5,13},{6,14},{7,15},{8,0},{9,1},... | collective-permute-start | bytes 2654216 | tf_op jit(solution)/shard_map/ppermute | solution.py:428
  104.0 27.9 %collective-permute-start.21 = (bf16[192,384]{1,0:T(8,128)(2,1)}, bf16[192,384]{1,0:T(8,128)(2,1)}, u32[]{:S(2)}, u32[]{:S(2)}) collective-permute-start(bf16[192,384]{1,0:T(8,128)(2,1)} %fusion.251), channel_id=1, source_target_pairs={{0,2},{1,3},{2,4},{3,5},{4,6},{5,7},{6,0},{7,1},{8,10},{9,11},{10,... | collective-permute-start | bytes 442376 | tf_op jit(solution)/shard_map/ppermute | solution.py:428
  109.4 23.1 %collective-permute-start.22 = (bf16[192,384]{1,0:T(8,128)(2,1)}, bf16[192,384]{1,0:T(8,128)(2,1)}, u32[]{:S(2)}, u32[]{:S(2)}) collective-permute-start(bf16[192,384]{1,0:T(8,128)(2,1)} %fusion.251), channel_id=1, source_target_pairs={{0,4},{1,5},{2,6},{3,7},{4,0},{5,1},{6,2},{7,3},{8,12},{9,13},{10,... | collective-permute-start | bytes 442376 | tf_op jit(solution)/shard_map/ppermute | solution.py:428
  121.1 34.5 %collective-permute-start.29 = (bf16[96,1152]{1,0:T(8,128)(2,1)}, bf16[96,1152]{1,0:T(8,128)(2,1)}, u32[]{:S(2)}, u32[]{:S(2)}) collective-permute-start(bf16[96,1152]{1,0:T(8,128)(2,1)} %fusion.250), channel_id=1, source_target_pairs={{0,2},{1,3},{2,4},{3,5},{4,6},{5,7},{6,0},{7,1},{8,10},{9,11},{10,... | collective-permute-start | bytes 663560 | tf_op jit(solution)/shard_map/ppermute | solution.py:428
  121.1 37.1 %collective-permute-start.30 = (bf16[96,1152]{1,0:T(8,128)(2,1)}, bf16[96,1152]{1,0:T(8,128)(2,1)}, u32[]{:S(2)}, u32[]{:S(2)}) collective-permute-start(bf16[96,1152]{1,0:T(8,128)(2,1)} %fusion.250), channel_id=1, source_target_pairs={{0,4},{1,5},{2,6},{3,7},{4,0},{5,1},{6,2},{7,3},{8,12},{9,13},{10,... | collective-permute-start | bytes 663560 | tf_op jit(solution)/shard_map/ppermute | solution.py:428
  132.0 26.5 %collective-permute-start.31 = (bf16[96,1152]{1,0:T(8,128)(2,1)S(1)}, bf16[96,1152]{1,0:T(8,128)(2,1)S(1)}, u32[]{:S(2)}, u32[]{:S(2)}) collective-permute-start(bf16[96,1152]{1,0:T(8,128)(2,1)S(1)} %copy-done.71), channel_id=1, source_target_pairs={{0,6},{1,7},{2,0},{3,1},{4,2},{5,3},{6,4},{7,5},{8,14},{9,15},{10,... | collective-permute-start | bytes 663560 | tf_op jit(solution)/shard_map/ppermute | solution.py:428
  141.6 51.5 %collective-permute-start.24 = (bf16[4,96,384]{2,1,0:T(8,128)(2,1)S(1)}, bf16[4,96,384]{2,1,0:T(8,128)(2,1)S(1)}, u32[]{:S(2)}, u32[]{:S(2)}) collective-permute-start(bf16[4,96,384]{2,1,0:T(8,128)(2,1)S(1)} %pad_maximum_fusion.8.refs_0_), channel_id=1, source_target_pairs={{0,8},{1,9},{2,10},{3,11},{4,12},{5,13},{6,14},{7,15},{8,0},{9,1},... | collective-permute-start | bytes 884744 | tf_op jit(solution)/shard_map/ppermute | solution.py:428
  152.4 41.9 %collective-permute-start.26 = (bf16[4,48,1536]{2,1,0:T(8,128)(2,1)}, bf16[4,48,1536]{2,1,0:T(8,128)(2,1)S(1)}, u32[]{:S(2)}, u32[]{:S(2)}) collective-permute-start(bf16[4,48,1536]{2,1,0:T(8,128)(2,1)} %pad_maximum_fusion.4.refs_0_), channel_id=1, source_target_pairs={{0,16},{1,17},{2,18},{3,19},{4,20},{5,21},{6,22},{7,23},{8,24},{9,... | collective-permute-start | bytes 1769480 | tf_op jit(solution)/shard_map/ppermute | solution.py:428
  155.6 39.6 %collective-permute-start.25 = (bf16[4,96,384]{2,1,0:T(8,128)(2,1)S(1)}, bf16[4,96,384]{2,1,0:T(8,128)(2,1)S(1)}, u32[]{:S(2)}, u32[]{:S(2)}) collective-permute-start(bf16[4,96,384]{2,1,0:T(8,128)(2,1)S(1)} %collective-permute-done.19.refs_2_), channel_id=1, source_target_pairs={{0,8},{1,9},{2,10},{3,11},{4,12},{5,13},{6,14},{7,15},{8,0},{9,1},... | collective-permute-start | bytes 884744 | tf_op jit(solution)/shard_map/ppermute | solution.py:428
  158.2 37.1 %collective-permute-start.27 = (bf16[4,48,1536]{2,1,0:T(8,128)(2,1)}, bf16[4,48,1536]{2,1,0:T(8,128)(2,1)S(1)}, u32[]{:S(2)}, u32[]{:S(2)}) collective-permute-start(bf16[4,48,1536]{2,1,0:T(8,128)(2,1)} %collective-permute-done.20.refs_2_), channel_id=1, source_target_pairs={{0,16},{1,17},{2,18},{3,19},{4,20},{5,21},{6,22},{7,23},{8,24},{9,... | collective-permute-start | bytes 1769480 | tf_op jit(solution)/shard_map/ppermute | solution.py:428
  158.5 36.9 %collective-permute-start.28 = (bf16[4,192,384]{2,1,0:T(8,128)(2,1)}, bf16[4,192,384]{2,1,0:T(8,128)(2,1)}, u32[]{:S(2)}, u32[]{:S(2)}) collective-permute-start(bf16[4,192,384]{2,1,0:T(8,128)(2,1)} %pad_maximum_fusion.5.refs_0_), channel_id=1, source_target_pairs={{0,1},{1,0},{2,3},{3,2},{4,5},{5,4},{6,7},{7,6},{8,9},{9,8},{10,11... | collective-permute-start | bytes 1769480 | tf_op jit(solution)/shard_map/ppermute | solution.py:428
  193.1 28.6 %collective-permute-start.39 = (bf16[96,384]{1,0:T(8,128)(2,1)}, bf16[96,384]{1,0:T(8,128)(2,1)}, u32[]{:S(2)}, u32[]{:S(2)}) collective-permute-start(bf16[96,384]{1,0:T(8,128)(2,1)} %fusion.249), channel_id=1, source_target_pairs={{0,2},{1,3},{2,4},{3,5},{4,6},{5,7},{6,0},{7,1},{8,10},{9,11},{10,... | collective-permute-start | bytes 221192 | tf_op jit(solution)/shard_map/ppermute | solution.py:428
  214.9 48.1 %collective-permute-start.43 = (bf16[48,1536]{1,0:T(8,128)(2,1)S(1)}, bf16[48,1536]{1,0:T(8,128)(2,1)S(1)}, u32[]{:S(2)}, u32[]{:S(2)}) collective-permute-start(bf16[48,1536]{1,0:T(8,128)(2,1)S(1)} %copy-done.75), channel_id=1, source_target_pairs={{0,4},{1,5},{2,6},{3,7},{4,0},{5,1},{6,2},{7,3},{8,12},{9,13},{10,... | collective-permute-start | bytes 442376 | tf_op jit(solution)/shard_map/ppermute | solution.py:428
  221.7 41.3 %collective-permute-start.44 = (bf16[48,1536]{1,0:T(8,128)(2,1)S(1)}, bf16[48,1536]{1,0:T(8,128)(2,1)S(1)}, u32[]{:S(2)}, u32[]{:S(2)}) collective-permute-start(bf16[48,1536]{1,0:T(8,128)(2,1)S(1)} %copy-done.75), channel_id=1, source_target_pairs={{0,6},{1,7},{2,0},{3,1},{4,2},{5,3},{6,4},{7,5},{8,14},{9,15},{10,... | collective-permute-start | bytes 442376 | tf_op jit(solution)/shard_map/ppermute | solution.py:428
  224.1 41.1 %collective-permute-start.36 = (bf16[4,192,384]{2,1,0:T(8,128)(2,1)}, bf16[4,192,384]{2,1,0:T(8,128)(2,1)}, u32[]{:S(2)}, u32[]{:S(2)}) collective-permute-start(bf16[4,192,384]{2,1,0:T(8,128)(2,1)} %pad_maximum_fusion.5.refs_0_), channel_id=1, source_target_pairs={{0,16},{1,17},{2,18},{3,19},{4,20},{5,21},{6,22},{7,23},{8,24},{9,... | collective-permute-start | bytes 1769480 | tf_op jit(solution)/shard_map/ppermute | solution.py:428
  225.3 39.9 %collective-permute-start.37 = (bf16[4,192,384]{2,1,0:T(8,128)(2,1)}, bf16[4,192,384]{2,1,0:T(8,128)(2,1)}, u32[]{:S(2)}, u32[]{:S(2)}) collective-permute-start(bf16[4,192,384]{2,1,0:T(8,128)(2,1)} %collective-permute-done.28.refs_2_), channel_id=1, source_target_pairs={{0,16},{1,17},{2,18},{3,19},{4,20},{5,21},{6,22},{7,23},{8,24},{9,... | collective-permute-start | bytes 1769480 | tf_op jit(solution)/shard_map/ppermute | solution.py:428
  225.5 39.7 %collective-permute-start.38 = (bf16[4,96,1152]{2,1,0:T(8,128)(2,1)}, bf16[4,96,1152]{2,1,0:T(8,128)(2,1)}, u32[]{:S(2)}, u32[]{:S(2)}) collective-permute-start(bf16[4,96,1152]{2,1,0:T(8,128)(2,1)} %pad_maximum_fusion.3.refs_0_), channel_id=1, source_target_pairs={{0,1},{1,0},{2,3},{3,2},{4,5},{5,4},{6,7},{7,6},{8,9},{9,8},{10,11... | collective-permute-start | bytes 2654216 | tf_op jit(solution)/shard_map/ppermute | solution.py:428
  262.9 41.9 %collective-permute-start.55 = (bf16[192,384]{1,0:T(8,128)(2,1)}, bf16[192,384]{1,0:T(8,128)(2,1)}, u32[]{:S(2)}, u32[]{:S(2)}) collective-permute-start(bf16[192,384]{1,0:T(8,128)(2,1)} %fusion.247), channel_id=1, source_target_pairs={{0,2},{1,3},{2,4},{3,5},{4,6},{5,7},{6,0},{7,1},{8,10},{9,11},{10,... | collective-permute-start | bytes 442376 | tf_op jit(solution)/shard_map/ppermute | solution.py:428
  273.8 40.0 %collective-permute-start.56 = (bf16[192,384]{1,0:T(8,128)(2,1)}, bf16[192,384]{1,0:T(8,128)(2,1)}, u32[]{:S(2)}, u32[]{:S(2)}) collective-permute-start(bf16[192,384]{1,0:T(8,128)(2,1)} %fusion.247), channel_id=1, source_target_pairs={{0,4},{1,5},{2,6},{3,7},{4,0},{5,1},{6,2},{7,3},{8,12},{9,13},{10,... | collective-permute-start | bytes 442376 | tf_op jit(solution)/shard_map/ppermute | solution.py:428
  313.8 43.3 %collective-permute-start.58 = (bf16[4,48,1536]{2,1,0:T(8,128)(2,1)S(1)}, bf16[4,48,1536]{2,1,0:T(8,128)(2,1)}, u32[]{:S(2)}, u32[]{:S(2)}) collective-permute-start(bf16[4,48,1536]{2,1,0:T(8,128)(2,1)S(1)} %copy-done.27), channel_id=1, source_target_pairs={{0,16},{1,17},{2,18},{3,19},{4,20},{5,21},{6,22},{7,23},{8,24},{9,... | collective-permute-start | bytes 1769480 | tf_op jit(solution)/shard_map/ppermute | solution.py:428
  315.0 47.5 %collective-permute-start.61 = (bf16[4,48,1536]{2,1,0:T(8,128)(2,1)S(1)}, bf16[4,48,1536]{2,1,0:T(8,128)(2,1)}, u32[]{:S(2)}, u32[]{:S(2)}) collective-permute-start(bf16[4,48,1536]{2,1,0:T(8,128)(2,1)S(1)} %copy-done.27), channel_id=1, source_target_pairs={{0,8},{1,9},{2,10},{3,11},{4,12},{5,13},{6,14},{7,15},{8,0},{9,1},... | collective-permute-start | bytes 1769480 | tf_op jit(solution)/shard_map/ppermute | solution.py:428
  315.5 42.9 %collective-permute-start.59 = (bf16[4,48,1536]{2,1,0:T(8,128)(2,1)}, bf16[4,48,1536]{2,1,0:T(8,128)(2,1)}, u32[]{:S(2)}, u32[]{:S(2)}) collective-permute-start(bf16[4,48,1536]{2,1,0:T(8,128)(2,1)} %collective-permute-done.54.refs_2_), channel_id=1, source_target_pairs={{0,16},{1,17},{2,18},{3,19},{4,20},{5,21},{6,22},{7,23},{8,24},{9,... | collective-permute-start | bytes 1769480 | tf_op jit(solution)/shard_map/ppermute | solution.py:428
  315.8 48.4 %collective-permute-start.62 = (bf16[4,48,1536]{2,1,0:T(8,128)(2,1)}, bf16[4,48,1536]{2,1,0:T(8,128)(2,1)}, u32[]{:S(2)}, u32[]{:S(2)}) collective-permute-start(bf16[4,48,1536]{2,1,0:T(8,128)(2,1)} %collective-permute-done.54.refs_2_), channel_id=1, source_target_pairs={{0,8},{1,9},{2,10},{3,11},{4,12},{5,13},{6,14},{7,15},{8,0},{9,1},... | collective-permute-start | bytes 1769480 | tf_op jit(solution)/shard_map/ppermute | solution.py:428
  318.1 40.3 %collective-permute-start.60 = (bf16[4,192,384]{2,1,0:T(8,128)(2,1)}, bf16[4,192,384]{2,1,0:T(8,128)(2,1)}, u32[]{:S(2)}, u32[]{:S(2)}) collective-permute-start(bf16[4,192,384]{2,1,0:T(8,128)(2,1)} %pad_maximum_fusion.7.refs_0_), channel_id=1, source_target_pairs={{0,1},{1,0},{2,3},{3,2},{4,5},{5,4},{6,7},{7,6},{8,9},{9,8},{10,11... | collective-permute-start | bytes 1769480 | tf_op jit(solution)/shard_map/ppermute | solution.py:428
  362.6 21.9 %collective-permute-start.66 = (bf16[4,192,384]{2,1,0:T(8,128)(2,1)}, bf16[4,192,384]{2,1,0:T(8,128)(2,1)S(1)}, u32[]{:S(2)}, u32[]{:S(2)}) collective-permute-start(bf16[4,192,384]{2,1,0:T(8,128)(2,1)} %collective-permute-done.60.refs_2_), channel_id=1, source_target_pairs={{0,16},{1,17},{2,18},{3,19},{4,20},{5,21},{6,22},{7,23},{8,24},{9,... | collective-permute-start | bytes 1769480 | tf_op jit(solution)/shard_map/ppermute | solution.py:428
  364.2 63.7 %collective-permute-start.67 = (bf16[4,192,384]{2,1,0:T(8,128)(2,1)}, bf16[4,192,384]{2,1,0:T(8,128)(2,1)S(1)}, u32[]{:S(2)}, u32[]{:S(2)}) collective-permute-start(bf16[4,192,384]{2,1,0:T(8,128)(2,1)} %pad_maximum_fusion.7.refs_0_), channel_id=1, source_target_pairs={{0,8},{1,9},{2,10},{3,11},{4,12},{5,13},{6,14},{7,15},{8,0},{9,1},... | collective-permute-start | bytes 1769480 | tf_op jit(solution)/shard_map/ppermute | solution.py:428
  371.9 56.0 %collective-permute-start.68 = (bf16[4,192,384]{2,1,0:T(8,128)(2,1)}, bf16[4,192,384]{2,1,0:T(8,128)(2,1)S(1)}, u32[]{:S(2)}, u32[]{:S(2)}) collective-permute-start(bf16[4,192,384]{2,1,0:T(8,128)(2,1)} %collective-permute-done.60.refs_2_), channel_id=1, source_target_pairs={{0,8},{1,9},{2,10},{3,11},{4,12},{5,13},{6,14},{7,15},{8,0},{9,1},... | collective-permute-start | bytes 1769480 | tf_op jit(solution)/shard_map/ppermute | solution.py:428
  384.5 43.5 %collective-permute-start.69 = (bf16[4,192,384]{2,1,0:T(8,128)(2,1)}, bf16[4,192,384]{2,1,0:T(8,128)(2,1)S(1)}, u32[]{:S(2)}, u32[]{:S(2)}) collective-permute-start(bf16[4,192,384]{2,1,0:T(8,128)(2,1)} %collective-permute-done.65.refs_4_), channel_id=1, source_target_pairs={{0,8},{1,9},{2,10},{3,11},{4,12},{5,13},{6,14},{7,15},{8,0},{9,1},... | collective-permute-start | bytes 1769480 | tf_op jit(solution)/shard_map/ppermute | solution.py:428
  385.8 42.2 %collective-permute-start.70 = (bf16[4,192,384]{2,1,0:T(8,128)(2,1)S(1)}, bf16[4,192,384]{2,1,0:T(8,128)(2,1)}, u32[]{:S(2)}, u32[]{:S(2)}) collective-permute-start(bf16[4,192,384]{2,1,0:T(8,128)(2,1)S(1)} %collective-permute-done.66.refs_6_), channel_id=1, source_target_pairs={{0,8},{1,9},{2,10},{3,11},{4,12},{5,13},{6,14},{7,15},{8,0},{9,1},... | collective-permute-start | bytes 1769480 | tf_op jit(solution)/shard_map/ppermute | solution.py:428
  499.9 29.8 %collective-permute-start.73 = (bf16[4,2,2,48,1536]{4,3,2,1,0:T(8,128)(2,1)S(1)}, bf16[4,2,2,48,1536]{4,3,2,1,0:T(8,128)(2,1)S(1)}, u32[]{:S(2)}, u32[]{:S(2)}) collective-permute-start(bf16[4,2,2,48,1536]{4,3,2,1,0:T(8,128)(2,1)S(1)} %bitcast.530), channel_id=1, source_target_pairs={{0,8},{1,9},{2,10},{3,11},{4,12},{5,13},{6,14},{7,15},{8,0},{9,1},... | collective-permute-start | bytes 7077896 | tf_op jit(solution)/shard_map/ppermute | solution.py:428
  502.6 27.2 %collective-permute-start.72 = (bf16[1,4,2,192,384]{4,3,2,1,0:T(8,128)(2,1)S(1)}, bf16[1,4,2,192,384]{4,3,2,1,0:T(8,128)(2,1)S(1)}, u32[]{:S(2)}, u32[]{:S(2)}) collective-permute-start(bf16[1,4,2,192,384]{4,3,2,1,0:T(8,128)(2,1)S(1)} %fusion.53), channel_id=1, source_target_pairs={{0,1},{1,0},{2,3},{3,2},{4,5},{5,4},{6,7},{7,6},{8,9},{9,8},{10,11... | collective-permute-start | bytes 3538952 | tf_op jit(solution)/shard_map/ppermute | solution.py:428
  530.7 32.8 %collective-permute-start.77 = (bf16[1,4,2,48,1536]{4,3,2,1,0:T(8,128)(2,1)S(1)}, bf16[1,4,2,48,1536]{4,3,2,1,0:T(8,128)(2,1)S(1)}, u32[]{:S(2)}, u32[]{:S(2)}) collective-permute-start(bf16[1,4,2,48,1536]{4,3,2,1,0:T(8,128)(2,1)S(1)} %fusion.54), channel_id=1, source_target_pairs={{0,16},{1,17},{2,18},{3,19},{4,20},{5,21},{6,22},{7,23},{8,24},{9,... | collective-permute-start | bytes 3538952 | tf_op jit(solution)/shard_map/ppermute | solution.py:428
  533.0 30.4 %collective-permute-start.78 = (bf16[4,2,2,48,384]{4,3,2,1,0:T(8,128)(2,1)S(1)}, bf16[4,2,2,48,384]{4,3,2,1,0:T(8,128)(2,1)S(1)}, u32[]{:S(2)}, u32[]{:S(2)}) collective-permute-start(bf16[4,2,2,48,384]{4,3,2,1,0:T(8,128)(2,1)S(1)} %bitcast.532), channel_id=1, source_target_pairs={{0,8},{1,9},{2,10},{3,11},{4,12},{5,13},{6,14},{7,15},{8,0},{9,1},... | collective-permute-start | bytes 1769480 | tf_op jit(solution)/shard_map/ppermute | solution.py:428
  538.5 25.0 %collective-permute-start.76 = (bf16[1,2,192,384]{3,2,1,0:T(8,128)(2,1)S(1)}, bf16[1,2,192,384]{3,2,1,0:T(8,128)(2,1)S(1)}, u32[]{:S(2)}, u32[]{:S(2)}) collective-permute-start(bf16[1,2,192,384]{3,2,1,0:T(8,128)(2,1)S(1)} %get-tuple-element.531), channel_id=1, source_target_pairs={{0,6},{1,7},{2,0},{3,1},{4,2},{5,3},{6,4},{7,5},{8,14},{9,15},{10,... | collective-permute-start | bytes 884744 | tf_op jit(solution)/shard_map/ppermute | solution.py:428
  563.6 40.1 %collective-permute-start.79 = (bf16[1,2,192,384]{3,2,1,0:T(8,128)(2,1)S(1)}, bf16[1,2,192,384]{3,2,1,0:T(8,128)(2,1)S(1)}, u32[]{:S(2)}, u32[]{:S(2)}) collective-permute-start(bf16[1,2,192,384]{3,2,1,0:T(8,128)(2,1)S(1)} %fusion.89), channel_id=1, source_target_pairs={{0,16},{1,17},{2,18},{3,19},{4,20},{5,21},{6,22},{7,23},{8,24},{9,... | collective-permute-start | bytes 884744 | tf_op jit(solution)/shard_map/ppermute | solution.py:428
  566.5 37.2 %collective-permute-start.80 = (bf16[1,4,48,1536]{3,2,1,0:T(8,128)(2,1)}, bf16[1,4,48,1536]{3,2,1,0:T(8,128)(2,1)}, u32[]{:S(2)}, u32[]{:S(2)}) collective-permute-start(bf16[1,4,48,1536]{3,2,1,0:T(8,128)(2,1)} %fusion.82), channel_id=1, source_target_pairs={{0,1},{1,0},{2,3},{3,2},{4,5},{5,4},{6,7},{7,6},{8,9},{9,8},{10,11... | collective-permute-start | bytes 1769480 | tf_op jit(solution)/shard_map/ppermute | solution.py:428
  568.7 35.0 %collective-permute-start.81 = (bf16[1,4,2,48,384]{4,3,2,1,0:T(8,128)(2,1)}, bf16[1,4,2,48,384]{4,3,2,1,0:T(8,128)(2,1)}, u32[]{:S(2)}, u32[]{:S(2)}) collective-permute-start(bf16[1,4,2,48,384]{4,3,2,1,0:T(8,128)(2,1)} %fusion.97), channel_id=1, source_target_pairs={{0,1},{1,0},{2,3},{3,2},{4,5},{5,4},{6,7},{7,6},{8,9},{9,8},{10,11... | collective-permute-start | bytes 884744 | tf_op jit(solution)/shard_map/ppermute | solution.py:428
  623.1 29.0 %collective-permute-start.89 = (bf16[4,2,2,48,384]{4,3,0,1,2:T(8,128)(2,1)S(1)}, bf16[4,2,2,48,384]{4,3,0,1,2:T(8,128)(2,1)S(1)}, u32[]{:S(2)}, u32[]{:S(2)}) collective-permute-start(bf16[4,2,2,48,384]{4,3,0,1,2:T(8,128)(2,1)S(1)} %copy.446), channel_id=1, source_target_pairs={{0,8},{1,9},{2,10},{3,11},{4,12},{5,13},{6,14},{7,15},{8,0},{9,1},... | collective-permute-start | bytes 1769480 | tf_op jit(solution)/shard_map/ppermute | solution.py:428
  625.8 26.2 %collective-permute-start.90 = (bf16[4,2,2,48,384]{4,3,0,1,2:T(8,128)(2,1)S(1)}, bf16[4,2,2,48,384]{4,3,0,1,2:T(8,128)(2,1)S(1)}, u32[]{:S(2)}, u32[]{:S(2)}) collective-permute-start(bf16[4,2,2,48,384]{4,3,0,1,2:T(8,128)(2,1)S(1)} %copy.447), channel_id=1, source_target_pairs={{0,8},{1,9},{2,10},{3,11},{4,12},{5,13},{6,14},{7,15},{8,0},{9,1},... | collective-permute-start | bytes 1769480 | tf_op jit(solution)/shard_map/ppermute | solution.py:428
  626.0 26.1 %collective-permute-start.91 = (bf16[4,2,2,48,384]{4,3,0,1,2:T(8,128)(2,1)S(1)}, bf16[4,2,2,48,384]{4,3,0,1,2:T(8,128)(2,1)S(1)}, u32[]{:S(2)}, u32[]{:S(2)}) collective-permute-start(bf16[4,2,2,48,384]{4,3,0,1,2:T(8,128)(2,1)S(1)} %copy.448), channel_id=1, source_target_pairs={{0,8},{1,9},{2,10},{3,11},{4,12},{5,13},{6,14},{7,15},{8,0},{9,1},... | collective-permute-start | bytes 1769480 | tf_op jit(solution)/shard_map/ppermute | solution.py:428
  654.2 23.8 %collective-permute-start.92 = (bf16[1,48,1536]{2,1,0:T(8,128)(2,1)S(1)}, bf16[1,48,1536]{2,1,0:T(8,128)(2,1)S(1)}, u32[]{:S(2)}, u32[]{:S(2)}) collective-permute-start(bf16[1,48,1536]{2,1,0:T(8,128)(2,1)S(1)} %fusion.107), channel_id=1, source_target_pairs={{0,16},{1,17},{2,18},{3,19},{4,20},{5,21},{6,22},{7,23},{8,24},{9,... | collective-permute-start | bytes 442376 | tf_op jit(solution)/shard_map/ppermute | solution.py:428
  687.5 26.4 %collective-permute-start.95 = (bf16[1,96,1536]{2,1,0:T(8,128)(2,1)S(1)}, bf16[1,96,1536]{2,1,0:T(8,128)(2,1)}, u32[]{:S(2)}, u32[]{:S(2)}) collective-permute-start(bf16[1,96,1536]{2,1,0:T(8,128)(2,1)S(1)} %bitcast.483), channel_id=1, source_target_pairs={{0,8},{1,9},{2,10},{3,11},{4,12},{5,13},{6,14},{7,15},{8,0},{9,1},... | collective-permute-start | bytes 884744 | tf_op jit(solution)/shard_map/ppermute | solution.py:428
  691.2 22.7 %collective-permute-start.96 = (bf16[1,96,384]{2,1,0:T(8,128)(2,1)S(1)}, bf16[1,96,384]{2,1,0:T(8,128)(2,1)}, u32[]{:S(2)}, u32[]{:S(2)}) collective-permute-start(bf16[1,96,384]{2,1,0:T(8,128)(2,1)S(1)} %bitcast.509), channel_id=1, source_target_pairs={{0,8},{1,9},{2,10},{3,11},{4,12},{5,13},{6,14},{7,15},{8,0},{9,1},... | collective-permute-start | bytes 221192 | tf_op jit(solution)/shard_map/ppermute | solution.py:428
  737.7 26.8 %collective-permute-start.102 = (bf16[1,4,2,192,384]{4,3,2,1,0:T(8,128)(2,1)S(1)}, bf16[1,4,2,192,384]{4,3,2,1,0:T(8,128)(2,1)}, u32[]{:S(2)}, u32[]{:S(2)}) collective-permute-start(bf16[1,4,2,192,384]{4,3,2,1,0:T(8,128)(2,1)S(1)} %fusion.55), channel_id=1, source_target_pairs={{0,1},{1,0},{2,3},{3,2},{4,5},{5,4},{6,7},{7,6},{8,9},{9,8},{10,11... | collective-permute-start | bytes 3538952 | tf_op jit(solution)/shard_map/ppermute | solution.py:428
  739.2 25.3 %collective-permute-start.103 = (bf16[4,2,2,48,1536]{4,3,0,1,2:T(8,128)(2,1)S(1)}, bf16[4,2,2,48,1536]{4,3,0,1,2:T(8,128)(2,1)S(1)}, u32[]{:S(2)}, u32[]{:S(2)}) collective-permute-start(bf16[4,2,2,48,1536]{4,3,0,1,2:T(8,128)(2,1)S(1)} %copy.453), channel_id=1, source_target_pairs={{0,8},{1,9},{2,10},{3,11},{4,12},{5,13},{6,14},{7,15},{8,0},{9,1},... | collective-permute-start | bytes 7077896 | tf_op jit(solution)/shard_map/ppermute | solution.py:428
  767.4 38.5 %collective-permute-start.104 = (bf16[3,48,384]{2,1,0:T(8,128)(2,1)S(1)}, bf16[3,48,384]{2,1,0:T(8,128)(2,1)S(1)}, u32[]{:S(2)}, u32[]{:S(2)}) collective-permute-start(bf16[3,48,384]{2,1,0:T(8,128)(2,1)S(1)} %fusion.113), channel_id=1, source_target_pairs={{0,16},{1,17},{2,18},{3,19},{4,20},{5,21},{6,22},{7,23},{8,24},{9,... | collective-permute-start | bytes 331784 | tf_op jit(solution)/shard_map/ppermute | solution.py:428
  772.4 37.0 %collective-permute-start.105 = (bf16[1,2,192,384]{3,2,1,0:T(8,128)(2,1)S(1)}, bf16[1,2,192,384]{3,2,1,0:T(8,128)(2,1)S(1)}, u32[]{:S(2)}, u32[]{:S(2)}) collective-permute-start(bf16[1,2,192,384]{3,2,1,0:T(8,128)(2,1)S(1)} %get-tuple-element.530), channel_id=1, source_target_pairs={{0,2},{1,3},{2,4},{3,5},{4,6},{5,7},{6,0},{7,1},{8,10},{9,11},{10,... | collective-permute-start | bytes 884744 | tf_op jit(solution)/shard_map/ppermute | solution.py:428
  772.4 36.9 %collective-permute-start.106 = (bf16[1,2,192,384]{3,2,1,0:T(8,128)(2,1)S(1)}, bf16[1,2,192,384]{3,2,1,0:T(8,128)(2,1)S(1)}, u32[]{:S(2)}, u32[]{:S(2)}) collective-permute-start(bf16[1,2,192,384]{3,2,1,0:T(8,128)(2,1)S(1)} %get-tuple-element.529), channel_id=1, source_target_pairs={{0,4},{1,5},{2,6},{3,7},{4,0},{5,1},{6,2},{7,3},{8,12},{9,13},{10,... | collective-permute-start | bytes 884744 | tf_op jit(solution)/shard_map/ppermute | solution.py:428
  799.6 25.8 %collective-permute-start.108 = (bf16[1,4,2,48,1536]{4,3,1,2,0:T(8,128)(2,1)S(1)}, bf16[1,4,2,48,1536]{4,3,1,2,0:T(8,128)(2,1)S(1)}, u32[]{:S(2)}, u32[]{:S(2)}) collective-permute-start(bf16[1,4,2,48,1536]{4,3,1,2,0:T(8,128)(2,1)S(1)} %fusion.56), channel_id=1, source_target_pairs={{0,16},{1,17},{2,18},{3,19},{4,20},{5,21},{6,22},{7,23},{8,24},{9,... | collective-permute-start | bytes 3538952 | tf_op jit(solution)/shard_map/ppermute | solution.py:428
  825.4 42.7 %collective-permute-start.110 = (bf16[3,96,384]{2,1,0:T(8,128)(2,1)S(1)}, bf16[3,96,384]{2,1,0:T(8,128)(2,1)}, u32[]{:S(2)}, u32[]{:S(2)}) collective-permute-start(bf16[3,96,384]{2,1,0:T(8,128)(2,1)S(1)} %bitcast.487), channel_id=1, source_target_pairs={{0,8},{1,9},{2,10},{3,11},{4,12},{5,13},{6,14},{7,15},{8,0},{9,1},... | collective-permute-start | bytes 663560 | tf_op jit(solution)/shard_map/ppermute | solution.py:428
  828.2 39.9 %collective-permute-start.111 = (bf16[1,2,192,384]{3,2,1,0:T(8,128)(2,1)S(1)}, bf16[1,2,192,384]{3,2,1,0:T(8,128)(2,1)S(1)}, u32[]{:S(2)}, u32[]{:S(2)}) collective-permute-start(bf16[1,2,192,384]{3,2,1,0:T(8,128)(2,1)S(1)} %fusion.86), channel_id=1, source_target_pairs={{0,16},{1,17},{2,18},{3,19},{4,20},{5,21},{6,22},{7,23},{8,24},{9,... | collective-permute-start | bytes 884744 | tf_op jit(solution)/shard_map/ppermute | solution.py:428
  831.4 36.8 %collective-permute-start.112 = (bf16[1,4,48,1536]{3,2,1,0:T(8,128)(2,1)}, bf16[1,4,48,1536]{3,2,1,0:T(8,128)(2,1)}, u32[]{:S(2)}, u32[]{:S(2)}) collective-permute-start(bf16[1,4,48,1536]{3,2,1,0:T(8,128)(2,1)} %fusion.83), channel_id=1, source_target_pairs={{0,1},{1,0},{2,3},{3,2},{4,5},{5,4},{6,7},{7,6},{8,9},{9,8},{10,11... | collective-permute-start | bytes 1769480 | tf_op jit(solution)/shard_map/ppermute | solution.py:428
  834.5 33.7 %collective-permute-start.113 = (bf16[1,4,2,48,384]{4,3,2,1,0:T(8,128)(2,1)}, bf16[1,4,2,48,384]{4,3,2,1,0:T(8,128)(2,1)}, u32[]{:S(2)}, u32[]{:S(2)}) collective-permute-start(bf16[1,4,2,48,384]{4,3,2,1,0:T(8,128)(2,1)} %fusion.101), channel_id=1, source_target_pairs={{0,1},{1,0},{2,3},{3,2},{4,5},{5,4},{6,7},{7,6},{8,9},{9,8},{10,11... | collective-permute-start | bytes 884744 | tf_op jit(solution)/shard_map/ppermute | solution.py:428
  881.7 27.3 %collective-permute-start.118 = (bf16[1,2,48,384]{3,2,1,0:T(8,128)(2,1)S(1)}, bf16[1,2,48,384]{3,2,1,0:T(8,128)(2,1)S(1)}, u32[]{:S(2)}, u32[]{:S(2)}) collective-permute-start(bf16[1,2,48,384]{3,2,1,0:T(8,128)(2,1)S(1)} %get-tuple-element.554), channel_id=1, source_target_pairs={{0,2},{1,3},{2,4},{3,5},{4,6},{5,7},{6,0},{7,1},{8,10},{9,11},{10,... | collective-permute-start | bytes 221192 | tf_op jit(solution)/shard_map/ppermute | solution.py:428
  885.3 28.0 %collective-permute-start.119 = (bf16[1,2,48,384]{3,2,1,0:T(8,128)(2,1)S(1)}, bf16[1,2,48,384]{3,2,1,0:T(8,128)(2,1)S(1)}, u32[]{:S(2)}, u32[]{:S(2)}) collective-permute-start(bf16[1,2,48,384]{3,2,1,0:T(8,128)(2,1)S(1)} %get-tuple-element.553), channel_id=1, source_target_pairs={{0,4},{1,5},{2,6},{3,7},{4,0},{5,1},{6,2},{7,3},{8,12},{9,13},{10,... | collective-permute-start | bytes 221192 | tf_op jit(solution)/shard_map/ppermute | solution.py:428
  (216 other events, 2880.2 us)

commit v3 on v2

v3 whole, which is shorter than its diff:
```python
import functools

import jax
import jax.numpy as jnp
from jax import lax
from jax.experimental import pallas as pl
from jax.experimental.pallas import tpu as pltpu
from jax.sharding import PartitionSpec as P

D = 768
HEADS = 12
HEAD_DIM = 64
LAYERS = 2
CLUSTER = 128
TREE_LEN = 1024
SEGMENTS = 13
PAIRS = HEADS // 2
LANES = 2 * HEAD_DIM
KERNEL_VMEM = 60 * 2**20
ROW_TILE = 256
FEED_TILE = 768
DEPTH_TILE = 384
INV_ROOT = (2.0 * 3.141592653589793) ** -0.5
MATRICES = (0, 2, 6, 8)
VECTORS = (1, 3, 4, 5, 7, 9, 10, 11)
AXES = ("rep", "shard")
CHIPS_Z, CHIPS_X, CHIPS_Y, CORES = 4, 2, 2, 2
norm_eps = 1e-06


def one_hot_rows(slot_row):
    length = slot_row.shape[-1]
    rows = lax.broadcasted_iota(jnp.int32, (length, length), 0)
    return jnp.where(rows == slot_row, 1.0, 0.0).astype(jnp.bfloat16)


def first_lanes(length):
    return lax.broadcasted_iota(jnp.int32, (length, LANES), 1) < HEAD_DIM


def contract_last(left_side, right_side):
    return lax.dot_general(
        left_side, right_side, (((1,), (1,)), ((), ())), preferred_element_type=jnp.float32
    )


def contract_first(left_side, right_side):
    return lax.dot_general(
        left_side, right_side, (((0,), (0,)), ((), ())), preferred_element_type=jnp.float32
    )


def cluster_blocks(values):
    return [values[at : at + CLUSTER] for at in range(0, values.shape[0], CLUSTER)]


def attend_kernel(slot_ref, query_ref, key_ref, value_ref, bias_ref, ctx_ref, qk_ref, val_ref, p_ref):
    low = first_lanes(TREE_LEN)
    query = query_ref[...] * jnp.bfloat16(HEAD_DIM**-0.5)
    key = key_ref[...]
    value = value_ref[...]
    packed = (
        jnp.where(low, query, pltpu.roll(key, HEAD_DIM, 1)),
        jnp.where(low, pltpu.roll(query, HEAD_DIM, 1), key),
    )
    context = []
    for head in range(2):
        table = one_hot_rows(slot_ref[0, 0, head : head + 1, :])
        joined = jnp.concatenate([packed[head], value], axis=1)
        slots = jnp.dot(table, joined, preferred_element_type=jnp.float32).astype(jnp.bfloat16)
        both, values = slots[:, :LANES], slots[:, LANES:]
        qk_ref[0, head] = both
        val_ref[0, head] = values
        queries = jnp.where(low, both, jnp.bfloat16(0))
        keys = pltpu.roll(both, HEAD_DIM, 1)
        scores = jnp.concatenate(
            [contract_last(q, k) for q, k in zip(cluster_blocks(queries), cluster_blocks(keys))],
            axis=0,
        )
        scores = scores + bias_ref[0, head].astype(jnp.float32)
        numerator = jnp.exp(scores - jnp.max(scores, axis=1, keepdims=True))
        total = jnp.sum(numerator, axis=1, keepdims=True)
        soft = (numerator * (1.0 / total)).astype(jnp.bfloat16)
        p_ref[0, head] = soft
        out = jnp.concatenate(
            [
                jnp.dot(p, v, preferred_element_type=jnp.float32)
                for p, v in zip(cluster_blocks(soft), cluster_blocks(values))
            ],
            axis=0,
        ).astype(jnp.bfloat16)
        context.append(contract_first(table, out))
    ctx_ref[...] = jnp.where(low, context[0], context[1]).astype(jnp.bfloat16)


def attend_back_kernel(slot_ref, grad_ref, qk_ref, val_ref, p_ref, out_ref, sums_ref):
    low = first_lanes(TREE_LEN)
    grads = grad_ref[...]
    placed = []
    for head in range(2):
        table = one_hot_rows(slot_ref[0, 0, head : head + 1, :])
        slots = jnp.dot(table, grads, preferred_element_type=jnp.float32)
        slots = jnp.where(low == (head == 0), slots, 0.0).astype(jnp.bfloat16)
        both, values, soft = qk_ref[0, head], val_ref[0, head], p_ref[0, head]
        grad_soft = jnp.concatenate(
            [contract_last(g, v) for g, v in zip(cluster_blocks(slots), cluster_blocks(values))],
            axis=0,
        )
        grad_value = jnp.concatenate(
            [contract_first(p, g) for p, g in zip(cluster_blocks(soft), cluster_blocks(slots))],
            axis=0,
        ).astype(jnp.bfloat16)
        weights = soft.astype(jnp.float32)
        delta = jnp.sum(weights * grad_soft, axis=1, keepdims=True)
        grad_scores = (weights * (grad_soft - delta)).astype(jnp.bfloat16)
        pairs = list(zip(cluster_blocks(grad_scores), cluster_blocks(both)))
        by_key = jnp.concatenate([contract_first(s, b) for s, b in pairs], axis=0)
        by_query = jnp.concatenate(
            [jnp.dot(s, b, preferred_element_type=jnp.float32) for s, b in pairs], axis=0
        )
        mixed = jnp.where(low, by_key, by_query * HEAD_DIM**-0.5).astype(jnp.bfloat16)
        joined = jnp.concatenate([mixed, grad_value], axis=1)
        placed.append(contract_first(table, joined))
    first, second = placed
    queries = jnp.where(low, pltpu.roll(first[:, :LANES], HEAD_DIM, 1), second[:, :LANES])
    keys = jnp.where(low, first[:, :LANES], pltpu.roll(second[:, :LANES], HEAD_DIM, 1))
    values = jnp.where(low, first[:, LANES:], second[:, LANES:])
    sums = []
    for part, grad in enumerate((queries, keys, values)):
        rounded = grad.astype(jnp.bfloat16)
        out_ref[part] = rounded
        sums.append(rows_sum(rounded.astype(jnp.float32)))
    sums_ref[0, 0] = jnp.concatenate(sums + [jnp.zeros((5, LANES), jnp.float32)], axis=0)


def slot_spec():
    return pl.BlockSpec((1, 1, 2, TREE_LEN), lambda tree, pair: (tree, pair, 0, 0))


def head_spec():
    return pl.BlockSpec((1, 2, TREE_LEN, LANES), lambda tree, pair: (tree, pair, 0, 0))


def column_spec(offset):
    return pl.BlockSpec((TREE_LEN, LANES), lambda tree, pair: (tree, offset + pair))


def kernel_params():
    return pltpu.CompilerParams(vmem_limit_bytes=KERNEL_VMEM)


def attend(projected, slots, bias):
    trees = slots.shape[0]
    stored = jax.ShapeDtypeStruct((trees, HEADS, TREE_LEN, LANES), jnp.bfloat16)
    return pl.pallas_call(
        attend_kernel,
        grid=(trees, PAIRS),
        in_specs=[
            slot_spec(),
            column_spec(0),
            column_spec(PAIRS),
            column_spec(2 * PAIRS),
            head_spec(),
        ],
        out_specs=[column_spec(0), head_spec(), head_spec(), head_spec()],
        out_shape=[
            jax.ShapeDtypeStruct((trees * TREE_LEN, D), jnp.bfloat16),
            stored,
            stored,
            stored,
        ],
        compiler_params=kernel_params(),
        cost_estimate=pl.CostEstimate(
            flops=trees * 30_000_000_000, bytes_accessed=trees * 20_000_000, transcendentals=0
        ),
    )(slots, projected, projected, projected, bias)


def attend_back(grad_context, slots, kept):
    trees = slots.shape[0]
    return pl.pallas_call(
        attend_back_kernel,
        grid=(trees, PAIRS),
        in_specs=[slot_spec(), column_spec(0), head_spec(), head_spec(), head_spec()],
        out_specs=[
            pl.BlockSpec((3, TREE_LEN, LANES), lambda tree, pair: (0, tree, pair)),
            pl.BlockSpec((1, 1, 8, LANES), lambda tree, pair: (tree, pair, 0, 0)),
        ],
        out_shape=[
            jax.ShapeDtypeStruct((3, trees * TREE_LEN, D), jnp.bfloat16),
            jax.ShapeDtypeStruct((trees, PAIRS, 8, LANES), jnp.float32),
        ],
        compiler_params=kernel_params(),
        cost_estimate=pl.CostEstimate(
            flops=trees * 40_000_000_000, bytes_accessed=trees * 20_000_000, transcendentals=0
        ),
    )(slots, grad_context, *kept)


def erf_parts(values):
    size = jnp.abs(values)
    turn = 1.0 / (1.0 + (0.3275911 * 0.5**0.5) * size)
    bell = jnp.exp(-0.5 * values * values)
    series = 1.061405429 * 0.5
    for factor in (-1.453152027, 1.421413741, -0.284496736, 0.254829592):
        series = series * turn + factor * 0.5
    tail = series * turn * bell
    return jnp.where(values < 0.0, tail, 1.0 - tail), bell


def norm_parts(values):
    centred = values - jnp.mean(values, axis=-1, keepdims=True)
    scale = lax.rsqrt(jnp.mean(centred * centred, axis=-1, keepdims=True) + norm_eps)
    return centred * scale, scale


def norm_back(grad, normal, scale, gain):
    inner = grad * gain
    mean = jnp.mean(inner, axis=-1, keepdims=True)
    along = jnp.mean(inner * normal, axis=-1, keepdims=True)
    return scale * (inner - mean - normal * along)


def spread(column):
    return jnp.broadcast_to(column, (column.shape[0], 128))


def rows_sum(values):
    return jnp.sum(values, axis=0, keepdims=True)


def project_kernel(rows_ref, weight_ref, bias_ref, out_ref):
    product = jnp.dot(rows_ref[...], weight_ref[...], preferred_element_type=jnp.float32)
    out_ref[...] = (product + bias_ref[...]).astype(jnp.bfloat16)


def feed_kernel(
    context_ref,
    rows_ref,
    out_weight_ref,
    ffin_weight_ref,
    ffout_weight_ref,
    out_bias_ref,
    attn_gain_ref,
    attn_shift_ref,
    ffin_bias_ref,
    ffout_bias_ref,
    ffn_gain_ref,
    ffn_shift_ref,
    hidden_ref,
    act_ref,
    slope_ref,
    attn_normal_ref,
    attn_scale_ref,
    ffn_normal_ref,
    ffn_scale_ref,
    result_ref,
    result_low_ref,
):
    product = jnp.dot(context_ref[...], out_weight_ref[...], preferred_element_type=jnp.float32)
    attn_sum = rows_ref[...].astype(jnp.float32) + product + out_bias_ref[...]
    normal, scale = norm_parts(attn_sum)
    attn_normal_ref[...] = normal
    attn_scale_ref[...] = spread(scale)
    hidden = normal * attn_gain_ref[...] + attn_shift_ref[...]
    hidden_low = hidden.astype(jnp.bfloat16)
    hidden_ref[...] = hidden_low
    total = hidden + ffout_bias_ref[...]
    width = ffin_weight_ref.shape[1]
    for at in range(0, width, FEED_TILE):
        part = slice(at, at + FEED_TILE)
        pre = (
            jnp.dot(hidden_low, ffin_weight_ref[:, part], preferred_element_type=jnp.float32)
            + ffin_bias_ref[:, part]
        )
        below, bell = erf_parts(pre)
        act = (pre * below).astype(jnp.bfloat16)
        act_ref[:, part] = act
        slope_ref[:, part] = (below + pre * bell * INV_ROOT).astype(jnp.bfloat16)
        total = total + jnp.dot(
            act, ffout_weight_ref[part, :], preferred_element_type=jnp.float32
        )
    normal, scale = norm_parts(total)
    ffn_normal_ref[...] = normal
    ffn_scale_ref[...] = spread(scale)
    result = normal * ffn_gain_ref[...] + ffn_shift_ref[...]
    result_ref[...] = result
    result_low_ref[...] = result.astype(jnp.bfloat16)


def feed_back_kernel(with_proj, *refs):
    if with_proj:
        above_ref, proj_ref, qkv_weight_ref, *refs = refs
        grad = above_ref[...]
        for part in range(3):
            grad = grad + contract_last(
                proj_ref[part], qkv_weight_ref[:, part * D : (part + 1) * D]
            )
    else:
        above_ref, *refs = refs
        grad = above_ref[...].astype(jnp.float32)
    (
        ffn_normal_ref,
        ffn_scale_ref,
        slope_ref,
        attn_normal_ref,
        attn_scale_ref,
        out_weight_ref,
        ffin_weight_ref,
        ffout_weight_ref,
        attn_gain_ref,
        ffn_gain_ref,
        down_ref,
        pre_ref,
        attn_ref,
        attn_low_ref,
        context_ref,
        sums_ref,
        ffin_sum_ref,
    ) = refs

    @pl.when(pl.program_id(0) == 0)
    def _():
        sums_ref[...] = jnp.zeros_like(sums_ref)
        ffin_sum_ref[...] = jnp.zeros_like(ffin_sum_ref)

    normal = ffn_normal_ref[...]
    sums_ref[0:1] += rows_sum(grad * normal)
    sums_ref[1:2] += rows_sum(grad)
    grad_sum = norm_back(grad, normal, ffn_scale_ref[:, 0:1], ffn_gain_ref[...])
    down = grad_sum.astype(jnp.bfloat16)
    down_ref[...] = down
    sums_ref[2:3] += rows_sum(down.astype(jnp.float32))
    total = grad_sum
    width = ffin_weight_ref.shape[1]
    for at in range(0, width, FEED_TILE):
        part = slice(at, at + FEED_TILE)
        grad_act = contract_last(down, ffout_weight_ref[part, :])
        pre = (grad_act * slope_ref[:, part].astype(jnp.float32)).astype(jnp.bfloat16)
        pre_ref[:, part] = pre
        ffin_sum_ref[:, part] += rows_sum(pre.astype(jnp.float32))
        total = total + contract_last(pre, ffin_weight_ref[:, part])
    normal = attn_normal_ref[...]
    sums_ref[3:4] += rows_sum(total * normal)
    sums_ref[4:5] += rows_sum(total)
    attn = norm_back(total, normal, attn_scale_ref[:, 0:1], attn_gain_ref[...])
    attn_ref[...] = attn
    low = attn.astype(jnp.bfloat16)
    attn_low_ref[...] = low
    sums_ref[5:6] += rows_sum(low.astype(jnp.float32))
    context_ref[...] = contract_last(low, out_weight_ref[...]).astype(jnp.bfloat16)


def input_grad_kernel(above_ref, proj_ref, weight_ref, out_ref):
    grad = above_ref[...]
    for part in range(3):
        grad = grad + contract_last(proj_ref[part], weight_ref[:, part * D : (part + 1) * D])
    out_ref[...] = grad


def prep_kernel(parent_ref, segment_ref, cluster_ref, slot_ref, bias_ref):
    tree = pl.program_id(0)
    segs = segment_ref[0]
    length = segs.shape[1]

    def parent_of(values):
        found = jnp.zeros_like(values)
        for number in range(SEGMENTS):
            found = jnp.where(values == number, parent_ref[tree, number], found)
        return found

    parents = parent_of(segs)
    grands = parent_of(parents)
    ids = jnp.concatenate([segs, parents, grands, jnp.zeros((5, length), jnp.int32)], axis=0)
    ids = jnp.concatenate([ids, jnp.zeros((8, length), jnp.int32)], axis=0)
    ids = ids.astype(jnp.float32).astype(jnp.bfloat16)
    count = length // CLUSTER
    order = lax.broadcasted_iota(jnp.int32, (count, length), 0)
    lanes = lax.broadcasted_iota(jnp.int32, (count, length), 1)
    for head in range(2):
        member = order == cluster_ref[0, 0, head : head + 1, :]
        ranks = member.astype(jnp.int32)
        step = 1
        while step < length:
            ranks = ranks + jnp.where(lanes >= step, pltpu.roll(ranks, step, 1), 0)
            step *= 2
        slot = jnp.sum(
            jnp.where(member, ranks - 1 + CLUSTER * order, 0), axis=0, keepdims=True
        )
        slot_ref[0, 0, head : head + 1, :] = slot
        table = one_hot_rows(slot)
        rows = contract_last(ids, table)
        columns = jnp.concatenate([rows] * (128 // rows.shape[0]), axis=0).T
        for at in range(0, length, CLUSTER):
            here = rows[0:1, at : at + CLUSTER]
            block = columns[at : at + CLUSTER]
            allowed = (
                (here == block[:, 0:1]) | (here == block[:, 1:2]) | (here == block[:, 2:3])
            )
            bias_ref[0, head, at : at + CLUSTER, :] = jnp.where(allowed, 0.0, -1e30).astype(
                jnp.bfloat16
            )


def row_spec(width, rows=ROW_TILE):
    return pl.BlockSpec((rows, width), lambda i: (i, 0))


def whole_spec(shape):
    return pl.BlockSpec(
        shape, lambda i: (0,) * len(shape), pipeline_mode=pl.Buffered(1)
    )


def part_spec(rows=ROW_TILE):
    return pl.BlockSpec((3, rows, D), lambda i: (0, i, 0))


def cost(flops, *arrays):
    moved = sum(array.size * array.dtype.itemsize for array in arrays)
    return pl.CostEstimate(flops=int(flops), bytes_accessed=moved, transcendentals=0)


def shape_of(rows, width, kind=jnp.bfloat16):
    return jax.ShapeDtypeStruct((rows, width), kind)


def project(rows, weight, bias):
    count, width = rows.shape[0], weight.shape[1]
    return pl.pallas_call(
        project_kernel,
        grid=(count // ROW_TILE,),
        in_specs=[row_spec(D), whole_spec(weight.shape), whole_spec((1, width))],
        out_specs=row_spec(width),
        out_shape=shape_of(count, width),
        compiler_params=kernel_params(),
        cost_estimate=cost(2.4 * count * D * width, rows, weight),
    )(rows, weight, bias[None])


def feed(context, rows, weights, vectors):
    count = context.shape[0]
    width = weights[1].shape[1]
    f32 = jnp.float32
    vectors = [vector[None] for vector in vectors]
    return pl.pallas_call(
        feed_kernel,
        grid=(count // ROW_TILE,),
        in_specs=[row_spec(D), row_spec(D)]
        + [whole_spec(weight.shape) for weight in weights]
        + [whole_spec(vector.shape) for vector in vectors],
        out_specs=[
            row_spec(D),
            row_spec(width),
            row_spec(width),
            row_spec(D),
            row_spec(128),
            row_spec(D),
            row_spec(128),
            row_spec(D),
            row_spec(D),
        ],
        out_shape=[
            shape_of(count, D),
            shape_of(count, width),
            shape_of(count, width),
            shape_of(count, D, f32),
            shape_of(count, 128, f32),
            shape_of(count, D, f32),
            shape_of(count, 128, f32),
            shape_of(count, D, f32),
            shape_of(count, D),
        ],
        compiler_params=kernel_params(),
        cost_estimate=cost(5 * count * D * (2 * width + D), context, *weights),
    )(context, rows, *weights, *vectors)


def feed_back(above, proj, qkv_weight, saved, weights, gains):
    count = above.shape[0]
    width = weights[1].shape[1]
    f32 = jnp.float32
    gains = [gain[None] for gain in gains]
    lead, lead_specs = [above], [row_spec(D)]
    if proj is not None:
        lead += [proj, qkv_weight]
        lead_specs += [part_spec(), whole_spec(qkv_weight.shape)]
    return pl.pallas_call(
        functools.partial(feed_back_kernel, proj is not None),
        grid=(count // ROW_TILE,),
        in_specs=lead_specs
        + [row_spec(D), row_spec(128), row_spec(width), row_spec(D), row_spec(128)]
        + [whole_spec(weight.shape) for weight in weights]
        + [whole_spec(gain.shape) for gain in gains],
        out_specs=[
            row_spec(D),
            row_spec(width),
            row_spec(D),
            row_spec(D),
            row_spec(D),
            pl.BlockSpec((8, D), lambda i: (0, 0)),
            pl.BlockSpec((1, width), lambda i: (0, 0)),
        ],
        out_shape=[
            shape_of(count, D),
            shape_of(count, width),
            shape_of(count, D, f32),
            shape_of(count, D),
            shape_of(count, D),
            shape_of(8, D, f32),
            shape_of(1, width, f32),
        ],
        compiler_params=kernel_params(),
        cost_estimate=cost(5 * count * D * (2 * width + D), above, *weights),
    )(*lead, *saved, *weights, *gains)


def input_grad(above, proj, qkv_weight):
    count = above.shape[0]
    return pl.pallas_call(
        input_grad_kernel,
        grid=(count // ROW_TILE,),
        in_specs=[row_spec(D), part_spec(), whole_spec(qkv_weight.shape)],
        out_specs=row_spec(D),
        out_shape=shape_of(count, D, jnp.float32),
        compiler_params=kernel_params(),
        cost_estimate=cost(2.4 * count * D * 3 * D, above, proj, qkv_weight),
    )(above, proj, qkv_weight)


def prepare(segment, parent, clusters):
    trees = parent.shape[0]
    segment = segment.reshape(trees, 1, TREE_LEN)
    clusters = clusters.reshape(PAIRS, 2, trees, TREE_LEN).transpose(2, 0, 1, 3)
    return pl.pallas_call(
        prep_kernel,
        grid=(trees, PAIRS),
        in_specs=[
            pl.BlockSpec(memory_space=pltpu.SMEM),
            pl.BlockSpec((1, 1, TREE_LEN), lambda tree, pair: (tree, 0, 0)),
            slot_spec(),
        ],
        out_specs=[slot_spec(), head_spec()],
        out_shape=[
            jax.ShapeDtypeStruct((trees, PAIRS, 2, TREE_LEN), jnp.int32),
            jax.ShapeDtypeStruct((trees, HEADS, TREE_LEN, LANES), jnp.bfloat16),
        ],
        compiler_params=kernel_params(),
        cost_estimate=pl.CostEstimate(
            flops=trees * 20_000_000_000, bytes_accessed=trees * 4_000_000, transcendentals=0
        ),
    )(parent, segment, clusters)


def weight_grad_kernel(at_ref, left_ref, right_ref, out_ref):
    for part in range(right_ref.shape[0]):
        out_ref[part] = contract_first(left_ref[...], right_ref[part]).astype(jnp.bfloat16)


def weight_grad(left, right, at, other):
    count, depth = left.shape
    parts, _, width = right.shape
    half = width // CORES
    flip = 1 if other else 0
    return pl.pallas_call(
        weight_grad_kernel,
        grid_spec=pltpu.PrefetchScalarGridSpec(
            num_scalar_prefetch=1,
            grid=(depth // DEPTH_TILE,),
            in_specs=[
                pl.BlockSpec((count, DEPTH_TILE), lambda i, at: (0, i)),
                pl.BlockSpec(
                    (parts, count, half), lambda i, at: (0, 0, lax.rem(at[3] + flip, CORES))
                ),
            ],
            out_specs=pl.BlockSpec((parts, DEPTH_TILE, half), lambda i, at: (0, i, 0)),
        ),
        out_shape=jax.ShapeDtypeStruct((parts, depth, half), jnp.bfloat16),
        compiler_params=kernel_params(),
        cost_estimate=cost(3 * count * depth * parts * half, left, right),
    )(at, left, right)


def combine_kernel(groups, at_ref, *refs):
    total = sum(groups)
    ins, outs = refs[:total], refs[total:]
    first = 0
    for count, out_ref in zip(groups, outs):
        value = None
        for ref in ins[first : first + count]:
            term = ref[...].astype(jnp.float32).reshape(out_ref.shape)
            value = term if value is None else value + term
        out_ref[...] = value.astype(out_ref.dtype)
        first += count


def combine(at, steps, groups, blocks):
    terms = [term for group in groups for term in group]
    return pl.pallas_call(
        functools.partial(combine_kernel, [len(group) for group in groups]),
        grid_spec=pltpu.PrefetchScalarGridSpec(
            num_scalar_prefetch=1,
            grid=(steps,),
            in_specs=[pl.BlockSpec(block, index) for _, block, index in terms],
            out_specs=[pl.BlockSpec(block, index) for _, block, index in blocks],
        ),
        out_shape=[jax.ShapeDtypeStruct(shape, jnp.bfloat16) for shape, _, _ in blocks],
        compiler_params=kernel_params(),
        cost_estimate=pl.CostEstimate(
            flops=0, bytes_accessed=2_000_000, transcendentals=0
        ),
    )(at, *[array for array, _, _ in terms])


FORWARD = {
    "begin": ((), ((0, 0),)),
    "prepared": (((0, 0),), ((0, 2), (0, 6), (0, 8))),
    "ready": (((0, 0),), ()),
    (0, "projected"): (((0, 6), (0, 2), (0, 8)), ()),
    (0, "context"): (((0, 6), (0, 2), (0, 8)), ((1, 0), (1, 6))),
    (0, "feed"): (((0, 6), (1, 0), (1, 6)), ((1, 2), (1, 8))),
    (0, "result"): (((1, 0), (1, 6), (1, 2), (1, 8)), ()),
    (1, "projected"): (((1, 2), (1, 8)), ()),
    (1, "context"): (((1, 6), (1, 8)), ()),
}


class Place:
    def __init__(self):
        rep = lax.axis_index("rep")
        shard = lax.axis_index("shard")
        self.y, self.core = rep // CORES, rep % CORES
        self.z, self.x = shard // CHIPS_X, shard % CHIPS_X
        self.at = jnp.stack([self.z, self.x, self.y, self.core]).astype(jnp.int32)


def hop(value, dz=0, dx=0, dy=0, dc=0):
    pairs = []
    for y in range(CHIPS_Y):
        for c in range(CORES):
            for z in range(CHIPS_Z):
                for x in range(CHIPS_X):
                    source = ((y * CORES + c) * CHIPS_Z + z) * CHIPS_X + x
                    y2, c2 = (y + dy) % CHIPS_Y, (c + dc) % CORES
                    z2, x2 = (z + dz) % CHIPS_Z, (x + dx) % CHIPS_X
                    pairs.append((source, ((y2 * CORES + c2) * CHIPS_Z + z2) * CHIPS_X + x2))
    return lax.ppermute(value, AXES, pairs)


def place_kernel(split_y, half, at_ref, *refs):
    pieces, out_ref = refs[:-1], refs[-1]
    for number, piece in enumerate(pieces):
        core = (at_ref[3] + number % CORES) % CORES
        x = (at_ref[1] + number // CORES % CHIPS_X) % CHIPS_X
        row = (at_ref[2] + number // (CORES * CHIPS_X)) % CHIPS_Y if split_y else 0
        out_ref[x, row, :, pl.ds(pl.multiple_of(core * half, 128), half)] = piece[0]


def place_pieces(pieces, split_y, place):
    _, rows, half = pieces[0].shape
    splits = CHIPS_Y if split_y else 1
    whole = pl.pallas_call(
        functools.partial(place_kernel, split_y, half),
        grid_spec=pltpu.PrefetchScalarGridSpec(
            num_scalar_prefetch=1,
            grid=(CHIPS_Z,),
            in_specs=[pl.BlockSpec((1, rows, half), lambda k, at: (k, 0, 0))] * len(pieces),
            out_specs=pl.BlockSpec(
                (CHIPS_X, splits, rows, 2 * half),
                lambda k, at: (lax.rem(at[0] + CHIPS_Z - k, CHIPS_Z), 0, 0, 0),
            ),
        ),
        out_shape=jax.ShapeDtypeStruct(
            (CHIPS_Z * CHIPS_X, splits, rows, 2 * half), jnp.bfloat16
        ),
        compiler_params=kernel_params(),
        cost_estimate=pl.CostEstimate(
            flops=0,
            bytes_accessed=4 * CHIPS_Z * len(pieces) * rows * half,
            transcendentals=0,
        ),
    )(place.at, *pieces)
    return whole.reshape(CHIPS_Z * CHIPS_X * splits * rows, 2 * half)


def gather_chain(block, split_y, place):
    parts = yield [hop(block, dz=k) for k in range(1, CHIPS_Z)]
    stack = jnp.stack([block, *parts])
    (across,) = yield [hop(stack, dx=1)]
    pieces = [stack, across]
    if split_y:
        pieces = pieces + (yield [hop(piece, dy=1) for piece in pieces])
    others = yield [hop(piece, dc=1) for piece in pieces]
    return place_pieces(
        [item for pair in zip(pieces, others) for item in pair], split_y, place
    )


class Flow:
    def __init__(self):
        self.running, self.done = {}, {}

    def start(self, name, chain):
        self.running[name] = (chain, next(chain))

    def advance(self, name, arrived):
        chain, _ = self.running.pop(name)
        try:
            self.running[name] = (chain, chain.send(list(arrived)))
        except StopIteration as end:
            self.done[name] = end.value

    def tick(self, main, *names):
        names = [name for name in names if name in self.running]
        pending = [self.running[name][1] for name in names]
        main, pending = lax.optimization_barrier((main, pending))
        for name, arrived in zip(names, pending):
            self.advance(name, arrived)
        return main

    def finish(self, name):
        while name in self.running:
            self.advance(name, self.running[name][1])
        return self.done[name]


def gather_vectors(vectors, place):
    sizes = [vector.shape[1] for vector in vectors]
    own = jnp.concatenate(vectors, axis=1)
    layers, width = own.shape
    count = CHIPS_Z * CHIPS_X
    rounds = [
        hop(own, dz=dz, dx=dx) if dz or dx else own
        for dz in range(CHIPS_Z)
        for dx in range(CHIPS_X)
    ]
    stack = jnp.stack(rounds).astype(jnp.float32)
    wanted = jnp.arange(count, dtype=jnp.int32)
    behind = (place.z - wanted // CHIPS_X) % CHIPS_Z * CHIPS_X + (
        place.x - wanted % CHIPS_X
    ) % CHIPS_X
    turn = (behind[:, None] == wanted[None, :]).astype(jnp.float32)
    stack = jnp.sum(turn[:, :, None, None] * stack[None], axis=1)
    out, at = [], 0
    for size in sizes:
        out.append(
            stack[:, :, at : at + size].transpose(1, 0, 2).reshape(layers, count * size)
        )
        at += size
    return out


def gather_block(weights, layer, number, place):
    shard = weights[number][layer]
    rows, columns = shard.shape
    split_y = number == 6 or (number == 8 and layer > 0)
    tall = rows // CHIPS_Y if split_y else rows
    start = (place.y * tall if split_y else 0, place.core * (columns // 2))
    return lax.dynamic_slice(shard, start, (tall, columns // 2)), split_y


def reduce_chain(left, right, place, y_first):
    at = place.at
    parts, _, columns = right.shape
    half = columns // CORES
    rows = left.shape[1] // (CHIPS_Z * CHIPS_X * CHIPS_Y)
    grid = (parts, CHIPS_Z, CHIPS_X, CHIPS_Y, rows, half)
    away = weight_grad(left, right, at, True)
    sent = [hop(away.reshape(grid), dc=1)]
    kept = weight_grad(left, right, at, False).reshape(grid)
    (near,) = yield sent
    flip = lambda value: 1 - value
    if y_first:
        block = (parts, 1, CHIPS_X, 1, rows, half)
        index = lambda i, at: (0, i, 0, flip(at[2]), 0, 0)
        shape = (parts, CHIPS_Z, CHIPS_X, rows, half)
        (send,) = combine(
            at,
            CHIPS_Z,
            [[(kept, block, index), (near, block, index)]],
            [(shape, (parts, 1, CHIPS_X, rows, half), lambda i, at: (0, i, 0, 0, 0))],
        )
        (over,) = yield [hop(send, dy=1)]
        block = (parts, 1, 1, 1, rows, half)
        index = lambda i, at: (0, i, flip(at[1]), at[2], 0, 0)
        shape = (parts, CHIPS_Z, rows, half)
        (send,) = combine(
            at,
            CHIPS_Z,
            [
                [
                    (kept, block, index),
                    (near, block, index),
                    (over, block[:-3] + (rows, half), lambda i, at: (0, i, flip(at[1]), 0, 0)),
                ]
            ],
            [(shape, (parts, 1, rows, half), lambda i, at: (0, i, 0, 0))],
        )
        (across,) = yield [hop(send, dx=1)]

        def terms(k):
            turn = lambda at: lax.rem(at[0] + k, CHIPS_Z)
            index = lambda i, at: (0, turn(at), at[1], at[2], 0, 0)
            return [
                (kept, block, index),
                (near, block, index),
                (over, block[:-3] + (rows, half), lambda i, at: (0, turn(at), at[1], 0, 0)),
                (across, (parts, 1, rows, half), lambda i, at: (0, turn(at), 0, 0)),
            ]

        piece = (parts, rows, half)
    else:
        block = (parts, 1, 1, CHIPS_Y, rows, half)
        index = lambda i, at: (0, i, flip(at[1]), 0, 0, 0)
        shape = (parts, CHIPS_Z, CHIPS_Y, rows, half)
        (send,) = combine(
            at,
            CHIPS_Z,
            [[(kept, block, index), (near, block, index)]],
            [(shape, (parts, 1, CHIPS_Y, rows, half), lambda i, at: (0, i, 0, 0, 0))],
        )
        (across,) = yield [hop(send, dx=1)]

        def terms(k):
            turn = lambda at: lax.rem(at[0] + k, CHIPS_Z)
            index = lambda i, at: (0, turn(at), at[1], 0, 0, 0)
            return [
                (kept, block, index),
                (near, block, index),
                (across, (parts, 1, CHIPS_Y, rows, half), lambda i, at: (0, turn(at), 0, 0, 0)),
            ]

        piece = (parts, CHIPS_Y, rows, half)
    zeros = lambda i, at: (0,) * len(piece)
    whole = (piece, piece, zeros)
    own, *sends = combine(at, 1, [terms(k) for k in range(CHIPS_Z)], [whole] * CHIPS_Z)
    landed = yield [hop(send, dz=k) for k, send in zip(range(1, CHIPS_Z), sends)]
    (own,) = combine(at, 1, [[(term, piece, zeros) for term in (own, *landed)]], [whole])
    (other,) = yield [hop(own, dy=1)]
    if y_first:
        pieces = [own, other]
    else:
        pieces = combine(at, 1, [[(own, piece, zeros), (other, piece, zeros)]], [whole])
    others = yield [hop(item, dc=1) for item in pieces]
    return [*pieces, *others]


def join_kernel(at_ref, *refs):
    out_ref = refs[-1]
    half = refs[0].shape[-1]
    per_layer = (len(refs) - 1) // LAYERS
    for number, ref in enumerate(refs[:-1]):
        layer, place = divmod(number, per_layer)
        core = lax.rem(at_ref[3] + place // (per_layer // CORES), CORES)
        row = 0
        if per_layer > CORES:
            row = lax.rem(at_ref[2] + place % CHIPS_Y, CHIPS_Y) * ref.shape[1]
            row = pl.multiple_of(row, 16)
        for part in range(ref.shape[0]):
            column = pl.multiple_of((part * CORES + core) * half, 128)
            out_ref[layer, pl.ds(row, ref.shape[1]), pl.ds(column, half)] = ref[part].astype(
                jnp.float32
            )


def join(at, layers):
    pieces = []
    for layer in layers:
        for piece in layer:
            if piece.ndim == 4:
                piece = piece.reshape(piece.shape[0], -1, piece.shape[-1])
            pieces.append(piece)
    parts, rows, half = pieces[0].shape
    tall = rows * (len(pieces) // LAYERS // CORES)
    zeros = lambda i, at: (0, 0, 0)
    shape = (LAYERS, tall, parts * CORES * half)
    return pl.pallas_call(
        join_kernel,
        grid_spec=pltpu.PrefetchScalarGridSpec(
            num_scalar_prefetch=1,
            grid=(1,),
            in_specs=[pl.BlockSpec(piece.shape, zeros) for piece in pieces],
            out_specs=pl.BlockSpec(shape, zeros),
        ),
        out_shape=jax.ShapeDtypeStruct(shape, jnp.float32),
        compiler_params=kernel_params(),
        cost_estimate=pl.CostEstimate(flops=0, bytes_accessed=4_000_000, transcendentals=0),
    )(at, *pieces)


def reduce_total(total, place):
    for step in (dict(dc=1), dict(dy=1), dict(dx=1), dict(dz=2)):
        (other,) = yield [hop(total, **step)]
        total = total + other
    up, down = yield [hop(total, dz=1), hop(total, dz=3)]
    return total + jnp.where(place.z % 2 == 0, down, up)


def path_vectors(qv_bias):
    low = qv_bias.astype(jnp.float32)
    return jnp.concatenate([low[:D], jnp.zeros((D,), jnp.float32), low[D:]])


def local(
    fast,
    inputs,
    cotangent,
    segment,
    parent,
    clusters,
    *weights,
):
    flow = Flow()
    if fast:
        place = Place()
        vectors = gather_vectors([weights[number] for number in VECTORS], place)

        def begin(layer, number):
            flow.start(
                (layer, number), gather_chain(*gather_block(weights, layer, number, place), place)
            )

        def get(layer, number):
            if number in VECTORS:
                return vectors[VECTORS.index(number)][layer]
            return flow.finish((layer, number))

        def step(point, main):
            advanced, started = FORWARD.get(point, ((), ()))
            main = flow.tick(main, *advanced)
            for name in started:
                begin(*name)
            return main

        def reduce(layer, number, left, right):
            flow.start(
                ("grad", layer, number), reduce_chain(left, right, place, number in (0, 6))
            )

        def back_step(main, *only):
            return flow.tick(
                main,
                *[
                    name
                    for name in flow.running
                    if name[0] == "grad" and (not only or name[1:] in only)
                ],
            )

    else:

        def get(layer, number):
            whole = lax.all_gather(weights[number][layer], "shard", axis=0, tiled=True)
            return whole.astype(jnp.float32) if number in VECTORS else whole

        def step(point, main):
            return main

        def reduce(layer, number, left, right):
            grads = jnp.concatenate([contract_first(left, part) for part in right], axis=1)
            grads = lax.psum_scatter(grads, "shard", scatter_dimension=0, tiled=True)
            grads = lax.psum(grads.astype(jnp.bfloat16), "rep").astype(jnp.float32)
            flow.done[("grad", layer, number)] = grads

        def back_step(main, *only):
            return main

    step("begin", ())
    slots, bias = step("prepared", prepare(segment, parent, clusters))
    hidden, hidden_low = step("ready", (inputs, inputs))
    saved = []
    for layer in range(LAYERS):
        pull = functools.partial(get, layer)
        projected = project(hidden_low, pull(0), path_vectors(pull(1)))
        projected = step((layer, "projected"), projected)
        context, *heads = attend(projected, slots, bias)
        context = step((layer, "context"), context)
        context = step((layer, "feed"), context)
        entered = hidden_low
        middle, act, slope, *norms, hidden, hidden_low = feed(
            context,
            hidden,
            [pull(2), pull(6), pull(8)],
            [pull(number) for number in (3, 4, 5, 7, 9, 10, 11)],
        )
        hidden_low = step((layer, "result"), hidden_low)
        saved.append((entered, heads, context, middle, act, slope, norms))
    result = hidden_low
    above, proj = cotangent, None
    sums = [None] * LAYERS
    for layer in reversed(range(LAYERS)):
        entered, heads, context, middle, act, slope, norms = saved[layer]
        pull = functools.partial(get, layer)
        down, grad_pre, grad_attn, attn_low, grad_context, row_sums, ffin_sum = feed_back(
            above,
            proj,
            None if proj is None else get(layer + 1, 0),
            [norms[2], norms[3], slope, norms[0], norms[1]],
            [pull(2), pull(6), pull(8)],
            [pull(4), pull(10)],
        )
        down = back_step(down)
        reduce(layer, 8, act, down[None])
        reduce(layer, 6, middle, grad_pre[None])
        reduce(layer, 2, context, attn_low[None])
        grad_context = back_step(grad_context)
        proj, proj_sums = attend_back(grad_context, slots, heads)
        proj = back_step(proj)
        reduce(layer, 0, entered, proj)
        proj = back_step(proj, (layer, 0))
        above = grad_attn
        sums[layer] = (row_sums, ffin_sum, jnp.sum(proj_sums, axis=0))
    grad_input = input_grad(above, proj, get(0, 0))

    def qv_sum(layer):
        return jnp.concatenate([sums[layer][2][:, part].reshape(D) for part in (0, 2)])

    early = jnp.concatenate(
        [qv_sum(1)]
        + [piece for layer in range(LAYERS) for piece in (sums[layer][0][:6].reshape(-1), sums[layer][1][0])]
    )
    totals = {"early": early, "late": qv_sum(0)}
    count = lax.axis_size("shard")
    shard = lax.axis_index("shard")
    for name, total in totals.items():
        if fast:
            flow.start(name, reduce_total(total, place))
            totals[name] = flow.finish(name)
        else:
            totals[name] = lax.psum(total, AXES)
    early, late = totals["early"], totals["late"]
    ff = sums[0][1].shape[1]
    rest = early[2 * D :].reshape(LAYERS, 6 * D + ff)

    def share(stacked):
        width = stacked.shape[1] // count
        return lax.dynamic_slice_in_dim(stacked, shard * width, width, axis=1)

    grads = {1: share(jnp.stack([late, early[: 2 * D]])), 7: share(rest[:, 6 * D :])}
    for number, row in ((10, 0), (11, 1), (9, 2), (4, 3), (5, 4), (3, 5)):
        grads[number] = share(rest[:, row * D : (row + 1) * D])
    for number in (8, 6, 2, 0):
        done = [flow.finish(("grad", layer, number)) for layer in range(LAYERS)]
        grads[number] = join(place.at, done) if fast else jnp.stack(done)
    return (result, grad_input, *[grads[number] for number in range(12)])


def solution(mesh):
    in_specs = (
        P(("rep", "shard"), None),
        P(("rep", "shard"), None),
        P(("rep", "shard")),
        P(("rep", "shard"), None),
        P(None, ("rep", "shard")),
        P(None, "shard", None),
        P(None, "shard"),
        P(None, "shard", None),
        P(None, "shard"),
        P(None, "shard"),
        P(None, "shard"),
        P(None, "shard", None),
        P(None, "shard"),
        P(None, "shard", None),
        P(None, "shard"),
        P(None, "shard"),
        P(None, "shard"),
    )
    out_specs = (
        P(("rep", "shard"), None),
        P(("rep", "shard"), None),
        P(None, "shard", None),
        P(None, "shard"),
        P(None, "shard", None),
        P(None, "shard"),
        P(None, "shard"),
        P(None, "shard"),
        P(None, "shard", None),
        P(None, "shard"),
        P(None, "shard", None),
        P(None, "shard"),
        P(None, "shard"),
        P(None, "shard"),
    )
    fast = mesh.shape["rep"] == CHIPS_Y * CORES and mesh.shape["shard"] == CHIPS_Z * CHIPS_X
    return jax.shard_map(
        functools.partial(local, fast),
        mesh=mesh,
        in_specs=in_specs,
        out_specs=out_specs,
        check_vma=False,
    )
```

time: 1000 us -> 879 us (0.88)
  Pallas kernels: 193 us -> 554 us
  matrix products: 247 us -> 0 us
  waiting for transfers between devices: 202 us -> 78 us
  other arithmetic: 86.1 us -> 9.42 us
  local copies, waits for them, and re-layouts: 88.2 us -> 46.3 us
    pallas_call x1 -> x60, Pallas kernels: 16.8 us -> 378 us  [the longest x16 108 us: weight_grad(): pl.pallas_call(weight_grad_kernel, grid_spec=pltpu.PrefetchScalarGridSpec...]
    dot_general x45 -> x0, matrix products: 247 us -> none  [the longest x12 77.7 us: dot_last(): lax.dot_general(left_side, right_side, (((1,), (1,)), ((), ())), preferre...]
    ppermute x147 -> x143, waiting for transfers between devices: 202 us -> 78 us  [hop(): return lax.ppermute(value, AXES, pairs)]
    unnamed x285 -> x243, local copies, waits for them, and re-layouts: 35.7 us -> 12 us
    add x30 -> x10, other arithmetic: 17.1 us -> 0.08 us  [the longest x8 0.06 us: reduce_total(): total = total + other]
    reduce_sum x19 -> x0, other arithmetic: 16 us -> none  [the longest x3 5.05 us: layer_norm(): return centred * lax.rsqrt(variance + norm_eps) * norm_gain + norm_shift]
    another operation x25 -> x2, other arithmetic: 16.7 us -> 1.3 us  [the longest x1 0.66 us: local(): jnp.stack([late, early[:2 * D]])]
    convert_element_type x21 -> x0, other arithmetic: 11.8 us -> none  [the longest x2 2.8 us: layer_forward(): layer_low = layer_in.astype(jnp.bfloat16)]
  transfers between devices with their start and end apart: 147 -> 143, of which waited for: 33 -> 21; matrix products, arithmetic and copies ran while one was open for 30% -> 5% of each run, Pallas kernels for 19% -> 54%
where the time goes in v3:
time: 879 us; the launch traced here: 866 us
  Pallas kernels  554 us (63%)
  starting transfers between devices  176 us (20%)
  waiting for transfers between devices  78 us (9%)
  local copies, waits for them, and re-layouts  46.3 us (5%)
  other arithmetic  9.42 us (1%)
    ppermute x143, starting transfers between devices, hop(): return lax.ppermute(value, AXES, pairs)  176 us
    pallas_call x16, Pallas kernels, weight_grad(): pl.pallas_call(weight_grad_kernel, grid_spec=pltpu.PrefetchScalarGridSpec...  108 us
    pallas_call x32, Pallas kernels, combine(): pl.pallas_call(functools.partial(combine_kernel, [len(group) for group in...  107 us
    ppermute x143, waiting for transfers between devices, hop(): return lax.ppermute(value, AXES, pairs)  78 us
    pallas_call x2, Pallas kernels, attend_back(): pl.pallas_call(attend_back_kernel, grid=(trees, PAIRS), in_specs=[slot_sp...  66.9 us
    pallas_call x2, Pallas kernels, attend(): pl.pallas_call(attend_kernel, grid=(trees, PAIRS), in_specs=[slot_spec(),...  66.8 us
    pallas_call x2, Pallas kernels, feed(): pl.pallas_call(feed_kernel, grid=(count // ROW_TILE,), in_specs=[row_spec...  56.2 us
    pallas_call x2, Pallas kernels, feed_back(): pl.pallas_call(functools.partial(feed_back_kernel, proj is not None), gri...  50.8 us
  transfers between devices with their start and end apart: 143, of which 21 were waited for; matrix products, arithmetic and copies ran while one was open for 5% of the time, Pallas kernels for 54%

profile of v3, /device:TPU:17, one launch (start us, length us, event | category | flops | bytes accessed | tf_op | source)
XLA Modules:
  0.0 866.3 jit_solution(5396565222441432347)
XLA Ops:
  11.3 19.0 %shard_map.272 = (s32[1,6,2,1024]{3,2,1,0:T(2,128)}, bf16[1,12,1024,128]{3,2,1,0:T(8,128)(2,1)}) custom-call(s32[1,13]{1,0:T(1,128)} %parent_ref.1, s32[1,1,1024]{2,1,0:T(1,128)} %bitcast.231, s32[1,6,2,1024]{3,2,1,0:T(2,128)} %transpose_reshape.3.cluster_ref), custom_call_target="tpu_custom_call" | custom-call | flops 20000000000 | bytes 4000000 | tf_op jit(solution)/shard_map/pallas_call | solution.py:535
  40.2 13.4 %collective-permute-done.3.refs_2_ = bf16[4,96,1152]{2,1,0:T(8,128)(2,1)} collective-permute-done((bf16[4,96,1152]{2,1,0:T(8,128)(2,1)S(1)}, bf16[4,96,1152]{2,1,0:T(8,128)(2,1)}, u32[]{:S(2)}, u32[]{:S(2)}) %collective-permute-start.3) | collective-permute-done | bytes 884768 | tf_op jit(solution)/shard_map/ppermute | solution.py:647
  72.7 5.2 shard_map.273
  83.5 7.8 shard_map.274.query_ref.key_ref.value_ref
  92.1 7.4 collective-permute-done.15
  99.5 3.8 collective-permute-done.19
  103.3 8.8 %collective-permute-done.20 = bf16[384,384]{1,0:T(8,128)(2,1)S(1)} collective-permute-done((bf16[384,384]{1,0:T(8,128)(2,1)S(1)}, bf16[384,384]{1,0:T(8,128)(2,1)S(1)}, u32[]{:S(2)}, u32[]{:S(2)}) %collective-permute-start.20) | collective-permute-done | bytes 294944 | tf_op jit(solution)/shard_map/ppermute | solution.py:647
  112.2 6.3 collective-permute-done.21
  123.6 33.4 %shard_map.275 = (bf16[1024,768]{1,0:T(8,128)(2,1)}, bf16[1,12,1024,128]{3,2,1,0:T(8,128)(2,1)}, bf16[1,12,1024,128]{3,2,1,0:T(8,128)(2,1)}, bf16[1,12,1024,128]{3,2,1,0:T(8,128)(2,1)}) custom-call(s32[1,6,2,1024]{3,2,1,0:T(2,128)} %get-tuple-element.182.slot_ref, bf16[1024,2304]{1,0:T(8,128)(2,1)} %shard_map.274.query_ref.key_ref.value_ref, ...), custom_call_target="tpu_custom_call" | custom-call | flops 30000001024 | bytes 20000000 | tf_op jit(solution)/shard_map/pallas_call | solution.py:155
  159.3 4.6 collective-permute-done.22.refs_2_
  167.1 3.3 collective-permute-start.28
  172.4 14.6 %collective-permute-start.35 = (bf16[4,48,1536]{2,1,0:T(8,128)(2,1)S(1)}, bf16[4,48,1536]{2,1,0:T(8,128)(2,1)S(1)}, u32[]{:S(2)}, u32[]{:S(2)}) collective-permute-start(bf16[4,48,1536]{2,1,0:T(8,128)(2,1)S(1)} %pad_maximum_fusion.3.refs_0_), channel_id=1, source_target_pairs={{0,8},{1,9},{2,10},{3,11},{4,12},{5,13},{6,14},{7,15},{8,0},{9,1},... | collective-permute-start | bytes 1769480 | tf_op jit(solution)/shard_map/ppermute | solution.py:647
  197.7 4.2 shard_map.276
  207.7 5.8 shard_map.277
  215.8 5.7 shard_map.278
  225.6 28.2 %shard_map.279 = (bf16[1024,768]{1,0:T(8,128)(2,1)}, bf16[1024,3072]{1,0:T(8,128)(2,1)}, bf16[1024,3072]{1,0:T(8,128)(2,1)}, f32[1024,768]{1,0:T(8,128)}, f32[10...) custom-call(bf16[1024,768]{1,0:T(8,128)(2,1)} %get-tuple-element.202, ...), custom_call_target="tpu_custom_call" | custom-call | flops 27179089920 | bytes 12189696 | tf_op jit(solution)/shard_map/pallas_call | solution.py:446
  267.0 5.1 shard_map.280
  272.2 7.8 shard_map.281.query_ref.key_ref.value_ref
  283.2 33.5 %shard_map.282 = (bf16[1024,768]{1,0:T(8,128)(2,1)}, bf16[1,12,1024,128]{3,2,1,0:T(8,128)(2,1)}, bf16[1,12,1024,128]{3,2,1,0:T(8,128)(2,1)}, bf16[1,12,1024,128]{3,2,1,0:T(8,128)(2,1)}) custom-call(s32[1,6,2,1024]{3,2,1,0:T(2,128)} %get-tuple-element.182.slot_ref, bf16[1024,2304]{1,0:T(8,128)(2,1)} %shard_map.281.query_ref.key_ref.value_ref, ...), custom_call_target="tpu_custom_call" | custom-call | flops 30000001024 | bytes 20000000 | tf_op jit(solution)/shard_map/pallas_call | solution.py:155
  329.3 4.2 shard_map.283
  333.6 5.8 shard_map.285
  340.2 5.7 shard_map.284
  346.0 27.9 %shard_map.286 = (bf16[1024,768]{1,0:T(8,128)(2,1)}, bf16[1024,3072]{1,0:T(8,128)(2,1)}, bf16[1024,3072]{1,0:T(8,128)(2,1)}, f32[1024,768]{1,0:T(8,128)}, f32[10...) custom-call(bf16[1024,768]{1,0:T(8,128)(2,1)} %get-tuple-element.227, ...), custom_call_target="tpu_custom_call" | custom-call | flops 27179089920 | bytes 12189696 | tf_op jit(solution)/shard_map/pallas_call | solution.py:446
  373.9 21.7 %shard_map.287 = (bf16[1024,768]{1,0:T(8,128)(2,1)}, bf16[1024,3072]{1,0:T(8,128)(2,1)}, f32[1024,768]{1,0:T(8,128)}, bf16[1024,768]{1,0:T(8,128)(2,1)}, bf16[10...) custom-call(bf16[1024,768]{1,0:T(8,128)(2,1)} %refs_0_.1, f32[1024,768]{1,0:T(8,128)} %get-tuple-element.235.refs_1_, ...), custom_call_target="tpu_custom_call" | custom-call | flops 27179089920 | bytes 12189696 | tf_op jit(solution)/shard_map/pallas_call | solution.py:488
  395.6 6.7 shard_map.289
  402.7 9.7 %shard_map.288 = bf16[1,3072,384]{2,1,0:T(8,128)(2,1)} custom-call(s32[4]{0:T(128)} %pad_add_fusion.at_ref, bf16[1024,3072]{1,0:T(8,128)(2,1)} %get-tuple-element.242.left_ref, bf16[1,1024,768]{2,1,0:T(8,128)(2,1)} %bitcast.238), custom_call_target="tpu_custom_call" | custom-call | flops 3623878656 | bytes 7864320 | tf_op jit(solution)/shard_map/pallas_call | solution.py:565
  412.6 4.0 shard_map.290
  416.9 4.2 shard_map.296
  421.1 6.7 shard_map.294
  427.8 9.7 %shard_map.292 = bf16[1,3072,384]{2,1,0:T(8,128)(2,1)} custom-call(s32[4]{0:T(128)} %pad_add_fusion.at_ref, bf16[1024,3072]{1,0:T(8,128)(2,1)} %get-tuple-element.242.left_ref, bf16[1,1024,768]{2,1,0:T(8,128)(2,1)} %bitcast.239), custom_call_target="tpu_custom_call" | custom-call | flops 3623878656 | bytes 7864320 | tf_op jit(solution)/shard_map/pallas_call | solution.py:565
  438.4 3.8 shard_map.297
  443.4 4.4 shard_map.295
  449.0 4.4 shard_map.293
  453.7 33.5 %shard_map.291 = (bf16[3,1024,768]{2,1,0:T(8,128)(2,1)}, f32[1,6,8,128]{3,2,1,0:T(8,128)}) custom-call(s32[1,6,2,1024]{3,2,1,0:T(2,128)} %get-tuple-element.182.slot_ref, bf16[1024,768]{1,0:T(8,128)(2,1)} %get-tuple-element.247.grad_ref, bf16[1,12,1024,128]{3,2,1,0:T(8,128)(2,1)} %get-tuple-element.248.qk_ref, ...), custom_call_target="tpu_custom_call" | custom-call | flops 40000000000 | bytes 20000000 | tf_op jit(solution)/shard_map/pallas_call | solution.py:181
  487.3 6.5 shard_map.298
  500.9 4.6 shard_map.301
  506.7 3.8 shard_map.300
  510.5 6.4 shard_map.303
  518.1 4.3 shard_map.304
  522.6 29.1 %shard_map.299 = (bf16[1024,768]{1,0:T(8,128)(2,1)}, bf16[1024,3072]{1,0:T(8,128)(2,1)}, f32[1024,768]{1,0:T(8,128)}, bf16[1024,768]{1,0:T(8,128)(2,1)}, bf16[10...) custom-call(f32[1024,768]{1,0:T(8,128)} %get-tuple-element.240.refs_0_, ...), custom_call_target="tpu_custom_call" | custom-call | flops 27179089920 | bytes 13762560 | tf_op jit(solution)/shard_map/pallas_call | solution.py:488
  555.6 6.7 shard_map.310
  562.3 13.5 %collective-permute-start.89 = (bf16[1,4,2,2,48,1536]{5,4,3,2,1,0:T(8,128)(2,1)}, bf16[1,4,2,2,48,1536]{5,4,3,2,1,0:T(8,128)(2,1)S(1)}, u32[]{:S(2)}, u32[]{:S(2)}) collective-permute-start(bf16[1,4,2,2,48,1536]{5,4,3,2,1,0:T(8,128)(2,1)} %bitcast.225), channel_id=1, source_target_pairs={{0,8},{1,9},{2,10},{3,11},{4,12},{5,13},{6,14},{7,15},{8,0},{9,1},... | collective-permute-start | bytes 7077896 | tf_op jit(solution)/shard_map/ppermute | solution.py:647
  578.7 9.7 %shard_map.309 = bf16[1,3072,384]{2,1,0:T(8,128)(2,1)} custom-call(s32[4]{0:T(128)} %pad_add_fusion.at_ref, bf16[1024,3072]{1,0:T(8,128)(2,1)} %get-tuple-element.288.left_ref, bf16[1,1024,768]{2,1,0:T(8,128)(2,1)} %bitcast.236), custom_call_target="tpu_custom_call" | custom-call | flops 3623878656 | bytes 7864320 | tf_op jit(solution)/shard_map/pallas_call | solution.py:565
  589.7 4.0 shard_map.311
  604.6 4.2 shard_map.308
  613.7 6.8 shard_map.319
  620.6 4.0 shard_map.321
  638.0 9.8 %shard_map.317 = bf16[1,3072,384]{2,1,0:T(8,128)(2,1)} custom-call(s32[4]{0:T(128)} %pad_add_fusion.at_ref, bf16[1024,3072]{1,0:T(8,128)(2,1)} %get-tuple-element.288.left_ref, bf16[1,1024,768]{2,1,0:T(8,128)(2,1)} %bitcast.237), custom_call_target="tpu_custom_call" | custom-call | flops 3623878656 | bytes 7864320 | tf_op jit(solution)/shard_map/pallas_call | solution.py:565
  647.8 3.8 shard_map.322
  655.3 4.4 shard_map.320
  659.7 4.5 shard_map.318
  669.6 33.4 %shard_map.312 = (bf16[3,1024,768]{2,1,0:T(8,128)(2,1)}, f32[1,6,8,128]{3,2,1,0:T(8,128)}) custom-call(s32[1,6,2,1024]{3,2,1,0:T(2,128)} %get-tuple-element.182.slot_ref, bf16[1024,768]{1,0:T(8,128)(2,1)} %get-tuple-element.293.grad_ref, bf16[1,12,1024,128]{3,2,1,0:T(8,128)(2,1)} %get-tuple-element.294.qk_ref, ...), custom_call_target="tpu_custom_call" | custom-call | flops 40000000000 | bytes 20000000 | tf_op jit(solution)/shard_map/pallas_call | solution.py:181
  703.2 6.7 shard_map.323
  727.7 6.6 shard_map.325
  734.2 4.2 shard_map.336
  741.0 4.3 shard_map.326
  746.0 3.8 shard_map.340
  757.0 5.3 collective-permute-done.101.refs_2_.refs_6_.refs_10_.refs_14_
  763.6 4.1 shard_map.327
  773.6 5.5 collective-permute-done.140.refs_3_
  795.6 9.0 %collective-permute-start.136 = (bf16[1,48,1536]{2,1,0:T(8,128)(2,1)S(1)}, bf16[1,48,1536]{2,1,0:T(8,128)(2,1)S(1)}, u32[]{:S(2)}, u32[]{:S(2)}) collective-permute-start(bf16[1,48,1536]{2,1,0:T(8,128)(2,1)S(1)} %copy-done.46), channel_id=1, source_target_pairs={{0,8},{1,9},{2,10},{3,11},{4,12},{5,13},{6,14},{7,15},{8,0},{9,1},... | collective-permute-start | bytes 442376 | tf_op jit(solution)/shard_map/ppermute | solution.py:647
  842.9 3.5 shard_map.343
  848.5 3.6 shard_map.339
  852.6 8.8 %shard_map.324 = f32[1024,768]{1,0:T(8,128)} custom-call(f32[1024,768]{1,0:T(8,128)} %get-tuple-element.262.above_ref, bf16[3,1024,768]{2,1,0:T(8,128)(2,1)} %get-tuple-element.312.right_ref.proj_ref, bf16[768,2304]{1,0:T(8,128)(2,1)} %bitcast.178), custom_call_target="tpu_custom_call" | custom-call | flops 4348654592 | bytes 11403264 | tf_op jit(solution)/shard_map/pallas_call | solution.py:520
  (641 shorter events, 267.9 us)
Async XLA Ops:
  2.7 27.7 %collective-permute-start = (bf16[96,1152]{1,0:T(8,128)(2,1)}, bf16[96,1152]{1,0:T(8,128)(2,1)S(1)}, u32[]{:S(2)}, u32[]{:S(2)}) collective-permute-start(bf16[96,1152]{1,0:T(8,128)(2,1)} %fusion.24), channel_id=1, source_target_pairs={{0,2},{1,3},{2,4},{3,5},{4,6},{5,7},{6,0},{7,1},{8,10},{9,11},{10,... | collective-permute-start | bytes 663560 | tf_op jit(solution)/shard_map/ppermute | solution.py:647
  4.0 29.5 %collective-permute-start.1 = (bf16[96,1152]{1,0:T(8,128)(2,1)}, bf16[96,1152]{1,0:T(8,128)(2,1)}, u32[]{:S(2)}, u32[]{:S(2)}) collective-permute-start(bf16[96,1152]{1,0:T(8,128)(2,1)} %fusion.24), channel_id=1, source_target_pairs={{0,4},{1,5},{2,6},{3,7},{4,0},{5,1},{6,2},{7,3},{8,12},{9,13},{10,... | collective-permute-start | bytes 663560 | tf_op jit(solution)/shard_map/ppermute | solution.py:647
  4.1 29.4 %collective-permute-start.2 = (bf16[96,1152]{1,0:T(8,128)(2,1)}, bf16[96,1152]{1,0:T(8,128)(2,1)}, u32[]{:S(2)}, u32[]{:S(2)}) collective-permute-start(bf16[96,1152]{1,0:T(8,128)(2,1)} %fusion.24), channel_id=1, source_target_pairs={{0,6},{1,7},{2,0},{3,1},{4,2},{5,3},{6,4},{7,5},{8,14},{9,15},{10,... | collective-permute-start | bytes 663560 | tf_op jit(solution)/shard_map/ppermute | solution.py:647
  6.1 51.5 %collective-permute-start.6 = (bf16[2,1152]{1,0:T(2,128)(2,1)S(1)}, bf16[2,1152]{1,0:T(2,128)(2,1)}, u32[]{:S(2)}, u32[]{:S(2)}) collective-permute-start(bf16[2,1152]{1,0:T(2,128)(2,1)S(1)} %concatenate.19), channel_id=1, source_target_pairs={{0,1},{1,0},{2,3},{3,2},{4,5},{5,4},{6,7},{7,6},{8,9},{9,8},{10,11... | collective-permute-start | bytes 13832 | tf_op jit(solution)/shard_map/ppermute | solution.py:647
  7.3 50.9 %collective-permute-start.7 = (bf16[2,1152]{1,0:T(2,128)(2,1)S(1)}, bf16[2,1152]{1,0:T(2,128)(2,1)}, u32[]{:S(2)}, u32[]{:S(2)}) collective-permute-start(bf16[2,1152]{1,0:T(2,128)(2,1)S(1)} %concatenate.19), channel_id=1, source_target_pairs={{0,2},{1,3},{2,4},{3,5},{4,6},{5,7},{6,0},{7,1},{8,10},{9,11},{10,... | collective-permute-start | bytes 13832 | tf_op jit(solution)/shard_map/ppermute | solution.py:647
  30.4 31.1 %collective-permute-start.8 = (bf16[2,1152]{1,0:T(2,128)(2,1)S(1)}, bf16[2,1152]{1,0:T(2,128)(2,1)S(1)}, u32[]{:S(2)}, u32[]{:S(2)}) collective-permute-start(bf16[2,1152]{1,0:T(2,128)(2,1)S(1)} %concatenate.19), channel_id=1, source_target_pairs={{0,3},{1,2},{2,5},{3,4},{4,7},{5,6},{6,1},{7,0},{8,11},{9,10},{10,... | collective-permute-start | bytes 13832 | tf_op jit(solution)/shard_map/ppermute | solution.py:647
  37.5 31.9 %collective-permute-start.4 = (bf16[4,96,1152]{2,1,0:T(8,128)(2,1)S(1)}, bf16[4,96,1152]{2,1,0:T(8,128)(2,1)}, u32[]{:S(2)}, u32[]{:S(2)}) collective-permute-start(bf16[4,96,1152]{2,1,0:T(8,128)(2,1)S(1)} %pad_maximum_fusion.1.refs_0_), channel_id=1, source_target_pairs={{0,8},{1,9},{2,10},{3,11},{4,12},{5,13},{6,14},{7,15},{8,0},{9,1},... | collective-permute-start | bytes 2654216 | tf_op jit(solution)/shard_map/ppermute | solution.py:647
  78.7 24.7 %collective-permute-start.19 = (bf16[384,384]{1,0:T(8,128)(2,1)S(1)}, bf16[384,384]{1,0:T(8,128)(2,1)S(1)}, u32[]{:S(2)}, u32[]{:S(2)}) collective-permute-start(bf16[384,384]{1,0:T(8,128)(2,1)S(1)} %copy-done.58), channel_id=1, source_target_pairs={{0,2},{1,3},{2,4},{3,5},{4,6},{5,7},{6,0},{7,1},{8,10},{9,11},{10,... | collective-permute-start | bytes 884744 | tf_op jit(solution)/shard_map/ppermute | solution.py:647
  80.5 31.7 %collective-permute-start.20 = (bf16[384,384]{1,0:T(8,128)(2,1)S(1)}, bf16[384,384]{1,0:T(8,128)(2,1)S(1)}, u32[]{:S(2)}, u32[]{:S(2)}) collective-permute-start(bf16[384,384]{1,0:T(8,128)(2,1)S(1)} %copy-done.58), channel_id=1, source_target_pairs={{0,4},{1,5},{2,6},{3,7},{4,0},{5,1},{6,2},{7,3},{8,12},{9,13},{10,... | collective-permute-start | bytes 884744 | tf_op jit(solution)/shard_map/ppermute | solution.py:647
  81.2 37.3 %collective-permute-start.21 = (bf16[384,384]{1,0:T(8,128)(2,1)S(1)}, bf16[384,384]{1,0:T(8,128)(2,1)S(1)}, u32[]{:S(2)}, u32[]{:S(2)}) collective-permute-start(bf16[384,384]{1,0:T(8,128)(2,1)S(1)} %copy-done.58), channel_id=1, source_target_pairs={{0,6},{1,7},{2,0},{3,1},{4,2},{5,3},{6,4},{7,5},{8,14},{9,15},{10,... | collective-permute-start | bytes 884744 | tf_op jit(solution)/shard_map/ppermute | solution.py:647
  91.3 74.9 %collective-permute-start.30 = (bf16[48,1536]{1,0:T(8,128)(2,1)}, bf16[48,1536]{1,0:T(8,128)(2,1)}, u32[]{:S(2)}, u32[]{:S(2)}) collective-permute-start(bf16[48,1536]{1,0:T(8,128)(2,1)} %fusion.19), channel_id=1, source_target_pairs={{0,2},{1,3},{2,4},{3,5},{4,6},{5,7},{6,0},{7,1},{8,10},{9,11},{10,... | collective-permute-start | bytes 442376 | tf_op jit(solution)/shard_map/ppermute | solution.py:647
  99.5 67.5 %collective-permute-start.31 = (bf16[48,1536]{1,0:T(8,128)(2,1)}, bf16[48,1536]{1,0:T(8,128)(2,1)}, u32[]{:S(2)}, u32[]{:S(2)}) collective-permute-start(bf16[48,1536]{1,0:T(8,128)(2,1)} %fusion.19), channel_id=1, source_target_pairs={{0,4},{1,5},{2,6},{3,7},{4,0},{5,1},{6,2},{7,3},{8,12},{9,13},{10,... | collective-permute-start | bytes 442376 | tf_op jit(solution)/shard_map/ppermute | solution.py:647
  118.7 46.4 %collective-permute-start.24 = (bf16[4,384,384]{2,1,0:T(8,128)(2,1)S(1)}, bf16[4,384,384]{2,1,0:T(8,128)(2,1)}, u32[]{:S(2)}, u32[]{:S(2)}) collective-permute-start(bf16[4,384,384]{2,1,0:T(8,128)(2,1)S(1)} %pad_maximum_fusion.refs_0_), channel_id=1, source_target_pairs={{0,1},{1,0},{2,3},{3,2},{4,5},{5,4},{6,7},{7,6},{8,9},{9,8},{10,11... | collective-permute-start | bytes 3538952 | tf_op jit(solution)/shard_map/ppermute | solution.py:647
  121.0 36.0 %collective-permute-start.23 = (bf16[4,96,384]{2,1,0:T(8,128)(2,1)S(1)}, bf16[4,96,384]{2,1,0:T(8,128)(2,1)S(1)}, u32[]{:S(2)}, u32[]{:S(2)}) collective-permute-start(bf16[4,96,384]{2,1,0:T(8,128)(2,1)S(1)} %pad_maximum_fusion.6.refs_0_), channel_id=1, source_target_pairs={{0,1},{1,0},{2,3},{3,2},{4,5},{5,4},{6,7},{7,6},{8,9},{9,8},{10,11... | collective-permute-start | bytes 884744 | tf_op jit(solution)/shard_map/ppermute | solution.py:647
  122.4 41.4 %collective-permute-start.22 = (bf16[4,48,1536]{2,1,0:T(8,128)(2,1)S(1)}, bf16[4,48,1536]{2,1,0:T(8,128)(2,1)}, u32[]{:S(2)}, u32[]{:S(2)}) collective-permute-start(bf16[4,48,1536]{2,1,0:T(8,128)(2,1)S(1)} %pad_maximum_fusion.3.refs_0_), channel_id=1, source_target_pairs={{0,1},{1,0},{2,3},{3,2},{4,5},{5,4},{6,7},{7,6},{8,9},{9,8},{10,11... | collective-permute-start | bytes 1769480 | tf_op jit(solution)/shard_map/ppermute | solution.py:647
  163.8 26.0 %collective-permute-start.25 = (bf16[4,48,1536]{2,1,0:T(8,128)(2,1)S(1)}, bf16[4,48,1536]{2,1,0:T(8,128)(2,1)}, u32[]{:S(2)}, u32[]{:S(2)}) collective-permute-start(bf16[4,48,1536]{2,1,0:T(8,128)(2,1)S(1)} %pad_maximum_fusion.3.refs_0_), channel_id=1, source_target_pairs={{0,16},{1,17},{2,18},{3,19},{4,20},{5,21},{6,22},{7,23},{8,24},{9,... | collective-permute-start | bytes 1769480 | tf_op jit(solution)/shard_map/ppermute | solution.py:647
  165.1 25.2 %collective-permute-start.26 = (bf16[4,48,1536]{2,1,0:T(8,128)(2,1)}, bf16[4,48,1536]{2,1,0:T(8,128)(2,1)}, u32[]{:S(2)}, u32[]{:S(2)}) collective-permute-start(bf16[4,48,1536]{2,1,0:T(8,128)(2,1)} %collective-permute-done.22.refs_2_), channel_id=1, source_target_pairs={{0,16},{1,17},{2,18},{3,19},{4,20},{5,21},{6,22},{7,23},{8,24},{9,... | collective-permute-start | bytes 1769480 | tf_op jit(solution)/shard_map/ppermute | solution.py:647
  167.1 22.1 %collective-permute-start.28 = (bf16[96,1152]{1,0:T(8,128)(2,1)}, bf16[96,1152]{1,0:T(8,128)(2,1)S(1)}, u32[]{:S(2)}, u32[]{:S(2)}) collective-permute-start(bf16[96,1152]{1,0:T(8,128)(2,1)} %fusion.20), channel_id=1, source_target_pairs={{0,4},{1,5},{2,6},{3,7},{4,0},{5,1},{6,2},{7,3},{8,12},{9,13},{10,... | collective-permute-start | bytes 663560 | tf_op jit(solution)/shard_map/ppermute | solution.py:647
  172.4 22.0 %collective-permute-start.35 = (bf16[4,48,1536]{2,1,0:T(8,128)(2,1)S(1)}, bf16[4,48,1536]{2,1,0:T(8,128)(2,1)S(1)}, u32[]{:S(2)}, u32[]{:S(2)}) collective-permute-start(bf16[4,48,1536]{2,1,0:T(8,128)(2,1)S(1)} %pad_maximum_fusion.3.refs_0_), channel_id=1, source_target_pairs={{0,8},{1,9},{2,10},{3,11},{4,12},{5,13},{6,14},{7,15},{8,0},{9,1},... | collective-permute-start | bytes 1769480 | tf_op jit(solution)/shard_map/ppermute | solution.py:647
  189.1 24.3 %collective-permute-start.39 = (bf16[4,384,384]{2,1,0:T(8,128)(2,1)S(1)}, bf16[4,384,384]{2,1,0:T(8,128)(2,1)}, u32[]{:S(2)}, u32[]{:S(2)}) collective-permute-start(bf16[4,384,384]{2,1,0:T(8,128)(2,1)S(1)} %pad_maximum_fusion.refs_0_), channel_id=1, source_target_pairs={{0,8},{1,9},{2,10},{3,11},{4,12},{5,13},{6,14},{7,15},{8,0},{9,1},... | collective-permute-start | bytes 3538952 | tf_op jit(solution)/shard_map/ppermute | solution.py:647
  189.8 25.2 %collective-permute-start.40 = (bf16[4,384,384]{2,1,0:T(8,128)(2,1)}, bf16[4,384,384]{2,1,0:T(8,128)(2,1)}, u32[]{:S(2)}, u32[]{:S(2)}) collective-permute-start(bf16[4,384,384]{2,1,0:T(8,128)(2,1)} %collective-permute-done.24.refs_2_), channel_id=1, source_target_pairs={{0,8},{1,9},{2,10},{3,11},{4,12},{5,13},{6,14},{7,15},{8,0},{9,1},... | collective-permute-start | bytes 3538952 | tf_op jit(solution)/shard_map/ppermute | solution.py:647
  213.4 40.4 %collective-permute-start.46 = (bf16[192,384]{1,0:T(8,128)(2,1)}, bf16[192,384]{1,0:T(8,128)(2,1)S(1)}, u32[]{:S(2)}, u32[]{:S(2)}) collective-permute-start(bf16[192,384]{1,0:T(8,128)(2,1)} %fusion.17), channel_id=1, source_target_pairs={{0,2},{1,3},{2,4},{3,5},{4,6},{5,7},{6,0},{7,1},{8,10},{9,11},{10,... | collective-permute-start | bytes 442376 | tf_op jit(solution)/shard_map/ppermute | solution.py:647
  215.0 41.0 %collective-permute-start.47 = (bf16[192,384]{1,0:T(8,128)(2,1)}, bf16[192,384]{1,0:T(8,128)(2,1)S(1)}, u32[]{:S(2)}, u32[]{:S(2)}) collective-permute-start(bf16[192,384]{1,0:T(8,128)(2,1)} %fusion.17), channel_id=1, source_target_pairs={{0,4},{1,5},{2,6},{3,7},{4,0},{5,1},{6,2},{7,3},{8,12},{9,13},{10,... | collective-permute-start | bytes 442376 | tf_op jit(solution)/shard_map/ppermute | solution.py:647
  221.5 34.5 %collective-permute-start.48 = (bf16[192,384]{1,0:T(8,128)(2,1)}, bf16[192,384]{1,0:T(8,128)(2,1)S(1)}, u32[]{:S(2)}, u32[]{:S(2)}) collective-permute-start(bf16[192,384]{1,0:T(8,128)(2,1)} %fusion.17), channel_id=1, source_target_pairs={{0,6},{1,7},{2,0},{3,1},{4,2},{5,3},{6,4},{7,5},{8,14},{9,15},{10,... | collective-permute-start | bytes 442376 | tf_op jit(solution)/shard_map/ppermute | solution.py:647
  223.8 32.3 %collective-permute-start.42 = (bf16[4,48,1536]{2,1,0:T(8,128)(2,1)S(1)}, bf16[4,48,1536]{2,1,0:T(8,128)(2,1)S(1)}, u32[]{:S(2)}, u32[]{:S(2)}) collective-permute-start(bf16[4,48,1536]{2,1,0:T(8,128)(2,1)S(1)} %pad_maximum_fusion.4.refs_0_), channel_id=1, source_target_pairs={{0,1},{1,0},{2,3},{3,2},{4,5},{5,4},{6,7},{7,6},{8,9},{9,8},{10,11... | collective-permute-start | bytes 1769480 | tf_op jit(solution)/shard_map/ppermute | solution.py:647
  225.0 31.1 %collective-permute-start.41 = (bf16[4,96,1152]{2,1,0:T(8,128)(2,1)S(1)}, bf16[4,96,1152]{2,1,0:T(8,128)(2,1)S(1)}, u32[]{:S(2)}, u32[]{:S(2)}) collective-permute-start(bf16[4,96,1152]{2,1,0:T(8,128)(2,1)S(1)} %pad_maximum_fusion.2.refs_0_), channel_id=1, source_target_pairs={{0,1},{1,0},{2,3},{3,2},{4,5},{5,4},{6,7},{7,6},{8,9},{9,8},{10,11... | collective-permute-start | bytes 2654216 | tf_op jit(solution)/shard_map/ppermute | solution.py:647
  260.4 22.5 %collective-permute-start.52 = (bf16[4,192,384]{2,1,0:T(8,128)(2,1)S(1)}, bf16[4,192,384]{2,1,0:T(8,128)(2,1)}, u32[]{:S(2)}, u32[]{:S(2)}) collective-permute-start(bf16[4,192,384]{2,1,0:T(8,128)(2,1)S(1)} %pad_maximum_fusion.5.refs_0_), channel_id=1, source_target_pairs={{0,1},{1,0},{2,3},{3,2},{4,5},{5,4},{6,7},{7,6},{8,9},{9,8},{10,11... | collective-permute-start | bytes 1769480 | tf_op jit(solution)/shard_map/ppermute | solution.py:647
  262.3 54.3 %collective-permute-start.53 = (bf16[4,48,1536]{2,1,0:T(8,128)(2,1)S(1)}, bf16[4,48,1536]{2,1,0:T(8,128)(2,1)}, u32[]{:S(2)}, u32[]{:S(2)}) collective-permute-start(bf16[4,48,1536]{2,1,0:T(8,128)(2,1)S(1)} %pad_maximum_fusion.4.refs_0_), channel_id=1, source_target_pairs={{0,16},{1,17},{2,18},{3,19},{4,20},{5,21},{6,22},{7,23},{8,24},{9,... | collective-permute-start | bytes 1769480 | tf_op jit(solution)/shard_map/ppermute | solution.py:647
  263.6 54.7 %collective-permute-start.55 = (bf16[4,192,384]{2,1,0:T(8,128)(2,1)S(1)}, bf16[4,192,384]{2,1,0:T(8,128)(2,1)}, u32[]{:S(2)}, u32[]{:S(2)}) collective-permute-start(bf16[4,192,384]{2,1,0:T(8,128)(2,1)S(1)} %pad_maximum_fusion.5.refs_0_), channel_id=1, source_target_pairs={{0,16},{1,17},{2,18},{3,19},{4,20},{5,21},{6,22},{7,23},{8,24},{9,... | collective-permute-start | bytes 1769480 | tf_op jit(solution)/shard_map/ppermute | solution.py:647
  264.8 56.3 %collective-permute-start.63 = (bf16[4,192,384]{2,1,0:T(8,128)(2,1)S(1)}, bf16[4,192,384]{2,1,0:T(8,128)(2,1)S(1)}, u32[]{:S(2)}, u32[]{:S(2)}) collective-permute-start(bf16[4,192,384]{2,1,0:T(8,128)(2,1)S(1)} %pad_maximum_fusion.5.refs_0_), channel_id=1, source_target_pairs={{0,8},{1,9},{2,10},{3,11},{4,12},{5,13},{6,14},{7,15},{8,0},{9,1},... | collective-permute-start | bytes 1769480 | tf_op jit(solution)/shard_map/ppermute | solution.py:647
  281.7 36.6 %collective-permute-start.54 = (bf16[4,48,1536]{2,1,0:T(8,128)(2,1)S(1)}, bf16[4,48,1536]{2,1,0:T(8,128)(2,1)S(1)}, u32[]{:S(2)}, u32[]{:S(2)}) collective-permute-start(bf16[4,48,1536]{2,1,0:T(8,128)(2,1)S(1)} %collective-permute-done.42.refs_2_), channel_id=1, source_target_pairs={{0,16},{1,17},{2,18},{3,19},{4,20},{5,21},{6,22},{7,23},{8,24},{9,... | collective-permute-start | bytes 1769480 | tf_op jit(solution)/shard_map/ppermute | solution.py:647
  282.9 35.3 %collective-permute-start.56 = (bf16[4,192,384]{2,1,0:T(8,128)(2,1)}, bf16[4,192,384]{2,1,0:T(8,128)(2,1)S(1)}, u32[]{:S(2)}, u32[]{:S(2)}) collective-permute-start(bf16[4,192,384]{2,1,0:T(8,128)(2,1)} %collective-permute-done.52.refs_2_), channel_id=1, source_target_pairs={{0,16},{1,17},{2,18},{3,19},{4,20},{5,21},{6,22},{7,23},{8,24},{9,... | collective-permute-start | bytes 1769480 | tf_op jit(solution)/shard_map/ppermute | solution.py:647
  402.3 35.2 %collective-permute-start.68 = (bf16[1,4,2,2,48,1536]{5,4,3,2,1,0:T(8,128)(2,1)}, bf16[1,4,2,2,48,1536]{5,4,3,2,1,0:T(8,128)(2,1)S(1)}, u32[]{:S(2)}, u32[]{:S(2)}) collective-permute-start(bf16[1,4,2,2,48,1536]{5,4,3,2,1,0:T(8,128)(2,1)} %bitcast.227), channel_id=1, source_target_pairs={{0,8},{1,9},{2,10},{3,11},{4,12},{5,13},{6,14},{7,15},{8,0},{9,1},... | collective-permute-start | bytes 7077896 | tf_op jit(solution)/shard_map/ppermute | solution.py:647
  412.4 25.1 %collective-permute-start.67 = (bf16[1,4,2,2,192,384]{5,4,3,2,1,0:T(8,128)(2,1)}, bf16[1,4,2,2,192,384]{5,4,3,2,1,0:T(8,128)(2,1)}, u32[]{:S(2)}, u32[]{:S(2)}) collective-permute-start(bf16[1,4,2,2,192,384]{5,4,3,2,1,0:T(8,128)(2,1)} %bitcast.228), channel_id=1, source_target_pairs={{0,8},{1,9},{2,10},{3,11},{4,12},{5,13},{6,14},{7,15},{8,0},{9,1},... | collective-permute-start | bytes 7077896 | tf_op jit(solution)/shard_map/ppermute | solution.py:647
  442.2 45.0 %collective-permute-start.72 = (bf16[1,4,2,48,384]{4,3,2,1,0:T(8,128)(2,1)}, bf16[1,4,2,48,384]{4,3,2,1,0:T(8,128)(2,1)S(1)}, u32[]{:S(2)}, u32[]{:S(2)}) collective-permute-start(bf16[1,4,2,48,384]{4,3,2,1,0:T(8,128)(2,1)} %shard_map.297), channel_id=1, source_target_pairs={{0,1},{1,0},{2,3},{3,2},{4,5},{5,4},{6,7},{7,6},{8,9},{9,8},{10,11... | collective-permute-start | bytes 884744 | tf_op jit(solution)/shard_map/ppermute | solution.py:647
  447.8 39.4 %collective-permute-start.71 = (bf16[1,4,2,48,1536]{4,3,2,1,0:T(8,128)(2,1)}, bf16[1,4,2,48,1536]{4,3,2,1,0:T(8,128)(2,1)S(1)}, u32[]{:S(2)}, u32[]{:S(2)}) collective-permute-start(bf16[1,4,2,48,1536]{4,3,2,1,0:T(8,128)(2,1)} %shard_map.295), channel_id=1, source_target_pairs={{0,16},{1,17},{2,18},{3,19},{4,20},{5,21},{6,22},{7,23},{8,24},{9,... | collective-permute-start | bytes 3538952 | tf_op jit(solution)/shard_map/ppermute | solution.py:647
  453.4 33.8 %collective-permute-start.70 = (bf16[1,4,2,192,384]{4,3,2,1,0:T(8,128)(2,1)}, bf16[1,4,2,192,384]{4,3,2,1,0:T(8,128)(2,1)S(1)}, u32[]{:S(2)}, u32[]{:S(2)}) collective-permute-start(bf16[1,4,2,192,384]{4,3,2,1,0:T(8,128)(2,1)} %shard_map.293), channel_id=1, source_target_pairs={{0,1},{1,0},{2,3},{3,2},{4,5},{5,4},{6,7},{7,6},{8,9},{9,8},{10,11... | collective-permute-start | bytes 3538952 | tf_op jit(solution)/shard_map/ppermute | solution.py:647
  493.8 23.1 %collective-permute-start.73 = (bf16[3,4,2,2,48,384]{5,4,3,2,1,0:T(8,128)(2,1)}, bf16[3,4,2,2,48,384]{5,4,3,2,1,0:T(8,128)(2,1)S(1)}, u32[]{:S(2)}, u32[]{:S(2)}) collective-permute-start(bf16[3,4,2,2,48,384]{5,4,3,2,1,0:T(8,128)(2,1)} %bitcast.230), channel_id=1, source_target_pairs={{0,8},{1,9},{2,10},{3,11},{4,12},{5,13},{6,14},{7,15},{8,0},{9,1},... | collective-permute-start | bytes 5308424 | tf_op jit(solution)/shard_map/ppermute | solution.py:647
  497.5 54.2 %collective-permute-start.78 = (bf16[1,2,48,384]{3,2,1,0:T(8,128)(2,1)}, bf16[1,2,48,384]{3,2,1,0:T(8,128)(2,1)S(1)}, u32[]{:S(2)}, u32[]{:S(2)}) collective-permute-start(bf16[1,2,48,384]{3,2,1,0:T(8,128)(2,1)} %get-tuple-element.272), channel_id=1, source_target_pairs={{0,2},{1,3},{2,4},{3,5},{4,6},{5,7},{6,0},{7,1},{8,10},{9,11},{10,... | collective-permute-start | bytes 221192 | tf_op jit(solution)/shard_map/ppermute | solution.py:647
  497.5 54.3 %collective-permute-start.79 = (bf16[1,2,48,384]{3,2,1,0:T(8,128)(2,1)}, bf16[1,2,48,384]{3,2,1,0:T(8,128)(2,1)S(1)}, u32[]{:S(2)}, u32[]{:S(2)}) collective-permute-start(bf16[1,2,48,384]{3,2,1,0:T(8,128)(2,1)} %get-tuple-element.273), channel_id=1, source_target_pairs={{0,4},{1,5},{2,6},{3,7},{4,0},{5,1},{6,2},{7,3},{8,12},{9,13},{10,... | collective-permute-start | bytes 221192 | tf_op jit(solution)/shard_map/ppermute | solution.py:647
  498.8 54.5 %collective-permute-start.80 = (bf16[1,2,48,384]{3,2,1,0:T(8,128)(2,1)}, bf16[1,2,48,384]{3,2,1,0:T(8,128)(2,1)S(1)}, u32[]{:S(2)}, u32[]{:S(2)}) collective-permute-start(bf16[1,2,48,384]{3,2,1,0:T(8,128)(2,1)} %get-tuple-element.274), channel_id=1, source_target_pairs={{0,6},{1,7},{2,0},{3,1},{4,2},{5,3},{6,4},{7,5},{8,14},{9,15},{10,... | collective-permute-start | bytes 221192 | tf_op jit(solution)/shard_map/ppermute | solution.py:647
  505.5 73.2 %collective-permute-start.77 = (bf16[1,4,48,1536]{3,2,1,0:T(8,128)(2,1)}, bf16[1,4,48,1536]{3,2,1,0:T(8,128)(2,1)}, u32[]{:S(2)}, u32[]{:S(2)}) collective-permute-start(bf16[1,4,48,1536]{3,2,1,0:T(8,128)(2,1)} %shard_map.301), channel_id=1, source_target_pairs={{0,1},{1,0},{2,3},{3,2},{4,5},{5,4},{6,7},{7,6},{8,9},{9,8},{10,11... | collective-permute-start | bytes 1769480 | tf_op jit(solution)/shard_map/ppermute | solution.py:647
  522.4 56.3 %collective-permute-start.81 = (bf16[3,4,2,48,384]{4,3,2,1,0:T(8,128)(2,1)}, bf16[3,4,2,48,384]{4,3,2,1,0:T(8,128)(2,1)S(1)}, u32[]{:S(2)}, u32[]{:S(2)}) collective-permute-start(bf16[3,4,2,48,384]{4,3,2,1,0:T(8,128)(2,1)} %shard_map.304), channel_id=1, source_target_pairs={{0,16},{1,17},{2,18},{3,19},{4,20},{5,21},{6,22},{7,23},{8,24},{9,... | collective-permute-start | bytes 2654216 | tf_op jit(solution)/shard_map/ppermute | solution.py:647
  551.8 24.0 %collective-permute-start.75 = (bf16[1,2,192,384]{3,2,1,0:T(8,128)(2,1)}, bf16[1,2,192,384]{3,2,1,0:T(8,128)(2,1)S(1)}, u32[]{:S(2)}, u32[]{:S(2)}) collective-permute-start(bf16[1,2,192,384]{3,2,1,0:T(8,128)(2,1)} %get-tuple-element.268), channel_id=1, source_target_pairs={{0,4},{1,5},{2,6},{3,7},{4,0},{5,1},{6,2},{7,3},{8,12},{9,13},{10,... | collective-permute-start | bytes 884744 | tf_op jit(solution)/shard_map/ppermute | solution.py:647
  553.3 25.4 %collective-permute-start.76 = (bf16[1,2,192,384]{3,2,1,0:T(8,128)(2,1)}, bf16[1,2,192,384]{3,2,1,0:T(8,128)(2,1)}, u32[]{:S(2)}, u32[]{:S(2)}) collective-permute-start(bf16[1,2,192,384]{3,2,1,0:T(8,128)(2,1)} %get-tuple-element.269), channel_id=1, source_target_pairs={{0,6},{1,7},{2,0},{3,1},{4,2},{5,3},{6,4},{7,5},{8,14},{9,15},{10,... | collective-permute-start | bytes 884744 | tf_op jit(solution)/shard_map/ppermute | solution.py:647
  562.3 62.3 %collective-permute-start.89 = (bf16[1,4,2,2,48,1536]{5,4,3,2,1,0:T(8,128)(2,1)}, bf16[1,4,2,2,48,1536]{5,4,3,2,1,0:T(8,128)(2,1)S(1)}, u32[]{:S(2)}, u32[]{:S(2)}) collective-permute-start(bf16[1,4,2,2,48,1536]{5,4,3,2,1,0:T(8,128)(2,1)} %bitcast.225), channel_id=1, source_target_pairs={{0,8},{1,9},{2,10},{3,11},{4,12},{5,13},{6,14},{7,15},{8,0},{9,1},... | collective-permute-start | bytes 7077896 | tf_op jit(solution)/shard_map/ppermute | solution.py:647
  588.5 36.2 %collective-permute-start.88 = (bf16[1,4,2,2,192,384]{5,4,3,2,1,0:T(8,128)(2,1)}, bf16[1,4,2,2,192,384]{5,4,3,2,1,0:T(8,128)(2,1)}, u32[]{:S(2)}, u32[]{:S(2)}) collective-permute-start(bf16[1,4,2,2,192,384]{5,4,3,2,1,0:T(8,128)(2,1)} %bitcast.226), channel_id=1, source_target_pairs={{0,8},{1,9},{2,10},{3,11},{4,12},{5,13},{6,14},{7,15},{8,0},{9,1},... | collective-permute-start | bytes 7077896 | tf_op jit(solution)/shard_map/ppermute | solution.py:647
  628.6 39.5 %collective-permute-start.94 = (bf16[3,48,384]{2,1,0:T(8,128)(2,1)}, bf16[3,48,384]{2,1,0:T(8,128)(2,1)}, u32[]{:S(2)}, u32[]{:S(2)}) collective-permute-start(bf16[3,48,384]{2,1,0:T(8,128)(2,1)} %get-tuple-element.305), channel_id=1, source_target_pairs={{0,2},{1,3},{2,4},{3,5},{4,6},{5,7},{6,0},{7,1},{8,10},{9,11},{10,... | collective-permute-start | bytes 331784 | tf_op jit(solution)/shard_map/ppermute | solution.py:647
  630.0 38.3 %collective-permute-start.95 = (bf16[3,48,384]{2,1,0:T(8,128)(2,1)}, bf16[3,48,384]{2,1,0:T(8,128)(2,1)}, u32[]{:S(2)}, u32[]{:S(2)}) collective-permute-start(bf16[3,48,384]{2,1,0:T(8,128)(2,1)} %get-tuple-element.306), channel_id=1, source_target_pairs={{0,4},{1,5},{2,6},{3,7},{4,0},{5,1},{6,2},{7,3},{8,12},{9,13},{10,... | collective-permute-start | bytes 331784 | tf_op jit(solution)/shard_map/ppermute | solution.py:647
  630.7 37.8 %collective-permute-start.96 = (bf16[3,48,384]{2,1,0:T(8,128)(2,1)}, bf16[3,48,384]{2,1,0:T(8,128)(2,1)}, u32[]{:S(2)}, u32[]{:S(2)}) collective-permute-start(bf16[3,48,384]{2,1,0:T(8,128)(2,1)} %get-tuple-element.307), channel_id=1, source_target_pairs={{0,6},{1,7},{2,0},{3,1},{4,2},{5,3},{6,4},{7,5},{8,14},{9,15},{10,... | collective-permute-start | bytes 331784 | tf_op jit(solution)/shard_map/ppermute | solution.py:647
  635.3 31.5 %collective-permute-start.93 = (bf16[1,2,48,384]{3,2,1,0:T(8,128)(2,1)}, bf16[1,2,48,384]{3,2,1,0:T(8,128)(2,1)}, u32[]{:S(2)}, u32[]{:S(2)}) collective-permute-start(bf16[1,2,48,384]{3,2,1,0:T(8,128)(2,1)} %shard_map.315), channel_id=1, source_target_pairs={{0,8},{1,9},{2,10},{3,11},{4,12},{5,13},{6,14},{7,15},{8,0},{9,1},... | collective-permute-start | bytes 221192 | tf_op jit(solution)/shard_map/ppermute | solution.py:647
  651.6 51.5 %collective-permute-start.99 = (bf16[1,4,2,48,384]{4,3,2,1,0:T(8,128)(2,1)}, bf16[1,4,2,48,384]{4,3,2,1,0:T(8,128)(2,1)S(1)}, u32[]{:S(2)}, u32[]{:S(2)}) collective-permute-start(bf16[1,4,2,48,384]{4,3,2,1,0:T(8,128)(2,1)} %shard_map.322), channel_id=1, source_target_pairs={{0,1},{1,0},{2,3},{3,2},{4,5},{5,4},{6,7},{7,6},{8,9},{9,8},{10,11... | collective-permute-start | bytes 884744 | tf_op jit(solution)/shard_map/ppermute | solution.py:647
  666.8 36.3 %collective-permute-start.98 = (bf16[1,4,2,48,1536]{4,3,2,1,0:T(8,128)(2,1)S(1)}, bf16[1,4,2,48,1536]{4,3,2,1,0:T(8,128)(2,1)S(1)}, u32[]{:S(2)}, u32[]{:S(2)}) collective-permute-start(bf16[1,4,2,48,1536]{4,3,2,1,0:T(8,128)(2,1)S(1)} %copy-done.31), channel_id=1, source_target_pairs={{0,16},{1,17},{2,18},{3,19},{4,20},{5,21},{6,22},{7,23},{8,24},{9,... | collective-permute-start | bytes 3538952 | tf_op jit(solution)/shard_map/ppermute | solution.py:647
  668.0 35.1 %collective-permute-start.97 = (bf16[1,4,2,192,384]{4,3,2,1,0:T(8,128)(2,1)}, bf16[1,4,2,192,384]{4,3,2,1,0:T(8,128)(2,1)S(1)}, u32[]{:S(2)}, u32[]{:S(2)}) collective-permute-start(bf16[1,4,2,192,384]{4,3,2,1,0:T(8,128)(2,1)} %shard_map.318), channel_id=1, source_target_pairs={{0,1},{1,0},{2,3},{3,2},{4,5},{5,4},{6,7},{7,6},{8,9},{9,8},{10,11... | collective-permute-start | bytes 3538952 | tf_op jit(solution)/shard_map/ppermute | solution.py:647
  668.3 34.8 %collective-permute-start.92 = (bf16[1,48,1536]{2,1,0:T(8,128)(2,1)}, bf16[1,48,1536]{2,1,0:T(8,128)(2,1)}, u32[]{:S(2)}, u32[]{:S(2)}) collective-permute-start(bf16[1,48,1536]{2,1,0:T(8,128)(2,1)} %shard_map.314.refs_4_), channel_id=1, source_target_pairs={{0,16},{1,17},{2,18},{3,19},{4,20},{5,21},{6,22},{7,23},{8,24},{9,... | collective-permute-start | bytes 442376 | tf_op jit(solution)/shard_map/ppermute | solution.py:647
  668.5 34.6 %collective-permute-start.91 = (bf16[1,2,192,384]{3,2,1,0:T(8,128)(2,1)S(1)}, bf16[1,2,192,384]{3,2,1,0:T(8,128)(2,1)}, u32[]{:S(2)}, u32[]{:S(2)}) collective-permute-start(bf16[1,2,192,384]{3,2,1,0:T(8,128)(2,1)S(1)} %copy-done.28), channel_id=1, source_target_pairs={{0,8},{1,9},{2,10},{3,11},{4,12},{5,13},{6,14},{7,15},{8,0},{9,1},... | collective-permute-start | bytes 884744 | tf_op jit(solution)/shard_map/ppermute | solution.py:647
  709.9 29.8 %collective-permute-start.100 = (bf16[3,4,2,2,48,384]{5,4,3,2,1,0:T(8,128)(2,1)}, bf16[3,4,2,2,48,384]{5,4,3,2,1,0:T(8,128)(2,1)S(1)}, u32[]{:S(2)}, u32[]{:S(2)}) collective-permute-start(bf16[3,4,2,2,48,384]{5,4,3,2,1,0:T(8,128)(2,1)} %bitcast.229), channel_id=1, source_target_pairs={{0,8},{1,9},{2,10},{3,11},{4,12},{5,13},{6,14},{7,15},{8,0},{9,1},... | collective-permute-start | bytes 5308424 | tf_op jit(solution)/shard_map/ppermute | solution.py:647
  738.5 44.1 %collective-permute-start.129 = (bf16[1,4,48,1536]{3,2,1,0:T(8,128)(2,1)}, bf16[1,4,48,1536]{3,2,1,0:T(8,128)(2,1)S(1)}, u32[]{:S(2)}, u32[]{:S(2)}) collective-permute-start(bf16[1,4,48,1536]{3,2,1,0:T(8,128)(2,1)} %shard_map.336), channel_id=1, source_target_pairs={{0,1},{1,0},{2,3},{3,2},{4,5},{5,4},{6,7},{7,6},{8,9},{9,8},{10,11... | collective-permute-start | bytes 1769480 | tf_op jit(solution)/shard_map/ppermute | solution.py:647
  752.4 26.7 %collective-permute-start.140 = (bf16[1,2,192,384]{3,2,1,0:T(8,128)(2,1)}, bf16[1,2,192,384]{3,2,1,0:T(8,128)(2,1)S(1)}, u32[]{:S(2)}, u32[]{:S(2)}) collective-permute-start(bf16[1,2,192,384]{3,2,1,0:T(8,128)(2,1)} %get-tuple-element.344), channel_id=1, source_target_pairs={{0,6},{1,7},{2,0},{3,1},{4,2},{5,3},{6,4},{7,5},{8,14},{9,15},{10,... | collective-permute-start | bytes 884744 | tf_op jit(solution)/shard_map/ppermute | solution.py:647
  762.3 25.8 %collective-permute-start.115 = (f32[1536]{0:T(1024)S(1)}, f32[1536]{0:T(1024)S(1)}, u32[]{:S(2)}, u32[]{:S(2)}) collective-permute-start(f32[1536]{0:T(1024)S(1)} %add.129), channel_id=1, source_target_pairs={{0,4},{1,5},{2,6},{3,7},{4,0},{5,1},{6,2},{7,3},{8,12},{9,13},{10,... | collective-permute-start | bytes 18440 | tf_op jit(solution)/shard_map/ppermute | solution.py:647
  767.8 21.7 %collective-permute-start.124 = (bf16[1,2,48,384]{3,2,1,0:T(8,128)(2,1)S(1)}, bf16[1,2,48,384]{3,2,1,0:T(8,128)(2,1)S(1)}, u32[]{:S(2)}, u32[]{:S(2)}) collective-permute-start(bf16[1,2,48,384]{3,2,1,0:T(8,128)(2,1)S(1)} %copy-done.118), channel_id=1, source_target_pairs={{0,2},{1,3},{2,4},{3,5},{4,6},{5,7},{6,0},{7,1},{8,10},{9,11},{10,... | collective-permute-start | bytes 221192 | tf_op jit(solution)/shard_map/ppermute | solution.py:647
  771.2 40.7 %collective-permute-start.102 = (bf16[3,4,48,384]{3,2,1,0:T(8,128)(2,1)}, bf16[3,4,48,384]{3,2,1,0:T(8,128)(2,1)S(1)}, u32[]{:S(2)}, u32[]{:S(2)}) collective-permute-start(bf16[3,4,48,384]{3,2,1,0:T(8,128)(2,1)} %shard_map.327), channel_id=1, source_target_pairs={{0,1},{1,0},{2,3},{3,2},{4,5},{5,4},{6,7},{7,6},{8,9},{9,8},{10,11... | collective-permute-start | bytes 1327112 | tf_op jit(solution)/shard_map/ppermute | solution.py:647
  788.1 23.5 %collective-permute-start.141 = (bf16[1,2,192,384]{3,2,1,0:T(8,128)(2,1)S(1)}, bf16[1,2,192,384]{3,2,1,0:T(8,128)(2,1)S(1)}, u32[]{:S(2)}, u32[]{:S(2)}) collective-permute-start(bf16[1,2,192,384]{3,2,1,0:T(8,128)(2,1)S(1)} %copy-done.30), channel_id=1, source_target_pairs={{0,16},{1,17},{2,18},{3,19},{4,20},{5,21},{6,22},{7,23},{8,24},{9,... | collective-permute-start | bytes 884744 | tf_op jit(solution)/shard_map/ppermute | solution.py:647
  795.6 27.0 %collective-permute-start.136 = (bf16[1,48,1536]{2,1,0:T(8,128)(2,1)S(1)}, bf16[1,48,1536]{2,1,0:T(8,128)(2,1)S(1)}, u32[]{:S(2)}, u32[]{:S(2)}) collective-permute-start(bf16[1,48,1536]{2,1,0:T(8,128)(2,1)S(1)} %copy-done.46), channel_id=1, source_target_pairs={{0,8},{1,9},{2,10},{3,11},{4,12},{5,13},{6,14},{7,15},{8,0},{9,1},... | collective-permute-start | bytes 442376 | tf_op jit(solution)/shard_map/ppermute | solution.py:647
  (198 other events, 2750.4 us)

commit v4 on v3

--- a/solution.py
+++ b/solution.py
@@ -54,7 +54,8 @@
     return [values[at : at + CLUSTER] for at in range(0, values.shape[0], CLUSTER)]
 
 
-def attend_kernel(slot_ref, query_ref, key_ref, value_ref, bias_ref, ctx_ref, qk_ref, val_ref, p_ref):
+def attend_kernel(slot_ref, query_ref, key_ref, value_ref, bias_ref, *refs):
+    ctx_ref, qk_ref, val_ref, p_ref = refs[-4:]
     low = first_lanes(TREE_LEN)
     query = query_ref[...] * jnp.bfloat16(HEAD_DIM**-0.5)
     key = key_ref[...]
@@ -93,7 +94,7 @@
     ctx_ref[...] = jnp.where(low, context[0], context[1]).astype(jnp.bfloat16)
 
 
-def attend_back_kernel(slot_ref, grad_ref, qk_ref, val_ref, p_ref, out_ref, sums_ref):
+def attend_back_kernel(at_ref, slot_ref, grad_ref, qk_ref, val_ref, p_ref, out_ref, sums_ref):
     low = first_lanes(TREE_LEN)
     grads = grad_ref[...]
     placed = []
@@ -133,12 +134,12 @@
     sums_ref[0, 0] = jnp.concatenate(sums + [jnp.zeros((5, LANES), jnp.float32)], axis=0)
 
 
-def slot_spec():
-    return pl.BlockSpec((1, 1, 2, TREE_LEN), lambda tree, pair: (tree, pair, 0, 0))
-
-
-def head_spec():
-    return pl.BlockSpec((1, 2, TREE_LEN, LANES), lambda tree, pair: (tree, pair, 0, 0))
+def slot_spec(start=0):
+    return pl.BlockSpec((1, 1, 2, TREE_LEN), lambda tree, pair: (tree, start + pair, 0, 0))
+
+
+def head_spec(start=0):
+    return pl.BlockSpec((1, 2, TREE_LEN, LANES), lambda tree, pair: (tree, start + pair, 0, 0))
 
 
 def column_spec(offset):
@@ -149,52 +150,75 @@
     return pltpu.CompilerParams(vmem_limit_bytes=KERNEL_VMEM)
 
 
-def attend(projected, slots, bias):
+def attend(projected, slots, bias, half, before):
     trees = slots.shape[0]
+    start = half * (PAIRS // 2)
     stored = jax.ShapeDtypeStruct((trees, HEADS, TREE_LEN, LANES), jnp.bfloat16)
     return pl.pallas_call(
         attend_kernel,
-        grid=(trees, PAIRS),
+        grid=(trees, PAIRS // 2),
         in_specs=[
-            slot_spec(),
-            column_spec(0),
-            column_spec(PAIRS),
-            column_spec(2 * PAIRS),
-            head_spec(),
-        ],
-        out_specs=[column_spec(0), head_spec(), head_spec(), head_spec()],
+            slot_spec(start),
+            column_spec(start),
+            column_spec(PAIRS + start),
+            column_spec(2 * PAIRS + start),
+            head_spec(start),
+        ]
+        + [pl.BlockSpec(memory_space=pl.ANY)] * len(before),
+        out_specs=[column_spec(start), head_spec(start), head_spec(start), head_spec(start)],
         out_shape=[
             jax.ShapeDtypeStruct((trees * TREE_LEN, D), jnp.bfloat16),
             stored,
             stored,
             stored,
         ],
+        input_output_aliases={5 + place: place for place in range(len(before))},
         compiler_params=kernel_params(),
         cost_estimate=pl.CostEstimate(
-            flops=trees * 30_000_000_000, bytes_accessed=trees * 20_000_000, transcendentals=0
+            flops=trees * 15_000_000_000, bytes_accessed=trees * 10_000_000, transcendentals=0
         ),
-    )(slots, projected, projected, projected, bias)
-
-
-def attend_back(grad_context, slots, kept):
+    )(slots, projected, projected, projected, bias, *before)
+
+
+def attend_back(grad_context, slots, kept, at, other):
     trees = slots.shape[0]
+    count = PAIRS // CORES
+    flip = 1 if other else 0
+
+    def pair_of(pair, at):
+        return lax.rem(at[3] + flip, CORES) * count + pair
+
+    head = pl.BlockSpec(
+        (1, 2, TREE_LEN, LANES), lambda tree, pair, at: (tree, pair_of(pair, at), 0, 0)
+    )
     return pl.pallas_call(
         attend_back_kernel,
-        grid=(trees, PAIRS),
-        in_specs=[slot_spec(), column_spec(0), head_spec(), head_spec(), head_spec()],
-        out_specs=[
-            pl.BlockSpec((3, TREE_LEN, LANES), lambda tree, pair: (0, tree, pair)),
-            pl.BlockSpec((1, 1, 8, LANES), lambda tree, pair: (tree, pair, 0, 0)),
-        ],
+        grid_spec=pltpu.PrefetchScalarGridSpec(
+            num_scalar_prefetch=1,
+            grid=(trees, count),
+            in_specs=[
+                pl.BlockSpec(
+                    (1, 1, 2, TREE_LEN), lambda tree, pair, at: (tree, pair_of(pair, at), 0, 0)
+                ),
+                pl.BlockSpec((TREE_LEN, LANES), lambda tree, pair, at: (tree, pair_of(pair, at))),
+                head,
+                head,
+                head,
+            ],
+            out_specs=[
+                pl.BlockSpec((3, TREE_LEN, LANES), lambda tree, pair, at: (0, tree, pair)),
+                pl.BlockSpec((1, 1, 8, LANES), lambda tree, pair, at: (tree, pair, 0, 0)),
+            ],
+        ),
         out_shape=[
-            jax.ShapeDtypeStruct((3, trees * TREE_LEN, D), jnp.bfloat16),
-            jax.ShapeDtypeStruct((trees, PAIRS, 8, LANES), jnp.float32),
+            jax.ShapeDtypeStruct((3, trees * TREE_LEN, D // CORES), jnp.bfloat16),
+            jax.ShapeDtypeStruct((trees, count, 8, LANES), jnp.float32),
         ],
         compiler_params=kernel_params(),
         cost_estimate=pl.CostEstimate(
-            flops=trees * 40_000_000_000, bytes_accessed=trees * 20_000_000, transcendentals=0
+            flops=trees * 17_000_000_000, bytes_accessed=trees * 10_000_000, transcendentals=0
         ),
-    )(slots, grad_context, *kept)
+    )(at, slots, grad_context, *kept)
 
 
 def erf_parts(values):
@@ -288,14 +312,20 @@
     result_low_ref[...] = result.astype(jnp.bfloat16)
 
 
+def add_projected(grad, at_ref, own_ref, away_ref, weight_ref):
+    half = own_ref.shape[2]
+    for flip, ref in enumerate((own_ref, away_ref)):
+        core = lax.rem(at_ref[3] + flip, CORES)
+        for part in range(3):
+            column = pl.multiple_of((part * CORES + core) * half, 128)
+            grad = grad + contract_last(ref[part], weight_ref[:, pl.ds(column, half)])
+    return grad
+
+
 def feed_back_kernel(with_proj, *refs):
     if with_proj:
-        above_ref, proj_ref, qkv_weight_ref, *refs = refs
-        grad = above_ref[...]
-        for part in range(3):
-            grad = grad + contract_last(
-                proj_ref[part], qkv_weight_ref[:, part * D : (part + 1) * D]
-            )
+        above_ref, at_ref, own_ref, away_ref, qkv_weight_ref, *refs = refs
+        grad = add_projected(above_ref[...], at_ref, own_ref, away_ref, qkv_weight_ref)
     else:
         above_ref, *refs = refs
         grad = above_ref[...].astype(jnp.float32)
@@ -351,11 +381,8 @@
     context_ref[...] = contract_last(low, out_weight_ref[...]).astype(jnp.bfloat16)
 
 
-def input_grad_kernel(above_ref, proj_ref, weight_ref, out_ref):
-    grad = above_ref[...]
-    for part in range(3):
-        grad = grad + contract_last(proj_ref[part], weight_ref[:, part * D : (part + 1) * D])
-    out_ref[...] = grad
+def input_grad_kernel(above_ref, at_ref, own_ref, away_ref, weight_ref, out_ref):
+    out_ref[...] = add_projected(above_ref[...], at_ref, own_ref, away_ref, weight_ref)
 
 
 def prep_kernel(parent_ref, segment_ref, cluster_ref, slot_ref, bias_ref):
@@ -413,7 +440,7 @@
 
 
 def part_spec(rows=ROW_TILE):
-    return pl.BlockSpec((3, rows, D), lambda i: (0, i, 0))
+    return pl.BlockSpec((3, rows, D // CORES), lambda i: (0, i, 0))
 
 
 def cost(flops, *arrays):
@@ -476,15 +503,20 @@
     )(context, rows, *weights, *vectors)
 
 
-def feed_back(above, proj, qkv_weight, saved, weights, gains):
+def feed_back(above, proj, qkv_weight, at, saved, weights, gains):
     count = above.shape[0]
     width = weights[1].shape[1]
     f32 = jnp.float32
     gains = [gain[None] for gain in gains]
     lead, lead_specs = [above], [row_spec(D)]
     if proj is not None:
-        lead += [proj, qkv_weight]
-        lead_specs += [part_spec(), whole_spec(qkv_weight.shape)]
+        lead += [at, *proj, qkv_weight]
+        lead_specs += [
+            pl.BlockSpec(memory_space=pltpu.SMEM),
+            part_spec(),
+            part_spec(),
+            whole_spec(qkv_weight.shape),
+        ]
     return pl.pallas_call(
         functools.partial(feed_back_kernel, proj is not None),
         grid=(count // ROW_TILE,),
@@ -515,17 +547,23 @@
     )(*lead, *saved, *weights, *gains)
 
 
-def input_grad(above, proj, qkv_weight):
+def input_grad(above, proj, qkv_weight, at):
     count = above.shape[0]
     return pl.pallas_call(
         input_grad_kernel,
         grid=(count // ROW_TILE,),
-        in_specs=[row_spec(D), part_spec(), whole_spec(qkv_weight.shape)],
+        in_specs=[
+            row_spec(D),
+            pl.BlockSpec(memory_space=pltpu.SMEM),
+            part_spec(),
+            part_spec(),
+            whole_spec(qkv_weight.shape),
+        ],
         out_specs=row_spec(D),
         out_shape=shape_of(count, D, jnp.float32),
         compiler_params=kernel_params(),
-        cost_estimate=cost(2.4 * count * D * 3 * D, above, proj, qkv_weight),
-    )(above, proj, qkv_weight)
+        cost_estimate=cost(2.4 * count * D * 3 * D, above, qkv_weight),
+    )(above, at, *proj, qkv_weight)
 
 
 def prepare(segment, parent, clusters):
@@ -552,33 +590,84 @@
     )(parent, segment, clusters)
 
 
-def weight_grad_kernel(at_ref, left_ref, right_ref, out_ref):
-    for part in range(right_ref.shape[0]):
-        out_ref[part] = contract_first(left_ref[...], right_ref[part]).astype(jnp.bfloat16)
-
-
-def weight_grad(left, right, at, other):
-    count, depth = left.shape
-    parts, _, width = right.shape
-    half = width // CORES
-    flip = 1 if other else 0
-    return pl.pallas_call(
-        weight_grad_kernel,
-        grid_spec=pltpu.PrefetchScalarGridSpec(
-            num_scalar_prefetch=1,
-            grid=(depth // DEPTH_TILE,),
-            in_specs=[
-                pl.BlockSpec((count, DEPTH_TILE), lambda i, at: (0, i)),
-                pl.BlockSpec(
-                    (parts, count, half), lambda i, at: (0, 0, lax.rem(at[3] + flip, CORES))
-                ),
-            ],
-            out_specs=pl.BlockSpec((parts, DEPTH_TILE, half), lambda i, at: (0, i, 0)),
-        ),
-        out_shape=jax.ShapeDtypeStruct((parts, depth, half), jnp.bfloat16),
-        compiler_params=kernel_params(),
-        cost_estimate=cost(3 * count * depth * parts * half, left, right),
-    )(at, left, right)
+def weight_grad_kernel(split_y, at_ref, left_ref, right_ref, *refs):
+    product = contract_first(
+        left_ref[...].reshape(left_ref.shape[-2:]), right_ref[...].reshape(right_ref.shape[-2:])
+    )
+    if split_y is None:
+        (out_ref,) = refs
+        out_ref[...] = product.astype(jnp.bfloat16).reshape(out_ref.shape)
+        return
+    near_ref, send_ref, keep_ref, sum_ref = refs
+    total = product + near_ref[...].astype(jnp.float32).reshape(product.shape)
+    sum_ref[...] = total.astype(jnp.bfloat16).reshape(sum_ref.shape)
+    if split_y:
+        send_ref[0] = sum_ref[:, :, 1 - at_ref[2]]
+        keep_ref[0] = sum_ref[:, :, at_ref[2]]
+    else:
+        send_ref[0] = sum_ref[:, 1 - at_ref[1]]
+        keep_ref[0] = sum_ref[:, at_ref[1]]
+
+
+class Grad:
+    def __init__(self, left, own, away, cut, tiles, half):
+        self.left, self.rights = left, (own, away)
+        self.cut, self.tiles, self.half = cut, tiles, half
+        self.depth = left.shape[1]
+        self.parts = 1 if self.depth > D else tiles
+        self.rows = self.depth // (CHIPS_Z * CHIPS_X)
+
+    def product(self, at, other, split_y=None, near=None):
+        flip = 1 if other else 0
+        left, right = self.left, self.rights[flip]
+        count = left.shape[0]
+        tall = self.depth > D
+        core = lambda at: lax.rem(at[3] + flip, CORES)
+        in_specs = [
+            pl.BlockSpec((count, D), (lambda i, at: (0, i)) if tall else (lambda i, at: (0, 0)))
+        ]
+        if not self.cut:
+            in_specs.append(pl.BlockSpec((1, count, self.half), lambda i, at: (i, 0, 0)))
+        elif tall:
+            in_specs.append(pl.BlockSpec((count, self.half), lambda i, at: (0, core(at))))
+        else:
+            in_specs.append(
+                pl.BlockSpec((count, self.half), lambda i, at: (0, core(at) * self.tiles + i))
+            )
+        zs = D // (self.rows * CHIPS_X)
+        place = (lambda i: (0, i)) if tall else (lambda i: (i, 0))
+        whole = (self.parts, CHIPS_Z, CHIPS_X, self.rows, self.half)
+        block = (1, zs, CHIPS_X, self.rows, self.half)
+        full = pl.BlockSpec(block, lambda i, at: (*place(i), 0, 0, 0))
+        args, scratch = [left, right], []
+        if split_y is None:
+            out_specs, shapes = full, jax.ShapeDtypeStruct(whole, jnp.bfloat16)
+        else:
+            in_specs.append(full)
+            args.append(near)
+            if split_y:
+                short = self.rows // CHIPS_Y
+                kept = (CHIPS_X, short, self.half)
+                scratch = [pltpu.VMEM((zs, CHIPS_X, CHIPS_Y, short, self.half), jnp.bfloat16)]
+            else:
+                kept = (self.rows, self.half)
+                scratch = [pltpu.VMEM((zs, CHIPS_X, self.rows, self.half), jnp.bfloat16)]
+            rest = (0,) * len(kept)
+            out_specs = [pl.BlockSpec((1, zs, *kept), lambda i, at: (*place(i), *rest))] * 2
+            shapes = [jax.ShapeDtypeStruct((self.parts, CHIPS_Z, *kept), jnp.bfloat16)] * 2
+        return pl.pallas_call(
+            functools.partial(weight_grad_kernel, split_y),
+            grid_spec=pltpu.PrefetchScalarGridSpec(
+                num_scalar_prefetch=1,
+                grid=(self.tiles,),
+                in_specs=in_specs,
+                out_specs=out_specs,
+                scratch_shapes=scratch,
+            ),
+            out_shape=shapes,
+            compiler_params=kernel_params(),
+            cost_estimate=cost(4 * count * D * self.tiles * self.half, left, right),
+        )(at, *args)
 
 
 def combine_kernel(groups, at_ref, *refs):
@@ -616,12 +705,12 @@
     "begin": ((), ((0, 0),)),
     "prepared": (((0, 0),), ((0, 2), (0, 6), (0, 8))),
     "ready": (((0, 0),), ()),
-    (0, "projected"): (((0, 6), (0, 2), (0, 8)), ()),
-    (0, "context"): (((0, 6), (0, 2), (0, 8)), ((1, 0), (1, 6))),
-    (0, "feed"): (((0, 6), (1, 0), (1, 6)), ((1, 2), (1, 8))),
-    (0, "result"): (((1, 0), (1, 6), (1, 2), (1, 8)), ()),
-    (1, "projected"): (((1, 2), (1, 8)), ()),
-    (1, "context"): (((1, 6), (1, 8)), ()),
+    (0, "projected"): (((0, 6), (0, 2)), ()),
+    (0, "half"): (((0, 6), (0, 2), (0, 8)), ((1, 0),)),
+    (0, "context"): (((0, 6), (0, 8), (1, 0)), ((1, 6), (1, 2))),
+    (0, "placed"): (((1, 0), (1, 6), (1, 2)), ((1, 8),)),
+    (0, "result"): (((1, 6), (1, 2), (1, 8)), ()),
+    (1, "half"): (((1, 6), (1, 8)), ()),
 }
 
 
@@ -649,22 +738,24 @@
 
 def place_kernel(split_y, half, at_ref, *refs):
     pieces, out_ref = refs[:-1], refs[-1]
+    rows = out_ref.shape[2]
     for number, piece in enumerate(pieces):
         core = (at_ref[3] + number % CORES) % CORES
         x = (at_ref[1] + number // CORES % CHIPS_X) % CHIPS_X
         row = (at_ref[2] + number // (CORES * CHIPS_X)) % CHIPS_Y if split_y else 0
-        out_ref[x, row, :, pl.ds(pl.multiple_of(core * half, 128), half)] = piece[0]
-
-
-def place_pieces(pieces, split_y, place):
-    _, rows, half = pieces[0].shape
+        column = pl.multiple_of(core * half, 128)
+        out_ref[x, row, :, pl.ds(column, half)] = piece[0, 0:rows]
+
+
+def place_pieces(pieces, rows, split_y, place):
+    _, held, half = pieces[0].shape
     splits = CHIPS_Y if split_y else 1
     whole = pl.pallas_call(
         functools.partial(place_kernel, split_y, half),
         grid_spec=pltpu.PrefetchScalarGridSpec(
             num_scalar_prefetch=1,
             grid=(CHIPS_Z,),
-            in_specs=[pl.BlockSpec((1, rows, half), lambda k, at: (k, 0, 0))] * len(pieces),
+            in_specs=[pl.BlockSpec((1, held, half), lambda k, at: (k, 0, 0))] * len(pieces),
             out_specs=pl.BlockSpec(
                 (CHIPS_X, splits, rows, 2 * half),
                 lambda k, at: (lax.rem(at[0] + CHIPS_Z - k, CHIPS_Z), 0, 0, 0),
@@ -683,7 +774,7 @@
     return whole.reshape(CHIPS_Z * CHIPS_X * splits * rows, 2 * half)
 
 
-def gather_chain(block, split_y, place):
+def gather_chain(block, rows, split_y, place):
     parts = yield [hop(block, dz=k) for k in range(1, CHIPS_Z)]
     stack = jnp.stack([block, *parts])
     (across,) = yield [hop(stack, dx=1)]
@@ -691,9 +782,10 @@
     if split_y:
         pieces = pieces + (yield [hop(piece, dy=1) for piece in pieces])
     others = yield [hop(piece, dc=1) for piece in pieces]
-    return place_pieces(
-        [item for pair in zip(pieces, others) for item in pair], split_y, place
+    whole = place_pieces(
+        [item for pair in zip(pieces, others) for item in pair], rows, split_y, place
     )
+    return whole, jnp.stack([stack[:, rows:], across[:, rows:]], axis=1)
 
 
 class Flow:
@@ -724,17 +816,9 @@
         return self.done[name]
 
 
-def gather_vectors(vectors, place):
-    sizes = [vector.shape[1] for vector in vectors]
-    own = jnp.concatenate(vectors, axis=1)
-    layers, width = own.shape
+def spread_vectors(stack, sizes, place):
     count = CHIPS_Z * CHIPS_X
-    rounds = [
-        hop(own, dz=dz, dx=dx) if dz or dx else own
-        for dz in range(CHIPS_Z)
-        for dx in range(CHIPS_X)
-    ]
-    stack = jnp.stack(rounds).astype(jnp.float32)
+    stack = stack[:, :, :LAYERS].reshape(count, LAYERS, -1).astype(jnp.float32)
     wanted = jnp.arange(count, dtype=jnp.int32)
     behind = (place.z - wanted // CHIPS_X) % CHIPS_Z * CHIPS_X + (
         place.x - wanted % CHIPS_X
@@ -744,7 +828,7 @@
     out, at = [], 0
     for size in sizes:
         out.append(
-            stack[:, :, at : at + size].transpose(1, 0, 2).reshape(layers, count * size)
+            stack[:, :, at : at + size].transpose(1, 0, 2).reshape(LAYERS, count * size)
         )
         at += size
     return out
@@ -753,99 +837,76 @@
 def gather_block(weights, layer, number, place):
     shard = weights[number][layer]
     rows, columns = shard.shape
-    split_y = number == 6 or (number == 8 and layer > 0)
+    split_y = number == 6
     tall = rows // CHIPS_Y if split_y else rows
     start = (place.y * tall if split_y else 0, place.core * (columns // 2))
-    return lax.dynamic_slice(shard, start, (tall, columns // 2)), split_y
-
-
-def reduce_chain(left, right, place, y_first):
+    block = lax.dynamic_slice(shard, start, (tall, columns // 2))
+    if (layer, number) == (0, 0):
+        vectors = jnp.concatenate([weights[member] for member in VECTORS], axis=1)
+        block = jnp.concatenate([block, jnp.pad(vectors, ((0, 16 - LAYERS), (0, 0)))])
+    return block, tall, split_y
+
+
+def reduce_chain(grad, place, y_first):
     at = place.at
-    parts, _, columns = right.shape
-    half = columns // CORES
-    rows = left.shape[1] // (CHIPS_Z * CHIPS_X * CHIPS_Y)
-    grid = (parts, CHIPS_Z, CHIPS_X, CHIPS_Y, rows, half)
-    away = weight_grad(left, right, at, True)
-    sent = [hop(away.reshape(grid), dc=1)]
-    kept = weight_grad(left, right, at, False).reshape(grid)
-    (near,) = yield sent
+    parts, half = grad.parts, grad.half
+    away = grad.product(at, True)
+    (near,) = yield [hop(away, dc=1)]
+    send, keep = grad.product(at, False, y_first, near)
     flip = lambda value: 1 - value
     if y_first:
-        block = (parts, 1, CHIPS_X, 1, rows, half)
-        index = lambda i, at: (0, i, 0, flip(at[2]), 0, 0)
-        shape = (parts, CHIPS_Z, CHIPS_X, rows, half)
+        rows = grad.rows // CHIPS_Y
+        (over,) = yield [hop(send, dy=1)]
+        block = (parts, 1, 1, rows, half)
+        index = lambda i, at: (0, i, flip(at[1]), 0, 0)
         (send,) = combine(
             at,
             CHIPS_Z,
-            [[(kept, block, index), (near, block, index)]],
-            [(shape, (parts, 1, CHIPS_X, rows, half), lambda i, at: (0, i, 0, 0, 0))],
-        )
-        (over,) = yield [hop(send, dy=1)]
-        block = (parts, 1, 1, 1, rows, half)
-        index = lambda i, at: (0, i, flip(at[1]), at[2], 0, 0)
-        shape = (parts, CHIPS_Z, rows, half)
-        (send,) = combine(
-            at,
-            CHIPS_Z,
+            [[(keep, block, index), (over, block, index)]],
             [
-                [
-                    (kept, block, index),
-                    (near, block, index),
-                    (over, block[:-3] + (rows, half), lambda i, at: (0, i, flip(at[1]), 0, 0)),
-                ]
+                (
+                    (parts, CHIPS_Z, rows, half),
+                    (parts, 1, rows, half),
+                    lambda i, at: (0, i, 0, 0),
+                )
             ],
-            [(shape, (parts, 1, rows, half), lambda i, at: (0, i, 0, 0))],
         )
         (across,) = yield [hop(send, dx=1)]
 
         def terms(k):
             turn = lambda at: lax.rem(at[0] + k, CHIPS_Z)
-            index = lambda i, at: (0, turn(at), at[1], at[2], 0, 0)
+            index = lambda i, at: (0, turn(at), at[1], 0, 0)
             return [
-                (kept, block, index),
-                (near, block, index),
-                (over, block[:-3] + (rows, half), lambda i, at: (0, turn(at), at[1], 0, 0)),
+                (keep, block, index),
+                (over, block, index),
                 (across, (parts, 1, rows, half), lambda i, at: (0, turn(at), 0, 0)),
             ]
 
-        piece = (parts, rows, half)
     else:
-        block = (parts, 1, 1, CHIPS_Y, rows, half)
-        index = lambda i, at: (0, i, flip(at[1]), 0, 0, 0)
-        shape = (parts, CHIPS_Z, CHIPS_Y, rows, half)
-        (send,) = combine(
-            at,
-            CHIPS_Z,
-            [[(kept, block, index), (near, block, index)]],
-            [(shape, (parts, 1, CHIPS_Y, rows, half), lambda i, at: (0, i, 0, 0, 0))],
-        )
+        rows = grad.rows
         (across,) = yield [hop(send, dx=1)]
+        block = (parts, 1, rows, half)
 
         def terms(k):
-            turn = lambda at: lax.rem(at[0] + k, CHIPS_Z)
-            index = lambda i, at: (0, turn(at), at[1], 0, 0, 0)
-            return [
-                (kept, block, index),
-                (near, block, index),
-                (across, (parts, 1, CHIPS_Y, rows, half), lambda i, at: (0, turn(at), 0, 0, 0)),
-            ]
-
-        piece = (parts, CHIPS_Y, rows, half)
-    zeros = lambda i, at: (0,) * len(piece)
+            index = lambda i, at: (0, lax.rem(at[0] + k, CHIPS_Z), 0, 0)
+            return [(keep, block, index), (across, block, index)]
+
+    piece = (parts, rows, half)
+    zeros = lambda i, at: (0, 0, 0)
     whole = (piece, piece, zeros)
     own, *sends = combine(at, 1, [terms(k) for k in range(CHIPS_Z)], [whole] * CHIPS_Z)
     landed = yield [hop(send, dz=k) for k, send in zip(range(1, CHIPS_Z), sends)]
     (own,) = combine(at, 1, [[(term, piece, zeros) for term in (own, *landed)]], [whole])
+    if y_first:
+        others = yield [hop(own, dy=1), hop(own, dc=1), hop(own, dy=1, dc=1)]
+        return [own, *others]
     (other,) = yield [hop(own, dy=1)]
-    if y_first:
-        pieces = [own, other]
-    else:
-        pieces = combine(at, 1, [[(own, piece, zeros), (other, piece, zeros)]], [whole])
-    others = yield [hop(item, dc=1) for item in pieces]
-    return [*pieces, *others]
-
-
-def join_kernel(at_ref, *refs):
+    (own,) = combine(at, 1, [[(own, piece, zeros), (other, piece, zeros)]], [whole])
+    (other,) = yield [hop(own, dc=1)]
+    return [own, other]
+
+
+def join_kernel(parts_outer, at_ref, *refs):
     out_ref = refs[-1]
     half = refs[0].shape[-1]
     per_layer = (len(refs) - 1) // LAYERS
@@ -857,25 +918,21 @@
             row = lax.rem(at_ref[2] + place % CHIPS_Y, CHIPS_Y) * ref.shape[1]
             row = pl.multiple_of(row, 16)
         for part in range(ref.shape[0]):
-            column = pl.multiple_of((part * CORES + core) * half, 128)
+            column = part * CORES + core if parts_outer else core * ref.shape[0] + part
+            column = pl.multiple_of(column * half, 128)
             out_ref[layer, pl.ds(row, ref.shape[1]), pl.ds(column, half)] = ref[part].astype(
                 jnp.float32
             )
 
 
-def join(at, layers):
-    pieces = []
-    for layer in layers:
-        for piece in layer:
-            if piece.ndim == 4:
-                piece = piece.reshape(piece.shape[0], -1, piece.shape[-1])
-            pieces.append(piece)
+def join(at, layers, parts_outer):
+    pieces = [piece for layer in layers for piece in layer]
     parts, rows, half = pieces[0].shape
     tall = rows * (len(pieces) // LAYERS // CORES)
     zeros = lambda i, at: (0, 0, 0)
     shape = (LAYERS, tall, parts * CORES * half)
     return pl.pallas_call(
-        join_kernel,
+        functools.partial(join_kernel, parts_outer),
         grid_spec=pltpu.PrefetchScalarGridSpec(
             num_scalar_prefetch=1,
             grid=(1,),
@@ -894,6 +951,15 @@
         total = total + other
     up, down = yield [hop(total, dz=1), hop(total, dz=3)]
     return total + jnp.where(place.z % 2 == 0, down, up)
+
+
+def qv_sum(halves):
+    own, away, at = halves
+    own, away = jnp.sum(own, axis=0), jnp.sum(away, axis=0)
+    order = jnp.where(
+        at[3] == 0, jnp.concatenate([own, away], axis=0), jnp.concatenate([away, own], axis=0)
+    )
+    return jnp.concatenate([order[:, part].reshape(D) for part in (0, 2)])
 
 
 def path_vectors(qv_bias):
@@ -913,41 +979,35 @@
     flow = Flow()
     if fast:
         place = Place()
-        vectors = gather_vectors([weights[number] for number in VECTORS], place)
-
-        def begin(layer, number):
-            flow.start(
-                (layer, number), gather_chain(*gather_block(weights, layer, number, place), place)
-            )
+        at = place.at
+        sizes = [weights[number].shape[1] for number in VECTORS]
+        spread_out = []
 
         def get(layer, number):
-            if number in VECTORS:
-                return vectors[VECTORS.index(number)][layer]
-            return flow.finish((layer, number))
+            if number not in VECTORS:
+                return flow.finish((layer, number))[0]
+            if not spread_out:
+                spread_out.extend(spread_vectors(flow.finish((0, 0))[1], sizes, place))
+            return spread_out[VECTORS.index(number)][layer]
 
         def step(point, main):
             advanced, started = FORWARD.get(point, ((), ()))
             main = flow.tick(main, *advanced)
             for name in started:
-                begin(*name)
+                flow.start(name, gather_chain(*gather_block(weights, *name, place), place))
             return main
 
-        def reduce(layer, number, left, right):
-            flow.start(
-                ("grad", layer, number), reduce_chain(left, right, place, number in (0, 6))
-            )
-
-        def back_step(main, *only):
-            return flow.tick(
-                main,
-                *[
-                    name
-                    for name in flow.running
-                    if name[0] == "grad" and (not only or name[1:] in only)
-                ],
-            )
+        def reduce(layer, number, grad):
+            flow.start(("grad", layer, number), reduce_chain(grad, place, number in (0, 6)))
+
+        def back_step(main, *held):
+            return flow.tick(main, *[name for name in flow.running if name not in held])
+
+        def add_up(name, total):
+            flow.start(name, reduce_total(total, place))
 
     else:
+        at = jnp.zeros((4,), jnp.int32)
 
         def get(layer, number):
             whole = lax.all_gather(weights[number][layer], "shard", axis=0, tiled=True)
@@ -956,14 +1016,21 @@
         def step(point, main):
             return main
 
-        def reduce(layer, number, left, right):
-            grads = jnp.concatenate([contract_first(left, part) for part in right], axis=1)
-            grads = lax.psum_scatter(grads, "shard", scatter_dimension=0, tiled=True)
-            grads = lax.psum(grads.astype(jnp.bfloat16), "rep").astype(jnp.float32)
-            flow.done[("grad", layer, number)] = grads
-
-        def back_step(main, *only):
+        def reduce(layer, number, grad):
+            own, away = grad.rights
+            if not grad.cut:
+                own = jnp.concatenate([own, away], axis=2)
+                own = own.transpose(1, 0, 2).reshape(own.shape[1], -1)
+            total = contract_first(grad.left, own)
+            total = lax.psum_scatter(total, "shard", scatter_dimension=0, tiled=True)
+            total = lax.psum(total.astype(jnp.bfloat16), "rep").astype(jnp.float32)
+            flow.done[("grad", layer, number)] = total
+
+        def back_step(main, *held):
             return main
+
+        def add_up(name, total):
+            flow.done[name] = lax.psum(total, AXES)
 
     step("begin", ())
     slots, bias = step("prepared", prepare(segment, parent, clusters))
@@ -973,14 +1040,16 @@
         pull = functools.partial(get, layer)
         projected = project(hidden_low, pull(0), path_vectors(pull(1)))
         projected = step((layer, "projected"), projected)
-        context, *heads = attend(projected, slots, bias)
+        first = attend(projected, slots, bias, 0, ())
+        first = step((layer, "half"), first)
+        context, *heads = attend(projected, slots, bias, 1, first)
         context = step((layer, "context"), context)
-        context = step((layer, "feed"), context)
+        context, *wide = step((layer, "placed"), (context, pull(2), pull(6), pull(8)))
         entered = hidden_low
         middle, act, slope, *norms, hidden, hidden_low = feed(
             context,
             hidden,
-            [pull(2), pull(6), pull(8)],
+            wide,
             [pull(number) for number in (3, 4, 5, 7, 9, 10, 11)],
         )
         hidden_low = step((layer, "result"), hidden_low)
@@ -995,40 +1064,39 @@
             above,
             proj,
             None if proj is None else get(layer + 1, 0),
+            at,
             [norms[2], norms[3], slope, norms[0], norms[1]],
             [pull(2), pull(6), pull(8)],
             [pull(4), pull(10)],
         )
+        sums[layer] = [row_sums, ffin_sum, None]
         down = back_step(down)
-        reduce(layer, 8, act, down[None])
-        reduce(layer, 6, middle, grad_pre[None])
-        reduce(layer, 2, context, attn_low[None])
+        wide = grad_pre.shape[1] // CORES
+        reduce(layer, 8, Grad(act, down, down, True, act.shape[1] // D, D // CORES))
+        reduce(layer, 6, Grad(middle, grad_pre, grad_pre, True, wide // D, D))
+        reduce(layer, 2, Grad(context, attn_low, attn_low, True, 1, D // CORES))
+        if layer == 0:
+            pieces = [qv_sum(sums[1][2])]
+            for row_sums, ffin_sum, _ in sums:
+                pieces += [row_sums[:6].reshape(-1), ffin_sum[0]]
+            add_up("early", jnp.concatenate(pieces))
         grad_context = back_step(grad_context)
-        proj, proj_sums = attend_back(grad_context, slots, heads)
-        proj = back_step(proj)
-        reduce(layer, 0, entered, proj)
-        proj = back_step(proj, (layer, 0))
+        away, away_sums = attend_back(grad_context, slots, heads, at, True)
+        grad_context, away = back_step((grad_context, away))
+        own, own_sums = attend_back(grad_context, slots, heads, at, False)
+        proj = (own, away)
+        reduce(layer, 0, Grad(entered, own, away, False, 3, D // CORES))
+        sums[layer][2] = (own_sums, away_sums, at)
+        proj = back_step(proj, ("grad", layer, 8))
         above = grad_attn
-        sums[layer] = (row_sums, ffin_sum, jnp.sum(proj_sums, axis=0))
-    grad_input = input_grad(above, proj, get(0, 0))
-
-    def qv_sum(layer):
-        return jnp.concatenate([sums[layer][2][:, part].reshape(D) for part in (0, 2)])
-
-    early = jnp.concatenate(
-        [qv_sum(1)]
-        + [piece for layer in range(LAYERS) for piece in (sums[layer][0][:6].reshape(-1), sums[layer][1][0])]
-    )
-    totals = {"early": early, "late": qv_sum(0)}
+    add_up("late", qv_sum(sums[0][2]))
+    grad_input = input_grad(above, proj, get(0, 0), at)
+    grad_input = back_step(grad_input)
+    while flow.running:
+        grad_input = back_step(grad_input)
+    early, late = flow.finish("early"), flow.finish("late")
     count = lax.axis_size("shard")
     shard = lax.axis_index("shard")
-    for name, total in totals.items():
-        if fast:
-            flow.start(name, reduce_total(total, place))
-            totals[name] = flow.finish(name)
-        else:
-            totals[name] = lax.psum(total, AXES)
-    early, late = totals["early"], totals["late"]
     ff = sums[0][1].shape[1]
     rest = early[2 * D :].reshape(LAYERS, 6 * D + ff)
 
@@ -1041,7 +1109,7 @@
         grads[number] = share(rest[:, row * D : (row + 1) * D])
     for number in (8, 6, 2, 0):
         done = [flow.finish(("grad", layer, number)) for layer in range(LAYERS)]
-        grads[number] = join(place.at, done) if fast else jnp.stack(done)
+        grads[number] = join(at, done, number == 0) if fast else jnp.stack(done)
     return (result, grad_input, *[grads[number] for number in range(12)])
 
 

time: 879 us -> 841 us (0.957)
  Pallas kernels: 554 us -> 528 us
  starting transfers between devices: 176 us -> 152 us
  waiting for transfers between devices: 78 us -> 93.2 us
  local copies, waits for them, and re-layouts: 46.3 us -> 36.7 us
    pallas_call x32 -> x24, Pallas kernels: 107 us -> 69.5 us  [combine(): pl.pallas_call(functools.partial(combine_kernel, [len(group) for group in...]
    ppermute x143 -> x132, starting transfers between devices: 176 us -> 152 us  [hop(): return lax.ppermute(value, AXES, pairs)]
    ppermute x143 -> x132, waiting for transfers between devices: 78 us -> 93.2 us  [hop(): return lax.ppermute(value, AXES, pairs)]
    pallas_call x24 -> x28, Pallas kernels: 255 us -> 262 us  [the longest x16 104 us: product(): pl.pallas_call(functools.partial(weight_grad_kernel, split_y), grid_spec=...]
  transfers between devices with their start and end apart: 143 -> 132, of which waited for: 21 -> 21; matrix products, arithmetic and copies ran while one was open for 5% -> 5% of each run, Pallas kernels for 54% -> 53%
where the time goes in v4:
time: 841 us; the launch traced here: 824 us
  Pallas kernels  528 us (63%)
  starting transfers between devices  152 us (18%)
  waiting for transfers between devices  93.2 us (11%)
  local copies, waits for them, and re-layouts  36.7 us (4%)
  other arithmetic  11.9 us (1%)
    ppermute x132, starting transfers between devices, hop(): return lax.ppermute(value, AXES, pairs)  152 us
    pallas_call x16, Pallas kernels, product(): pl.pallas_call(functools.partial(weight_grad_kernel, split_y), grid_spec=...  104 us
    ppermute x132, waiting for transfers between devices, hop(): return lax.ppermute(value, AXES, pairs)  93.2 us
    pallas_call x4, Pallas kernels, attend_back(): pl.pallas_call(attend_back_kernel, grid_spec=pltpu.PrefetchScalarGridSpec...  74.8 us
    pallas_call x4, Pallas kernels, attend(): pl.pallas_call(attend_kernel, grid=(trees, PAIRS // 2), in_specs=[slot_sp...  70.8 us
    pallas_call x24, Pallas kernels, combine(): pl.pallas_call(functools.partial(combine_kernel, [len(group) for group in...  69.5 us
    pallas_call x2, Pallas kernels, feed(): pl.pallas_call(feed_kernel, grid=(count // ROW_TILE,), in_specs=[row_spec...  56.2 us
    pallas_call x2, Pallas kernels, feed_back(): pl.pallas_call(functools.partial(feed_back_kernel, proj is not None), gri...  53.3 us
  transfers between devices with their start and end apart: 132, of which 21 were waited for; matrix products, arithmetic and copies ran while one was open for 5% of the time, Pallas kernels for 53%

profile of v4, /device:TPU:17, one launch (start us, length us, event | category | flops | bytes accessed | tf_op | source)
XLA Modules:
  0.0 824.3 jit_solution(597236157276002865)
XLA Ops:
  12.5 19.1 %shard_map.272 = (s32[1,6,2,1024]{3,2,1,0:T(2,128)}, bf16[1,12,1024,128]{3,2,1,0:T(8,128)(2,1)}) custom-call(s32[1,13]{1,0:T(1,128)} %parent_ref.1, s32[1,1,1024]{2,1,0:T(1,128)} %bitcast.139, s32[1,6,2,1024]{3,2,1,0:T(2,128)} %transpose_reshape.3.cluster_ref), custom_call_target="tpu_custom_call" | custom-call | flops 20000000000 | bytes 4000000 | tf_op jit(solution)/shard_map/pallas_call | solution.py:573
  40.0 17.1 %collective-permute-done.3.refs_2_ = bf16[4,112,1152]{2,1,0:T(8,128)(2,1)} collective-permute-done((bf16[4,112,1152]{2,1,0:T(8,128)(2,1)S(1)}, bf16[4,112,1152]{2,1,0:T(8,128)(2,1)}, u32[]{:S(2)}, u32[]{:S(2)}) %collective-permute-start.3) | collective-permute-done | bytes 1032224 | tf_op jit(solution)/shard_map/ppermute | solution.py:736
  57.1 3.3 collective-permute-start.5
  69.6 5.4 shard_map.273
  76.4 7.9 shard_map.274.query_ref.key_ref.value_ref
  93.0 17.7 %shard_map.275 = (bf16[1024,768]{1,0:T(8,128)(2,1)}, bf16[1,12,1024,128]{3,2,1,0:T(8,128)(2,1)}, bf16[1,12,1024,128]{3,2,1,0:T(8,128)(2,1)}, bf16[1,12,1024,128]{3,2,1,0:T(8,128)(2,1)}) custom-call(s32[1,6,2,1024]{3,2,1,0:T(2,128)} %get-tuple-element.272.slot_ref, bf16[1024,2304]{1,0:T(8,128)(2,1)} %shard_map.274.query_ref.key_ref.value_ref, ...), custom_call_target="tpu_custom_call" | custom-call | flops 15000000512 | bytes 10000000 | tf_op jit(solution)/shard_map/pallas_call | solution.py:157
  119.8 3.6 collective-permute-done.35
  125.1 9.5 %collective-permute-done.21 = bf16[96,1152]{1,0:T(8,128)(2,1)S(1)} collective-permute-done((bf16[96,1152]{1,0:T(8,128)(2,1)S(1)}, bf16[96,1152]{1,0:T(8,128)(2,1)S(1)}, u32[]{:S(2)}, u32[]{:S(2)}) %collective-permute-start.21) | collective-permute-done | bytes 221216 | tf_op jit(solution)/shard_map/ppermute | solution.py:736
  141.6 3.6 collective-permute-start.29
  146.1 17.8 %shard_map.276 = (bf16[1024,768]{1,0:T(8,128)(2,1)}, bf16[1,12,1024,128]{3,2,1,0:T(8,128)(2,1)}, bf16[1,12,1024,128]{3,2,1,0:T(8,128)(2,1)}, bf16[1,12,1024,128]{3,2,1,0:T(8,128)(2,1)}) custom-call(s32[1,6,2,1024]{3,2,1,0:T(2,128)} %get-tuple-element.272.slot_ref, ...), custom_call_target="tpu_custom_call", output_to_operand_aliasing={{0}: (5, {}), {1}: (6, {}), {2}: (7, {}), {3}: (8, {})} | custom-call | flops 15000000512 | bytes 10000000 | tf_op jit(solution)/shard_map/pallas_call | solution.py:157
  168.2 3.4 collective-permute-start.32
  183.8 4.2 shard_map.277
  188.0 5.8 shard_map.278
  193.8 5.8 shard_map.279
  208.9 12.1 %collective-permute-done.41 = bf16[384,384]{1,0:T(8,128)(2,1)S(1)} collective-permute-done((bf16[384,384]{1,0:T(8,128)(2,1)S(1)}, bf16[384,384]{1,0:T(8,128)(2,1)S(1)}, u32[]{:S(2)}, u32[]{:S(2)}) %collective-permute-start.41) | collective-permute-done | bytes 294944 | tf_op jit(solution)/shard_map/ppermute | solution.py:736
  221.0 4.2 collective-permute-start.44
  225.3 28.3 %shard_map.280 = (bf16[1024,768]{1,0:T(8,128)(2,1)}, bf16[1024,3072]{1,0:T(8,128)(2,1)}, bf16[1024,3072]{1,0:T(8,128)(2,1)}, f32[1024,768]{1,0:T(8,128)}, f32[10...) custom-call(bf16[1024,768]{1,0:T(8,128)(2,1)} %get-tuple-element.307, ...), custom_call_target="tpu_custom_call" | custom-call | flops 27179089920 | bytes 12189696 | tf_op jit(solution)/shard_map/pallas_call | solution.py:473
  257.4 5.1 shard_map.281
  262.6 7.9 shard_map.282.query_ref.key_ref.value_ref
  271.4 17.7 %shard_map.283 = (bf16[1024,768]{1,0:T(8,128)(2,1)}, bf16[1,12,1024,128]{3,2,1,0:T(8,128)(2,1)}, bf16[1,12,1024,128]{3,2,1,0:T(8,128)(2,1)}, bf16[1,12,1024,128]{3,2,1,0:T(8,128)(2,1)}) custom-call(s32[1,6,2,1024]{3,2,1,0:T(2,128)} %get-tuple-element.272.slot_ref, bf16[1024,2304]{1,0:T(8,128)(2,1)} %shard_map.282.query_ref.key_ref.value_ref, ...), custom_call_target="tpu_custom_call" | custom-call | flops 15000000512 | bytes 10000000 | tf_op jit(solution)/shard_map/pallas_call | solution.py:157
  289.8 4.3 shard_map.285
  295.4 17.7 %shard_map.284 = (bf16[1024,768]{1,0:T(8,128)(2,1)}, bf16[1,12,1024,128]{3,2,1,0:T(8,128)(2,1)}, bf16[1,12,1024,128]{3,2,1,0:T(8,128)(2,1)}, bf16[1,12,1024,128]{3,2,1,0:T(8,128)(2,1)}) custom-call(s32[1,6,2,1024]{3,2,1,0:T(2,128)} %get-tuple-element.272.slot_ref, ...), custom_call_target="tpu_custom_call", output_to_operand_aliasing={{0}: (5, {}), {1}: (6, {}), {2}: (7, {}), {3}: (8, {})} | custom-call | flops 15000000512 | bytes 10000000 | tf_op jit(solution)/shard_map/pallas_call | solution.py:157
  314.7 5.8 shard_map.286
  320.5 5.7 shard_map.287
  326.2 27.9 %shard_map.288 = (bf16[1024,768]{1,0:T(8,128)(2,1)}, bf16[1024,3072]{1,0:T(8,128)(2,1)}, bf16[1024,3072]{1,0:T(8,128)(2,1)}, f32[1024,768]{1,0:T(8,128)}, f32[10...) custom-call(bf16[1024,768]{1,0:T(8,128)(2,1)} %get-tuple-element.338, ...), custom_call_target="tpu_custom_call" | custom-call | flops 27179089920 | bytes 12189696 | tf_op jit(solution)/shard_map/pallas_call | solution.py:473
  354.1 21.9 %shard_map.289 = (bf16[1024,768]{1,0:T(8,128)(2,1)}, bf16[1024,3072]{1,0:T(8,128)(2,1)}, f32[1024,768]{1,0:T(8,128)}, bf16[1024,768]{1,0:T(8,128)(2,1)}, bf16[10...) custom-call(bf16[1024,768]{1,0:T(8,128)(2,1)} %refs_0_.1, f32[1024,768]{1,0:T(8,128)} %get-tuple-element.344.refs_1_, ...), custom_call_target="tpu_custom_call" | custom-call | flops 27179089920 | bytes 12189696 | tf_op jit(solution)/shard_map/pallas_call | solution.py:520
  376.0 6.5 shard_map.291
  382.5 7.9 shard_map.290
  390.9 4.1 shard_map.292
  398.0 4.3 shard_map.296
  403.5 7.0 shard_map.295
  411.7 8.4 %shard_map.294 = (bf16[1,4,384,384]{3,2,1,0:T(8,128)(2,1)}, bf16[1,4,384,384]{3,2,1,0:T(8,128)(2,1)}) custom-call(s32[4]{0:T(128)} %pad_add_fusion.at_ref.refs_1_, bf16[1024,3072]{1,0:T(8,128)(2,1)} %get-tuple-element.351.left_ref, bf16[1024,768]{1,0:T(8,128)(2,1)} %get-tuple-element.352.right_ref, bf16[1,4,2,384,384]{4,3,2,1,0:T(8,128)(2,1)} %copy-done.123), custom_call_target="tpu_custom_call" | custom-call | flops 4831838208 | bytes 7864320 | tf_op jit(solution)/shard_map/pallas_call | solution.py:658
  420.3 19.0 %shard_map.293 = (bf16[3,1024,384]{2,1,0:T(8,128)(2,1)}, f32[1,3,8,128]{3,2,1,0:T(8,128)}) custom-call(s32[4]{0:T(128)} %pad_add_fusion.at_ref.refs_1_, s32[1,6,2,1024]{3,2,1,0:T(2,128)} %get-tuple-element.272.slot_ref, bf16[1024,768]{1,0:T(8,128)(2,1)} %get-tuple-element.367.grad_ref, bf16[1,12,1024,128]{3,2,1,0:T(8,128)(2,1)} %get-tuple-element.357.qk_ref, ...), custom_call_target="tpu_custom_call" | custom-call | flops 16999999488 | bytes 10000000 | tf_op jit(solution)/shard_map/pallas_call | solution.py:194
  439.4 7.7 collective-permute-done.59.refs_1_.refs_3_.refs_5_.refs_7_
  447.1 6.5 shard_map.300
  457.8 4.0 collective-permute-start.63
  463.1 4.1 shard_map.298
  468.4 18.6 %shard_map.297 = (bf16[3,1024,384]{2,1,0:T(8,128)(2,1)}, f32[1,3,8,128]{3,2,1,0:T(8,128)}) custom-call(s32[4]{0:T(128)} %pad_add_fusion.at_ref.refs_1_, s32[1,6,2,1024]{3,2,1,0:T(2,128)} %get-tuple-element.272.slot_ref, bf16[1024,768]{1,0:T(8,128)(2,1)} %get-tuple-element.367.grad_ref, bf16[1,12,1024,128]{3,2,1,0:T(8,128)(2,1)} %get-tuple-element.357.qk_ref, ...), custom_call_target="tpu_custom_call" | custom-call | flops 16999999488 | bytes 10000000 | tf_op jit(solution)/shard_map/pallas_call | solution.py:194
  487.0 3.3 shard_map.302
  494.1 7.0 shard_map.305
  504.9 31.4 %shard_map.301 = (bf16[1024,768]{1,0:T(8,128)(2,1)}, bf16[1024,3072]{1,0:T(8,128)(2,1)}, f32[1024,768]{1,0:T(8,128)}, bf16[1024,768]{1,0:T(8,128)(2,1)}, bf16[10...) custom-call(f32[1024,768]{1,0:T(8,128)} %get-tuple-element.349.refs_0_, s32[4]{0:T(128)} %pad_add_fusion.at_ref.refs_1_, ...), custom_call_target="tpu_custom_call" | custom-call | flops 27179089920 | bytes 13762560 | tf_op jit(solution)/shard_map/pallas_call | solution.py:520
  543.3 6.5 shard_map.311
  553.4 8.0 shard_map.310
  563.1 4.2 shard_map.312
  570.7 4.1 shard_map.309
  583.4 9.5 %collective-permute-done.78.refs_7_ = bf16[2,48,768]{2,1,0:T(8,128)(2,1)S(1)} collective-permute-done((bf16[2,48,768]{2,1,0:T(8,128)(2,1)S(1)}, bf16[2,48,768]{2,1,0:T(8,128)(2,1)S(1)}, u32[]{:S(2)}, u32[]{:S(2)}) %collective-permute-start.78) | collective-permute-done | bytes 147488 | tf_op jit(solution)/shard_map/ppermute | solution.py:736
  594.3 4.3 shard_map.318
  599.9 7.0 shard_map.317
  613.3 8.4 %shard_map.316 = (bf16[1,4,384,384]{3,2,1,0:T(8,128)(2,1)}, bf16[1,4,384,384]{3,2,1,0:T(8,128)(2,1)}) custom-call(s32[4]{0:T(128)} %pad_add_fusion.at_ref.refs_1_, bf16[1024,3072]{1,0:T(8,128)(2,1)} %get-tuple-element.413.left_ref, bf16[1024,768]{1,0:T(8,128)(2,1)} %get-tuple-element.414.right_ref, bf16[1,4,2,384,384]{4,3,2,1,0:T(8,128)(2,1)} %collective-permute-done.81.refs_0_), custom_call_target="tpu_custom_call" | custom-call | flops 4831838208 | bytes 7864320 | tf_op jit(solution)/shard_map/pallas_call | solution.py:658
  626.4 18.6 %shard_map.313 = (bf16[3,1024,384]{2,1,0:T(8,128)(2,1)}, f32[1,3,8,128]{3,2,1,0:T(8,128)}) custom-call(s32[4]{0:T(128)} %pad_add_fusion.at_ref.refs_1_, s32[1,6,2,1024]{3,2,1,0:T(2,128)} %get-tuple-element.272.slot_ref, bf16[1024,768]{1,0:T(8,128)(2,1)} %get-tuple-element.441.grad_ref, bf16[1,12,1024,128]{3,2,1,0:T(8,128)(2,1)} %get-tuple-element.425.qk_ref, ...), custom_call_target="tpu_custom_call" | custom-call | flops 16999999488 | bytes 10000000 | tf_op jit(solution)/shard_map/pallas_call | solution.py:194
  645.2 5.6 collective-permute-done.89.refs_1_.refs_3_.refs_5_.refs_7_
  650.7 6.5 shard_map.323
  665.9 4.1 shard_map.321
  676.5 18.6 %shard_map.319 = (bf16[3,1024,384]{2,1,0:T(8,128)(2,1)}, f32[1,3,8,128]{3,2,1,0:T(8,128)}) custom-call(s32[4]{0:T(128)} %pad_add_fusion.at_ref.refs_1_, s32[1,6,2,1024]{3,2,1,0:T(2,128)} %get-tuple-element.272.slot_ref, bf16[1024,768]{1,0:T(8,128)(2,1)} %get-tuple-element.441.grad_ref, bf16[1,12,1024,128]{3,2,1,0:T(8,128)(2,1)} %get-tuple-element.425.qk_ref, ...), custom_call_target="tpu_custom_call" | custom-call | flops 16999999488 | bytes 10000000 | tf_op jit(solution)/shard_map/pallas_call | solution.py:194
  695.3 6.9 shard_map.328
  703.5 3.5 shard_map.325
  720.2 7.0 collective-permute-done.103.refs_2_
  727.2 9.2 %collective-permute-start.105 = (bf16[2,48,768]{2,1,0:T(8,128)(2,1)}, bf16[2,48,768]{2,1,0:T(8,128)(2,1)S(1)}, u32[]{:S(2)}, u32[]{:S(2)}) collective-permute-start(bf16[2,48,768]{2,1,0:T(8,128)(2,1)} %get-tuple-element.464), channel_id=1, source_target_pairs={{0,2},{1,3},{2,4},{3,5},{4,6},{5,7},{6,0},{7,1},{8,10},{9,11},{10,... | collective-permute-start | bytes 442376 | tf_op jit(solution)/shard_map/ppermute | solution.py:736
  737.6 9.6 %shard_map.324 = f32[1024,768]{1,0:T(8,128)} custom-call(f32[1024,768]{1,0:T(8,128)} %get-tuple-element.384.above_ref, s32[4]{0:T(128)} %pad_add_fusion.at_ref.refs_1_, bf16[3,1024,384]{2,1,0:T(8,128)(2,1)} %get-tuple-element.456.own_ref.right_ref, bf16[3,1024,384]{2,1,0:T(8,128)(2,1)} %get-tuple-element.457.right_ref.away_ref, bf16[768,2304]{1,0:T(8,128)(2,1)} %bitcast.103), custom_call_target="tpu_custom_call" | custom-call | flops 4348654592 | bytes 6684672 | tf_op jit(solution)/shard_map/pallas_call | solution.py:552
  750.7 4.0 shard_map.332
  775.4 6.1 collective-permute-done.115.refs_3_
  812.8 3.6 shard_map.338
  816.4 3.5 shard_map.339
  819.9 3.2 shard_map.336
  (628 shorter events, 236.9 us)
Async XLA Ops:
  2.4 31.2 %collective-permute-start = (bf16[112,1152]{1,0:T(8,128)(2,1)S(1)}, bf16[112,1152]{1,0:T(8,128)(2,1)}, u32[]{:S(2)}, u32[]{:S(2)}) collective-permute-start(bf16[112,1152]{1,0:T(8,128)(2,1)S(1)} %get-tuple-element.555), channel_id=1, source_target_pairs={{0,2},{1,3},{2,4},{3,5},{4,6},{5,7},{6,0},{7,1},{8,10},{9,11},{10,... | collective-permute-start | bytes 774152 | tf_op jit(solution)/shard_map/ppermute | solution.py:736
  3.7 29.9 %collective-permute-start.1 = (bf16[112,1152]{1,0:T(8,128)(2,1)S(1)}, bf16[112,1152]{1,0:T(8,128)(2,1)}, u32[]{:S(2)}, u32[]{:S(2)}) collective-permute-start(bf16[112,1152]{1,0:T(8,128)(2,1)S(1)} %get-tuple-element.555), channel_id=1, source_target_pairs={{0,4},{1,5},{2,6},{3,7},{4,0},{5,1},{6,2},{7,3},{8,12},{9,13},{10,... | collective-permute-start | bytes 774152 | tf_op jit(solution)/shard_map/ppermute | solution.py:736
  3.8 29.9 %collective-permute-start.2 = (bf16[112,1152]{1,0:T(8,128)(2,1)S(1)}, bf16[112,1152]{1,0:T(8,128)(2,1)}, u32[]{:S(2)}, u32[]{:S(2)}) collective-permute-start(bf16[112,1152]{1,0:T(8,128)(2,1)S(1)} %get-tuple-element.555), channel_id=1, source_target_pairs={{0,6},{1,7},{2,0},{3,1},{4,2},{5,3},{6,4},{7,5},{8,14},{9,15},{10,... | collective-permute-start | bytes 774152 | tf_op jit(solution)/shard_map/ppermute | solution.py:736
  6.6 80.4 %collective-permute-start.6 = (bf16[48,1536]{1,0:T(8,128)(2,1)}, bf16[48,1536]{1,0:T(8,128)(2,1)}, u32[]{:S(2)}, u32[]{:S(2)}) collective-permute-start(bf16[48,1536]{1,0:T(8,128)(2,1)} %fusion.27), channel_id=1, source_target_pairs={{0,2},{1,3},{2,4},{3,5},{4,6},{5,7},{6,0},{7,1},{8,10},{9,11},{10,... | collective-permute-start | bytes 442376 | tf_op jit(solution)/shard_map/ppermute | solution.py:736
  6.9 82.4 %collective-permute-start.7 = (bf16[48,1536]{1,0:T(8,128)(2,1)}, bf16[48,1536]{1,0:T(8,128)(2,1)}, u32[]{:S(2)}, u32[]{:S(2)}) collective-permute-start(bf16[48,1536]{1,0:T(8,128)(2,1)} %fusion.27), channel_id=1, source_target_pairs={{0,4},{1,5},{2,6},{3,7},{4,0},{5,1},{6,2},{7,3},{8,12},{9,13},{10,... | collective-permute-start | bytes 442376 | tf_op jit(solution)/shard_map/ppermute | solution.py:736
  33.6 41.4 %collective-permute-start.10 = (bf16[96,384]{1,0:T(8,128)(2,1)}, bf16[96,384]{1,0:T(8,128)(2,1)}, u32[]{:S(2)}, u32[]{:S(2)}) collective-permute-start(bf16[96,384]{1,0:T(8,128)(2,1)} %fusion.26), channel_id=1, source_target_pairs={{0,4},{1,5},{2,6},{3,7},{4,0},{5,1},{6,2},{7,3},{8,12},{9,13},{10,... | collective-permute-start | bytes 221192 | tf_op jit(solution)/shard_map/ppermute | solution.py:736
  35.0 22.1 %collective-permute-start.3 = (bf16[4,112,1152]{2,1,0:T(8,128)(2,1)S(1)}, bf16[4,112,1152]{2,1,0:T(8,128)(2,1)}, u32[]{:S(2)}, u32[]{:S(2)}) collective-permute-start(bf16[4,112,1152]{2,1,0:T(8,128)(2,1)S(1)} %pad_maximum_fusion.2.refs_0_), channel_id=1, source_target_pairs={{0,1},{1,0},{2,3},{3,2},{4,5},{5,4},{6,7},{7,6},{8,9},{9,8},{10,11... | collective-permute-start | bytes 3096584 | tf_op jit(solution)/shard_map/ppermute | solution.py:736
  37.3 29.7 %collective-permute-start.4 = (bf16[4,112,1152]{2,1,0:T(8,128)(2,1)S(1)}, bf16[4,112,1152]{2,1,0:T(8,128)(2,1)S(1)}, u32[]{:S(2)}, u32[]{:S(2)}) collective-permute-start(bf16[4,112,1152]{2,1,0:T(8,128)(2,1)S(1)} %pad_maximum_fusion.2.refs_0_), channel_id=1, source_target_pairs={{0,8},{1,9},{2,10},{3,11},{4,12},{5,13},{6,14},{7,15},{8,0},{9,1},... | collective-permute-start | bytes 3096584 | tf_op jit(solution)/shard_map/ppermute | solution.py:736
  67.0 22.3 %collective-permute-start.8 = (bf16[48,1536]{1,0:T(8,128)(2,1)}, bf16[48,1536]{1,0:T(8,128)(2,1)S(1)}, u32[]{:S(2)}, u32[]{:S(2)}) collective-permute-start(bf16[48,1536]{1,0:T(8,128)(2,1)} %fusion.27), channel_id=1, source_target_pairs={{0,6},{1,7},{2,0},{3,1},{4,2},{5,3},{6,4},{7,5},{8,14},{9,15},{10,... | collective-permute-start | bytes 442376 | tf_op jit(solution)/shard_map/ppermute | solution.py:736
  84.3 26.4 %collective-permute-start.14 = (bf16[384,384]{1,0:T(8,128)(2,1)S(1)}, bf16[384,384]{1,0:T(8,128)(2,1)S(1)}, u32[]{:S(2)}, u32[]{:S(2)}) collective-permute-start(bf16[384,384]{1,0:T(8,128)(2,1)S(1)} %copy-done.54), channel_id=1, source_target_pairs={{0,2},{1,3},{2,4},{3,5},{4,6},{5,7},{6,0},{7,1},{8,10},{9,11},{10,... | collective-permute-start | bytes 884744 | tf_op jit(solution)/shard_map/ppermute | solution.py:736
  86.8 23.9 %collective-permute-start.15 = (bf16[384,384]{1,0:T(8,128)(2,1)S(1)}, bf16[384,384]{1,0:T(8,128)(2,1)S(1)}, u32[]{:S(2)}, u32[]{:S(2)}) collective-permute-start(bf16[384,384]{1,0:T(8,128)(2,1)S(1)} %copy-done.54), channel_id=1, source_target_pairs={{0,4},{1,5},{2,6},{3,7},{4,0},{5,1},{6,2},{7,3},{8,12},{9,13},{10,... | collective-permute-start | bytes 884744 | tf_op jit(solution)/shard_map/ppermute | solution.py:736
  87.0 24.9 %collective-permute-start.16 = (bf16[384,384]{1,0:T(8,128)(2,1)S(1)}, bf16[384,384]{1,0:T(8,128)(2,1)S(1)}, u32[]{:S(2)}, u32[]{:S(2)}) collective-permute-start(bf16[384,384]{1,0:T(8,128)(2,1)S(1)} %copy-done.54), channel_id=1, source_target_pairs={{0,6},{1,7},{2,0},{3,1},{4,2},{5,3},{6,4},{7,5},{8,14},{9,15},{10,... | collective-permute-start | bytes 884744 | tf_op jit(solution)/shard_map/ppermute | solution.py:736
  90.3 21.6 %collective-permute-start.13 = (bf16[4,96,384]{2,1,0:T(8,128)(2,1)S(1)}, bf16[4,96,384]{2,1,0:T(8,128)(2,1)}, u32[]{:S(2)}, u32[]{:S(2)}) collective-permute-start(bf16[4,96,384]{2,1,0:T(8,128)(2,1)S(1)} %pad_maximum_fusion.6.refs_0_), channel_id=1, source_target_pairs={{0,1},{1,0},{2,3},{3,2},{4,5},{5,4},{6,7},{7,6},{8,9},{9,8},{10,11... | collective-permute-start | bytes 884744 | tf_op jit(solution)/shard_map/ppermute | solution.py:736
  114.0 31.3 %collective-permute-start.19 = (bf16[4,384,384]{2,1,0:T(8,128)(2,1)S(1)}, bf16[4,384,384]{2,1,0:T(8,128)(2,1)}, u32[]{:S(2)}, u32[]{:S(2)}) collective-permute-start(bf16[4,384,384]{2,1,0:T(8,128)(2,1)S(1)} %pad_maximum_fusion.refs_0_), channel_id=1, source_target_pairs={{0,1},{1,0},{2,3},{3,2},{4,5},{5,4},{6,7},{7,6},{8,9},{9,8},{10,11... | collective-permute-start | bytes 3538952 | tf_op jit(solution)/shard_map/ppermute | solution.py:736
  116.8 23.9 %collective-permute-start.17 = (bf16[4,48,1536]{2,1,0:T(8,128)(2,1)S(1)}, bf16[4,48,1536]{2,1,0:T(8,128)(2,1)S(1)}, u32[]{:S(2)}, u32[]{:S(2)}) collective-permute-start(bf16[4,48,1536]{2,1,0:T(8,128)(2,1)S(1)} %pad_maximum_fusion.4.refs_0_), channel_id=1, source_target_pairs={{0,16},{1,17},{2,18},{3,19},{4,20},{5,21},{6,22},{7,23},{8,24},{9,... | collective-permute-start | bytes 1769480 | tf_op jit(solution)/shard_map/ppermute | solution.py:736
  118.1 23.5 %collective-permute-start.18 = (bf16[4,48,1536]{2,1,0:T(8,128)(2,1)}, bf16[4,48,1536]{2,1,0:T(8,128)(2,1)S(1)}, u32[]{:S(2)}, u32[]{:S(2)}) collective-permute-start(bf16[4,48,1536]{2,1,0:T(8,128)(2,1)} %collective-permute-done.12.refs_2_), channel_id=1, source_target_pairs={{0,16},{1,17},{2,18},{3,19},{4,20},{5,21},{6,22},{7,23},{8,24},{9,... | collective-permute-start | bytes 1769480 | tf_op jit(solution)/shard_map/ppermute | solution.py:736
  134.6 29.3 %collective-permute-start.36 = (bf16[96,384]{1,0:T(8,128)(2,1)S(1)}, bf16[96,384]{1,0:T(8,128)(2,1)S(1)}, u32[]{:S(2)}, u32[]{:S(2)}) collective-permute-start(bf16[96,384]{1,0:T(8,128)(2,1)S(1)} %fusion.22), channel_id=1, source_target_pairs={{0,4},{1,5},{2,6},{3,7},{4,0},{5,1},{6,2},{7,3},{8,12},{9,13},{10,... | collective-permute-start | bytes 221192 | tf_op jit(solution)/shard_map/ppermute | solution.py:736
  139.3 26.7 %collective-permute-start.25 = (bf16[4,48,1536]{2,1,0:T(8,128)(2,1)S(1)}, bf16[4,48,1536]{2,1,0:T(8,128)(2,1)}, u32[]{:S(2)}, u32[]{:S(2)}) collective-permute-start(bf16[4,48,1536]{2,1,0:T(8,128)(2,1)S(1)} %pad_maximum_fusion.4.refs_0_), channel_id=1, source_target_pairs={{0,8},{1,9},{2,10},{3,11},{4,12},{5,13},{6,14},{7,15},{8,0},{9,1},... | collective-permute-start | bytes 1769480 | tf_op jit(solution)/shard_map/ppermute | solution.py:736
  140.7 23.3 %collective-permute-start.23 = (bf16[4,96,384]{2,1,0:T(8,128)(2,1)S(1)}, bf16[4,96,384]{2,1,0:T(8,128)(2,1)S(1)}, u32[]{:S(2)}, u32[]{:S(2)}) collective-permute-start(bf16[4,96,384]{2,1,0:T(8,128)(2,1)S(1)} %pad_maximum_fusion.6.refs_0_), channel_id=1, source_target_pairs={{0,8},{1,9},{2,10},{3,11},{4,12},{5,13},{6,14},{7,15},{8,0},{9,1},... | collective-permute-start | bytes 884744 | tf_op jit(solution)/shard_map/ppermute | solution.py:736
  141.6 26.6 %collective-permute-start.29 = (bf16[4,384,384]{2,1,0:T(8,128)(2,1)S(1)}, bf16[4,384,384]{2,1,0:T(8,128)(2,1)}, u32[]{:S(2)}, u32[]{:S(2)}) collective-permute-start(bf16[4,384,384]{2,1,0:T(8,128)(2,1)S(1)} %pad_maximum_fusion.refs_0_), channel_id=1, source_target_pairs={{0,8},{1,9},{2,10},{3,11},{4,12},{5,13},{6,14},{7,15},{8,0},{9,1},... | collective-permute-start | bytes 3538952 | tf_op jit(solution)/shard_map/ppermute | solution.py:736
  145.3 22.0 %collective-permute-start.26 = (bf16[4,48,1536]{2,1,0:T(8,128)(2,1)}, bf16[4,48,1536]{2,1,0:T(8,128)(2,1)}, u32[]{:S(2)}, u32[]{:S(2)}) collective-permute-start(bf16[4,48,1536]{2,1,0:T(8,128)(2,1)} %collective-permute-done.12.refs_2_), channel_id=1, source_target_pairs={{0,8},{1,9},{2,10},{3,11},{4,12},{5,13},{6,14},{7,15},{8,0},{9,1},... | collective-permute-start | bytes 1769480 | tf_op jit(solution)/shard_map/ppermute | solution.py:736
  166.1 39.2 %collective-permute-start.31 = (bf16[4,96,1152]{2,1,0:T(8,128)(2,1)S(1)}, bf16[4,96,1152]{2,1,0:T(8,128)(2,1)}, u32[]{:S(2)}, u32[]{:S(2)}) collective-permute-start(bf16[4,96,1152]{2,1,0:T(8,128)(2,1)S(1)} %pad_maximum_fusion.3.refs_0_), channel_id=1, source_target_pairs={{0,1},{1,0},{2,3},{3,2},{4,5},{5,4},{6,7},{7,6},{8,9},{9,8},{10,11... | collective-permute-start | bytes 2654216 | tf_op jit(solution)/shard_map/ppermute | solution.py:736
  168.2 32.2 %collective-permute-start.32 = (bf16[48,1536]{1,0:T(8,128)(2,1)}, bf16[48,1536]{1,0:T(8,128)(2,1)S(1)}, u32[]{:S(2)}, u32[]{:S(2)}) collective-permute-start(bf16[48,1536]{1,0:T(8,128)(2,1)} %fusion.23), channel_id=1, source_target_pairs={{0,2},{1,3},{2,4},{3,5},{4,6},{5,7},{6,0},{7,1},{8,10},{9,11},{10,... | collective-permute-start | bytes 442376 | tf_op jit(solution)/shard_map/ppermute | solution.py:736
  171.7 30.4 %collective-permute-start.33 = (bf16[48,1536]{1,0:T(8,128)(2,1)}, bf16[48,1536]{1,0:T(8,128)(2,1)S(1)}, u32[]{:S(2)}, u32[]{:S(2)}) collective-permute-start(bf16[48,1536]{1,0:T(8,128)(2,1)} %fusion.23), channel_id=1, source_target_pairs={{0,4},{1,5},{2,6},{3,7},{4,0},{5,1},{6,2},{7,3},{8,12},{9,13},{10,... | collective-permute-start | bytes 442376 | tf_op jit(solution)/shard_map/ppermute | solution.py:736
  172.5 30.6 %collective-permute-start.34 = (bf16[48,1536]{1,0:T(8,128)(2,1)}, bf16[48,1536]{1,0:T(8,128)(2,1)}, u32[]{:S(2)}, u32[]{:S(2)}) collective-permute-start(bf16[48,1536]{1,0:T(8,128)(2,1)} %fusion.23), channel_id=1, source_target_pairs={{0,6},{1,7},{2,0},{3,1},{4,2},{5,3},{6,4},{7,5},{8,14},{9,15},{10,... | collective-permute-start | bytes 442376 | tf_op jit(solution)/shard_map/ppermute | solution.py:736
  177.0 22.6 %collective-permute-start.37 = (bf16[96,384]{1,0:T(8,128)(2,1)}, bf16[96,384]{1,0:T(8,128)(2,1)}, u32[]{:S(2)}, u32[]{:S(2)}) collective-permute-start(bf16[96,384]{1,0:T(8,128)(2,1)} %copy-done.99), channel_id=1, source_target_pairs={{0,6},{1,7},{2,0},{3,1},{4,2},{5,3},{6,4},{7,5},{8,14},{9,15},{10,... | collective-permute-start | bytes 221192 | tf_op jit(solution)/shard_map/ppermute | solution.py:736
  202.1 51.5 %collective-permute-start.42 = (bf16[384,384]{1,0:T(8,128)(2,1)S(1)}, bf16[384,384]{1,0:T(8,128)(2,1)S(1)}, u32[]{:S(2)}, u32[]{:S(2)}) collective-permute-start(bf16[384,384]{1,0:T(8,128)(2,1)S(1)} %copy-done.53), channel_id=1, source_target_pairs={{0,6},{1,7},{2,0},{3,1},{4,2},{5,3},{6,4},{7,5},{8,14},{9,15},{10,... | collective-permute-start | bytes 884744 | tf_op jit(solution)/shard_map/ppermute | solution.py:736
  203.1 53.8 %collective-permute-start.43 = (bf16[4,96,1152]{2,1,0:T(8,128)(2,1)S(1)}, bf16[4,96,1152]{2,1,0:T(8,128)(2,1)}, u32[]{:S(2)}, u32[]{:S(2)}) collective-permute-start(bf16[4,96,1152]{2,1,0:T(8,128)(2,1)S(1)} %pad_maximum_fusion.3.refs_0_), channel_id=1, source_target_pairs={{0,8},{1,9},{2,10},{3,11},{4,12},{5,13},{6,14},{7,15},{8,0},{9,1},... | collective-permute-start | bytes 2654216 | tf_op jit(solution)/shard_map/ppermute | solution.py:736
  206.2 48.8 %collective-permute-start.39 = (bf16[4,96,384]{2,1,0:T(8,128)(2,1)S(1)}, bf16[4,96,384]{2,1,0:T(8,128)(2,1)S(1)}, u32[]{:S(2)}, u32[]{:S(2)}) collective-permute-start(bf16[4,96,384]{2,1,0:T(8,128)(2,1)S(1)} %pad_maximum_fusion.7.refs_0_), channel_id=1, source_target_pairs={{0,1},{1,0},{2,3},{3,2},{4,5},{5,4},{6,7},{7,6},{8,9},{9,8},{10,11... | collective-permute-start | bytes 884744 | tf_op jit(solution)/shard_map/ppermute | solution.py:736
  208.6 46.7 %collective-permute-start.38 = (bf16[4,48,1536]{2,1,0:T(8,128)(2,1)S(1)}, bf16[4,48,1536]{2,1,0:T(8,128)(2,1)}, u32[]{:S(2)}, u32[]{:S(2)}) collective-permute-start(bf16[4,48,1536]{2,1,0:T(8,128)(2,1)S(1)} %pad_maximum_fusion.5.refs_0_), channel_id=1, source_target_pairs={{0,1},{1,0},{2,3},{3,2},{4,5},{5,4},{6,7},{7,6},{8,9},{9,8},{10,11... | collective-permute-start | bytes 1769480 | tf_op jit(solution)/shard_map/ppermute | solution.py:736
  221.0 36.2 %collective-permute-start.44 = (bf16[4,96,1152]{2,1,0:T(8,128)(2,1)}, bf16[4,96,1152]{2,1,0:T(8,128)(2,1)}, u32[]{:S(2)}, u32[]{:S(2)}) collective-permute-start(bf16[4,96,1152]{2,1,0:T(8,128)(2,1)} %collective-permute-done.31.refs_2_), channel_id=1, source_target_pairs={{0,8},{1,9},{2,10},{3,11},{4,12},{5,13},{6,14},{7,15},{8,0},{9,1},... | collective-permute-start | bytes 2654216 | tf_op jit(solution)/shard_map/ppermute | solution.py:736
  253.7 40.5 %collective-permute-start.45 = (bf16[4,48,1536]{2,1,0:T(8,128)(2,1)S(1)}, bf16[4,48,1536]{2,1,0:T(8,128)(2,1)}, u32[]{:S(2)}, u32[]{:S(2)}) collective-permute-start(bf16[4,48,1536]{2,1,0:T(8,128)(2,1)S(1)} %pad_maximum_fusion.5.refs_0_), channel_id=1, source_target_pairs={{0,16},{1,17},{2,18},{3,19},{4,20},{5,21},{6,22},{7,23},{8,24},{9,... | collective-permute-start | bytes 1769480 | tf_op jit(solution)/shard_map/ppermute | solution.py:736
  255.0 40.0 %collective-permute-start.50 = (bf16[4,48,1536]{2,1,0:T(8,128)(2,1)S(1)}, bf16[4,48,1536]{2,1,0:T(8,128)(2,1)}, u32[]{:S(2)}, u32[]{:S(2)}) collective-permute-start(bf16[4,48,1536]{2,1,0:T(8,128)(2,1)S(1)} %pad_maximum_fusion.5.refs_0_), channel_id=1, source_target_pairs={{0,8},{1,9},{2,10},{3,11},{4,12},{5,13},{6,14},{7,15},{8,0},{9,1},... | collective-permute-start | bytes 1769480 | tf_op jit(solution)/shard_map/ppermute | solution.py:736
  256.9 37.4 %collective-permute-start.47 = (bf16[4,384,384]{2,1,0:T(8,128)(2,1)S(1)}, bf16[4,384,384]{2,1,0:T(8,128)(2,1)S(1)}, u32[]{:S(2)}, u32[]{:S(2)}) collective-permute-start(bf16[4,384,384]{2,1,0:T(8,128)(2,1)S(1)} %pad_maximum_fusion.1.refs_0_), channel_id=1, source_target_pairs={{0,1},{1,0},{2,3},{3,2},{4,5},{5,4},{6,7},{7,6},{8,9},{9,8},{10,11... | collective-permute-start | bytes 3538952 | tf_op jit(solution)/shard_map/ppermute | solution.py:736
  257.2 37.1 %collective-permute-start.46 = (bf16[4,48,1536]{2,1,0:T(8,128)(2,1)}, bf16[4,48,1536]{2,1,0:T(8,128)(2,1)}, u32[]{:S(2)}, u32[]{:S(2)}) collective-permute-start(bf16[4,48,1536]{2,1,0:T(8,128)(2,1)} %collective-permute-done.38.refs_2_), channel_id=1, source_target_pairs={{0,16},{1,17},{2,18},{3,19},{4,20},{5,21},{6,22},{7,23},{8,24},{9,... | collective-permute-start | bytes 1769480 | tf_op jit(solution)/shard_map/ppermute | solution.py:736
  289.1 31.3 %collective-permute-start.54 = (bf16[4,384,384]{2,1,0:T(8,128)(2,1)S(1)}, bf16[4,384,384]{2,1,0:T(8,128)(2,1)}, u32[]{:S(2)}, u32[]{:S(2)}) collective-permute-start(bf16[4,384,384]{2,1,0:T(8,128)(2,1)S(1)} %pad_maximum_fusion.1.refs_0_), channel_id=1, source_target_pairs={{0,8},{1,9},{2,10},{3,11},{4,12},{5,13},{6,14},{7,15},{8,0},{9,1},... | collective-permute-start | bytes 3538952 | tf_op jit(solution)/shard_map/ppermute | solution.py:736
  294.3 26.1 %collective-permute-start.55 = (bf16[4,384,384]{2,1,0:T(8,128)(2,1)S(1)}, bf16[4,384,384]{2,1,0:T(8,128)(2,1)}, u32[]{:S(2)}, u32[]{:S(2)}) collective-permute-start(bf16[4,384,384]{2,1,0:T(8,128)(2,1)S(1)} %collective-permute-done.47.refs_2_), channel_id=1, source_target_pairs={{0,8},{1,9},{2,10},{3,11},{4,12},{5,13},{6,14},{7,15},{8,0},{9,1},... | collective-permute-start | bytes 3538952 | tf_op jit(solution)/shard_map/ppermute | solution.py:736
  402.3 37.1 %collective-permute-start.61 = (bf16[1,4,96,384]{3,2,1,0:T(8,128)(2,1)}, bf16[1,4,96,384]{3,2,1,0:T(8,128)(2,1)S(1)}, u32[]{:S(2)}, u32[]{:S(2)}) collective-permute-start(bf16[1,4,96,384]{3,2,1,0:T(8,128)(2,1)} %get-tuple-element.366), channel_id=1, source_target_pairs={{0,1},{1,0},{2,3},{3,2},{4,5},{5,4},{6,7},{7,6},{8,9},{9,8},{10,11... | collective-permute-start | bytes 884744 | tf_op jit(solution)/shard_map/ppermute | solution.py:736
  410.5 28.9 %collective-permute-start.60 = (bf16[2,4,2,48,768]{4,3,2,1,0:T(8,128)(2,1)}, bf16[2,4,2,48,768]{4,3,2,1,0:T(8,128)(2,1)S(1)}, u32[]{:S(2)}, u32[]{:S(2)}) collective-permute-start(bf16[2,4,2,48,768]{4,3,2,1,0:T(8,128)(2,1)} %get-tuple-element.364), channel_id=1, source_target_pairs={{0,16},{1,17},{2,18},{3,19},{4,20},{5,21},{6,22},{7,23},{8,24},{9,... | collective-permute-start | bytes 3538952 | tf_op jit(solution)/shard_map/ppermute | solution.py:736
  420.1 27.0 %collective-permute-start.59 = (bf16[1,4,384,384]{3,2,1,0:T(8,128)(2,1)}, bf16[1,4,384,384]{3,2,1,0:T(8,128)(2,1)S(1)}, u32[]{:S(2)}, u32[]{:S(2)}) collective-permute-start(bf16[1,4,384,384]{3,2,1,0:T(8,128)(2,1)} %get-tuple-element.362), channel_id=1, source_target_pairs={{0,1},{1,0},{2,3},{3,2},{4,5},{5,4},{6,7},{7,6},{8,9},{9,8},{10,11... | collective-permute-start | bytes 3538952 | tf_op jit(solution)/shard_map/ppermute | solution.py:736
  453.6 40.5 %collective-permute-start.66 = (bf16[3,4,2,96,384]{4,3,2,1,0:T(8,128)(2,1)}, bf16[3,4,2,96,384]{4,3,2,1,0:T(8,128)(2,1)}, u32[]{:S(2)}, u32[]{:S(2)}) collective-permute-start(bf16[3,4,2,96,384]{4,3,2,1,0:T(8,128)(2,1)} %shard_map.300), channel_id=1, source_target_pairs={{0,8},{1,9},{2,10},{3,11},{4,12},{5,13},{6,14},{7,15},{8,0},{9,1},... | collective-permute-start | bytes 5308424 | tf_op jit(solution)/shard_map/ppermute | solution.py:736
  457.8 32.5 %collective-permute-start.63 = (bf16[1,96,384]{2,1,0:T(8,128)(2,1)}, bf16[1,96,384]{2,1,0:T(8,128)(2,1)S(1)}, u32[]{:S(2)}, u32[]{:S(2)}) collective-permute-start(bf16[1,96,384]{2,1,0:T(8,128)(2,1)} %get-tuple-element.374), channel_id=1, source_target_pairs={{0,2},{1,3},{2,4},{3,5},{4,6},{5,7},{6,0},{7,1},{8,10},{9,11},{10,... | collective-permute-start | bytes 221192 | tf_op jit(solution)/shard_map/ppermute | solution.py:736
  461.9 28.8 %collective-permute-start.64 = (bf16[1,96,384]{2,1,0:T(8,128)(2,1)}, bf16[1,96,384]{2,1,0:T(8,128)(2,1)S(1)}, u32[]{:S(2)}, u32[]{:S(2)}) collective-permute-start(bf16[1,96,384]{2,1,0:T(8,128)(2,1)} %get-tuple-element.375), channel_id=1, source_target_pairs={{0,4},{1,5},{2,6},{3,7},{4,0},{5,1},{6,2},{7,3},{8,12},{9,13},{10,... | collective-permute-start | bytes 221192 | tf_op jit(solution)/shard_map/ppermute | solution.py:736
  461.9 31.1 %collective-permute-start.65 = (bf16[1,96,384]{2,1,0:T(8,128)(2,1)}, bf16[1,96,384]{2,1,0:T(8,128)(2,1)S(1)}, u32[]{:S(2)}, u32[]{:S(2)}) collective-permute-start(bf16[1,96,384]{2,1,0:T(8,128)(2,1)} %get-tuple-element.376), channel_id=1, source_target_pairs={{0,6},{1,7},{2,0},{3,1},{4,2},{5,3},{6,4},{7,5},{8,14},{9,15},{10,... | collective-permute-start | bytes 221192 | tf_op jit(solution)/shard_map/ppermute | solution.py:736
  467.2 26.9 %collective-permute-start.62 = (bf16[2,4,48,768]{3,2,1,0:T(8,128)(2,1)}, bf16[2,4,48,768]{3,2,1,0:T(8,128)(2,1)S(1)}, u32[]{:S(2)}, u32[]{:S(2)}) collective-permute-start(bf16[2,4,48,768]{3,2,1,0:T(8,128)(2,1)} %shard_map.298), channel_id=1, source_target_pairs={{0,1},{1,0},{2,3},{3,2},{4,5},{5,4},{6,7},{7,6},{8,9},{9,8},{10,11... | collective-permute-start | bytes 1769480 | tf_op jit(solution)/shard_map/ppermute | solution.py:736
  490.4 49.1 %collective-permute-start.67 = (bf16[1,384,384]{2,1,0:T(8,128)(2,1)}, bf16[1,384,384]{2,1,0:T(8,128)(2,1)S(1)}, u32[]{:S(2)}, u32[]{:S(2)}) collective-permute-start(bf16[1,384,384]{2,1,0:T(8,128)(2,1)} %get-tuple-element.390), channel_id=1, source_target_pairs={{0,2},{1,3},{2,4},{3,5},{4,6},{5,7},{6,0},{7,1},{8,10},{9,11},{10,... | collective-permute-start | bytes 884744 | tf_op jit(solution)/shard_map/ppermute | solution.py:736
  490.7 49.4 %collective-permute-start.68 = (bf16[1,384,384]{2,1,0:T(8,128)(2,1)}, bf16[1,384,384]{2,1,0:T(8,128)(2,1)S(1)}, u32[]{:S(2)}, u32[]{:S(2)}) collective-permute-start(bf16[1,384,384]{2,1,0:T(8,128)(2,1)} %get-tuple-element.391), channel_id=1, source_target_pairs={{0,4},{1,5},{2,6},{3,7},{4,0},{5,1},{6,2},{7,3},{8,12},{9,13},{10,... | collective-permute-start | bytes 884744 | tf_op jit(solution)/shard_map/ppermute | solution.py:736
  493.0 47.8 %collective-permute-start.69 = (bf16[1,384,384]{2,1,0:T(8,128)(2,1)}, bf16[1,384,384]{2,1,0:T(8,128)(2,1)S(1)}, u32[]{:S(2)}, u32[]{:S(2)}) collective-permute-start(bf16[1,384,384]{2,1,0:T(8,128)(2,1)} %get-tuple-element.392), channel_id=1, source_target_pairs={{0,6},{1,7},{2,0},{3,1},{4,2},{5,3},{6,4},{7,5},{8,14},{9,15},{10,... | collective-permute-start | bytes 884744 | tf_op jit(solution)/shard_map/ppermute | solution.py:736
  501.1 52.3 %collective-permute-start.74 = (bf16[3,4,2,48,384]{4,3,2,1,0:T(8,128)(2,1)}, bf16[3,4,2,48,384]{4,3,2,1,0:T(8,128)(2,1)S(1)}, u32[]{:S(2)}, u32[]{:S(2)}) collective-permute-start(bf16[3,4,2,48,384]{4,3,2,1,0:T(8,128)(2,1)} %get-tuple-element.402), channel_id=1, source_target_pairs={{0,16},{1,17},{2,18},{3,19},{4,20},{5,21},{6,22},{7,23},{8,24},{9,... | collective-permute-start | bytes 2654216 | tf_op jit(solution)/shard_map/ppermute | solution.py:736
  503.7 46.1 %collective-permute-start.73 = (bf16[1,96,384]{2,1,0:T(8,128)(2,1)}, bf16[1,96,384]{2,1,0:T(8,128)(2,1)S(1)}, u32[]{:S(2)}, u32[]{:S(2)}) collective-permute-start(bf16[1,96,384]{2,1,0:T(8,128)(2,1)} %shard_map.304.refs_0_), channel_id=1, source_target_pairs={{0,16},{1,17},{2,18},{3,19},{4,20},{5,21},{6,22},{7,23},{8,24},{9,... | collective-permute-start | bytes 221192 | tf_op jit(solution)/shard_map/ppermute | solution.py:736
  549.8 43.1 %collective-permute-start.82 = (bf16[2,4,2,96,768]{4,3,2,1,0:T(8,128)(2,1)}, bf16[2,4,2,96,768]{4,3,2,1,0:T(8,128)(2,1)}, u32[]{:S(2)}, u32[]{:S(2)}) collective-permute-start(bf16[2,4,2,96,768]{4,3,2,1,0:T(8,128)(2,1)} %shard_map.311), channel_id=1, source_target_pairs={{0,8},{1,9},{2,10},{3,11},{4,12},{5,13},{6,14},{7,15},{8,0},{9,1},... | collective-permute-start | bytes 7077896 | tf_op jit(solution)/shard_map/ppermute | solution.py:736
  561.5 31.5 %collective-permute-start.81 = (bf16[1,4,2,384,384]{4,3,2,1,0:T(8,128)(2,1)}, bf16[1,4,2,384,384]{4,3,2,1,0:T(8,128)(2,1)}, u32[]{:S(2)}, u32[]{:S(2)}) collective-permute-start(bf16[1,4,2,384,384]{4,3,2,1,0:T(8,128)(2,1)} %shard_map.310), channel_id=1, source_target_pairs={{0,8},{1,9},{2,10},{3,11},{4,12},{5,13},{6,14},{7,15},{8,0},{9,1},... | collective-permute-start | bytes 7077896 | tf_op jit(solution)/shard_map/ppermute | solution.py:736
  593.0 31.3 %collective-permute-start.92 = (f32[16896]{0:T(1024)S(1)}, f32[16896]{0:T(1024)S(1)}, u32[]{:S(2)}, u32[]{:S(2)}) collective-permute-start(f32[16896]{0:T(1024)S(1)} %add.125), channel_id=1, source_target_pairs={{0,16},{1,17},{2,18},{3,19},{4,20},{5,21},{6,22},{7,23},{8,24},{9,... | collective-permute-start | bytes 202760 | tf_op jit(solution)/shard_map/ppermute | solution.py:736
  598.6 46.5 %collective-permute-start.91 = (bf16[1,4,96,384]{3,2,1,0:T(8,128)(2,1)}, bf16[1,4,96,384]{3,2,1,0:T(8,128)(2,1)S(1)}, u32[]{:S(2)}, u32[]{:S(2)}) collective-permute-start(bf16[1,4,96,384]{3,2,1,0:T(8,128)(2,1)} %get-tuple-element.439), channel_id=1, source_target_pairs={{0,1},{1,0},{2,3},{3,2},{4,5},{5,4},{6,7},{7,6},{8,9},{9,8},{10,11... | collective-permute-start | bytes 884744 | tf_op jit(solution)/shard_map/ppermute | solution.py:736
  606.9 38.2 %collective-permute-start.90 = (bf16[2,4,2,48,768]{4,3,2,1,0:T(8,128)(2,1)}, bf16[2,4,2,48,768]{4,3,2,1,0:T(8,128)(2,1)S(1)}, u32[]{:S(2)}, u32[]{:S(2)}) collective-permute-start(bf16[2,4,2,48,768]{4,3,2,1,0:T(8,128)(2,1)} %get-tuple-element.437), channel_id=1, source_target_pairs={{0,16},{1,17},{2,18},{3,19},{4,20},{5,21},{6,22},{7,23},{8,24},{9,... | collective-permute-start | bytes 3538952 | tf_op jit(solution)/shard_map/ppermute | solution.py:736
  624.2 26.5 %collective-permute-start.89 = (bf16[1,4,384,384]{3,2,1,0:T(8,128)(2,1)}, bf16[1,4,384,384]{3,2,1,0:T(8,128)(2,1)S(1)}, u32[]{:S(2)}, u32[]{:S(2)}) collective-permute-start(bf16[1,4,384,384]{3,2,1,0:T(8,128)(2,1)} %get-tuple-element.435), channel_id=1, source_target_pairs={{0,1},{1,0},{2,3},{3,2},{4,5},{5,4},{6,7},{7,6},{8,9},{9,8},{10,11... | collective-permute-start | bytes 3538952 | tf_op jit(solution)/shard_map/ppermute | solution.py:736
  657.3 38.0 %collective-permute-start.101 = (bf16[3,4,2,96,384]{4,3,2,1,0:T(8,128)(2,1)}, bf16[3,4,2,96,384]{4,3,2,1,0:T(8,128)(2,1)}, u32[]{:S(2)}, u32[]{:S(2)}) collective-permute-start(bf16[3,4,2,96,384]{4,3,2,1,0:T(8,128)(2,1)} %shard_map.323), channel_id=1, source_target_pairs={{0,8},{1,9},{2,10},{3,11},{4,12},{5,13},{6,14},{7,15},{8,0},{9,1},... | collective-permute-start | bytes 5308424 | tf_op jit(solution)/shard_map/ppermute | solution.py:736
  672.4 22.8 %collective-permute-start.93 = (bf16[3,48,384]{2,1,0:T(8,128)(2,1)}, bf16[3,48,384]{2,1,0:T(8,128)(2,1)S(1)}, u32[]{:S(2)}, u32[]{:S(2)}) collective-permute-start(bf16[3,48,384]{2,1,0:T(8,128)(2,1)} %shard_map.320.refs_4_), channel_id=1, source_target_pairs={{0,16},{1,17},{2,18},{3,19},{4,20},{5,21},{6,22},{7,23},{8,24},{9,... | collective-permute-start | bytes 331784 | tf_op jit(solution)/shard_map/ppermute | solution.py:736
  702.2 47.5 %collective-permute-start.110 = (bf16[3,4,2,48,384]{4,3,2,1,0:T(8,128)(2,1)}, bf16[3,4,2,48,384]{4,3,2,1,0:T(8,128)(2,1)S(1)}, u32[]{:S(2)}, u32[]{:S(2)}) collective-permute-start(bf16[3,4,2,48,384]{4,3,2,1,0:T(8,128)(2,1)} %get-tuple-element.473), channel_id=1, source_target_pairs={{0,16},{1,17},{2,18},{3,19},{4,20},{5,21},{6,22},{7,23},{8,24},{9,... | collective-permute-start | bytes 2654216 | tf_op jit(solution)/shard_map/ppermute | solution.py:736
  708.4 28.0 %collective-permute-start.104 = (bf16[1,384,384]{2,1,0:T(8,128)(2,1)}, bf16[1,384,384]{2,1,0:T(8,128)(2,1)S(1)}, u32[]{:S(2)}, u32[]{:S(2)}) collective-permute-start(bf16[1,384,384]{2,1,0:T(8,128)(2,1)} %get-tuple-element.462), channel_id=1, source_target_pairs={{0,6},{1,7},{2,0},{3,1},{4,2},{5,3},{6,4},{7,5},{8,14},{9,15},{10,... | collective-permute-start | bytes 884744 | tf_op jit(solution)/shard_map/ppermute | solution.py:736
  713.5 22.9 %collective-permute-start.109 = (f32[16896]{0:T(1024)S(1)}, f32[16896]{0:T(1024)S(1)}, u32[]{:S(2)}, u32[]{:S(2)}) collective-permute-start(f32[16896]{0:T(1024)S(1)} %add.127), channel_id=1, source_target_pairs={{0,4},{1,5},{2,6},{3,7},{4,0},{5,1},{6,2},{7,3},{8,12},{9,13},{10,... | collective-permute-start | bytes 202760 | tf_op jit(solution)/shard_map/ppermute | solution.py:736
  720.0 27.3 %collective-permute-start.108 = (bf16[1,96,384]{2,1,0:T(8,128)(2,1)}, bf16[1,96,384]{2,1,0:T(8,128)(2,1)S(1)}, u32[]{:S(2)}, u32[]{:S(2)}) collective-permute-start(bf16[1,96,384]{2,1,0:T(8,128)(2,1)} %shard_map.327.refs_0_), channel_id=1, source_target_pairs={{0,16},{1,17},{2,18},{3,19},{4,20},{5,21},{6,22},{7,23},{8,24},{9,... | collective-permute-start | bytes 221192 | tf_op jit(solution)/shard_map/ppermute | solution.py:736
  754.7 26.9 %collective-permute-start.119 = (bf16[3,4,48,384]{3,2,1,0:T(8,128)(2,1)}, bf16[3,4,48,384]{3,2,1,0:T(8,128)(2,1)S(1)}, u32[]{:S(2)}, u32[]{:S(2)}) collective-permute-start(bf16[3,4,48,384]{3,2,1,0:T(8,128)(2,1)} %shard_map.332), channel_id=1, source_target_pairs={{0,1},{1,0},{2,3},{3,2},{4,5},{5,4},{6,7},{7,6},{8,9},{9,8},{10,11... | collective-permute-start | bytes 1327112 | tf_op jit(solution)/shard_map/ppermute | solution.py:736
  757.6 23.9 %collective-permute-start.112 = (bf16[1,384,384]{2,1,0:T(8,128)(2,1)}, bf16[1,384,384]{2,1,0:T(8,128)(2,1)S(1)}, u32[]{:S(2)}, u32[]{:S(2)}) collective-permute-start(bf16[1,384,384]{2,1,0:T(8,128)(2,1)} %shard_map.329.refs_0_), channel_id=1, source_target_pairs={{0,16},{1,17},{2,18},{3,19},{4,20},{5,21},{6,22},{7,23},{8,24},{9,... | collective-permute-start | bytes 884744 | tf_op jit(solution)/shard_map/ppermute | solution.py:736
  (195 other events, 2282.1 us)

commit v5 on v4

--- a/solution.py
+++ b/solution.py
@@ -23,6 +23,7 @@
 INV_ROOT = (2.0 * 3.141592653589793) ** -0.5
 MATRICES = (0, 2, 6, 8)
 VECTORS = (1, 3, 4, 5, 7, 9, 10, 11)
+UNIT = 384
 AXES = ("rep", "shard")
 CHIPS_Z, CHIPS_X, CHIPS_Y, CORES = 4, 2, 2, 2
 norm_eps = 1e-06
@@ -598,26 +599,27 @@
         (out_ref,) = refs
         out_ref[...] = product.astype(jnp.bfloat16).reshape(out_ref.shape)
         return
-    near_ref, send_ref, keep_ref, sum_ref = refs
+    near_ref, (send_ref, keep_ref, sum_ref) = refs[0], refs[-3:]
     total = product + near_ref[...].astype(jnp.float32).reshape(product.shape)
     sum_ref[...] = total.astype(jnp.bfloat16).reshape(sum_ref.shape)
     if split_y:
         send_ref[0] = sum_ref[:, :, 1 - at_ref[2]]
         keep_ref[0] = sum_ref[:, :, at_ref[2]]
     else:
-        send_ref[0] = sum_ref[:, 1 - at_ref[1]]
-        keep_ref[0] = sum_ref[:, at_ref[1]]
+        send_ref[...] = sum_ref[:, 1 - at_ref[1]]
+        keep_ref[...] = sum_ref[:, at_ref[1]]
 
 
 class Grad:
-    def __init__(self, left, own, away, cut, tiles, half):
+    def __init__(self, number, left, own, away, cut, tiles, half):
+        self.number = number
         self.left, self.rights = left, (own, away)
         self.cut, self.tiles, self.half = cut, tiles, half
         self.depth = left.shape[1]
         self.parts = 1 if self.depth > D else tiles
         self.rows = self.depth // (CHIPS_Z * CHIPS_X)
 
-    def product(self, at, other, split_y=None, near=None):
+    def product(self, at, other, split_y=None, near=None, start=0, total=0, before=()):
         flip = 1 if other else 0
         left, right = self.left, self.rights[flip]
         count = left.shape[0]
@@ -645,16 +647,21 @@
         else:
             in_specs.append(full)
             args.append(near)
+            in_specs += [pl.BlockSpec(memory_space=pl.ANY)] * len(before)
+            args += before
             if split_y:
                 short = self.rows // CHIPS_Y
                 kept = (CHIPS_X, short, self.half)
                 scratch = [pltpu.VMEM((zs, CHIPS_X, CHIPS_Y, short, self.half), jnp.bfloat16)]
+                spec = pl.BlockSpec((1, zs, *kept), lambda i, at: (*place(i), 0, 0, 0))
+                shape = (self.parts, CHIPS_Z, *kept)
             else:
-                kept = (self.rows, self.half)
                 scratch = [pltpu.VMEM((zs, CHIPS_X, self.rows, self.half), jnp.bfloat16)]
-            rest = (0,) * len(kept)
-            out_specs = [pl.BlockSpec((1, zs, *kept), lambda i, at: (*place(i), *rest))] * 2
-            shapes = [jax.ShapeDtypeStruct((self.parts, CHIPS_Z, *kept), jnp.bfloat16)] * 2
+                first = start // self.rows
+                index = (lambda i, at: (i, first, 0)) if tall else (lambda i, at: (0, first + i, 0))
+                spec = pl.BlockSpec((zs, self.rows, self.half), index)
+                shape = (CHIPS_Z, total, self.half)
+            out_specs, shapes = [spec] * 2, [jax.ShapeDtypeStruct(shape, jnp.bfloat16)] * 2
         return pl.pallas_call(
             functools.partial(weight_grad_kernel, split_y),
             grid_spec=pltpu.PrefetchScalarGridSpec(
@@ -665,6 +672,7 @@
                 scratch_shapes=scratch,
             ),
             out_shape=shapes,
+            input_output_aliases={4 + place: place for place in range(len(before))},
             compiler_params=kernel_params(),
             cost_estimate=cost(4 * count * D * self.tiles * self.half, left, right),
         )(at, *args)
@@ -701,16 +709,22 @@
     )(at, *[array for array, _, _ in terms])
 
 
+CHUNKS = {
+    "first": (0, (0,), False),
+    "rest": (0, (2, 6, 8), True),
+    "next": (1, (0, 2), False),
+    "last": (1, (6, 8), False),
+}
 FORWARD = {
-    "begin": ((), ((0, 0),)),
-    "prepared": (((0, 0),), ((0, 2), (0, 6), (0, 8))),
-    "ready": (((0, 0),), ()),
-    (0, "projected"): (((0, 6), (0, 2)), ()),
-    (0, "half"): (((0, 6), (0, 2), (0, 8)), ((1, 0),)),
-    (0, "context"): (((0, 6), (0, 8), (1, 0)), ((1, 6), (1, 2))),
-    (0, "placed"): (((1, 0), (1, 6), (1, 2)), ((1, 8),)),
-    (0, "result"): (((1, 6), (1, 2), (1, 8)), ()),
-    (1, "half"): (((1, 6), (1, 8)), ()),
+    "begin": ((), ("first",)),
+    "packed": (("first",), ("rest",)),
+    "prepared": (("first",), ()),
+    "ready": (("rest",), ("next",)),
+    (0, "half"): (("rest", "next"), ("last",)),
+    (0, "context"): (("next",), ()),
+    (0, "waited"): (("rest",), ()),
+    (0, "placed"): (("last",), ()),
+    (1, "half"): (("last",), ()),
 }
 
 
@@ -736,45 +750,96 @@
     return lax.ppermute(value, AXES, pairs)
 
 
-def place_kernel(split_y, half, at_ref, *refs):
-    pieces, out_ref = refs[:-1], refs[-1]
-    rows = out_ref.shape[2]
+def pack_kernel(plan, at_ref, *refs):
+    ins, outs = refs[: len(MATRICES)], refs[len(MATRICES) :]
+    for out_ref, (layer, numbers, split_y) in zip(outs, plan):
+        start = 0
+        for number in numbers:
+            ref = ins[MATRICES.index(number)]
+            rows, half = ref.shape[1], ref.shape[2] // CORES
+            first = 0
+            if split_y:
+                rows = rows // CHIPS_Y
+                first = pl.multiple_of(at_ref[2] * rows, 16)
+            for at in range(0, half, UNIT):
+                column = pl.multiple_of(at_ref[3] * half + at, 128)
+                out_ref[start : start + rows] = ref[layer, pl.ds(first, rows), pl.ds(column, UNIT)]
+                start += rows
+
+
+def chunk_rows(weights, numbers, split_y):
+    found = []
+    for number in numbers:
+        _, rows, columns = weights[number].shape
+        found.append((columns // (CORES * UNIT), rows // (CHIPS_Y if split_y else 1)))
+    return found
+
+
+def pack(weights, names, place):
+    plan = [CHUNKS[name] for name in names]
+    shapes = []
+    for _, numbers, split_y in plan:
+        shapes.append((sum(u * r for u, r in chunk_rows(weights, numbers, split_y)), UNIT))
+    matrices = [weights[number] for number in MATRICES]
+    packed = pl.pallas_call(
+        functools.partial(pack_kernel, plan),
+        grid_spec=pltpu.PrefetchScalarGridSpec(
+            num_scalar_prefetch=1,
+            grid=(1,),
+            in_specs=[pl.BlockSpec(matrix.shape, lambda i, at: (0, 0, 0)) for matrix in matrices],
+            out_specs=[pl.BlockSpec(shape, lambda i, at: (0, 0)) for shape in shapes],
+        ),
+        out_shape=[jax.ShapeDtypeStruct(shape, jnp.bfloat16) for shape in shapes],
+        compiler_params=kernel_params(),
+        cost_estimate=cost(0, *matrices),
+    )(place.at, *matrices)
+    return dict(zip(names, packed))
+
+
+def place_kernel(layout, split_y, count, at_ref, *refs):
+    pieces, outs = refs[:count], refs[count:]
     for number, piece in enumerate(pieces):
         core = (at_ref[3] + number % CORES) % CORES
         x = (at_ref[1] + number // CORES % CHIPS_X) % CHIPS_X
         row = (at_ref[2] + number // (CORES * CHIPS_X)) % CHIPS_Y if split_y else 0
-        column = pl.multiple_of(core * half, 128)
-        out_ref[x, row, :, pl.ds(column, half)] = piece[0, 0:rows]
-
-
-def place_pieces(pieces, rows, split_y, place):
-    _, held, half = pieces[0].shape
+        start, unit = 0, piece.shape[2]
+        for out_ref, (units, rows) in zip(outs, layout):
+            for at in range(units):
+                column = pl.multiple_of((core * units + at) * unit, 128)
+                out_ref[x, row, :, pl.ds(column, unit)] = piece[0, start : start + rows]
+                start += rows
+
+
+def place_pieces(pieces, layout, split_y, place):
+    _, held, unit = pieces[0].shape
     splits = CHIPS_Y if split_y else 1
-    whole = pl.pallas_call(
-        functools.partial(place_kernel, split_y, half),
+    shapes = [(CHIPS_Z * CHIPS_X, splits, rows, CORES * units * unit) for units, rows in layout]
+    wholes = pl.pallas_call(
+        functools.partial(place_kernel, layout, split_y, len(pieces)),
         grid_spec=pltpu.PrefetchScalarGridSpec(
             num_scalar_prefetch=1,
             grid=(CHIPS_Z,),
-            in_specs=[pl.BlockSpec((1, held, half), lambda k, at: (k, 0, 0))] * len(pieces),
-            out_specs=pl.BlockSpec(
-                (CHIPS_X, splits, rows, 2 * half),
-                lambda k, at: (lax.rem(at[0] + CHIPS_Z - k, CHIPS_Z), 0, 0, 0),
-            ),
+            in_specs=[pl.BlockSpec((1, held, unit), lambda k, at: (k, 0, 0))] * len(pieces),
+            out_specs=[
+                pl.BlockSpec(
+                    (CHIPS_X, *shape[1:]),
+                    lambda k, at: (lax.rem(at[0] + CHIPS_Z - k, CHIPS_Z), 0, 0, 0),
+                )
+                for shape in shapes
+            ],
         ),
-        out_shape=jax.ShapeDtypeStruct(
-            (CHIPS_Z * CHIPS_X, splits, rows, 2 * half), jnp.bfloat16
-        ),
+        out_shape=[jax.ShapeDtypeStruct(shape, jnp.bfloat16) for shape in shapes],
         compiler_params=kernel_params(),
         cost_estimate=pl.CostEstimate(
             flops=0,
-            bytes_accessed=4 * CHIPS_Z * len(pieces) * rows * half,
+            bytes_accessed=4 * CHIPS_Z * len(pieces) * held * unit,
             transcendentals=0,
         ),
     )(place.at, *pieces)
-    return whole.reshape(CHIPS_Z * CHIPS_X * splits * rows, 2 * half)
-
-
-def gather_chain(block, rows, split_y, place):
+    return [whole.reshape(-1, whole.shape[-1]) for whole in wholes]
+
+
+def gather_chain(block, layout, split_y, place):
     parts = yield [hop(block, dz=k) for k in range(1, CHIPS_Z)]
     stack = jnp.stack([block, *parts])
     (across,) = yield [hop(stack, dx=1)]
@@ -782,10 +847,11 @@
     if split_y:
         pieces = pieces + (yield [hop(piece, dy=1) for piece in pieces])
     others = yield [hop(piece, dc=1) for piece in pieces]
-    whole = place_pieces(
-        [item for pair in zip(pieces, others) for item in pair], rows, split_y, place
-    )
-    return whole, jnp.stack([stack[:, rows:], across[:, rows:]], axis=1)
+    wholes = place_pieces(
+        [item for pair in zip(pieces, others) for item in pair], layout, split_y, place
+    )
+    rows = sum(units * tall for units, tall in layout)
+    return wholes, jnp.stack([stack[:, rows:], across[:, rows:]], axis=1)
 
 
 class Flow:
@@ -834,115 +900,131 @@
     return out
 
 
-def gather_block(weights, layer, number, place):
-    shard = weights[number][layer]
-    rows, columns = shard.shape
-    split_y = number == 6
-    tall = rows // CHIPS_Y if split_y else rows
-    start = (place.y * tall if split_y else 0, place.core * (columns // 2))
-    block = lax.dynamic_slice(shard, start, (tall, columns // 2))
-    if (layer, number) == (0, 0):
-        vectors = jnp.concatenate([weights[member] for member in VECTORS], axis=1)
-        block = jnp.concatenate([block, jnp.pad(vectors, ((0, 16 - LAYERS), (0, 0)))])
-    return block, tall, split_y
-
-
-def reduce_chain(grad, place, y_first):
+def first_block(weights, place):
+    shard = weights[0][0]
+    half = shard.shape[1] // CORES
+    block = lax.dynamic_slice_in_dim(shard, place.core * half, half, axis=1)
+    vectors = jnp.concatenate([weights[member] for member in VECTORS], axis=1)
+    return jnp.concatenate([block, jnp.pad(vectors, ((0, 16 - LAYERS), (0, 0)))])
+
+
+def pick_sum(at, own, terms, rows, steps):
+    groups = [[(array, block, index(k)) for array, block, index in terms] for k in range(CHIPS_Z)]
+    return combine(at, steps, groups, [own] * CHIPS_Z)
+
+
+def reduce_y_first(grad, place):
     at = place.at
     parts, half = grad.parts, grad.half
+    rows = grad.rows // CHIPS_Y
     away = grad.product(at, True)
     (near,) = yield [hop(away, dc=1)]
-    send, keep = grad.product(at, False, y_first, near)
+    send, keep = grad.product(at, False, True, near)
     flip = lambda value: 1 - value
-    if y_first:
-        rows = grad.rows // CHIPS_Y
-        (over,) = yield [hop(send, dy=1)]
-        block = (parts, 1, 1, rows, half)
-        index = lambda i, at: (0, i, flip(at[1]), 0, 0)
-        (send,) = combine(
-            at,
-            CHIPS_Z,
-            [[(keep, block, index), (over, block, index)]],
-            [
-                (
-                    (parts, CHIPS_Z, rows, half),
-                    (parts, 1, rows, half),
-                    lambda i, at: (0, i, 0, 0),
-                )
-            ],
-        )
-        (across,) = yield [hop(send, dx=1)]
-
-        def terms(k):
-            turn = lambda at: lax.rem(at[0] + k, CHIPS_Z)
-            index = lambda i, at: (0, turn(at), at[1], 0, 0)
-            return [
-                (keep, block, index),
-                (over, block, index),
-                (across, (parts, 1, rows, half), lambda i, at: (0, turn(at), 0, 0)),
-            ]
-
-    else:
-        rows = grad.rows
-        (across,) = yield [hop(send, dx=1)]
-        block = (parts, 1, rows, half)
-
-        def terms(k):
-            index = lambda i, at: (0, lax.rem(at[0] + k, CHIPS_Z), 0, 0)
-            return [(keep, block, index), (across, block, index)]
-
+    (over,) = yield [hop(send, dy=1)]
+    block = (parts, 1, 1, rows, half)
+    short = (parts, 1, rows, half)
+    index = lambda i, at: (0, i, flip(at[1]), 0, 0)
+    (send,) = combine(
+        at,
+        CHIPS_Z,
+        [[(keep, block, index), (over, block, index)]],
+        [((parts, CHIPS_Z, rows, half), short, lambda i, at: (0, i, 0, 0))],
+    )
+    (across,) = yield [hop(send, dx=1)]
+    turn = lambda at, k: lax.rem(at[0] + k, CHIPS_Z)
+    mine = lambda k: lambda i, at: (0, turn(at, k), at[1], 0, 0)
     piece = (parts, rows, half)
-    zeros = lambda i, at: (0, 0, 0)
-    whole = (piece, piece, zeros)
-    own, *sends = combine(at, 1, [terms(k) for k in range(CHIPS_Z)], [whole] * CHIPS_Z)
+    whole = (piece, piece, lambda i, at: (0, 0, 0))
+    own, *sends = pick_sum(
+        at,
+        whole,
+        [
+            (keep, block, mine),
+            (over, block, mine),
+            (across, short, lambda k: lambda i, at: (0, turn(at, k), 0, 0)),
+        ],
+        rows,
+        1,
+    )
     landed = yield [hop(send, dz=k) for k, send in zip(range(1, CHIPS_Z), sends)]
-    (own,) = combine(at, 1, [[(term, piece, zeros) for term in (own, *landed)]], [whole])
-    if y_first:
-        others = yield [hop(own, dy=1), hop(own, dc=1), hop(own, dy=1, dc=1)]
-        return [own, *others]
+    (own,) = combine(at, 1, [[(term, piece, whole[2]) for term in (own, *landed)]], [whole])
+    others = yield [hop(own, dy=1), hop(own, dc=1), hop(own, dy=1, dc=1)]
+    pieces = [item.reshape(parts * rows, half) for item in (own, *others)]
+    return {grad.number: (pieces, 0, rows)}
+
+
+def reduce_x_first(grads, place):
+    at = place.at
+    away = [grad.product(at, True) for grad in grads]
+    near = yield [hop(item, dc=1) for item in away]
+    total = sum(grad.parts * grad.rows for grad in grads)
+    starts, flat = [0], ()
+    for grad, item in zip(grads, near):
+        flat = grad.product(at, False, False, item, starts[-1], total, tuple(flat))
+        starts.append(starts[-1] + grad.parts * grad.rows)
+    send, keep = flat
+    (across,) = yield [hop(send, dx=1)]
+    steps = 3
+    tall = total // steps
+    ahead = lambda k: lambda i, at: (lax.rem(at[0] + k, CHIPS_Z), i, 0)
+    piece = ((total, UNIT), (tall, UNIT), lambda i, at: (i, 0))
+    own, *sends = pick_sum(
+        at, piece, [(item, (1, tall, UNIT), ahead) for item in (keep, across)], tall, steps
+    )
+    landed = yield [hop(send, dz=k) for k, send in zip(range(1, CHIPS_Z), sends)]
+    add = lambda *terms: combine(at, steps, [[(term, *piece[1:]) for term in terms]], [piece])[0]
+    own = add(own, *landed)
     (other,) = yield [hop(own, dy=1)]
-    (own,) = combine(at, 1, [[(own, piece, zeros), (other, piece, zeros)]], [whole])
+    own = add(own, other)
     (other,) = yield [hop(own, dc=1)]
-    return [own, other]
-
-
-def join_kernel(parts_outer, at_ref, *refs):
-    out_ref = refs[-1]
-    half = refs[0].shape[-1]
-    per_layer = (len(refs) - 1) // LAYERS
-    for number, ref in enumerate(refs[:-1]):
-        layer, place = divmod(number, per_layer)
-        core = lax.rem(at_ref[3] + place // (per_layer // CORES), CORES)
+    return {
+        grad.number: ([own, other], start, grad.rows) for grad, start in zip(grads, starts)
+    }
+
+
+def join_kernel(plan, count, at_ref, *refs):
+    for ref, out, layer, outer, parts, dc, dy, start, rows in plan:
+        ref, out_ref = refs[ref], refs[count + out]
+        half = ref.shape[1]
+        core = lax.rem(at_ref[3] + dc, CORES)
         row = 0
-        if per_layer > CORES:
-            row = lax.rem(at_ref[2] + place % CHIPS_Y, CHIPS_Y) * ref.shape[1]
-            row = pl.multiple_of(row, 16)
-        for part in range(ref.shape[0]):
-            column = part * CORES + core if parts_outer else core * ref.shape[0] + part
+        if dy is not None:
+            row = pl.multiple_of(lax.rem(at_ref[2] + dy, CHIPS_Y) * rows, 16)
+        for part in range(parts):
+            column = part * CORES + core if outer else core * parts + part
             column = pl.multiple_of(column * half, 128)
-            out_ref[layer, pl.ds(row, ref.shape[1]), pl.ds(column, half)] = ref[part].astype(
-                jnp.float32
-            )
-
-
-def join(at, layers, parts_outer):
-    pieces = [piece for layer in layers for piece in layer]
-    parts, rows, half = pieces[0].shape
-    tall = rows * (len(pieces) // LAYERS // CORES)
-    zeros = lambda i, at: (0, 0, 0)
-    shape = (LAYERS, tall, parts * CORES * half)
+            value = ref[start + part * rows : start + (part + 1) * rows]
+            out_ref[layer, pl.ds(row, rows), pl.ds(column, half)] = value.astype(jnp.float32)
+
+
+def join(at, done, shapes):
+    arrays, plan = [], []
+    for out, (number, (tall, wide)) in enumerate(shapes.items()):
+        for layer in range(LAYERS):
+            pieces, start, rows = done[layer][number]
+            for place, piece in enumerate(pieces):
+                known = [other is piece for other in arrays]
+                if not any(known):
+                    arrays.append(piece)
+                    known.append(True)
+                parts = wide // (CORES * piece.shape[1])
+                dy, dc = (place % CHIPS_Y, place // CHIPS_Y) if len(pieces) > CORES else (None, place)
+                plan.append((known.index(True), out, layer, number == 0, parts, dc, dy, start, rows))
+    zeros = lambda i, at: (0, 0)
+    outs = [(LAYERS, *shape) for shape in shapes.values()]
     return pl.pallas_call(
-        functools.partial(join_kernel, parts_outer),
+        functools.partial(join_kernel, plan, len(arrays)),
         grid_spec=pltpu.PrefetchScalarGridSpec(
             num_scalar_prefetch=1,
             grid=(1,),
-            in_specs=[pl.BlockSpec(piece.shape, zeros) for piece in pieces],
-            out_specs=pl.BlockSpec(shape, zeros),
+            in_specs=[pl.BlockSpec(array.shape, zeros) for array in arrays],
+            out_specs=[pl.BlockSpec(out, lambda i, at: (0, 0, 0)) for out in outs],
         ),
-        out_shape=jax.ShapeDtypeStruct(shape, jnp.float32),
+        out_shape=[jax.ShapeDtypeStruct(out, jnp.float32) for out in outs],
         compiler_params=kernel_params(),
         cost_estimate=pl.CostEstimate(flops=0, bytes_accessed=4_000_000, transcendentals=0),
-    )(at, *pieces)
+    )(at, *arrays)
 
 
 def reduce_total(total, place):
@@ -983,22 +1065,34 @@
         sizes = [weights[number].shape[1] for number in VECTORS]
         spread_out = []
 
+        blocks = {"first": first_block(weights, place)}
+
         def get(layer, number):
             if number not in VECTORS:
-                return flow.finish((layer, number))[0]
+                for name, (chunk_layer, numbers, _) in CHUNKS.items():
+                    if chunk_layer == layer and number in numbers:
+                        return flow.finish(name)[0][numbers.index(number)]
             if not spread_out:
-                spread_out.extend(spread_vectors(flow.finish((0, 0))[1], sizes, place))
+                spread_out.extend(spread_vectors(flow.finish("first")[1], sizes, place))
             return spread_out[VECTORS.index(number)][layer]
 
         def step(point, main):
             advanced, started = FORWARD.get(point, ((), ()))
             main = flow.tick(main, *advanced)
             for name in started:
-                flow.start(name, gather_chain(*gather_block(weights, *name, place), place))
+                _, numbers, split_y = CHUNKS[name]
+                layout = chunk_rows(weights, numbers, split_y)
+                if name == "first":
+                    layout = [(1, layout[0][1])]
+                flow.start(name, gather_chain(blocks[name], layout, split_y, place))
             return main
 
-        def reduce(layer, number, grad):
-            flow.start(("grad", layer, number), reduce_chain(grad, place, number in (0, 6)))
+        def reduce(layer, *grads):
+            name = ("grad", layer, grads[0].number)
+            if grads[0].number in (0, 6):
+                flow.start(name, reduce_y_first(*grads, place))
+            else:
+                flow.start(name, reduce_x_first(grads, place))
 
         def back_step(main, *held):
             return flow.tick(main, *[name for name in flow.running if name not in held])
@@ -1016,15 +1110,16 @@
         def step(point, main):
             return main
 
-        def reduce(layer, number, grad):
-            own, away = grad.rights
-            if not grad.cut:
-                own = jnp.concatenate([own, away], axis=2)
-                own = own.transpose(1, 0, 2).reshape(own.shape[1], -1)
-            total = contract_first(grad.left, own)
-            total = lax.psum_scatter(total, "shard", scatter_dimension=0, tiled=True)
-            total = lax.psum(total.astype(jnp.bfloat16), "rep").astype(jnp.float32)
-            flow.done[("grad", layer, number)] = total
+        def reduce(layer, *grads):
+            for grad in grads:
+                own, away = grad.rights
+                if not grad.cut:
+                    own = jnp.concatenate([own, away], axis=2)
+                    own = own.transpose(1, 0, 2).reshape(own.shape[1], -1)
+                total = contract_first(grad.left, own)
+                total = lax.psum_scatter(total, "shard", scatter_dimension=0, tiled=True)
+                total = lax.psum(total.astype(jnp.bfloat16), "rep").astype(jnp.float32)
+                flow.done[("grad", layer, grad.number)] = total
 
         def back_step(main, *held):
             return main
@@ -1033,17 +1128,25 @@
             flow.done[name] = lax.psum(total, AXES)
 
     step("begin", ())
+    if fast:
+        blocks.update(pack(weights, [name for name in CHUNKS if name != "first"], place))
+        segment, parent, clusters, blocks["rest"] = step(
+            "packed", (segment, parent, clusters, blocks["rest"])
+        )
     slots, bias = step("prepared", prepare(segment, parent, clusters))
-    hidden, hidden_low = step("ready", (inputs, inputs))
+    hidden, hidden_low = inputs, inputs
     saved = []
     for layer in range(LAYERS):
         pull = functools.partial(get, layer)
-        projected = project(hidden_low, pull(0), path_vectors(pull(1)))
-        projected = step((layer, "projected"), projected)
+        weight = pull(0)
+        if layer == 0:
+            weight = step("ready", weight)
+        projected = project(hidden_low, weight, path_vectors(pull(1)))
         first = attend(projected, slots, bias, 0, ())
         first = step((layer, "half"), first)
         context, *heads = attend(projected, slots, bias, 1, first)
         context = step((layer, "context"), context)
+        context = step((layer, "waited"), context)
         context, *wide = step((layer, "placed"), (context, pull(2), pull(6), pull(8)))
         entered = hidden_low
         middle, act, slope, *norms, hidden, hidden_low = feed(
@@ -1052,7 +1155,6 @@
             wide,
             [pull(number) for number in (3, 4, 5, 7, 9, 10, 11)],
         )
-        hidden_low = step((layer, "result"), hidden_low)
         saved.append((entered, heads, context, middle, act, slope, norms))
     result = hidden_low
     above, proj = cotangent, None
@@ -1072,22 +1174,29 @@
         sums[layer] = [row_sums, ffin_sum, None]
         down = back_step(down)
         wide = grad_pre.shape[1] // CORES
-        reduce(layer, 8, Grad(act, down, down, True, act.shape[1] // D, D // CORES))
-        reduce(layer, 6, Grad(middle, grad_pre, grad_pre, True, wide // D, D))
-        reduce(layer, 2, Grad(context, attn_low, attn_low, True, 1, D // CORES))
+        grad_8 = Grad(8, act, down, down, True, act.shape[1] // D, UNIT)
+        grad_2 = Grad(2, context, attn_low, attn_low, True, 1, UNIT)
+        if layer == 0:
+            reduce(layer, grad_8, grad_2)
+            reduce(layer, Grad(6, middle, grad_pre, grad_pre, True, wide // D, D))
+        else:
+            grad_6 = Grad(6, middle, grad_pre, grad_pre, True, wide // UNIT, UNIT)
+            reduce(layer, grad_8, grad_6, grad_2)
         if layer == 0:
             pieces = [qv_sum(sums[1][2])]
             for row_sums, ffin_sum, _ in sums:
                 pieces += [row_sums[:6].reshape(-1), ffin_sum[0]]
             add_up("early", jnp.concatenate(pieces))
-        grad_context = back_step(grad_context)
+        above_chain = () if layer else (("grad", 1, 8),)
+        grad_context = back_step(grad_context, *above_chain)
         away, away_sums = attend_back(grad_context, slots, heads, at, True)
-        grad_context, away = back_step((grad_context, away))
+        wide_chains = (("grad", layer, 8), ("grad", layer, 6))
+        grad_context, away = back_step((grad_context, away), *above_chain, *wide_chains)
         own, own_sums = attend_back(grad_context, slots, heads, at, False)
         proj = (own, away)
-        reduce(layer, 0, Grad(entered, own, away, False, 3, D // CORES))
+        reduce(layer, Grad(0, entered, own, away, False, 3, UNIT))
         sums[layer][2] = (own_sums, away_sums, at)
-        proj = back_step(proj, ("grad", layer, 8))
+        proj = back_step(proj, *(wide_chains if layer else ()))
         above = grad_attn
     add_up("late", qv_sum(sums[0][2]))
     grad_input = input_grad(above, proj, get(0, 0), at)
@@ -1107,9 +1216,17 @@
     grads = {1: share(jnp.stack([late, early[: 2 * D]])), 7: share(rest[:, 6 * D :])}
     for number, row in ((10, 0), (11, 1), (9, 2), (4, 3), (5, 4), (3, 5)):
         grads[number] = share(rest[:, row * D : (row + 1) * D])
-    for number in (8, 6, 2, 0):
-        done = [flow.finish(("grad", layer, number)) for layer in range(LAYERS)]
-        grads[number] = join(at, done, number == 0) if fast else jnp.stack(done)
+    if fast:
+        done = [{}, {}]
+        for name, value in flow.done.items():
+            if name[0] == "grad":
+                done[name[1]].update(value)
+        for numbers in ((8, 6, 2), (0,)):
+            shapes = {number: weights[number].shape[1:] for number in numbers}
+            grads.update(zip(numbers, join(at, done, shapes)))
+    else:
+        for number in MATRICES:
+            grads[number] = jnp.stack([flow.done[("grad", layer, number)] for layer in range(LAYERS)])
     return (result, grad_input, *[grads[number] for number in range(12)])
 
 

time: 841 us -> 785 us (0.933)
  starting transfers between devices: 152 us -> 88.9 us
  waiting for transfers between devices: 93.2 us -> 148 us
  Pallas kernels: 528 us -> 502 us
  local copies, waits for them, and re-layouts: 36.7 us -> 26.8 us
    ppermute x132 -> x84, starting transfers between devices: 152 us -> 88.9 us  [hop(): return lax.ppermute(value, AXES, pairs)]
    ppermute x132 -> x84, waiting for transfers between devices: 93.2 us -> 148 us  [hop(): return lax.ppermute(value, AXES, pairs)]
    pallas_call x24 -> x15, Pallas kernels: 69.5 us -> 53.4 us  [combine(): pl.pallas_call(functools.partial(combine_kernel, [len(group) for group in...]
    pallas_call x12 -> x7, Pallas kernels: 54.9 us -> 40.8 us  [the longest x4 28.6 us: place_pieces(): pl.pallas_call(functools.partial(place_kernel, layout, split_y, len(piece...]
  transfers between devices with their start and end apart: 132 -> 84, of which waited for: 21 -> 26; matrix products, arithmetic and copies ran while one was open for 5% -> 3% of each run, Pallas kernels for 53% -> 51%
where the time goes in v5:
time: 785 us; the launch traced here: 775 us
  Pallas kernels  502 us (64%)
  waiting for transfers between devices  148 us (19%)
  starting transfers between devices  88.9 us (11%)
  local copies, waits for them, and re-layouts  26.8 us (3%)
  other arithmetic  7.96 us (1%)
    ppermute x84, waiting for transfers between devices, hop(): return lax.ppermute(value, AXES, pairs)  148 us
    pallas_call x16, Pallas kernels, product(): pl.pallas_call(functools.partial(weight_grad_kernel, split_y), grid_spec=...  107 us
    ppermute x84, starting transfers between devices, hop(): return lax.ppermute(value, AXES, pairs)  88.9 us
    pallas_call x4, Pallas kernels, attend_back(): pl.pallas_call(attend_back_kernel, grid_spec=pltpu.PrefetchScalarGridSpec...  75 us
    pallas_call x4, Pallas kernels, attend(): pl.pallas_call(attend_kernel, grid=(trees, PAIRS // 2), in_specs=[slot_sp...  71.1 us
    pallas_call x2, Pallas kernels, feed(): pl.pallas_call(feed_kernel, grid=(count // ROW_TILE,), in_specs=[row_spec...  55.8 us
    pallas_call x2, Pallas kernels, feed_back(): pl.pallas_call(functools.partial(feed_back_kernel, proj is not None), gri...  53.8 us
    pallas_call x15, Pallas kernels, combine(): pl.pallas_call(functools.partial(combine_kernel, [len(group) for group in...  53.4 us
  transfers between devices with their start and end apart: 84, of which 26 were waited for; matrix products, arithmetic and copies ran while one was open for 3% of the time, Pallas kernels for 51%

profile of v5, /device:TPU:17, one launch (start us, length us, event | category | flops | bytes accessed | tf_op | source)
XLA Modules:
  0.0 774.6 jit_solution(12662735165474941003)
XLA Ops:
  5.9 3.9 shard_map.272
  14.4 6.6 collective-permute-done.1
  21.1 19.5 %collective-permute-done.2 = bf16[112,1152]{1,0:T(8,128)(2,1)S(1)} collective-permute-done((bf16[112,1152]{1,0:T(8,128)(2,1)S(1)}, bf16[112,1152]{1,0:T(8,128)(2,1)S(1)}, u32[]{:S(2)}, u32[]{:S(2)}) %collective-permute-start.2) | collective-permute-done | bytes 258080 | tf_op jit(solution)/shard_map/ppermute | solution.py:750
  43.5 19.1 %shard_map.273 = (s32[1,6,2,1024]{3,2,1,0:T(2,128)}, bf16[1,12,1024,128]{3,2,1,0:T(8,128)(2,1)}) custom-call(s32[1,13]{1,0:T(1,128)} %parent_ref, s32[1,1,1024]{2,1,0:T(1,128)} %bitcast.132, s32[1,6,2,1024]{3,2,1,0:T(2,128)} %transpose_reshape.3.cluster_ref), custom_call_target="tpu_custom_call" | custom-call | flops 20000000000 | bytes 4000000 | tf_op jit(solution)/shard_map/pallas_call | solution.py:574
  70.8 5.3 shard_map.274
  80.7 7.8 %shard_map.275.query_ref.key_ref.value_ref = bf16[1024,2304]{1,0:T(8,128)(2,1)} custom-call(bf16[1024,768]{1,0:T(8,128)(2,1)} %left_ref.3, bf16[768,2304]{1,0:T(8,128)(2,1)} %bitcast.81, f32[1,2304]{1,0:T(1,128)} %broadcast_in_dim.4.bias_ref), custom_call_target="tpu_custom_call" | custom-call | flops 4348654592 | bytes 5111808 | tf_op jit(solution)/shard_map/pallas_call | solution.py:458
  88.5 17.7 %shard_map.276 = (bf16[1024,768]{1,0:T(8,128)(2,1)}, bf16[1,12,1024,128]{3,2,1,0:T(8,128)(2,1)}, bf16[1,12,1024,128]{3,2,1,0:T(8,128)(2,1)}, bf16[1,12,1024,128]{3,2,1,0:T(8,128)(2,1)}) custom-call(s32[1,6,2,1024]{3,2,1,0:T(2,128)} %get-tuple-element.243.slot_ref, bf16[1024,2304]{1,0:T(8,128)(2,1)} %shard_map.275.query_ref.key_ref.value_ref, ...), custom_call_target="tpu_custom_call" | custom-call | flops 15000000512 | bytes 10000000 | tf_op jit(solution)/shard_map/pallas_call | solution.py:158
  114.0 17.7 %shard_map.277 = (bf16[1024,768]{1,0:T(8,128)(2,1)}, bf16[1,12,1024,128]{3,2,1,0:T(8,128)(2,1)}, bf16[1,12,1024,128]{3,2,1,0:T(8,128)(2,1)}, bf16[1,12,1024,128]{3,2,1,0:T(8,128)(2,1)}) custom-call(s32[1,6,2,1024]{3,2,1,0:T(2,128)} %get-tuple-element.243.slot_ref, ...), custom_call_target="tpu_custom_call", output_to_operand_aliasing={{0}: (5, {}), {1}: (6, {}), {2}: (7, {}), {3}: (8, {})} | custom-call | flops 15000000512 | bytes 10000000 | tf_op jit(solution)/shard_map/pallas_call | solution.py:158
  131.7 8.8 %collective-permute-done.13.refs_2_ = bf16[4,384,384]{2,1,0:T(8,128)(2,1)} collective-permute-done((bf16[4,384,384]{2,1,0:T(8,128)(2,1)S(1)}, bf16[4,384,384]{2,1,0:T(8,128)(2,1)}, u32[]{:S(2)}, u32[]{:S(2)}) %collective-permute-start.13) | collective-permute-done | bytes 1179680 | tf_op jit(solution)/shard_map/ppermute | solution.py:750
  159.8 5.8 shard_map.280
  165.6 9.2 %shard_map.278 = (bf16[8,2,48,768]{3,2,1,0:T(8,128)(2,1)}, bf16[8,2,48,3072]{3,2,1,0:T(8,128)(2,1)}, bf16[8,2,192,768]{3,2,1,0:T(8,128)(2,1)}) custom-call(s32[4]{0:T(128)} %pad_add_fusion.at_ref.refs_1_, bf16[4,432,384]{2,1,0:T(8,128)(2,1)} %copy-done.9, bf16[4,432,384]{2,1,0:T(8,128)(2,1)} %collective-permute-done.16.refs_1_, ...), custom_call_target="tpu_custom_call" | custom-call | bytes 21233664 | tf_op jit(solution)/shard_map/pallas_call | solution.py:817
  174.7 12.6 %collective-permute-done.21 = bf16[768,384]{1,0:T(8,128)(2,1)S(1)} collective-permute-done((bf16[768,384]{1,0:T(8,128)(2,1)}, bf16[768,384]{1,0:T(8,128)(2,1)S(1)}, u32[]{:S(2)}, u32[]{:S(2)}) %collective-permute-start.21) | collective-permute-done | bytes 589856 | tf_op jit(solution)/shard_map/ppermute | solution.py:750
  187.3 12.6 %collective-permute-done.22 = bf16[768,384]{1,0:T(8,128)(2,1)S(1)} collective-permute-done((bf16[768,384]{1,0:T(8,128)(2,1)}, bf16[768,384]{1,0:T(8,128)(2,1)S(1)}, u32[]{:S(2)}, u32[]{:S(2)}) %collective-permute-start.22) | collective-permute-done | bytes 589856 | tf_op jit(solution)/shard_map/ppermute | solution.py:750
  204.4 27.9 %shard_map.279 = (bf16[1024,768]{1,0:T(8,128)(2,1)}, bf16[1024,3072]{1,0:T(8,128)(2,1)}, bf16[1024,3072]{1,0:T(8,128)(2,1)}, f32[1024,768]{1,0:T(8,128)}, f32[10...) custom-call(bf16[1024,768]{1,0:T(8,128)(2,1)} %get-tuple-element.272, ...), custom_call_target="tpu_custom_call" | custom-call | flops 27179089920 | bytes 12189696 | tf_op jit(solution)/shard_map/pallas_call | solution.py:474
  232.4 7.8 %shard_map.281.query_ref.key_ref.value_ref = bf16[1024,2304]{1,0:T(8,128)(2,1)} custom-call(bf16[1024,768]{1,0:T(8,128)(2,1)} %get-tuple-element.276.rows_ref.left_ref, bf16[768,2304]{1,0:T(8,128)(2,1)} %bitcast.126, f32[1,2304]{1,0:T(1,128)} %broadcast_in_dim.5.bias_ref), custom_call_target="tpu_custom_call" | custom-call | flops 4348654592 | bytes 5111808 | tf_op jit(solution)/shard_map/pallas_call | solution.py:458
  240.2 17.9 %shard_map.282 = (bf16[1024,768]{1,0:T(8,128)(2,1)}, bf16[1,12,1024,128]{3,2,1,0:T(8,128)(2,1)}, bf16[1,12,1024,128]{3,2,1,0:T(8,128)(2,1)}, bf16[1,12,1024,128]{3,2,1,0:T(8,128)(2,1)}) custom-call(s32[1,6,2,1024]{3,2,1,0:T(2,128)} %get-tuple-element.243.slot_ref, bf16[1024,2304]{1,0:T(8,128)(2,1)} %shard_map.281.query_ref.key_ref.value_ref, ...), custom_call_target="tpu_custom_call" | custom-call | flops 15000000512 | bytes 10000000 | tf_op jit(solution)/shard_map/pallas_call | solution.py:158
  262.2 17.7 %shard_map.283 = (bf16[1024,768]{1,0:T(8,128)(2,1)}, bf16[1,12,1024,128]{3,2,1,0:T(8,128)(2,1)}, bf16[1,12,1024,128]{3,2,1,0:T(8,128)(2,1)}, bf16[1,12,1024,128]{3,2,1,0:T(8,128)(2,1)}) custom-call(s32[1,6,2,1024]{3,2,1,0:T(2,128)} %get-tuple-element.243.slot_ref, ...), custom_call_target="tpu_custom_call", output_to_operand_aliasing={{0}: (5, {}), {1}: (6, {}), {2}: (7, {}), {3}: (8, {})} | custom-call | flops 15000000512 | bytes 10000000 | tf_op jit(solution)/shard_map/pallas_call | solution.py:158
  280.0 8.4 %shard_map.284 = (bf16[8,1,96,3072]{3,2,1,0:T(8,128)(2,1)}, bf16[8,1,384,768]{3,2,1,0:T(8,128)(2,1)}) custom-call(s32[4]{0:T(128)} %pad_add_fusion.at_ref.refs_1_, bf16[4,768,384]{2,1,0:T(8,128)(2,1)} %copy-done.6, bf16[4,768,384]{2,1,0:T(8,128)(2,1)} %collective-permute-done.26.refs_1_, bf16[4,768,384]{2,1,0:T(8,128)(2,1)} %collective-permute-done.25.refs_2_, ...), custom_call_target="tpu_custom_call" | custom-call | bytes 18874368 | tf_op jit(solution)/shard_map/pallas_call | solution.py:817
  288.3 27.9 %shard_map.285 = (bf16[1024,768]{1,0:T(8,128)(2,1)}, bf16[1024,3072]{1,0:T(8,128)(2,1)}, bf16[1024,3072]{1,0:T(8,128)(2,1)}, f32[1024,768]{1,0:T(8,128)}, f32[10...) custom-call(bf16[1024,768]{1,0:T(8,128)(2,1)} %get-tuple-element.295, ...), custom_call_target="tpu_custom_call" | custom-call | flops 27179089920 | bytes 12189696 | tf_op jit(solution)/shard_map/pallas_call | solution.py:474
  316.3 22.2 %shard_map.286 = (bf16[1024,768]{1,0:T(8,128)(2,1)}, bf16[1024,3072]{1,0:T(8,128)(2,1)}, f32[1024,768]{1,0:T(8,128)}, bf16[1024,768]{1,0:T(8,128)(2,1)}, bf16[10...) custom-call(bf16[1024,768]{1,0:T(8,128)(2,1)} %refs_0_.3, f32[1024,768]{1,0:T(8,128)} %get-tuple-element.301.refs_1_, ...), custom_call_target="tpu_custom_call" | custom-call | flops 27179089920 | bytes 12189696 | tf_op jit(solution)/shard_map/pallas_call | solution.py:521
  338.5 7.6 shard_map.288
  346.6 7.9 %shard_map.287 = bf16[1,4,2,384,384]{4,3,2,1,0:T(8,128)(2,1)} custom-call(s32[4]{0:T(128)} %pad_add_fusion.at_ref.refs_1_, bf16[1024,3072]{1,0:T(8,128)(2,1)} %get-tuple-element.308.left_ref, bf16[1024,768]{1,0:T(8,128)(2,1)} %get-tuple-element.309.right_ref), custom_call_target="tpu_custom_call" | custom-call | flops 4831838208 | bytes 7864320 | tf_op jit(solution)/shard_map/pallas_call | solution.py:665
  354.5 4.1 shard_map.289
  361.0 18.9 %shard_map.290 = (bf16[3,1024,384]{2,1,0:T(8,128)(2,1)}, f32[1,3,8,128]{3,2,1,0:T(8,128)}) custom-call(s32[4]{0:T(128)} %pad_add_fusion.at_ref.refs_1_, s32[1,6,2,1024]{3,2,1,0:T(2,128)} %get-tuple-element.243.slot_ref, bf16[1024,768]{1,0:T(8,128)(2,1)} %get-tuple-element.318.grad_ref, bf16[1,12,1024,128]{3,2,1,0:T(8,128)(2,1)} %get-tuple-element.314.qk_ref, ...), custom_call_target="tpu_custom_call" | custom-call | flops 16999999488 | bytes 10000000 | tf_op jit(solution)/shard_map/pallas_call | solution.py:195
  379.9 6.5 shard_map.292
  386.8 8.6 %shard_map.295 = (bf16[4,864,384]{2,1,0:T(8,128)(2,1)}, bf16[4,864,384]{2,1,0:T(8,128)(2,1)}) custom-call(s32[4]{0:T(128)} %pad_add_fusion.at_ref.refs_1_, bf16[1024,3072]{1,0:T(8,128)(2,1)} %get-tuple-element.308.left_ref, bf16[1024,768]{1,0:T(8,128)(2,1)} %get-tuple-element.309.right_ref, bf16[1,4,2,384,384]{4,3,2,1,0:T(8,128)(2,1)} %collective-permute-done.28.refs_0_), custom_call_target="tpu_custom_call" | custom-call | flops 4831838208 | bytes 7864320 | tf_op jit(solution)/shard_map/pallas_call | solution.py:665
  395.3 8.2 %shard_map.296 = (bf16[4,864,384]{2,1,0:T(8,128)(2,1)}, bf16[4,864,384]{2,1,0:T(8,128)(2,1)}) custom-call(s32[4]{0:T(128)} %pad_add_fusion.at_ref.refs_1_, bf16[1024,768]{1,0:T(8,128)(2,1)} %get-tuple-element.310.left_ref, bf16[1024,3072]{1,0:T(8,128)(2,1)} %get-tuple-element.311.right_ref, ...), custom_call_target="tpu_custom_call", output_to_operand_aliasing={{0}: (4, {}), {1}: (5, {})} | custom-call | flops 4831838208 | bytes 7864320 | tf_op jit(solution)/shard_map/pallas_call | solution.py:665
  403.6 4.3 shard_map.297
  408.2 18.6 %shard_map.291 = (bf16[3,1024,384]{2,1,0:T(8,128)(2,1)}, f32[1,3,8,128]{3,2,1,0:T(8,128)}) custom-call(s32[4]{0:T(128)} %pad_add_fusion.at_ref.refs_1_, s32[1,6,2,1024]{3,2,1,0:T(2,128)} %get-tuple-element.243.slot_ref, bf16[1024,768]{1,0:T(8,128)(2,1)} %get-tuple-element.318.grad_ref, bf16[1,12,1024,128]{3,2,1,0:T(8,128)(2,1)} %get-tuple-element.314.qk_ref, ...), custom_call_target="tpu_custom_call" | custom-call | flops 16999999488 | bytes 10000000 | tf_op jit(solution)/shard_map/pallas_call | solution.py:195
  426.8 6.9 shard_map.294
  434.0 31.5 %shard_map.293 = (bf16[1024,768]{1,0:T(8,128)(2,1)}, bf16[1024,3072]{1,0:T(8,128)(2,1)}, f32[1024,768]{1,0:T(8,128)}, bf16[1024,768]{1,0:T(8,128)(2,1)}, bf16[10...) custom-call(f32[1024,768]{1,0:T(8,128)} %get-tuple-element.306.refs_0_, s32[4]{0:T(128)} %pad_add_fusion.at_ref.refs_1_, ...), custom_call_target="tpu_custom_call" | custom-call | flops 27179089920 | bytes 13762560 | tf_op jit(solution)/shard_map/pallas_call | solution.py:521
  465.5 6.5 shard_map.301
  472.8 8.4 %shard_map.299 = bf16[1,4,2,384,384]{4,3,2,1,0:T(8,128)(2,1)} custom-call(s32[4]{0:T(128)} %pad_add_fusion.at_ref.refs_1_, bf16[1024,3072]{1,0:T(8,128)(2,1)} %get-tuple-element.343.left_ref, bf16[1024,768]{1,0:T(8,128)(2,1)} %get-tuple-element.344.right_ref), custom_call_target="tpu_custom_call" | custom-call | flops 4831838208 | bytes 7864320 | tf_op jit(solution)/shard_map/pallas_call | solution.py:665
  481.4 4.2 shard_map.300
  486.2 4.0 shard_map.298
  491.8 5.5 shard_map.305
  497.4 4.7 collective-permute-done.34.refs_2_.refs_5_.refs_8_.refs_11_
  509.6 18.9 %shard_map.302 = (bf16[3,1024,384]{2,1,0:T(8,128)(2,1)}, f32[1,3,8,128]{3,2,1,0:T(8,128)}) custom-call(s32[4]{0:T(128)} %pad_add_fusion.at_ref.refs_1_, s32[1,6,2,1024]{3,2,1,0:T(2,128)} %get-tuple-element.243.slot_ref, bf16[1024,768]{1,0:T(8,128)(2,1)} %get-tuple-element.364.grad_ref, bf16[1,12,1024,128]{3,2,1,0:T(8,128)(2,1)} %get-tuple-element.355.qk_ref, ...), custom_call_target="tpu_custom_call" | custom-call | flops 16999999488 | bytes 10000000 | tf_op jit(solution)/shard_map/pallas_call | solution.py:195
  528.5 7.1 shard_map.308
  538.4 7.0 shard_map.310
  548.0 8.4 %shard_map.306 = (bf16[4,480,384]{2,1,0:T(8,128)(2,1)}, bf16[4,480,384]{2,1,0:T(8,128)(2,1)}) custom-call(s32[4]{0:T(128)} %pad_add_fusion.at_ref.refs_1_, bf16[1024,3072]{1,0:T(8,128)(2,1)} %get-tuple-element.343.left_ref, bf16[1024,768]{1,0:T(8,128)(2,1)} %get-tuple-element.344.right_ref, bf16[1,4,2,384,384]{4,3,2,1,0:T(8,128)(2,1)} %collective-permute-done.35.refs_0_), custom_call_target="tpu_custom_call" | custom-call | flops 4831838208 | bytes 7864320 | tf_op jit(solution)/shard_map/pallas_call | solution.py:665
  561.0 4.5 shard_map.307
  566.7 13.4 %collective-permute-done.45.refs_3_ = bf16[864,384]{1,0:T(8,128)(2,1)S(1)} collective-permute-done((bf16[864,384]{1,0:T(8,128)(2,1)S(1)}, bf16[864,384]{1,0:T(8,128)(2,1)S(1)}, u32[]{:S(2)}, u32[]{:S(2)}) %collective-permute-start.45) | collective-permute-done | bytes 663584 | tf_op jit(solution)/shard_map/ppermute | solution.py:750
  583.6 18.6 %shard_map.304 = (bf16[3,1024,384]{2,1,0:T(8,128)(2,1)}, f32[1,3,8,128]{3,2,1,0:T(8,128)}) custom-call(s32[4]{0:T(128)} %pad_add_fusion.at_ref.refs_1_, s32[1,6,2,1024]{3,2,1,0:T(2,128)} %get-tuple-element.243.slot_ref, bf16[1024,768]{1,0:T(8,128)(2,1)} %get-tuple-element.364.grad_ref, bf16[1,12,1024,128]{3,2,1,0:T(8,128)(2,1)} %get-tuple-element.355.qk_ref, ...), custom_call_target="tpu_custom_call" | custom-call | flops 16999999488 | bytes 10000000 | tf_op jit(solution)/shard_map/pallas_call | solution.py:195
  602.3 12.3 %collective-permute-done.46.refs_1_.refs_3_.refs_5_.refs_7_ = bf16[4,480,384]{2,1,0:T(8,128)(2,1)S(1)} collective-permute-done((bf16[4,480,384]{2,1,0:T(8,128)(2,1)}, bf16[4,480,384]{2,1,0:T(8,128)(2,1)S(1)}, u32[]{:S(2)}, u32[]{:S(2)}) %collective-permute-start.46) | collective-permute-done | bytes 1474592 | tf_op jit(solution)/shard_map/ppermute | solution.py:750
  614.6 7.0 shard_map.315
  622.3 4.6 shard_map.313
  626.9 3.6 collective-permute-start.54
  630.5 4.2 shard_map.312.refs_0_
  635.4 4.1 shard_map.314
  644.5 4.5 collective-permute-done.58
  650.6 9.7 %shard_map.311 = f32[1024,768]{1,0:T(8,128)} custom-call(f32[1024,768]{1,0:T(8,128)} %get-tuple-element.328.above_ref, s32[4]{0:T(128)} %pad_add_fusion.at_ref.refs_1_, bf16[3,1024,384]{2,1,0:T(8,128)(2,1)} %get-tuple-element.384.own_ref.right_ref, bf16[3,1024,384]{2,1,0:T(8,128)(2,1)} %get-tuple-element.385.right_ref.away_ref, bf16[768,2304]{1,0:T(8,128)(2,1)} %bitcast.82), custom_call_target="tpu_custom_call" | custom-call | flops 4348654592 | bytes 6684672 | tf_op jit(solution)/shard_map/pallas_call | solution.py:553
  660.3 5.1 collective-permute-done.55.refs_2_
  665.4 7.8 %collective-permute-done.56.refs_3_ = bf16[480,384]{1,0:T(8,128)(2,1)S(1)} collective-permute-done((bf16[480,384]{1,0:T(8,128)(2,1)S(1)}, bf16[480,384]{1,0:T(8,128)(2,1)S(1)}, u32[]{:S(2)}, u32[]{:S(2)}) %collective-permute-start.56) | collective-permute-done | bytes 368672 | tf_op jit(solution)/shard_map/ppermute | solution.py:750
  674.0 3.7 shard_map.316.refs_2_
  678.2 4.0 shard_map.319
  688.9 3.7 shard_map.317.refs_0_
  694.1 8.5 %collective-permute-done.69 = f32[1536]{0:T(1024)S(1)} collective-permute-done((f32[1536]{0:T(1024)S(1)}, f32[1536]{0:T(1024)S(1)}, u32[]{:S(2)}, u32[]{:S(2)}) %collective-permute-start.69) | collective-permute-done | bytes 6176 | tf_op jit(solution)/shard_map/ppermute | solution.py:750
  714.8 4.0 collective-permute-done.65.refs_3_
  732.7 3.4 shard_map.320.refs_0_
  740.4 4.5 collective-permute-done.75.refs_2_
  745.5 3.7 collective-permute-done.76.refs_3_
  761.2 3.5 collective-permute-start.82
  765.4 5.1 shard_map.325
  (381 shorter events, 154.8 us)
Async XLA Ops:
  2.7 9.8 %collective-permute-start = (bf16[112,1152]{1,0:T(8,128)(2,1)S(1)}, bf16[112,1152]{1,0:T(8,128)(2,1)S(1)}, u32[]{:S(2)}, u32[]{:S(2)}) collective-permute-start(bf16[112,1152]{1,0:T(8,128)(2,1)S(1)} %get-tuple-element.475), channel_id=1, source_target_pairs={{0,2},{1,3},{2,4},{3,5},{4,6},{5,7},{6,0},{7,1},{8,10},{9,11},{10,... | collective-permute-start | bytes 774152 | tf_op jit(solution)/shard_map/ppermute | solution.py:750
  4.0 17.0 %collective-permute-start.1 = (bf16[112,1152]{1,0:T(8,128)(2,1)S(1)}, bf16[112,1152]{1,0:T(8,128)(2,1)S(1)}, u32[]{:S(2)}, u32[]{:S(2)}) collective-permute-start(bf16[112,1152]{1,0:T(8,128)(2,1)S(1)} %get-tuple-element.475), channel_id=1, source_target_pairs={{0,4},{1,5},{2,6},{3,7},{4,0},{5,1},{6,2},{7,3},{8,12},{9,13},{10,... | collective-permute-start | bytes 774152 | tf_op jit(solution)/shard_map/ppermute | solution.py:750
  4.1 36.5 %collective-permute-start.2 = (bf16[112,1152]{1,0:T(8,128)(2,1)S(1)}, bf16[112,1152]{1,0:T(8,128)(2,1)S(1)}, u32[]{:S(2)}, u32[]{:S(2)}) collective-permute-start(bf16[112,1152]{1,0:T(8,128)(2,1)S(1)} %get-tuple-element.475), channel_id=1, source_target_pairs={{0,6},{1,7},{2,0},{3,1},{4,2},{5,3},{6,4},{7,5},{8,14},{9,15},{10,... | collective-permute-start | bytes 774152 | tf_op jit(solution)/shard_map/ppermute | solution.py:750
  9.8 66.3 %collective-permute-start.6 = (bf16[432,384]{1,0:T(8,128)(2,1)}, bf16[432,384]{1,0:T(8,128)(2,1)}, u32[]{:S(2)}, u32[]{:S(2)}) collective-permute-start(bf16[432,384]{1,0:T(8,128)(2,1)} %get-tuple-element.234), channel_id=1, source_target_pairs={{0,2},{1,3},{2,4},{3,5},{4,6},{5,7},{6,0},{7,1},{8,10},{9,11},{10,... | collective-permute-start | bytes 995336 | tf_op jit(solution)/shard_map/ppermute | solution.py:750
  10.0 66.6 %collective-permute-start.7 = (bf16[432,384]{1,0:T(8,128)(2,1)}, bf16[432,384]{1,0:T(8,128)(2,1)}, u32[]{:S(2)}, u32[]{:S(2)}) collective-permute-start(bf16[432,384]{1,0:T(8,128)(2,1)} %get-tuple-element.234), channel_id=1, source_target_pairs={{0,4},{1,5},{2,6},{3,7},{4,0},{5,1},{6,2},{7,3},{8,12},{9,13},{10,... | collective-permute-start | bytes 995336 | tf_op jit(solution)/shard_map/ppermute | solution.py:750
  12.4 64.2 %collective-permute-start.8 = (bf16[432,384]{1,0:T(8,128)(2,1)}, bf16[432,384]{1,0:T(8,128)(2,1)}, u32[]{:S(2)}, u32[]{:S(2)}) collective-permute-start(bf16[432,384]{1,0:T(8,128)(2,1)} %get-tuple-element.234), channel_id=1, source_target_pairs={{0,6},{1,7},{2,0},{3,1},{4,2},{5,3},{6,4},{7,5},{8,14},{9,15},{10,... | collective-permute-start | bytes 995336 | tf_op jit(solution)/shard_map/ppermute | solution.py:750
  40.7 23.8 %collective-permute-start.3 = (bf16[4,112,1152]{2,1,0:T(8,128)(2,1)S(1)}, bf16[4,112,1152]{2,1,0:T(8,128)(2,1)S(1)}, u32[]{:S(2)}, u32[]{:S(2)}) collective-permute-start(bf16[4,112,1152]{2,1,0:T(8,128)(2,1)S(1)} %pad_maximum_fusion.3.refs_0_), channel_id=1, source_target_pairs={{0,1},{1,0},{2,3},{3,2},{4,5},{5,4},{6,7},{7,6},{8,9},{9,8},{10,11... | collective-permute-start | bytes 3096584 | tf_op jit(solution)/shard_map/ppermute | solution.py:750
  42.0 25.4 %collective-permute-start.4 = (bf16[4,112,1152]{2,1,0:T(8,128)(2,1)S(1)}, bf16[4,112,1152]{2,1,0:T(8,128)(2,1)S(1)}, u32[]{:S(2)}, u32[]{:S(2)}) collective-permute-start(bf16[4,112,1152]{2,1,0:T(8,128)(2,1)S(1)} %pad_maximum_fusion.3.refs_0_), channel_id=1, source_target_pairs={{0,8},{1,9},{2,10},{3,11},{4,12},{5,13},{6,14},{7,15},{8,0},{9,1},... | collective-permute-start | bytes 3096584 | tf_op jit(solution)/shard_map/ppermute | solution.py:750
  67.4 38.8 %collective-permute-start.10 = (bf16[384,384]{1,0:T(8,128)(2,1)}, bf16[384,384]{1,0:T(8,128)(2,1)}, u32[]{:S(2)}, u32[]{:S(2)}) collective-permute-start(bf16[384,384]{1,0:T(8,128)(2,1)} %get-tuple-element.254), channel_id=1, source_target_pairs={{0,2},{1,3},{2,4},{3,5},{4,6},{5,7},{6,0},{7,1},{8,10},{9,11},{10,... | collective-permute-start | bytes 884744 | tf_op jit(solution)/shard_map/ppermute | solution.py:750
  68.4 39.0 %collective-permute-start.11 = (bf16[384,384]{1,0:T(8,128)(2,1)}, bf16[384,384]{1,0:T(8,128)(2,1)}, u32[]{:S(2)}, u32[]{:S(2)}) collective-permute-start(bf16[384,384]{1,0:T(8,128)(2,1)} %get-tuple-element.254), channel_id=1, source_target_pairs={{0,4},{1,5},{2,6},{3,7},{4,0},{5,1},{6,2},{7,3},{8,12},{9,13},{10,... | collective-permute-start | bytes 884744 | tf_op jit(solution)/shard_map/ppermute | solution.py:750
  76.1 31.3 %collective-permute-start.12 = (bf16[384,384]{1,0:T(8,128)(2,1)}, bf16[384,384]{1,0:T(8,128)(2,1)S(1)}, u32[]{:S(2)}, u32[]{:S(2)}) collective-permute-start(bf16[384,384]{1,0:T(8,128)(2,1)} %get-tuple-element.254), channel_id=1, source_target_pairs={{0,6},{1,7},{2,0},{3,1},{4,2},{5,3},{6,4},{7,5},{8,14},{9,15},{10,... | collective-permute-start | bytes 884744 | tf_op jit(solution)/shard_map/ppermute | solution.py:750
  78.1 30.3 %collective-permute-start.9 = (bf16[4,432,384]{2,1,0:T(8,128)(2,1)S(1)}, bf16[4,432,384]{2,1,0:T(8,128)(2,1)S(1)}, u32[]{:S(2)}, u32[]{:S(2)}) collective-permute-start(bf16[4,432,384]{2,1,0:T(8,128)(2,1)S(1)} %pad_maximum_fusion.1.refs_0_), channel_id=1, source_target_pairs={{0,1},{1,0},{2,3},{3,2},{4,5},{5,4},{6,7},{7,6},{8,9},{9,8},{10,11... | collective-permute-start | bytes 3981320 | tf_op jit(solution)/shard_map/ppermute | solution.py:750
  79.4 61.8 %collective-permute-start.14 = (bf16[4,432,384]{2,1,0:T(8,128)(2,1)S(1)}, bf16[4,432,384]{2,1,0:T(8,128)(2,1)}, u32[]{:S(2)}, u32[]{:S(2)}) collective-permute-start(bf16[4,432,384]{2,1,0:T(8,128)(2,1)S(1)} %pad_maximum_fusion.1.refs_0_), channel_id=1, source_target_pairs={{0,16},{1,17},{2,18},{3,19},{4,20},{5,21},{6,22},{7,23},{8,24},{9,... | collective-permute-start | bytes 3981320 | tf_op jit(solution)/shard_map/ppermute | solution.py:750
  106.2 35.6 %collective-permute-start.16 = (bf16[4,432,384]{2,1,0:T(8,128)(2,1)S(1)}, bf16[4,432,384]{2,1,0:T(8,128)(2,1)}, u32[]{:S(2)}, u32[]{:S(2)}) collective-permute-start(bf16[4,432,384]{2,1,0:T(8,128)(2,1)S(1)} %pad_maximum_fusion.1.refs_0_), channel_id=1, source_target_pairs={{0,8},{1,9},{2,10},{3,11},{4,12},{5,13},{6,14},{7,15},{8,0},{9,1},... | collective-permute-start | bytes 3981320 | tf_op jit(solution)/shard_map/ppermute | solution.py:750
  108.4 32.9 %collective-permute-start.15 = (bf16[4,432,384]{2,1,0:T(8,128)(2,1)S(1)}, bf16[4,432,384]{2,1,0:T(8,128)(2,1)}, u32[]{:S(2)}, u32[]{:S(2)}) collective-permute-start(bf16[4,432,384]{2,1,0:T(8,128)(2,1)S(1)} %collective-permute-done.9.refs_2_), channel_id=1, source_target_pairs={{0,16},{1,17},{2,18},{3,19},{4,20},{5,21},{6,22},{7,23},{8,24},{9,... | collective-permute-start | bytes 3981320 | tf_op jit(solution)/shard_map/ppermute | solution.py:750
  109.7 36.4 %collective-permute-start.17 = (bf16[4,432,384]{2,1,0:T(8,128)(2,1)S(1)}, bf16[4,432,384]{2,1,0:T(8,128)(2,1)}, u32[]{:S(2)}, u32[]{:S(2)}) collective-permute-start(bf16[4,432,384]{2,1,0:T(8,128)(2,1)S(1)} %collective-permute-done.9.refs_2_), channel_id=1, source_target_pairs={{0,8},{1,9},{2,10},{3,11},{4,12},{5,13},{6,14},{7,15},{8,0},{9,1},... | collective-permute-start | bytes 3981320 | tf_op jit(solution)/shard_map/ppermute | solution.py:750
  112.7 27.8 %collective-permute-start.13 = (bf16[4,384,384]{2,1,0:T(8,128)(2,1)S(1)}, bf16[4,384,384]{2,1,0:T(8,128)(2,1)}, u32[]{:S(2)}, u32[]{:S(2)}) collective-permute-start(bf16[4,384,384]{2,1,0:T(8,128)(2,1)S(1)} %pad_maximum_fusion.2.refs_0_), channel_id=1, source_target_pairs={{0,1},{1,0},{2,3},{3,2},{4,5},{5,4},{6,7},{7,6},{8,9},{9,8},{10,11... | collective-permute-start | bytes 3538952 | tf_op jit(solution)/shard_map/ppermute | solution.py:750
  141.3 24.2 %collective-permute-start.18 = (bf16[4,432,384]{2,1,0:T(8,128)(2,1)}, bf16[4,432,384]{2,1,0:T(8,128)(2,1)}, u32[]{:S(2)}, u32[]{:S(2)}) collective-permute-start(bf16[4,432,384]{2,1,0:T(8,128)(2,1)} %collective-permute-done.14.refs_4_), channel_id=1, source_target_pairs={{0,8},{1,9},{2,10},{3,11},{4,12},{5,13},{6,14},{7,15},{8,0},{9,1},... | collective-permute-start | bytes 3981320 | tf_op jit(solution)/shard_map/ppermute | solution.py:750
  141.8 23.8 %collective-permute-start.19 = (bf16[4,432,384]{2,1,0:T(8,128)(2,1)}, bf16[4,432,384]{2,1,0:T(8,128)(2,1)}, u32[]{:S(2)}, u32[]{:S(2)}) collective-permute-start(bf16[4,432,384]{2,1,0:T(8,128)(2,1)} %collective-permute-done.15.refs_6_), channel_id=1, source_target_pairs={{0,8},{1,9},{2,10},{3,11},{4,12},{5,13},{6,14},{7,15},{8,0},{9,1},... | collective-permute-start | bytes 3981320 | tf_op jit(solution)/shard_map/ppermute | solution.py:750
  144.7 30.0 %collective-permute-start.20 = (bf16[768,384]{1,0:T(8,128)(2,1)}, bf16[768,384]{1,0:T(8,128)(2,1)S(1)}, u32[]{:S(2)}, u32[]{:S(2)}) collective-permute-start(bf16[768,384]{1,0:T(8,128)(2,1)} %get-tuple-element.271), channel_id=1, source_target_pairs={{0,2},{1,3},{2,4},{3,5},{4,6},{5,7},{6,0},{7,1},{8,10},{9,11},{10,... | collective-permute-start | bytes 1769480 | tf_op jit(solution)/shard_map/ppermute | solution.py:750
  146.1 41.2 %collective-permute-start.21 = (bf16[768,384]{1,0:T(8,128)(2,1)}, bf16[768,384]{1,0:T(8,128)(2,1)S(1)}, u32[]{:S(2)}, u32[]{:S(2)}) collective-permute-start(bf16[768,384]{1,0:T(8,128)(2,1)} %get-tuple-element.271), channel_id=1, source_target_pairs={{0,4},{1,5},{2,6},{3,7},{4,0},{5,1},{6,2},{7,3},{8,12},{9,13},{10,... | collective-permute-start | bytes 1769480 | tf_op jit(solution)/shard_map/ppermute | solution.py:750
  148.8 51.2 %collective-permute-start.22 = (bf16[768,384]{1,0:T(8,128)(2,1)}, bf16[768,384]{1,0:T(8,128)(2,1)S(1)}, u32[]{:S(2)}, u32[]{:S(2)}) collective-permute-start(bf16[768,384]{1,0:T(8,128)(2,1)} %get-tuple-element.271), channel_id=1, source_target_pairs={{0,6},{1,7},{2,0},{3,1},{4,2},{5,3},{6,4},{7,5},{8,14},{9,15},{10,... | collective-permute-start | bytes 1769480 | tf_op jit(solution)/shard_map/ppermute | solution.py:750
  202.4 55.7 %collective-permute-start.25 = (bf16[4,768,384]{2,1,0:T(8,128)(2,1)S(1)}, bf16[4,768,384]{2,1,0:T(8,128)(2,1)}, u32[]{:S(2)}, u32[]{:S(2)}) collective-permute-start(bf16[4,768,384]{2,1,0:T(8,128)(2,1)S(1)} %pad_maximum_fusion.refs_0_), channel_id=1, source_target_pairs={{0,1},{1,0},{2,3},{3,2},{4,5},{5,4},{6,7},{7,6},{8,9},{9,8},{10,11... | collective-permute-start | bytes 7077896 | tf_op jit(solution)/shard_map/ppermute | solution.py:750
  203.7 76.3 %collective-permute-start.26 = (bf16[4,768,384]{2,1,0:T(8,128)(2,1)S(1)}, bf16[4,768,384]{2,1,0:T(8,128)(2,1)}, u32[]{:S(2)}, u32[]{:S(2)}) collective-permute-start(bf16[4,768,384]{2,1,0:T(8,128)(2,1)S(1)} %pad_maximum_fusion.refs_0_), channel_id=1, source_target_pairs={{0,8},{1,9},{2,10},{3,11},{4,12},{5,13},{6,14},{7,15},{8,0},{9,1},... | collective-permute-start | bytes 7077896 | tf_op jit(solution)/shard_map/ppermute | solution.py:750
  258.1 21.8 %collective-permute-start.27 = (bf16[4,768,384]{2,1,0:T(8,128)(2,1)}, bf16[4,768,384]{2,1,0:T(8,128)(2,1)}, u32[]{:S(2)}, u32[]{:S(2)}) collective-permute-start(bf16[4,768,384]{2,1,0:T(8,128)(2,1)} %collective-permute-done.25.refs_2_), channel_id=1, source_target_pairs={{0,8},{1,9},{2,10},{3,11},{4,12},{5,13},{6,14},{7,15},{8,0},{9,1},... | collective-permute-start | bytes 7077896 | tf_op jit(solution)/shard_map/ppermute | solution.py:750
  346.1 14.8 %collective-permute-start.29 = (bf16[4,4,2,96,384]{4,3,2,1,0:T(8,128)(2,1)}, bf16[4,4,2,96,384]{4,3,2,1,0:T(8,128)(2,1)S(1)}, u32[]{:S(2)}, u32[]{:S(2)}) collective-permute-start(bf16[4,4,2,96,384]{4,3,2,1,0:T(8,128)(2,1)} %shard_map.288), channel_id=1, source_target_pairs={{0,8},{1,9},{2,10},{3,11},{4,12},{5,13},{6,14},{7,15},{8,0},{9,1},... | collective-permute-start | bytes 7077896 | tf_op jit(solution)/shard_map/ppermute | solution.py:750
  386.4 40.4 %collective-permute-start.31 = (bf16[3,4,2,96,384]{4,3,2,1,0:T(8,128)(2,1)}, bf16[3,4,2,96,384]{4,3,2,1,0:T(8,128)(2,1)}, u32[]{:S(2)}, u32[]{:S(2)}) collective-permute-start(bf16[3,4,2,96,384]{4,3,2,1,0:T(8,128)(2,1)} %shard_map.292), channel_id=1, source_target_pairs={{0,8},{1,9},{2,10},{3,11},{4,12},{5,13},{6,14},{7,15},{8,0},{9,1},... | collective-permute-start | bytes 5308424 | tf_op jit(solution)/shard_map/ppermute | solution.py:750
  407.9 64.8 %collective-permute-start.32 = (bf16[4,864,384]{2,1,0:T(8,128)(2,1)}, bf16[4,864,384]{2,1,0:T(8,128)(2,1)S(1)}, u32[]{:S(2)}, u32[]{:S(2)}) collective-permute-start(bf16[4,864,384]{2,1,0:T(8,128)(2,1)} %get-tuple-element.340), channel_id=1, source_target_pairs={{0,1},{1,0},{2,3},{3,2},{4,5},{5,4},{6,7},{7,6},{8,9},{9,8},{10,11... | collective-permute-start | bytes 7962632 | tf_op jit(solution)/shard_map/ppermute | solution.py:750
  433.7 39.0 %collective-permute-start.33 = (bf16[3,4,2,48,384]{4,3,2,1,0:T(8,128)(2,1)}, bf16[3,4,2,48,384]{4,3,2,1,0:T(8,128)(2,1)S(1)}, u32[]{:S(2)}, u32[]{:S(2)}) collective-permute-start(bf16[3,4,2,48,384]{4,3,2,1,0:T(8,128)(2,1)} %get-tuple-element.341), channel_id=1, source_target_pairs={{0,16},{1,17},{2,18},{3,19},{4,20},{5,21},{6,22},{7,23},{8,24},{9,... | collective-permute-start | bytes 2654216 | tf_op jit(solution)/shard_map/ppermute | solution.py:750
  472.0 30.1 %collective-permute-start.37 = (bf16[2,4,2,96,768]{4,3,2,1,0:T(8,128)(2,1)}, bf16[2,4,2,96,768]{4,3,2,1,0:T(8,128)(2,1)}, u32[]{:S(2)}, u32[]{:S(2)}) collective-permute-start(bf16[2,4,2,96,768]{4,3,2,1,0:T(8,128)(2,1)} %shard_map.301), channel_id=1, source_target_pairs={{0,8},{1,9},{2,10},{3,11},{4,12},{5,13},{6,14},{7,15},{8,0},{9,1},... | collective-permute-start | bytes 7077896 | tf_op jit(solution)/shard_map/ppermute | solution.py:750
  481.2 20.9 %collective-permute-start.35 = (bf16[1,4,2,384,384]{4,3,2,1,0:T(8,128)(2,1)}, bf16[1,4,2,384,384]{4,3,2,1,0:T(8,128)(2,1)}, u32[]{:S(2)}, u32[]{:S(2)}) collective-permute-start(bf16[1,4,2,384,384]{4,3,2,1,0:T(8,128)(2,1)} %shard_map.299), channel_id=1, source_target_pairs={{0,8},{1,9},{2,10},{3,11},{4,12},{5,13},{6,14},{7,15},{8,0},{9,1},... | collective-permute-start | bytes 7077896 | tf_op jit(solution)/shard_map/ppermute | solution.py:750
  485.7 11.7 %collective-permute-start.36 = (bf16[1,4,2,96,384]{4,3,2,1,0:T(8,128)(2,1)}, bf16[1,4,2,96,384]{4,3,2,1,0:T(8,128)(2,1)S(1)}, u32[]{:S(2)}, u32[]{:S(2)}) collective-permute-start(bf16[1,4,2,96,384]{4,3,2,1,0:T(8,128)(2,1)} %shard_map.300), channel_id=1, source_target_pairs={{0,8},{1,9},{2,10},{3,11},{4,12},{5,13},{6,14},{7,15},{8,0},{9,1},... | collective-permute-start | bytes 1769480 | tf_op jit(solution)/shard_map/ppermute | solution.py:750
  490.1 12.0 %collective-permute-start.34 = (bf16[3,4,48,384]{3,2,1,0:T(8,128)(2,1)}, bf16[3,4,48,384]{3,2,1,0:T(8,128)(2,1)S(1)}, u32[]{:S(2)}, u32[]{:S(2)}) collective-permute-start(bf16[3,4,48,384]{3,2,1,0:T(8,128)(2,1)} %shard_map.298), channel_id=1, source_target_pairs={{0,1},{1,0},{2,3},{3,2},{4,5},{5,4},{6,7},{7,6},{8,9},{9,8},{10,11... | collective-permute-start | bytes 1327112 | tf_op jit(solution)/shard_map/ppermute | solution.py:750
  497.3 63.4 %collective-permute-start.43 = (bf16[864,384]{1,0:T(8,128)(2,1)}, bf16[864,384]{1,0:T(8,128)(2,1)S(1)}, u32[]{:S(2)}, u32[]{:S(2)}) collective-permute-start(bf16[864,384]{1,0:T(8,128)(2,1)} %get-tuple-element.369), channel_id=1, source_target_pairs={{0,2},{1,3},{2,4},{3,5},{4,6},{5,7},{6,0},{7,1},{8,10},{9,11},{10,... | collective-permute-start | bytes 1990664 | tf_op jit(solution)/shard_map/ppermute | solution.py:750
  502.1 33.5 %collective-permute-start.42 = (f32[16896]{0:T(1024)S(1)}, f32[16896]{0:T(1024)S(1)}, u32[]{:S(2)}, u32[]{:S(2)}) collective-permute-start(f32[16896]{0:T(1024)S(1)} %add.107), channel_id=1, source_target_pairs={{0,16},{1,17},{2,18},{3,19},{4,20},{5,21},{6,22},{7,23},{8,24},{9,... | collective-permute-start | bytes 202760 | tf_op jit(solution)/shard_map/ppermute | solution.py:750
  506.3 31.5 %collective-permute-start.39 = (bf16[3,48,384]{2,1,0:T(8,128)(2,1)}, bf16[3,48,384]{2,1,0:T(8,128)(2,1)S(1)}, u32[]{:S(2)}, u32[]{:S(2)}) collective-permute-start(bf16[3,48,384]{2,1,0:T(8,128)(2,1)} %get-tuple-element.360), channel_id=1, source_target_pairs={{0,2},{1,3},{2,4},{3,5},{4,6},{5,7},{6,0},{7,1},{8,10},{9,11},{10,... | collective-permute-start | bytes 331784 | tf_op jit(solution)/shard_map/ppermute | solution.py:750
  506.3 32.0 %collective-permute-start.40 = (bf16[3,48,384]{2,1,0:T(8,128)(2,1)}, bf16[3,48,384]{2,1,0:T(8,128)(2,1)S(1)}, u32[]{:S(2)}, u32[]{:S(2)}) collective-permute-start(bf16[3,48,384]{2,1,0:T(8,128)(2,1)} %get-tuple-element.361), channel_id=1, source_target_pairs={{0,4},{1,5},{2,6},{3,7},{4,0},{5,1},{6,2},{7,3},{8,12},{9,13},{10,... | collective-permute-start | bytes 331784 | tf_op jit(solution)/shard_map/ppermute | solution.py:750
  509.6 28.7 %collective-permute-start.41 = (bf16[3,48,384]{2,1,0:T(8,128)(2,1)}, bf16[3,48,384]{2,1,0:T(8,128)(2,1)S(1)}, u32[]{:S(2)}, u32[]{:S(2)}) collective-permute-start(bf16[3,48,384]{2,1,0:T(8,128)(2,1)} %get-tuple-element.362), channel_id=1, source_target_pairs={{0,6},{1,7},{2,0},{3,1},{4,2},{5,3},{6,4},{7,5},{8,14},{9,15},{10,... | collective-permute-start | bytes 331784 | tf_op jit(solution)/shard_map/ppermute | solution.py:750
  535.7 30.4 %collective-permute-start.44 = (bf16[864,384]{1,0:T(8,128)(2,1)}, bf16[864,384]{1,0:T(8,128)(2,1)S(1)}, u32[]{:S(2)}, u32[]{:S(2)}) collective-permute-start(bf16[864,384]{1,0:T(8,128)(2,1)} %get-tuple-element.370), channel_id=1, source_target_pairs={{0,4},{1,5},{2,6},{3,7},{4,0},{5,1},{6,2},{7,3},{8,12},{9,13},{10,... | collective-permute-start | bytes 1990664 | tf_op jit(solution)/shard_map/ppermute | solution.py:750
  537.8 42.4 %collective-permute-start.45 = (bf16[864,384]{1,0:T(8,128)(2,1)S(1)}, bf16[864,384]{1,0:T(8,128)(2,1)S(1)}, u32[]{:S(2)}, u32[]{:S(2)}) collective-permute-start(bf16[864,384]{1,0:T(8,128)(2,1)S(1)} %copy-done.67), channel_id=1, source_target_pairs={{0,6},{1,7},{2,0},{3,1},{4,2},{5,3},{6,4},{7,5},{8,14},{9,15},{10,... | collective-permute-start | bytes 1990664 | tf_op jit(solution)/shard_map/ppermute | solution.py:750
  545.4 69.2 %collective-permute-start.52 = (bf16[3,4,2,96,384]{4,3,2,1,0:T(8,128)(2,1)}, bf16[3,4,2,96,384]{4,3,2,1,0:T(8,128)(2,1)}, u32[]{:S(2)}, u32[]{:S(2)}) collective-permute-start(bf16[3,4,2,96,384]{4,3,2,1,0:T(8,128)(2,1)} %shard_map.310), channel_id=1, source_target_pairs={{0,8},{1,9},{2,10},{3,11},{4,12},{5,13},{6,14},{7,15},{8,0},{9,1},... | collective-permute-start | bytes 5308424 | tf_op jit(solution)/shard_map/ppermute | solution.py:750
  557.0 25.2 %collective-permute-start.51 = (f32[16896]{0:T(1024)}, f32[16896]{0:T(1024)}, u32[]{:S(2)}, u32[]{:S(2)}) collective-permute-start(f32[16896]{0:T(1024)} %add.108), channel_id=1, source_target_pairs={{0,1},{1,0},{2,3},{3,2},{4,5},{5,4},{6,7},{7,6},{8,9},{9,8},{10,11... | collective-permute-start | bytes 202760 | tf_op jit(solution)/shard_map/ppermute | solution.py:750
  560.7 22.3 %collective-permute-start.48 = (bf16[3,48,384]{2,1,0:T(8,128)(2,1)}, bf16[3,48,384]{2,1,0:T(8,128)(2,1)}, u32[]{:S(2)}, u32[]{:S(2)}) collective-permute-start(bf16[3,48,384]{2,1,0:T(8,128)(2,1)} %shard_map.309), channel_id=1, source_target_pairs={{0,16},{1,17},{2,18},{3,19},{4,20},{5,21},{6,22},{7,23},{8,24},{9,... | collective-permute-start | bytes 331784 | tf_op jit(solution)/shard_map/ppermute | solution.py:750
  566.1 36.2 %collective-permute-start.47 = (bf16[2,4,2,48,768]{4,3,2,1,0:T(8,128)(2,1)}, bf16[2,4,2,48,768]{4,3,2,1,0:T(8,128)(2,1)S(1)}, u32[]{:S(2)}, u32[]{:S(2)}) collective-permute-start(bf16[2,4,2,48,768]{4,3,2,1,0:T(8,128)(2,1)} %get-tuple-element.378), channel_id=1, source_target_pairs={{0,16},{1,17},{2,18},{3,19},{4,20},{5,21},{6,22},{7,23},{8,24},{9,... | collective-permute-start | bytes 3538952 | tf_op jit(solution)/shard_map/ppermute | solution.py:750
  581.0 33.6 %collective-permute-start.46 = (bf16[4,480,384]{2,1,0:T(8,128)(2,1)}, bf16[4,480,384]{2,1,0:T(8,128)(2,1)S(1)}, u32[]{:S(2)}, u32[]{:S(2)}) collective-permute-start(bf16[4,480,384]{2,1,0:T(8,128)(2,1)} %get-tuple-element.376), channel_id=1, source_target_pairs={{0,1},{1,0},{2,3},{3,2},{4,5},{5,4},{6,7},{7,6},{8,9},{9,8},{10,11... | collective-permute-start | bytes 4423688 | tf_op jit(solution)/shard_map/ppermute | solution.py:750
  582.2 20.0 %collective-permute-start.49 = (bf16[3,48,384]{2,1,0:T(8,128)(2,1)S(1)}, bf16[3,48,384]{2,1,0:T(8,128)(2,1)S(1)}, u32[]{:S(2)}, u32[]{:S(2)}) collective-permute-start(bf16[3,48,384]{2,1,0:T(8,128)(2,1)S(1)} %copy-done.27), channel_id=1, source_target_pairs={{0,8},{1,9},{2,10},{3,11},{4,12},{5,13},{6,14},{7,15},{8,0},{9,1},... | collective-permute-start | bytes 331784 | tf_op jit(solution)/shard_map/ppermute | solution.py:750
  583.0 19.3 %collective-permute-start.50 = (bf16[3,48,384]{2,1,0:T(8,128)(2,1)S(1)}, bf16[3,48,384]{2,1,0:T(8,128)(2,1)S(1)}, u32[]{:S(2)}, u32[]{:S(2)}) collective-permute-start(bf16[3,48,384]{2,1,0:T(8,128)(2,1)S(1)} %copy-done.27), channel_id=1, source_target_pairs={{0,24},{1,25},{2,26},{3,27},{4,28},{5,29},{6,30},{7,31},{8,16},{9,... | collective-permute-start | bytes 331784 | tf_op jit(solution)/shard_map/ppermute | solution.py:750
  621.6 51.6 %collective-permute-start.59 = (bf16[3,4,2,48,384]{4,3,2,1,0:T(8,128)(2,1)}, bf16[3,4,2,48,384]{4,3,2,1,0:T(8,128)(2,1)S(1)}, u32[]{:S(2)}, u32[]{:S(2)}) collective-permute-start(bf16[3,4,2,48,384]{4,3,2,1,0:T(8,128)(2,1)} %get-tuple-element.399), channel_id=1, source_target_pairs={{0,16},{1,17},{2,18},{3,19},{4,20},{5,21},{6,22},{7,23},{8,24},{9,... | collective-permute-start | bytes 2654216 | tf_op jit(solution)/shard_map/ppermute | solution.py:750
  626.9 23.6 %collective-permute-start.54 = (bf16[480,384]{1,0:T(8,128)(2,1)}, bf16[480,384]{1,0:T(8,128)(2,1)S(1)}, u32[]{:S(2)}, u32[]{:S(2)}) collective-permute-start(bf16[480,384]{1,0:T(8,128)(2,1)} %get-tuple-element.392), channel_id=1, source_target_pairs={{0,2},{1,3},{2,4},{3,5},{4,6},{5,7},{6,0},{7,1},{8,10},{9,11},{10,... | collective-permute-start | bytes 1105928 | tf_op jit(solution)/shard_map/ppermute | solution.py:750
  634.7 38.5 %collective-permute-start.53 = (bf16[864,384]{1,0:T(8,128)(2,1)}, bf16[864,384]{1,0:T(8,128)(2,1)S(1)}, u32[]{:S(2)}, u32[]{:S(2)}) collective-permute-start(bf16[864,384]{1,0:T(8,128)(2,1)} %shard_map.312.refs_0_), channel_id=1, source_target_pairs={{0,16},{1,17},{2,18},{3,19},{4,20},{5,21},{6,22},{7,23},{8,24},{9,... | collective-permute-start | bytes 1990664 | tf_op jit(solution)/shard_map/ppermute | solution.py:750
  639.5 33.7 %collective-permute-start.57 = (bf16[2,4,48,768]{3,2,1,0:T(8,128)(2,1)}, bf16[2,4,48,768]{3,2,1,0:T(8,128)(2,1)S(1)}, u32[]{:S(2)}, u32[]{:S(2)}) collective-permute-start(bf16[2,4,48,768]{3,2,1,0:T(8,128)(2,1)} %shard_map.314), channel_id=1, source_target_pairs={{0,1},{1,0},{2,3},{3,2},{4,5},{5,4},{6,7},{7,6},{8,9},{9,8},{10,11... | collective-permute-start | bytes 1769480 | tf_op jit(solution)/shard_map/ppermute | solution.py:750
  649.0 16.4 %collective-permute-start.55 = (bf16[480,384]{1,0:T(8,128)(2,1)}, bf16[480,384]{1,0:T(8,128)(2,1)S(1)}, u32[]{:S(2)}, u32[]{:S(2)}) collective-permute-start(bf16[480,384]{1,0:T(8,128)(2,1)} %get-tuple-element.393), channel_id=1, source_target_pairs={{0,4},{1,5},{2,6},{3,7},{4,0},{5,1},{6,2},{7,3},{8,12},{9,13},{10,... | collective-permute-start | bytes 1105928 | tf_op jit(solution)/shard_map/ppermute | solution.py:750
  650.5 22.7 %collective-permute-start.56 = (bf16[480,384]{1,0:T(8,128)(2,1)S(1)}, bf16[480,384]{1,0:T(8,128)(2,1)S(1)}, u32[]{:S(2)}, u32[]{:S(2)}) collective-permute-start(bf16[480,384]{1,0:T(8,128)(2,1)S(1)} %copy-done.68), channel_id=1, source_target_pairs={{0,6},{1,7},{2,0},{3,1},{4,2},{5,3},{6,4},{7,5},{8,14},{9,15},{10,... | collective-permute-start | bytes 1105928 | tf_op jit(solution)/shard_map/ppermute | solution.py:750
  677.8 41.0 %collective-permute-start.61 = (bf16[864,384]{1,0:T(8,128)(2,1)}, bf16[864,384]{1,0:T(8,128)(2,1)S(1)}, u32[]{:S(2)}, u32[]{:S(2)}) collective-permute-start(bf16[864,384]{1,0:T(8,128)(2,1)} %shard_map.316.refs_2_), channel_id=1, source_target_pairs={{0,8},{1,9},{2,10},{3,11},{4,12},{5,13},{6,14},{7,15},{8,0},{9,1},... | collective-permute-start | bytes 1990664 | tf_op jit(solution)/shard_map/ppermute | solution.py:750
  682.2 36.6 %collective-permute-start.68 = (bf16[3,4,48,384]{3,2,1,0:T(8,128)(2,1)}, bf16[3,4,48,384]{3,2,1,0:T(8,128)(2,1)S(1)}, u32[]{:S(2)}, u32[]{:S(2)}) collective-permute-start(bf16[3,4,48,384]{3,2,1,0:T(8,128)(2,1)} %shard_map.319), channel_id=1, source_target_pairs={{0,1},{1,0},{2,3},{3,2},{4,5},{5,4},{6,7},{7,6},{8,9},{9,8},{10,11... | collective-permute-start | bytes 1327112 | tf_op jit(solution)/shard_map/ppermute | solution.py:750
  685.6 25.4 %collective-permute-start.63 = (bf16[2,48,768]{2,1,0:T(8,128)(2,1)}, bf16[2,48,768]{2,1,0:T(8,128)(2,1)S(1)}, u32[]{:S(2)}, u32[]{:S(2)}) collective-permute-start(bf16[2,48,768]{2,1,0:T(8,128)(2,1)} %get-tuple-element.409), channel_id=1, source_target_pairs={{0,2},{1,3},{2,4},{3,5},{4,6},{5,7},{6,0},{7,1},{8,10},{9,11},{10,... | collective-permute-start | bytes 442376 | tf_op jit(solution)/shard_map/ppermute | solution.py:750
  692.6 26.2 %collective-permute-start.62 = (bf16[480,384]{1,0:T(8,128)(2,1)}, bf16[480,384]{1,0:T(8,128)(2,1)S(1)}, u32[]{:S(2)}, u32[]{:S(2)}) collective-permute-start(bf16[480,384]{1,0:T(8,128)(2,1)} %shard_map.317.refs_0_), channel_id=1, source_target_pairs={{0,16},{1,17},{2,18},{3,19},{4,20},{5,21},{6,22},{7,23},{8,24},{9,... | collective-permute-start | bytes 1105928 | tf_op jit(solution)/shard_map/ppermute | solution.py:750
  693.4 9.2 %collective-permute-start.69 = (f32[1536]{0:T(1024)S(1)}, f32[1536]{0:T(1024)S(1)}, u32[]{:S(2)}, u32[]{:S(2)}) collective-permute-start(f32[1536]{0:T(1024)S(1)} %fusion.13), channel_id=1, source_target_pairs={{0,16},{1,17},{2,18},{3,19},{4,20},{5,21},{6,22},{7,23},{8,24},{9,... | collective-permute-start | bytes 18440 | tf_op jit(solution)/shard_map/ppermute | solution.py:750
  721.9 27.3 %collective-permute-start.71 = (bf16[2,48,768]{2,1,0:T(8,128)(2,1)}, bf16[2,48,768]{2,1,0:T(8,128)(2,1)S(1)}, u32[]{:S(2)}, u32[]{:S(2)}) collective-permute-start(bf16[2,48,768]{2,1,0:T(8,128)(2,1)} %shard_map.321), channel_id=1, source_target_pairs={{0,16},{1,17},{2,18},{3,19},{4,20},{5,21},{6,22},{7,23},{8,24},{9,... | collective-permute-start | bytes 442376 | tf_op jit(solution)/shard_map/ppermute | solution.py:750
  722.7 26.5 %collective-permute-start.72 = (bf16[2,48,768]{2,1,0:T(8,128)(2,1)}, bf16[2,48,768]{2,1,0:T(8,128)(2,1)S(1)}, u32[]{:S(2)}, u32[]{:S(2)}) collective-permute-start(bf16[2,48,768]{2,1,0:T(8,128)(2,1)} %shard_map.321), channel_id=1, source_target_pairs={{0,8},{1,9},{2,10},{3,11},{4,12},{5,13},{6,14},{7,15},{8,0},{9,1},... | collective-permute-start | bytes 442376 | tf_op jit(solution)/shard_map/ppermute | solution.py:750
  725.9 12.7 %collective-permute-start.77 = (f32[1536]{0:T(1024)S(1)}, f32[1536]{0:T(1024)S(1)}, u32[]{:S(2)}, u32[]{:S(2)}) collective-permute-start(f32[1536]{0:T(1024)S(1)} %add.112), channel_id=1, source_target_pairs={{0,1},{1,0},{2,3},{3,2},{4,5},{5,4},{6,7},{7,6},{8,9},{9,8},{10,11... | collective-permute-start | bytes 18440 | tf_op jit(solution)/shard_map/ppermute | solution.py:750
  736.1 13.1 %collective-permute-start.70 = (bf16[480,384]{1,0:T(8,128)(2,1)}, bf16[480,384]{1,0:T(8,128)(2,1)S(1)}, u32[]{:S(2)}, u32[]{:S(2)}) collective-permute-start(bf16[480,384]{1,0:T(8,128)(2,1)} %shard_map.320.refs_0_), channel_id=1, source_target_pairs={{0,8},{1,9},{2,10},{3,11},{4,12},{5,13},{6,14},{7,15},{8,0},{9,1},... | collective-permute-start | bytes 1105928 | tf_op jit(solution)/shard_map/ppermute | solution.py:750
  738.5 10.7 %collective-permute-start.73 = (bf16[2,48,768]{2,1,0:T(8,128)(2,1)S(1)}, bf16[2,48,768]{2,1,0:T(8,128)(2,1)S(1)}, u32[]{:S(2)}, u32[]{:S(2)}) collective-permute-start(bf16[2,48,768]{2,1,0:T(8,128)(2,1)S(1)} %copy-done.25), channel_id=1, source_target_pairs={{0,24},{1,25},{2,26},{3,27},{4,28},{5,29},{6,30},{7,31},{8,16},{9,... | collective-permute-start | bytes 442376 | tf_op jit(solution)/shard_map/ppermute | solution.py:750
  761.2 12.6 %collective-permute-start.82 = (f32[1536]{0:T(1024)S(1)}, f32[1536]{0:T(1024)S(1)}, u32[]{:S(2)}, u32[]{:S(2)}) collective-permute-start(f32[1536]{0:T(1024)S(1)} %add.114), channel_id=1, source_target_pairs={{0,2},{1,3},{2,4},{3,5},{4,6},{5,7},{6,0},{7,1},{8,10},{9,11},{10,... | collective-permute-start | bytes 18440 | tf_op jit(solution)/shard_map/ppermute | solution.py:750
  (89 other events, 1081.2 us)

commit v6 on v5

--- a/solution.py
+++ b/solution.py
@@ -913,15 +913,19 @@
     return combine(at, steps, groups, [own] * CHIPS_Z)
 
 
-def reduce_y_first(grad, place):
+def reduce_y_first(grad, place, stop=None):
     at = place.at
     parts, half = grad.parts, grad.half
     rows = grad.rows // CHIPS_Y
     away = grad.product(at, True)
     (near,) = yield [hop(away, dc=1)]
     send, keep = grad.product(at, False, True, near)
+    if stop == "sums":
+        return send, keep, False
     flip = lambda value: 1 - value
     (over,) = yield [hop(send, dy=1)]
+    if stop == "y":
+        return over, keep, True
     block = (parts, 1, 1, rows, half)
     short = (parts, 1, rows, half)
     index = lambda i, at: (0, i, flip(at[1]), 0, 0)
@@ -954,7 +958,7 @@
     return {grad.number: (pieces, 0, rows)}
 
 
-def reduce_x_first(grads, place):
+def reduce_x_first(grads, place, stop):
     at = place.at
     away = [grad.product(at, True) for grad in grads]
     near = yield [hop(item, dc=1) for item in away]
@@ -965,6 +969,8 @@
         starts.append(starts[-1] + grad.parts * grad.rows)
     send, keep = flat
     (across,) = yield [hop(send, dx=1)]
+    if stop == "x":
+        return across, keep
     steps = 3
     tall = total // steps
     ahead = lambda k: lambda i, at: (lax.rem(at[0] + k, CHIPS_Z), i, 0)
@@ -974,13 +980,200 @@
     )
     landed = yield [hop(send, dz=k) for k, send in zip(range(1, CHIPS_Z), sends)]
     add = lambda *terms: combine(at, steps, [[(term, *piece[1:]) for term in terms]], [piece])[0]
-    own = add(own, *landed)
-    (other,) = yield [hop(own, dy=1)]
-    own = add(own, other)
-    (other,) = yield [hop(own, dc=1)]
-    return {
-        grad.number: ([own, other], start, grad.rows) for grad, start in zip(grads, starts)
-    }
+    return add(own, *landed)
+
+
+def tail_kernel(arrived, *refs):
+    take = iter(refs)
+    count = len(arrived)
+    a_in, a_keep = next(take), next(take)
+    b_ins = [(next(take), next(take)) for _ in range(count)]
+    l_in, vec = next(take), next(take)
+    a_own, a_other = next(take), next(take)
+    b_outs = [next(take) for _ in range(count)]
+    l_own, l_other, vec_out = next(take), next(take), next(take)
+    a_zsend, a_zland, a_ysend, a_yland, a_cland = [next(take) for _ in range(5)]
+    b_scratch = [[next(take) for _ in range(6)] for _ in range(count)]
+    l_yland, l_cland = next(take), next(take)
+    v_send, v_land = next(take), next(take)
+    a_sems, b_sems, v_sems = next(take), [next(take) for _ in range(count)], next(take)
+    rep, shard = lax.axis_index("rep"), lax.axis_index("shard")
+    y, core = lax.div(rep, CORES), lax.rem(rep, CORES)
+    z, x = lax.div(shard, CHIPS_X), lax.rem(shard, CHIPS_X)
+
+    def device(dz=0, dx=0, dy=0, dc=0):
+        to_y, to_core = lax.rem(y + dy, CHIPS_Y), lax.rem(core + dc, CORES)
+        to_z, to_x = lax.rem(z + dz, CHIPS_Z), lax.rem(x + dx, CHIPS_X)
+        return (to_y * CORES + to_core, to_z * CHIPS_X + to_x)
+
+    flip_z = 1 + 2 * lax.rem(z, 2)
+    mates = [dict(dx=1), dict(dy=1), dict(dc=1), dict(dy=1, dc=1)]
+    mates += [dict(dz=k) for k in range(1, CHIPS_Z)]
+    barrier = pltpu.get_barrier_semaphore()
+    for mate in mates:
+        pl.semaphore_signal(
+            barrier, inc=1, device_id=device(**mate), device_id_type=pl.DeviceIdType.MESH
+        )
+    pl.semaphore_wait(barrier, len(mates))
+    sent = []
+
+    def send(source, target, sems, number, **step):
+        copy = pltpu.make_async_remote_copy(
+            src_ref=source,
+            dst_ref=target,
+            send_sem=sems.at[0, number],
+            recv_sem=sems.at[1, number],
+            device_id=device(**step),
+            device_id_type=pl.DeviceIdType.MESH,
+        )
+        copy.start()
+        sent.append(copy)
+        return copy
+
+    def wide(value):
+        return value.astype(jnp.float32)
+
+    order = (2, 1, 3, 0)
+    ahead = [lax.rem(z + k, CHIPS_Z) for k in order]
+    v_send[0] = vec[...]
+    v_copies = [send(v_send.at[0], v_land.at[0], v_sems, 0, dc=1)]
+    a_across = a_in
+    l_y = send(l_in, l_yland, a_sems, 0, dy=1)
+    b_y = [[] for _ in range(count)]
+    for j, to in enumerate(ahead):
+        for i, (b_send, _) in enumerate(b_ins):
+            if arrived[i]:
+                continue
+            b_y[i].append(send(b_send.at[:, to], b_scratch[i][0].at[j], b_sems[i], j, dy=1))
+    steps = (dict(dc=1), dict(dy=1), dict(dx=1), dict(dz=2), dict(dz=flip_z))
+
+    def add_vectors(s):
+        v_copies[s].wait_recv()
+        total = v_send[s] + v_land[s]
+        if s + 1 == len(steps):
+            vec_out[...] = total
+        else:
+            v_send[s + 1] = total
+            v_copies.append(
+                send(v_send.at[s + 1], v_land.at[s + 1], v_sems, s + 1, **steps[s + 1])
+            )
+
+    def over(i, j, side):
+        if arrived[i]:
+            return wide(b_ins[i][0][:, ahead[j], side])
+        return wide(b_scratch[i][0][j, :, side])
+
+    a_z, b_x, b_z = [], [[] for _ in range(count)], [[] for _ in range(count)]
+
+    def b_along_z(j):
+        k = order[j]
+        for i, (_, keep) in enumerate(b_ins):
+            _, _, x_land, z_send, z_land, _ = b_scratch[i]
+            b_x[i][j].wait_recv()
+            if k:
+                total = wide(keep[:, ahead[j], x]) + over(i, j, x) + wide(x_land[j])
+                z_send[k - 1] = total.astype(jnp.bfloat16)
+                b_z[i].append(
+                    send(z_send.at[k - 1], z_land.at[k - 1], b_sems[i], 7 + k, dz=k)
+                )
+
+    for j, k in enumerate(order):
+        if k:
+            total = wide(a_keep[ahead[j]]) + wide(a_across[ahead[j]])
+            a_zsend[k - 1] = total.astype(jnp.bfloat16)
+            a_z.append(send(a_zsend.at[k - 1], a_zland.at[k - 1], a_sems, 3 + k, dz=k))
+        for i, (_, keep) in enumerate(b_ins):
+            _, x_send, x_land, *_ = b_scratch[i]
+            if not arrived[i]:
+                b_y[i][j].wait_recv()
+            total = wide(keep[:, ahead[j], 1 - x]) + over(i, j, 1 - x)
+            x_send[j] = total.astype(jnp.bfloat16)
+            b_x[i].append(send(x_send.at[j], x_land.at[j], b_sems[i], 4 + j, dx=1))
+        if j:
+            b_along_z(j - 1)
+        add_vectors(j)
+    b_along_z(CHIPS_Z - 1)
+    l_y.wait_recv()
+    l_own[...] = (wide(l_in[...]) + wide(l_yland[...])).astype(jnp.bfloat16)
+    ends = [send(l_own, l_cland, a_sems, 1, dc=1)]
+    add_vectors(4)
+    for copy in a_z:
+        copy.wait_recv()
+    total = wide(a_keep[z]) + wide(a_across[z])
+    for k in range(CHIPS_Z - 1):
+        total = total + wide(a_zland[k])
+    a_ysend[...] = total.astype(jnp.bfloat16)
+    a_y = send(a_ysend, a_yland, a_sems, 7, dy=1)
+    for i, (_, keep) in enumerate(b_ins):
+        _, _, x_land, _, z_land, end_land = b_scratch[i]
+        for copy in b_z[i]:
+            copy.wait_recv()
+        total = wide(keep[:, z, x]) + over(i, 3, x) + wide(x_land[3])
+        for k in range(CHIPS_Z - 1):
+            total = total + wide(z_land[k])
+        b_outs[i][0] = total.astype(jnp.bfloat16)
+        for number, step in enumerate((dict(dy=1), dict(dc=1), dict(dy=1, dc=1))):
+            ends.append(
+                send(b_outs[i].at[0], end_land.at[number], b_sems[i], 11 + number, **step)
+            )
+    a_y.wait_recv()
+    a_own[...] = (wide(a_ysend[...]) + wide(a_yland[...])).astype(jnp.bfloat16)
+    ends.append(send(a_own, a_cland, a_sems, 8, dc=1))
+    for copy in ends:
+        copy.wait_recv()
+    for i in range(count):
+        b_outs[i][1:4] = b_scratch[i][5][...]
+    a_other[...] = a_cland[...]
+    l_other[...] = l_cland[...]
+    for copy in sent:
+        copy.wait_send()
+
+
+def reduce_tail(flat, pairs, last, vec):
+    low = jnp.bfloat16
+    _, total, unit = flat[0].shape
+    whole = pl.BlockSpec(memory_space=pltpu.VMEM)
+    far = pl.BlockSpec(memory_space=pl.ANY)
+    piece = (total, unit)
+    outs = [piece, piece]
+    scratch = [(CHIPS_Z - 1, *piece), (CHIPS_Z - 1, *piece), piece, piece, piece]
+    args, specs, arrived = [*flat], [whole, whole], []
+    for first, keep, here in pairs:
+        parts, _, _, rows, half = keep.shape
+        block = (parts, rows, half)
+        args += [first, keep]
+        specs += [whole if here else far, whole]
+        arrived.append(here)
+        outs.append((CORES * CHIPS_Y, *block))
+        scratch += [
+            (16, 128) if here else (CHIPS_Z, parts, CHIPS_X, rows, half),
+            (CHIPS_Z, *block),
+            (CHIPS_Z, *block),
+            (CHIPS_Z - 1, *block),
+            (CHIPS_Z - 1, *block),
+            (CORES * CHIPS_Y - 1, *block),
+        ]
+    outs += [last.shape, last.shape]
+    scratch += [last.shape, last.shape]
+    shapes = [jax.ShapeDtypeStruct(shape, low) for shape in outs]
+    shapes.append(jax.ShapeDtypeStruct(vec.shape, jnp.float32))
+    scratch = [pltpu.VMEM(shape, low) for shape in scratch]
+    scratch += [pltpu.VMEM((5, *vec.shape), jnp.float32)] * 2
+    scratch += [pltpu.SemaphoreType.DMA((2, 9))]
+    scratch += [pltpu.SemaphoreType.DMA((2, 14))] * len(pairs)
+    scratch += [pltpu.SemaphoreType.DMA((2, 5))]
+    own, other, *rest = pl.pallas_call(
+        functools.partial(tail_kernel, arrived),
+        in_specs=[*specs, whole, whole],
+        out_specs=[whole] * len(shapes),
+        out_shape=shapes,
+        scratch_shapes=scratch,
+        compiler_params=pltpu.CompilerParams(
+            vmem_limit_bytes=KERNEL_VMEM, collective_id=0, has_side_effects=True
+        ),
+        cost_estimate=pl.CostEstimate(flops=0, bytes_accessed=200_000_000, transcendentals=0),
+    )(*args, last, vec)
+    return [own, other], rest[:-3], list(rest[-3:-1]), rest[-1]
 
 
 def join_kernel(plan, count, at_ref, *refs):
@@ -1027,14 +1220,6 @@
     )(at, *arrays)
 
 
-def reduce_total(total, place):
-    for step in (dict(dc=1), dict(dy=1), dict(dx=1), dict(dz=2)):
-        (other,) = yield [hop(total, **step)]
-        total = total + other
-    up, down = yield [hop(total, dz=1), hop(total, dz=3)]
-    return total + jnp.where(place.z % 2 == 0, down, up)
-
-
 def qv_sum(halves):
     own, away, at = halves
     own, away = jnp.sum(own, axis=0), jnp.sum(away, axis=0)
@@ -1089,16 +1274,16 @@
 
         def reduce(layer, *grads):
             name = ("grad", layer, grads[0].number)
-            if grads[0].number in (0, 6):
-                flow.start(name, reduce_y_first(*grads, place))
+            if name[2] == 0:
+                chain = reduce_y_first(*grads, place, None if layer else "sums")
+            elif name[2] == 6:
+                chain = reduce_y_first(*grads, place, "y")
             else:
-                flow.start(name, reduce_x_first(grads, place))
+                chain = reduce_x_first(grads, place, "z" if layer else "x")
+            flow.start(name, chain)
 
         def back_step(main, *held):
             return flow.tick(main, *[name for name in flow.running if name not in held])
-
-        def add_up(name, total):
-            flow.start(name, reduce_total(total, place))
 
     else:
         at = jnp.zeros((4,), jnp.int32)
@@ -1123,9 +1308,6 @@
 
         def back_step(main, *held):
             return main
-
-        def add_up(name, total):
-            flow.done[name] = lax.psum(total, AXES)
 
     step("begin", ())
     if fast:
@@ -1182,11 +1364,6 @@
         else:
             grad_6 = Grad(6, middle, grad_pre, grad_pre, True, wide // UNIT, UNIT)
             reduce(layer, grad_8, grad_6, grad_2)
-        if layer == 0:
-            pieces = [qv_sum(sums[1][2])]
-            for row_sums, ffin_sum, _ in sums:
-                pieces += [row_sums[:6].reshape(-1), ffin_sum[0]]
-            add_up("early", jnp.concatenate(pieces))
         above_chain = () if layer else (("grad", 1, 8),)
         grad_context = back_step(grad_context, *above_chain)
         away, away_sums = attend_back(grad_context, slots, heads, at, True)
@@ -1198,32 +1375,52 @@
         sums[layer][2] = (own_sums, away_sums, at)
         proj = back_step(proj, *(wide_chains if layer else ()))
         above = grad_attn
-    add_up("late", qv_sum(sums[0][2]))
     grad_input = input_grad(above, proj, get(0, 0), at)
-    grad_input = back_step(grad_input)
-    while flow.running:
-        grad_input = back_step(grad_input)
-    early, late = flow.finish("early"), flow.finish("late")
+    pieces = [qv_sum(sums[layer][2]) for layer in range(LAYERS)]
+    for row_sums, ffin_sum, _ in sums:
+        pieces += [row_sums[:6].reshape(-1), ffin_sum[0]]
+    total = jnp.concatenate(pieces)
+    if fast:
+        while flow.running:
+            grad_input = back_step(grad_input)
+        done = flow.done
+        vec = total.reshape(-1, 128)
+        last, vec, grad_input = lax.optimization_barrier(
+            (done["grad", 1, 8], vec, grad_input)
+        )
+        flat, ends, last, vec = reduce_tail(
+            done["grad", 0, 8], [done["grad", 0, 6], done["grad", 0, 0]], last, vec
+        )
+        total = vec.reshape(-1)
+    else:
+        total = lax.psum(total, AXES)
     count = lax.axis_size("shard")
     shard = lax.axis_index("shard")
     ff = sums[0][1].shape[1]
-    rest = early[2 * D :].reshape(LAYERS, 6 * D + ff)
+    rest = total[4 * D :].reshape(LAYERS, 6 * D + ff)
 
     def share(stacked):
         width = stacked.shape[1] // count
         return lax.dynamic_slice_in_dim(stacked, shard * width, width, axis=1)
 
-    grads = {1: share(jnp.stack([late, early[: 2 * D]])), 7: share(rest[:, 6 * D :])}
+    grads = {1: share(total[: 4 * D].reshape(LAYERS, 2 * D)), 7: share(rest[:, 6 * D :])}
     for number, row in ((10, 0), (11, 1), (9, 2), (4, 3), (5, 4), (3, 5)):
         grads[number] = share(rest[:, row * D : (row + 1) * D])
     if fast:
-        done = [{}, {}]
-        for name, value in flow.done.items():
-            if name[0] == "grad":
-                done[name[1]].update(value)
-        for numbers in ((8, 6, 2), (0,)):
+        rows = {number: weights[number].shape[1] for number in MATRICES}
+        parts = {number: weights[number].shape[2] // (CORES * UNIT) for number in MATRICES}
+        known = [{}, dict(done["grad", 1, 0])]
+        for layer, pieces, numbers in ((0, flat, (8, 2)), (1, last, (8, 6, 2))):
+            start = 0
+            for number in numbers:
+                known[layer][number] = (pieces, start, rows[number])
+                start += rows[number] * parts[number]
+        for number, end in zip((6, 0), ends):
+            end = end.reshape(end.shape[0], -1, end.shape[-1])
+            known[0][number] = (list(end), 0, rows[number] // CHIPS_Y)
+        for numbers in (MATRICES,):
             shapes = {number: weights[number].shape[1:] for number in numbers}
-            grads.update(zip(numbers, join(at, done, shapes)))
+            grads.update(zip(numbers, join(at, known, shapes)))
     else:
         for number in MATRICES:
             grads[number] = jnp.stack([flow.done[("grad", layer, number)] for layer in range(LAYERS)])

time: 785 us -> 747 us (0.952)
  waiting for transfers between devices: 148 us -> 83.8 us
  Pallas kernels: 502 us -> 559 us
  starting transfers between devices: 88.9 us -> 47.4 us
  local copies, waits for them, and re-layouts: 26.8 us -> 39.4 us
    pallas_call x0 -> x1, Pallas kernels: none -> 94.7 us  [reduce_tail(): pl.pallas_call(functools.partial(tail_kernel, arrived), in_specs=[*specs,...]
    ppermute x84 -> x50, waiting for transfers between devices: 148 us -> 83.8 us  [hop(): return lax.ppermute(value, AXES, pairs)]
    ppermute x84 -> x50, starting transfers between devices: 88.9 us -> 47.4 us  [hop(): return lax.ppermute(value, AXES, pairs)]
    pallas_call x15 -> x5, Pallas kernels: 53.4 us -> 19 us  [combine(): pl.pallas_call(functools.partial(combine_kernel, [len(group) for group in...]
  transfers between devices with their start and end apart: 84 -> 50, of which waited for: 26 -> 14; matrix products, arithmetic and copies ran while one was open for 3% -> 4% of each run, Pallas kernels for 51% -> 47%
where the time goes in v6:
time: 747 us; the launch traced here: 738 us
  Pallas kernels  559 us (75%)
  waiting for transfers between devices  83.8 us (11%)
  starting transfers between devices  47.4 us (6%)
  local copies, waits for them, and re-layouts  39.4 us (5%)
    pallas_call x16, Pallas kernels, product(): pl.pallas_call(functools.partial(weight_grad_kernel, split_y), grid_spec=...  107 us
    pallas_call x1, Pallas kernels, reduce_tail(): pl.pallas_call(functools.partial(tail_kernel, arrived), in_specs=[*specs,...  94.7 us
    ppermute x50, waiting for transfers between devices, hop(): return lax.ppermute(value, AXES, pairs)  83.8 us
    pallas_call x4, Pallas kernels, attend_back(): pl.pallas_call(attend_back_kernel, grid_spec=pltpu.PrefetchScalarGridSpec...  75.1 us
    pallas_call x4, Pallas kernels, attend(): pl.pallas_call(attend_kernel, grid=(trees, PAIRS // 2), in_specs=[slot_sp...  71.3 us
    pallas_call x2, Pallas kernels, feed(): pl.pallas_call(feed_kernel, grid=(count // ROW_TILE,), in_specs=[row_spec...  55.9 us
    pallas_call x2, Pallas kernels, feed_back(): pl.pallas_call(functools.partial(feed_back_kernel, proj is not None), gri...  53.7 us
    ppermute x50, starting transfers between devices, hop(): return lax.ppermute(value, AXES, pairs)  47.4 us
  transfers between devices with their start and end apart: 50, of which 14 were waited for; matrix products, arithmetic and copies ran while one was open for 4% of the time, Pallas kernels for 47%

profile of v6, /device:TPU:17, one launch (start us, length us, event | category | flops | bytes accessed | tf_op | source)
XLA Modules:
  0.0 738.0 jit_solution(835297196076856872)
XLA Ops:
  5.9 3.9 shard_map.272
  10.0 2.3 collective-permute-start.7
  12.4 2.0 collective-permute-start.8
  14.4 6.6 collective-permute-done.1
  21.1 19.5 %collective-permute-done.2 = bf16[112,1152]{1,0:T(8,128)(2,1)S(1)} collective-permute-done((bf16[112,1152]{1,0:T(8,128)(2,1)S(1)}, bf16[112,1152]{1,0:T(8,128)(2,1)S(1)}, u32[]{:S(2)}, u32[]{:S(2)}) %collective-permute-start.2) | collective-permute-done | bytes 258080 | tf_op jit(solution)/shard_map/ppermute | solution.py:750
  43.5 19.1 %shard_map.273 = (s32[1,6,2,1024]{3,2,1,0:T(2,128)}, bf16[1,12,1024,128]{3,2,1,0:T(8,128)(2,1)}) custom-call(s32[1,13]{1,0:T(1,128)} %parent_ref, s32[1,1,1024]{2,1,0:T(1,128)} %bitcast.134, s32[1,6,2,1024]{3,2,1,0:T(2,128)} %transpose_reshape.3.cluster_ref), custom_call_target="tpu_custom_call" | custom-call | flops 20000000000 | bytes 4000000 | tf_op jit(solution)/shard_map/pallas_call | solution.py:574
  62.6 2.0 collective-permute-done.3.refs_2_
  68.4 2.4 collective-permute-start.11
  70.9 5.3 shard_map.274
  80.4 7.8 %shard_map.275.query_ref.key_ref.value_ref = bf16[1024,2304]{1,0:T(8,128)(2,1)} custom-call(bf16[1024,768]{1,0:T(8,128)(2,1)} %left_ref.3, bf16[768,2304]{1,0:T(8,128)(2,1)} %bitcast.84, f32[1,2304]{1,0:T(1,128)} %broadcast_in_dim.4.bias_ref), custom_call_target="tpu_custom_call" | custom-call | flops 4348654592 | bytes 5111808 | tf_op jit(solution)/shard_map/pallas_call | solution.py:458
  88.2 17.7 %shard_map.276 = (bf16[1024,768]{1,0:T(8,128)(2,1)}, bf16[1,12,1024,128]{3,2,1,0:T(8,128)(2,1)}, bf16[1,12,1024,128]{3,2,1,0:T(8,128)(2,1)}, bf16[1,12,1024,128]{3,2,1,0:T(8,128)(2,1)}) custom-call(s32[1,6,2,1024]{3,2,1,0:T(2,128)} %get-tuple-element.203.slot_ref, bf16[1024,2304]{1,0:T(8,128)(2,1)} %shard_map.275.query_ref.key_ref.value_ref, ...), custom_call_target="tpu_custom_call" | custom-call | flops 15000000512 | bytes 10000000 | tf_op jit(solution)/shard_map/pallas_call | solution.py:158
  113.7 17.7 %shard_map.277 = (bf16[1024,768]{1,0:T(8,128)(2,1)}, bf16[1,12,1024,128]{3,2,1,0:T(8,128)(2,1)}, bf16[1,12,1024,128]{3,2,1,0:T(8,128)(2,1)}, bf16[1,12,1024,128]{3,2,1,0:T(8,128)(2,1)}) custom-call(s32[1,6,2,1024]{3,2,1,0:T(2,128)} %get-tuple-element.203.slot_ref, ...), custom_call_target="tpu_custom_call", output_to_operand_aliasing={{0}: (5, {}), {1}: (6, {}), {2}: (7, {}), {3}: (8, {})} | custom-call | flops 15000000512 | bytes 10000000 | tf_op jit(solution)/shard_map/pallas_call | solution.py:158
  131.4 8.8 %collective-permute-done.13.refs_2_ = bf16[4,384,384]{2,1,0:T(8,128)(2,1)} collective-permute-done((bf16[4,384,384]{2,1,0:T(8,128)(2,1)S(1)}, bf16[4,384,384]{2,1,0:T(8,128)(2,1)}, u32[]{:S(2)}, u32[]{:S(2)}) %collective-permute-start.13) | collective-permute-done | bytes 1179680 | tf_op jit(solution)/shard_map/ppermute | solution.py:750
  142.3 2.1 collective-permute-done.23.refs_1_
  145.8 2.6 collective-permute-start.21
  157.3 5.7 shard_map.280
  163.0 9.1 %shard_map.278 = (bf16[8,2,48,768]{3,2,1,0:T(8,128)(2,1)}, bf16[8,2,48,3072]{3,2,1,0:T(8,128)(2,1)}, bf16[8,2,192,768]{3,2,1,0:T(8,128)(2,1)}) custom-call(s32[4]{0:T(128)} %pad_add_fusion.at_ref.refs_1_, bf16[4,432,384]{2,1,0:T(8,128)(2,1)} %copy-done.4, bf16[4,432,384]{2,1,0:T(8,128)(2,1)} %collective-permute-done.16.refs_1_, ...), custom_call_target="tpu_custom_call" | custom-call | bytes 21233664 | tf_op jit(solution)/shard_map/pallas_call | solution.py:817
  172.2 14.8 %collective-permute-done.21 = bf16[768,384]{1,0:T(8,128)(2,1)} collective-permute-done((bf16[768,384]{1,0:T(8,128)(2,1)}, bf16[768,384]{1,0:T(8,128)(2,1)}, u32[]{:S(2)}, u32[]{:S(2)}) %collective-permute-start.21) | collective-permute-done | bytes 589856 | tf_op jit(solution)/shard_map/ppermute | solution.py:750
  187.0 12.6 %collective-permute-done.22 = bf16[768,384]{1,0:T(8,128)(2,1)} collective-permute-done((bf16[768,384]{1,0:T(8,128)(2,1)}, bf16[768,384]{1,0:T(8,128)(2,1)}, u32[]{:S(2)}, u32[]{:S(2)}) %collective-permute-start.22) | collective-permute-done | bytes 589856 | tf_op jit(solution)/shard_map/ppermute | solution.py:750
  203.3 28.0 %shard_map.279 = (bf16[1024,768]{1,0:T(8,128)(2,1)}, bf16[1024,3072]{1,0:T(8,128)(2,1)}, bf16[1024,3072]{1,0:T(8,128)(2,1)}, f32[1024,768]{1,0:T(8,128)}, f32[10...) custom-call(bf16[1024,768]{1,0:T(8,128)(2,1)} %get-tuple-element.232, ...), custom_call_target="tpu_custom_call" | custom-call | flops 27179089920 | bytes 12189696 | tf_op jit(solution)/shard_map/pallas_call | solution.py:474
  231.3 7.8 %shard_map.281.query_ref.key_ref.value_ref = bf16[1024,2304]{1,0:T(8,128)(2,1)} custom-call(bf16[1024,768]{1,0:T(8,128)(2,1)} %get-tuple-element.236.rows_ref.left_ref, bf16[768,2304]{1,0:T(8,128)(2,1)} %bitcast.128, f32[1,2304]{1,0:T(1,128)} %broadcast_in_dim.5.bias_ref), custom_call_target="tpu_custom_call" | custom-call | flops 4348654592 | bytes 5111808 | tf_op jit(solution)/shard_map/pallas_call | solution.py:458
  239.1 18.1 %shard_map.282 = (bf16[1024,768]{1,0:T(8,128)(2,1)}, bf16[1,12,1024,128]{3,2,1,0:T(8,128)(2,1)}, bf16[1,12,1024,128]{3,2,1,0:T(8,128)(2,1)}, bf16[1,12,1024,128]{3,2,1,0:T(8,128)(2,1)}) custom-call(s32[1,6,2,1024]{3,2,1,0:T(2,128)} %get-tuple-element.203.slot_ref, bf16[1024,2304]{1,0:T(8,128)(2,1)} %shard_map.281.query_ref.key_ref.value_ref, ...), custom_call_target="tpu_custom_call" | custom-call | flops 15000000512 | bytes 10000000 | tf_op jit(solution)/shard_map/pallas_call | solution.py:158
  261.4 17.7 %shard_map.283 = (bf16[1024,768]{1,0:T(8,128)(2,1)}, bf16[1,12,1024,128]{3,2,1,0:T(8,128)(2,1)}, bf16[1,12,1024,128]{3,2,1,0:T(8,128)(2,1)}, bf16[1,12,1024,128]{3,2,1,0:T(8,128)(2,1)}) custom-call(s32[1,6,2,1024]{3,2,1,0:T(2,128)} %get-tuple-element.203.slot_ref, ...), custom_call_target="tpu_custom_call", output_to_operand_aliasing={{0}: (5, {}), {1}: (6, {}), {2}: (7, {}), {3}: (8, {})} | custom-call | flops 15000000512 | bytes 10000000 | tf_op jit(solution)/shard_map/pallas_call | solution.py:158
  279.1 8.4 %shard_map.284 = (bf16[8,1,96,3072]{3,2,1,0:T(8,128)(2,1)}, bf16[8,1,384,768]{3,2,1,0:T(8,128)(2,1)}) custom-call(s32[4]{0:T(128)} %pad_add_fusion.at_ref.refs_1_, bf16[4,768,384]{2,1,0:T(8,128)(2,1)} %copy-done.2, bf16[4,768,384]{2,1,0:T(8,128)(2,1)} %collective-permute-done.26.refs_1_, bf16[4,768,384]{2,1,0:T(8,128)(2,1)} %collective-permute-done.25.refs_2_, ...), custom_call_target="tpu_custom_call" | custom-call | bytes 18874368 | tf_op jit(solution)/shard_map/pallas_call | solution.py:817
  287.5 27.9 %shard_map.285 = (bf16[1024,768]{1,0:T(8,128)(2,1)}, bf16[1024,3072]{1,0:T(8,128)(2,1)}, bf16[1024,3072]{1,0:T(8,128)(2,1)}, f32[1024,768]{1,0:T(8,128)}, f32[10...) custom-call(bf16[1024,768]{1,0:T(8,128)(2,1)} %get-tuple-element.255, ...), custom_call_target="tpu_custom_call" | custom-call | flops 27179089920 | bytes 12189696 | tf_op jit(solution)/shard_map/pallas_call | solution.py:474
  315.5 21.9 %shard_map.286 = (bf16[1024,768]{1,0:T(8,128)(2,1)}, bf16[1024,3072]{1,0:T(8,128)(2,1)}, f32[1024,768]{1,0:T(8,128)}, bf16[1024,768]{1,0:T(8,128)(2,1)}, bf16[10...) custom-call(bf16[1024,768]{1,0:T(8,128)(2,1)} %refs_0_.3, f32[1024,768]{1,0:T(8,128)} %get-tuple-element.261.refs_1_, ...), custom_call_target="tpu_custom_call" | custom-call | flops 27179089920 | bytes 12189696 | tf_op jit(solution)/shard_map/pallas_call | solution.py:521
  337.3 7.6 %shard_map.288 = bf16[4,4,2,96,384]{4,3,2,1,0:T(8,128)(2,1)} custom-call(s32[4]{0:T(128)} %pad_add_fusion.at_ref.refs_1_, bf16[1024,768]{1,0:T(8,128)(2,1)} %get-tuple-element.270.left_ref, bf16[1024,3072]{1,0:T(8,128)(2,1)} %get-tuple-element.271.right_ref), custom_call_target="tpu_custom_call" | custom-call | flops 4831838208 | bytes 7864320 | tf_op jit(solution)/shard_map/pallas_call | solution.py:665
  345.4 7.9 %shard_map.287 = bf16[1,4,2,384,384]{4,3,2,1,0:T(8,128)(2,1)} custom-call(s32[4]{0:T(128)} %pad_add_fusion.at_ref.refs_1_, bf16[1024,3072]{1,0:T(8,128)(2,1)} %get-tuple-element.268.left_ref, bf16[1024,768]{1,0:T(8,128)(2,1)} %get-tuple-element.269.right_ref), custom_call_target="tpu_custom_call" | custom-call | flops 4831838208 | bytes 7864320 | tf_op jit(solution)/shard_map/pallas_call | solution.py:665
  353.4 4.1 shard_map.289
  357.9 1.8 collective-permute-done.30.refs_0_
  359.8 18.9 %shard_map.293 = (bf16[3,1024,384]{2,1,0:T(8,128)(2,1)}, f32[1,3,8,128]{3,2,1,0:T(8,128)}) custom-call(s32[4]{0:T(128)} %pad_add_fusion.at_ref.refs_1_, s32[1,6,2,1024]{3,2,1,0:T(2,128)} %get-tuple-element.203.slot_ref, bf16[1024,768]{1,0:T(8,128)(2,1)} %get-tuple-element.286.grad_ref, bf16[1,12,1024,128]{3,2,1,0:T(8,128)(2,1)} %get-tuple-element.282.qk_ref, ...), custom_call_target="tpu_custom_call" | custom-call | flops 16999999488 | bytes 10000000 | tf_op jit(solution)/shard_map/pallas_call | solution.py:195
  378.7 6.5 shard_map.295
  385.6 8.6 %shard_map.290 = (bf16[4,864,384]{2,1,0:T(8,128)(2,1)}, bf16[4,864,384]{2,1,0:T(8,128)(2,1)}) custom-call(s32[4]{0:T(128)} %pad_add_fusion.at_ref.refs_1_, bf16[1024,3072]{1,0:T(8,128)(2,1)} %get-tuple-element.268.left_ref, bf16[1024,768]{1,0:T(8,128)(2,1)} %get-tuple-element.269.right_ref, bf16[1,4,2,384,384]{4,3,2,1,0:T(8,128)(2,1)} %collective-permute-done.28.refs_0_), custom_call_target="tpu_custom_call" | custom-call | flops 4831838208 | bytes 7864320 | tf_op jit(solution)/shard_map/pallas_call | solution.py:665
  394.2 8.2 %shard_map.291 = (bf16[4,864,384]{2,1,0:T(8,128)(2,1)}, bf16[4,864,384]{2,1,0:T(8,128)(2,1)}) custom-call(s32[4]{0:T(128)} %pad_add_fusion.at_ref.refs_1_, bf16[1024,768]{1,0:T(8,128)(2,1)} %get-tuple-element.270.left_ref, bf16[1024,3072]{1,0:T(8,128)(2,1)} %get-tuple-element.271.right_ref, ...), custom_call_target="tpu_custom_call", output_to_operand_aliasing={{0}: (4, {}), {1}: (5, {})} | custom-call | flops 4831838208 | bytes 7864320 | tf_op jit(solution)/shard_map/pallas_call | solution.py:665
  402.5 4.3 shard_map.292
  407.0 18.6 %shard_map.294 = (bf16[3,1024,384]{2,1,0:T(8,128)(2,1)}, f32[1,3,8,128]{3,2,1,0:T(8,128)}) custom-call(s32[4]{0:T(128)} %pad_add_fusion.at_ref.refs_1_, s32[1,6,2,1024]{3,2,1,0:T(2,128)} %get-tuple-element.203.slot_ref, bf16[1024,768]{1,0:T(8,128)(2,1)} %get-tuple-element.286.grad_ref, bf16[1,12,1024,128]{3,2,1,0:T(8,128)(2,1)} %get-tuple-element.282.qk_ref, ...), custom_call_target="tpu_custom_call" | custom-call | flops 16999999488 | bytes 10000000 | tf_op jit(solution)/shard_map/pallas_call | solution.py:195
  425.7 7.0 shard_map.297
  432.9 31.8 %shard_map.296 = (bf16[1024,768]{1,0:T(8,128)(2,1)}, bf16[1024,3072]{1,0:T(8,128)(2,1)}, f32[1024,768]{1,0:T(8,128)}, bf16[1024,768]{1,0:T(8,128)(2,1)}, bf16[10...) custom-call(f32[1024,768]{1,0:T(8,128)} %get-tuple-element.280.refs_0_, s32[4]{0:T(128)} %pad_add_fusion.at_ref.refs_1_, ...), custom_call_target="tpu_custom_call" | custom-call | flops 27179089920 | bytes 13762560 | tf_op jit(solution)/shard_map/pallas_call | solution.py:521
  464.7 6.5 shard_map.302
  471.9 8.4 %shard_map.300 = bf16[1,4,2,384,384]{4,3,2,1,0:T(8,128)(2,1)} custom-call(s32[4]{0:T(128)} %pad_add_fusion.at_ref.refs_1_, bf16[1024,3072]{1,0:T(8,128)(2,1)} %get-tuple-element.305.left_ref, bf16[1024,768]{1,0:T(8,128)(2,1)} %get-tuple-element.306.right_ref), custom_call_target="tpu_custom_call" | custom-call | flops 4831838208 | bytes 7864320 | tf_op jit(solution)/shard_map/pallas_call | solution.py:665
  480.4 4.2 shard_map.301
  485.1 4.0 shard_map.299
  491.0 5.5 shard_map.298
  496.5 3.2 collective-permute-start.42
  501.8 2.9 shard_map.304
  504.7 3.3 collective-permute-start.39
  507.9 7.2 shard_map.308
  515.1 8.4 %shard_map.306 = (bf16[4,480,384]{2,1,0:T(8,128)(2,1)}, bf16[4,480,384]{2,1,0:T(8,128)(2,1)}) custom-call(s32[4]{0:T(128)} %pad_add_fusion.at_ref.refs_1_, bf16[1024,3072]{1,0:T(8,128)(2,1)} %get-tuple-element.305.left_ref, bf16[1024,768]{1,0:T(8,128)(2,1)} %get-tuple-element.306.right_ref, bf16[1,4,2,384,384]{4,3,2,1,0:T(8,128)(2,1)} %collective-permute-done.35.refs_0_), custom_call_target="tpu_custom_call" | custom-call | flops 4831838208 | bytes 7864320 | tf_op jit(solution)/shard_map/pallas_call | solution.py:665
  523.6 18.6 %shard_map.303 = (bf16[3,1024,384]{2,1,0:T(8,128)(2,1)}, f32[1,3,8,128]{3,2,1,0:T(8,128)}) custom-call(s32[4]{0:T(128)} %pad_add_fusion.at_ref.refs_1_, s32[1,6,2,1024]{3,2,1,0:T(2,128)} %get-tuple-element.203.slot_ref, bf16[1024,768]{1,0:T(8,128)(2,1)} %get-tuple-element.319.grad_ref, bf16[1,12,1024,128]{3,2,1,0:T(8,128)(2,1)} %get-tuple-element.311.qk_ref, ...), custom_call_target="tpu_custom_call" | custom-call | flops 16999999488 | bytes 10000000 | tf_op jit(solution)/shard_map/pallas_call | solution.py:195
  542.2 4.3 shard_map.307
  546.5 2.9 collective-permute-done.38.refs_1_
  551.5 6.5 shard_map.310
  558.1 1.8 collective-permute-start.49
  559.9 19.0 %shard_map.305 = (bf16[3,1024,384]{2,1,0:T(8,128)(2,1)}, f32[1,3,8,128]{3,2,1,0:T(8,128)}) custom-call(s32[4]{0:T(128)} %pad_add_fusion.at_ref.refs_1_, s32[1,6,2,1024]{3,2,1,0:T(2,128)} %get-tuple-element.203.slot_ref, bf16[1024,768]{1,0:T(8,128)(2,1)} %get-tuple-element.319.grad_ref, bf16[1,12,1024,128]{3,2,1,0:T(8,128)(2,1)} %get-tuple-element.311.qk_ref, ...), custom_call_target="tpu_custom_call" | custom-call | flops 16999999488 | bytes 10000000 | tf_op jit(solution)/shard_map/pallas_call | solution.py:195
  583.6 2.4 shard_map.309
  592.3 7.0 collective-permute-done.43.refs_3_
  602.5 2.4 collective-permute-done.48
  605.6 6.9 shard_map.313
  612.6 9.6 %shard_map.312 = f32[1024,768]{1,0:T(8,128)} custom-call(f32[1024,768]{1,0:T(8,128)} %get-tuple-element.347.above_ref, s32[4]{0:T(128)} %pad_add_fusion.at_ref.refs_1_, bf16[3,1024,384]{2,1,0:T(8,128)(2,1)} %get-tuple-element.348.own_ref.right_ref, bf16[3,1024,384]{2,1,0:T(8,128)(2,1)} %get-tuple-element.349.right_ref.away_ref, bf16[768,2304]{1,0:T(8,128)(2,1)} %bitcast.85), custom_call_target="tpu_custom_call" | custom-call | flops 4348654592 | bytes 6684672 | tf_op jit(solution)/shard_map/pallas_call | solution.py:553
  622.2 4.2 shard_map.311.refs_6_
  626.4 94.7 %shard_map.314 = (bf16[480,384]{1,0:T(8,128)(2,1)}, bf16[480,384]{1,0:T(8,128)(2,1)}, bf16[4,2,48,768]{3,2,1,0:T(8,128)(2,1)}, bf16[4,3,48,384]{3,2,1,0:T(8,128)...) custom-call(bf16[4,480,384]{2,1,0:T(8,128)(2,1)} %copy-done.7, ...), custom_call_target="tpu_custom_call" | custom-call | bytes 200000000 | tf_op jit(solution)/shard_map/pallas_call | solution.py:1165
  722.8 2.0 fusion.13
  724.7 1.8 fusion.14
  731.6 6.1 shard_map.315
  (243 shorter events, 75.0 us)
Async XLA Ops:
  2.7 9.8 %collective-permute-start = (bf16[112,1152]{1,0:T(8,128)(2,1)S(1)}, bf16[112,1152]{1,0:T(8,128)(2,1)S(1)}, u32[]{:S(2)}, u32[]{:S(2)}) collective-permute-start(bf16[112,1152]{1,0:T(8,128)(2,1)S(1)} %get-tuple-element.403), channel_id=1, source_target_pairs={{0,2},{1,3},{2,4},{3,5},{4,6},{5,7},{6,0},{7,1},{8,10},{9,11},{10,... | collective-permute-start | bytes 774152 | tf_op jit(solution)/shard_map/ppermute | solution.py:750
  4.0 17.0 %collective-permute-start.1 = (bf16[112,1152]{1,0:T(8,128)(2,1)S(1)}, bf16[112,1152]{1,0:T(8,128)(2,1)S(1)}, u32[]{:S(2)}, u32[]{:S(2)}) collective-permute-start(bf16[112,1152]{1,0:T(8,128)(2,1)S(1)} %get-tuple-element.403), channel_id=1, source_target_pairs={{0,4},{1,5},{2,6},{3,7},{4,0},{5,1},{6,2},{7,3},{8,12},{9,13},{10,... | collective-permute-start | bytes 774152 | tf_op jit(solution)/shard_map/ppermute | solution.py:750
  4.1 36.5 %collective-permute-start.2 = (bf16[112,1152]{1,0:T(8,128)(2,1)S(1)}, bf16[112,1152]{1,0:T(8,128)(2,1)S(1)}, u32[]{:S(2)}, u32[]{:S(2)}) collective-permute-start(bf16[112,1152]{1,0:T(8,128)(2,1)S(1)} %get-tuple-element.403), channel_id=1, source_target_pairs={{0,6},{1,7},{2,0},{3,1},{4,2},{5,3},{6,4},{7,5},{8,14},{9,15},{10,... | collective-permute-start | bytes 774152 | tf_op jit(solution)/shard_map/ppermute | solution.py:750
  5.9 37.0 %copy-start.30 = (s32[12,1024]{1,0:T(8,128)S(1)}, s32[12,1024]{1,0:T(8,128)}, u32[]{:S(2)}) copy-start(s32[12,1024]{1,0:T(8,128)} %param.21) | copy-start | bytes 147460
  9.8 66.4 %collective-permute-start.6 = (bf16[432,384]{1,0:T(8,128)(2,1)}, bf16[432,384]{1,0:T(8,128)(2,1)}, u32[]{:S(2)}, u32[]{:S(2)}) collective-permute-start(bf16[432,384]{1,0:T(8,128)(2,1)} %get-tuple-element.194), channel_id=1, source_target_pairs={{0,2},{1,3},{2,4},{3,5},{4,6},{5,7},{6,0},{7,1},{8,10},{9,11},{10,... | collective-permute-start | bytes 995336 | tf_op jit(solution)/shard_map/ppermute | solution.py:750
  10.0 66.4 %collective-permute-start.7 = (bf16[432,384]{1,0:T(8,128)(2,1)}, bf16[432,384]{1,0:T(8,128)(2,1)}, u32[]{:S(2)}, u32[]{:S(2)}) collective-permute-start(bf16[432,384]{1,0:T(8,128)(2,1)} %get-tuple-element.194), channel_id=1, source_target_pairs={{0,4},{1,5},{2,6},{3,7},{4,0},{5,1},{6,2},{7,3},{8,12},{9,13},{10,... | collective-permute-start | bytes 995336 | tf_op jit(solution)/shard_map/ppermute | solution.py:750
  12.4 64.0 %collective-permute-start.8 = (bf16[432,384]{1,0:T(8,128)(2,1)}, bf16[432,384]{1,0:T(8,128)(2,1)}, u32[]{:S(2)}, u32[]{:S(2)}) collective-permute-start(bf16[432,384]{1,0:T(8,128)(2,1)} %get-tuple-element.194), channel_id=1, source_target_pairs={{0,6},{1,7},{2,0},{3,1},{4,2},{5,3},{6,4},{7,5},{8,14},{9,15},{10,... | collective-permute-start | bytes 995336 | tf_op jit(solution)/shard_map/ppermute | solution.py:750
  40.7 21.9 %copy-start.5 = (bf16[4,112,1152]{2,1,0:T(8,128)(2,1)}, bf16[4,112,1152]{2,1,0:T(8,128)(2,1)S(1)}, u32[]{:S(2)}) copy-start(bf16[4,112,1152]{2,1,0:T(8,128)(2,1)S(1)} %pad_maximum_fusion.3.refs_0_) | copy-start | bytes 3096580
  40.7 23.8 %collective-permute-start.3 = (bf16[4,112,1152]{2,1,0:T(8,128)(2,1)S(1)}, bf16[4,112,1152]{2,1,0:T(8,128)(2,1)S(1)}, u32[]{:S(2)}, u32[]{:S(2)}) collective-permute-start(bf16[4,112,1152]{2,1,0:T(8,128)(2,1)S(1)} %pad_maximum_fusion.3.refs_0_), channel_id=1, source_target_pairs={{0,1},{1,0},{2,3},{3,2},{4,5},{5,4},{6,7},{7,6},{8,9},{9,8},{10,11... | collective-permute-start | bytes 3096584 | tf_op jit(solution)/shard_map/ppermute | solution.py:750
  42.0 25.4 %collective-permute-start.4 = (bf16[4,112,1152]{2,1,0:T(8,128)(2,1)S(1)}, bf16[4,112,1152]{2,1,0:T(8,128)(2,1)S(1)}, u32[]{:S(2)}, u32[]{:S(2)}) collective-permute-start(bf16[4,112,1152]{2,1,0:T(8,128)(2,1)S(1)} %pad_maximum_fusion.3.refs_0_), channel_id=1, source_target_pairs={{0,8},{1,9},{2,10},{3,11},{4,12},{5,13},{6,14},{7,15},{8,0},{9,1},... | collective-permute-start | bytes 3096584 | tf_op jit(solution)/shard_map/ppermute | solution.py:750
  64.6 3.8 collective-permute-start.5
  66.4 75.2 %copy-start.18 = (f32[8,2,1152]{2,1,0:T(2,128)}, f32[8,2,1152]{2,1,0:T(2,128)S(1)}, u32[]{:S(2)}) copy-start(f32[8,2,1152]{2,1,0:T(2,128)S(1)} %multiply_reduce_fusion) | copy-start | bytes 221188
  67.4 38.5 %collective-permute-start.10 = (bf16[384,384]{1,0:T(8,128)(2,1)}, bf16[384,384]{1,0:T(8,128)(2,1)S(1)}, u32[]{:S(2)}, u32[]{:S(2)}) collective-permute-start(bf16[384,384]{1,0:T(8,128)(2,1)} %get-tuple-element.214), channel_id=1, source_target_pairs={{0,2},{1,3},{2,4},{3,5},{4,6},{5,7},{6,0},{7,1},{8,10},{9,11},{10,... | collective-permute-start | bytes 884744 | tf_op jit(solution)/shard_map/ppermute | solution.py:750
  68.4 38.7 %collective-permute-start.11 = (bf16[384,384]{1,0:T(8,128)(2,1)}, bf16[384,384]{1,0:T(8,128)(2,1)S(1)}, u32[]{:S(2)}, u32[]{:S(2)}) collective-permute-start(bf16[384,384]{1,0:T(8,128)(2,1)} %get-tuple-element.214), channel_id=1, source_target_pairs={{0,4},{1,5},{2,6},{3,7},{4,0},{5,1},{6,2},{7,3},{8,12},{9,13},{10,... | collective-permute-start | bytes 884744 | tf_op jit(solution)/shard_map/ppermute | solution.py:750
  76.2 31.0 %collective-permute-start.12 = (bf16[384,384]{1,0:T(8,128)(2,1)S(1)}, bf16[384,384]{1,0:T(8,128)(2,1)S(1)}, u32[]{:S(2)}, u32[]{:S(2)}) collective-permute-start(bf16[384,384]{1,0:T(8,128)(2,1)S(1)} %copy-done.20), channel_id=1, source_target_pairs={{0,6},{1,7},{2,0},{3,1},{4,2},{5,3},{6,4},{7,5},{8,14},{9,15},{10,... | collective-permute-start | bytes 884744 | tf_op jit(solution)/shard_map/ppermute | solution.py:750
  77.8 28.1 %copy-start.4 = (bf16[4,432,384]{2,1,0:T(8,128)(2,1)}, bf16[4,432,384]{2,1,0:T(8,128)(2,1)S(1)}, u32[]{:S(2)}) copy-start(bf16[4,432,384]{2,1,0:T(8,128)(2,1)S(1)} %pad_maximum_fusion.1.refs_0_) | copy-start | bytes 3981316
  77.8 30.3 %collective-permute-start.9 = (bf16[4,432,384]{2,1,0:T(8,128)(2,1)S(1)}, bf16[4,432,384]{2,1,0:T(8,128)(2,1)S(1)}, u32[]{:S(2)}, u32[]{:S(2)}) collective-permute-start(bf16[4,432,384]{2,1,0:T(8,128)(2,1)S(1)} %pad_maximum_fusion.1.refs_0_), channel_id=1, source_target_pairs={{0,1},{1,0},{2,3},{3,2},{4,5},{5,4},{6,7},{7,6},{8,9},{9,8},{10,11... | collective-permute-start | bytes 3981320 | tf_op jit(solution)/shard_map/ppermute | solution.py:750
  79.1 61.8 %collective-permute-start.14 = (bf16[4,432,384]{2,1,0:T(8,128)(2,1)S(1)}, bf16[4,432,384]{2,1,0:T(8,128)(2,1)}, u32[]{:S(2)}, u32[]{:S(2)}) collective-permute-start(bf16[4,432,384]{2,1,0:T(8,128)(2,1)S(1)} %pad_maximum_fusion.1.refs_0_), channel_id=1, source_target_pairs={{0,16},{1,17},{2,18},{3,19},{4,20},{5,21},{6,22},{7,23},{8,24},{9,... | collective-permute-start | bytes 3981320 | tf_op jit(solution)/shard_map/ppermute | solution.py:750
  106.0 35.5 %collective-permute-start.16 = (bf16[4,432,384]{2,1,0:T(8,128)(2,1)S(1)}, bf16[4,432,384]{2,1,0:T(8,128)(2,1)}, u32[]{:S(2)}, u32[]{:S(2)}) collective-permute-start(bf16[4,432,384]{2,1,0:T(8,128)(2,1)S(1)} %pad_maximum_fusion.1.refs_0_), channel_id=1, source_target_pairs={{0,8},{1,9},{2,10},{3,11},{4,12},{5,13},{6,14},{7,15},{8,0},{9,1},... | collective-permute-start | bytes 3981320 | tf_op jit(solution)/shard_map/ppermute | solution.py:750
  108.1 23.3 %copy-start.9 = (bf16[4,432,384]{2,1,0:T(8,128)(2,1)}, bf16[4,432,384]{2,1,0:T(8,128)(2,1)S(1)}, u32[]{:S(2)}) copy-start(bf16[4,432,384]{2,1,0:T(8,128)(2,1)S(1)} %collective-permute-done.9.refs_2_) | copy-start | bytes 3981316
  108.1 32.9 %collective-permute-start.15 = (bf16[4,432,384]{2,1,0:T(8,128)(2,1)S(1)}, bf16[4,432,384]{2,1,0:T(8,128)(2,1)}, u32[]{:S(2)}, u32[]{:S(2)}) collective-permute-start(bf16[4,432,384]{2,1,0:T(8,128)(2,1)S(1)} %collective-permute-done.9.refs_2_), channel_id=1, source_target_pairs={{0,16},{1,17},{2,18},{3,19},{4,20},{5,21},{6,22},{7,23},{8,24},{9,... | collective-permute-start | bytes 3981320 | tf_op jit(solution)/shard_map/ppermute | solution.py:750
  109.4 36.4 %collective-permute-start.17 = (bf16[4,432,384]{2,1,0:T(8,128)(2,1)S(1)}, bf16[4,432,384]{2,1,0:T(8,128)(2,1)}, u32[]{:S(2)}, u32[]{:S(2)}) collective-permute-start(bf16[4,432,384]{2,1,0:T(8,128)(2,1)S(1)} %collective-permute-done.9.refs_2_), channel_id=1, source_target_pairs={{0,8},{1,9},{2,10},{3,11},{4,12},{5,13},{6,14},{7,15},{8,0},{9,1},... | collective-permute-start | bytes 3981320 | tf_op jit(solution)/shard_map/ppermute | solution.py:750
  112.4 27.8 %copy-start.6 = (bf16[4,384,384]{2,1,0:T(8,128)(2,1)}, bf16[4,384,384]{2,1,0:T(8,128)(2,1)S(1)}, u32[]{:S(2)}) copy-start(bf16[4,384,384]{2,1,0:T(8,128)(2,1)S(1)} %pad_maximum_fusion.2.refs_0_) | copy-start | bytes 3538948
  112.4 27.8 %collective-permute-start.13 = (bf16[4,384,384]{2,1,0:T(8,128)(2,1)S(1)}, bf16[4,384,384]{2,1,0:T(8,128)(2,1)}, u32[]{:S(2)}, u32[]{:S(2)}) collective-permute-start(bf16[4,384,384]{2,1,0:T(8,128)(2,1)S(1)} %pad_maximum_fusion.2.refs_0_), channel_id=1, source_target_pairs={{0,1},{1,0},{2,3},{3,2},{4,5},{5,4},{6,7},{7,6},{8,9},{9,8},{10,11... | collective-permute-start | bytes 3538952 | tf_op jit(solution)/shard_map/ppermute | solution.py:750
  140.2 4.2 collective-permute-start.23
  141.0 7.4 %collective-permute-start.24 = (bf16[4,384,384]{2,1,0:T(8,128)(2,1)}, bf16[4,384,384]{2,1,0:T(8,128)(2,1)}, u32[]{:S(2)}, u32[]{:S(2)}) collective-permute-start(bf16[4,384,384]{2,1,0:T(8,128)(2,1)} %collective-permute-done.13.refs_2_), channel_id=1, source_target_pairs={{0,8},{1,9},{2,10},{3,11},{4,12},{5,13},{6,14},{7,15},{8,0},{9,1},... | collective-permute-start | bytes 3538952 | tf_op jit(solution)/shard_map/ppermute | solution.py:750
  141.0 22.0 %collective-permute-start.18 = (bf16[4,432,384]{2,1,0:T(8,128)(2,1)}, bf16[4,432,384]{2,1,0:T(8,128)(2,1)}, u32[]{:S(2)}, u32[]{:S(2)}) collective-permute-start(bf16[4,432,384]{2,1,0:T(8,128)(2,1)} %collective-permute-done.14.refs_4_), channel_id=1, source_target_pairs={{0,8},{1,9},{2,10},{3,11},{4,12},{5,13},{6,14},{7,15},{8,0},{9,1},... | collective-permute-start | bytes 3981320 | tf_op jit(solution)/shard_map/ppermute | solution.py:750
  141.5 21.6 %collective-permute-start.19 = (bf16[4,432,384]{2,1,0:T(8,128)(2,1)}, bf16[4,432,384]{2,1,0:T(8,128)(2,1)}, u32[]{:S(2)}, u32[]{:S(2)}) collective-permute-start(bf16[4,432,384]{2,1,0:T(8,128)(2,1)} %collective-permute-done.15.refs_6_), channel_id=1, source_target_pairs={{0,8},{1,9},{2,10},{3,11},{4,12},{5,13},{6,14},{7,15},{8,0},{9,1},... | collective-permute-start | bytes 3981320 | tf_op jit(solution)/shard_map/ppermute | solution.py:750
  144.4 27.8 %collective-permute-start.20 = (bf16[768,384]{1,0:T(8,128)(2,1)}, bf16[768,384]{1,0:T(8,128)(2,1)S(1)}, u32[]{:S(2)}, u32[]{:S(2)}) collective-permute-start(bf16[768,384]{1,0:T(8,128)(2,1)} %get-tuple-element.231), channel_id=1, source_target_pairs={{0,2},{1,3},{2,4},{3,5},{4,6},{5,7},{6,0},{7,1},{8,10},{9,11},{10,... | collective-permute-start | bytes 1769480 | tf_op jit(solution)/shard_map/ppermute | solution.py:750
  145.8 41.2 %collective-permute-start.21 = (bf16[768,384]{1,0:T(8,128)(2,1)}, bf16[768,384]{1,0:T(8,128)(2,1)}, u32[]{:S(2)}, u32[]{:S(2)}) collective-permute-start(bf16[768,384]{1,0:T(8,128)(2,1)} %get-tuple-element.231), channel_id=1, source_target_pairs={{0,4},{1,5},{2,6},{3,7},{4,0},{5,1},{6,2},{7,3},{8,12},{9,13},{10,... | collective-permute-start | bytes 1769480 | tf_op jit(solution)/shard_map/ppermute | solution.py:750
  148.4 51.2 %collective-permute-start.22 = (bf16[768,384]{1,0:T(8,128)(2,1)}, bf16[768,384]{1,0:T(8,128)(2,1)}, u32[]{:S(2)}, u32[]{:S(2)}) collective-permute-start(bf16[768,384]{1,0:T(8,128)(2,1)} %get-tuple-element.231), channel_id=1, source_target_pairs={{0,6},{1,7},{2,0},{3,1},{4,2},{5,3},{6,4},{7,5},{8,14},{9,15},{10,... | collective-permute-start | bytes 1769480 | tf_op jit(solution)/shard_map/ppermute | solution.py:750
  163.0 36.6 %copy-start.15 = (bf16[768,384]{1,0:T(8,128)(2,1)S(1)}, bf16[768,384]{1,0:T(8,128)(2,1)}, u32[]{:S(2)}) copy-start(bf16[768,384]{1,0:T(8,128)(2,1)} %get-tuple-element.231) | copy-start | bytes 1769476
  201.2 30.0 %copy-start.2 = (bf16[4,768,384]{2,1,0:T(8,128)(2,1)}, bf16[4,768,384]{2,1,0:T(8,128)(2,1)S(1)}, u32[]{:S(2)}) copy-start(bf16[4,768,384]{2,1,0:T(8,128)(2,1)S(1)} %pad_maximum_fusion.refs_0_) | copy-start | bytes 7077892
  201.3 56.0 %collective-permute-start.25 = (bf16[4,768,384]{2,1,0:T(8,128)(2,1)S(1)}, bf16[4,768,384]{2,1,0:T(8,128)(2,1)}, u32[]{:S(2)}, u32[]{:S(2)}) collective-permute-start(bf16[4,768,384]{2,1,0:T(8,128)(2,1)S(1)} %pad_maximum_fusion.refs_0_), channel_id=1, source_target_pairs={{0,1},{1,0},{2,3},{3,2},{4,5},{5,4},{6,7},{7,6},{8,9},{9,8},{10,11... | collective-permute-start | bytes 7077896 | tf_op jit(solution)/shard_map/ppermute | solution.py:750
  202.5 76.6 %collective-permute-start.26 = (bf16[4,768,384]{2,1,0:T(8,128)(2,1)S(1)}, bf16[4,768,384]{2,1,0:T(8,128)(2,1)}, u32[]{:S(2)}, u32[]{:S(2)}) collective-permute-start(bf16[4,768,384]{2,1,0:T(8,128)(2,1)S(1)} %pad_maximum_fusion.refs_0_), channel_id=1, source_target_pairs={{0,8},{1,9},{2,10},{3,11},{4,12},{5,13},{6,14},{7,15},{8,0},{9,1},... | collective-permute-start | bytes 7077896 | tf_op jit(solution)/shard_map/ppermute | solution.py:750
  239.1 20.9 %copy-start.37 = (f32[8,96]{1,0:T(8,128)S(1)}, f32[8,96]{1,0:T(8,128)}, u32[]{:S(2)}) copy-start(f32[8,96]{1,0:T(8,128)} %get-tuple-element.421) | copy-start | bytes 9220
  239.1 21.6 %copy-start.36 = (f32[8,96]{1,0:T(8,128)S(1)}, f32[8,96]{1,0:T(8,128)}, u32[]{:S(2)}) copy-start(f32[8,96]{1,0:T(8,128)} %get-tuple-element.382) | copy-start | bytes 9220
  257.3 21.8 %collective-permute-start.27 = (bf16[4,768,384]{2,1,0:T(8,128)(2,1)}, bf16[4,768,384]{2,1,0:T(8,128)(2,1)}, u32[]{:S(2)}, u32[]{:S(2)}) collective-permute-start(bf16[4,768,384]{2,1,0:T(8,128)(2,1)} %collective-permute-done.25.refs_2_), channel_id=1, source_target_pairs={{0,8},{1,9},{2,10},{3,11},{4,12},{5,13},{6,14},{7,15},{8,0},{9,1},... | collective-permute-start | bytes 7077896 | tf_op jit(solution)/shard_map/ppermute | solution.py:750
  345.0 14.8 %collective-permute-start.29 = (bf16[4,4,2,96,384]{4,3,2,1,0:T(8,128)(2,1)}, bf16[4,4,2,96,384]{4,3,2,1,0:T(8,128)(2,1)S(1)}, u32[]{:S(2)}, u32[]{:S(2)}) collective-permute-start(bf16[4,4,2,96,384]{4,3,2,1,0:T(8,128)(2,1)} %shard_map.288), channel_id=1, source_target_pairs={{0,8},{1,9},{2,10},{3,11},{4,12},{5,13},{6,14},{7,15},{8,0},{9,1},... | collective-permute-start | bytes 7077896 | tf_op jit(solution)/shard_map/ppermute | solution.py:750
  353.3 6.5 collective-permute-start.28
  357.5 2.3 collective-permute-start.30
  385.3 40.4 %collective-permute-start.31 = (bf16[3,4,2,96,384]{4,3,2,1,0:T(8,128)(2,1)}, bf16[3,4,2,96,384]{4,3,2,1,0:T(8,128)(2,1)}, u32[]{:S(2)}, u32[]{:S(2)}) collective-permute-start(bf16[3,4,2,96,384]{4,3,2,1,0:T(8,128)(2,1)} %shard_map.295), channel_id=1, source_target_pairs={{0,8},{1,9},{2,10},{3,11},{4,12},{5,13},{6,14},{7,15},{8,0},{9,1},... | collective-permute-start | bytes 5308424 | tf_op jit(solution)/shard_map/ppermute | solution.py:750
  406.8 65.1 %collective-permute-start.32 = (bf16[4,864,384]{2,1,0:T(8,128)(2,1)}, bf16[4,864,384]{2,1,0:T(8,128)(2,1)S(1)}, u32[]{:S(2)}, u32[]{:S(2)}) collective-permute-start(bf16[4,864,384]{2,1,0:T(8,128)(2,1)} %get-tuple-element.297), channel_id=1, source_target_pairs={{0,1},{1,0},{2,3},{3,2},{4,5},{5,4},{6,7},{7,6},{8,9},{9,8},{10,11... | collective-permute-start | bytes 7962632 | tf_op jit(solution)/shard_map/ppermute | solution.py:750
  432.6 39.3 %collective-permute-start.33 = (bf16[3,4,2,48,384]{4,3,2,1,0:T(8,128)(2,1)}, bf16[3,4,2,48,384]{4,3,2,1,0:T(8,128)(2,1)S(1)}, u32[]{:S(2)}, u32[]{:S(2)}) collective-permute-start(bf16[3,4,2,48,384]{4,3,2,1,0:T(8,128)(2,1)} %get-tuple-element.299), channel_id=1, source_target_pairs={{0,16},{1,17},{2,18},{3,19},{4,20},{5,21},{6,22},{7,23},{8,24},{9,... | collective-permute-start | bytes 2654216 | tf_op jit(solution)/shard_map/ppermute | solution.py:750
  471.2 29.9 %collective-permute-start.37 = (bf16[2,4,2,96,768]{4,3,2,1,0:T(8,128)(2,1)}, bf16[2,4,2,96,768]{4,3,2,1,0:T(8,128)(2,1)}, u32[]{:S(2)}, u32[]{:S(2)}) collective-permute-start(bf16[2,4,2,96,768]{4,3,2,1,0:T(8,128)(2,1)} %shard_map.302), channel_id=1, source_target_pairs={{0,8},{1,9},{2,10},{3,11},{4,12},{5,13},{6,14},{7,15},{8,0},{9,1},... | collective-permute-start | bytes 7077896 | tf_op jit(solution)/shard_map/ppermute | solution.py:750
  480.4 20.7 %collective-permute-start.35 = (bf16[1,4,2,384,384]{4,3,2,1,0:T(8,128)(2,1)}, bf16[1,4,2,384,384]{4,3,2,1,0:T(8,128)(2,1)}, u32[]{:S(2)}, u32[]{:S(2)}) collective-permute-start(bf16[1,4,2,384,384]{4,3,2,1,0:T(8,128)(2,1)} %shard_map.300), channel_id=1, source_target_pairs={{0,8},{1,9},{2,10},{3,11},{4,12},{5,13},{6,14},{7,15},{8,0},{9,1},... | collective-permute-start | bytes 7077896 | tf_op jit(solution)/shard_map/ppermute | solution.py:750
  484.6 11.9 %collective-permute-start.36 = (bf16[1,4,2,96,384]{4,3,2,1,0:T(8,128)(2,1)}, bf16[1,4,2,96,384]{4,3,2,1,0:T(8,128)(2,1)S(1)}, u32[]{:S(2)}, u32[]{:S(2)}) collective-permute-start(bf16[1,4,2,96,384]{4,3,2,1,0:T(8,128)(2,1)} %shard_map.301), channel_id=1, source_target_pairs={{0,8},{1,9},{2,10},{3,11},{4,12},{5,13},{6,14},{7,15},{8,0},{9,1},... | collective-permute-start | bytes 1769480 | tf_op jit(solution)/shard_map/ppermute | solution.py:750
  489.1 12.0 %collective-permute-start.34 = (bf16[3,4,48,384]{3,2,1,0:T(8,128)(2,1)}, bf16[3,4,48,384]{3,2,1,0:T(8,128)(2,1)S(1)}, u32[]{:S(2)}, u32[]{:S(2)}) collective-permute-start(bf16[3,4,48,384]{3,2,1,0:T(8,128)(2,1)} %shard_map.299), channel_id=1, source_target_pairs={{0,1},{1,0},{2,3},{3,2},{4,5},{5,4},{6,7},{7,6},{8,9},{9,8},{10,11... | collective-permute-start | bytes 1327112 | tf_op jit(solution)/shard_map/ppermute | solution.py:750
  496.5 85.8 %collective-permute-start.41 = (bf16[864,384]{1,0:T(8,128)(2,1)}, bf16[864,384]{1,0:T(8,128)(2,1)S(1)}, u32[]{:S(2)}, u32[]{:S(2)}) collective-permute-start(bf16[864,384]{1,0:T(8,128)(2,1)} %get-tuple-element.322), channel_id=1, source_target_pairs={{0,2},{1,3},{2,4},{3,5},{4,6},{5,7},{6,0},{7,1},{8,10},{9,11},{10,... | collective-permute-start | bytes 1990664 | tf_op jit(solution)/shard_map/ppermute | solution.py:750
  496.5 93.4 %collective-permute-start.42 = (bf16[864,384]{1,0:T(8,128)(2,1)}, bf16[864,384]{1,0:T(8,128)(2,1)S(1)}, u32[]{:S(2)}, u32[]{:S(2)}) collective-permute-start(bf16[864,384]{1,0:T(8,128)(2,1)} %get-tuple-element.323), channel_id=1, source_target_pairs={{0,4},{1,5},{2,6},{3,7},{4,0},{5,1},{6,2},{7,3},{8,12},{9,13},{10,... | collective-permute-start | bytes 1990664 | tf_op jit(solution)/shard_map/ppermute | solution.py:750
  504.7 44.7 %collective-permute-start.38 = (bf16[3,48,384]{2,1,0:T(8,128)(2,1)}, bf16[3,48,384]{2,1,0:T(8,128)(2,1)S(1)}, u32[]{:S(2)}, u32[]{:S(2)}) collective-permute-start(bf16[3,48,384]{2,1,0:T(8,128)(2,1)} %get-tuple-element.316), channel_id=1, source_target_pairs={{0,2},{1,3},{2,4},{3,5},{4,6},{5,7},{6,0},{7,1},{8,10},{9,11},{10,... | collective-permute-start | bytes 331784 | tf_op jit(solution)/shard_map/ppermute | solution.py:750
  504.7 46.0 %collective-permute-start.39 = (bf16[3,48,384]{2,1,0:T(8,128)(2,1)}, bf16[3,48,384]{2,1,0:T(8,128)(2,1)S(1)}, u32[]{:S(2)}, u32[]{:S(2)}) collective-permute-start(bf16[3,48,384]{2,1,0:T(8,128)(2,1)} %get-tuple-element.317), channel_id=1, source_target_pairs={{0,4},{1,5},{2,6},{3,7},{4,0},{5,1},{6,2},{7,3},{8,12},{9,13},{10,... | collective-permute-start | bytes 331784 | tf_op jit(solution)/shard_map/ppermute | solution.py:750
  507.9 43.6 %collective-permute-start.40 = (bf16[3,48,384]{2,1,0:T(8,128)(2,1)}, bf16[3,48,384]{2,1,0:T(8,128)(2,1)}, u32[]{:S(2)}, u32[]{:S(2)}) collective-permute-start(bf16[3,48,384]{2,1,0:T(8,128)(2,1)} %get-tuple-element.318), channel_id=1, source_target_pairs={{0,6},{1,7},{2,0},{3,1},{4,2},{5,3},{6,4},{7,5},{8,14},{9,15},{10,... | collective-permute-start | bytes 331784 | tf_op jit(solution)/shard_map/ppermute | solution.py:750
  549.4 55.6 %collective-permute-start.45 = (bf16[2,4,2,48,768]{4,3,2,1,0:T(8,128)(2,1)}, bf16[2,4,2,48,768]{4,3,2,1,0:T(8,128)(2,1)S(1)}, u32[]{:S(2)}, u32[]{:S(2)}) collective-permute-start(bf16[2,4,2,48,768]{4,3,2,1,0:T(8,128)(2,1)} %get-tuple-element.331), channel_id=1, source_target_pairs={{0,16},{1,17},{2,18},{3,19},{4,20},{5,21},{6,22},{7,23},{8,24},{9,... | collective-permute-start | bytes 3538952 | tf_op jit(solution)/shard_map/ppermute | solution.py:750
  551.3 53.7 %collective-permute-start.44 = (bf16[4,480,384]{2,1,0:T(8,128)(2,1)}, bf16[4,480,384]{2,1,0:T(8,128)(2,1)S(1)}, u32[]{:S(2)}, u32[]{:S(2)}) collective-permute-start(bf16[4,480,384]{2,1,0:T(8,128)(2,1)} %get-tuple-element.329), channel_id=1, source_target_pairs={{0,1},{1,0},{2,3},{3,2},{4,5},{5,4},{6,7},{7,6},{8,9},{9,8},{10,11... | collective-permute-start | bytes 4423688 | tf_op jit(solution)/shard_map/ppermute | solution.py:750
  558.1 46.9 %collective-permute-start.49 = (bf16[3,4,2,96,384]{4,3,2,1,0:T(8,128)(2,1)}, bf16[3,4,2,96,384]{4,3,2,1,0:T(8,128)(2,1)}, u32[]{:S(2)}, u32[]{:S(2)}) collective-permute-start(bf16[3,4,2,96,384]{4,3,2,1,0:T(8,128)(2,1)} %shard_map.310), channel_id=1, source_target_pairs={{0,8},{1,9},{2,10},{3,11},{4,12},{5,13},{6,14},{7,15},{8,0},{9,1},... | collective-permute-start | bytes 5308424 | tf_op jit(solution)/shard_map/ppermute | solution.py:750
  559.9 27.4 %copy-start.29 = (f32[4608]{0:T(1024)S(1)}, f32[4608]{0:T(1024)}, u32[]{:S(2)}) copy-start(f32[4608]{0:T(1024)} %reshape.224) | copy-start | bytes 55300
  559.9 28.8 %copy-start.38 = (f32[1,3072]{1,0:T(1,128)S(1)}, f32[1,3072]{1,0:T(1,128)}, u32[]{:S(2)}) copy-start(f32[1,3072]{1,0:T(1,128)} %get-tuple-element.344) | copy-start | bytes 36868
  582.2 30.3 %copy-start.13 = (bf16[864,384]{1,0:T(8,128)(2,1)}, bf16[864,384]{1,0:T(8,128)(2,1)S(1)}, u32[]{:S(2)}) copy-start(bf16[864,384]{1,0:T(8,128)(2,1)S(1)} %collective-permute-done.41.refs_1_) | copy-start | bytes 1990660
  582.2 17.0 %collective-permute-start.43 = (bf16[864,384]{1,0:T(8,128)(2,1)}, bf16[864,384]{1,0:T(8,128)(2,1)}, u32[]{:S(2)}, u32[]{:S(2)}) collective-permute-start(bf16[864,384]{1,0:T(8,128)(2,1)} %get-tuple-element.324), channel_id=1, source_target_pairs={{0,6},{1,7},{2,0},{3,1},{4,2},{5,3},{6,4},{7,5},{8,14},{9,15},{10,... | collective-permute-start | bytes 1990664 | tf_op jit(solution)/shard_map/ppermute | solution.py:750
  590.0 22.6 %copy-start.14 = (bf16[864,384]{1,0:T(8,128)(2,1)}, bf16[864,384]{1,0:T(8,128)(2,1)S(1)}, u32[]{:S(2)}) copy-start(bf16[864,384]{1,0:T(8,128)(2,1)S(1)} %collective-permute-done.42.refs_2_) | copy-start | bytes 1990660
  590.0 10.1 %collective-permute-start.46 = (bf16[3,48,384]{2,1,0:T(8,128)(2,1)}, bf16[3,48,384]{2,1,0:T(8,128)(2,1)S(1)}, u32[]{:S(2)}, u32[]{:S(2)}) collective-permute-start(bf16[3,48,384]{2,1,0:T(8,128)(2,1)} %shard_map.309), channel_id=1, source_target_pairs={{0,16},{1,17},{2,18},{3,19},{4,20},{5,21},{6,22},{7,23},{8,24},{9,... | collective-permute-start | bytes 331784 | tf_op jit(solution)/shard_map/ppermute | solution.py:750
  599.3 3.2 collective-permute-start.47
  600.0 5.0 collective-permute-start.48
  (29 other events, 272.6 us)

commit v7 on v6

--- a/solution.py
+++ b/solution.py
@@ -254,12 +254,16 @@
     return jnp.sum(values, axis=0, keepdims=True)
 
 
-def project_kernel(rows_ref, weight_ref, bias_ref, out_ref):
+def project_kernel(layer, rows_ref, weight_ref, bias_ref, out_ref):
     product = jnp.dot(rows_ref[...], weight_ref[...], preferred_element_type=jnp.float32)
-    out_ref[...] = (product + bias_ref[...]).astype(jnp.bfloat16)
+    bias = bias_ref[layer : layer + 1]
+    out_ref[:, :D] = (product[:, :D] + bias[:, :D]).astype(jnp.bfloat16)
+    out_ref[:, D : 2 * D] = product[:, D : 2 * D].astype(jnp.bfloat16)
+    out_ref[:, 2 * D :] = (product[:, 2 * D :] + bias[:, D:]).astype(jnp.bfloat16)
 
 
 def feed_kernel(
+    layer,
     context_ref,
     rows_ref,
     out_weight_ref,
@@ -282,21 +286,22 @@
     result_ref,
     result_low_ref,
 ):
+    here = slice(layer, layer + 1)
     product = jnp.dot(context_ref[...], out_weight_ref[...], preferred_element_type=jnp.float32)
-    attn_sum = rows_ref[...].astype(jnp.float32) + product + out_bias_ref[...]
+    attn_sum = rows_ref[...].astype(jnp.float32) + product + out_bias_ref[here]
     normal, scale = norm_parts(attn_sum)
     attn_normal_ref[...] = normal
     attn_scale_ref[...] = spread(scale)
-    hidden = normal * attn_gain_ref[...] + attn_shift_ref[...]
+    hidden = normal * attn_gain_ref[here] + attn_shift_ref[here]
     hidden_low = hidden.astype(jnp.bfloat16)
     hidden_ref[...] = hidden_low
-    total = hidden + ffout_bias_ref[...]
+    total = hidden + ffout_bias_ref[here]
     width = ffin_weight_ref.shape[1]
     for at in range(0, width, FEED_TILE):
         part = slice(at, at + FEED_TILE)
         pre = (
             jnp.dot(hidden_low, ffin_weight_ref[:, part], preferred_element_type=jnp.float32)
-            + ffin_bias_ref[:, part]
+            + ffin_bias_ref[here, part]
         )
         below, bell = erf_parts(pre)
         act = (pre * below).astype(jnp.bfloat16)
@@ -308,7 +313,7 @@
     normal, scale = norm_parts(total)
     ffn_normal_ref[...] = normal
     ffn_scale_ref[...] = spread(scale)
-    result = normal * ffn_gain_ref[...] + ffn_shift_ref[...]
+    result = normal * ffn_gain_ref[here] + ffn_shift_ref[here]
     result_ref[...] = result
     result_low_ref[...] = result.astype(jnp.bfloat16)
 
@@ -323,7 +328,8 @@
     return grad
 
 
-def feed_back_kernel(with_proj, *refs):
+def feed_back_kernel(layer, with_proj, *refs):
+    here = slice(layer, layer + 1)
     if with_proj:
         above_ref, at_ref, own_ref, away_ref, qkv_weight_ref, *refs = refs
         grad = add_projected(above_ref[...], at_ref, own_ref, away_ref, qkv_weight_ref)
@@ -358,7 +364,7 @@
     normal = ffn_normal_ref[...]
     sums_ref[0:1] += rows_sum(grad * normal)
     sums_ref[1:2] += rows_sum(grad)
-    grad_sum = norm_back(grad, normal, ffn_scale_ref[:, 0:1], ffn_gain_ref[...])
+    grad_sum = norm_back(grad, normal, ffn_scale_ref[:, 0:1], ffn_gain_ref[here])
     down = grad_sum.astype(jnp.bfloat16)
     down_ref[...] = down
     sums_ref[2:3] += rows_sum(down.astype(jnp.float32))
@@ -374,7 +380,7 @@
     normal = attn_normal_ref[...]
     sums_ref[3:4] += rows_sum(total * normal)
     sums_ref[4:5] += rows_sum(total)
-    attn = norm_back(total, normal, attn_scale_ref[:, 0:1], attn_gain_ref[...])
+    attn = norm_back(total, normal, attn_scale_ref[:, 0:1], attn_gain_ref[here])
     attn_ref[...] = attn
     low = attn.astype(jnp.bfloat16)
     attn_low_ref[...] = low
@@ -386,15 +392,14 @@
     out_ref[...] = add_projected(above_ref[...], at_ref, own_ref, away_ref, weight_ref)
 
 
-def prep_kernel(parent_ref, segment_ref, cluster_ref, slot_ref, bias_ref):
-    tree = pl.program_id(0)
-    segs = segment_ref[0]
+def prep_pair(parent_ref, segment_ref, cluster_ref, slot_ref, bias_ref, row, tree, pair):
+    segs = segment_ref[tree]
     length = segs.shape[1]
 
     def parent_of(values):
         found = jnp.zeros_like(values)
         for number in range(SEGMENTS):
-            found = jnp.where(values == number, parent_ref[tree, number], found)
+            found = jnp.where(values == number, parent_ref[row, number], found)
         return found
 
     parents = parent_of(segs)
@@ -406,7 +411,7 @@
     order = lax.broadcasted_iota(jnp.int32, (count, length), 0)
     lanes = lax.broadcasted_iota(jnp.int32, (count, length), 1)
     for head in range(2):
-        member = order == cluster_ref[0, 0, head : head + 1, :]
+        member = order == cluster_ref[tree, pair, head : head + 1, :]
         ranks = member.astype(jnp.int32)
         step = 1
         while step < length:
@@ -415,7 +420,7 @@
         slot = jnp.sum(
             jnp.where(member, ranks - 1 + CLUSTER * order, 0), axis=0, keepdims=True
         )
-        slot_ref[0, 0, head : head + 1, :] = slot
+        slot_ref[tree, pair, head : head + 1, :] = slot
         table = one_hot_rows(slot)
         rows = contract_last(ids, table)
         columns = jnp.concatenate([rows] * (128 // rows.shape[0]), axis=0).T
@@ -425,9 +430,13 @@
             allowed = (
                 (here == block[:, 0:1]) | (here == block[:, 1:2]) | (here == block[:, 2:3])
             )
-            bias_ref[0, head, at : at + CLUSTER, :] = jnp.where(allowed, 0.0, -1e30).astype(
+            bias_ref[tree, 2 * pair + head, at : at + CLUSTER, :] = jnp.where(allowed, 0.0, -1e30).astype(
                 jnp.bfloat16
             )
+
+
+def prep_kernel(*refs):
+    prep_pair(*refs, pl.program_id(0), 0, 0)
 
 
 def row_spec(width, rows=ROW_TILE):
@@ -453,26 +462,25 @@
     return jax.ShapeDtypeStruct((rows, width), kind)
 
 
-def project(rows, weight, bias):
+def project(layer, rows, weight, bias):
     count, width = rows.shape[0], weight.shape[1]
     return pl.pallas_call(
-        project_kernel,
+        functools.partial(project_kernel, layer),
         grid=(count // ROW_TILE,),
-        in_specs=[row_spec(D), whole_spec(weight.shape), whole_spec((1, width))],
+        in_specs=[row_spec(D), whole_spec(weight.shape), whole_spec(bias.shape)],
         out_specs=row_spec(width),
         out_shape=shape_of(count, width),
         compiler_params=kernel_params(),
         cost_estimate=cost(2.4 * count * D * width, rows, weight),
-    )(rows, weight, bias[None])
-
-
-def feed(context, rows, weights, vectors):
+    )(rows, weight, bias)
+
+
+def feed(layer, context, rows, weights, vectors):
     count = context.shape[0]
     width = weights[1].shape[1]
     f32 = jnp.float32
-    vectors = [vector[None] for vector in vectors]
     return pl.pallas_call(
-        feed_kernel,
+        functools.partial(feed_kernel, layer),
         grid=(count // ROW_TILE,),
         in_specs=[row_spec(D), row_spec(D)]
         + [whole_spec(weight.shape) for weight in weights]
@@ -504,11 +512,10 @@
     )(context, rows, *weights, *vectors)
 
 
-def feed_back(above, proj, qkv_weight, at, saved, weights, gains):
+def feed_back(layer, above, proj, qkv_weight, at, saved, weights, gains):
     count = above.shape[0]
     width = weights[1].shape[1]
     f32 = jnp.float32
-    gains = [gain[None] for gain in gains]
     lead, lead_specs = [above], [row_spec(D)]
     if proj is not None:
         lead += [at, *proj, qkv_weight]
@@ -519,7 +526,7 @@
             whole_spec(qkv_weight.shape),
         ]
     return pl.pallas_call(
-        functools.partial(feed_back_kernel, proj is not None),
+        functools.partial(feed_back_kernel, layer, proj is not None),
         grid=(count // ROW_TILE,),
         in_specs=lead_specs
         + [row_spec(D), row_spec(128), row_spec(width), row_spec(D), row_spec(128)]
@@ -710,21 +717,15 @@
 
 
 CHUNKS = {
-    "first": (0, (0,), False),
-    "rest": (0, (2, 6, 8), True),
     "next": (1, (0, 2), False),
     "last": (1, (6, 8), False),
 }
 FORWARD = {
-    "begin": ((), ("first",)),
-    "packed": (("first",), ("rest",)),
-    "prepared": (("first",), ()),
-    "ready": (("rest",), ("next",)),
-    (0, "half"): (("rest", "next"), ("last",)),
-    (0, "context"): (("next",), ()),
-    (0, "waited"): (("rest",), ()),
-    (0, "placed"): (("last",), ()),
-    (1, "half"): (("last",), ()),
+    "ready": ((), ("next",)),
+    (0, "half"): (("next",), ("last",)),
+    (0, "result"): (("next",), ()),
+    (1, "projected"): (("last",), ()),
+    (1, "context"): (("last",), ()),
 }
 
 
@@ -850,8 +851,7 @@
     wholes = place_pieces(
         [item for pair in zip(pieces, others) for item in pair], layout, split_y, place
     )
-    rows = sum(units * tall for units, tall in layout)
-    return wholes, jnp.stack([stack[:, rows:], across[:, rows:]], axis=1)
+    return wholes
 
 
 class Flow:
@@ -882,30 +882,13 @@
         return self.done[name]
 
 
-def spread_vectors(stack, sizes, place):
-    count = CHIPS_Z * CHIPS_X
-    stack = stack[:, :, :LAYERS].reshape(count, LAYERS, -1).astype(jnp.float32)
-    wanted = jnp.arange(count, dtype=jnp.int32)
-    behind = (place.z - wanted // CHIPS_X) % CHIPS_Z * CHIPS_X + (
-        place.x - wanted % CHIPS_X
-    ) % CHIPS_X
-    turn = (behind[:, None] == wanted[None, :]).astype(jnp.float32)
-    stack = jnp.sum(turn[:, :, None, None] * stack[None], axis=1)
+def spread_vectors(found, sizes):
+    found = found[:, :, 0, :LAYERS].reshape(-1, LAYERS, found.shape[-1]).transpose(1, 0, 2)
     out, at = [], 0
     for size in sizes:
-        out.append(
-            stack[:, :, at : at + size].transpose(1, 0, 2).reshape(LAYERS, count * size)
-        )
+        out.append(found[:, :, at : at + size].reshape(LAYERS, -1).astype(jnp.float32))
         at += size
     return out
-
-
-def first_block(weights, place):
-    shard = weights[0][0]
-    half = shard.shape[1] // CORES
-    block = lax.dynamic_slice_in_dim(shard, place.core * half, half, axis=1)
-    vectors = jnp.concatenate([weights[member] for member in VECTORS], axis=1)
-    return jnp.concatenate([block, jnp.pad(vectors, ((0, 16 - LAYERS), (0, 0)))])
 
 
 def pick_sum(at, own, terms, rows, steps):
@@ -983,12 +966,182 @@
     return add(own, *landed)
 
 
+def gather_kernel(plan, *refs):
+    count = len(plan)
+    prep_ins, ins, refs = refs[:3], refs[3 : 3 + count], refs[3 + count :]
+    prep_outs, outs, sems, local_sem = refs[:2], refs[2 : 2 + count], refs[2 + count : -1], refs[-1]
+    rep, shard = lax.axis_index("rep"), lax.axis_index("shard")
+    y, core = lax.div(rep, CORES), lax.rem(rep, CORES)
+    z, x = lax.div(shard, CHIPS_X), lax.rem(shard, CHIPS_X)
+
+    def device(dz=0, dx=0, dy=0, dc=0):
+        to_y, to_core = lax.rem(y + dy, CHIPS_Y), lax.rem(core + dc, CORES)
+        to_z, to_x = lax.rem(z + dz, CHIPS_Z), lax.rem(x + dx, CHIPS_X)
+        return (to_y * CORES + to_core, to_z * CHIPS_X + to_x)
+
+    mates = [dict(dx=1), dict(dy=1), dict(dc=1)] + [dict(dz=k) for k in range(1, CHIPS_Z)]
+    barrier = pltpu.get_barrier_semaphore()
+    for mate in mates:
+        pl.semaphore_signal(
+            barrier, inc=1, device_id=device(**mate), device_id_type=pl.DeviceIdType.MESH
+        )
+    sent = []
+
+    def send(source, target, m, number, **step):
+        copy = pltpu.make_async_remote_copy(
+            src_ref=source,
+            dst_ref=target,
+            send_sem=sems[m].at[0, number],
+            recv_sem=sems[m].at[1, number],
+            device_id=device(**step),
+            device_id_type=pl.DeviceIdType.MESH,
+        )
+        copy.start()
+        sent.append(copy)
+        return copy
+
+    def part(m, at_z, at_x, at_y, at_core):
+        out, (layer, split_y, by_core) = outs[m], plan[m]
+        columns = slice(None)
+        if by_core:
+            half = out.shape[-1] // CORES
+            columns = pl.ds(pl.multiple_of(at_core * half, 128), half)
+        at_z = slice(None) if at_z is None else at_z
+        at_x = slice(None) if at_x is None else at_x
+        return out.at[at_z, at_x, at_y if split_y else 0, :, columns]
+
+    locals_ = []
+    for m, (layer, split_y, by_core) in enumerate(plan):
+        rows = outs[m].shape[3]
+        source = ins[m] if layer is None else ins[m].at[layer]
+        if by_core:
+            half = outs[m].shape[-1] // CORES
+            first = pl.multiple_of(y * rows, 16) if split_y else 0
+            source = source.at[pl.ds(first, rows), pl.ds(pl.multiple_of(core * half, 128), half)]
+        copy = pltpu.make_async_copy(source, part(m, z, x, y, core), local_sem.at[m])
+        copy.start()
+        locals_.append(copy)
+    pl.semaphore_wait(barrier, len(mates))
+    along_z, along_x, over_y, last = {}, {}, {}, []
+
+    def spread(m, at_z, at_x):
+        piece = part(m, at_z, at_x, y, core)
+        if at_x is x:
+            along_x[m].append(send(piece, piece, m, 3 + len(along_x[m]), dx=1))
+        if plan[m][1]:
+            over_y[m].append(send(piece, piece, m, 7 + len(over_y[m]), dy=1))
+
+    def behind(k):
+        return lax.rem(z + CHIPS_Z - k, CHIPS_Z)
+
+    def after_x(m):
+        for k in range(CHIPS_Z):
+            along_x[m][k].wait_recv()
+            spread(m, behind(k), 1 - x)
+        if plan[m][2]:
+            piece = part(m, None, None, y, core)
+            last.append(send(piece, piece, m, 15, dc=1))
+
+    def after_y(m):
+        if over_y[m]:
+            for copy in over_y[m]:
+                copy.wait_recv()
+            piece = part(m, None, None, 1 - y, core)
+            last.append(send(piece, piece, m, 16, dc=1))
+
+    order = sorted(range(count), key=lambda m: (not plan[m][1], -outs[m].shape[-1]))
+    for m in order:
+        locals_[m].wait()
+        mine = part(m, z, x, y, core)
+        along_z[m] = [send(mine, mine, m, k - 1, dz=k) for k in range(1, CHIPS_Z)]
+        along_x[m], over_y[m] = [], []
+        spread(m, z, x)
+    trees, pairs = prep_ins[2].shape[:2]
+    todo = [(tree, tree, pair) for tree in range(trees) for pair in range(pairs)]
+    for place, m in enumerate(order):
+        for k in range(1, CHIPS_Z):
+            if todo:
+                prep_pair(*prep_ins, *prep_outs, *todo.pop(0))
+            along_z[m][k - 1].wait_recv()
+            spread(m, behind(k), x)
+        if place:
+            after_x(order[place - 1])
+    for item in todo:
+        prep_pair(*prep_ins, *prep_outs, *item)
+    after_x(order[-1])
+    for m in order:
+        after_y(m)
+    for copy in last:
+        copy.wait_recv()
+    for copy in sent:
+        copy.wait_send()
+
+
+def gather_layer(segment, parent, clusters, vectors, weights, layer, tall):
+    low = jnp.bfloat16
+    args, plan, shapes = [vectors], [(None, False, False)], [(1, *vectors.shape)]
+    for number in MATRICES:
+        _, rows, columns = weights[number].shape
+        split = CHIPS_Y if number in tall else 1
+        args.append(weights[number])
+        plan.append((layer, split > 1, True))
+        shapes.append((split, rows // split, columns))
+    shapes = [jax.ShapeDtypeStruct((CHIPS_Z, CHIPS_X, *shape), low) for shape in shapes]
+    trees = parent.shape[0]
+    segment = segment.reshape(trees, 1, TREE_LEN)
+    clusters = clusters.reshape(PAIRS, 2, trees, TREE_LEN).transpose(2, 0, 1, 3)
+    prepared = [
+        jax.ShapeDtypeStruct(clusters.shape, jnp.int32),
+        jax.ShapeDtypeStruct((trees, HEADS, TREE_LEN, LANES), low),
+    ]
+    whole = pl.BlockSpec(memory_space=pltpu.VMEM)
+    slots, bias, *found = pl.pallas_call(
+        functools.partial(gather_kernel, plan),
+        in_specs=[pl.BlockSpec(memory_space=pltpu.SMEM), whole, whole]
+        + [pl.BlockSpec(memory_space=pl.ANY)] * len(args),
+        out_specs=[whole] * (2 + len(args)),
+        out_shape=prepared + shapes,
+        scratch_shapes=[pltpu.SemaphoreType.DMA((2, 17))] * len(args)
+        + [pltpu.SemaphoreType.DMA((len(args),))],
+        compiler_params=pltpu.CompilerParams(
+            vmem_limit_bytes=KERNEL_VMEM, collective_id=1, has_side_effects=True
+        ),
+        cost_estimate=pl.CostEstimate(flops=0, bytes_accessed=200_000_000, transcendentals=0),
+    )(parent, segment, clusters, *args)
+    return slots, bias, found[0], [item.reshape(-1, item.shape[-1]) for item in found[1:]]
+
+
+def pack_sums(out_ref, core, ins):
+    rows = 8 * LAYERS
+    width = out_ref.shape[1]
+    for layer in range(LAYERS):
+        sums_ref, ffin_ref, own_ref, away_ref = ins[4 * layer : 4 * layer + 4]
+        out_ref[8 * layer : 8 * layer + 8] = sums_ref[...]
+        for at in range(0, ffin_ref.shape[1], width):
+            out_ref[rows : rows + 1] = ffin_ref[:, at : at + width]
+            rows += 1
+    for layer in range(LAYERS):
+        for flip, ref in enumerate(ins[4 * layer + 2 : 4 * layer + 4]):
+            half = lax.rem(core + flip, CORES) * ref.shape[1]
+            for pair in range(ref.shape[1]):
+                value = ref[0, pair]
+                for tree in range(1, ref.shape[0]):
+                    value = value + ref[tree, pair]
+                column = pl.multiple_of((half + pair) * LANES, LANES)
+                out_ref[rows : rows + 8, pl.ds(column, LANES)] = value
+        rows += 8
+
+
+def sum_rows(ffin_width):
+    return LAYERS * (16 + ffin_width // D)
+
+
 def tail_kernel(arrived, *refs):
     take = iter(refs)
     count = len(arrived)
     a_in, a_keep = next(take), next(take)
     b_ins = [(next(take), next(take)) for _ in range(count)]
-    l_in, vec = next(take), next(take)
+    l_in, vec_ins = next(take), [next(take) for _ in range(4 * LAYERS)]
     a_own, a_other = next(take), next(take)
     b_outs = [next(take) for _ in range(count)]
     l_own, l_other, vec_out = next(take), next(take), next(take)
@@ -1035,10 +1188,9 @@
 
     order = (2, 1, 3, 0)
     ahead = [lax.rem(z + k, CHIPS_Z) for k in order]
-    v_send[0] = vec[...]
+    pack_sums(v_send.at[0], core, vec_ins)
     v_copies = [send(v_send.at[0], v_land.at[0], v_sems, 0, dc=1)]
     a_across = a_in
-    l_y = send(l_in, l_yland, a_sems, 0, dy=1)
     b_y = [[] for _ in range(count)]
     for j, to in enumerate(ahead):
         for i, (b_send, _) in enumerate(b_ins):
@@ -1065,38 +1217,48 @@
 
     a_z, b_x, b_z = [], [[] for _ in range(count)], [[] for _ in range(count)]
 
-    def b_along_z(j):
-        k = order[j]
-        for i, (_, keep) in enumerate(b_ins):
-            _, _, x_land, z_send, z_land, _ = b_scratch[i]
-            b_x[i][j].wait_recv()
-            if k:
-                total = wide(keep[:, ahead[j], x]) + over(i, j, x) + wide(x_land[j])
-                z_send[k - 1] = total.astype(jnp.bfloat16)
-                b_z[i].append(
-                    send(z_send.at[k - 1], z_land.at[k - 1], b_sems[i], 7 + k, dz=k)
-                )
+    def b_along_z(i, j):
+        k, keep = order[j], b_ins[i][1]
+        _, _, x_land, z_send, z_land, _ = b_scratch[i]
+        b_x[i][j].wait_recv()
+        if k:
+            total = wide(keep[:, ahead[j], x]) + over(i, j, x) + wide(x_land[j])
+            z_send[k - 1] = total.astype(jnp.bfloat16)
+            b_z[i].append(send(z_send.at[k - 1], z_land.at[k - 1], b_sems[i], 7 + k, dz=k))
+
+    def b_along_x(i, j):
+        keep, (_, x_send, x_land, *_) = b_ins[i][1], b_scratch[i]
+        if not arrived[i]:
+            b_y[i][j].wait_recv()
+        total = wide(keep[:, ahead[j], 1 - x]) + over(i, j, 1 - x)
+        x_send[j] = total.astype(jnp.bfloat16)
+        b_x[i].append(send(x_send.at[j], x_land.at[j], b_sems[i], 4 + j, dx=1))
 
     for j, k in enumerate(order):
         if k:
             total = wide(a_keep[ahead[j]]) + wide(a_across[ahead[j]])
             a_zsend[k - 1] = total.astype(jnp.bfloat16)
             a_z.append(send(a_zsend.at[k - 1], a_zland.at[k - 1], a_sems, 3 + k, dz=k))
-        for i, (_, keep) in enumerate(b_ins):
-            _, x_send, x_land, *_ = b_scratch[i]
+        for i in range(count):
+            if arrived[i]:
+                b_along_x(i, j)
+    l_y = send(l_in, l_yland, a_sems, 0, dy=1)
+    add_vectors(0)
+    for j in range(CHIPS_Z):
+        for i in range(count):
             if not arrived[i]:
-                b_y[i][j].wait_recv()
-            total = wide(keep[:, ahead[j], 1 - x]) + over(i, j, 1 - x)
-            x_send[j] = total.astype(jnp.bfloat16)
-            b_x[i].append(send(x_send.at[j], x_land.at[j], b_sems[i], 4 + j, dx=1))
-        if j:
-            b_along_z(j - 1)
-        add_vectors(j)
-    b_along_z(CHIPS_Z - 1)
+                b_along_x(i, j)
+        for i in range(count):
+            if arrived[i]:
+                b_along_z(i, j)
+        add_vectors(j + 1)
+    for j in range(CHIPS_Z):
+        for i in range(count):
+            if not arrived[i]:
+                b_along_z(i, j)
     l_y.wait_recv()
     l_own[...] = (wide(l_in[...]) + wide(l_yland[...])).astype(jnp.bfloat16)
     ends = [send(l_own, l_cland, a_sems, 1, dc=1)]
-    add_vectors(4)
     for copy in a_z:
         copy.wait_recv()
     total = wide(a_keep[z]) + wide(a_across[z])
@@ -1129,7 +1291,7 @@
         copy.wait_send()
 
 
-def reduce_tail(flat, pairs, last, vec):
+def reduce_tail(flat, pairs, last, sums):
     low = jnp.bfloat16
     _, total, unit = flat[0].shape
     whole = pl.BlockSpec(memory_space=pltpu.VMEM)
@@ -1156,15 +1318,16 @@
     outs += [last.shape, last.shape]
     scratch += [last.shape, last.shape]
     shapes = [jax.ShapeDtypeStruct(shape, low) for shape in outs]
-    shapes.append(jax.ShapeDtypeStruct(vec.shape, jnp.float32))
+    vec = (sum_rows(sums[1].shape[1]), D)
+    shapes.append(jax.ShapeDtypeStruct(vec, jnp.float32))
     scratch = [pltpu.VMEM(shape, low) for shape in scratch]
-    scratch += [pltpu.VMEM((5, *vec.shape), jnp.float32)] * 2
+    scratch += [pltpu.VMEM((5, *vec), jnp.float32)] * 2
     scratch += [pltpu.SemaphoreType.DMA((2, 9))]
     scratch += [pltpu.SemaphoreType.DMA((2, 14))] * len(pairs)
     scratch += [pltpu.SemaphoreType.DMA((2, 5))]
     own, other, *rest = pl.pallas_call(
         functools.partial(tail_kernel, arrived),
-        in_specs=[*specs, whole, whole],
+        in_specs=[*specs, whole] + [whole] * len(sums),
         out_specs=[whole] * len(shapes),
         out_shape=shapes,
         scratch_shapes=scratch,
@@ -1172,7 +1335,7 @@
             vmem_limit_bytes=KERNEL_VMEM, collective_id=0, has_side_effects=True
         ),
         cost_estimate=pl.CostEstimate(flops=0, bytes_accessed=200_000_000, transcendentals=0),
-    )(*args, last, vec)
+    )(*args, last, *sums)
     return [own, other], rest[:-3], list(rest[-3:-1]), rest[-1]
 
 
@@ -1220,20 +1383,6 @@
     )(at, *arrays)
 
 
-def qv_sum(halves):
-    own, away, at = halves
-    own, away = jnp.sum(own, axis=0), jnp.sum(away, axis=0)
-    order = jnp.where(
-        at[3] == 0, jnp.concatenate([own, away], axis=0), jnp.concatenate([away, own], axis=0)
-    )
-    return jnp.concatenate([order[:, part].reshape(D) for part in (0, 2)])
-
-
-def path_vectors(qv_bias):
-    low = qv_bias.astype(jnp.float32)
-    return jnp.concatenate([low[:D], jnp.zeros((D,), jnp.float32), low[D:]])
-
-
 def local(
     fast,
     inputs,
@@ -1247,29 +1396,30 @@
     if fast:
         place = Place()
         at = place.at
-        sizes = [weights[number].shape[1] for number in VECTORS]
-        spread_out = []
-
-        blocks = {"first": first_block(weights, place)}
+        blocks = pack(weights, list(CHUNKS), place)
+        own_vectors = jnp.concatenate([weights[member] for member in VECTORS], axis=1)
+        own_vectors = jnp.pad(own_vectors, ((0, 16 - LAYERS), (0, 0)))
+        slots, bias, found, lowest = gather_layer(
+            segment, parent, clusters, own_vectors, weights, 0, (6, 8, 2)
+        )
+        vectors = spread_vectors(found, [weights[number].shape[1] for number in VECTORS])
 
         def get(layer, number):
-            if number not in VECTORS:
+            if layer == 0:
+                return lowest[MATRICES.index(number)]
+            else:
                 for name, (chunk_layer, numbers, _) in CHUNKS.items():
                     if chunk_layer == layer and number in numbers:
-                        return flow.finish(name)[0][numbers.index(number)]
-            if not spread_out:
-                spread_out.extend(spread_vectors(flow.finish("first")[1], sizes, place))
-            return spread_out[VECTORS.index(number)][layer]
+                        return flow.finish(name)[numbers.index(number)]
 
         def step(point, main):
             advanced, started = FORWARD.get(point, ((), ()))
-            main = flow.tick(main, *advanced)
-            for name in started:
+            fresh = [blocks[name] for name in started]
+            main, fresh = flow.tick((main, fresh), *advanced)
+            for name, block in zip(started, fresh):
                 _, numbers, split_y = CHUNKS[name]
                 layout = chunk_rows(weights, numbers, split_y)
-                if name == "first":
-                    layout = [(1, layout[0][1])]
-                flow.start(name, gather_chain(blocks[name], layout, split_y, place))
+                flow.start(name, gather_chain(block, layout, split_y, place))
             return main
 
         def reduce(layer, *grads):
@@ -1288,9 +1438,14 @@
     else:
         at = jnp.zeros((4,), jnp.int32)
 
+        slots, bias = prepare(segment, parent, clusters)
+        vectors = [
+            lax.all_gather(weights[number], "shard", axis=1, tiled=True).astype(jnp.float32)
+            for number in VECTORS
+        ]
+
         def get(layer, number):
-            whole = lax.all_gather(weights[number][layer], "shard", axis=0, tiled=True)
-            return whole.astype(jnp.float32) if number in VECTORS else whole
+            return lax.all_gather(weights[number][layer], "shard", axis=0, tiled=True)
 
         def step(point, main):
             return main
@@ -1309,13 +1464,7 @@
         def back_step(main, *held):
             return main
 
-    step("begin", ())
-    if fast:
-        blocks.update(pack(weights, [name for name in CHUNKS if name != "first"], place))
-        segment, parent, clusters, blocks["rest"] = step(
-            "packed", (segment, parent, clusters, blocks["rest"])
-        )
-    slots, bias = step("prepared", prepare(segment, parent, clusters))
+    vector = dict(zip(VECTORS, vectors))
     hidden, hidden_low = inputs, inputs
     saved = []
     for layer in range(LAYERS):
@@ -1323,20 +1472,21 @@
         weight = pull(0)
         if layer == 0:
             weight = step("ready", weight)
-        projected = project(hidden_low, weight, path_vectors(pull(1)))
+        projected = project(layer, hidden_low, weight, vector[1])
+        projected = step((layer, "projected"), projected)
         first = attend(projected, slots, bias, 0, ())
         first = step((layer, "half"), first)
         context, *heads = attend(projected, slots, bias, 1, first)
         context = step((layer, "context"), context)
-        context = step((layer, "waited"), context)
-        context, *wide = step((layer, "placed"), (context, pull(2), pull(6), pull(8)))
         entered = hidden_low
         middle, act, slope, *norms, hidden, hidden_low = feed(
+            layer,
             context,
             hidden,
-            wide,
-            [pull(number) for number in (3, 4, 5, 7, 9, 10, 11)],
+            [pull(2), pull(6), pull(8)],
+            [vector[number] for number in (3, 4, 5, 7, 9, 10, 11)],
         )
+        hidden_low = step((layer, "result"), hidden_low)
         saved.append((entered, heads, context, middle, act, slope, norms))
     result = hidden_low
     above, proj = cotangent, None
@@ -1345,15 +1495,16 @@
         entered, heads, context, middle, act, slope, norms = saved[layer]
         pull = functools.partial(get, layer)
         down, grad_pre, grad_attn, attn_low, grad_context, row_sums, ffin_sum = feed_back(
+            layer,
             above,
             proj,
             None if proj is None else get(layer + 1, 0),
             at,
             [norms[2], norms[3], slope, norms[0], norms[1]],
             [pull(2), pull(6), pull(8)],
-            [pull(4), pull(10)],
+            [vector[4], vector[10]],
         )
-        sums[layer] = [row_sums, ffin_sum, None]
+        sums[layer] = [row_sums, ffin_sum]
         down = back_step(down)
         wide = grad_pre.shape[1] // CORES
         grad_8 = Grad(8, act, down, down, True, act.shape[1] // D, UNIT)
@@ -1372,40 +1523,44 @@
         own, own_sums = attend_back(grad_context, slots, heads, at, False)
         proj = (own, away)
         reduce(layer, Grad(0, entered, own, away, False, 3, UNIT))
-        sums[layer][2] = (own_sums, away_sums, at)
+        sums[layer] += [own_sums, away_sums]
         proj = back_step(proj, *(wide_chains if layer else ()))
         above = grad_attn
     grad_input = input_grad(above, proj, get(0, 0), at)
-    pieces = [qv_sum(sums[layer][2]) for layer in range(LAYERS)]
-    for row_sums, ffin_sum, _ in sums:
-        pieces += [row_sums[:6].reshape(-1), ffin_sum[0]]
-    total = jnp.concatenate(pieces)
+    sums = [item for layer in sums for item in layer]
     if fast:
         while flow.running:
             grad_input = back_step(grad_input)
         done = flow.done
-        vec = total.reshape(-1, 128)
-        last, vec, grad_input = lax.optimization_barrier(
-            (done["grad", 1, 8], vec, grad_input)
+        last, grad_input = lax.optimization_barrier((done["grad", 1, 8], grad_input))
+        flat, ends, last, total = reduce_tail(
+            done["grad", 0, 8], [done["grad", 0, 6], done["grad", 0, 0]], last, sums
         )
-        flat, ends, last, vec = reduce_tail(
-            done["grad", 0, 8], [done["grad", 0, 6], done["grad", 0, 0]], last, vec
-        )
-        total = vec.reshape(-1)
     else:
-        total = lax.psum(total, AXES)
+        norms, wide, heads = [], [], []
+        for row_sums, ffin_sum, own_sums, away_sums in (sums[:4], sums[4:]):
+            norms.append(row_sums)
+            wide.append(ffin_sum.reshape(-1, D))
+            found = jnp.concatenate([own_sums.sum(0), away_sums.sum(0)])
+            heads.append(found.transpose(1, 0, 2).reshape(8, D))
+        total = lax.psum(jnp.concatenate(norms + wide + heads), AXES)
     count = lax.axis_size("shard")
     shard = lax.axis_index("shard")
-    ff = sums[0][1].shape[1]
-    rest = total[4 * D :].reshape(LAYERS, 6 * D + ff)
-
-    def share(stacked):
+    ffin_rows = sums[1].shape[1] // D
+
+    def share(rows):
+        stacked = jnp.stack([total[row].reshape(-1) for row in rows])
         width = stacked.shape[1] // count
         return lax.dynamic_slice_in_dim(stacked, shard * width, width, axis=1)
 
-    grads = {1: share(total[: 4 * D].reshape(LAYERS, 2 * D)), 7: share(rest[:, 6 * D :])}
+    starts = [0, 8, 16, 16 + ffin_rows]
+    heads_at = [16 + 2 * ffin_rows, 24 + 2 * ffin_rows]
+    grads = {
+        1: share([slice(at, at + 3, 2) for at in heads_at]),
+        7: share([slice(at, at + ffin_rows) for at in starts[2:]]),
+    }
     for number, row in ((10, 0), (11, 1), (9, 2), (4, 3), (5, 4), (3, 5)):
-        grads[number] = share(rest[:, row * D : (row + 1) * D])
+        grads[number] = share([row, 8 + row])
     if fast:
         rows = {number: weights[number].shape[1] for number in MATRICES}
         parts = {number: weights[number].shape[2] // (CORES * UNIT) for number in MATRICES}

time: 747 us -> 775 us (1.037)
  Pallas kernels: 559 us -> 607 us
  local copies, waits for them, and re-layouts: 39.4 us -> 18.4 us
  starting transfers between devices: 47.4 us -> 31.8 us
  waiting for transfers between devices: 83.8 us -> 98.8 us
    pallas_call x7, Pallas kernels: 144 us -> 217 us  [the longest x1 80.7 us: gather_layer(): pl.pallas_call(functools.partial(gather_kernel, plan), in_specs=[pl.Block...]
    ppermute x50 -> x34, starting transfers between devices: 47.4 us -> 31.8 us  [hop(): return lax.ppermute(value, AXES, pairs)]
    ppermute x50 -> x34, waiting for transfers between devices: 83.8 us -> 98.8 us  [hop(): return lax.ppermute(value, AXES, pairs)]
    pallas_call x4 -> x2, Pallas kernels: 28.5 us -> 14.1 us  [place_pieces(): pl.pallas_call(functools.partial(place_kernel, layout, split_y, len(piece...]
    slice x28 -> x4, local copies, waits for them, and re-layouts: 13.5 us -> 3.56 us  [the longest x3 2.63 us: share(): stacked = jnp.stack([total[row].reshape(-1) for row in rows])]
    pallas_call x1, Pallas kernels: 94.7 us -> 84.9 us  [reduce_tail(): pl.pallas_call(functools.partial(tail_kernel, arrived), in_specs=[*specs,...]
    unnamed x93 -> x46, local copies, waits for them, and re-layouts: 11.4 us -> 3.34 us
  transfers between devices with their start and end apart: 50 -> 34, of which waited for: 14 -> 9; matrix products, arithmetic and copies ran while one was open for 4% -> 1% of each run, Pallas kernels for 47% -> 42%
where the time goes in v7:
time: 775 us; the launch traced here: 764 us
  Pallas kernels  607 us (78%)
  waiting for transfers between devices  98.8 us (13%)
  starting transfers between devices  31.8 us (4%)
  local copies, waits for them, and re-layouts  18.4 us (2%)
    pallas_call x16, Pallas kernels, product(): pl.pallas_call(functools.partial(weight_grad_kernel, split_y), grid_spec=...  107 us
    ppermute x34, waiting for transfers between devices, hop(): return lax.ppermute(value, AXES, pairs)  98.8 us
    pallas_call x1, Pallas kernels, reduce_tail(): pl.pallas_call(functools.partial(tail_kernel, arrived), in_specs=[*specs,...  84.9 us
    pallas_call x1, Pallas kernels, gather_layer(): pl.pallas_call(functools.partial(gather_kernel, plan), in_specs=[pl.Block...  80.7 us
    pallas_call x4, Pallas kernels, attend_back(): pl.pallas_call(attend_back_kernel, grid_spec=pltpu.PrefetchScalarGridSpec...  75 us
    pallas_call x4, Pallas kernels, attend(): pl.pallas_call(attend_kernel, grid=(trees, PAIRS // 2), in_specs=[slot_sp...  70.8 us
    pallas_call x2, Pallas kernels, feed(): pl.pallas_call(functools.partial(feed_kernel, layer), grid=(count // ROW_...  68 us
    pallas_call x2, Pallas kernels, feed_back(): pl.pallas_call(functools.partial(feed_back_kernel, layer, proj is not Non...  53 us
  transfers between devices with their start and end apart: 34, of which 9 were waited for; matrix products, arithmetic and copies ran while one was open for 1% of the time, Pallas kernels for 42%

profile of v7, /device:TPU:17, one launch (start us, length us, event | category | flops | bytes accessed | tf_op | source)
XLA Modules:
  0.0 764.0 jit_solution(14419179282151791053)
XLA Ops:
  0.7 1.5 transpose_reshape.3.refs_2_
  4.3 3.6 shard_map.273
  7.9 80.7 %shard_map.272 = (s32[1,6,2,1024]{3,2,1,0:T(2,128)}, bf16[1,12,1024,128]{3,2,1,0:T(8,128)(2,1)}, bf16[4,2,1,16,1152]{4,3,2,1,0:T(8,128)(2,1)}, bf16[4,2,1,96,230...) custom-call(s32[1,13]{1,0:T(1,128)} %refs_0_.3, ...), custom_call_target="tpu_custom_call" | custom-call | bytes 200000000 | tf_op jit(solution)/shard_map/pallas_call | solution.py:1098
  89.9 4.0 collective-permute-start.1
  95.5 7.8 %shard_map.274.query_ref.key_ref.value_ref = bf16[1024,2304]{1,0:T(8,128)(2,1)} custom-call(bf16[1024,768]{1,0:T(8,128)(2,1)} %left_ref.3, bf16[768,2304]{1,0:T(8,128)(2,1)} %bitcast.89, f32[2,1536]{1,0:T(2,128)} %reshape.122.bias_ref), custom_call_target="tpu_custom_call" | custom-call | flops 4348654592 | bytes 5111808 | tf_op jit(solution)/shard_map/pallas_call | solution.py:467
  103.4 17.7 %shard_map.275 = (bf16[1024,768]{1,0:T(8,128)(2,1)}, bf16[1,12,1024,128]{3,2,1,0:T(8,128)(2,1)}, bf16[1,12,1024,128]{3,2,1,0:T(8,128)(2,1)}, bf16[1,12,1024,128]{3,2,1,0:T(8,128)(2,1)}) custom-call(s32[1,6,2,1024]{3,2,1,0:T(2,128)} %get-tuple-element.170.slot_ref, bf16[1024,2304]{1,0:T(8,128)(2,1)} %shard_map.274.query_ref.key_ref.value_ref, ...), custom_call_target="tpu_custom_call" | custom-call | flops 15000000512 | bytes 10000000 | tf_op jit(solution)/shard_map/pallas_call | solution.py:158
  126.1 1.6 collective-permute-start.3
  128.5 17.7 %shard_map.276 = (bf16[1024,768]{1,0:T(8,128)(2,1)}, bf16[1,12,1024,128]{3,2,1,0:T(8,128)(2,1)}, bf16[1,12,1024,128]{3,2,1,0:T(8,128)(2,1)}, bf16[1,12,1024,128]{3,2,1,0:T(8,128)(2,1)}) custom-call(s32[1,6,2,1024]{3,2,1,0:T(2,128)} %get-tuple-element.170.slot_ref, ...), custom_call_target="tpu_custom_call", output_to_operand_aliasing={{0}: (5, {}), {1}: (6, {}), {2}: (7, {}), {3}: (8, {})} | custom-call | flops 15000000512 | bytes 10000000 | tf_op jit(solution)/shard_map/pallas_call | solution.py:158
  146.3 39.9 %shard_map.277 = (bf16[1024,768]{1,0:T(8,128)(2,1)}, bf16[1024,3072]{1,0:T(8,128)(2,1)}, bf16[1024,3072]{1,0:T(8,128)(2,1)}, f32[1024,768]{1,0:T(8,128)}, f32[10...) custom-call(bf16[1024,768]{1,0:T(8,128)(2,1)} %get-tuple-element.186, ...), custom_call_target="tpu_custom_call" | custom-call | flops 27179089920 | bytes 12189696 | tf_op jit(solution)/shard_map/pallas_call | solution.py:482
  186.3 1.8 collective-permute-start.6
  188.6 2.3 collective-permute-start.8
  191.9 5.7 shard_map.278
  197.5 7.9 %shard_map.279.query_ref.key_ref.value_ref = bf16[1024,2304]{1,0:T(8,128)(2,1)} custom-call(bf16[1024,768]{1,0:T(8,128)(2,1)} %get-tuple-element.194.rows_ref.left_ref, bf16[768,2304]{1,0:T(8,128)(2,1)} %bitcast.91, f32[2,1536]{1,0:T(2,128)} %reshape.122.bias_ref), custom_call_target="tpu_custom_call" | custom-call | flops 4348654592 | bytes 5111808 | tf_op jit(solution)/shard_map/pallas_call | solution.py:467
  205.4 20.8 %collective-permute-done.7 = bf16[768,384]{1,0:T(8,128)(2,1)} collective-permute-done((bf16[768,384]{1,0:T(8,128)(2,1)S(1)}, bf16[768,384]{1,0:T(8,128)(2,1)}, u32[]{:S(2)}, u32[]{:S(2)}) %collective-permute-start.7) | collective-permute-done | bytes 589856 | tf_op jit(solution)/shard_map/ppermute | solution.py:751
  226.2 12.6 %collective-permute-done.8 = bf16[768,384]{1,0:T(8,128)(2,1)} collective-permute-done((bf16[768,384]{1,0:T(8,128)(2,1)S(1)}, bf16[768,384]{1,0:T(8,128)(2,1)}, u32[]{:S(2)}, u32[]{:S(2)}) %collective-permute-start.8) | collective-permute-done | bytes 589856 | tf_op jit(solution)/shard_map/ppermute | solution.py:751
  238.9 1.8 pad_maximum_fusion.refs_0_
  240.7 1.4 collective-permute-start.10
  242.2 17.7 %shard_map.280 = (bf16[1024,768]{1,0:T(8,128)(2,1)}, bf16[1,12,1024,128]{3,2,1,0:T(8,128)(2,1)}, bf16[1,12,1024,128]{3,2,1,0:T(8,128)(2,1)}, bf16[1,12,1024,128]{3,2,1,0:T(8,128)(2,1)}) custom-call(s32[1,6,2,1024]{3,2,1,0:T(2,128)} %get-tuple-element.170.slot_ref, bf16[1024,2304]{1,0:T(8,128)(2,1)} %shard_map.279.query_ref.key_ref.value_ref, ...), custom_call_target="tpu_custom_call" | custom-call | flops 15000000512 | bytes 10000000 | tf_op jit(solution)/shard_map/pallas_call | solution.py:158
  259.9 17.7 %shard_map.281 = (bf16[1024,768]{1,0:T(8,128)(2,1)}, bf16[1,12,1024,128]{3,2,1,0:T(8,128)(2,1)}, bf16[1,12,1024,128]{3,2,1,0:T(8,128)(2,1)}, bf16[1,12,1024,128]{3,2,1,0:T(8,128)(2,1)}) custom-call(s32[1,6,2,1024]{3,2,1,0:T(2,128)} %get-tuple-element.170.slot_ref, ...), custom_call_target="tpu_custom_call", output_to_operand_aliasing={{0}: (5, {}), {1}: (6, {}), {2}: (7, {}), {3}: (8, {})} | custom-call | flops 15000000512 | bytes 10000000 | tf_op jit(solution)/shard_map/pallas_call | solution.py:158
  277.6 14.8 %collective-permute-done.9.refs_2_ = bf16[4,768,384]{2,1,0:T(8,128)(2,1)} collective-permute-done((bf16[4,768,384]{2,1,0:T(8,128)(2,1)S(1)}, bf16[4,768,384]{2,1,0:T(8,128)(2,1)}, u32[]{:S(2)}, u32[]{:S(2)}) %collective-permute-start.9) | collective-permute-done | bytes 2359328 | tf_op jit(solution)/shard_map/ppermute | solution.py:751
  292.4 2.1 collective-permute-start.11
  294.5 4.5 collective-permute-done.11.refs_3_
  299.0 8.4 %shard_map.282 = (bf16[8,1,96,3072]{3,2,1,0:T(8,128)(2,1)}, bf16[8,1,384,768]{3,2,1,0:T(8,128)(2,1)}) custom-call(s32[4]{0:T(128)} %pad_add_fusion.at_ref.refs_1_, bf16[4,768,384]{2,1,0:T(8,128)(2,1)} %copy-done.2, bf16[4,768,384]{2,1,0:T(8,128)(2,1)} %collective-permute-done.10.refs_1_, bf16[4,768,384]{2,1,0:T(8,128)(2,1)} %collective-permute-done.9.refs_2_, ...), custom_call_target="tpu_custom_call" | custom-call | bytes 18874368 | tf_op jit(solution)/shard_map/pallas_call | solution.py:818
  307.4 28.2 %shard_map.283 = (bf16[1024,768]{1,0:T(8,128)(2,1)}, bf16[1024,3072]{1,0:T(8,128)(2,1)}, bf16[1024,3072]{1,0:T(8,128)(2,1)}, f32[1024,768]{1,0:T(8,128)}, f32[10...) custom-call(bf16[1024,768]{1,0:T(8,128)(2,1)} %get-tuple-element.207, ...), custom_call_target="tpu_custom_call" | custom-call | flops 27179089920 | bytes 12189696 | tf_op jit(solution)/shard_map/pallas_call | solution.py:482
  335.6 21.7 %shard_map.284 = (bf16[1024,768]{1,0:T(8,128)(2,1)}, bf16[1024,3072]{1,0:T(8,128)(2,1)}, f32[1024,768]{1,0:T(8,128)}, bf16[1024,768]{1,0:T(8,128)(2,1)}, bf16[10...) custom-call(bf16[1024,768]{1,0:T(8,128)(2,1)} %refs_0_.5, f32[1024,768]{1,0:T(8,128)} %get-tuple-element.214.refs_1_, ...), custom_call_target="tpu_custom_call" | custom-call | flops 27179089920 | bytes 12189696 | tf_op jit(solution)/shard_map/pallas_call | solution.py:528
  357.3 7.6 shard_map.286
  365.3 7.9 %shard_map.285 = bf16[1,4,2,384,384]{4,3,2,1,0:T(8,128)(2,1)} custom-call(s32[4]{0:T(128)} %pad_add_fusion.at_ref.refs_1_, bf16[1024,3072]{1,0:T(8,128)(2,1)} %get-tuple-element.221.left_ref, bf16[1024,768]{1,0:T(8,128)(2,1)} %get-tuple-element.222.right_ref), custom_call_target="tpu_custom_call" | custom-call | flops 4831838208 | bytes 7864320 | tf_op jit(solution)/shard_map/pallas_call | solution.py:672
  373.4 4.1 shard_map.287
  377.8 1.8 collective-permute-done.14.refs_0_
  379.7 19.0 %shard_map.291 = (bf16[3,1024,384]{2,1,0:T(8,128)(2,1)}, f32[1,3,8,128]{3,2,1,0:T(8,128)}) custom-call(s32[4]{0:T(128)} %pad_add_fusion.at_ref.refs_1_, s32[1,6,2,1024]{3,2,1,0:T(2,128)} %get-tuple-element.170.slot_ref, bf16[1024,768]{1,0:T(8,128)(2,1)} %get-tuple-element.239.grad_ref, bf16[1,12,1024,128]{3,2,1,0:T(8,128)(2,1)} %get-tuple-element.235.qk_ref, ...), custom_call_target="tpu_custom_call" | custom-call | flops 16999999488 | bytes 10000000 | tf_op jit(solution)/shard_map/pallas_call | solution.py:195
  398.7 6.5 shard_map.293
  405.6 8.4 %shard_map.288 = (bf16[4,864,384]{2,1,0:T(8,128)(2,1)}, bf16[4,864,384]{2,1,0:T(8,128)(2,1)}) custom-call(s32[4]{0:T(128)} %pad_add_fusion.at_ref.refs_1_, bf16[1024,3072]{1,0:T(8,128)(2,1)} %get-tuple-element.221.left_ref, bf16[1024,768]{1,0:T(8,128)(2,1)} %get-tuple-element.222.right_ref, bf16[1,4,2,384,384]{4,3,2,1,0:T(8,128)(2,1)} %collective-permute-done.12.refs_0_), custom_call_target="tpu_custom_call" | custom-call | flops 4831838208 | bytes 7864320 | tf_op jit(solution)/shard_map/pallas_call | solution.py:672
  414.0 8.2 %shard_map.289 = (bf16[4,864,384]{2,1,0:T(8,128)(2,1)}, bf16[4,864,384]{2,1,0:T(8,128)(2,1)}) custom-call(s32[4]{0:T(128)} %pad_add_fusion.at_ref.refs_1_, bf16[1024,768]{1,0:T(8,128)(2,1)} %get-tuple-element.223.left_ref, bf16[1024,3072]{1,0:T(8,128)(2,1)} %get-tuple-element.224.right_ref, ...), custom_call_target="tpu_custom_call", output_to_operand_aliasing={{0}: (4, {}), {1}: (5, {})} | custom-call | flops 4831838208 | bytes 7864320 | tf_op jit(solution)/shard_map/pallas_call | solution.py:672
  422.2 4.3 shard_map.290
  426.6 18.8 %shard_map.292 = (bf16[3,1024,384]{2,1,0:T(8,128)(2,1)}, f32[1,3,8,128]{3,2,1,0:T(8,128)}) custom-call(s32[4]{0:T(128)} %pad_add_fusion.at_ref.refs_1_, s32[1,6,2,1024]{3,2,1,0:T(2,128)} %get-tuple-element.170.slot_ref, bf16[1024,768]{1,0:T(8,128)(2,1)} %get-tuple-element.239.grad_ref, bf16[1,12,1024,128]{3,2,1,0:T(8,128)(2,1)} %get-tuple-element.235.qk_ref, ...), custom_call_target="tpu_custom_call" | custom-call | flops 16999999488 | bytes 10000000 | tf_op jit(solution)/shard_map/pallas_call | solution.py:195
  445.4 6.9 shard_map.295
  452.3 31.3 %shard_map.294 = (bf16[1024,768]{1,0:T(8,128)(2,1)}, bf16[1024,3072]{1,0:T(8,128)(2,1)}, f32[1024,768]{1,0:T(8,128)}, bf16[1024,768]{1,0:T(8,128)(2,1)}, bf16[10...) custom-call(f32[1024,768]{1,0:T(8,128)} %get-tuple-element.233.refs_0_, s32[4]{0:T(128)} %pad_add_fusion.at_ref.refs_1_, ...), custom_call_target="tpu_custom_call" | custom-call | flops 27179089920 | bytes 13762560 | tf_op jit(solution)/shard_map/pallas_call | solution.py:528
  483.6 6.5 shard_map.300
  490.8 8.4 %shard_map.298 = bf16[1,4,2,384,384]{4,3,2,1,0:T(8,128)(2,1)} custom-call(s32[4]{0:T(128)} %pad_add_fusion.at_ref.refs_1_, bf16[1024,3072]{1,0:T(8,128)(2,1)} %get-tuple-element.258.left_ref, bf16[1024,768]{1,0:T(8,128)(2,1)} %get-tuple-element.259.right_ref), custom_call_target="tpu_custom_call" | custom-call | flops 4831838208 | bytes 7864320 | tf_op jit(solution)/shard_map/pallas_call | solution.py:672
  499.3 4.1 shard_map.299
  503.9 4.0 shard_map.297
  509.0 5.5 shard_map.296
  515.5 2.5 collective-permute-start.26
  518.0 1.8 collective-permute-done.18.refs_2_.refs_5_.refs_8_.refs_11_
  520.6 2.9 shard_map.302
  524.4 2.5 collective-permute-start.23
  526.9 18.6 %shard_map.301 = (bf16[3,1024,384]{2,1,0:T(8,128)(2,1)}, f32[1,3,8,128]{3,2,1,0:T(8,128)}) custom-call(s32[4]{0:T(128)} %pad_add_fusion.at_ref.refs_1_, s32[1,6,2,1024]{3,2,1,0:T(2,128)} %get-tuple-element.170.slot_ref, bf16[1024,768]{1,0:T(8,128)(2,1)} %get-tuple-element.272.grad_ref, bf16[1,12,1024,128]{3,2,1,0:T(8,128)(2,1)} %get-tuple-element.264.qk_ref, ...), custom_call_target="tpu_custom_call" | custom-call | flops 16999999488 | bytes 10000000 | tf_op jit(solution)/shard_map/pallas_call | solution.py:195
  545.5 7.0 shard_map.306
  552.5 29.3 %collective-permute-done.22.refs_1_ = bf16[3,48,384]{2,1,0:T(8,128)(2,1)S(1)} collective-permute-done((bf16[3,48,384]{2,1,0:T(8,128)(2,1)}, bf16[3,48,384]{2,1,0:T(8,128)(2,1)S(1)}, u32[]{:S(2)}, u32[]{:S(2)}) %collective-permute-start.22) | collective-permute-done | bytes 110624 | tf_op jit(solution)/shard_map/ppermute | solution.py:751
  581.9 6.8 shard_map.308
  589.9 8.4 %shard_map.304 = (bf16[4,480,384]{2,1,0:T(8,128)(2,1)}, bf16[4,480,384]{2,1,0:T(8,128)(2,1)}) custom-call(s32[4]{0:T(128)} %pad_add_fusion.at_ref.refs_1_, bf16[1024,3072]{1,0:T(8,128)(2,1)} %get-tuple-element.258.left_ref, bf16[1024,768]{1,0:T(8,128)(2,1)} %get-tuple-element.259.right_ref, bf16[1,4,2,384,384]{4,3,2,1,0:T(8,128)(2,1)} %collective-permute-done.19.refs_0_), custom_call_target="tpu_custom_call" | custom-call | flops 4831838208 | bytes 7864320 | tf_op jit(solution)/shard_map/pallas_call | solution.py:672
  598.3 2.4 shard_map.307
  600.8 1.7 collective-permute-start.30
  602.4 4.4 shard_map.305
  609.2 18.6 %shard_map.303 = (bf16[3,1024,384]{2,1,0:T(8,128)(2,1)}, f32[1,3,8,128]{3,2,1,0:T(8,128)}) custom-call(s32[4]{0:T(128)} %pad_add_fusion.at_ref.refs_1_, s32[1,6,2,1024]{3,2,1,0:T(2,128)} %get-tuple-element.170.slot_ref, bf16[1024,768]{1,0:T(8,128)(2,1)} %get-tuple-element.272.grad_ref, bf16[1,12,1024,128]{3,2,1,0:T(8,128)(2,1)} %get-tuple-element.264.qk_ref, ...), custom_call_target="tpu_custom_call" | custom-call | flops 16999999488 | bytes 10000000 | tf_op jit(solution)/shard_map/pallas_call | solution.py:195
  627.8 9.6 %collective-permute-done.32 = bf16[3,48,384]{2,1,0:T(8,128)(2,1)} collective-permute-done((bf16[3,48,384]{2,1,0:T(8,128)(2,1)S(1)}, bf16[3,48,384]{2,1,0:T(8,128)(2,1)}, u32[]{:S(2)}, u32[]{:S(2)}) %collective-permute-start.32) | collective-permute-done | bytes 110624 | tf_op jit(solution)/shard_map/ppermute | solution.py:751
  637.5 3.3 collective-permute-done.28.refs_0_
  640.8 6.9 shard_map.311
  647.7 9.6 %shard_map.310 = f32[1024,768]{1,0:T(8,128)} custom-call(f32[1024,768]{1,0:T(8,128)} %get-tuple-element.292.above_ref, s32[4]{0:T(128)} %pad_add_fusion.at_ref.refs_1_, bf16[3,1024,384]{2,1,0:T(8,128)(2,1)} %get-tuple-element.293.own_ref.right_ref, bf16[3,1024,384]{2,1,0:T(8,128)(2,1)} %get-tuple-element.294.right_ref.away_ref, bf16[768,2304]{1,0:T(8,128)(2,1)} %bitcast.90), custom_call_target="tpu_custom_call" | custom-call | flops 4348654592 | bytes 6684672 | tf_op jit(solution)/shard_map/pallas_call | solution.py:560
  657.4 4.5 shard_map.309.refs_6_
  661.8 84.9 %shard_map.312 = (bf16[480,384]{1,0:T(8,128)(2,1)}, bf16[480,384]{1,0:T(8,128)(2,1)}, bf16[4,2,48,768]{3,2,1,0:T(8,128)(2,1)}, bf16[4,3,48,384]{3,2,1,0:T(8,128)...) custom-call(bf16[4,480,384]{2,1,0:T(8,128)(2,1)} %copy-done.5, ...), custom_call_target="tpu_custom_call" | custom-call | bytes 200000000 | tf_op jit(solution)/shard_map/pallas_call | solution.py:1328
  750.3 2.0 fusion.8
  752.3 1.8 fusion.9
  757.3 6.1 shard_map.313
  (120 shorter events, 29.4 us)
Async XLA Ops:
  7.9 80.8 %copy-start.15 = (bf16[384,384]{1,0:T(8,128)(2,1)S(1)}, bf16[384,384]{1,0:T(8,128)(2,1)}, u32[]{:S(2)}) copy-start(bf16[384,384]{1,0:T(8,128)(2,1)} %get-tuple-element.181) | copy-start | bytes 884740
  88.7 37.2 %collective-permute-start = (bf16[384,384]{1,0:T(8,128)(2,1)S(1)}, bf16[384,384]{1,0:T(8,128)(2,1)S(1)}, u32[]{:S(2)}, u32[]{:S(2)}) collective-permute-start(bf16[384,384]{1,0:T(8,128)(2,1)S(1)} %copy-done.15), channel_id=1, source_target_pairs={{0,2},{1,3},{2,4},{3,5},{4,6},{5,7},{6,0},{7,1},{8,10},{9,11},{10,... | collective-permute-start | bytes 884744 | tf_op jit(solution)/shard_map/ppermute | solution.py:751
  89.9 36.0 %collective-permute-start.1 = (bf16[384,384]{1,0:T(8,128)(2,1)S(1)}, bf16[384,384]{1,0:T(8,128)(2,1)S(1)}, u32[]{:S(2)}, u32[]{:S(2)}) collective-permute-start(bf16[384,384]{1,0:T(8,128)(2,1)S(1)} %copy-done.15), channel_id=1, source_target_pairs={{0,4},{1,5},{2,6},{3,7},{4,0},{5,1},{6,2},{7,3},{8,12},{9,13},{10,... | collective-permute-start | bytes 884744 | tf_op jit(solution)/shard_map/ppermute | solution.py:751
  93.9 32.0 %collective-permute-start.2 = (bf16[384,384]{1,0:T(8,128)(2,1)S(1)}, bf16[384,384]{1,0:T(8,128)(2,1)S(1)}, u32[]{:S(2)}, u32[]{:S(2)}) collective-permute-start(bf16[384,384]{1,0:T(8,128)(2,1)S(1)} %copy-done.15), channel_id=1, source_target_pairs={{0,6},{1,7},{2,0},{3,1},{4,2},{5,3},{6,4},{7,5},{8,14},{9,15},{10,... | collective-permute-start | bytes 884744 | tf_op jit(solution)/shard_map/ppermute | solution.py:751
  126.1 20.2 %copy-start.4 = (bf16[4,384,384]{2,1,0:T(8,128)(2,1)}, bf16[4,384,384]{2,1,0:T(8,128)(2,1)S(1)}, u32[]{:S(2)}) copy-start(bf16[4,384,384]{2,1,0:T(8,128)(2,1)S(1)} %pad_maximum_fusion.1.refs_0_) | copy-start | bytes 3538948
  126.1 60.1 %collective-permute-start.3 = (bf16[4,384,384]{2,1,0:T(8,128)(2,1)S(1)}, bf16[4,384,384]{2,1,0:T(8,128)(2,1)S(1)}, u32[]{:S(2)}, u32[]{:S(2)}) collective-permute-start(bf16[4,384,384]{2,1,0:T(8,128)(2,1)S(1)} %pad_maximum_fusion.1.refs_0_), channel_id=1, source_target_pairs={{0,1},{1,0},{2,3},{3,2},{4,5},{5,4},{6,7},{7,6},{8,9},{9,8},{10,11... | collective-permute-start | bytes 3538952 | tf_op jit(solution)/shard_map/ppermute | solution.py:751
  127.7 63.2 %collective-permute-start.4 = (bf16[4,384,384]{2,1,0:T(8,128)(2,1)S(1)}, bf16[4,384,384]{2,1,0:T(8,128)(2,1)S(1)}, u32[]{:S(2)}, u32[]{:S(2)}) collective-permute-start(bf16[4,384,384]{2,1,0:T(8,128)(2,1)S(1)} %pad_maximum_fusion.1.refs_0_), channel_id=1, source_target_pairs={{0,8},{1,9},{2,10},{3,11},{4,12},{5,13},{6,14},{7,15},{8,0},{9,1},... | collective-permute-start | bytes 3538952 | tf_op jit(solution)/shard_map/ppermute | solution.py:751
  146.3 40.0 %copy-start.11 = (bf16[768,384]{1,0:T(8,128)(2,1)S(1)}, bf16[768,384]{1,0:T(8,128)(2,1)}, u32[]{:S(2)}) copy-start(bf16[768,384]{1,0:T(8,128)(2,1)} %get-tuple-element.197) | copy-start | bytes 1769476
  186.2 4.7 copy-start.6
  186.2 4.7 collective-permute-start.5
  186.3 19.1 %collective-permute-start.6 = (bf16[768,384]{1,0:T(8,128)(2,1)S(1)}, bf16[768,384]{1,0:T(8,128)(2,1)}, u32[]{:S(2)}, u32[]{:S(2)}) collective-permute-start(bf16[768,384]{1,0:T(8,128)(2,1)S(1)} %copy-done.11), channel_id=1, source_target_pairs={{0,2},{1,3},{2,4},{3,5},{4,6},{5,7},{6,0},{7,1},{8,10},{9,11},{10,... | collective-permute-start | bytes 1769480 | tf_op jit(solution)/shard_map/ppermute | solution.py:751
  188.1 38.2 %collective-permute-start.7 = (bf16[768,384]{1,0:T(8,128)(2,1)S(1)}, bf16[768,384]{1,0:T(8,128)(2,1)}, u32[]{:S(2)}, u32[]{:S(2)}) collective-permute-start(bf16[768,384]{1,0:T(8,128)(2,1)S(1)} %copy-done.11), channel_id=1, source_target_pairs={{0,4},{1,5},{2,6},{3,7},{4,0},{5,1},{6,2},{7,3},{8,12},{9,13},{10,... | collective-permute-start | bytes 1769480 | tf_op jit(solution)/shard_map/ppermute | solution.py:751
  188.6 50.3 %collective-permute-start.8 = (bf16[768,384]{1,0:T(8,128)(2,1)S(1)}, bf16[768,384]{1,0:T(8,128)(2,1)}, u32[]{:S(2)}, u32[]{:S(2)}) collective-permute-start(bf16[768,384]{1,0:T(8,128)(2,1)S(1)} %copy-done.11), channel_id=1, source_target_pairs={{0,6},{1,7},{2,0},{3,1},{4,2},{5,3},{6,4},{7,5},{8,14},{9,15},{10,... | collective-permute-start | bytes 1769480 | tf_op jit(solution)/shard_map/ppermute | solution.py:751
  190.8 1.0 copy-start.7
  240.7 19.2 %copy-start.2 = (bf16[4,768,384]{2,1,0:T(8,128)(2,1)}, bf16[4,768,384]{2,1,0:T(8,128)(2,1)S(1)}, u32[]{:S(2)}) copy-start(bf16[4,768,384]{2,1,0:T(8,128)(2,1)S(1)} %pad_maximum_fusion.refs_0_) | copy-start | bytes 7077892
  240.7 51.7 %collective-permute-start.9 = (bf16[4,768,384]{2,1,0:T(8,128)(2,1)S(1)}, bf16[4,768,384]{2,1,0:T(8,128)(2,1)}, u32[]{:S(2)}, u32[]{:S(2)}) collective-permute-start(bf16[4,768,384]{2,1,0:T(8,128)(2,1)S(1)} %pad_maximum_fusion.refs_0_), channel_id=1, source_target_pairs={{0,1},{1,0},{2,3},{3,2},{4,5},{5,4},{6,7},{7,6},{8,9},{9,8},{10,11... | collective-permute-start | bytes 7077896 | tf_op jit(solution)/shard_map/ppermute | solution.py:751
  240.7 53.8 %collective-permute-start.10 = (bf16[4,768,384]{2,1,0:T(8,128)(2,1)S(1)}, bf16[4,768,384]{2,1,0:T(8,128)(2,1)}, u32[]{:S(2)}, u32[]{:S(2)}) collective-permute-start(bf16[4,768,384]{2,1,0:T(8,128)(2,1)S(1)} %pad_maximum_fusion.refs_0_), channel_id=1, source_target_pairs={{0,8},{1,9},{2,10},{3,11},{4,12},{5,13},{6,14},{7,15},{8,0},{9,1},... | collective-permute-start | bytes 7077896 | tf_op jit(solution)/shard_map/ppermute | solution.py:751
  292.4 6.6 collective-permute-start.11
  364.9 14.7 %collective-permute-start.13 = (bf16[4,4,2,96,384]{4,3,2,1,0:T(8,128)(2,1)}, bf16[4,4,2,96,384]{4,3,2,1,0:T(8,128)(2,1)S(1)}, u32[]{:S(2)}, u32[]{:S(2)}) collective-permute-start(bf16[4,4,2,96,384]{4,3,2,1,0:T(8,128)(2,1)} %shard_map.286), channel_id=1, source_target_pairs={{0,8},{1,9},{2,10},{3,11},{4,12},{5,13},{6,14},{7,15},{8,0},{9,1},... | collective-permute-start | bytes 7077896 | tf_op jit(solution)/shard_map/ppermute | solution.py:751
  373.2 6.5 collective-permute-start.12
  377.4 2.2 collective-permute-start.14
  379.7 19.0 %copy-start.12 = (bf16[1,4,2,96,384]{4,3,2,1,0:T(8,128)(2,1)}, bf16[1,4,2,96,384]{4,3,2,1,0:T(8,128)(2,1)S(1)}, u32[]{:S(2)}) copy-start(bf16[1,4,2,96,384]{4,3,2,1,0:T(8,128)(2,1)S(1)} %collective-permute-done.14.refs_0_) | copy-start | bytes 1769476
  379.7 19.0 %copy-start.19 = (bf16[4,4,2,96,384]{4,3,2,1,0:T(8,128)(2,1)}, bf16[4,4,2,96,384]{4,3,2,1,0:T(8,128)(2,1)S(1)}, u32[]{:S(2)}) copy-start(bf16[4,4,2,96,384]{4,3,2,1,0:T(8,128)(2,1)S(1)} %collective-permute-done.13.refs_0_) | copy-start | bytes 7077892
  405.2 40.1 %collective-permute-start.15 = (bf16[3,4,2,96,384]{4,3,2,1,0:T(8,128)(2,1)}, bf16[3,4,2,96,384]{4,3,2,1,0:T(8,128)(2,1)}, u32[]{:S(2)}, u32[]{:S(2)}) collective-permute-start(bf16[3,4,2,96,384]{4,3,2,1,0:T(8,128)(2,1)} %shard_map.293), channel_id=1, source_target_pairs={{0,8},{1,9},{2,10},{3,11},{4,12},{5,13},{6,14},{7,15},{8,0},{9,1},... | collective-permute-start | bytes 5308424 | tf_op jit(solution)/shard_map/ppermute | solution.py:751
  426.6 64.3 %collective-permute-start.16 = (bf16[4,864,384]{2,1,0:T(8,128)(2,1)}, bf16[4,864,384]{2,1,0:T(8,128)(2,1)S(1)}, u32[]{:S(2)}, u32[]{:S(2)}) collective-permute-start(bf16[4,864,384]{2,1,0:T(8,128)(2,1)} %get-tuple-element.250), channel_id=1, source_target_pairs={{0,1},{1,0},{2,3},{3,2},{4,5},{5,4},{6,7},{7,6},{8,9},{9,8},{10,11... | collective-permute-start | bytes 7962632 | tf_op jit(solution)/shard_map/ppermute | solution.py:751
  452.3 38.5 %collective-permute-start.17 = (bf16[3,4,2,48,384]{4,3,2,1,0:T(8,128)(2,1)}, bf16[3,4,2,48,384]{4,3,2,1,0:T(8,128)(2,1)S(1)}, u32[]{:S(2)}, u32[]{:S(2)}) collective-permute-start(bf16[3,4,2,48,384]{4,3,2,1,0:T(8,128)(2,1)} %get-tuple-element.252), channel_id=1, source_target_pairs={{0,16},{1,17},{2,18},{3,19},{4,20},{5,21},{6,22},{7,23},{8,24},{9,... | collective-permute-start | bytes 2654216 | tf_op jit(solution)/shard_map/ppermute | solution.py:751
  490.1 29.7 %collective-permute-start.21 = (bf16[2,4,2,96,768]{4,3,2,1,0:T(8,128)(2,1)}, bf16[2,4,2,96,768]{4,3,2,1,0:T(8,128)(2,1)}, u32[]{:S(2)}, u32[]{:S(2)}) collective-permute-start(bf16[2,4,2,96,768]{4,3,2,1,0:T(8,128)(2,1)} %shard_map.300), channel_id=1, source_target_pairs={{0,8},{1,9},{2,10},{3,11},{4,12},{5,13},{6,14},{7,15},{8,0},{9,1},... | collective-permute-start | bytes 7077896 | tf_op jit(solution)/shard_map/ppermute | solution.py:751
  490.8 8.4 %copy-start.1 = (bf16[3,4,2,48,384]{4,3,2,1,0:T(8,128)(2,1)}, bf16[3,4,2,48,384]{4,3,2,1,0:T(8,128)(2,1)S(1)}, u32[]{:S(2)}) copy-start(bf16[3,4,2,48,384]{4,3,2,1,0:T(8,128)(2,1)S(1)} %collective-permute-done.17.refs_1_.refs_4_.refs_7_.refs_10_) | copy-start | bytes 2654212
  490.8 8.4 %copy-start = (bf16[4,864,384]{2,1,0:T(8,128)(2,1)}, bf16[4,864,384]{2,1,0:T(8,128)(2,1)S(1)}, u32[]{:S(2)}) copy-start(bf16[4,864,384]{2,1,0:T(8,128)(2,1)S(1)} %collective-permute-done.16.refs_1_.refs_3_.refs_5_.refs_7_) | copy-start | bytes 7962628
  499.3 20.6 %collective-permute-start.19 = (bf16[1,4,2,384,384]{4,3,2,1,0:T(8,128)(2,1)}, bf16[1,4,2,384,384]{4,3,2,1,0:T(8,128)(2,1)}, u32[]{:S(2)}, u32[]{:S(2)}) collective-permute-start(bf16[1,4,2,384,384]{4,3,2,1,0:T(8,128)(2,1)} %shard_map.298), channel_id=1, source_target_pairs={{0,8},{1,9},{2,10},{3,11},{4,12},{5,13},{6,14},{7,15},{8,0},{9,1},... | collective-permute-start | bytes 7077896 | tf_op jit(solution)/shard_map/ppermute | solution.py:751
  503.4 12.2 %collective-permute-start.20 = (bf16[1,4,2,96,384]{4,3,2,1,0:T(8,128)(2,1)}, bf16[1,4,2,96,384]{4,3,2,1,0:T(8,128)(2,1)S(1)}, u32[]{:S(2)}, u32[]{:S(2)}) collective-permute-start(bf16[1,4,2,96,384]{4,3,2,1,0:T(8,128)(2,1)} %shard_map.299), channel_id=1, source_target_pairs={{0,8},{1,9},{2,10},{3,11},{4,12},{5,13},{6,14},{7,15},{8,0},{9,1},... | collective-permute-start | bytes 1769480 | tf_op jit(solution)/shard_map/ppermute | solution.py:751
  507.8 12.0 %collective-permute-start.18 = (bf16[3,4,48,384]{3,2,1,0:T(8,128)(2,1)}, bf16[3,4,48,384]{3,2,1,0:T(8,128)(2,1)S(1)}, u32[]{:S(2)}, u32[]{:S(2)}) collective-permute-start(bf16[3,4,48,384]{3,2,1,0:T(8,128)(2,1)} %shard_map.297), channel_id=1, source_target_pairs={{0,1},{1,0},{2,3},{3,2},{4,5},{5,4},{6,7},{7,6},{8,9},{9,8},{10,11... | collective-permute-start | bytes 1327112 | tf_op jit(solution)/shard_map/ppermute | solution.py:751
  514.5 92.4 %collective-permute-start.25 = (bf16[864,384]{1,0:T(8,128)(2,1)}, bf16[864,384]{1,0:T(8,128)(2,1)S(1)}, u32[]{:S(2)}, u32[]{:S(2)}) collective-permute-start(bf16[864,384]{1,0:T(8,128)(2,1)} %get-tuple-element.275), channel_id=1, source_target_pairs={{0,2},{1,3},{2,4},{3,5},{4,6},{5,7},{6,0},{7,1},{8,10},{9,11},{10,... | collective-permute-start | bytes 1990664 | tf_op jit(solution)/shard_map/ppermute | solution.py:751
  515.5 30.0 %copy-start.13 = (bf16[1,4,2,96,384]{4,3,2,1,0:T(8,128)(2,1)}, bf16[1,4,2,96,384]{4,3,2,1,0:T(8,128)(2,1)S(1)}, u32[]{:S(2)}) copy-start(bf16[1,4,2,96,384]{4,3,2,1,0:T(8,128)(2,1)S(1)} %collective-permute-done.20.refs_0_) | copy-start | bytes 1769476
  515.5 91.4 %collective-permute-start.26 = (bf16[864,384]{1,0:T(8,128)(2,1)}, bf16[864,384]{1,0:T(8,128)(2,1)S(1)}, u32[]{:S(2)}, u32[]{:S(2)}) collective-permute-start(bf16[864,384]{1,0:T(8,128)(2,1)} %get-tuple-element.276), channel_id=1, source_target_pairs={{0,4},{1,5},{2,6},{3,7},{4,0},{5,1},{6,2},{7,3},{8,12},{9,13},{10,... | collective-permute-start | bytes 1990664 | tf_op jit(solution)/shard_map/ppermute | solution.py:751
  519.8 0.8 copy-start.3
  523.5 58.4 %collective-permute-start.22 = (bf16[3,48,384]{2,1,0:T(8,128)(2,1)}, bf16[3,48,384]{2,1,0:T(8,128)(2,1)S(1)}, u32[]{:S(2)}, u32[]{:S(2)}) collective-permute-start(bf16[3,48,384]{2,1,0:T(8,128)(2,1)} %get-tuple-element.269), channel_id=1, source_target_pairs={{0,2},{1,3},{2,4},{3,5},{4,6},{5,7},{6,0},{7,1},{8,10},{9,11},{10,... | collective-permute-start | bytes 331784 | tf_op jit(solution)/shard_map/ppermute | solution.py:751
  524.4 57.4 %collective-permute-start.23 = (bf16[3,48,384]{2,1,0:T(8,128)(2,1)}, bf16[3,48,384]{2,1,0:T(8,128)(2,1)S(1)}, u32[]{:S(2)}, u32[]{:S(2)}) collective-permute-start(bf16[3,48,384]{2,1,0:T(8,128)(2,1)} %get-tuple-element.270), channel_id=1, source_target_pairs={{0,4},{1,5},{2,6},{3,7},{4,0},{5,1},{6,2},{7,3},{8,12},{9,13},{10,... | collective-permute-start | bytes 331784 | tf_op jit(solution)/shard_map/ppermute | solution.py:751
  526.9 55.0 %collective-permute-start.24 = (bf16[3,48,384]{2,1,0:T(8,128)(2,1)}, bf16[3,48,384]{2,1,0:T(8,128)(2,1)S(1)}, u32[]{:S(2)}, u32[]{:S(2)}) collective-permute-start(bf16[3,48,384]{2,1,0:T(8,128)(2,1)} %get-tuple-element.271), channel_id=1, source_target_pairs={{0,6},{1,7},{2,0},{3,1},{4,2},{5,3},{6,4},{7,5},{8,14},{9,15},{10,... | collective-permute-start | bytes 331784 | tf_op jit(solution)/shard_map/ppermute | solution.py:751
  581.9 6.8 copy-start.16
  581.9 25.1 %collective-permute-start.27 = (bf16[864,384]{1,0:T(8,128)(2,1)}, bf16[864,384]{1,0:T(8,128)(2,1)}, u32[]{:S(2)}, u32[]{:S(2)}) collective-permute-start(bf16[864,384]{1,0:T(8,128)(2,1)} %get-tuple-element.277), channel_id=1, source_target_pairs={{0,6},{1,7},{2,0},{3,1},{4,2},{5,3},{6,4},{7,5},{8,14},{9,15},{10,... | collective-permute-start | bytes 1990664 | tf_op jit(solution)/shard_map/ppermute | solution.py:751
  581.9 6.8 copy-start.17
  581.9 6.8 copy-start.18
  588.7 52.1 %collective-permute-start.33 = (bf16[3,4,2,96,384]{4,3,2,1,0:T(8,128)(2,1)}, bf16[3,4,2,96,384]{4,3,2,1,0:T(8,128)(2,1)}, u32[]{:S(2)}, u32[]{:S(2)}) collective-permute-start(bf16[3,4,2,96,384]{4,3,2,1,0:T(8,128)(2,1)} %shard_map.308), channel_id=1, source_target_pairs={{0,8},{1,9},{2,10},{3,11},{4,12},{5,13},{6,14},{7,15},{8,0},{9,1},... | collective-permute-start | bytes 5308424 | tf_op jit(solution)/shard_map/ppermute | solution.py:751
  600.8 7.1 collective-permute-start.30
  602.4 4.6 copy-start.14
  606.9 20.9 %copy-start.9 = (bf16[864,384]{1,0:T(8,128)(2,1)}, bf16[864,384]{1,0:T(8,128)(2,1)S(1)}, u32[]{:S(2)}) copy-start(bf16[864,384]{1,0:T(8,128)(2,1)S(1)} %collective-permute-done.25.refs_1_) | copy-start | bytes 1990660
  606.9 30.6 %collective-permute-start.29 = (bf16[2,4,2,48,768]{4,3,2,1,0:T(8,128)(2,1)}, bf16[2,4,2,48,768]{4,3,2,1,0:T(8,128)(2,1)S(1)}, u32[]{:S(2)}, u32[]{:S(2)}) collective-permute-start(bf16[2,4,2,48,768]{4,3,2,1,0:T(8,128)(2,1)} %get-tuple-element.284), channel_id=1, source_target_pairs={{0,16},{1,17},{2,18},{3,19},{4,20},{5,21},{6,22},{7,23},{8,24},{9,... | collective-permute-start | bytes 3538952 | tf_op jit(solution)/shard_map/ppermute | solution.py:751
  606.9 20.9 %copy-start.10 = (bf16[864,384]{1,0:T(8,128)(2,1)}, bf16[864,384]{1,0:T(8,128)(2,1)S(1)}, u32[]{:S(2)}) copy-start(bf16[864,384]{1,0:T(8,128)(2,1)S(1)} %collective-permute-done.26.refs_2_) | copy-start | bytes 1990660
  606.9 33.9 %collective-permute-start.28 = (bf16[4,480,384]{2,1,0:T(8,128)(2,1)}, bf16[4,480,384]{2,1,0:T(8,128)(2,1)S(1)}, u32[]{:S(2)}, u32[]{:S(2)}) collective-permute-start(bf16[4,480,384]{2,1,0:T(8,128)(2,1)} %get-tuple-element.282), channel_id=1, source_target_pairs={{0,1},{1,0},{2,3},{3,2},{4,5},{5,4},{6,7},{7,6},{8,9},{9,8},{10,11... | collective-permute-start | bytes 4423688 | tf_op jit(solution)/shard_map/ppermute | solution.py:751
  607.0 20.8 %collective-permute-start.31 = (bf16[3,48,384]{2,1,0:T(8,128)(2,1)S(1)}, bf16[3,48,384]{2,1,0:T(8,128)(2,1)}, u32[]{:S(2)}, u32[]{:S(2)}) collective-permute-start(bf16[3,48,384]{2,1,0:T(8,128)(2,1)S(1)} %copy-done.14), channel_id=1, source_target_pairs={{0,8},{1,9},{2,10},{3,11},{4,12},{5,13},{6,14},{7,15},{8,0},{9,1},... | collective-permute-start | bytes 331784 | tf_op jit(solution)/shard_map/ppermute | solution.py:751
  607.8 29.6 %collective-permute-start.32 = (bf16[3,48,384]{2,1,0:T(8,128)(2,1)S(1)}, bf16[3,48,384]{2,1,0:T(8,128)(2,1)}, u32[]{:S(2)}, u32[]{:S(2)}) collective-permute-start(bf16[3,48,384]{2,1,0:T(8,128)(2,1)S(1)} %copy-done.14), channel_id=1, source_target_pairs={{0,24},{1,25},{2,26},{3,27},{4,28},{5,29},{6,30},{7,31},{8,16},{9,... | collective-permute-start | bytes 331784 | tf_op jit(solution)/shard_map/ppermute | solution.py:751
  637.5 10.3 %copy-start.8 = (bf16[2,4,2,48,768]{4,3,2,1,0:T(8,128)(2,1)}, bf16[2,4,2,48,768]{4,3,2,1,0:T(8,128)(2,1)S(1)}, u32[]{:S(2)}) copy-start(bf16[2,4,2,48,768]{4,3,2,1,0:T(8,128)(2,1)S(1)} %collective-permute-done.29.refs_2_) | copy-start | bytes 3538948
  640.8 6.9 copy-start.5

commit v8 on v7

--- a/solution.py
+++ b/solution.py
@@ -55,35 +55,32 @@
     return [values[at : at + CLUSTER] for at in range(0, values.shape[0], CLUSTER)]
 
 
-def attend_kernel(slot_ref, query_ref, key_ref, value_ref, bias_ref, *refs):
-    ctx_ref, qk_ref, val_ref, p_ref = refs[-4:]
+def attend_pair(slots, query, key, value, bias, store):
     low = first_lanes(TREE_LEN)
-    query = query_ref[...] * jnp.bfloat16(HEAD_DIM**-0.5)
-    key = key_ref[...]
-    value = value_ref[...]
+    query = query * jnp.bfloat16(HEAD_DIM**-0.5)
     packed = (
         jnp.where(low, query, pltpu.roll(key, HEAD_DIM, 1)),
         jnp.where(low, pltpu.roll(query, HEAD_DIM, 1), key),
     )
     context = []
     for head in range(2):
-        table = one_hot_rows(slot_ref[0, 0, head : head + 1, :])
+        table = one_hot_rows(slots[head : head + 1])
         joined = jnp.concatenate([packed[head], value], axis=1)
-        slots = jnp.dot(table, joined, preferred_element_type=jnp.float32).astype(jnp.bfloat16)
-        both, values = slots[:, :LANES], slots[:, LANES:]
-        qk_ref[0, head] = both
-        val_ref[0, head] = values
+        found = jnp.dot(table, joined, preferred_element_type=jnp.float32).astype(jnp.bfloat16)
+        both, values = found[:, :LANES], found[:, LANES:]
+        store("both", head, both)
+        store("values", head, values)
         queries = jnp.where(low, both, jnp.bfloat16(0))
         keys = pltpu.roll(both, HEAD_DIM, 1)
         scores = jnp.concatenate(
             [contract_last(q, k) for q, k in zip(cluster_blocks(queries), cluster_blocks(keys))],
             axis=0,
         )
-        scores = scores + bias_ref[0, head].astype(jnp.float32)
+        scores = scores + bias[head].astype(jnp.float32)
         numerator = jnp.exp(scores - jnp.max(scores, axis=1, keepdims=True))
         total = jnp.sum(numerator, axis=1, keepdims=True)
         soft = (numerator * (1.0 / total)).astype(jnp.bfloat16)
-        p_ref[0, head] = soft
+        store("soft", head, soft)
         out = jnp.concatenate(
             [
                 jnp.dot(p, v, preferred_element_type=jnp.float32)
@@ -92,7 +89,49 @@
             axis=0,
         ).astype(jnp.bfloat16)
         context.append(contract_first(table, out))
-    ctx_ref[...] = jnp.where(low, context[0], context[1]).astype(jnp.bfloat16)
+        if head == 0:
+            yield
+    store("context", None, jnp.where(low, context[0], context[1]).astype(jnp.bfloat16))
+
+
+def attend_kernel(slot_ref, query_ref, key_ref, value_ref, bias_ref, ctx_ref, qk_ref, val_ref, p_ref):
+    refs = {"both": qk_ref, "values": val_ref, "soft": p_ref}
+
+    def store(name, head, value):
+        if head is None:
+            ctx_ref[...] = value
+        else:
+            refs[name][0, head] = value
+
+    for _ in attend_pair(
+        slot_ref[0, 0], query_ref[...], key_ref[...], value_ref[...], bias_ref[0], store
+    ):
+        pass
+
+
+def attend_steps(ins, outs):
+    projected_ref, slot_ref, bias_ref = ins
+    ctx_ref, qk_ref, val_ref, p_ref = outs
+    refs = {"both": qk_ref, "values": val_ref, "soft": p_ref}
+    for tree in range(slot_ref.shape[0]):
+        rows = slice(tree * TREE_LEN, (tree + 1) * TREE_LEN)
+        for pair in range(PAIRS):
+            lanes = [slice((part * PAIRS + pair) * LANES, (part * PAIRS + pair + 1) * LANES) for part in range(3)]
+            heads = slice(2 * pair, 2 * pair + 2)
+
+            def store(name, head, value):
+                if head is None:
+                    ctx_ref[rows, lanes[0]] = value
+                else:
+                    refs[name][tree, 2 * pair + head] = value
+
+            yield from attend_pair(
+                slot_ref[tree, pair],
+                *[projected_ref[rows, part] for part in lanes],
+                bias_ref[tree, heads],
+                store,
+            )
+            yield
 
 
 def attend_back_kernel(at_ref, slot_ref, grad_ref, qk_ref, val_ref, p_ref, out_ref, sums_ref):
@@ -151,34 +190,30 @@
     return pltpu.CompilerParams(vmem_limit_bytes=KERNEL_VMEM)
 
 
-def attend(projected, slots, bias, half, before):
+def attend_shapes(trees):
+    stored = jax.ShapeDtypeStruct((trees, HEADS, TREE_LEN, LANES), jnp.bfloat16)
+    return [jax.ShapeDtypeStruct((trees * TREE_LEN, D), jnp.bfloat16), stored, stored, stored]
+
+
+def attend(projected, slots, bias):
     trees = slots.shape[0]
-    start = half * (PAIRS // 2)
-    stored = jax.ShapeDtypeStruct((trees, HEADS, TREE_LEN, LANES), jnp.bfloat16)
     return pl.pallas_call(
         attend_kernel,
-        grid=(trees, PAIRS // 2),
+        grid=(trees, PAIRS),
         in_specs=[
-            slot_spec(start),
-            column_spec(start),
-            column_spec(PAIRS + start),
-            column_spec(2 * PAIRS + start),
-            head_spec(start),
-        ]
-        + [pl.BlockSpec(memory_space=pl.ANY)] * len(before),
-        out_specs=[column_spec(start), head_spec(start), head_spec(start), head_spec(start)],
-        out_shape=[
-            jax.ShapeDtypeStruct((trees * TREE_LEN, D), jnp.bfloat16),
-            stored,
-            stored,
-            stored,
+            slot_spec(),
+            column_spec(0),
+            column_spec(PAIRS),
+            column_spec(2 * PAIRS),
+            head_spec(),
         ],
-        input_output_aliases={5 + place: place for place in range(len(before))},
+        out_specs=[column_spec(0), head_spec(), head_spec(), head_spec()],
+        out_shape=attend_shapes(trees),
         compiler_params=kernel_params(),
         cost_estimate=pl.CostEstimate(
-            flops=trees * 15_000_000_000, bytes_accessed=trees * 10_000_000, transcendentals=0
+            flops=trees * 30_000_000_000, bytes_accessed=trees * 20_000_000, transcendentals=0
         ),
-    )(slots, projected, projected, projected, bias, *before)
+    )(slots, projected, projected, projected, bias)
 
 
 def attend_back(grad_context, slots, kept, at, other):
@@ -716,19 +751,6 @@
     )(at, *[array for array, _, _ in terms])
 
 
-CHUNKS = {
-    "next": (1, (0, 2), False),
-    "last": (1, (6, 8), False),
-}
-FORWARD = {
-    "ready": ((), ("next",)),
-    (0, "half"): (("next",), ("last",)),
-    (0, "result"): (("next",), ()),
-    (1, "projected"): (("last",), ()),
-    (1, "context"): (("last",), ()),
-}
-
-
 class Place:
     def __init__(self):
         rep = lax.axis_index("rep")
@@ -749,109 +771,6 @@
                     z2, x2 = (z + dz) % CHIPS_Z, (x + dx) % CHIPS_X
                     pairs.append((source, ((y2 * CORES + c2) * CHIPS_Z + z2) * CHIPS_X + x2))
     return lax.ppermute(value, AXES, pairs)
-
-
-def pack_kernel(plan, at_ref, *refs):
-    ins, outs = refs[: len(MATRICES)], refs[len(MATRICES) :]
-    for out_ref, (layer, numbers, split_y) in zip(outs, plan):
-        start = 0
-        for number in numbers:
-            ref = ins[MATRICES.index(number)]
-            rows, half = ref.shape[1], ref.shape[2] // CORES
-            first = 0
-            if split_y:
-                rows = rows // CHIPS_Y
-                first = pl.multiple_of(at_ref[2] * rows, 16)
-            for at in range(0, half, UNIT):
-                column = pl.multiple_of(at_ref[3] * half + at, 128)
-                out_ref[start : start + rows] = ref[layer, pl.ds(first, rows), pl.ds(column, UNIT)]
-                start += rows
-
-
-def chunk_rows(weights, numbers, split_y):
-    found = []
-    for number in numbers:
-        _, rows, columns = weights[number].shape
-        found.append((columns // (CORES * UNIT), rows // (CHIPS_Y if split_y else 1)))
-    return found
-
-
-def pack(weights, names, place):
-    plan = [CHUNKS[name] for name in names]
-    shapes = []
-    for _, numbers, split_y in plan:
-        shapes.append((sum(u * r for u, r in chunk_rows(weights, numbers, split_y)), UNIT))
-    matrices = [weights[number] for number in MATRICES]
-    packed = pl.pallas_call(
-        functools.partial(pack_kernel, plan),
-        grid_spec=pltpu.PrefetchScalarGridSpec(
-            num_scalar_prefetch=1,
-            grid=(1,),
-            in_specs=[pl.BlockSpec(matrix.shape, lambda i, at: (0, 0, 0)) for matrix in matrices],
-            out_specs=[pl.BlockSpec(shape, lambda i, at: (0, 0)) for shape in shapes],
-        ),
-        out_shape=[jax.ShapeDtypeStruct(shape, jnp.bfloat16) for shape in shapes],
-        compiler_params=kernel_params(),
-        cost_estimate=cost(0, *matrices),
-    )(place.at, *matrices)
-    return dict(zip(names, packed))
-
-
-def place_kernel(layout, split_y, count, at_ref, *refs):
-    pieces, outs = refs[:count], refs[count:]
-    for number, piece in enumerate(pieces):
-        core = (at_ref[3] + number % CORES) % CORES
-        x = (at_ref[1] + number // CORES % CHIPS_X) % CHIPS_X
-        row = (at_ref[2] + number // (CORES * CHIPS_X)) % CHIPS_Y if split_y else 0
-        start, unit = 0, piece.shape[2]
-        for out_ref, (units, rows) in zip(outs, layout):
-            for at in range(units):
-                column = pl.multiple_of((core * units + at) * unit, 128)
-                out_ref[x, row, :, pl.ds(column, unit)] = piece[0, start : start + rows]
-                start += rows
-
-
-def place_pieces(pieces, layout, split_y, place):
-    _, held, unit = pieces[0].shape
-    splits = CHIPS_Y if split_y else 1
-    shapes = [(CHIPS_Z * CHIPS_X, splits, rows, CORES * units * unit) for units, rows in layout]
-    wholes = pl.pallas_call(
-        functools.partial(place_kernel, layout, split_y, len(pieces)),
-        grid_spec=pltpu.PrefetchScalarGridSpec(
-            num_scalar_prefetch=1,
-            grid=(CHIPS_Z,),
-            in_specs=[pl.BlockSpec((1, held, unit), lambda k, at: (k, 0, 0))] * len(pieces),
-            out_specs=[
-                pl.BlockSpec(
-                    (CHIPS_X, *shape[1:]),
-                    lambda k, at: (lax.rem(at[0] + CHIPS_Z - k, CHIPS_Z), 0, 0, 0),
-                )
-                for shape in shapes
-            ],
-        ),
-        out_shape=[jax.ShapeDtypeStruct(shape, jnp.bfloat16) for shape in shapes],
-        compiler_params=kernel_params(),
-        cost_estimate=pl.CostEstimate(
-            flops=0,
-            bytes_accessed=4 * CHIPS_Z * len(pieces) * held * unit,
-            transcendentals=0,
-        ),
-    )(place.at, *pieces)
-    return [whole.reshape(-1, whole.shape[-1]) for whole in wholes]
-
-
-def gather_chain(block, layout, split_y, place):
-    parts = yield [hop(block, dz=k) for k in range(1, CHIPS_Z)]
-    stack = jnp.stack([block, *parts])
-    (across,) = yield [hop(stack, dx=1)]
-    pieces = [stack, across]
-    if split_y:
-        pieces = pieces + (yield [hop(piece, dy=1) for piece in pieces])
-    others = yield [hop(piece, dc=1) for piece in pieces]
-    wholes = place_pieces(
-        [item for pair in zip(pieces, others) for item in pair], layout, split_y, place
-    )
-    return wholes
 
 
 class Flow:
@@ -966,10 +885,20 @@
     return add(own, *landed)
 
 
-def gather_kernel(plan, *refs):
+def prep_steps(ins, outs):
+    trees, pairs = ins[2].shape[:2]
+    for tree in range(trees):
+        for pair in range(pairs):
+            prep_pair(*ins, *outs, tree, tree, pair)
+            yield
+
+
+def gather_kernel(plan, work, work_ins, work_outs, *refs):
     count = len(plan)
-    prep_ins, ins, refs = refs[:3], refs[3 : 3 + count], refs[3 + count :]
-    prep_outs, outs, sems, local_sem = refs[:2], refs[2 : 2 + count], refs[2 + count : -1], refs[-1]
+    own_ins, ins, refs = refs[:work_ins], refs[work_ins : work_ins + count], refs[work_ins + count :]
+    own_outs, outs = refs[:work_outs], refs[work_outs : work_outs + count]
+    sems, local_sem = refs[work_outs + count : -1], refs[-1]
+    todo = work(own_ins, own_outs)
     rep, shard = lax.axis_index("rep"), lax.axis_index("shard")
     y, core = lax.div(rep, CORES), lax.rem(rep, CORES)
     z, x = lax.div(shard, CHIPS_X), lax.rem(shard, CHIPS_X)
@@ -1036,6 +965,8 @@
 
     def after_x(m):
         for k in range(CHIPS_Z):
+            if k % 2:
+                next(todo, None)
             along_x[m][k].wait_recv()
             spread(m, behind(k), 1 - x)
         if plan[m][2]:
@@ -1056,59 +987,53 @@
         along_z[m] = [send(mine, mine, m, k - 1, dz=k) for k in range(1, CHIPS_Z)]
         along_x[m], over_y[m] = [], []
         spread(m, z, x)
-    trees, pairs = prep_ins[2].shape[:2]
-    todo = [(tree, tree, pair) for tree in range(trees) for pair in range(pairs)]
     for place, m in enumerate(order):
         for k in range(1, CHIPS_Z):
-            if todo:
-                prep_pair(*prep_ins, *prep_outs, *todo.pop(0))
+            next(todo, None)
             along_z[m][k - 1].wait_recv()
             spread(m, behind(k), x)
         if place:
             after_x(order[place - 1])
-    for item in todo:
-        prep_pair(*prep_ins, *prep_outs, *item)
     after_x(order[-1])
     for m in order:
         after_y(m)
+        next(todo, None)
+    for _ in todo:
+        pass
     for copy in last:
         copy.wait_recv()
     for copy in sent:
         copy.wait_send()
 
 
-def gather_layer(segment, parent, clusters, vectors, weights, layer, tall):
+def gather(weights, wanted, work, work_args, work_shapes, number):
     low = jnp.bfloat16
-    args, plan, shapes = [vectors], [(None, False, False)], [(1, *vectors.shape)]
-    for number in MATRICES:
-        _, rows, columns = weights[number].shape
-        split = CHIPS_Y if number in tall else 1
-        args.append(weights[number])
-        plan.append((layer, split > 1, True))
-        shapes.append((split, rows // split, columns))
-    shapes = [jax.ShapeDtypeStruct((CHIPS_Z, CHIPS_X, *shape), low) for shape in shapes]
-    trees = parent.shape[0]
-    segment = segment.reshape(trees, 1, TREE_LEN)
-    clusters = clusters.reshape(PAIRS, 2, trees, TREE_LEN).transpose(2, 0, 1, 3)
-    prepared = [
-        jax.ShapeDtypeStruct(clusters.shape, jnp.int32),
-        jax.ShapeDtypeStruct((trees, HEADS, TREE_LEN, LANES), low),
-    ]
+    args, plan, shapes = [], [], []
+    for which, layer, split_y in wanted:
+        args.append(weights[which])
+        plan.append((layer, split_y, layer is not None))
+        rows, columns = weights[which].shape[-2:]
+        split = CHIPS_Y if split_y else 1
+        shapes.append((CHIPS_Z, CHIPS_X, split, rows // split, columns))
     whole = pl.BlockSpec(memory_space=pltpu.VMEM)
-    slots, bias, *found = pl.pallas_call(
-        functools.partial(gather_kernel, plan),
-        in_specs=[pl.BlockSpec(memory_space=pltpu.SMEM), whole, whole]
+    small = pl.BlockSpec(memory_space=pltpu.SMEM)
+    found = pl.pallas_call(
+        functools.partial(gather_kernel, plan, work, len(work_args), len(work_shapes)),
+        in_specs=[small if arg.shape[-1] == SEGMENTS else whole for arg in work_args]
         + [pl.BlockSpec(memory_space=pl.ANY)] * len(args),
-        out_specs=[whole] * (2 + len(args)),
-        out_shape=prepared + shapes,
+        out_specs=[whole] * (len(work_shapes) + len(args)),
+        out_shape=work_shapes + [jax.ShapeDtypeStruct(shape, low) for shape in shapes],
         scratch_shapes=[pltpu.SemaphoreType.DMA((2, 17))] * len(args)
         + [pltpu.SemaphoreType.DMA((len(args),))],
         compiler_params=pltpu.CompilerParams(
-            vmem_limit_bytes=KERNEL_VMEM, collective_id=1, has_side_effects=True
+            vmem_limit_bytes=KERNEL_VMEM, collective_id=number, has_side_effects=True
         ),
         cost_estimate=pl.CostEstimate(flops=0, bytes_accessed=200_000_000, transcendentals=0),
-    )(parent, segment, clusters, *args)
-    return slots, bias, found[0], [item.reshape(-1, item.shape[-1]) for item in found[1:]]
+    )(*work_args, *args)
+    results, arrays = list(found[: len(work_shapes)]), found[len(work_shapes) :]
+    for item, array in zip(wanted, arrays):
+        results.append(array if item[1] is None else array.reshape(-1, array.shape[-1]))
+    return results
 
 
 def pack_sums(out_ref, core, ins):
@@ -1396,31 +1321,43 @@
     if fast:
         place = Place()
         at = place.at
-        blocks = pack(weights, list(CHUNKS), place)
-        own_vectors = jnp.concatenate([weights[member] for member in VECTORS], axis=1)
-        own_vectors = jnp.pad(own_vectors, ((0, 16 - LAYERS), (0, 0)))
-        slots, bias, found, lowest = gather_layer(
-            segment, parent, clusters, own_vectors, weights, 0, (6, 8, 2)
+        shards = dict(enumerate(weights))
+        shards["vectors"] = jnp.pad(
+            jnp.concatenate([weights[member] for member in VECTORS], axis=1),
+            ((0, 16 - LAYERS), (0, 0)),
+        )
+        trees = parent.shape[0]
+        slots, bias, found, qkv = gather(
+            shards,
+            (("vectors", None, False), (0, 0, True)),
+            prep_steps,
+            (
+                parent,
+                segment.reshape(trees, 1, TREE_LEN),
+                clusters.reshape(PAIRS, 2, trees, TREE_LEN).transpose(2, 0, 1, 3),
+            ),
+            [
+                jax.ShapeDtypeStruct((trees, PAIRS, 2, TREE_LEN), jnp.int32),
+                jax.ShapeDtypeStruct((trees, HEADS, TREE_LEN, LANES), jnp.bfloat16),
+            ],
+            1,
         )
         vectors = spread_vectors(found, [weights[number].shape[1] for number in VECTORS])
+        whole = {(0, 0): qkv}
+
+        def attend_layer(layer, projected):
+            wanted = [(6, layer, True), (8, layer, True), (2, layer, True)]
+            if layer + 1 < LAYERS:
+                wanted.insert(2, (0, layer + 1, False))
+            results = gather(
+                shards, wanted, attend_steps, (projected, slots, bias), attend_shapes(trees), 2 + layer
+            )
+            for (number, at_layer, _), array in zip(wanted, results[4:]):
+                whole[at_layer, number] = array
+            return results[:4]
 
         def get(layer, number):
-            if layer == 0:
-                return lowest[MATRICES.index(number)]
-            else:
-                for name, (chunk_layer, numbers, _) in CHUNKS.items():
-                    if chunk_layer == layer and number in numbers:
-                        return flow.finish(name)[numbers.index(number)]
-
-        def step(point, main):
-            advanced, started = FORWARD.get(point, ((), ()))
-            fresh = [blocks[name] for name in started]
-            main, fresh = flow.tick((main, fresh), *advanced)
-            for name, block in zip(started, fresh):
-                _, numbers, split_y = CHUNKS[name]
-                layout = chunk_rows(weights, numbers, split_y)
-                flow.start(name, gather_chain(block, layout, split_y, place))
-            return main
+            return whole[layer, number]
 
         def reduce(layer, *grads):
             name = ("grad", layer, grads[0].number)
@@ -1444,11 +1381,11 @@
             for number in VECTORS
         ]
 
+        def attend_layer(layer, projected):
+            return attend(projected, slots, bias)
+
         def get(layer, number):
             return lax.all_gather(weights[number][layer], "shard", axis=0, tiled=True)
-
-        def step(point, main):
-            return main
 
         def reduce(layer, *grads):
             for grad in grads:
@@ -1469,15 +1406,8 @@
     saved = []
     for layer in range(LAYERS):
         pull = functools.partial(get, layer)
-        weight = pull(0)
-        if layer == 0:
-            weight = step("ready", weight)
-        projected = project(layer, hidden_low, weight, vector[1])
-        projected = step((layer, "projected"), projected)
-        first = attend(projected, slots, bias, 0, ())
-        first = step((layer, "half"), first)
-        context, *heads = attend(projected, slots, bias, 1, first)
-        context = step((layer, "context"), context)
+        projected = project(layer, hidden_low, pull(0), vector[1])
+        context, *heads = attend_layer(layer, projected)
         entered = hidden_low
         middle, act, slope, *norms, hidden, hidden_low = feed(
             layer,
@@ -1486,7 +1416,6 @@
             [pull(2), pull(6), pull(8)],
             [vector[number] for number in (3, 4, 5, 7, 9, 10, 11)],
         )
-        hidden_low = step((layer, "result"), hidden_low)
         saved.append((entered, heads, context, middle, act, slope, norms))
     result = hidden_low
     above, proj = cotangent, None

time: 775 us -> 741 us (0.956)
  waiting for transfers between devices: 98.8 us -> 49.4 us
  Pallas kernels: 607 us -> 645 us
  starting transfers between devices: 31.8 us -> 12.7 us
    pallas_call x8 -> x3, Pallas kernels: 169 us -> 220 us  [gather(): pl.pallas_call(functools.partial(gather_kernel, plan, work, len(work_args...]
    ppermute x34 -> x22, waiting for transfers between devices: 98.8 us -> 49.4 us  [hop(): return lax.ppermute(value, AXES, pairs)]
    ppermute x34 -> x22, starting transfers between devices: 31.8 us -> 12.7 us  [hop(): return lax.ppermute(value, AXES, pairs)]
    pallas_call x2, Pallas kernels: 68 us -> 56.3 us  [feed(): pl.pallas_call(functools.partial(feed_kernel, layer), grid=(count // ROW_...]
  transfers between devices with their start and end apart: 34 -> 22, of which waited for: 9 -> 5; matrix products, arithmetic and copies ran while one was open for 1% -> 0% of each run, Pallas kernels for 42% -> 26%
where the time goes in v8:
time: 741 us; the launch traced here: 730 us
  Pallas kernels  645 us (87%)
  waiting for transfers between devices  49.4 us (7%)
  local copies, waits for them, and re-layouts  17.4 us (2%)
  starting transfers between devices  12.7 us (2%)
    pallas_call x3, Pallas kernels, gather(): pl.pallas_call(functools.partial(gather_kernel, plan, work, len(work_args...  220 us
    pallas_call x16, Pallas kernels, product(): pl.pallas_call(functools.partial(weight_grad_kernel, split_y), grid_spec=...  107 us
    pallas_call x1, Pallas kernels, reduce_tail(): pl.pallas_call(functools.partial(tail_kernel, arrived), in_specs=[*specs,...  83.8 us
    pallas_call x4, Pallas kernels, attend_back(): pl.pallas_call(attend_back_kernel, grid_spec=pltpu.PrefetchScalarGridSpec...  74.9 us
    pallas_call x2, Pallas kernels, feed(): pl.pallas_call(functools.partial(feed_kernel, layer), grid=(count // ROW_...  56.3 us
    pallas_call x2, Pallas kernels, feed_back(): pl.pallas_call(functools.partial(feed_back_kernel, layer, proj is not Non...  53.1 us
    ppermute x22, waiting for transfers between devices, hop(): return lax.ppermute(value, AXES, pairs)  49.4 us
    pallas_call x5, Pallas kernels, combine(): pl.pallas_call(functools.partial(combine_kernel, [len(group) for group in...  19.2 us
  transfers between devices with their start and end apart: 22, of which 5 were waited for; matrix products, arithmetic and copies ran while one was open for 0% of the time, Pallas kernels for 26%

profile of v8, /device:TPU:17, one launch (start us, length us, event | category | flops | bytes accessed | tf_op | source)
XLA Modules:
  0.0 730.2 jit_solution(15680111161782903393)
XLA Ops:
  0.6 1.5 transpose_reshape.3.refs_2_
  2.1 0.9 concatenate.3
  3.6 40.2 %shard_map.272 = (s32[1,6,2,1024]{3,2,1,0:T(2,128)}, bf16[1,12,1024,128]{3,2,1,0:T(8,128)(2,1)}, bf16[4,2,1,16,1152]{4,3,2,1,0:T(8,128)(2,1)}, bf16[4,2,2,48,2304]{4,3,2,1,0:T(8,128)(2,1)}) custom-call(s32[1,13]{1,0:T(1,128)} %refs_0_.2, s32[1,1,1024]{2,1,0:T(1,128)} %bitcast.67, s32[1,6,2,1024]{3,2,1,0:T(2,128)} %transpose_reshape.3.refs_2_, ...), custom_call_target="tpu_custom_call" | custom-call | bytes 200000000 | tf_op jit(solution)/shard_map/pallas_call | solution.py:1020
  43.8 0.9 slice.83
  45.1 0.7 reshape.122.bias_ref
  46.4 0.7 reshape.128.ffn_gain_ref.refs_10_.refs_14_
  49.1 0.7 reshape.129.ffn_shift_ref
  50.4 7.9 %shard_map.273.refs_0_ = bf16[1024,2304]{1,0:T(8,128)(2,1)} custom-call(bf16[1024,768]{1,0:T(8,128)(2,1)} %left_ref.3, bf16[768,2304]{1,0:T(8,128)(2,1)} %bitcast.76, f32[2,1536]{1,0:T(2,128)} %reshape.122.bias_ref), custom_call_target="tpu_custom_call" | custom-call | flops 4348654592 | bytes 5111808 | tf_op jit(solution)/shard_map/pallas_call | solution.py:502
  58.3 91.5 %shard_map.274 = (bf16[1024,768]{1,0:T(8,128)(2,1)}, bf16[1,12,1024,128]{3,2,1,0:T(8,128)(2,1)}, bf16[1,12,1024,128]{3,2,1,0:T(8,128)(2,1)}, bf16[1,12,1024,128]...) custom-call(bf16[1024,2304]{1,0:T(8,128)(2,1)} %shard_map.273.refs_0, ...), custom_call_target="tpu_custom_call" | custom-call | bytes 200000000 | tf_op jit(solution)/shard_map/pallas_call | solution.py:1020
  149.8 27.9 %shard_map.275 = (bf16[1024,768]{1,0:T(8,128)(2,1)}, bf16[1024,3072]{1,0:T(8,128)(2,1)}, bf16[1024,3072]{1,0:T(8,128)(2,1)}, f32[1024,768]{1,0:T(8,128)}, f32[10...) custom-call(bf16[1024,768]{1,0:T(8,128)(2,1)} %get-tuple-element.146, ...), custom_call_target="tpu_custom_call" | custom-call | flops 27179089920 | bytes 12189696 | tf_op jit(solution)/shard_map/pallas_call | solution.py:517
  177.7 8.2 %shard_map.276.refs_0_ = bf16[1024,2304]{1,0:T(8,128)(2,1)} custom-call(bf16[1024,768]{1,0:T(8,128)(2,1)} %get-tuple-element.150.rows_ref.left_ref, bf16[768,2304]{1,0:T(8,128)(2,1)} %bitcast.78, f32[2,1536]{1,0:T(2,128)} %reshape.122.bias_ref), custom_call_target="tpu_custom_call" | custom-call | flops 4348654592 | bytes 5111808 | tf_op jit(solution)/shard_map/pallas_call | solution.py:502
  186.0 88.0 %shard_map.277 = (bf16[1024,768]{1,0:T(8,128)(2,1)}, bf16[1,12,1024,128]{3,2,1,0:T(8,128)(2,1)}, bf16[1,12,1024,128]{3,2,1,0:T(8,128)(2,1)}, bf16[1,12,1024,128]...) custom-call(bf16[1024,2304]{1,0:T(8,128)(2,1)} %shard_map.276.refs_0, ...), custom_call_target="tpu_custom_call" | custom-call | bytes 200000000 | tf_op jit(solution)/shard_map/pallas_call | solution.py:1020
  274.6 28.4 %shard_map.278 = (bf16[1024,768]{1,0:T(8,128)(2,1)}, bf16[1024,3072]{1,0:T(8,128)(2,1)}, bf16[1024,3072]{1,0:T(8,128)(2,1)}, f32[1024,768]{1,0:T(8,128)}, f32[10...) custom-call(bf16[1024,768]{1,0:T(8,128)(2,1)} %get-tuple-element.152, ...), custom_call_target="tpu_custom_call" | custom-call | flops 27179089920 | bytes 12189696 | tf_op jit(solution)/shard_map/pallas_call | solution.py:517
  303.0 21.7 %shard_map.279 = (bf16[1024,768]{1,0:T(8,128)(2,1)}, bf16[1024,3072]{1,0:T(8,128)(2,1)}, f32[1024,768]{1,0:T(8,128)}, bf16[1024,768]{1,0:T(8,128)(2,1)}, bf16[10...) custom-call(bf16[1024,768]{1,0:T(8,128)(2,1)} %refs_0_.3, f32[1024,768]{1,0:T(8,128)} %get-tuple-element.158.refs_1_, ...), custom_call_target="tpu_custom_call" | custom-call | flops 27179089920 | bytes 12189696 | tf_op jit(solution)/shard_map/pallas_call | solution.py:563
  324.7 7.6 %shard_map.281 = bf16[4,4,2,96,384]{4,3,2,1,0:T(8,128)(2,1)} custom-call(s32[4]{0:T(128)} %pad_add_fusion.at_ref.refs_1_, bf16[1024,768]{1,0:T(8,128)(2,1)} %get-tuple-element.167.left_ref, bf16[1024,3072]{1,0:T(8,128)(2,1)} %get-tuple-element.168.right_ref), custom_call_target="tpu_custom_call" | custom-call | flops 4831838208 | bytes 7864320 | tf_op jit(solution)/shard_map/pallas_call | solution.py:707
  332.4 7.9 %shard_map.280 = bf16[1,4,2,384,384]{4,3,2,1,0:T(8,128)(2,1)} custom-call(s32[4]{0:T(128)} %pad_add_fusion.at_ref.refs_1_, bf16[1024,3072]{1,0:T(8,128)(2,1)} %get-tuple-element.165.left_ref, bf16[1024,768]{1,0:T(8,128)(2,1)} %get-tuple-element.166.right_ref), custom_call_target="tpu_custom_call" | custom-call | flops 4831838208 | bytes 7864320 | tf_op jit(solution)/shard_map/pallas_call | solution.py:707
  340.7 4.1 shard_map.282
  344.9 2.1 collective-permute-done.2.refs_0_
  347.0 18.9 %shard_map.286 = (bf16[3,1024,384]{2,1,0:T(8,128)(2,1)}, f32[1,3,8,128]{3,2,1,0:T(8,128)}) custom-call(s32[4]{0:T(128)} %pad_add_fusion.at_ref.refs_1_, s32[1,6,2,1024]{3,2,1,0:T(2,128)} %get-tuple-element.144.refs_1_.slot_ref, bf16[1024,768]{1,0:T(8,128)(2,1)} %get-tuple-element.183.grad_ref, bf16[1,12,1024,128]{3,2,1,0:T(8,128)(2,1)} %get-tuple-element.179.qk_ref, ...), custom_call_target="tpu_custom_call" | custom-call | flops 16999999488 | bytes 10000000 | tf_op jit(solution)/shard_map/pallas_call | solution.py:230
  366.0 6.5 shard_map.288
  372.6 8.4 %shard_map.283 = (bf16[4,864,384]{2,1,0:T(8,128)(2,1)}, bf16[4,864,384]{2,1,0:T(8,128)(2,1)}) custom-call(s32[4]{0:T(128)} %pad_add_fusion.at_ref.refs_1_, bf16[1024,3072]{1,0:T(8,128)(2,1)} %get-tuple-element.165.left_ref, bf16[1024,768]{1,0:T(8,128)(2,1)} %get-tuple-element.166.right_ref, bf16[1,4,2,384,384]{4,3,2,1,0:T(8,128)(2,1)} %collective-permute-done.refs_0_), custom_call_target="tpu_custom_call" | custom-call | flops 4831838208 | bytes 7864320 | tf_op jit(solution)/shard_map/pallas_call | solution.py:707
  381.0 8.3 %shard_map.284 = (bf16[4,864,384]{2,1,0:T(8,128)(2,1)}, bf16[4,864,384]{2,1,0:T(8,128)(2,1)}) custom-call(s32[4]{0:T(128)} %pad_add_fusion.at_ref.refs_1_, bf16[1024,768]{1,0:T(8,128)(2,1)} %get-tuple-element.167.left_ref, bf16[1024,3072]{1,0:T(8,128)(2,1)} %get-tuple-element.168.right_ref, ...), custom_call_target="tpu_custom_call", output_to_operand_aliasing={{0}: (4, {}), {1}: (5, {})} | custom-call | flops 4831838208 | bytes 7864320 | tf_op jit(solution)/shard_map/pallas_call | solution.py:707
  389.3 4.3 shard_map.285
  393.8 18.8 %shard_map.287 = (bf16[3,1024,384]{2,1,0:T(8,128)(2,1)}, f32[1,3,8,128]{3,2,1,0:T(8,128)}) custom-call(s32[4]{0:T(128)} %pad_add_fusion.at_ref.refs_1_, s32[1,6,2,1024]{3,2,1,0:T(2,128)} %get-tuple-element.144.refs_1_.slot_ref, bf16[1024,768]{1,0:T(8,128)(2,1)} %get-tuple-element.183.grad_ref, bf16[1,12,1024,128]{3,2,1,0:T(8,128)(2,1)} %get-tuple-element.179.qk_ref, ...), custom_call_target="tpu_custom_call" | custom-call | flops 16999999488 | bytes 10000000 | tf_op jit(solution)/shard_map/pallas_call | solution.py:230
  412.7 7.0 shard_map.290
  419.6 1.2 collective-permute-start.5
  420.8 31.4 %shard_map.289 = (bf16[1024,768]{1,0:T(8,128)(2,1)}, bf16[1024,3072]{1,0:T(8,128)(2,1)}, f32[1024,768]{1,0:T(8,128)}, bf16[1024,768]{1,0:T(8,128)(2,1)}, bf16[10...) custom-call(f32[1024,768]{1,0:T(8,128)} %get-tuple-element.177.refs_0_, s32[4]{0:T(128)} %pad_add_fusion.at_ref.refs_1_, ...), custom_call_target="tpu_custom_call" | custom-call | flops 27179089920 | bytes 13762560 | tf_op jit(solution)/shard_map/pallas_call | solution.py:563
  452.2 6.5 shard_map.295
  458.7 0.9 collective-permute-start.9
  459.6 8.4 %shard_map.293 = bf16[1,4,2,384,384]{4,3,2,1,0:T(8,128)(2,1)} custom-call(s32[4]{0:T(128)} %pad_add_fusion.at_ref.refs_1_, bf16[1024,3072]{1,0:T(8,128)(2,1)} %get-tuple-element.202.left_ref, bf16[1024,768]{1,0:T(8,128)(2,1)} %get-tuple-element.203.right_ref), custom_call_target="tpu_custom_call" | custom-call | flops 4831838208 | bytes 7864320 | tf_op jit(solution)/shard_map/pallas_call | solution.py:707
  468.1 4.1 shard_map.294
  472.6 4.0 shard_map.292
  476.6 1.2 collective-permute-start.6
  477.8 5.5 shard_map.291
  483.3 1.0 collective-permute-start.13
  484.3 4.3 collective-permute-done.6.refs_2_.refs_5_.refs_8_.refs_11_
  488.6 0.8 copy-done.2
  489.4 2.9 shard_map.297
  492.3 1.0 collective-permute-start.10
  493.2 1.2 collective-permute-start.12
  494.5 18.6 %shard_map.296 = (bf16[3,1024,384]{2,1,0:T(8,128)(2,1)}, f32[1,3,8,128]{3,2,1,0:T(8,128)}) custom-call(s32[4]{0:T(128)} %pad_add_fusion.at_ref.refs_1_, s32[1,6,2,1024]{3,2,1,0:T(2,128)} %get-tuple-element.144.refs_1_.slot_ref, bf16[1024,768]{1,0:T(8,128)(2,1)} %get-tuple-element.216.grad_ref, bf16[1,12,1024,128]{3,2,1,0:T(8,128)(2,1)} %get-tuple-element.208.qk_ref, ...), custom_call_target="tpu_custom_call" | custom-call | flops 16999999488 | bytes 10000000 | tf_op jit(solution)/shard_map/pallas_call | solution.py:230
  513.1 7.0 shard_map.301
  520.1 29.5 %collective-permute-done.10.refs_1_ = bf16[3,48,384]{2,1,0:T(8,128)(2,1)S(1)} collective-permute-done((bf16[3,48,384]{2,1,0:T(8,128)(2,1)}, bf16[3,48,384]{2,1,0:T(8,128)(2,1)S(1)}, u32[]{:S(2)}, u32[]{:S(2)}) %collective-permute-start.10) | collective-permute-done | bytes 110624 | tf_op jit(solution)/shard_map/ppermute | solution.py:773
  549.6 6.7 shard_map.303
  556.3 1.9 collective-permute-start.21
  558.2 8.5 %shard_map.299 = (bf16[4,480,384]{2,1,0:T(8,128)(2,1)}, bf16[4,480,384]{2,1,0:T(8,128)(2,1)}) custom-call(s32[4]{0:T(128)} %pad_add_fusion.at_ref.refs_1_, bf16[1024,3072]{1,0:T(8,128)(2,1)} %get-tuple-element.202.left_ref, bf16[1024,768]{1,0:T(8,128)(2,1)} %get-tuple-element.203.right_ref, bf16[1,4,2,384,384]{4,3,2,1,0:T(8,128)(2,1)} %collective-permute-done.7.refs_0_), custom_call_target="tpu_custom_call" | custom-call | flops 4831838208 | bytes 7864320 | tf_op jit(solution)/shard_map/pallas_call | solution.py:707
  566.6 2.4 shard_map.302
  569.4 4.5 shard_map.300
  573.8 1.2 collective-permute-start.17
  575.3 0.9 collective-permute-start.19
  576.4 18.6 %shard_map.298 = (bf16[3,1024,384]{2,1,0:T(8,128)(2,1)}, f32[1,3,8,128]{3,2,1,0:T(8,128)}) custom-call(s32[4]{0:T(128)} %pad_add_fusion.at_ref.refs_1_, s32[1,6,2,1024]{3,2,1,0:T(2,128)} %get-tuple-element.144.refs_1_.slot_ref, bf16[1024,768]{1,0:T(8,128)(2,1)} %get-tuple-element.216.grad_ref, bf16[1,12,1024,128]{3,2,1,0:T(8,128)(2,1)} %get-tuple-element.208.qk_ref, ...), custom_call_target="tpu_custom_call" | custom-call | flops 16999999488 | bytes 10000000 | tf_op jit(solution)/shard_map/pallas_call | solution.py:230
  595.0 9.4 %collective-permute-done.20 = bf16[3,48,384]{2,1,0:T(8,128)(2,1)} collective-permute-done((bf16[3,48,384]{2,1,0:T(8,128)(2,1)S(1)}, bf16[3,48,384]{2,1,0:T(8,128)(2,1)}, u32[]{:S(2)}, u32[]{:S(2)}) %collective-permute-start.20) | collective-permute-done | bytes 110624 | tf_op jit(solution)/shard_map/ppermute | solution.py:773
  604.4 4.1 collective-permute-done.16.refs_0_
  608.5 6.9 shard_map.306
  615.4 9.6 %shard_map.305 = f32[1024,768]{1,0:T(8,128)} custom-call(f32[1024,768]{1,0:T(8,128)} %get-tuple-element.236.above_ref, s32[4]{0:T(128)} %pad_add_fusion.at_ref.refs_1_, bf16[3,1024,384]{2,1,0:T(8,128)(2,1)} %get-tuple-element.237.own_ref.right_ref, bf16[3,1024,384]{2,1,0:T(8,128)(2,1)} %get-tuple-element.238.right_ref.away_ref, bf16[768,2304]{1,0:T(8,128)(2,1)} %bitcast.77), custom_call_target="tpu_custom_call" | custom-call | flops 4348654592 | bytes 6684672 | tf_op jit(solution)/shard_map/pallas_call | solution.py:595
  625.1 4.4 shard_map.304.refs_6_
  629.5 83.8 %shard_map.307 = (bf16[480,384]{1,0:T(8,128)(2,1)}, bf16[480,384]{1,0:T(8,128)(2,1)}, bf16[4,2,48,768]{3,2,1,0:T(8,128)(2,1)}, bf16[4,3,48,384]{3,2,1,0:T(8,128)...) custom-call(bf16[4,480,384]{2,1,0:T(8,128)(2,1)} %copy-done.3, ...), custom_call_target="tpu_custom_call" | custom-call | bytes 200000000 | tf_op jit(solution)/shard_map/pallas_call | solution.py:1253
  713.3 1.1 fusion.10
  714.4 0.8 slice_bitcast_fusion
  715.2 0.8 slice.92
  716.0 0.8 slice.93
  716.8 2.0 fusion.8
  718.7 1.9 fusion.9
  723.9 6.1 shard_map.308
  (77 shorter events, 10.5 us)
Async XLA Ops:
  332.3 14.7 %collective-permute-start.1 = (bf16[4,4,2,96,384]{4,3,2,1,0:T(8,128)(2,1)}, bf16[4,4,2,96,384]{4,3,2,1,0:T(8,128)(2,1)S(1)}, u32[]{:S(2)}, u32[]{:S(2)}) collective-permute-start(bf16[4,4,2,96,384]{4,3,2,1,0:T(8,128)(2,1)} %shard_map.281), channel_id=1, source_target_pairs={{0,8},{1,9},{2,10},{3,11},{4,12},{5,13},{6,14},{7,15},{8,0},{9,1},... | collective-permute-start | bytes 7077896 | tf_op jit(solution)/shard_map/ppermute | solution.py:773
  340.3 6.8 collective-permute-start
  344.8 2.2 collective-permute-start.2
  347.0 18.9 %copy-start.7 = (bf16[1,4,2,96,384]{4,3,2,1,0:T(8,128)(2,1)}, bf16[1,4,2,96,384]{4,3,2,1,0:T(8,128)(2,1)S(1)}, u32[]{:S(2)}) copy-start(bf16[1,4,2,96,384]{4,3,2,1,0:T(8,128)(2,1)S(1)} %collective-permute-done.2.refs_0_) | copy-start | bytes 1769476
  347.0 18.9 %copy-start.13 = (bf16[4,4,2,96,384]{4,3,2,1,0:T(8,128)(2,1)}, bf16[4,4,2,96,384]{4,3,2,1,0:T(8,128)(2,1)S(1)}, u32[]{:S(2)}) copy-start(bf16[4,4,2,96,384]{4,3,2,1,0:T(8,128)(2,1)S(1)} %collective-permute-done.1.refs_0_) | copy-start | bytes 7077892
  372.5 40.2 %collective-permute-start.3 = (bf16[3,4,2,96,384]{4,3,2,1,0:T(8,128)(2,1)}, bf16[3,4,2,96,384]{4,3,2,1,0:T(8,128)(2,1)}, u32[]{:S(2)}, u32[]{:S(2)}) collective-permute-start(bf16[3,4,2,96,384]{4,3,2,1,0:T(8,128)(2,1)} %shard_map.288), channel_id=1, source_target_pairs={{0,8},{1,9},{2,10},{3,11},{4,12},{5,13},{6,14},{7,15},{8,0},{9,1},... | collective-permute-start | bytes 5308424 | tf_op jit(solution)/shard_map/ppermute | solution.py:773
  393.6 66.0 %collective-permute-start.4 = (bf16[4,864,384]{2,1,0:T(8,128)(2,1)}, bf16[4,864,384]{2,1,0:T(8,128)(2,1)S(1)}, u32[]{:S(2)}, u32[]{:S(2)}) collective-permute-start(bf16[4,864,384]{2,1,0:T(8,128)(2,1)} %get-tuple-element.194), channel_id=1, source_target_pairs={{0,1},{1,0},{2,3},{3,2},{4,5},{5,4},{6,7},{7,6},{8,9},{9,8},{10,11... | collective-permute-start | bytes 7962632 | tf_op jit(solution)/shard_map/ppermute | solution.py:773
  419.6 40.0 %collective-permute-start.5 = (bf16[3,4,2,48,384]{4,3,2,1,0:T(8,128)(2,1)}, bf16[3,4,2,48,384]{4,3,2,1,0:T(8,128)(2,1)S(1)}, u32[]{:S(2)}, u32[]{:S(2)}) collective-permute-start(bf16[3,4,2,48,384]{4,3,2,1,0:T(8,128)(2,1)} %get-tuple-element.196), channel_id=1, source_target_pairs={{0,16},{1,17},{2,18},{3,19},{4,20},{5,21},{6,22},{7,23},{8,24},{9,... | collective-permute-start | bytes 2654216 | tf_op jit(solution)/shard_map/ppermute | solution.py:773
  458.7 29.9 %collective-permute-start.9 = (bf16[2,4,2,96,768]{4,3,2,1,0:T(8,128)(2,1)}, bf16[2,4,2,96,768]{4,3,2,1,0:T(8,128)(2,1)}, u32[]{:S(2)}, u32[]{:S(2)}) collective-permute-start(bf16[2,4,2,96,768]{4,3,2,1,0:T(8,128)(2,1)} %shard_map.295), channel_id=1, source_target_pairs={{0,8},{1,9},{2,10},{3,11},{4,12},{5,13},{6,14},{7,15},{8,0},{9,1},... | collective-permute-start | bytes 7077896 | tf_op jit(solution)/shard_map/ppermute | solution.py:773
  459.6 8.4 %copy-start = (bf16[4,864,384]{2,1,0:T(8,128)(2,1)}, bf16[4,864,384]{2,1,0:T(8,128)(2,1)S(1)}, u32[]{:S(2)}) copy-start(bf16[4,864,384]{2,1,0:T(8,128)(2,1)S(1)} %collective-permute-done.4.refs_1_.refs_3_.refs_5_.refs_7_) | copy-start | bytes 7962628
  459.6 8.4 %copy-start.1 = (bf16[3,4,2,48,384]{4,3,2,1,0:T(8,128)(2,1)}, bf16[3,4,2,48,384]{4,3,2,1,0:T(8,128)(2,1)S(1)}, u32[]{:S(2)}) copy-start(bf16[3,4,2,48,384]{4,3,2,1,0:T(8,128)(2,1)S(1)} %collective-permute-done.5.refs_1_.refs_4_.refs_7_.refs_10_) | copy-start | bytes 2654212
  468.0 20.6 %collective-permute-start.7 = (bf16[1,4,2,384,384]{4,3,2,1,0:T(8,128)(2,1)}, bf16[1,4,2,384,384]{4,3,2,1,0:T(8,128)(2,1)}, u32[]{:S(2)}, u32[]{:S(2)}) collective-permute-start(bf16[1,4,2,384,384]{4,3,2,1,0:T(8,128)(2,1)} %shard_map.293), channel_id=1, source_target_pairs={{0,8},{1,9},{2,10},{3,11},{4,12},{5,13},{6,14},{7,15},{8,0},{9,1},... | collective-permute-start | bytes 7077896 | tf_op jit(solution)/shard_map/ppermute | solution.py:773
  472.1 12.2 %collective-permute-start.8 = (bf16[1,4,2,96,384]{4,3,2,1,0:T(8,128)(2,1)}, bf16[1,4,2,96,384]{4,3,2,1,0:T(8,128)(2,1)S(1)}, u32[]{:S(2)}, u32[]{:S(2)}) collective-permute-start(bf16[1,4,2,96,384]{4,3,2,1,0:T(8,128)(2,1)} %shard_map.294), channel_id=1, source_target_pairs={{0,8},{1,9},{2,10},{3,11},{4,12},{5,13},{6,14},{7,15},{8,0},{9,1},... | collective-permute-start | bytes 1769480 | tf_op jit(solution)/shard_map/ppermute | solution.py:773
  476.6 12.0 %collective-permute-start.6 = (bf16[3,4,48,384]{3,2,1,0:T(8,128)(2,1)}, bf16[3,4,48,384]{3,2,1,0:T(8,128)(2,1)S(1)}, u32[]{:S(2)}, u32[]{:S(2)}) collective-permute-start(bf16[3,4,48,384]{3,2,1,0:T(8,128)(2,1)} %shard_map.292), channel_id=1, source_target_pairs={{0,1},{1,0},{2,3},{3,2},{4,5},{5,4},{6,7},{7,6},{8,9},{9,8},{10,11... | collective-permute-start | bytes 1327112 | tf_op jit(solution)/shard_map/ppermute | solution.py:773
  483.3 90.5 %collective-permute-start.13 = (bf16[864,384]{1,0:T(8,128)(2,1)}, bf16[864,384]{1,0:T(8,128)(2,1)S(1)}, u32[]{:S(2)}, u32[]{:S(2)}) collective-permute-start(bf16[864,384]{1,0:T(8,128)(2,1)} %get-tuple-element.219), channel_id=1, source_target_pairs={{0,2},{1,3},{2,4},{3,5},{4,6},{5,7},{6,0},{7,1},{8,10},{9,11},{10,... | collective-permute-start | bytes 1990664 | tf_op jit(solution)/shard_map/ppermute | solution.py:773
  484.3 28.8 %copy-start.8 = (bf16[1,4,2,96,384]{4,3,2,1,0:T(8,128)(2,1)}, bf16[1,4,2,96,384]{4,3,2,1,0:T(8,128)(2,1)S(1)}, u32[]{:S(2)}) copy-start(bf16[1,4,2,96,384]{4,3,2,1,0:T(8,128)(2,1)S(1)} %collective-permute-done.8.refs_0_) | copy-start | bytes 1769476
  484.3 90.7 %collective-permute-start.14 = (bf16[864,384]{1,0:T(8,128)(2,1)}, bf16[864,384]{1,0:T(8,128)(2,1)S(1)}, u32[]{:S(2)}, u32[]{:S(2)}) collective-permute-start(bf16[864,384]{1,0:T(8,128)(2,1)} %get-tuple-element.220), channel_id=1, source_target_pairs={{0,4},{1,5},{2,6},{3,7},{4,0},{5,1},{6,2},{7,3},{8,12},{9,13},{10,... | collective-permute-start | bytes 1990664 | tf_op jit(solution)/shard_map/ppermute | solution.py:773
  488.6 0.8 copy-start.2
  492.3 57.3 %collective-permute-start.10 = (bf16[3,48,384]{2,1,0:T(8,128)(2,1)}, bf16[3,48,384]{2,1,0:T(8,128)(2,1)S(1)}, u32[]{:S(2)}, u32[]{:S(2)}) collective-permute-start(bf16[3,48,384]{2,1,0:T(8,128)(2,1)} %get-tuple-element.213), channel_id=1, source_target_pairs={{0,2},{1,3},{2,4},{3,5},{4,6},{5,7},{6,0},{7,1},{8,10},{9,11},{10,... | collective-permute-start | bytes 331784 | tf_op jit(solution)/shard_map/ppermute | solution.py:773
  493.2 56.3 %collective-permute-start.11 = (bf16[3,48,384]{2,1,0:T(8,128)(2,1)}, bf16[3,48,384]{2,1,0:T(8,128)(2,1)S(1)}, u32[]{:S(2)}, u32[]{:S(2)}) collective-permute-start(bf16[3,48,384]{2,1,0:T(8,128)(2,1)} %get-tuple-element.214), channel_id=1, source_target_pairs={{0,4},{1,5},{2,6},{3,7},{4,0},{5,1},{6,2},{7,3},{8,12},{9,13},{10,... | collective-permute-start | bytes 331784 | tf_op jit(solution)/shard_map/ppermute | solution.py:773
  493.2 56.3 %collective-permute-start.12 = (bf16[3,48,384]{2,1,0:T(8,128)(2,1)}, bf16[3,48,384]{2,1,0:T(8,128)(2,1)S(1)}, u32[]{:S(2)}, u32[]{:S(2)}) collective-permute-start(bf16[3,48,384]{2,1,0:T(8,128)(2,1)} %get-tuple-element.215), channel_id=1, source_target_pairs={{0,6},{1,7},{2,0},{3,1},{4,2},{5,3},{6,4},{7,5},{8,14},{9,15},{10,... | collective-permute-start | bytes 331784 | tf_op jit(solution)/shard_map/ppermute | solution.py:773
  549.5 6.7 copy-start.10
  549.6 25.7 %collective-permute-start.15 = (bf16[864,384]{1,0:T(8,128)(2,1)}, bf16[864,384]{1,0:T(8,128)(2,1)}, u32[]{:S(2)}, u32[]{:S(2)}) collective-permute-start(bf16[864,384]{1,0:T(8,128)(2,1)} %get-tuple-element.221), channel_id=1, source_target_pairs={{0,6},{1,7},{2,0},{3,1},{4,2},{5,3},{6,4},{7,5},{8,14},{9,15},{10,... | collective-permute-start | bytes 1990664 | tf_op jit(solution)/shard_map/ppermute | solution.py:773
  549.6 6.7 copy-start.11
  549.6 6.7 copy-start.12
  556.3 52.2 %collective-permute-start.21 = (bf16[3,4,2,96,384]{4,3,2,1,0:T(8,128)(2,1)}, bf16[3,4,2,96,384]{4,3,2,1,0:T(8,128)(2,1)}, u32[]{:S(2)}, u32[]{:S(2)}) collective-permute-start(bf16[3,4,2,96,384]{4,3,2,1,0:T(8,128)(2,1)} %shard_map.303), channel_id=1, source_target_pairs={{0,8},{1,9},{2,10},{3,11},{4,12},{5,13},{6,14},{7,15},{8,0},{9,1},... | collective-permute-start | bytes 5308424 | tf_op jit(solution)/shard_map/ppermute | solution.py:773
  569.1 7.1 collective-permute-start.18
  569.3 6.0 copy-start.9
  573.8 21.2 %copy-start.5 = (bf16[864,384]{1,0:T(8,128)(2,1)}, bf16[864,384]{1,0:T(8,128)(2,1)S(1)}, u32[]{:S(2)}) copy-start(bf16[864,384]{1,0:T(8,128)(2,1)S(1)} %collective-permute-done.13.refs_1_) | copy-start | bytes 1990660
  573.8 30.6 %collective-permute-start.17 = (bf16[2,4,2,48,768]{4,3,2,1,0:T(8,128)(2,1)}, bf16[2,4,2,48,768]{4,3,2,1,0:T(8,128)(2,1)S(1)}, u32[]{:S(2)}, u32[]{:S(2)}) collective-permute-start(bf16[2,4,2,48,768]{4,3,2,1,0:T(8,128)(2,1)} %get-tuple-element.228), channel_id=1, source_target_pairs={{0,16},{1,17},{2,18},{3,19},{4,20},{5,21},{6,22},{7,23},{8,24},{9,... | collective-permute-start | bytes 3538952 | tf_op jit(solution)/shard_map/ppermute | solution.py:773
  575.0 20.0 %copy-start.6 = (bf16[864,384]{1,0:T(8,128)(2,1)}, bf16[864,384]{1,0:T(8,128)(2,1)S(1)}, u32[]{:S(2)}) copy-start(bf16[864,384]{1,0:T(8,128)(2,1)S(1)} %collective-permute-done.14.refs_2_) | copy-start | bytes 1990660
  575.0 33.5 %collective-permute-start.16 = (bf16[4,480,384]{2,1,0:T(8,128)(2,1)}, bf16[4,480,384]{2,1,0:T(8,128)(2,1)S(1)}, u32[]{:S(2)}, u32[]{:S(2)}) collective-permute-start(bf16[4,480,384]{2,1,0:T(8,128)(2,1)} %get-tuple-element.226), channel_id=1, source_target_pairs={{0,1},{1,0},{2,3},{3,2},{4,5},{5,4},{6,7},{7,6},{8,9},{9,8},{10,11... | collective-permute-start | bytes 4423688 | tf_op jit(solution)/shard_map/ppermute | solution.py:773
  575.3 19.7 %collective-permute-start.19 = (bf16[3,48,384]{2,1,0:T(8,128)(2,1)S(1)}, bf16[3,48,384]{2,1,0:T(8,128)(2,1)}, u32[]{:S(2)}, u32[]{:S(2)}) collective-permute-start(bf16[3,48,384]{2,1,0:T(8,128)(2,1)S(1)} %copy-done.9), channel_id=1, source_target_pairs={{0,8},{1,9},{2,10},{3,11},{4,12},{5,13},{6,14},{7,15},{8,0},{9,1},... | collective-permute-start | bytes 331784 | tf_op jit(solution)/shard_map/ppermute | solution.py:773
  576.2 28.2 %collective-permute-start.20 = (bf16[3,48,384]{2,1,0:T(8,128)(2,1)S(1)}, bf16[3,48,384]{2,1,0:T(8,128)(2,1)}, u32[]{:S(2)}, u32[]{:S(2)}) collective-permute-start(bf16[3,48,384]{2,1,0:T(8,128)(2,1)S(1)} %copy-done.9), channel_id=1, source_target_pairs={{0,24},{1,25},{2,26},{3,27},{4,28},{5,29},{6,30},{7,31},{8,16},{9,... | collective-permute-start | bytes 331784 | tf_op jit(solution)/shard_map/ppermute | solution.py:773
  604.4 11.0 %copy-start.4 = (bf16[2,4,2,48,768]{4,3,2,1,0:T(8,128)(2,1)}, bf16[2,4,2,48,768]{4,3,2,1,0:T(8,128)(2,1)S(1)}, u32[]{:S(2)}) copy-start(bf16[2,4,2,48,768]{4,3,2,1,0:T(8,128)(2,1)S(1)} %collective-permute-done.17.refs_2_) | copy-start | bytes 3538948
  608.5 7.0 copy-start.3

commit v9 on v8

--- a/solution.py
+++ b/solution.py
@@ -134,21 +134,20 @@
             yield
 
 
-def attend_back_kernel(at_ref, slot_ref, grad_ref, qk_ref, val_ref, p_ref, out_ref, sums_ref):
+def attend_back_pair(slots, grads, both_of, values_of, soft_of, store):
     low = first_lanes(TREE_LEN)
-    grads = grad_ref[...]
     placed = []
     for head in range(2):
-        table = one_hot_rows(slot_ref[0, 0, head : head + 1, :])
-        slots = jnp.dot(table, grads, preferred_element_type=jnp.float32)
-        slots = jnp.where(low == (head == 0), slots, 0.0).astype(jnp.bfloat16)
-        both, values, soft = qk_ref[0, head], val_ref[0, head], p_ref[0, head]
+        table = one_hot_rows(slots[head : head + 1])
+        found = jnp.dot(table, grads, preferred_element_type=jnp.float32)
+        found = jnp.where(low == (head == 0), found, 0.0).astype(jnp.bfloat16)
+        both, values, soft = both_of(head), values_of(head), soft_of(head)
         grad_soft = jnp.concatenate(
-            [contract_last(g, v) for g, v in zip(cluster_blocks(slots), cluster_blocks(values))],
+            [contract_last(g, v) for g, v in zip(cluster_blocks(found), cluster_blocks(values))],
             axis=0,
         )
         grad_value = jnp.concatenate(
-            [contract_first(p, g) for p, g in zip(cluster_blocks(soft), cluster_blocks(slots))],
+            [contract_first(p, g) for p, g in zip(cluster_blocks(soft), cluster_blocks(found))],
             axis=0,
         ).astype(jnp.bfloat16)
         weights = soft.astype(jnp.float32)
@@ -162,6 +161,8 @@
         mixed = jnp.where(low, by_key, by_query * HEAD_DIM**-0.5).astype(jnp.bfloat16)
         joined = jnp.concatenate([mixed, grad_value], axis=1)
         placed.append(contract_first(table, joined))
+        if head == 0:
+            yield
     first, second = placed
     queries = jnp.where(low, pltpu.roll(first[:, :LANES], HEAD_DIM, 1), second[:, :LANES])
     keys = jnp.where(low, first[:, :LANES], pltpu.roll(second[:, :LANES], HEAD_DIM, 1))
@@ -169,9 +170,40 @@
     sums = []
     for part, grad in enumerate((queries, keys, values)):
         rounded = grad.astype(jnp.bfloat16)
-        out_ref[part] = rounded
+        store(part, rounded)
         sums.append(rows_sum(rounded.astype(jnp.float32)))
-    sums_ref[0, 0] = jnp.concatenate(sums + [jnp.zeros((5, LANES), jnp.float32)], axis=0)
+    store(None, jnp.concatenate(sums + [jnp.zeros((5, LANES), jnp.float32)], axis=0))
+
+
+def attend_back_kernel(slot_ref, grad_ref, qk_ref, val_ref, p_ref, out_ref, sums_ref):
+    def store(part, value):
+        if part is None:
+            sums_ref[0, 0] = value
+        else:
+            out_ref[part] = value
+
+    refs = [lambda head, ref=ref: ref[0, head] for ref in (qk_ref, val_ref, p_ref)]
+    for _ in attend_back_pair(slot_ref[0, 0], grad_ref[...], *refs, store):
+        pass
+
+
+def attend_back_steps(ins, outs):
+    slot_ref, grad_ref, *kept = ins
+    out_ref, sums_ref = outs
+    for tree in range(slot_ref.shape[0]):
+        rows = slice(tree * TREE_LEN, (tree + 1) * TREE_LEN)
+        for pair in range(PAIRS):
+            lanes = slice(pair * LANES, (pair + 1) * LANES)
+
+            def store(part, value):
+                if part is None:
+                    sums_ref[tree, pair] = value
+                else:
+                    out_ref[part, rows, lanes] = value
+
+            refs = [lambda head, ref=ref: ref[tree, 2 * pair + head] for ref in kept]
+            yield from attend_back_pair(slot_ref[tree, pair], grad_ref[rows, lanes], *refs, store)
+            yield
 
 
 def slot_spec(start=0):
@@ -216,45 +248,29 @@
     )(slots, projected, projected, projected, bias)
 
 
-def attend_back(grad_context, slots, kept, at, other):
+def attend_back_shapes(trees):
+    return [
+        jax.ShapeDtypeStruct((3, trees * TREE_LEN, D), jnp.bfloat16),
+        jax.ShapeDtypeStruct((trees, PAIRS, 8, LANES), jnp.float32),
+    ]
+
+
+def attend_back(grad_context, slots, kept):
     trees = slots.shape[0]
-    count = PAIRS // CORES
-    flip = 1 if other else 0
-
-    def pair_of(pair, at):
-        return lax.rem(at[3] + flip, CORES) * count + pair
-
-    head = pl.BlockSpec(
-        (1, 2, TREE_LEN, LANES), lambda tree, pair, at: (tree, pair_of(pair, at), 0, 0)
-    )
     return pl.pallas_call(
         attend_back_kernel,
-        grid_spec=pltpu.PrefetchScalarGridSpec(
-            num_scalar_prefetch=1,
-            grid=(trees, count),
-            in_specs=[
-                pl.BlockSpec(
-                    (1, 1, 2, TREE_LEN), lambda tree, pair, at: (tree, pair_of(pair, at), 0, 0)
-                ),
-                pl.BlockSpec((TREE_LEN, LANES), lambda tree, pair, at: (tree, pair_of(pair, at))),
-                head,
-                head,
-                head,
-            ],
-            out_specs=[
-                pl.BlockSpec((3, TREE_LEN, LANES), lambda tree, pair, at: (0, tree, pair)),
-                pl.BlockSpec((1, 1, 8, LANES), lambda tree, pair, at: (tree, pair, 0, 0)),
-            ],
-        ),
-        out_shape=[
-            jax.ShapeDtypeStruct((3, trees * TREE_LEN, D // CORES), jnp.bfloat16),
-            jax.ShapeDtypeStruct((trees, count, 8, LANES), jnp.float32),
+        grid=(trees, PAIRS),
+        in_specs=[slot_spec(), column_spec(0), head_spec(), head_spec(), head_spec()],
+        out_specs=[
+            pl.BlockSpec((3, TREE_LEN, LANES), lambda tree, pair: (0, tree, pair)),
+            pl.BlockSpec((1, 1, 8, LANES), lambda tree, pair: (tree, pair, 0, 0)),
         ],
+        out_shape=attend_back_shapes(trees),
         compiler_params=kernel_params(),
         cost_estimate=pl.CostEstimate(
-            flops=trees * 17_000_000_000, bytes_accessed=trees * 10_000_000, transcendentals=0
+            flops=trees * 35_000_000_000, bytes_accessed=trees * 20_000_000, transcendentals=0
         ),
-    )(at, slots, grad_context, *kept)
+    )(slots, grad_context, *kept)
 
 
 def erf_parts(values):
@@ -353,21 +369,17 @@
     result_low_ref[...] = result.astype(jnp.bfloat16)
 
 
-def add_projected(grad, at_ref, own_ref, away_ref, weight_ref):
-    half = own_ref.shape[2]
-    for flip, ref in enumerate((own_ref, away_ref)):
-        core = lax.rem(at_ref[3] + flip, CORES)
-        for part in range(3):
-            column = pl.multiple_of((part * CORES + core) * half, 128)
-            grad = grad + contract_last(ref[part], weight_ref[:, pl.ds(column, half)])
+def add_projected(grad, proj_ref, weight_ref):
+    for part in range(3):
+        grad = grad + contract_last(proj_ref[part], weight_ref[:, part * D : (part + 1) * D])
     return grad
 
 
 def feed_back_kernel(layer, with_proj, *refs):
     here = slice(layer, layer + 1)
     if with_proj:
-        above_ref, at_ref, own_ref, away_ref, qkv_weight_ref, *refs = refs
-        grad = add_projected(above_ref[...], at_ref, own_ref, away_ref, qkv_weight_ref)
+        above_ref, proj_ref, qkv_weight_ref, *refs = refs
+        grad = add_projected(above_ref[...], proj_ref, qkv_weight_ref)
     else:
         above_ref, *refs = refs
         grad = above_ref[...].astype(jnp.float32)
@@ -423,8 +435,8 @@
     context_ref[...] = contract_last(low, out_weight_ref[...]).astype(jnp.bfloat16)
 
 
-def input_grad_kernel(above_ref, at_ref, own_ref, away_ref, weight_ref, out_ref):
-    out_ref[...] = add_projected(above_ref[...], at_ref, own_ref, away_ref, weight_ref)
+def input_grad_kernel(above_ref, proj_ref, weight_ref, out_ref):
+    out_ref[...] = add_projected(above_ref[...], proj_ref, weight_ref)
 
 
 def prep_pair(parent_ref, segment_ref, cluster_ref, slot_ref, bias_ref, row, tree, pair):
@@ -485,7 +497,7 @@
 
 
 def part_spec(rows=ROW_TILE):
-    return pl.BlockSpec((3, rows, D // CORES), lambda i: (0, i, 0))
+    return pl.BlockSpec((3, rows, D), lambda i: (0, i, 0))
 
 
 def cost(flops, *arrays):
@@ -547,19 +559,14 @@
     )(context, rows, *weights, *vectors)
 
 
-def feed_back(layer, above, proj, qkv_weight, at, saved, weights, gains):
+def feed_back(layer, above, proj, qkv_weight, saved, weights, gains):
     count = above.shape[0]
     width = weights[1].shape[1]
     f32 = jnp.float32
     lead, lead_specs = [above], [row_spec(D)]
     if proj is not None:
-        lead += [at, *proj, qkv_weight]
-        lead_specs += [
-            pl.BlockSpec(memory_space=pltpu.SMEM),
-            part_spec(),
-            part_spec(),
-            whole_spec(qkv_weight.shape),
-        ]
+        lead += [proj, qkv_weight]
+        lead_specs += [part_spec(), whole_spec(qkv_weight.shape)]
     return pl.pallas_call(
         functools.partial(feed_back_kernel, layer, proj is not None),
         grid=(count // ROW_TILE,),
@@ -590,15 +597,13 @@
     )(*lead, *saved, *weights, *gains)
 
 
-def input_grad(above, proj, qkv_weight, at):
+def input_grad(above, proj, qkv_weight):
     count = above.shape[0]
     return pl.pallas_call(
         input_grad_kernel,
         grid=(count // ROW_TILE,),
         in_specs=[
             row_spec(D),
-            pl.BlockSpec(memory_space=pltpu.SMEM),
-            part_spec(),
             part_spec(),
             whole_spec(qkv_weight.shape),
         ],
@@ -606,7 +611,7 @@
         out_shape=shape_of(count, D, jnp.float32),
         compiler_params=kernel_params(),
         cost_estimate=cost(2.4 * count * D * 3 * D, above, qkv_weight),
-    )(above, at, *proj, qkv_weight)
+    )(above, proj, qkv_weight)
 
 
 def prepare(segment, parent, clusters):
@@ -653,25 +658,25 @@
 
 
 class Grad:
-    def __init__(self, number, left, own, away, cut, tiles, half):
+    def __init__(self, number, left, right, tiles, half):
         self.number = number
-        self.left, self.rights = left, (own, away)
-        self.cut, self.tiles, self.half = cut, tiles, half
+        self.left, self.right = left, right
+        self.tiles, self.half = tiles, half
         self.depth = left.shape[1]
         self.parts = 1 if self.depth > D else tiles
         self.rows = self.depth // (CHIPS_Z * CHIPS_X)
 
     def product(self, at, other, split_y=None, near=None, start=0, total=0, before=()):
         flip = 1 if other else 0
-        left, right = self.left, self.rights[flip]
+        left, right = self.left, self.right
         count = left.shape[0]
         tall = self.depth > D
         core = lambda at: lax.rem(at[3] + flip, CORES)
         in_specs = [
             pl.BlockSpec((count, D), (lambda i, at: (0, i)) if tall else (lambda i, at: (0, 0)))
         ]
-        if not self.cut:
-            in_specs.append(pl.BlockSpec((1, count, self.half), lambda i, at: (i, 0, 0)))
+        if right.ndim == 3:
+            in_specs.append(pl.BlockSpec((1, count, self.half), lambda i, at: (i, 0, core(at))))
         elif tall:
             in_specs.append(pl.BlockSpec((count, self.half), lambda i, at: (0, core(at))))
         else:
@@ -720,37 +725,6 @@
         )(at, *args)
 
 
-def combine_kernel(groups, at_ref, *refs):
-    total = sum(groups)
-    ins, outs = refs[:total], refs[total:]
-    first = 0
-    for count, out_ref in zip(groups, outs):
-        value = None
-        for ref in ins[first : first + count]:
-            term = ref[...].astype(jnp.float32).reshape(out_ref.shape)
-            value = term if value is None else value + term
-        out_ref[...] = value.astype(out_ref.dtype)
-        first += count
-
-
-def combine(at, steps, groups, blocks):
-    terms = [term for group in groups for term in group]
-    return pl.pallas_call(
-        functools.partial(combine_kernel, [len(group) for group in groups]),
-        grid_spec=pltpu.PrefetchScalarGridSpec(
-            num_scalar_prefetch=1,
-            grid=(steps,),
-            in_specs=[pl.BlockSpec(block, index) for _, block, index in terms],
-            out_specs=[pl.BlockSpec(block, index) for _, block, index in blocks],
-        ),
-        out_shape=[jax.ShapeDtypeStruct(shape, jnp.bfloat16) for shape, _, _ in blocks],
-        compiler_params=kernel_params(),
-        cost_estimate=pl.CostEstimate(
-            flops=0, bytes_accessed=2_000_000, transcendentals=0
-        ),
-    )(at, *[array for array, _, _ in terms])
-
-
 class Place:
     def __init__(self):
         rep = lax.axis_index("rep")
@@ -773,34 +747,6 @@
     return lax.ppermute(value, AXES, pairs)
 
 
-class Flow:
-    def __init__(self):
-        self.running, self.done = {}, {}
-
-    def start(self, name, chain):
-        self.running[name] = (chain, next(chain))
-
-    def advance(self, name, arrived):
-        chain, _ = self.running.pop(name)
-        try:
-            self.running[name] = (chain, chain.send(list(arrived)))
-        except StopIteration as end:
-            self.done[name] = end.value
-
-    def tick(self, main, *names):
-        names = [name for name in names if name in self.running]
-        pending = [self.running[name][1] for name in names]
-        main, pending = lax.optimization_barrier((main, pending))
-        for name, arrived in zip(names, pending):
-            self.advance(name, arrived)
-        return main
-
-    def finish(self, name):
-        while name in self.running:
-            self.advance(name, self.running[name][1])
-        return self.done[name]
-
-
 def spread_vectors(found, sizes):
     found = found[:, :, 0, :LAYERS].reshape(-1, LAYERS, found.shape[-1]).transpose(1, 0, 2)
     out, at = [], 0
@@ -810,79 +756,23 @@
     return out
 
 
-def pick_sum(at, own, terms, rows, steps):
-    groups = [[(array, block, index(k)) for array, block, index in terms] for k in range(CHIPS_Z)]
-    return combine(at, steps, groups, [own] * CHIPS_Z)
-
-
-def reduce_y_first(grad, place, stop=None):
+def cut_sums(place, groups):
     at = place.at
-    parts, half = grad.parts, grad.half
-    rows = grad.rows // CHIPS_Y
-    away = grad.product(at, True)
-    (near,) = yield [hop(away, dc=1)]
-    send, keep = grad.product(at, False, True, near)
-    if stop == "sums":
-        return send, keep, False
-    flip = lambda value: 1 - value
-    (over,) = yield [hop(send, dy=1)]
-    if stop == "y":
-        return over, keep, True
-    block = (parts, 1, 1, rows, half)
-    short = (parts, 1, rows, half)
-    index = lambda i, at: (0, i, flip(at[1]), 0, 0)
-    (send,) = combine(
-        at,
-        CHIPS_Z,
-        [[(keep, block, index), (over, block, index)]],
-        [((parts, CHIPS_Z, rows, half), short, lambda i, at: (0, i, 0, 0))],
-    )
-    (across,) = yield [hop(send, dx=1)]
-    turn = lambda at, k: lax.rem(at[0] + k, CHIPS_Z)
-    mine = lambda k: lambda i, at: (0, turn(at, k), at[1], 0, 0)
-    piece = (parts, rows, half)
-    whole = (piece, piece, lambda i, at: (0, 0, 0))
-    own, *sends = pick_sum(
-        at,
-        whole,
-        [
-            (keep, block, mine),
-            (over, block, mine),
-            (across, short, lambda k: lambda i, at: (0, turn(at, k), 0, 0)),
-        ],
-        rows,
-        1,
-    )
-    landed = yield [hop(send, dz=k) for k, send in zip(range(1, CHIPS_Z), sends)]
-    (own,) = combine(at, 1, [[(term, piece, whole[2]) for term in (own, *landed)]], [whole])
-    others = yield [hop(own, dy=1), hop(own, dc=1), hop(own, dy=1, dc=1)]
-    pieces = [item.reshape(parts * rows, half) for item in (own, *others)]
-    return {grad.number: (pieces, 0, rows)}
-
-
-def reduce_x_first(grads, place, stop):
-    at = place.at
-    away = [grad.product(at, True) for grad in grads]
-    near = yield [hop(item, dc=1) for item in away]
-    total = sum(grad.parts * grad.rows for grad in grads)
-    starts, flat = [0], ()
-    for grad, item in zip(grads, near):
-        flat = grad.product(at, False, False, item, starts[-1], total, tuple(flat))
-        starts.append(starts[-1] + grad.parts * grad.rows)
-    send, keep = flat
-    (across,) = yield [hop(send, dx=1)]
-    if stop == "x":
-        return across, keep
-    steps = 3
-    tall = total // steps
-    ahead = lambda k: lambda i, at: (lax.rem(at[0] + k, CHIPS_Z), i, 0)
-    piece = ((total, UNIT), (tall, UNIT), lambda i, at: (i, 0))
-    own, *sends = pick_sum(
-        at, piece, [(item, (1, tall, UNIT), ahead) for item in (keep, across)], tall, steps
-    )
-    landed = yield [hop(send, dz=k) for k, send in zip(range(1, CHIPS_Z), sends)]
-    add = lambda *terms: combine(at, steps, [[(term, *piece[1:]) for term in terms]], [piece])[0]
-    return add(own, *landed)
+    arrived = []
+    for grads, _ in groups:
+        arrived.append([hop(grad.product(at, True), dc=1) for grad in grads])
+    found = []
+    for (grads, y_first), near in zip(groups, arrived):
+        total = sum(grad.parts * grad.rows for grad in grads)
+        start, pair = 0, ()
+        for grad, item in zip(grads, near):
+            if y_first:
+                pair = grad.product(at, False, True, item)
+            else:
+                pair = grad.product(at, False, False, item, start, total, tuple(pair))
+            start += grad.parts * grad.rows
+        found.append(tuple(pair))
+    return found
 
 
 def prep_steps(ins, outs):
@@ -1036,24 +926,22 @@
     return results
 
 
-def pack_sums(out_ref, core, ins):
+def pack_sums(out_ref, ins):
     rows = 8 * LAYERS
     width = out_ref.shape[1]
     for layer in range(LAYERS):
-        sums_ref, ffin_ref, own_ref, away_ref = ins[4 * layer : 4 * layer + 4]
+        sums_ref, ffin_ref, _ = ins[3 * layer : 3 * layer + 3]
         out_ref[8 * layer : 8 * layer + 8] = sums_ref[...]
         for at in range(0, ffin_ref.shape[1], width):
             out_ref[rows : rows + 1] = ffin_ref[:, at : at + width]
             rows += 1
     for layer in range(LAYERS):
-        for flip, ref in enumerate(ins[4 * layer + 2 : 4 * layer + 4]):
-            half = lax.rem(core + flip, CORES) * ref.shape[1]
-            for pair in range(ref.shape[1]):
-                value = ref[0, pair]
-                for tree in range(1, ref.shape[0]):
-                    value = value + ref[tree, pair]
-                column = pl.multiple_of((half + pair) * LANES, LANES)
-                out_ref[rows : rows + 8, pl.ds(column, LANES)] = value
+        ref = ins[3 * layer + 2]
+        for pair in range(ref.shape[1]):
+            value = ref[0, pair]
+            for tree in range(1, ref.shape[0]):
+                value = value + ref[tree, pair]
+            out_ref[rows : rows + 8, pair * LANES : (pair + 1) * LANES] = value
         rows += 8
 
 
@@ -1061,20 +949,26 @@
     return LAYERS * (16 + ffin_width // D)
 
 
-def tail_kernel(arrived, *refs):
+def reduce_kernel(flats, count, vectors, work, work_ins, work_outs, *refs):
     take = iter(refs)
-    count = len(arrived)
-    a_in, a_keep = next(take), next(take)
-    b_ins = [(next(take), next(take)) for _ in range(count)]
-    l_in, vec_ins = next(take), [next(take) for _ in range(4 * LAYERS)]
-    a_own, a_other = next(take), next(take)
-    b_outs = [next(take) for _ in range(count)]
-    l_own, l_other, vec_out = next(take), next(take), next(take)
-    a_zsend, a_zland, a_ysend, a_yland, a_cland = [next(take) for _ in range(5)]
-    b_scratch = [[next(take) for _ in range(6)] for _ in range(count)]
-    l_yland, l_cland = next(take), next(take)
-    v_send, v_land = next(take), next(take)
-    a_sems, b_sems, v_sems = next(take), [next(take) for _ in range(count)], next(take)
+
+    def some(number):
+        return [next(take) for _ in range(number)]
+
+    own_ins = some(work_ins)
+    a_ins = [some(2) for _ in range(flats)]
+    b_ins = [some(2) for _ in range(count)]
+    vec_ins = some(vectors)
+    own_outs = some(work_outs)
+    a_outs = [some(2) for _ in range(flats)]
+    b_outs = some(count)
+    vec_outs = some(1 if vectors else 0)
+    a_scratch = [some(6) for _ in range(flats)]
+    b_scratch = [some(6) for _ in range(count)]
+    v_send, v_land = some(2) if vectors else (None, None)
+    a_sems, b_sems = some(flats), some(count)
+    v_sems = next(take) if vectors else None
+    todo = work(own_ins, own_outs)
     rep, shard = lax.axis_index("rep"), lax.axis_index("shard")
     y, core = lax.div(rep, CORES), lax.rem(rep, CORES)
     z, x = lax.div(shard, CHIPS_X), lax.rem(shard, CHIPS_X)
@@ -1113,89 +1007,88 @@
 
     order = (2, 1, 3, 0)
     ahead = [lax.rem(z + k, CHIPS_Z) for k in order]
-    pack_sums(v_send.at[0], core, vec_ins)
-    v_copies = [send(v_send.at[0], v_land.at[0], v_sems, 0, dc=1)]
-    a_across = a_in
-    b_y = [[] for _ in range(count)]
+    v_copies = []
+    if vectors:
+        pack_sums(v_send.at[0], vec_ins)
+        v_copies.append(send(v_send.at[0], v_land.at[0], v_sems, 0, dc=1))
+    a_x, b_y = [[] for _ in range(flats)], [[] for _ in range(count)]
     for j, to in enumerate(ahead):
-        for i, (b_send, _) in enumerate(b_ins):
-            if arrived[i]:
-                continue
-            b_y[i].append(send(b_send.at[:, to], b_scratch[i][0].at[j], b_sems[i], j, dy=1))
+        for i, (first, _) in enumerate(a_ins):
+            a_x[i].append(send(first.at[to], a_scratch[i][0].at[j], a_sems[i], j, dx=1))
+        for i, (first, _) in enumerate(b_ins):
+            b_y[i].append(send(first.at[:, to], b_scratch[i][0].at[j], b_sems[i], j, dy=1))
     steps = (dict(dc=1), dict(dy=1), dict(dx=1), dict(dz=2), dict(dz=flip_z))
 
     def add_vectors(s):
+        if not vectors:
+            return
         v_copies[s].wait_recv()
         total = v_send[s] + v_land[s]
         if s + 1 == len(steps):
-            vec_out[...] = total
+            vec_outs[0][...] = total
         else:
             v_send[s + 1] = total
             v_copies.append(
                 send(v_send.at[s + 1], v_land.at[s + 1], v_sems, s + 1, **steps[s + 1])
             )
 
-    def over(i, j, side):
-        if arrived[i]:
-            return wide(b_ins[i][0][:, ahead[j], side])
-        return wide(b_scratch[i][0][j, :, side])
-
-    a_z, b_x, b_z = [], [[] for _ in range(count)], [[] for _ in range(count)]
+    a_z, b_x, b_z = ([[] for _ in range(number)] for number in (flats, count, count))
 
     def b_along_z(i, j):
         k, keep = order[j], b_ins[i][1]
-        _, _, x_land, z_send, z_land, _ = b_scratch[i]
+        over, _, x_land, z_send, z_land, _ = b_scratch[i]
         b_x[i][j].wait_recv()
         if k:
-            total = wide(keep[:, ahead[j], x]) + over(i, j, x) + wide(x_land[j])
+            total = wide(keep[:, ahead[j], x]) + wide(over[j, :, x]) + wide(x_land[j])
             z_send[k - 1] = total.astype(jnp.bfloat16)
             b_z[i].append(send(z_send.at[k - 1], z_land.at[k - 1], b_sems[i], 7 + k, dz=k))
 
     def b_along_x(i, j):
-        keep, (_, x_send, x_land, *_) = b_ins[i][1], b_scratch[i]
-        if not arrived[i]:
-            b_y[i][j].wait_recv()
-        total = wide(keep[:, ahead[j], 1 - x]) + over(i, j, 1 - x)
+        keep, (over, x_send, x_land, *_) = b_ins[i][1], b_scratch[i]
+        b_y[i][j].wait_recv()
+        total = wide(keep[:, ahead[j], 1 - x]) + wide(over[j, :, 1 - x])
         x_send[j] = total.astype(jnp.bfloat16)
         b_x[i].append(send(x_send.at[j], x_land.at[j], b_sems[i], 4 + j, dx=1))
 
     for j, k in enumerate(order):
-        if k:
-            total = wide(a_keep[ahead[j]]) + wide(a_across[ahead[j]])
-            a_zsend[k - 1] = total.astype(jnp.bfloat16)
-            a_z.append(send(a_zsend.at[k - 1], a_zland.at[k - 1], a_sems, 3 + k, dz=k))
+        next(todo, None)
+        for i, (_, keep) in enumerate(a_ins):
+            across, z_send, z_land, *_ = a_scratch[i]
+            a_x[i][j].wait_recv()
+            if k:
+                total = wide(keep[ahead[j]]) + wide(across[j])
+                z_send[k - 1] = total.astype(jnp.bfloat16)
+                a_z[i].append(
+                    send(z_send.at[k - 1], z_land.at[k - 1], a_sems[i], 3 + k, dz=k)
+                )
+        next(todo, None)
         for i in range(count):
-            if arrived[i]:
-                b_along_x(i, j)
-    l_y = send(l_in, l_yland, a_sems, 0, dy=1)
-    add_vectors(0)
-    for j in range(CHIPS_Z):
-        for i in range(count):
-            if not arrived[i]:
-                b_along_x(i, j)
-        for i in range(count):
-            if arrived[i]:
-                b_along_z(i, j)
-        add_vectors(j + 1)
-    for j in range(CHIPS_Z):
-        for i in range(count):
-            if not arrived[i]:
-                b_along_z(i, j)
-    l_y.wait_recv()
-    l_own[...] = (wide(l_in[...]) + wide(l_yland[...])).astype(jnp.bfloat16)
-    ends = [send(l_own, l_cland, a_sems, 1, dc=1)]
-    for copy in a_z:
-        copy.wait_recv()
-    total = wide(a_keep[z]) + wide(a_across[z])
-    for k in range(CHIPS_Z - 1):
-        total = total + wide(a_zland[k])
-    a_ysend[...] = total.astype(jnp.bfloat16)
-    a_y = send(a_ysend, a_yland, a_sems, 7, dy=1)
+            b_along_x(i, j)
+        if j:
+            for i in range(count):
+                b_along_z(i, j - 1)
+        next(todo, None)
+        add_vectors(j)
+    for i in range(count):
+        b_along_z(i, CHIPS_Z - 1)
+    add_vectors(4)
+    for _ in todo:
+        pass
+    over_y, ends = [], []
+    for i, (_, keep) in enumerate(a_ins):
+        across, _, z_land, y_send, y_land, _ = a_scratch[i]
+        for copy in a_z[i]:
+            copy.wait_recv()
+        total = wide(keep[z]) + wide(across[CHIPS_Z - 1])
+        for k in range(CHIPS_Z - 1):
+            total = total + wide(z_land[k])
+        y_send[...] = total.astype(jnp.bfloat16)
+        over_y.append(send(y_send, y_land, a_sems[i], 7, dy=1))
     for i, (_, keep) in enumerate(b_ins):
-        _, _, x_land, _, z_land, end_land = b_scratch[i]
+        over, _, x_land, _, z_land, end_land = b_scratch[i]
         for copy in b_z[i]:
             copy.wait_recv()
-        total = wide(keep[:, z, x]) + over(i, 3, x) + wide(x_land[3])
+        total = wide(keep[:, z, x]) + wide(over[3, :, x]) + wide(x_land[3])
         for k in range(CHIPS_Z - 1):
             total = total + wide(z_land[k])
         b_outs[i][0] = total.astype(jnp.bfloat16)
@@ -1203,65 +1096,77 @@
             ends.append(
                 send(b_outs[i].at[0], end_land.at[number], b_sems[i], 11 + number, **step)
             )
-    a_y.wait_recv()
-    a_own[...] = (wide(a_ysend[...]) + wide(a_yland[...])).astype(jnp.bfloat16)
-    ends.append(send(a_own, a_cland, a_sems, 8, dc=1))
+    for i, (own, _) in enumerate(a_outs):
+        *_, y_send, y_land, c_land = a_scratch[i]
+        over_y[i].wait_recv()
+        own[...] = (wide(y_send[...]) + wide(y_land[...])).astype(jnp.bfloat16)
+        ends.append(send(own, c_land, a_sems[i], 8, dc=1))
     for copy in ends:
         copy.wait_recv()
     for i in range(count):
         b_outs[i][1:4] = b_scratch[i][5][...]
-    a_other[...] = a_cland[...]
-    l_other[...] = l_cland[...]
+    for i, (_, other) in enumerate(a_outs):
+        other[...] = a_scratch[i][5][...]
     for copy in sent:
         copy.wait_send()
 
 
-def reduce_tail(flat, pairs, last, sums):
+def no_work(ins, outs):
+    return iter(())
+
+
+def reduce_sums(flats, pairs, sums, number, work=no_work, work_args=(), work_shapes=()):
     low = jnp.bfloat16
-    _, total, unit = flat[0].shape
     whole = pl.BlockSpec(memory_space=pltpu.VMEM)
     far = pl.BlockSpec(memory_space=pl.ANY)
-    piece = (total, unit)
-    outs = [piece, piece]
-    scratch = [(CHIPS_Z - 1, *piece), (CHIPS_Z - 1, *piece), piece, piece, piece]
-    args, specs, arrived = [*flat], [whole, whole], []
-    for first, keep, here in pairs:
+    args, specs = list(work_args), [whole] * len(work_args)
+    outs, scratch = [], []
+    for first, keep in flats:
+        piece = keep.shape[1:]
+        args += [first, keep]
+        specs += [far, whole]
+        outs += [piece, piece]
+        scratch += [(CHIPS_Z, *piece), (CHIPS_Z - 1, *piece), (CHIPS_Z - 1, *piece)]
+        scratch += [piece] * 3
+    for first, keep in pairs:
         parts, _, _, rows, half = keep.shape
         block = (parts, rows, half)
         args += [first, keep]
-        specs += [whole if here else far, whole]
-        arrived.append(here)
+        specs += [far, whole]
         outs.append((CORES * CHIPS_Y, *block))
         scratch += [
-            (16, 128) if here else (CHIPS_Z, parts, CHIPS_X, rows, half),
+            (CHIPS_Z, parts, CHIPS_X, rows, half),
             (CHIPS_Z, *block),
             (CHIPS_Z, *block),
             (CHIPS_Z - 1, *block),
             (CHIPS_Z - 1, *block),
             (CORES * CHIPS_Y - 1, *block),
         ]
-    outs += [last.shape, last.shape]
-    scratch += [last.shape, last.shape]
-    shapes = [jax.ShapeDtypeStruct(shape, low) for shape in outs]
-    vec = (sum_rows(sums[1].shape[1]), D)
-    shapes.append(jax.ShapeDtypeStruct(vec, jnp.float32))
+    args += sums
+    specs += [whole] * len(sums)
+    shapes = list(work_shapes) + [jax.ShapeDtypeStruct(shape, low) for shape in outs]
     scratch = [pltpu.VMEM(shape, low) for shape in scratch]
-    scratch += [pltpu.VMEM((5, *vec), jnp.float32)] * 2
-    scratch += [pltpu.SemaphoreType.DMA((2, 9))]
+    if sums:
+        vec = (sum_rows(sums[1].shape[1]), D)
+        shapes.append(jax.ShapeDtypeStruct(vec, jnp.float32))
+        scratch += [pltpu.VMEM((5, *vec), jnp.float32)] * 2
+    scratch += [pltpu.SemaphoreType.DMA((2, 9))] * len(flats)
     scratch += [pltpu.SemaphoreType.DMA((2, 14))] * len(pairs)
-    scratch += [pltpu.SemaphoreType.DMA((2, 5))]
-    own, other, *rest = pl.pallas_call(
-        functools.partial(tail_kernel, arrived),
-        in_specs=[*specs, whole] + [whole] * len(sums),
+    if sums:
+        scratch.append(pltpu.SemaphoreType.DMA((2, 5)))
+    return pl.pallas_call(
+        functools.partial(
+            reduce_kernel, len(flats), len(pairs), len(sums), work, len(work_args), len(work_shapes)
+        ),
+        in_specs=specs,
         out_specs=[whole] * len(shapes),
         out_shape=shapes,
         scratch_shapes=scratch,
         compiler_params=pltpu.CompilerParams(
-            vmem_limit_bytes=KERNEL_VMEM, collective_id=0, has_side_effects=True
+            vmem_limit_bytes=KERNEL_VMEM, collective_id=number, has_side_effects=True
         ),
         cost_estimate=pl.CostEstimate(flops=0, bytes_accessed=200_000_000, transcendentals=0),
-    )(*args, last, *sums)
-    return [own, other], rest[:-3], list(rest[-3:-1]), rest[-1]
+    )(*args)
 
 
 def join_kernel(plan, count, at_ref, *refs):
@@ -1317,7 +1222,7 @@
     clusters,
     *weights,
 ):
-    flow = Flow()
+    pieces = {}
     if fast:
         place = Place()
         at = place.at
@@ -1346,8 +1251,9 @@
         whole = {(0, 0): qkv}
 
         def attend_layer(layer, projected):
-            wanted = [(6, layer, True), (8, layer, True), (2, layer, True)]
-            if layer + 1 < LAYERS:
+            last = layer + 1 == LAYERS
+            wanted = [(6, layer, True), (8, layer, not last), (2, layer, last)]
+            if not last:
                 wanted.insert(2, (0, layer + 1, False))
             results = gather(
                 shards, wanted, attend_steps, (projected, slots, bias), attend_shapes(trees), 2 + layer
@@ -1359,22 +1265,24 @@
         def get(layer, number):
             return whole[layer, number]
 
-        def reduce(layer, *grads):
-            name = ("grad", layer, grads[0].number)
-            if name[2] == 0:
-                chain = reduce_y_first(*grads, place, None if layer else "sums")
-            elif name[2] == 6:
-                chain = reduce_y_first(*grads, place, "y")
-            else:
-                chain = reduce_x_first(grads, place, "z" if layer else "x")
-            flow.start(name, chain)
-
-        def back_step(main, *held):
-            return flow.tick(main, *[name for name in flow.running if name not in held])
+        def attend_back_layer(layer, grad_context, heads, groups, waiting):
+            flat, pair = cut_sums(place, groups)
+            proj, head_sums, *ends = reduce_sums(
+                [flat],
+                [pair, *waiting],
+                [],
+                2 + LAYERS + layer,
+                attend_back_steps,
+                (slots, grad_context, *heads),
+                attend_back_shapes(trees),
+            )
+            pieces[layer, "flat"] = ends[:2]
+            pieces[layer, 6] = ends[2]
+            if waiting:
+                pieces[layer + 1, 0] = ends[3]
+            return proj, head_sums
 
     else:
-        at = jnp.zeros((4,), jnp.int32)
-
         slots, bias = prepare(segment, parent, clusters)
         vectors = [
             lax.all_gather(weights[number], "shard", axis=1, tiled=True).astype(jnp.float32)
@@ -1387,19 +1295,18 @@
         def get(layer, number):
             return lax.all_gather(weights[number][layer], "shard", axis=0, tiled=True)
 
-        def reduce(layer, *grads):
-            for grad in grads:
-                own, away = grad.rights
-                if not grad.cut:
-                    own = jnp.concatenate([own, away], axis=2)
-                    own = own.transpose(1, 0, 2).reshape(own.shape[1], -1)
-                total = contract_first(grad.left, own)
-                total = lax.psum_scatter(total, "shard", scatter_dimension=0, tiled=True)
-                total = lax.psum(total.astype(jnp.bfloat16), "rep").astype(jnp.float32)
-                flow.done[("grad", layer, grad.number)] = total
-
-        def back_step(main, *held):
-            return main
+        def own_sum(left, right):
+            if right.ndim == 3:
+                right = right.transpose(1, 0, 2).reshape(right.shape[1], -1)
+            total = contract_first(left, right)
+            total = lax.psum_scatter(total, "shard", scatter_dimension=0, tiled=True)
+            return lax.psum(total.astype(jnp.bfloat16), "rep").astype(jnp.float32)
+
+        def attend_back_layer(layer, grad_context, heads, groups, waiting):
+            for grads, _ in groups:
+                for grad in grads:
+                    pieces[layer, grad.number] = own_sum(grad.left, grad.right)
+            return attend_back(grad_context, slots, heads)
 
     vector = dict(zip(VECTORS, vectors))
     hidden, hidden_low = inputs, inputs
@@ -1419,7 +1326,7 @@
         saved.append((entered, heads, context, middle, act, slope, norms))
     result = hidden_low
     above, proj = cotangent, None
-    sums = [None] * LAYERS
+    sums, waiting = [None] * LAYERS, []
     for layer in reversed(range(LAYERS)):
         entered, heads, context, middle, act, slope, norms = saved[layer]
         pull = functools.partial(get, layer)
@@ -1428,50 +1335,41 @@
             above,
             proj,
             None if proj is None else get(layer + 1, 0),
-            at,
             [norms[2], norms[3], slope, norms[0], norms[1]],
             [pull(2), pull(6), pull(8)],
             [vector[4], vector[10]],
         )
-        sums[layer] = [row_sums, ffin_sum]
-        down = back_step(down)
         wide = grad_pre.shape[1] // CORES
-        grad_8 = Grad(8, act, down, down, True, act.shape[1] // D, UNIT)
-        grad_2 = Grad(2, context, attn_low, attn_low, True, 1, UNIT)
-        if layer == 0:
-            reduce(layer, grad_8, grad_2)
-            reduce(layer, Grad(6, middle, grad_pre, grad_pre, True, wide // D, D))
-        else:
-            grad_6 = Grad(6, middle, grad_pre, grad_pre, True, wide // UNIT, UNIT)
-            reduce(layer, grad_8, grad_6, grad_2)
-        above_chain = () if layer else (("grad", 1, 8),)
-        grad_context = back_step(grad_context, *above_chain)
-        away, away_sums = attend_back(grad_context, slots, heads, at, True)
-        wide_chains = (("grad", layer, 8), ("grad", layer, 6))
-        grad_context, away = back_step((grad_context, away), *above_chain, *wide_chains)
-        own, own_sums = attend_back(grad_context, slots, heads, at, False)
-        proj = (own, away)
-        reduce(layer, Grad(0, entered, own, away, False, 3, UNIT))
-        sums[layer] += [own_sums, away_sums]
-        proj = back_step(proj, *(wide_chains if layer else ()))
+        groups = (
+            (
+                (
+                    Grad(8, act, down, act.shape[1] // D, UNIT),
+                    Grad(2, context, attn_low, 1, UNIT),
+                ),
+                False,
+            ),
+            ((Grad(6, middle, grad_pre, wide // D, D),), True),
+        )
+        proj, head_sums = attend_back_layer(layer, grad_context, heads, groups, waiting)
+        sums[layer] = [row_sums, ffin_sum, head_sums]
         above = grad_attn
-    grad_input = input_grad(above, proj, get(0, 0), at)
+        last = Grad(0, entered, proj, 3, UNIT)
+        if not fast:
+            pieces[layer, 0] = own_sum(last.left, last.right)
+        elif layer:
+            waiting = cut_sums(place, [((last,), True)])
+    grad_input = input_grad(above, proj, get(0, 0))
     sums = [item for layer in sums for item in layer]
     if fast:
-        while flow.running:
-            grad_input = back_step(grad_input)
-        done = flow.done
-        last, grad_input = lax.optimization_barrier((done["grad", 1, 8], grad_input))
-        flat, ends, last, total = reduce_tail(
-            done["grad", 0, 8], [done["grad", 0, 6], done["grad", 0, 0]], last, sums
-        )
+        (pair,) = cut_sums(place, [((last,), True)])
+        pair, grad_input = lax.optimization_barrier((pair, grad_input))
+        pieces[0, 0], total = reduce_sums([], [pair], sums, 0)
     else:
         norms, wide, heads = [], [], []
-        for row_sums, ffin_sum, own_sums, away_sums in (sums[:4], sums[4:]):
+        for row_sums, ffin_sum, head_sums in (sums[:3], sums[3:]):
             norms.append(row_sums)
             wide.append(ffin_sum.reshape(-1, D))
-            found = jnp.concatenate([own_sums.sum(0), away_sums.sum(0)])
-            heads.append(found.transpose(1, 0, 2).reshape(8, D))
+            heads.append(head_sums.sum(0).transpose(1, 0, 2).reshape(8, D))
         total = lax.psum(jnp.concatenate(norms + wide + heads), AXES)
     count = lax.axis_size("shard")
     shard = lax.axis_index("shard")
@@ -1493,21 +1391,22 @@
     if fast:
         rows = {number: weights[number].shape[1] for number in MATRICES}
         parts = {number: weights[number].shape[2] // (CORES * UNIT) for number in MATRICES}
-        known = [{}, dict(done["grad", 1, 0])]
-        for layer, pieces, numbers in ((0, flat, (8, 2)), (1, last, (8, 6, 2))):
+        known = [{} for _ in range(LAYERS)]
+        for layer in range(LAYERS):
             start = 0
-            for number in numbers:
-                known[layer][number] = (pieces, start, rows[number])
+            for number in (8, 2):
+                known[layer][number] = (pieces[layer, "flat"], start, rows[number])
                 start += rows[number] * parts[number]
-        for number, end in zip((6, 0), ends):
-            end = end.reshape(end.shape[0], -1, end.shape[-1])
-            known[0][number] = (list(end), 0, rows[number] // CHIPS_Y)
+            for number in (6, 0):
+                end = pieces[layer, number]
+                end = end.reshape(end.shape[0], -1, end.shape[-1])
+                known[layer][number] = (list(end), 0, rows[number] // CHIPS_Y)
         for numbers in (MATRICES,):
             shapes = {number: weights[number].shape[1:] for number in numbers}
-            grads.update(zip(numbers, join(at, known, shapes)))
+            grads.update(zip(numbers, join(place.at, known, shapes)))
     else:
         for number in MATRICES:
-            grads[number] = jnp.stack([flow.done[("grad", layer, number)] for layer in range(LAYERS)])
+            grads[number] = jnp.stack([pieces[layer, number] for layer in range(LAYERS)])
     return (result, grad_input, *[grads[number] for number in range(12)])
 
 

time: 741 us -> 735 us (level)
  waiting for transfers between devices: 49.4 us -> 0.02 us
  Pallas kernels: 645 us -> 685 us
  starting transfers between devices: 12.7 us -> 2.25 us
  other arithmetic: 4.17 us -> 13.4 us
    pallas_call x10 -> x3, Pallas kernels: 178 us -> 233 us  [reduce_sums(): pl.pallas_call(functools.partial(reduce_kernel, len(flats), len(pairs), l...]
    ppermute x22 -> x8, waiting for transfers between devices: 49.4 us -> 0.02 us  [hop(): return lax.ppermute(value, AXES, pairs)]
    ppermute x22 -> x8, starting transfers between devices: 12.7 us -> 2.25 us  [hop(): return lax.ppermute(value, AXES, pairs)]
    convert_element_type x2, other arithmetic: 0.24 us -> 9.48 us  [spread_vectors(): found[:, :, at:at + size].reshape(LAYERS, -1).astype(jnp.float32)]
    pallas_call x3, Pallas kernels: 220 us -> 211 us  [gather(): pl.pallas_call(functools.partial(gather_kernel, plan, work, len(work_args...]
  transfers between devices with their start and end apart: 22 -> 8, of which waited for: 5 -> 0; matrix products, arithmetic and copies ran while one was open for 0% -> 0% of each run, Pallas kernels for 26% -> 15%
where the time goes in v9:
time: 735 us; the launch traced here: 725 us
  Pallas kernels  685 us (93%)
  local copies, waits for them, and re-layouts  22.7 us (3%)
  other arithmetic  13.4 us (2%)
    pallas_call x3, Pallas kernels, reduce_sums(): pl.pallas_call(functools.partial(reduce_kernel, len(flats), len(pairs), l...  233 us
    pallas_call x3, Pallas kernels, gather(): pl.pallas_call(functools.partial(gather_kernel, plan, work, len(work_args...  211 us
    pallas_call x16, Pallas kernels, product(): pl.pallas_call(functools.partial(weight_grad_kernel, split_y), grid_spec=...  104 us
    pallas_call x2, Pallas kernels, feed(): pl.pallas_call(functools.partial(feed_kernel, layer), grid=(count // ROW_...  56.3 us
    pallas_call x2, Pallas kernels, feed_back(): pl.pallas_call(functools.partial(feed_back_kernel, layer, proj is not Non...  50.8 us
    pallas_call x2, Pallas kernels, project(): pl.pallas_call(functools.partial(project_kernel, layer), grid=(count // R...  16 us
  transfers between devices with their start and end apart: 8, of which 0 were waited for; matrix products, arithmetic and copies ran while one was open for 0% of the time, Pallas kernels for 15%

profile of v9, /device:TPU:17, one launch (start us, length us, event | category | flops | bytes accessed | tf_op | source)
XLA Modules:
  0.0 724.7 jit_solution(17378216438933305231)
XLA Ops:
  0.6 1.5 transpose_reshape.3.refs_2_
  2.1 0.9 concatenate.3
  3.0 0.6 pad.4.refs_3_
  3.6 40.2 %shard_map.272 = (s32[1,6,2,1024]{3,2,1,0:T(2,128)}, bf16[1,12,1024,128]{3,2,1,0:T(8,128)(2,1)}, bf16[4,2,1,16,1152]{4,3,2,1,0:T(8,128)(2,1)}, bf16[4,2,2,48,2304]{4,3,2,1,0:T(8,128)(2,1)}) custom-call(s32[1,13]{1,0:T(1,128)} %refs_0_.2, s32[1,1,1024]{2,1,0:T(1,128)} %bitcast.78, s32[1,6,2,1024]{3,2,1,0:T(2,128)} %transpose_reshape.3.refs_2_, ...), custom_call_target="tpu_custom_call" | custom-call | bytes 200000000 | tf_op jit(solution)/shard_map/pallas_call | solution.py:910
  43.8 0.9 slice.91
  44.8 9.5 %slice_convert_fusion.1 = (f32[2,8,96]{2,1,0:T(8,128)S(1)}, f32[2,8,96]{2,1,0:T(8,128)S(1)}, f32[2,8,96]{2,1,0:T(8,128)S(1)}, f32[2,8,96]{2,1,0:T(8,128)S(1)}, f...) fusion(bf16[2,8,1152]{2,1,0:T(8,128)(2,1)S(1)} %bitcast.67), kind=kLoop, calls=%fused_computation.21 | loop fusion | flops 9216 | bytes 55296 | tf_op jit(solution)/shard_map/convert_element_type | solution.py:754
  54.3 0.7 reshape.124.bias_ref
  55.0 0.7 reshape.126.attn_gain_ref.refs_9_.refs_11_
  55.7 0.7 reshape.130.ffn_gain_ref.refs_10_.refs_12_
  56.3 0.7 reshape.125.out_bias_ref
  57.0 0.7 reshape.127.attn_shift_ref
  57.7 0.7 reshape.129.ffout_bias_ref
  58.4 0.7 reshape.131.ffn_shift_ref
  59.0 0.6 copy.36
  59.7 7.8 %shard_map.273.refs_0_ = bf16[1024,2304]{1,0:T(8,128)(2,1)} custom-call(bf16[1024,768]{1,0:T(8,128)(2,1)} %left_ref.3, bf16[768,2304]{1,0:T(8,128)(2,1)} %bitcast.87, f32[2,1536]{1,0:T(2,128)} %reshape.124.bias_ref), custom_call_target="tpu_custom_call" | custom-call | flops 4348654592 | bytes 5111808 | tf_op jit(solution)/shard_map/pallas_call | solution.py:514
  67.4 88.0 %shard_map.274 = (bf16[1024,768]{1,0:T(8,128)(2,1)}, bf16[1,12,1024,128]{3,2,1,0:T(8,128)(2,1)}, bf16[1,12,1024,128]{3,2,1,0:T(8,128)(2,1)}, bf16[1,12,1024,128]...) custom-call(bf16[1024,2304]{1,0:T(8,128)(2,1)} %shard_map.273.refs_0, ...), custom_call_target="tpu_custom_call" | custom-call | bytes 200000000 | tf_op jit(solution)/shard_map/pallas_call | solution.py:910
  155.4 27.9 %shard_map.275 = (bf16[1024,768]{1,0:T(8,128)(2,1)}, bf16[1024,3072]{1,0:T(8,128)(2,1)}, bf16[1024,3072]{1,0:T(8,128)(2,1)}, f32[1024,768]{1,0:T(8,128)}, f32[10...) custom-call(bf16[1024,768]{1,0:T(8,128)(2,1)} %get-tuple-element.104, ...), custom_call_target="tpu_custom_call" | custom-call | flops 27179089920 | bytes 12189696 | tf_op jit(solution)/shard_map/pallas_call | solution.py:529
  183.3 8.2 %shard_map.276.refs_0_ = bf16[1024,2304]{1,0:T(8,128)(2,1)} custom-call(bf16[1024,768]{1,0:T(8,128)(2,1)} %get-tuple-element.108.rows_ref.left_ref, bf16[768,2304]{1,0:T(8,128)(2,1)} %bitcast.89, f32[2,1536]{1,0:T(2,128)} %reshape.124.bias_ref), custom_call_target="tpu_custom_call" | custom-call | flops 4348654592 | bytes 5111808 | tf_op jit(solution)/shard_map/pallas_call | solution.py:514
  191.6 82.4 %shard_map.277 = (bf16[1024,768]{1,0:T(8,128)(2,1)}, bf16[1,12,1024,128]{3,2,1,0:T(8,128)(2,1)}, bf16[1,12,1024,128]{3,2,1,0:T(8,128)(2,1)}, bf16[1,12,1024,128]...) custom-call(bf16[1024,2304]{1,0:T(8,128)(2,1)} %shard_map.276.refs_0, ...), custom_call_target="tpu_custom_call" | custom-call | bytes 200000000 | tf_op jit(solution)/shard_map/pallas_call | solution.py:910
  274.0 0.6 pad_add_fusion.at_ref
  274.6 28.4 %shard_map.278 = (bf16[1024,768]{1,0:T(8,128)(2,1)}, bf16[1024,3072]{1,0:T(8,128)(2,1)}, bf16[1024,3072]{1,0:T(8,128)(2,1)}, f32[1024,768]{1,0:T(8,128)}, f32[10...) custom-call(bf16[1024,768]{1,0:T(8,128)(2,1)} %get-tuple-element.110, ...), custom_call_target="tpu_custom_call" | custom-call | flops 27179089920 | bytes 12189696 | tf_op jit(solution)/shard_map/pallas_call | solution.py:529
  302.9 21.7 %shard_map.279 = (bf16[1024,768]{1,0:T(8,128)(2,1)}, bf16[1024,3072]{1,0:T(8,128)(2,1)}, f32[1024,768]{1,0:T(8,128)}, bf16[1024,768]{1,0:T(8,128)(2,1)}, bf16[10...) custom-call(bf16[1024,768]{1,0:T(8,128)(2,1)} %refs_0_.3, f32[1024,768]{1,0:T(8,128)} %get-tuple-element.116.refs_1_, ...), custom_call_target="tpu_custom_call" | custom-call | flops 27179089920 | bytes 12189696 | tf_op jit(solution)/shard_map/pallas_call | solution.py:570
  324.6 6.5 shard_map.284
  331.2 7.9 %shard_map.281 = bf16[1,4,2,384,384]{4,3,2,1,0:T(8,128)(2,1)} custom-call(s32[4]{0:T(128)} %pad_add_fusion.at_ref, bf16[1024,3072]{1,0:T(8,128)(2,1)} %get-tuple-element.127.left_ref, bf16[1024,768]{1,0:T(8,128)(2,1)} %get-tuple-element.128.right_ref), custom_call_target="tpu_custom_call" | custom-call | flops 4831838208 | bytes 7864320 | tf_op jit(solution)/shard_map/pallas_call | solution.py:712
  339.5 4.1 shard_map.280
  343.7 7.0 shard_map.285
  350.7 1.4 copy-done.6
  352.1 8.5 %shard_map.282 = (bf16[4,480,384]{2,1,0:T(8,128)(2,1)}, bf16[4,480,384]{2,1,0:T(8,128)(2,1)}) custom-call(s32[4]{0:T(128)} %pad_add_fusion.at_ref, bf16[1024,3072]{1,0:T(8,128)(2,1)} %get-tuple-element.127.left_ref, bf16[1024,768]{1,0:T(8,128)(2,1)} %get-tuple-element.128.right_ref, bf16[1,4,2,384,384]{4,3,2,1,0:T(8,128)(2,1)} %copy-done.6), custom_call_target="tpu_custom_call" | custom-call | flops 4831838208 | bytes 7864320 | tf_op jit(solution)/shard_map/pallas_call | solution.py:712
  360.7 0.8 copy-done.3
  361.5 4.3 shard_map.283
  365.8 88.9 %shard_map.286 = (bf16[3,1024,768]{2,1,0:T(8,128)(2,1)}, f32[1,6,8,128]{3,2,1,0:T(8,128)}, bf16[480,384]{1,0:T(8,128)(2,1)}, bf16[480,384]{1,0:T(8,128)(2,1)}, bf16[4,2,48,768]{3,2,1,0:T(8,128)(2,1)}) custom-call(s32[1,6,2,1024]{3,2,1,0:T(2,128)} %get-tuple-element.102.refs_1_.refs_0_, bf16[1024,768]{1,0:T(8,128)(2,1)} %get-tuple-element.122.refs_1_, ...), custom_call_target="tpu_custom_call" | custom-call | bytes 200000000 | tf_op jit(solution)/shard_map/pallas_call | solution.py:1157
  454.7 6.5 shard_map.294
  461.3 1.1 collective-permute-start.6
  462.4 29.1 %shard_map.287 = (bf16[1024,768]{1,0:T(8,128)(2,1)}, bf16[1024,3072]{1,0:T(8,128)(2,1)}, f32[1024,768]{1,0:T(8,128)}, bf16[1024,768]{1,0:T(8,128)(2,1)}, bf16[10...) custom-call(f32[1024,768]{1,0:T(8,128)} %get-tuple-element.121.refs_0_, ...), custom_call_target="tpu_custom_call" | custom-call | flops 27179089920 | bytes 13762560 | tf_op jit(solution)/shard_map/pallas_call | solution.py:570
  491.6 6.5 shard_map.292
  498.0 7.9 %shard_map.289 = bf16[1,4,2,384,384]{4,3,2,1,0:T(8,128)(2,1)} custom-call(s32[4]{0:T(128)} %pad_add_fusion.at_ref, bf16[1024,3072]{1,0:T(8,128)(2,1)} %get-tuple-element.148.left_ref, bf16[1024,768]{1,0:T(8,128)(2,1)} %get-tuple-element.149.right_ref), custom_call_target="tpu_custom_call" | custom-call | flops 4831838208 | bytes 7864320 | tf_op jit(solution)/shard_map/pallas_call | solution.py:712
  506.0 0.5 collective-permute-start.4
  506.4 4.1 shard_map.288
  510.6 7.0 shard_map.295
  517.5 7.0 shard_map.293
  524.5 1.4 copy-done.5
  525.9 8.6 %shard_map.290 = (bf16[4,480,384]{2,1,0:T(8,128)(2,1)}, bf16[4,480,384]{2,1,0:T(8,128)(2,1)}) custom-call(s32[4]{0:T(128)} %pad_add_fusion.at_ref, bf16[1024,3072]{1,0:T(8,128)(2,1)} %get-tuple-element.148.left_ref, bf16[1024,768]{1,0:T(8,128)(2,1)} %get-tuple-element.149.right_ref, bf16[1,4,2,384,384]{4,3,2,1,0:T(8,128)(2,1)} %copy-done.5), custom_call_target="tpu_custom_call" | custom-call | flops 4831838208 | bytes 7864320 | tf_op jit(solution)/shard_map/pallas_call | solution.py:712
  534.5 0.8 copy-done.2
  535.3 4.3 shard_map.291
  539.6 93.1 %shard_map.296 = (bf16[3,1024,768]{2,1,0:T(8,128)(2,1)}, f32[1,6,8,128]{3,2,1,0:T(8,128)}, bf16[480,384]{1,0:T(8,128)(2,1)}, bf16[480,384]{1,0:T(8,128)(2,1)}, b...) custom-call(s32[1,6,2,1024]{3,2,1,0:T(2,128)} %get-tuple-element.102.refs_1_.refs_0_, ...), custom_call_target="tpu_custom_call" | custom-call | bytes 200000000 | tf_op jit(solution)/shard_map/pallas_call | solution.py:1157
  632.8 6.7 shard_map.297
  639.4 0.8 fusion.8
  640.3 0.8 fusion.10
  641.1 0.8 fusion.9
  641.9 8.8 %shard_map.299 = f32[1024,768]{1,0:T(8,128)} custom-call(f32[1024,768]{1,0:T(8,128)} %get-tuple-element.163.above_ref, bf16[3,1024,768]{2,1,0:T(8,128)(2,1)} %get-tuple-element.160.right_ref.proj_ref, bf16[768,2304]{1,0:T(8,128)(2,1)} %bitcast.88), custom_call_target="tpu_custom_call" | custom-call | flops 4348654592 | bytes 6684672 | tf_op jit(solution)/shard_map/pallas_call | solution.py:602
  650.7 1.2 copy-done.7
  651.9 6.9 shard_map.298
  658.9 50.9 %shard_map.300 = (bf16[4,3,48,384]{3,2,1,0:T(8,128)(2,1)}, f32[40,768]{1,0:T(8,128)}) custom-call(bf16[3,4,2,48,384]{4,3,2,1,0:T(8,128)(2,1)} %get-tuple-element.165.refs_0_, bf16[3,4,2,48,384]{4,3,2,1,0:T(8,128)(2,1)} %get-tuple-element.166.refs_1_, f32[8,768]{1,0:T(8,128)} %get-tuple-element.167.refs_2_, f32[1,3072]{1,0:T(1,128)} %get-tuple-element.168.refs_3_, ...), custom_call_target="tpu_custom_call" | custom-call | bytes 200000000 | tf_op jit(solution)/shard_map/pallas_call | solution.py:1157
  709.8 1.1 fusion.12
  710.9 0.8 slice_bitcast_fusion
  711.7 0.8 slice.100
  712.5 0.8 slice.101
  713.3 1.8 fusion.11
  715.1 0.7 fusion
  715.8 0.7 fusion.1
  716.4 0.6 fusion.2
  717.1 0.6 fusion.4
  717.7 0.6 fusion.6
  718.4 6.1 shard_map.301
  (32 shorter events, 0.8 us)
Async XLA Ops:
  331.1 12.6 %collective-permute-start.2 = (bf16[2,4,2,96,768]{4,3,2,1,0:T(8,128)(2,1)}, bf16[2,4,2,96,768]{4,3,2,1,0:T(8,128)(2,1)}, u32[]{:S(2)}, u32[]{:S(2)}) collective-permute-start(bf16[2,4,2,96,768]{4,3,2,1,0:T(8,128)(2,1)} %shard_map.284), channel_id=1, source_target_pairs={{0,8},{1,9},{2,10},{3,11},{4,12},{5,13},{6,14},{7,15},{8,0},{9,1},... | collective-permute-start | bytes 7077896 | tf_op jit(solution)/shard_map/ppermute | solution.py:747
  339.1 11.7 %collective-permute-start.1 = (bf16[1,4,2,384,384]{4,3,2,1,0:T(8,128)(2,1)}, bf16[1,4,2,384,384]{4,3,2,1,0:T(8,128)(2,1)S(1)}, u32[]{:S(2)}, u32[]{:S(2)}) collective-permute-start(bf16[1,4,2,384,384]{4,3,2,1,0:T(8,128)(2,1)} %shard_map.281), channel_id=1, source_target_pairs={{0,8},{1,9},{2,10},{3,11},{4,12},{5,13},{6,14},{7,15},{8,0},{9,1},... | collective-permute-start | bytes 7077896 | tf_op jit(solution)/shard_map/ppermute | solution.py:747
  343.6 17.1 %collective-permute-start = (bf16[1,4,2,96,384]{4,3,2,1,0:T(8,128)(2,1)}, bf16[1,4,2,96,384]{4,3,2,1,0:T(8,128)(2,1)S(1)}, u32[]{:S(2)}, u32[]{:S(2)}) collective-permute-start(bf16[1,4,2,96,384]{4,3,2,1,0:T(8,128)(2,1)} %shard_map.280), channel_id=1, source_target_pairs={{0,8},{1,9},{2,10},{3,11},{4,12},{5,13},{6,14},{7,15},{8,0},{9,1},... | collective-permute-start | bytes 1769480 | tf_op jit(solution)/shard_map/ppermute | solution.py:747
  350.7 1.4 copy-start.6
  360.7 0.8 copy-start.3
  461.3 49.3 %collective-permute-start.6 = (bf16[3,4,2,96,384]{4,3,2,1,0:T(8,128)(2,1)}, bf16[3,4,2,96,384]{4,3,2,1,0:T(8,128)(2,1)}, u32[]{:S(2)}, u32[]{:S(2)}) collective-permute-start(bf16[3,4,2,96,384]{4,3,2,1,0:T(8,128)(2,1)} %shard_map.294), channel_id=1, source_target_pairs={{0,8},{1,9},{2,10},{3,11},{4,12},{5,13},{6,14},{7,15},{8,0},{9,1},... | collective-permute-start | bytes 5308424 | tf_op jit(solution)/shard_map/ppermute | solution.py:747
  498.0 19.5 %collective-permute-start.5 = (bf16[2,4,2,96,768]{4,3,2,1,0:T(8,128)(2,1)}, bf16[2,4,2,96,768]{4,3,2,1,0:T(8,128)(2,1)}, u32[]{:S(2)}, u32[]{:S(2)}) collective-permute-start(bf16[2,4,2,96,768]{4,3,2,1,0:T(8,128)(2,1)} %shard_map.292), channel_id=1, source_target_pairs={{0,8},{1,9},{2,10},{3,11},{4,12},{5,13},{6,14},{7,15},{8,0},{9,1},... | collective-permute-start | bytes 7077896 | tf_op jit(solution)/shard_map/ppermute | solution.py:747
  506.0 18.5 %collective-permute-start.4 = (bf16[1,4,2,384,384]{4,3,2,1,0:T(8,128)(2,1)}, bf16[1,4,2,384,384]{4,3,2,1,0:T(8,128)(2,1)S(1)}, u32[]{:S(2)}, u32[]{:S(2)}) collective-permute-start(bf16[1,4,2,384,384]{4,3,2,1,0:T(8,128)(2,1)} %shard_map.289), channel_id=1, source_target_pairs={{0,8},{1,9},{2,10},{3,11},{4,12},{5,13},{6,14},{7,15},{8,0},{9,1},... | collective-permute-start | bytes 7077896 | tf_op jit(solution)/shard_map/ppermute | solution.py:747
  510.5 23.9 %collective-permute-start.3 = (bf16[1,4,2,96,384]{4,3,2,1,0:T(8,128)(2,1)}, bf16[1,4,2,96,384]{4,3,2,1,0:T(8,128)(2,1)S(1)}, u32[]{:S(2)}, u32[]{:S(2)}) collective-permute-start(bf16[1,4,2,96,384]{4,3,2,1,0:T(8,128)(2,1)} %shard_map.288), channel_id=1, source_target_pairs={{0,8},{1,9},{2,10},{3,11},{4,12},{5,13},{6,14},{7,15},{8,0},{9,1},... | collective-permute-start | bytes 1769480 | tf_op jit(solution)/shard_map/ppermute | solution.py:747
  524.5 1.4 copy-start.5
  534.5 0.8 copy-start.2
  632.7 6.7 copy-start
  632.7 7.5 %copy-start.4 = (bf16[4,3,48,384]{3,2,1,0:T(8,128)(2,1)S(1)}, bf16[4,3,48,384]{3,2,1,0:T(8,128)(2,1)}, u32[]{:S(2)}) copy-start(bf16[4,3,48,384]{3,2,1,0:T(8,128)(2,1)} %get-tuple-element.174) | copy-start | bytes 1327108
  639.4 1.7 copy-start.1
  639.4 11.3 %collective-permute-start.7 = (bf16[3,4,2,96,384]{4,3,2,1,0:T(8,128)(2,1)}, bf16[3,4,2,96,384]{4,3,2,1,0:T(8,128)(2,1)S(1)}, u32[]{:S(2)}, u32[]{:S(2)}) collective-permute-start(bf16[3,4,2,96,384]{4,3,2,1,0:T(8,128)(2,1)} %shard_map.297), channel_id=1, source_target_pairs={{0,8},{1,9},{2,10},{3,11},{4,12},{5,13},{6,14},{7,15},{8,0},{9,1},... | collective-permute-start | bytes 5308424 | tf_op jit(solution)/shard_map/ppermute | solution.py:747
  650.7 1.2 copy-start.7

commit v10 on v9

--- a/solution.py
+++ b/solution.py
@@ -871,17 +871,23 @@
             last.append(send(piece, piece, m, 16, dc=1))
 
     order = sorted(range(count), key=lambda m: (not plan[m][1], -outs[m].shape[-1]))
-    for m in order:
+
+    def set_out(m):
         locals_[m].wait()
         mine = part(m, z, x, y, core)
         along_z[m] = [send(mine, mine, m, k - 1, dz=k) for k in range(1, CHIPS_Z)]
         along_x[m], over_y[m] = [], []
         spread(m, z, x)
+
+    for m in order[:2]:
+        set_out(m)
     for place, m in enumerate(order):
         for k in range(1, CHIPS_Z):
             next(todo, None)
             along_z[m][k - 1].wait_recv()
             spread(m, behind(k), x)
+        if place + 2 < count:
+            set_out(order[place + 2])
         if place:
             after_x(order[place - 1])
     after_x(order[-1])
@@ -1012,11 +1018,16 @@
         pack_sums(v_send.at[0], vec_ins)
         v_copies.append(send(v_send.at[0], v_land.at[0], v_sems, 0, dc=1))
     a_x, b_y = [[] for _ in range(flats)], [[] for _ in range(count)]
-    for j, to in enumerate(ahead):
+
+    def set_out(j):
+        to = ahead[j]
         for i, (first, _) in enumerate(a_ins):
             a_x[i].append(send(first.at[to], a_scratch[i][0].at[j], a_sems[i], j, dx=1))
         for i, (first, _) in enumerate(b_ins):
             b_y[i].append(send(first.at[:, to], b_scratch[i][0].at[j], b_sems[i], j, dy=1))
+
+    set_out(0)
+    set_out(1)
     steps = (dict(dc=1), dict(dy=1), dict(dx=1), dict(dz=2), dict(dz=flip_z))
 
     def add_vectors(s):
@@ -1064,6 +1075,8 @@
         next(todo, None)
         for i in range(count):
             b_along_x(i, j)
+        if j + 2 < CHIPS_Z:
+            set_out(j + 2)
         if j:
             for i in range(count):
                 b_along_z(i, j - 1)

time: 735 us -> 714 us (0.971)
  Pallas kernels: 685 us -> 665 us
    pallas_call x3, Pallas kernels: 233 us -> 218 us  [reduce_sums(): pl.pallas_call(functools.partial(reduce_kernel, len(flats), len(pairs), l...]
where the time goes in v10:
time: 714 us; the launch traced here: 704 us
  Pallas kernels  665 us (93%)
  local copies, waits for them, and re-layouts  22.7 us (3%)
  other arithmetic  13.4 us (2%)
    pallas_call x3, Pallas kernels, reduce_sums(): pl.pallas_call(functools.partial(reduce_kernel, len(flats), len(pairs), l...  218 us
    pallas_call x3, Pallas kernels, gather(): pl.pallas_call(functools.partial(gather_kernel, plan, work, len(work_args...  205 us
    pallas_call x16, Pallas kernels, product(): pl.pallas_call(functools.partial(weight_grad_kernel, split_y), grid_spec=...  104 us
    pallas_call x2, Pallas kernels, feed(): pl.pallas_call(functools.partial(feed_kernel, layer), grid=(count // ROW_...  56.3 us
    pallas_call x2, Pallas kernels, feed_back(): pl.pallas_call(functools.partial(feed_back_kernel, layer, proj is not Non...  50.8 us
    pallas_call x2, Pallas kernels, project(): pl.pallas_call(functools.partial(project_kernel, layer), grid=(count // R...  16 us
  transfers between devices with their start and end apart: 8, of which 0 were waited for; matrix products, arithmetic and copies ran while one was open for 0% of the time, Pallas kernels for 15%

profile of v10, /device:TPU:17, one launch (start us, length us, event | category | flops | bytes accessed | tf_op | source)
XLA Modules:
  0.0 703.8 jit_solution(15206703033943961340)
XLA Ops:
  0.6 1.5 transpose_reshape.3.refs_2_
  2.1 0.9 concatenate.3
  3.0 0.6 pad.4.refs_3_
  3.6 40.2 %shard_map.272 = (s32[1,6,2,1024]{3,2,1,0:T(2,128)}, bf16[1,12,1024,128]{3,2,1,0:T(8,128)(2,1)}, bf16[4,2,1,16,1152]{4,3,2,1,0:T(8,128)(2,1)}, bf16[4,2,2,48,2304]{4,3,2,1,0:T(8,128)(2,1)}) custom-call(s32[1,13]{1,0:T(1,128)} %refs_0_.2, s32[1,1,1024]{2,1,0:T(1,128)} %bitcast.78, s32[1,6,2,1024]{3,2,1,0:T(2,128)} %transpose_reshape.3.refs_2_, ...), custom_call_target="tpu_custom_call" | custom-call | bytes 200000000 | tf_op jit(solution)/shard_map/pallas_call | solution.py:916
  43.8 0.9 slice.91
  44.8 9.5 %slice_convert_fusion.1 = (f32[2,8,96]{2,1,0:T(8,128)S(1)}, f32[2,8,96]{2,1,0:T(8,128)S(1)}, f32[2,8,96]{2,1,0:T(8,128)S(1)}, f32[2,8,96]{2,1,0:T(8,128)S(1)}, f...) fusion(bf16[2,8,1152]{2,1,0:T(8,128)(2,1)S(1)} %bitcast.67), kind=kLoop, calls=%fused_computation.21 | loop fusion | flops 9216 | bytes 55296 | tf_op jit(solution)/shard_map/convert_element_type | solution.py:754
  54.3 0.7 reshape.124.bias_ref
  55.0 0.7 reshape.126.attn_gain_ref.refs_9_.refs_11_
  55.7 0.7 reshape.130.ffn_gain_ref.refs_10_.refs_12_
  56.3 0.7 reshape.125.out_bias_ref
  57.0 0.7 reshape.127.attn_shift_ref
  57.7 0.7 reshape.129.ffout_bias_ref
  58.4 0.7 reshape.131.ffn_shift_ref
  59.0 0.6 copy.36
  59.7 7.8 %shard_map.273.refs_0_ = bf16[1024,2304]{1,0:T(8,128)(2,1)} custom-call(bf16[1024,768]{1,0:T(8,128)(2,1)} %left_ref.3, bf16[768,2304]{1,0:T(8,128)(2,1)} %bitcast.87, f32[2,1536]{1,0:T(2,128)} %reshape.124.bias_ref), custom_call_target="tpu_custom_call" | custom-call | flops 4348654592 | bytes 5111808 | tf_op jit(solution)/shard_map/pallas_call | solution.py:514
  67.4 88.0 %shard_map.274 = (bf16[1024,768]{1,0:T(8,128)(2,1)}, bf16[1,12,1024,128]{3,2,1,0:T(8,128)(2,1)}, bf16[1,12,1024,128]{3,2,1,0:T(8,128)(2,1)}, bf16[1,12,1024,128]...) custom-call(bf16[1024,2304]{1,0:T(8,128)(2,1)} %shard_map.273.refs_0, ...), custom_call_target="tpu_custom_call" | custom-call | bytes 200000000 | tf_op jit(solution)/shard_map/pallas_call | solution.py:916
  155.4 27.9 %shard_map.275 = (bf16[1024,768]{1,0:T(8,128)(2,1)}, bf16[1024,3072]{1,0:T(8,128)(2,1)}, bf16[1024,3072]{1,0:T(8,128)(2,1)}, f32[1024,768]{1,0:T(8,128)}, f32[10...) custom-call(bf16[1024,768]{1,0:T(8,128)(2,1)} %get-tuple-element.104, ...), custom_call_target="tpu_custom_call" | custom-call | flops 27179089920 | bytes 12189696 | tf_op jit(solution)/shard_map/pallas_call | solution.py:529
  183.3 8.2 %shard_map.276.refs_0_ = bf16[1024,2304]{1,0:T(8,128)(2,1)} custom-call(bf16[1024,768]{1,0:T(8,128)(2,1)} %get-tuple-element.108.rows_ref.left_ref, bf16[768,2304]{1,0:T(8,128)(2,1)} %bitcast.89, f32[2,1536]{1,0:T(2,128)} %reshape.124.bias_ref), custom_call_target="tpu_custom_call" | custom-call | flops 4348654592 | bytes 5111808 | tf_op jit(solution)/shard_map/pallas_call | solution.py:514
  191.6 76.6 %shard_map.277 = (bf16[1024,768]{1,0:T(8,128)(2,1)}, bf16[1,12,1024,128]{3,2,1,0:T(8,128)(2,1)}, bf16[1,12,1024,128]{3,2,1,0:T(8,128)(2,1)}, bf16[1,12,1024,128]...) custom-call(bf16[1024,2304]{1,0:T(8,128)(2,1)} %shard_map.276.refs_0, ...), custom_call_target="tpu_custom_call" | custom-call | bytes 200000000 | tf_op jit(solution)/shard_map/pallas_call | solution.py:916
  268.2 0.6 pad_add_fusion.at_ref
  268.8 28.4 %shard_map.278 = (bf16[1024,768]{1,0:T(8,128)(2,1)}, bf16[1024,3072]{1,0:T(8,128)(2,1)}, bf16[1024,3072]{1,0:T(8,128)(2,1)}, f32[1024,768]{1,0:T(8,128)}, f32[10...) custom-call(bf16[1024,768]{1,0:T(8,128)(2,1)} %get-tuple-element.110, ...), custom_call_target="tpu_custom_call" | custom-call | flops 27179089920 | bytes 12189696 | tf_op jit(solution)/shard_map/pallas_call | solution.py:529
  297.2 21.7 %shard_map.279 = (bf16[1024,768]{1,0:T(8,128)(2,1)}, bf16[1024,3072]{1,0:T(8,128)(2,1)}, f32[1024,768]{1,0:T(8,128)}, bf16[1024,768]{1,0:T(8,128)(2,1)}, bf16[10...) custom-call(bf16[1024,768]{1,0:T(8,128)(2,1)} %refs_0_.3, f32[1024,768]{1,0:T(8,128)} %get-tuple-element.116.refs_1_, ...), custom_call_target="tpu_custom_call" | custom-call | flops 27179089920 | bytes 12189696 | tf_op jit(solution)/shard_map/pallas_call | solution.py:570
  318.8 6.5 shard_map.284
  325.4 7.9 %shard_map.281 = bf16[1,4,2,384,384]{4,3,2,1,0:T(8,128)(2,1)} custom-call(s32[4]{0:T(128)} %pad_add_fusion.at_ref, bf16[1024,3072]{1,0:T(8,128)(2,1)} %get-tuple-element.127.left_ref, bf16[1024,768]{1,0:T(8,128)(2,1)} %get-tuple-element.128.right_ref), custom_call_target="tpu_custom_call" | custom-call | flops 4831838208 | bytes 7864320 | tf_op jit(solution)/shard_map/pallas_call | solution.py:712
  333.7 4.1 shard_map.280
  337.9 7.0 %shard_map.285 = (bf16[2,4,2,48,768]{4,3,2,1,0:T(8,128)(2,1)}, bf16[2,4,2,48,768]{4,3,2,1,0:T(8,128)(2,1)}) custom-call(s32[4]{0:T(128)} %pad_add_fusion.at_ref, bf16[1024,768]{1,0:T(8,128)(2,1)} %get-tuple-element.133.left_ref, bf16[1024,3072]{1,0:T(8,128)(2,1)} %get-tuple-element.134.right_ref, bf16[2,4,2,96,768]{4,3,2,1,0:T(8,128)(2,1)} %collective-permute-done.2.refs_0_), custom_call_target="tpu_custom_call" | custom-call | flops 4831838208 | bytes 7864320 | tf_op jit(solution)/shard_map/pallas_call | solution.py:712
  344.9 1.4 copy-done.6
  346.3 8.5 %shard_map.282 = (bf16[4,480,384]{2,1,0:T(8,128)(2,1)}, bf16[4,480,384]{2,1,0:T(8,128)(2,1)}) custom-call(s32[4]{0:T(128)} %pad_add_fusion.at_ref, bf16[1024,3072]{1,0:T(8,128)(2,1)} %get-tuple-element.127.left_ref, bf16[1024,768]{1,0:T(8,128)(2,1)} %get-tuple-element.128.right_ref, bf16[1,4,2,384,384]{4,3,2,1,0:T(8,128)(2,1)} %copy-done.6), custom_call_target="tpu_custom_call" | custom-call | flops 4831838208 | bytes 7864320 | tf_op jit(solution)/shard_map/pallas_call | solution.py:712
  354.9 0.8 copy-done.3
  355.7 4.3 shard_map.283
  360.0 79.3 %shard_map.286 = (bf16[3,1024,768]{2,1,0:T(8,128)(2,1)}, f32[1,6,8,128]{3,2,1,0:T(8,128)}, bf16[480,384]{1,0:T(8,128)(2,1)}, bf16[480,384]{1,0:T(8,128)(2,1)}, bf16[4,2,48,768]{3,2,1,0:T(8,128)(2,1)}) custom-call(s32[1,6,2,1024]{3,2,1,0:T(2,128)} %get-tuple-element.102.refs_1_.refs_0_, bf16[1024,768]{1,0:T(8,128)(2,1)} %get-tuple-element.122.refs_1_, ...), custom_call_target="tpu_custom_call" | custom-call | bytes 200000000 | tf_op jit(solution)/shard_map/pallas_call | solution.py:1170
  439.3 6.5 shard_map.294
  445.8 29.1 %shard_map.287 = (bf16[1024,768]{1,0:T(8,128)(2,1)}, bf16[1024,3072]{1,0:T(8,128)(2,1)}, f32[1024,768]{1,0:T(8,128)}, bf16[1024,768]{1,0:T(8,128)(2,1)}, bf16[10...) custom-call(f32[1024,768]{1,0:T(8,128)} %get-tuple-element.121.refs_0_, ...), custom_call_target="tpu_custom_call" | custom-call | flops 27179089920 | bytes 13762560 | tf_op jit(solution)/shard_map/pallas_call | solution.py:570
  475.0 6.5 shard_map.292
  481.5 0.5 collective-permute-start.5
  482.0 7.9 %shard_map.289 = bf16[1,4,2,384,384]{4,3,2,1,0:T(8,128)(2,1)} custom-call(s32[4]{0:T(128)} %pad_add_fusion.at_ref, bf16[1024,3072]{1,0:T(8,128)(2,1)} %get-tuple-element.148.left_ref, bf16[1024,768]{1,0:T(8,128)(2,1)} %get-tuple-element.149.right_ref), custom_call_target="tpu_custom_call" | custom-call | flops 4831838208 | bytes 7864320 | tf_op jit(solution)/shard_map/pallas_call | solution.py:712
  489.9 4.1 shard_map.288
  494.0 0.5 collective-permute-start.3
  494.5 7.0 shard_map.295
  501.4 7.0 shard_map.293
  508.4 1.4 copy-done.5
  509.8 8.6 %shard_map.290 = (bf16[4,480,384]{2,1,0:T(8,128)(2,1)}, bf16[4,480,384]{2,1,0:T(8,128)(2,1)}) custom-call(s32[4]{0:T(128)} %pad_add_fusion.at_ref, bf16[1024,3072]{1,0:T(8,128)(2,1)} %get-tuple-element.148.left_ref, bf16[1024,768]{1,0:T(8,128)(2,1)} %get-tuple-element.149.right_ref, bf16[1,4,2,384,384]{4,3,2,1,0:T(8,128)(2,1)} %copy-done.5), custom_call_target="tpu_custom_call" | custom-call | flops 4831838208 | bytes 7864320 | tf_op jit(solution)/shard_map/pallas_call | solution.py:712
  518.4 0.8 copy-done.2
  519.2 4.3 shard_map.291
  523.5 90.6 %shard_map.296 = (bf16[3,1024,768]{2,1,0:T(8,128)(2,1)}, f32[1,6,8,128]{3,2,1,0:T(8,128)}, bf16[480,384]{1,0:T(8,128)(2,1)}, bf16[480,384]{1,0:T(8,128)(2,1)}, b...) custom-call(s32[1,6,2,1024]{3,2,1,0:T(2,128)} %get-tuple-element.102.refs_1_.refs_0_, ...), custom_call_target="tpu_custom_call" | custom-call | bytes 200000000 | tf_op jit(solution)/shard_map/pallas_call | solution.py:1170
  614.2 6.7 shard_map.297
  620.9 0.8 fusion.8
  621.7 0.8 fusion.10
  622.5 0.8 fusion.9
  623.4 8.8 %shard_map.299 = f32[1024,768]{1,0:T(8,128)} custom-call(f32[1024,768]{1,0:T(8,128)} %get-tuple-element.163.above_ref, bf16[3,1024,768]{2,1,0:T(8,128)(2,1)} %get-tuple-element.160.right_ref.proj_ref, bf16[768,2304]{1,0:T(8,128)(2,1)} %bitcast.88), custom_call_target="tpu_custom_call" | custom-call | flops 4348654592 | bytes 6684672 | tf_op jit(solution)/shard_map/pallas_call | solution.py:602
  632.2 1.2 copy-done.7
  633.4 6.9 shard_map.298
  640.3 48.6 %shard_map.300 = (bf16[4,3,48,384]{3,2,1,0:T(8,128)(2,1)}, f32[40,768]{1,0:T(8,128)}) custom-call(bf16[3,4,2,48,384]{4,3,2,1,0:T(8,128)(2,1)} %get-tuple-element.165.refs_0_, bf16[3,4,2,48,384]{4,3,2,1,0:T(8,128)(2,1)} %get-tuple-element.166.refs_1_, f32[8,768]{1,0:T(8,128)} %get-tuple-element.167.refs_2_, f32[1,3072]{1,0:T(1,128)} %get-tuple-element.168.refs_3_, ...), custom_call_target="tpu_custom_call" | custom-call | bytes 200000000 | tf_op jit(solution)/shard_map/pallas_call | solution.py:1170
  688.9 1.1 fusion.12
  690.0 0.8 slice_bitcast_fusion
  690.8 0.8 slice.100
  691.6 0.8 slice.101
  692.4 1.8 fusion.11
  694.2 0.7 fusion
  694.9 0.7 fusion.1
  695.5 0.6 fusion.2
  696.2 0.6 fusion.4
  696.8 0.6 fusion.6
  697.5 6.1 shard_map.301
  (32 shorter events, 0.8 us)
Async XLA Ops:
  325.3 12.6 %collective-permute-start.2 = (bf16[2,4,2,96,768]{4,3,2,1,0:T(8,128)(2,1)}, bf16[2,4,2,96,768]{4,3,2,1,0:T(8,128)(2,1)}, u32[]{:S(2)}, u32[]{:S(2)}) collective-permute-start(bf16[2,4,2,96,768]{4,3,2,1,0:T(8,128)(2,1)} %shard_map.284), channel_id=1, source_target_pairs={{0,8},{1,9},{2,10},{3,11},{4,12},{5,13},{6,14},{7,15},{8,0},{9,1},... | collective-permute-start | bytes 7077896 | tf_op jit(solution)/shard_map/ppermute | solution.py:747
  333.3 11.7 %collective-permute-start.1 = (bf16[1,4,2,384,384]{4,3,2,1,0:T(8,128)(2,1)}, bf16[1,4,2,384,384]{4,3,2,1,0:T(8,128)(2,1)S(1)}, u32[]{:S(2)}, u32[]{:S(2)}) collective-permute-start(bf16[1,4,2,384,384]{4,3,2,1,0:T(8,128)(2,1)} %shard_map.281), channel_id=1, source_target_pairs={{0,8},{1,9},{2,10},{3,11},{4,12},{5,13},{6,14},{7,15},{8,0},{9,1},... | collective-permute-start | bytes 7077896 | tf_op jit(solution)/shard_map/ppermute | solution.py:747
  337.8 17.1 %collective-permute-start = (bf16[1,4,2,96,384]{4,3,2,1,0:T(8,128)(2,1)}, bf16[1,4,2,96,384]{4,3,2,1,0:T(8,128)(2,1)S(1)}, u32[]{:S(2)}, u32[]{:S(2)}) collective-permute-start(bf16[1,4,2,96,384]{4,3,2,1,0:T(8,128)(2,1)} %shard_map.280), channel_id=1, source_target_pairs={{0,8},{1,9},{2,10},{3,11},{4,12},{5,13},{6,14},{7,15},{8,0},{9,1},... | collective-permute-start | bytes 1769480 | tf_op jit(solution)/shard_map/ppermute | solution.py:747
  344.9 1.4 copy-start.6
  354.9 0.8 copy-start.3
  445.8 48.7 %collective-permute-start.6 = (bf16[3,4,2,96,384]{4,3,2,1,0:T(8,128)(2,1)}, bf16[3,4,2,96,384]{4,3,2,1,0:T(8,128)(2,1)}, u32[]{:S(2)}, u32[]{:S(2)}) collective-permute-start(bf16[3,4,2,96,384]{4,3,2,1,0:T(8,128)(2,1)} %shard_map.294), channel_id=1, source_target_pairs={{0,8},{1,9},{2,10},{3,11},{4,12},{5,13},{6,14},{7,15},{8,0},{9,1},... | collective-permute-start | bytes 5308424 | tf_op jit(solution)/shard_map/ppermute | solution.py:747
  481.5 20.0 %collective-permute-start.5 = (bf16[2,4,2,96,768]{4,3,2,1,0:T(8,128)(2,1)}, bf16[2,4,2,96,768]{4,3,2,1,0:T(8,128)(2,1)}, u32[]{:S(2)}, u32[]{:S(2)}) collective-permute-start(bf16[2,4,2,96,768]{4,3,2,1,0:T(8,128)(2,1)} %shard_map.292), channel_id=1, source_target_pairs={{0,8},{1,9},{2,10},{3,11},{4,12},{5,13},{6,14},{7,15},{8,0},{9,1},... | collective-permute-start | bytes 7077896 | tf_op jit(solution)/shard_map/ppermute | solution.py:747
  489.9 18.5 %collective-permute-start.4 = (bf16[1,4,2,384,384]{4,3,2,1,0:T(8,128)(2,1)}, bf16[1,4,2,384,384]{4,3,2,1,0:T(8,128)(2,1)S(1)}, u32[]{:S(2)}, u32[]{:S(2)}) collective-permute-start(bf16[1,4,2,384,384]{4,3,2,1,0:T(8,128)(2,1)} %shard_map.289), channel_id=1, source_target_pairs={{0,8},{1,9},{2,10},{3,11},{4,12},{5,13},{6,14},{7,15},{8,0},{9,1},... | collective-permute-start | bytes 7077896 | tf_op jit(solution)/shard_map/ppermute | solution.py:747
  494.0 24.4 %collective-permute-start.3 = (bf16[1,4,2,96,384]{4,3,2,1,0:T(8,128)(2,1)}, bf16[1,4,2,96,384]{4,3,2,1,0:T(8,128)(2,1)S(1)}, u32[]{:S(2)}, u32[]{:S(2)}) collective-permute-start(bf16[1,4,2,96,384]{4,3,2,1,0:T(8,128)(2,1)} %shard_map.288), channel_id=1, source_target_pairs={{0,8},{1,9},{2,10},{3,11},{4,12},{5,13},{6,14},{7,15},{8,0},{9,1},... | collective-permute-start | bytes 1769480 | tf_op jit(solution)/shard_map/ppermute | solution.py:747
  508.4 1.4 copy-start.5
  518.4 0.8 copy-start.2
  614.2 6.7 copy-start
  614.2 7.5 %copy-start.4 = (bf16[4,3,48,384]{3,2,1,0:T(8,128)(2,1)S(1)}, bf16[4,3,48,384]{3,2,1,0:T(8,128)(2,1)}, u32[]{:S(2)}) copy-start(bf16[4,3,48,384]{3,2,1,0:T(8,128)(2,1)} %get-tuple-element.174) | copy-start | bytes 1327108
  620.9 1.7 copy-start.1
  620.9 11.3 %collective-permute-start.7 = (bf16[3,4,2,96,384]{4,3,2,1,0:T(8,128)(2,1)}, bf16[3,4,2,96,384]{4,3,2,1,0:T(8,128)(2,1)S(1)}, u32[]{:S(2)}, u32[]{:S(2)}) collective-permute-start(bf16[3,4,2,96,384]{4,3,2,1,0:T(8,128)(2,1)} %shard_map.297), channel_id=1, source_target_pairs={{0,8},{1,9},{2,10},{3,11},{4,12},{5,13},{6,14},{7,15},{8,0},{9,1},... | collective-permute-start | bytes 5308424 | tf_op jit(solution)/shard_map/ppermute | solution.py:747
  632.2 1.2 copy-start.7

commit v11 on v10

--- a/solution.py
+++ b/solution.py
@@ -747,15 +747,6 @@
     return lax.ppermute(value, AXES, pairs)
 
 
-def spread_vectors(found, sizes):
-    found = found[:, :, 0, :LAYERS].reshape(-1, LAYERS, found.shape[-1]).transpose(1, 0, 2)
-    out, at = [], 0
-    for size in sizes:
-        out.append(found[:, :, at : at + size].reshape(LAYERS, -1).astype(jnp.float32))
-        at += size
-    return out
-
-
 def cut_sums(place, groups):
     at = place.at
     arrived = []
@@ -779,15 +770,15 @@
     trees, pairs = ins[2].shape[:2]
     for tree in range(trees):
         for pair in range(pairs):
-            prep_pair(*ins, *outs, tree, tree, pair)
+            prep_pair(*ins, *outs[:2], tree, tree, pair)
             yield
 
 
-def gather_kernel(plan, work, work_ins, work_outs, *refs):
+def gather_kernel(plan, arrays, ending, work, work_ins, work_outs, *refs):
     count = len(plan)
-    own_ins, ins, refs = refs[:work_ins], refs[work_ins : work_ins + count], refs[work_ins + count :]
-    own_outs, outs = refs[:work_outs], refs[work_outs : work_outs + count]
-    sems, local_sem = refs[work_outs + count : -1], refs[-1]
+    own_ins, ins, refs = refs[:work_ins], refs[work_ins : work_ins + arrays], refs[work_ins + arrays :]
+    own_outs, outs = refs[:work_outs], refs[work_outs : work_outs + arrays]
+    sems, local_sem = refs[work_outs + arrays : -1], refs[-1]
     todo = work(own_ins, own_outs)
     rep, shard = lax.axis_index("rep"), lax.axis_index("shard")
     y, core = lax.div(rep, CORES), lax.rem(rep, CORES)
@@ -820,23 +811,25 @@
         return copy
 
     def part(m, at_z, at_x, at_y, at_core):
-        out, (layer, split_y, by_core) = outs[m], plan[m]
-        columns = slice(None)
+        which, _, split_y, by_core, row, rows, column, columns = plan[m]
+        out = outs[which]
+        at_columns = slice(None)
         if by_core:
-            half = out.shape[-1] // CORES
-            columns = pl.ds(pl.multiple_of(at_core * half, 128), half)
+            first = at_core * (out.shape[-1] // CORES) + column
+            at_columns = pl.ds(pl.multiple_of(first, 128), columns)
         at_z = slice(None) if at_z is None else at_z
         at_x = slice(None) if at_x is None else at_x
-        return out.at[at_z, at_x, at_y if split_y else 0, :, columns]
+        return out.at[at_z, at_x, at_y if split_y else 0, pl.ds(row, rows), at_columns]
 
     locals_ = []
-    for m, (layer, split_y, by_core) in enumerate(plan):
-        rows = outs[m].shape[3]
-        source = ins[m] if layer is None else ins[m].at[layer]
+    for m, (which, layer, split_y, by_core, row, rows, column, columns) in enumerate(plan):
+        source = ins[which] if layer is None else ins[which].at[layer]
         if by_core:
-            half = outs[m].shape[-1] // CORES
-            first = pl.multiple_of(y * rows, 16) if split_y else 0
-            source = source.at[pl.ds(first, rows), pl.ds(pl.multiple_of(core * half, 128), half)]
+            first = row
+            if split_y:
+                first = pl.multiple_of(y * outs[which].shape[3] + row, 16)
+            start = core * (outs[which].shape[-1] // CORES) + column
+            source = source.at[pl.ds(first, rows), pl.ds(pl.multiple_of(start, 128), columns)]
         copy = pltpu.make_async_copy(source, part(m, z, x, y, core), local_sem.at[m])
         copy.start()
         locals_.append(copy)
@@ -847,7 +840,7 @@
         piece = part(m, at_z, at_x, y, core)
         if at_x is x:
             along_x[m].append(send(piece, piece, m, 3 + len(along_x[m]), dx=1))
-        if plan[m][1]:
+        if plan[m][2]:
             over_y[m].append(send(piece, piece, m, 7 + len(over_y[m]), dy=1))
 
     def behind(k):
@@ -855,11 +848,11 @@
 
     def after_x(m):
         for k in range(CHIPS_Z):
-            if k % 2:
+            if k == 1:
                 next(todo, None)
             along_x[m][k].wait_recv()
             spread(m, behind(k), 1 - x)
-        if plan[m][2]:
+        if plan[m][3]:
             piece = part(m, None, None, y, core)
             last.append(send(piece, piece, m, 15, dc=1))
 
@@ -870,7 +863,7 @@
             piece = part(m, None, None, 1 - y, core)
             last.append(send(piece, piece, m, 16, dc=1))
 
-    order = sorted(range(count), key=lambda m: (not plan[m][1], -outs[m].shape[-1]))
+    order = range(count)
 
     def set_out(m):
         locals_[m].wait()
@@ -883,7 +876,8 @@
         set_out(m)
     for place, m in enumerate(order):
         for k in range(1, CHIPS_Z):
-            next(todo, None)
+            if k != 2:
+                next(todo, None)
             along_z[m][k - 1].wait_recv()
             spread(m, behind(k), x)
         if place + 2 < count:
@@ -891,6 +885,7 @@
         if place:
             after_x(order[place - 1])
     after_x(order[-1])
+    ending(own_outs, outs)
     for m in order:
         after_y(m)
         next(todo, None)
@@ -902,25 +897,56 @@
         copy.wait_send()
 
 
-def gather(weights, wanted, work, work_args, work_shapes, number):
+def no_ending(own_outs, outs):
+    pass
+
+
+def spread_vectors(sizes, own_outs, outs):
+    found = outs[0]
+    for shard in range(CHIPS_Z * CHIPS_X):
+        rows = found[shard // CHIPS_X, shard % CHIPS_X, 0].astype(jnp.float32)
+        at = 0
+        for out_ref, size in zip(own_outs[-len(sizes) :], sizes):
+            out_ref[:, shard * size : (shard + 1) * size] = rows[:LAYERS, at : at + size]
+            at += size
+
+
+def gather(weights, wanted, work, work_args, work_shapes, number, ending=no_ending):
     low = jnp.bfloat16
     args, plan, shapes = [], [], []
-    for which, layer, split_y in wanted:
-        args.append(weights[which])
-        plan.append((layer, split_y, layer is not None))
+    for which, layer, split_y, tall, wide in wanted:
         rows, columns = weights[which].shape[-2:]
         split = CHIPS_Y if split_y else 1
-        shapes.append((CHIPS_Z, CHIPS_X, split, rows // split, columns))
+        rows //= split
+        half = columns if layer is None else columns // CORES
+        for piece in range(tall * wide):
+            row, column = divmod(piece, wide)
+            plan.append(
+                (
+                    len(args),
+                    layer,
+                    split_y,
+                    layer is not None,
+                    row * (rows // tall),
+                    rows // tall,
+                    column * (half // wide),
+                    half // wide,
+                )
+            )
+        args.append(weights[which])
+        shapes.append((CHIPS_Z, CHIPS_X, split, rows, columns))
     whole = pl.BlockSpec(memory_space=pltpu.VMEM)
     small = pl.BlockSpec(memory_space=pltpu.SMEM)
     found = pl.pallas_call(
-        functools.partial(gather_kernel, plan, work, len(work_args), len(work_shapes)),
+        functools.partial(
+            gather_kernel, plan, len(args), ending, work, len(work_args), len(work_shapes)
+        ),
         in_specs=[small if arg.shape[-1] == SEGMENTS else whole for arg in work_args]
         + [pl.BlockSpec(memory_space=pl.ANY)] * len(args),
         out_specs=[whole] * (len(work_shapes) + len(args)),
         out_shape=work_shapes + [jax.ShapeDtypeStruct(shape, low) for shape in shapes],
-        scratch_shapes=[pltpu.SemaphoreType.DMA((2, 17))] * len(args)
-        + [pltpu.SemaphoreType.DMA((len(args),))],
+        scratch_shapes=[pltpu.SemaphoreType.DMA((2, 17))] * len(plan)
+        + [pltpu.SemaphoreType.DMA((len(plan),))],
         compiler_params=pltpu.CompilerParams(
             vmem_limit_bytes=KERNEL_VMEM, collective_id=number, has_side_effects=True
         ),
@@ -1245,9 +1271,10 @@
             ((0, 16 - LAYERS), (0, 0)),
         )
         trees = parent.shape[0]
-        slots, bias, found, qkv = gather(
+        sizes = [weights[number].shape[1] for number in VECTORS]
+        slots, bias, *vectors, _, qkv = gather(
             shards,
-            (("vectors", None, False), (0, 0, True)),
+            (("vectors", None, False, 1, 1), (0, 0, True, 1, 3)),
             prep_steps,
             (
                 parent,
@@ -1257,21 +1284,27 @@
             [
                 jax.ShapeDtypeStruct((trees, PAIRS, 2, TREE_LEN), jnp.int32),
                 jax.ShapeDtypeStruct((trees, HEADS, TREE_LEN, LANES), jnp.bfloat16),
+                *[
+                    jax.ShapeDtypeStruct((LAYERS, CHIPS_Z * CHIPS_X * size), jnp.float32)
+                    for size in sizes
+                ],
             ],
             1,
+            functools.partial(spread_vectors, sizes),
         )
-        vectors = spread_vectors(found, [weights[number].shape[1] for number in VECTORS])
         whole = {(0, 0): qkv}
 
         def attend_layer(layer, projected):
             last = layer + 1 == LAYERS
-            wanted = [(6, layer, True), (8, layer, not last), (2, layer, last)]
-            if not last:
-                wanted.insert(2, (0, layer + 1, False))
+            if last:
+                wanted = [(8, layer, False, 4, 1), (6, layer, True, 1, 2), (2, layer, True, 1, 1)]
+            else:
+                wanted = [(6, layer, True, 1, 2), (8, layer, True, 2, 1)]
+                wanted += [(0, layer + 1, False, 1, 3), (2, layer, False, 1, 1)]
             results = gather(
                 shards, wanted, attend_steps, (projected, slots, bias), attend_shapes(trees), 2 + layer
             )
-            for (number, at_layer, _), array in zip(wanted, results[4:]):
+            for (number, at_layer, *_), array in zip(wanted, results[4:]):
                 whole[at_layer, number] = array
             return results[:4]
 

time: 714 us -> 718 us (level)
  Pallas kernels: 665 us -> 685 us
  other arithmetic: 13.4 us -> 3.89 us
    pallas_call x3, Pallas kernels: 205 us -> 226 us  [gather(): pl.pallas_call(functools.partial(gather_kernel, plan, len(args), ending,...]
    convert_element_type x2 -> x0, other arithmetic: 9.48 us -> none  [spread_vectors(): found[:, :, at:at + size].reshape(LAYERS, -1).astype(jnp.float32)]
where the time goes in v11:
time: 718 us; the launch traced here: 708 us
  Pallas kernels  685 us (95%)
  local copies, waits for them, and re-layouts  16.4 us (2%)
    pallas_call x3, Pallas kernels, gather(): pl.pallas_call(functools.partial(gather_kernel, plan, len(args), ending,...  226 us
    pallas_call x3, Pallas kernels, reduce_sums(): pl.pallas_call(functools.partial(reduce_kernel, len(flats), len(pairs), l...  218 us
    pallas_call x16, Pallas kernels, product(): pl.pallas_call(functools.partial(weight_grad_kernel, split_y), grid_spec=...  104 us
    pallas_call x2, Pallas kernels, feed(): pl.pallas_call(functools.partial(feed_kernel, layer), grid=(count // ROW_...  56.2 us
    pallas_call x2, Pallas kernels, feed_back(): pl.pallas_call(functools.partial(feed_back_kernel, layer, proj is not Non...  50.8 us
    pallas_call x2, Pallas kernels, project(): pl.pallas_call(functools.partial(project_kernel, layer), grid=(count // R...  16 us
  transfers between devices with their start and end apart: 8, of which 0 were waited for; matrix products, arithmetic and copies ran while one was open for 0% of the time, Pallas kernels for 15%

profile of v11, /device:TPU:17, one launch (start us, length us, event | category | flops | bytes accessed | tf_op | source)
XLA Modules:
  0.0 708.1 jit_solution(3220106966681635324)
XLA Ops:
  0.7 1.5 transpose_reshape.3.refs_2_
  2.2 0.9 concatenate.3
  3.0 0.6 pad.4.refs_3_
  3.6 44.7 %shard_map.272 = (s32[1,6,2,1024]{3,2,1,0:T(2,128)}, bf16[1,12,1024,128]{3,2,1,0:T(8,128)(2,1)}, f32[2,1536]{1,0:T(2,128)}, f32[2,768]{1,0:T(2,128)}, f32[2,768]...) custom-call(s32[1,13]{1,0:T(1,128)} %refs_0_.2, ...), custom_call_target="tpu_custom_call" | custom-call | bytes 200000000 | tf_op jit(solution)/shard_map/pallas_call | solution.py:940
  48.4 7.8 %shard_map.273.refs_0_ = bf16[1024,2304]{1,0:T(8,128)(2,1)} custom-call(bf16[1024,768]{1,0:T(8,128)(2,1)} %left_ref.3, bf16[768,2304]{1,0:T(8,128)(2,1)} %bitcast.74, f32[2,1536]{1,0:T(2,128)} %get-tuple-element.108.bias_ref), custom_call_target="tpu_custom_call" | custom-call | flops 4348654592 | bytes 5111808 | tf_op jit(solution)/shard_map/pallas_call | solution.py:514
  56.2 87.4 %shard_map.274 = (bf16[1024,768]{1,0:T(8,128)(2,1)}, bf16[1,12,1024,128]{3,2,1,0:T(8,128)(2,1)}, bf16[1,12,1024,128]{3,2,1,0:T(8,128)(2,1)}, bf16[1,12,1024,128]...) custom-call(bf16[1024,2304]{1,0:T(8,128)(2,1)} %shard_map.273.refs_0, ...), custom_call_target="tpu_custom_call" | custom-call | bytes 200000000 | tf_op jit(solution)/shard_map/pallas_call | solution.py:940
  143.6 27.9 %shard_map.275 = (bf16[1024,768]{1,0:T(8,128)(2,1)}, bf16[1024,3072]{1,0:T(8,128)(2,1)}, bf16[1024,3072]{1,0:T(8,128)(2,1)}, f32[1024,768]{1,0:T(8,128)}, f32[10...) custom-call(bf16[1024,768]{1,0:T(8,128)(2,1)} %get-tuple-element.111, ...), custom_call_target="tpu_custom_call" | custom-call | flops 27179089920 | bytes 12189696 | tf_op jit(solution)/shard_map/pallas_call | solution.py:529
  171.5 8.2 %shard_map.276.refs_0_ = bf16[1024,2304]{1,0:T(8,128)(2,1)} custom-call(bf16[1024,768]{1,0:T(8,128)(2,1)} %get-tuple-element.122.rows_ref.left_ref, bf16[768,2304]{1,0:T(8,128)(2,1)} %bitcast.76, f32[2,1536]{1,0:T(2,128)} %get-tuple-element.108.bias_ref), custom_call_target="tpu_custom_call" | custom-call | flops 4348654592 | bytes 5111808 | tf_op jit(solution)/shard_map/pallas_call | solution.py:514
  179.7 93.4 %shard_map.277 = (bf16[1024,768]{1,0:T(8,128)(2,1)}, bf16[1,12,1024,128]{3,2,1,0:T(8,128)(2,1)}, bf16[1,12,1024,128]{3,2,1,0:T(8,128)(2,1)}, bf16[1,12,1024,128]...) custom-call(bf16[1024,2304]{1,0:T(8,128)(2,1)} %shard_map.276.refs_0, ...), custom_call_target="tpu_custom_call" | custom-call | bytes 200000000 | tf_op jit(solution)/shard_map/pallas_call | solution.py:940
  273.2 0.7 pad_add_fusion.at_ref
  273.8 28.4 %shard_map.278 = (bf16[1024,768]{1,0:T(8,128)(2,1)}, bf16[1024,3072]{1,0:T(8,128)(2,1)}, bf16[1024,3072]{1,0:T(8,128)(2,1)}, f32[1024,768]{1,0:T(8,128)}, f32[10...) custom-call(bf16[1024,768]{1,0:T(8,128)(2,1)} %get-tuple-element.124, ...), custom_call_target="tpu_custom_call" | custom-call | flops 27179089920 | bytes 12189696 | tf_op jit(solution)/shard_map/pallas_call | solution.py:529
  302.2 21.7 %shard_map.279 = (bf16[1024,768]{1,0:T(8,128)(2,1)}, bf16[1024,3072]{1,0:T(8,128)(2,1)}, f32[1024,768]{1,0:T(8,128)}, bf16[1024,768]{1,0:T(8,128)(2,1)}, bf16[10...) custom-call(bf16[1024,768]{1,0:T(8,128)(2,1)} %refs_0_.3, f32[1024,768]{1,0:T(8,128)} %get-tuple-element.130.refs_1_, ...), custom_call_target="tpu_custom_call" | custom-call | flops 27179089920 | bytes 12189696 | tf_op jit(solution)/shard_map/pallas_call | solution.py:570
  323.9 6.5 shard_map.284
  330.4 0.0 collective-permute-start.2
  330.4 7.9 %shard_map.281 = bf16[1,4,2,384,384]{4,3,2,1,0:T(8,128)(2,1)} custom-call(s32[4]{0:T(128)} %pad_add_fusion.at_ref, bf16[1024,3072]{1,0:T(8,128)(2,1)} %get-tuple-element.141.left_ref, bf16[1024,768]{1,0:T(8,128)(2,1)} %get-tuple-element.142.right_ref), custom_call_target="tpu_custom_call" | custom-call | flops 4831838208 | bytes 7864320 | tf_op jit(solution)/shard_map/pallas_call | solution.py:712
  338.3 0.5 collective-permute-start.1
  338.8 4.1 shard_map.280
  342.8 0.0 collective-permute-start
  342.9 0.0 collective-permute-done.2.refs_0_
  342.9 7.1 shard_map.285
  349.9 1.4 copy-done.6
  351.3 8.5 %shard_map.282 = (bf16[4,480,384]{2,1,0:T(8,128)(2,1)}, bf16[4,480,384]{2,1,0:T(8,128)(2,1)}) custom-call(s32[4]{0:T(128)} %pad_add_fusion.at_ref, bf16[1024,3072]{1,0:T(8,128)(2,1)} %get-tuple-element.141.left_ref, bf16[1024,768]{1,0:T(8,128)(2,1)} %get-tuple-element.142.right_ref, bf16[1,4,2,384,384]{4,3,2,1,0:T(8,128)(2,1)} %copy-done.6), custom_call_target="tpu_custom_call" | custom-call | flops 4831838208 | bytes 7864320 | tf_op jit(solution)/shard_map/pallas_call | solution.py:712
  359.9 0.0 copy-start.3
  359.9 0.8 copy-done.3
  360.7 4.3 shard_map.283
  365.0 78.5 %shard_map.286 = (bf16[3,1024,768]{2,1,0:T(8,128)(2,1)}, f32[1,6,8,128]{3,2,1,0:T(8,128)}, bf16[480,384]{1,0:T(8,128)(2,1)}, bf16[480,384]{1,0:T(8,128)(2,1)}, bf16[4,2,48,768]{3,2,1,0:T(8,128)(2,1)}) custom-call(s32[1,6,2,1024]{3,2,1,0:T(2,128)} %get-tuple-element.109.refs_1_.refs_0_, bf16[1024,768]{1,0:T(8,128)(2,1)} %get-tuple-element.136.refs_1_, ...), custom_call_target="tpu_custom_call" | custom-call | bytes 200000000 | tf_op jit(solution)/shard_map/pallas_call | solution.py:1196
  443.5 6.5 shard_map.294
  450.1 29.1 %shard_map.287 = (bf16[1024,768]{1,0:T(8,128)(2,1)}, bf16[1024,3072]{1,0:T(8,128)(2,1)}, f32[1024,768]{1,0:T(8,128)}, bf16[1024,768]{1,0:T(8,128)(2,1)}, bf16[10...) custom-call(f32[1024,768]{1,0:T(8,128)} %get-tuple-element.135.refs_0_, ...), custom_call_target="tpu_custom_call" | custom-call | flops 27179089920 | bytes 13762560 | tf_op jit(solution)/shard_map/pallas_call | solution.py:570
  479.2 6.5 shard_map.292
  485.7 0.5 collective-permute-start.5
  486.2 7.9 %shard_map.289 = bf16[1,4,2,384,384]{4,3,2,1,0:T(8,128)(2,1)} custom-call(s32[4]{0:T(128)} %pad_add_fusion.at_ref, bf16[1024,3072]{1,0:T(8,128)(2,1)} %get-tuple-element.162.left_ref, bf16[1024,768]{1,0:T(8,128)(2,1)} %get-tuple-element.163.right_ref), custom_call_target="tpu_custom_call" | custom-call | flops 4831838208 | bytes 7864320 | tf_op jit(solution)/shard_map/pallas_call | solution.py:712
  494.1 0.0 collective-permute-start.4
  494.1 4.1 shard_map.288
  498.2 0.5 collective-permute-start.3
  498.7 0.0 collective-permute-done.6.refs_0_
  498.7 7.0 shard_map.295
  505.7 7.0 shard_map.293
  512.7 1.4 copy-done.5
  514.1 8.6 %shard_map.290 = (bf16[4,480,384]{2,1,0:T(8,128)(2,1)}, bf16[4,480,384]{2,1,0:T(8,128)(2,1)}) custom-call(s32[4]{0:T(128)} %pad_add_fusion.at_ref, bf16[1024,3072]{1,0:T(8,128)(2,1)} %get-tuple-element.162.left_ref, bf16[1024,768]{1,0:T(8,128)(2,1)} %get-tuple-element.163.right_ref, bf16[1,4,2,384,384]{4,3,2,1,0:T(8,128)(2,1)} %copy-done.5), custom_call_target="tpu_custom_call" | custom-call | flops 4831838208 | bytes 7864320 | tf_op jit(solution)/shard_map/pallas_call | solution.py:712
  522.6 0.0 collective-permute-done.3.refs_0_
  522.6 0.0 copy-start.2
  522.7 0.8 copy-done.2
  523.5 4.3 shard_map.291
  527.8 90.6 %shard_map.296 = (bf16[3,1024,768]{2,1,0:T(8,128)(2,1)}, f32[1,6,8,128]{3,2,1,0:T(8,128)}, bf16[480,384]{1,0:T(8,128)(2,1)}, bf16[480,384]{1,0:T(8,128)(2,1)}, b...) custom-call(s32[1,6,2,1024]{3,2,1,0:T(2,128)} %get-tuple-element.109.refs_1_.refs_0_, ...), custom_call_target="tpu_custom_call" | custom-call | bytes 200000000 | tf_op jit(solution)/shard_map/pallas_call | solution.py:1196
  618.4 6.7 shard_map.297
  625.0 0.9 fusion.8
  625.9 0.8 fusion.10
  626.7 0.8 fusion.9
  627.5 8.8 %shard_map.299 = f32[1024,768]{1,0:T(8,128)} custom-call(f32[1024,768]{1,0:T(8,128)} %get-tuple-element.177.above_ref, bf16[3,1024,768]{2,1,0:T(8,128)(2,1)} %get-tuple-element.174.right_ref.proj_ref, bf16[768,2304]{1,0:T(8,128)(2,1)} %bitcast.75), custom_call_target="tpu_custom_call" | custom-call | flops 4348654592 | bytes 6684672 | tf_op jit(solution)/shard_map/pallas_call | solution.py:602
  636.3 0.0 collective-permute-done.7.refs_0_
  636.4 1.2 copy-done.7
  637.6 6.9 shard_map.298
  644.5 48.8 %shard_map.300 = (bf16[4,3,48,384]{3,2,1,0:T(8,128)(2,1)}, f32[40,768]{1,0:T(8,128)}) custom-call(bf16[3,4,2,48,384]{4,3,2,1,0:T(8,128)(2,1)} %get-tuple-element.179.refs_0_, bf16[3,4,2,48,384]{4,3,2,1,0:T(8,128)(2,1)} %get-tuple-element.180.refs_1_, f32[8,768]{1,0:T(8,128)} %get-tuple-element.181.refs_2_, f32[1,3072]{1,0:T(1,128)} %get-tuple-element.182.refs_3_, ...), custom_call_target="tpu_custom_call" | custom-call | bytes 200000000 | tf_op jit(solution)/shard_map/pallas_call | solution.py:1196
  693.3 1.1 fusion.12
  694.4 0.8 slice_bitcast_fusion
  695.2 0.8 slice.64
  696.0 0.8 slice.65
  696.8 1.8 fusion.11
  698.6 0.7 fusion
  699.3 0.7 fusion.1
  699.9 0.6 fusion.2
  700.6 0.6 fusion.4
  701.2 0.6 fusion.6
  701.9 6.1 shard_map.301
  (19 shorter events, 0.1 us)
Async XLA Ops:
  330.4 12.5 %collective-permute-start.2 = (bf16[2,4,2,96,768]{4,3,2,1,0:T(8,128)(2,1)}, bf16[2,4,2,96,768]{4,3,2,1,0:T(8,128)(2,1)}, u32[]{:S(2)}, u32[]{:S(2)}) collective-permute-start(bf16[2,4,2,96,768]{4,3,2,1,0:T(8,128)(2,1)} %shard_map.284), channel_id=1, source_target_pairs={{0,8},{1,9},{2,10},{3,11},{4,12},{5,13},{6,14},{7,15},{8,0},{9,1},... | collective-permute-start | bytes 7077896 | tf_op jit(solution)/shard_map/ppermute | solution.py:747
  338.3 11.7 %collective-permute-start.1 = (bf16[1,4,2,384,384]{4,3,2,1,0:T(8,128)(2,1)}, bf16[1,4,2,384,384]{4,3,2,1,0:T(8,128)(2,1)S(1)}, u32[]{:S(2)}, u32[]{:S(2)}) collective-permute-start(bf16[1,4,2,384,384]{4,3,2,1,0:T(8,128)(2,1)} %shard_map.281), channel_id=1, source_target_pairs={{0,8},{1,9},{2,10},{3,11},{4,12},{5,13},{6,14},{7,15},{8,0},{9,1},... | collective-permute-start | bytes 7077896 | tf_op jit(solution)/shard_map/ppermute | solution.py:747
  342.8 17.0 %collective-permute-start = (bf16[1,4,2,96,384]{4,3,2,1,0:T(8,128)(2,1)}, bf16[1,4,2,96,384]{4,3,2,1,0:T(8,128)(2,1)S(1)}, u32[]{:S(2)}, u32[]{:S(2)}) collective-permute-start(bf16[1,4,2,96,384]{4,3,2,1,0:T(8,128)(2,1)} %shard_map.280), channel_id=1, source_target_pairs={{0,8},{1,9},{2,10},{3,11},{4,12},{5,13},{6,14},{7,15},{8,0},{9,1},... | collective-permute-start | bytes 1769480 | tf_op jit(solution)/shard_map/ppermute | solution.py:747
  349.9 1.4 copy-start.6
  359.9 0.8 copy-start.3
  450.1 48.6 %collective-permute-start.6 = (bf16[3,4,2,96,384]{4,3,2,1,0:T(8,128)(2,1)}, bf16[3,4,2,96,384]{4,3,2,1,0:T(8,128)(2,1)}, u32[]{:S(2)}, u32[]{:S(2)}) collective-permute-start(bf16[3,4,2,96,384]{4,3,2,1,0:T(8,128)(2,1)} %shard_map.294), channel_id=1, source_target_pairs={{0,8},{1,9},{2,10},{3,11},{4,12},{5,13},{6,14},{7,15},{8,0},{9,1},... | collective-permute-start | bytes 5308424 | tf_op jit(solution)/shard_map/ppermute | solution.py:747
  485.7 20.0 %collective-permute-start.5 = (bf16[2,4,2,96,768]{4,3,2,1,0:T(8,128)(2,1)}, bf16[2,4,2,96,768]{4,3,2,1,0:T(8,128)(2,1)}, u32[]{:S(2)}, u32[]{:S(2)}) collective-permute-start(bf16[2,4,2,96,768]{4,3,2,1,0:T(8,128)(2,1)} %shard_map.292), channel_id=1, source_target_pairs={{0,8},{1,9},{2,10},{3,11},{4,12},{5,13},{6,14},{7,15},{8,0},{9,1},... | collective-permute-start | bytes 7077896 | tf_op jit(solution)/shard_map/ppermute | solution.py:747
  494.1 18.5 %collective-permute-start.4 = (bf16[1,4,2,384,384]{4,3,2,1,0:T(8,128)(2,1)}, bf16[1,4,2,384,384]{4,3,2,1,0:T(8,128)(2,1)S(1)}, u32[]{:S(2)}, u32[]{:S(2)}) collective-permute-start(bf16[1,4,2,384,384]{4,3,2,1,0:T(8,128)(2,1)} %shard_map.289), channel_id=1, source_target_pairs={{0,8},{1,9},{2,10},{3,11},{4,12},{5,13},{6,14},{7,15},{8,0},{9,1},... | collective-permute-start | bytes 7077896 | tf_op jit(solution)/shard_map/ppermute | solution.py:747
  498.2 24.4 %collective-permute-start.3 = (bf16[1,4,2,96,384]{4,3,2,1,0:T(8,128)(2,1)}, bf16[1,4,2,96,384]{4,3,2,1,0:T(8,128)(2,1)S(1)}, u32[]{:S(2)}, u32[]{:S(2)}) collective-permute-start(bf16[1,4,2,96,384]{4,3,2,1,0:T(8,128)(2,1)} %shard_map.288), channel_id=1, source_target_pairs={{0,8},{1,9},{2,10},{3,11},{4,12},{5,13},{6,14},{7,15},{8,0},{9,1},... | collective-permute-start | bytes 1769480 | tf_op jit(solution)/shard_map/ppermute | solution.py:747
  512.6 1.4 copy-start.5
  522.6 0.8 copy-start.2
  618.3 6.7 copy-start
  618.3 7.5 %copy-start.4 = (bf16[4,3,48,384]{3,2,1,0:T(8,128)(2,1)S(1)}, bf16[4,3,48,384]{3,2,1,0:T(8,128)(2,1)}, u32[]{:S(2)}) copy-start(bf16[4,3,48,384]{3,2,1,0:T(8,128)(2,1)} %get-tuple-element.188) | copy-start | bytes 1327108
  625.0 1.7 copy-start.1
  625.0 11.3 %collective-permute-start.7 = (bf16[3,4,2,96,384]{4,3,2,1,0:T(8,128)(2,1)}, bf16[3,4,2,96,384]{4,3,2,1,0:T(8,128)(2,1)S(1)}, u32[]{:S(2)}, u32[]{:S(2)}) collective-permute-start(bf16[3,4,2,96,384]{4,3,2,1,0:T(8,128)(2,1)} %shard_map.297), channel_id=1, source_target_pairs={{0,8},{1,9},{2,10},{3,11},{4,12},{5,13},{6,14},{7,15},{8,0},{9,1},... | collective-permute-start | bytes 5308424 | tf_op jit(solution)/shard_map/ppermute | solution.py:747
  636.4 1.2 copy-start.7

commit v12 on v11

--- a/solution.py
+++ b/solution.py
@@ -848,7 +848,7 @@
 
     def after_x(m):
         for k in range(CHIPS_Z):
-            if k == 1:
+            if k % 2:
                 next(todo, None)
             along_x[m][k].wait_recv()
             spread(m, behind(k), 1 - x)
@@ -876,8 +876,7 @@
         set_out(m)
     for place, m in enumerate(order):
         for k in range(1, CHIPS_Z):
-            if k != 2:
-                next(todo, None)
+            next(todo, None)
             along_z[m][k - 1].wait_recv()
             spread(m, behind(k), x)
         if place + 2 < count:
@@ -902,7 +901,7 @@
 
 
 def spread_vectors(sizes, own_outs, outs):
-    found = outs[0]
+    found = outs[-1]
     for shard in range(CHIPS_Z * CHIPS_X):
         rows = found[shard // CHIPS_X, shard % CHIPS_X, 0].astype(jnp.float32)
         at = 0
@@ -1272,9 +1271,9 @@
         )
         trees = parent.shape[0]
         sizes = [weights[number].shape[1] for number in VECTORS]
-        slots, bias, *vectors, _, qkv = gather(
+        slots, bias, *vectors, qkv, _ = gather(
             shards,
-            (("vectors", None, False, 1, 1), (0, 0, True, 1, 3)),
+            ((0, 0, True, 1, 1), ("vectors", None, False, 1, 1)),
             prep_steps,
             (
                 parent,
@@ -1297,10 +1296,10 @@
         def attend_layer(layer, projected):
             last = layer + 1 == LAYERS
             if last:
-                wanted = [(8, layer, False, 4, 1), (6, layer, True, 1, 2), (2, layer, True, 1, 1)]
+                wanted = [(6, layer, True, 1, 1), (2, layer, True, 1, 1), (8, layer, False, 1, 1)]
             else:
-                wanted = [(6, layer, True, 1, 2), (8, layer, True, 2, 1)]
-                wanted += [(0, layer + 1, False, 1, 3), (2, layer, False, 1, 1)]
+                wanted = [(6, layer, True, 1, 1), (8, layer, True, 1, 1)]
+                wanted += [(0, layer + 1, False, 1, 1), (2, layer, False, 1, 1)]
             results = gather(
                 shards, wanted, attend_steps, (projected, slots, bias), attend_shapes(trees), 2 + layer
             )

time: 718 us -> 707 us (0.985)
  Pallas kernels: 685 us -> 674 us
    pallas_call x3, Pallas kernels: 226 us -> 214 us  [gather(): pl.pallas_call(functools.partial(gather_kernel, plan, len(args), ending,...]
where the time goes in v12:
time: 707 us; the launch traced here: 697 us
  Pallas kernels  674 us (95%)
  local copies, waits for them, and re-layouts  16.4 us (2%)
    pallas_call x3, Pallas kernels, reduce_sums(): pl.pallas_call(functools.partial(reduce_kernel, len(flats), len(pairs), l...  218 us
    pallas_call x3, Pallas kernels, gather(): pl.pallas_call(functools.partial(gather_kernel, plan, len(args), ending,...  214 us
    pallas_call x16, Pallas kernels, product(): pl.pallas_call(functools.partial(weight_grad_kernel, split_y), grid_spec=...  104 us
    pallas_call x2, Pallas kernels, feed(): pl.pallas_call(functools.partial(feed_kernel, layer), grid=(count // ROW_...  56.2 us
    pallas_call x2, Pallas kernels, feed_back(): pl.pallas_call(functools.partial(feed_back_kernel, layer, proj is not Non...  50.8 us
    pallas_call x2, Pallas kernels, project(): pl.pallas_call(functools.partial(project_kernel, layer), grid=(count // R...  16 us
  transfers between devices with their start and end apart: 8, of which 0 were waited for; matrix products, arithmetic and copies ran while one was open for 0% of the time, Pallas kernels for 15%

profile of v12, /device:TPU:17, one launch (start us, length us, event | category | flops | bytes accessed | tf_op | source)
XLA Modules:
  0.0 697.1 jit_solution(4017418519615240691)
XLA Ops:
  0.7 1.5 transpose_reshape.3.refs_2_
  2.2 0.9 concatenate.3
  3.0 0.6 pad.4.refs_4_
  3.6 49.6 %shard_map.272 = (s32[1,6,2,1024]{3,2,1,0:T(2,128)}, bf16[1,12,1024,128]{3,2,1,0:T(8,128)(2,1)}, f32[2,1536]{1,0:T(2,128)}, f32[2,768]{1,0:T(2,128)}, f32[2,768]...) custom-call(s32[1,13]{1,0:T(1,128)} %refs_0_.2, ...), custom_call_target="tpu_custom_call" | custom-call | bytes 200000000 | tf_op jit(solution)/shard_map/pallas_call | solution.py:939
  53.2 7.8 %shard_map.273.refs_0_ = bf16[1024,2304]{1,0:T(8,128)(2,1)} custom-call(bf16[1024,768]{1,0:T(8,128)(2,1)} %left_ref.3, bf16[768,2304]{1,0:T(8,128)(2,1)} %bitcast.74, f32[2,1536]{1,0:T(2,128)} %get-tuple-element.108.bias_ref), custom_call_target="tpu_custom_call" | custom-call | flops 4348654592 | bytes 5111808 | tf_op jit(solution)/shard_map/pallas_call | solution.py:514
  61.0 88.0 %shard_map.274 = (bf16[1024,768]{1,0:T(8,128)(2,1)}, bf16[1,12,1024,128]{3,2,1,0:T(8,128)(2,1)}, bf16[1,12,1024,128]{3,2,1,0:T(8,128)(2,1)}, bf16[1,12,1024,128]...) custom-call(bf16[1024,2304]{1,0:T(8,128)(2,1)} %shard_map.273.refs_0, ...), custom_call_target="tpu_custom_call" | custom-call | bytes 200000000 | tf_op jit(solution)/shard_map/pallas_call | solution.py:939
  149.0 27.9 %shard_map.275 = (bf16[1024,768]{1,0:T(8,128)(2,1)}, bf16[1024,3072]{1,0:T(8,128)(2,1)}, bf16[1024,3072]{1,0:T(8,128)(2,1)}, f32[1024,768]{1,0:T(8,128)}, f32[10...) custom-call(bf16[1024,768]{1,0:T(8,128)(2,1)} %get-tuple-element.111, ...), custom_call_target="tpu_custom_call" | custom-call | flops 27179089920 | bytes 12189696 | tf_op jit(solution)/shard_map/pallas_call | solution.py:529
  176.9 8.2 %shard_map.276.refs_0_ = bf16[1024,2304]{1,0:T(8,128)(2,1)} custom-call(bf16[1024,768]{1,0:T(8,128)(2,1)} %get-tuple-element.122.rows_ref.left_ref, bf16[768,2304]{1,0:T(8,128)(2,1)} %bitcast.76, f32[2,1536]{1,0:T(2,128)} %get-tuple-element.108.bias_ref), custom_call_target="tpu_custom_call" | custom-call | flops 4348654592 | bytes 5111808 | tf_op jit(solution)/shard_map/pallas_call | solution.py:514
  185.1 76.6 %shard_map.277 = (bf16[1024,768]{1,0:T(8,128)(2,1)}, bf16[1,12,1024,128]{3,2,1,0:T(8,128)(2,1)}, bf16[1,12,1024,128]{3,2,1,0:T(8,128)(2,1)}, bf16[1,12,1024,128]...) custom-call(bf16[1024,2304]{1,0:T(8,128)(2,1)} %shard_map.276.refs_0, ...), custom_call_target="tpu_custom_call" | custom-call | bytes 200000000 | tf_op jit(solution)/shard_map/pallas_call | solution.py:939
  261.8 0.7 pad_add_fusion.at_ref
  262.4 28.4 %shard_map.278 = (bf16[1024,768]{1,0:T(8,128)(2,1)}, bf16[1024,3072]{1,0:T(8,128)(2,1)}, bf16[1024,3072]{1,0:T(8,128)(2,1)}, f32[1024,768]{1,0:T(8,128)}, f32[10...) custom-call(bf16[1024,768]{1,0:T(8,128)(2,1)} %get-tuple-element.124, ...), custom_call_target="tpu_custom_call" | custom-call | flops 27179089920 | bytes 12189696 | tf_op jit(solution)/shard_map/pallas_call | solution.py:529
  290.8 21.7 %shard_map.279 = (bf16[1024,768]{1,0:T(8,128)(2,1)}, bf16[1024,3072]{1,0:T(8,128)(2,1)}, f32[1024,768]{1,0:T(8,128)}, bf16[1024,768]{1,0:T(8,128)(2,1)}, bf16[10...) custom-call(bf16[1024,768]{1,0:T(8,128)(2,1)} %refs_0_.3, f32[1024,768]{1,0:T(8,128)} %get-tuple-element.130.refs_1_, ...), custom_call_target="tpu_custom_call" | custom-call | flops 27179089920 | bytes 12189696 | tf_op jit(solution)/shard_map/pallas_call | solution.py:570
  312.5 6.5 shard_map.284
  319.0 0.1 collective-permute-start.2
  319.0 7.9 %shard_map.281 = bf16[1,4,2,384,384]{4,3,2,1,0:T(8,128)(2,1)} custom-call(s32[4]{0:T(128)} %pad_add_fusion.at_ref, bf16[1024,3072]{1,0:T(8,128)(2,1)} %get-tuple-element.141.left_ref, bf16[1024,768]{1,0:T(8,128)(2,1)} %get-tuple-element.142.right_ref), custom_call_target="tpu_custom_call" | custom-call | flops 4831838208 | bytes 7864320 | tf_op jit(solution)/shard_map/pallas_call | solution.py:712
  326.9 0.4 collective-permute-start.1
  327.4 4.1 shard_map.280
  331.5 0.1 collective-permute-start
  331.5 0.0 collective-permute-done.2.refs_0_
  331.5 7.1 %shard_map.285 = (bf16[2,4,2,48,768]{4,3,2,1,0:T(8,128)(2,1)}, bf16[2,4,2,48,768]{4,3,2,1,0:T(8,128)(2,1)}) custom-call(s32[4]{0:T(128)} %pad_add_fusion.at_ref, bf16[1024,768]{1,0:T(8,128)(2,1)} %get-tuple-element.147.left_ref, bf16[1024,3072]{1,0:T(8,128)(2,1)} %get-tuple-element.148.right_ref, bf16[2,4,2,96,768]{4,3,2,1,0:T(8,128)(2,1)} %collective-permute-done.2.refs_0_), custom_call_target="tpu_custom_call" | custom-call | flops 4831838208 | bytes 7864320 | tf_op jit(solution)/shard_map/pallas_call | solution.py:712
  338.6 0.0 collective-permute-done.1.refs_0_
  338.6 1.4 copy-done.6
  340.0 8.5 %shard_map.282 = (bf16[4,480,384]{2,1,0:T(8,128)(2,1)}, bf16[4,480,384]{2,1,0:T(8,128)(2,1)}) custom-call(s32[4]{0:T(128)} %pad_add_fusion.at_ref, bf16[1024,3072]{1,0:T(8,128)(2,1)} %get-tuple-element.141.left_ref, bf16[1024,768]{1,0:T(8,128)(2,1)} %get-tuple-element.142.right_ref, bf16[1,4,2,384,384]{4,3,2,1,0:T(8,128)(2,1)} %copy-done.6), custom_call_target="tpu_custom_call" | custom-call | flops 4831838208 | bytes 7864320 | tf_op jit(solution)/shard_map/pallas_call | solution.py:712
  348.5 0.0 copy-start.3
  348.6 0.8 copy-done.3
  349.4 4.3 shard_map.283
  353.7 79.2 %shard_map.286 = (bf16[3,1024,768]{2,1,0:T(8,128)(2,1)}, f32[1,6,8,128]{3,2,1,0:T(8,128)}, bf16[480,384]{1,0:T(8,128)(2,1)}, bf16[480,384]{1,0:T(8,128)(2,1)}, bf16[4,2,48,768]{3,2,1,0:T(8,128)(2,1)}) custom-call(s32[1,6,2,1024]{3,2,1,0:T(2,128)} %get-tuple-element.109.refs_1_.refs_0_, bf16[1024,768]{1,0:T(8,128)(2,1)} %get-tuple-element.136.refs_1_, ...), custom_call_target="tpu_custom_call" | custom-call | bytes 200000000 | tf_op jit(solution)/shard_map/pallas_call | solution.py:1195
  432.9 6.5 shard_map.294
  439.5 0.0 collective-permute-start.6
  439.5 29.1 %shard_map.287 = (bf16[1024,768]{1,0:T(8,128)(2,1)}, bf16[1024,3072]{1,0:T(8,128)(2,1)}, f32[1024,768]{1,0:T(8,128)}, bf16[1024,768]{1,0:T(8,128)(2,1)}, bf16[10...) custom-call(f32[1024,768]{1,0:T(8,128)} %get-tuple-element.135.refs_0_, ...), custom_call_target="tpu_custom_call" | custom-call | flops 27179089920 | bytes 13762560 | tf_op jit(solution)/shard_map/pallas_call | solution.py:570
  468.6 6.5 shard_map.292
  475.1 0.5 collective-permute-start.5
  475.6 7.9 %shard_map.289 = bf16[1,4,2,384,384]{4,3,2,1,0:T(8,128)(2,1)} custom-call(s32[4]{0:T(128)} %pad_add_fusion.at_ref, bf16[1024,3072]{1,0:T(8,128)(2,1)} %get-tuple-element.162.left_ref, bf16[1024,768]{1,0:T(8,128)(2,1)} %get-tuple-element.163.right_ref), custom_call_target="tpu_custom_call" | custom-call | flops 4831838208 | bytes 7864320 | tf_op jit(solution)/shard_map/pallas_call | solution.py:712
  483.5 0.0 collective-permute-start.4
  483.5 4.1 shard_map.288
  487.6 0.5 collective-permute-start.3
  488.1 7.0 shard_map.295
  495.1 0.0 collective-permute-done.5.refs_0_
  495.1 7.0 shard_map.293
  502.0 1.4 copy-done.5
  503.4 8.6 %shard_map.290 = (bf16[4,480,384]{2,1,0:T(8,128)(2,1)}, bf16[4,480,384]{2,1,0:T(8,128)(2,1)}) custom-call(s32[4]{0:T(128)} %pad_add_fusion.at_ref, bf16[1024,3072]{1,0:T(8,128)(2,1)} %get-tuple-element.162.left_ref, bf16[1024,768]{1,0:T(8,128)(2,1)} %get-tuple-element.163.right_ref, bf16[1,4,2,384,384]{4,3,2,1,0:T(8,128)(2,1)} %copy-done.5), custom_call_target="tpu_custom_call" | custom-call | flops 4831838208 | bytes 7864320 | tf_op jit(solution)/shard_map/pallas_call | solution.py:712
  512.0 0.0 copy-start.2
  512.0 0.8 copy-done.2
  512.8 4.3 shard_map.291
  517.1 90.5 %shard_map.296 = (bf16[3,1024,768]{2,1,0:T(8,128)(2,1)}, f32[1,6,8,128]{3,2,1,0:T(8,128)}, bf16[480,384]{1,0:T(8,128)(2,1)}, bf16[480,384]{1,0:T(8,128)(2,1)}, b...) custom-call(s32[1,6,2,1024]{3,2,1,0:T(2,128)} %get-tuple-element.109.refs_1_.refs_0_, ...), custom_call_target="tpu_custom_call" | custom-call | bytes 200000000 | tf_op jit(solution)/shard_map/pallas_call | solution.py:1195
  607.7 6.7 shard_map.297
  614.4 0.9 fusion.8
  615.2 0.8 fusion.10
  616.0 0.8 fusion.9
  616.9 8.8 %shard_map.299 = f32[1024,768]{1,0:T(8,128)} custom-call(f32[1024,768]{1,0:T(8,128)} %get-tuple-element.177.above_ref, bf16[3,1024,768]{2,1,0:T(8,128)(2,1)} %get-tuple-element.174.right_ref.proj_ref, bf16[768,2304]{1,0:T(8,128)(2,1)} %bitcast.75), custom_call_target="tpu_custom_call" | custom-call | flops 4348654592 | bytes 6684672 | tf_op jit(solution)/shard_map/pallas_call | solution.py:602
  625.7 1.2 copy-done.7
  626.9 6.9 shard_map.298
  633.8 48.4 %shard_map.300 = (bf16[4,3,48,384]{3,2,1,0:T(8,128)(2,1)}, f32[40,768]{1,0:T(8,128)}) custom-call(bf16[3,4,2,48,384]{4,3,2,1,0:T(8,128)(2,1)} %get-tuple-element.179.refs_0_, bf16[3,4,2,48,384]{4,3,2,1,0:T(8,128)(2,1)} %get-tuple-element.180.refs_1_, f32[8,768]{1,0:T(8,128)} %get-tuple-element.181.refs_2_, f32[1,3072]{1,0:T(1,128)} %get-tuple-element.182.refs_3_, ...), custom_call_target="tpu_custom_call" | custom-call | bytes 200000000 | tf_op jit(solution)/shard_map/pallas_call | solution.py:1195
  682.2 1.1 fusion.12
  683.4 0.8 slice_bitcast_fusion
  684.2 0.8 slice.64
  684.9 0.8 slice.65
  685.8 1.8 fusion.11
  687.6 0.7 fusion
  688.2 0.7 fusion.1
  688.9 0.6 fusion.2
  689.5 0.6 fusion.4
  690.2 0.6 fusion.6
  690.8 6.1 shard_map.301
  (19 shorter events, 0.1 us)
Async XLA Ops:
  319.0 12.6 %collective-permute-start.2 = (bf16[2,4,2,96,768]{4,3,2,1,0:T(8,128)(2,1)}, bf16[2,4,2,96,768]{4,3,2,1,0:T(8,128)(2,1)}, u32[]{:S(2)}, u32[]{:S(2)}) collective-permute-start(bf16[2,4,2,96,768]{4,3,2,1,0:T(8,128)(2,1)} %shard_map.284), channel_id=1, source_target_pairs={{0,8},{1,9},{2,10},{3,11},{4,12},{5,13},{6,14},{7,15},{8,0},{9,1},... | collective-permute-start | bytes 7077896 | tf_op jit(solution)/shard_map/ppermute | solution.py:747
  326.9 11.7 %collective-permute-start.1 = (bf16[1,4,2,384,384]{4,3,2,1,0:T(8,128)(2,1)}, bf16[1,4,2,384,384]{4,3,2,1,0:T(8,128)(2,1)S(1)}, u32[]{:S(2)}, u32[]{:S(2)}) collective-permute-start(bf16[1,4,2,384,384]{4,3,2,1,0:T(8,128)(2,1)} %shard_map.281), channel_id=1, source_target_pairs={{0,8},{1,9},{2,10},{3,11},{4,12},{5,13},{6,14},{7,15},{8,0},{9,1},... | collective-permute-start | bytes 7077896 | tf_op jit(solution)/shard_map/ppermute | solution.py:747
  331.5 17.1 %collective-permute-start = (bf16[1,4,2,96,384]{4,3,2,1,0:T(8,128)(2,1)}, bf16[1,4,2,96,384]{4,3,2,1,0:T(8,128)(2,1)S(1)}, u32[]{:S(2)}, u32[]{:S(2)}) collective-permute-start(bf16[1,4,2,96,384]{4,3,2,1,0:T(8,128)(2,1)} %shard_map.280), channel_id=1, source_target_pairs={{0,8},{1,9},{2,10},{3,11},{4,12},{5,13},{6,14},{7,15},{8,0},{9,1},... | collective-permute-start | bytes 1769480 | tf_op jit(solution)/shard_map/ppermute | solution.py:747
  338.6 1.4 copy-start.6
  348.5 0.8 copy-start.3
  439.5 48.6 %collective-permute-start.6 = (bf16[3,4,2,96,384]{4,3,2,1,0:T(8,128)(2,1)}, bf16[3,4,2,96,384]{4,3,2,1,0:T(8,128)(2,1)}, u32[]{:S(2)}, u32[]{:S(2)}) collective-permute-start(bf16[3,4,2,96,384]{4,3,2,1,0:T(8,128)(2,1)} %shard_map.294), channel_id=1, source_target_pairs={{0,8},{1,9},{2,10},{3,11},{4,12},{5,13},{6,14},{7,15},{8,0},{9,1},... | collective-permute-start | bytes 5308424 | tf_op jit(solution)/shard_map/ppermute | solution.py:747
  475.1 20.0 %collective-permute-start.5 = (bf16[2,4,2,96,768]{4,3,2,1,0:T(8,128)(2,1)}, bf16[2,4,2,96,768]{4,3,2,1,0:T(8,128)(2,1)}, u32[]{:S(2)}, u32[]{:S(2)}) collective-permute-start(bf16[2,4,2,96,768]{4,3,2,1,0:T(8,128)(2,1)} %shard_map.292), channel_id=1, source_target_pairs={{0,8},{1,9},{2,10},{3,11},{4,12},{5,13},{6,14},{7,15},{8,0},{9,1},... | collective-permute-start | bytes 7077896 | tf_op jit(solution)/shard_map/ppermute | solution.py:747
  483.5 18.5 %collective-permute-start.4 = (bf16[1,4,2,384,384]{4,3,2,1,0:T(8,128)(2,1)}, bf16[1,4,2,384,384]{4,3,2,1,0:T(8,128)(2,1)S(1)}, u32[]{:S(2)}, u32[]{:S(2)}) collective-permute-start(bf16[1,4,2,384,384]{4,3,2,1,0:T(8,128)(2,1)} %shard_map.289), channel_id=1, source_target_pairs={{0,8},{1,9},{2,10},{3,11},{4,12},{5,13},{6,14},{7,15},{8,0},{9,1},... | collective-permute-start | bytes 7077896 | tf_op jit(solution)/shard_map/ppermute | solution.py:747
  487.6 24.4 %collective-permute-start.3 = (bf16[1,4,2,96,384]{4,3,2,1,0:T(8,128)(2,1)}, bf16[1,4,2,96,384]{4,3,2,1,0:T(8,128)(2,1)S(1)}, u32[]{:S(2)}, u32[]{:S(2)}) collective-permute-start(bf16[1,4,2,96,384]{4,3,2,1,0:T(8,128)(2,1)} %shard_map.288), channel_id=1, source_target_pairs={{0,8},{1,9},{2,10},{3,11},{4,12},{5,13},{6,14},{7,15},{8,0},{9,1},... | collective-permute-start | bytes 1769480 | tf_op jit(solution)/shard_map/ppermute | solution.py:747
  502.0 1.4 copy-start.5
  512.0 0.8 copy-start.2
  607.7 6.7 copy-start
  607.7 7.5 %copy-start.4 = (bf16[4,3,48,384]{3,2,1,0:T(8,128)(2,1)S(1)}, bf16[4,3,48,384]{3,2,1,0:T(8,128)(2,1)}, u32[]{:S(2)}) copy-start(bf16[4,3,48,384]{3,2,1,0:T(8,128)(2,1)} %get-tuple-element.188) | copy-start | bytes 1327108
  614.4 1.7 copy-start.1
  614.4 11.3 %collective-permute-start.7 = (bf16[3,4,2,96,384]{4,3,2,1,0:T(8,128)(2,1)}, bf16[3,4,2,96,384]{4,3,2,1,0:T(8,128)(2,1)S(1)}, u32[]{:S(2)}, u32[]{:S(2)}) collective-permute-start(bf16[3,4,2,96,384]{4,3,2,1,0:T(8,128)(2,1)} %shard_map.297), channel_id=1, source_target_pairs={{0,8},{1,9},{2,10},{3,11},{4,12},{5,13},{6,14},{7,15},{8,0},{9,1},... | collective-permute-start | bytes 5308424 | tf_op jit(solution)/shard_map/ppermute | solution.py:747
  625.7 1.2 copy-start.7

commit v13 on v12

--- a/solution.py
+++ b/solution.py
@@ -852,7 +852,9 @@
                 next(todo, None)
             along_x[m][k].wait_recv()
             spread(m, behind(k), 1 - x)
-        if plan[m][3]:
+        if not plan[m][3]:
+            ending(own_outs, outs)
+        else:
             piece = part(m, None, None, y, core)
             last.append(send(piece, piece, m, 15, dc=1))
 
@@ -884,7 +886,6 @@
         if place:
             after_x(order[place - 1])
     after_x(order[-1])
-    ending(own_outs, outs)
     for m in order:
         after_y(m)
         next(todo, None)
@@ -901,7 +902,7 @@
 
 
 def spread_vectors(sizes, own_outs, outs):
-    found = outs[-1]
+    found = outs[0]
     for shard in range(CHIPS_Z * CHIPS_X):
         rows = found[shard // CHIPS_X, shard % CHIPS_X, 0].astype(jnp.float32)
         at = 0
@@ -1271,9 +1272,9 @@
         )
         trees = parent.shape[0]
         sizes = [weights[number].shape[1] for number in VECTORS]
-        slots, bias, *vectors, qkv, _ = gather(
+        slots, bias, *vectors, _, qkv = gather(
             shards,
-            ((0, 0, True, 1, 1), ("vectors", None, False, 1, 1)),
+            (("vectors", None, False, 1, 1), (0, 0, True, 1, 1)),
             prep_steps,
             (
                 parent,

time: 707 us -> 709 us (level)
  no operation moved by 1% of the time
where the time goes in v13:
time: 709 us; the launch traced here: 699 us
  Pallas kernels  675 us (95%)
  local copies, waits for them, and re-layouts  16.4 us (2%)
    pallas_call x3, Pallas kernels, reduce_sums(): pl.pallas_call(functools.partial(reduce_kernel, len(flats), len(pairs), l...  219 us
    pallas_call x3, Pallas kernels, gather(): pl.pallas_call(functools.partial(gather_kernel, plan, len(args), ending,...  214 us
    pallas_call x16, Pallas kernels, product(): pl.pallas_call(functools.partial(weight_grad_kernel, split_y), grid_spec=...  104 us
    pallas_call x2, Pallas kernels, feed(): pl.pallas_call(functools.partial(feed_kernel, layer), grid=(count // ROW_...  56.2 us
    pallas_call x2, Pallas kernels, feed_back(): pl.pallas_call(functools.partial(feed_back_kernel, layer, proj is not Non...  50.8 us
    pallas_call x2, Pallas kernels, project(): pl.pallas_call(functools.partial(project_kernel, layer), grid=(count // R...  16 us
  transfers between devices with their start and end apart: 8, of which 0 were waited for; matrix products, arithmetic and copies ran while one was open for 0% of the time, Pallas kernels for 15%

profile of v13, /device:TPU:17, one launch (start us, length us, event | category | flops | bytes accessed | tf_op | source)
XLA Modules:
  0.0 699.1 jit_solution(3376341794808788389)
XLA Ops:
  0.7 1.5 transpose_reshape.3.refs_2_
  2.2 0.9 concatenate.3
  3.0 0.6 pad.4.refs_3_
  3.6 50.4 %shard_map.272 = (s32[1,6,2,1024]{3,2,1,0:T(2,128)}, bf16[1,12,1024,128]{3,2,1,0:T(8,128)(2,1)}, f32[2,1536]{1,0:T(2,128)}, f32[2,768]{1,0:T(2,128)}, f32[2,768]...) custom-call(s32[1,13]{1,0:T(1,128)} %refs_0_.2, ...), custom_call_target="tpu_custom_call" | custom-call | bytes 200000000 | tf_op jit(solution)/shard_map/pallas_call | solution.py:940
  54.0 7.8 %shard_map.273.refs_0_ = bf16[1024,2304]{1,0:T(8,128)(2,1)} custom-call(bf16[1024,768]{1,0:T(8,128)(2,1)} %left_ref.3, bf16[768,2304]{1,0:T(8,128)(2,1)} %bitcast.74, f32[2,1536]{1,0:T(2,128)} %get-tuple-element.108.bias_ref), custom_call_target="tpu_custom_call" | custom-call | flops 4348654592 | bytes 5111808 | tf_op jit(solution)/shard_map/pallas_call | solution.py:514
  61.8 84.8 %shard_map.274 = (bf16[1024,768]{1,0:T(8,128)(2,1)}, bf16[1,12,1024,128]{3,2,1,0:T(8,128)(2,1)}, bf16[1,12,1024,128]{3,2,1,0:T(8,128)(2,1)}, bf16[1,12,1024,128]...) custom-call(bf16[1024,2304]{1,0:T(8,128)(2,1)} %shard_map.273.refs_0, ...), custom_call_target="tpu_custom_call" | custom-call | bytes 200000000 | tf_op jit(solution)/shard_map/pallas_call | solution.py:940
  146.6 27.9 %shard_map.275 = (bf16[1024,768]{1,0:T(8,128)(2,1)}, bf16[1024,3072]{1,0:T(8,128)(2,1)}, bf16[1024,3072]{1,0:T(8,128)(2,1)}, f32[1024,768]{1,0:T(8,128)}, f32[10...) custom-call(bf16[1024,768]{1,0:T(8,128)(2,1)} %get-tuple-element.111, ...), custom_call_target="tpu_custom_call" | custom-call | flops 27179089920 | bytes 12189696 | tf_op jit(solution)/shard_map/pallas_call | solution.py:529
  174.5 8.2 %shard_map.276.refs_0_ = bf16[1024,2304]{1,0:T(8,128)(2,1)} custom-call(bf16[1024,768]{1,0:T(8,128)(2,1)} %get-tuple-element.122.rows_ref.left_ref, bf16[768,2304]{1,0:T(8,128)(2,1)} %bitcast.76, f32[2,1536]{1,0:T(2,128)} %get-tuple-element.108.bias_ref), custom_call_target="tpu_custom_call" | custom-call | flops 4348654592 | bytes 5111808 | tf_op jit(solution)/shard_map/pallas_call | solution.py:514
  182.7 79.2 %shard_map.277 = (bf16[1024,768]{1,0:T(8,128)(2,1)}, bf16[1,12,1024,128]{3,2,1,0:T(8,128)(2,1)}, bf16[1,12,1024,128]{3,2,1,0:T(8,128)(2,1)}, bf16[1,12,1024,128]...) custom-call(bf16[1024,2304]{1,0:T(8,128)(2,1)} %shard_map.276.refs_0, ...), custom_call_target="tpu_custom_call" | custom-call | bytes 200000000 | tf_op jit(solution)/shard_map/pallas_call | solution.py:940
  261.9 0.7 pad_add_fusion.at_ref
  262.6 28.4 %shard_map.278 = (bf16[1024,768]{1,0:T(8,128)(2,1)}, bf16[1024,3072]{1,0:T(8,128)(2,1)}, bf16[1024,3072]{1,0:T(8,128)(2,1)}, f32[1024,768]{1,0:T(8,128)}, f32[10...) custom-call(bf16[1024,768]{1,0:T(8,128)(2,1)} %get-tuple-element.124, ...), custom_call_target="tpu_custom_call" | custom-call | flops 27179089920 | bytes 12189696 | tf_op jit(solution)/shard_map/pallas_call | solution.py:529
  291.0 21.7 %shard_map.279 = (bf16[1024,768]{1,0:T(8,128)(2,1)}, bf16[1024,3072]{1,0:T(8,128)(2,1)}, f32[1024,768]{1,0:T(8,128)}, bf16[1024,768]{1,0:T(8,128)(2,1)}, bf16[10...) custom-call(bf16[1024,768]{1,0:T(8,128)(2,1)} %refs_0_.3, f32[1024,768]{1,0:T(8,128)} %get-tuple-element.130.refs_1_, ...), custom_call_target="tpu_custom_call" | custom-call | flops 27179089920 | bytes 12189696 | tf_op jit(solution)/shard_map/pallas_call | solution.py:570
  312.7 6.5 shard_map.284
  319.1 0.1 collective-permute-start.2
  319.2 7.9 %shard_map.281 = bf16[1,4,2,384,384]{4,3,2,1,0:T(8,128)(2,1)} custom-call(s32[4]{0:T(128)} %pad_add_fusion.at_ref, bf16[1024,3072]{1,0:T(8,128)(2,1)} %get-tuple-element.141.left_ref, bf16[1024,768]{1,0:T(8,128)(2,1)} %get-tuple-element.142.right_ref), custom_call_target="tpu_custom_call" | custom-call | flops 4831838208 | bytes 7864320 | tf_op jit(solution)/shard_map/pallas_call | solution.py:712
  327.1 0.4 collective-permute-start.1
  327.6 4.1 shard_map.280
  331.6 0.1 collective-permute-start
  331.7 0.0 collective-permute-done.2.refs_0_
  331.7 7.1 %shard_map.285 = (bf16[2,4,2,48,768]{4,3,2,1,0:T(8,128)(2,1)}, bf16[2,4,2,48,768]{4,3,2,1,0:T(8,128)(2,1)}) custom-call(s32[4]{0:T(128)} %pad_add_fusion.at_ref, bf16[1024,768]{1,0:T(8,128)(2,1)} %get-tuple-element.147.left_ref, bf16[1024,3072]{1,0:T(8,128)(2,1)} %get-tuple-element.148.right_ref, bf16[2,4,2,96,768]{4,3,2,1,0:T(8,128)(2,1)} %collective-permute-done.2.refs_0_), custom_call_target="tpu_custom_call" | custom-call | flops 4831838208 | bytes 7864320 | tf_op jit(solution)/shard_map/pallas_call | solution.py:712
  338.8 0.0 collective-permute-done.1.refs_0_
  338.8 1.4 copy-done.6
  340.2 8.5 %shard_map.282 = (bf16[4,480,384]{2,1,0:T(8,128)(2,1)}, bf16[4,480,384]{2,1,0:T(8,128)(2,1)}) custom-call(s32[4]{0:T(128)} %pad_add_fusion.at_ref, bf16[1024,3072]{1,0:T(8,128)(2,1)} %get-tuple-element.141.left_ref, bf16[1024,768]{1,0:T(8,128)(2,1)} %get-tuple-element.142.right_ref, bf16[1,4,2,384,384]{4,3,2,1,0:T(8,128)(2,1)} %copy-done.6), custom_call_target="tpu_custom_call" | custom-call | flops 4831838208 | bytes 7864320 | tf_op jit(solution)/shard_map/pallas_call | solution.py:712
  348.7 0.0 collective-permute-done.refs_0_
  348.7 0.0 copy-start.3
  348.7 0.8 copy-done.3
  349.5 4.3 shard_map.283
  353.8 79.1 %shard_map.286 = (bf16[3,1024,768]{2,1,0:T(8,128)(2,1)}, f32[1,6,8,128]{3,2,1,0:T(8,128)}, bf16[480,384]{1,0:T(8,128)(2,1)}, bf16[480,384]{1,0:T(8,128)(2,1)}, bf16[4,2,48,768]{3,2,1,0:T(8,128)(2,1)}) custom-call(s32[1,6,2,1024]{3,2,1,0:T(2,128)} %get-tuple-element.109.refs_1_.refs_0_, bf16[1024,768]{1,0:T(8,128)(2,1)} %get-tuple-element.136.refs_1_, ...), custom_call_target="tpu_custom_call" | custom-call | bytes 200000000 | tf_op jit(solution)/shard_map/pallas_call | solution.py:1196
  432.9 6.5 shard_map.294
  439.4 1.2 collective-permute-start.6
  440.7 29.1 %shard_map.287 = (bf16[1024,768]{1,0:T(8,128)(2,1)}, bf16[1024,3072]{1,0:T(8,128)(2,1)}, f32[1024,768]{1,0:T(8,128)}, bf16[1024,768]{1,0:T(8,128)(2,1)}, bf16[10...) custom-call(f32[1024,768]{1,0:T(8,128)} %get-tuple-element.135.refs_0_, ...), custom_call_target="tpu_custom_call" | custom-call | flops 27179089920 | bytes 13762560 | tf_op jit(solution)/shard_map/pallas_call | solution.py:570
  469.8 6.5 shard_map.292
  476.3 0.0 collective-permute-start.5
  476.3 7.9 %shard_map.289 = bf16[1,4,2,384,384]{4,3,2,1,0:T(8,128)(2,1)} custom-call(s32[4]{0:T(128)} %pad_add_fusion.at_ref, bf16[1024,3072]{1,0:T(8,128)(2,1)} %get-tuple-element.162.left_ref, bf16[1024,768]{1,0:T(8,128)(2,1)} %get-tuple-element.163.right_ref), custom_call_target="tpu_custom_call" | custom-call | flops 4831838208 | bytes 7864320 | tf_op jit(solution)/shard_map/pallas_call | solution.py:712
  484.2 0.5 collective-permute-start.4
  484.7 4.1 shard_map.288
  488.8 0.0 collective-permute-start.3
  488.8 7.0 shard_map.295
  495.8 7.0 shard_map.293
  502.8 1.4 copy-done.5
  504.1 8.6 %shard_map.290 = (bf16[4,480,384]{2,1,0:T(8,128)(2,1)}, bf16[4,480,384]{2,1,0:T(8,128)(2,1)}) custom-call(s32[4]{0:T(128)} %pad_add_fusion.at_ref, bf16[1024,3072]{1,0:T(8,128)(2,1)} %get-tuple-element.162.left_ref, bf16[1024,768]{1,0:T(8,128)(2,1)} %get-tuple-element.163.right_ref, bf16[1,4,2,384,384]{4,3,2,1,0:T(8,128)(2,1)} %copy-done.5), custom_call_target="tpu_custom_call" | custom-call | flops 4831838208 | bytes 7864320 | tf_op jit(solution)/shard_map/pallas_call | solution.py:712
  512.7 0.0 copy-start.2
  512.8 0.8 copy-done.2
  513.6 4.3 shard_map.291
  517.9 91.4 %shard_map.296 = (bf16[3,1024,768]{2,1,0:T(8,128)(2,1)}, f32[1,6,8,128]{3,2,1,0:T(8,128)}, bf16[480,384]{1,0:T(8,128)(2,1)}, bf16[480,384]{1,0:T(8,128)(2,1)}, b...) custom-call(s32[1,6,2,1024]{3,2,1,0:T(2,128)} %get-tuple-element.109.refs_1_.refs_0_, ...), custom_call_target="tpu_custom_call" | custom-call | bytes 200000000 | tf_op jit(solution)/shard_map/pallas_call | solution.py:1196
  609.3 6.7 shard_map.297
  616.0 0.9 fusion.8
  616.8 0.8 fusion.10
  617.6 0.8 fusion.9
  618.5 8.8 %shard_map.299 = f32[1024,768]{1,0:T(8,128)} custom-call(f32[1024,768]{1,0:T(8,128)} %get-tuple-element.177.above_ref, bf16[3,1024,768]{2,1,0:T(8,128)(2,1)} %get-tuple-element.174.right_ref.proj_ref, bf16[768,2304]{1,0:T(8,128)(2,1)} %bitcast.75), custom_call_target="tpu_custom_call" | custom-call | flops 4348654592 | bytes 6684672 | tf_op jit(solution)/shard_map/pallas_call | solution.py:602
  627.3 1.2 copy-done.7
  628.5 6.9 shard_map.298
  635.4 48.8 %shard_map.300 = (bf16[4,3,48,384]{3,2,1,0:T(8,128)(2,1)}, f32[40,768]{1,0:T(8,128)}) custom-call(bf16[3,4,2,48,384]{4,3,2,1,0:T(8,128)(2,1)} %get-tuple-element.179.refs_0_, bf16[3,4,2,48,384]{4,3,2,1,0:T(8,128)(2,1)} %get-tuple-element.180.refs_1_, f32[8,768]{1,0:T(8,128)} %get-tuple-element.181.refs_2_, f32[1,3072]{1,0:T(1,128)} %get-tuple-element.182.refs_3_, ...), custom_call_target="tpu_custom_call" | custom-call | bytes 200000000 | tf_op jit(solution)/shard_map/pallas_call | solution.py:1196
  684.2 1.1 fusion.12
  685.3 0.8 slice_bitcast_fusion
  686.1 0.8 slice.64
  686.9 0.8 slice.65
  687.7 1.8 fusion.11
  689.5 0.7 fusion
  690.2 0.7 fusion.1
  690.9 0.6 fusion.2
  691.5 0.6 fusion.4
  692.1 0.6 fusion.6
  692.8 6.1 shard_map.301
  (19 shorter events, 0.1 us)
Async XLA Ops:
  319.1 12.6 %collective-permute-start.2 = (bf16[2,4,2,96,768]{4,3,2,1,0:T(8,128)(2,1)}, bf16[2,4,2,96,768]{4,3,2,1,0:T(8,128)(2,1)}, u32[]{:S(2)}, u32[]{:S(2)}) collective-permute-start(bf16[2,4,2,96,768]{4,3,2,1,0:T(8,128)(2,1)} %shard_map.284), channel_id=1, source_target_pairs={{0,8},{1,9},{2,10},{3,11},{4,12},{5,13},{6,14},{7,15},{8,0},{9,1},... | collective-permute-start | bytes 7077896 | tf_op jit(solution)/shard_map/ppermute | solution.py:747
  327.1 11.7 %collective-permute-start.1 = (bf16[1,4,2,384,384]{4,3,2,1,0:T(8,128)(2,1)}, bf16[1,4,2,384,384]{4,3,2,1,0:T(8,128)(2,1)S(1)}, u32[]{:S(2)}, u32[]{:S(2)}) collective-permute-start(bf16[1,4,2,384,384]{4,3,2,1,0:T(8,128)(2,1)} %shard_map.281), channel_id=1, source_target_pairs={{0,8},{1,9},{2,10},{3,11},{4,12},{5,13},{6,14},{7,15},{8,0},{9,1},... | collective-permute-start | bytes 7077896 | tf_op jit(solution)/shard_map/ppermute | solution.py:747
  331.6 17.1 %collective-permute-start = (bf16[1,4,2,96,384]{4,3,2,1,0:T(8,128)(2,1)}, bf16[1,4,2,96,384]{4,3,2,1,0:T(8,128)(2,1)S(1)}, u32[]{:S(2)}, u32[]{:S(2)}) collective-permute-start(bf16[1,4,2,96,384]{4,3,2,1,0:T(8,128)(2,1)} %shard_map.280), channel_id=1, source_target_pairs={{0,8},{1,9},{2,10},{3,11},{4,12},{5,13},{6,14},{7,15},{8,0},{9,1},... | collective-permute-start | bytes 1769480 | tf_op jit(solution)/shard_map/ppermute | solution.py:747
  338.8 1.4 copy-start.6
  348.7 0.8 copy-start.3
  439.4 49.4 %collective-permute-start.6 = (bf16[3,4,2,96,384]{4,3,2,1,0:T(8,128)(2,1)}, bf16[3,4,2,96,384]{4,3,2,1,0:T(8,128)(2,1)}, u32[]{:S(2)}, u32[]{:S(2)}) collective-permute-start(bf16[3,4,2,96,384]{4,3,2,1,0:T(8,128)(2,1)} %shard_map.294), channel_id=1, source_target_pairs={{0,8},{1,9},{2,10},{3,11},{4,12},{5,13},{6,14},{7,15},{8,0},{9,1},... | collective-permute-start | bytes 5308424 | tf_op jit(solution)/shard_map/ppermute | solution.py:747
  476.3 19.5 %collective-permute-start.5 = (bf16[2,4,2,96,768]{4,3,2,1,0:T(8,128)(2,1)}, bf16[2,4,2,96,768]{4,3,2,1,0:T(8,128)(2,1)}, u32[]{:S(2)}, u32[]{:S(2)}) collective-permute-start(bf16[2,4,2,96,768]{4,3,2,1,0:T(8,128)(2,1)} %shard_map.292), channel_id=1, source_target_pairs={{0,8},{1,9},{2,10},{3,11},{4,12},{5,13},{6,14},{7,15},{8,0},{9,1},... | collective-permute-start | bytes 7077896 | tf_op jit(solution)/shard_map/ppermute | solution.py:747
  484.2 18.5 %collective-permute-start.4 = (bf16[1,4,2,384,384]{4,3,2,1,0:T(8,128)(2,1)}, bf16[1,4,2,384,384]{4,3,2,1,0:T(8,128)(2,1)S(1)}, u32[]{:S(2)}, u32[]{:S(2)}) collective-permute-start(bf16[1,4,2,384,384]{4,3,2,1,0:T(8,128)(2,1)} %shard_map.289), channel_id=1, source_target_pairs={{0,8},{1,9},{2,10},{3,11},{4,12},{5,13},{6,14},{7,15},{8,0},{9,1},... | collective-permute-start | bytes 7077896 | tf_op jit(solution)/shard_map/ppermute | solution.py:747
  488.8 23.9 %collective-permute-start.3 = (bf16[1,4,2,96,384]{4,3,2,1,0:T(8,128)(2,1)}, bf16[1,4,2,96,384]{4,3,2,1,0:T(8,128)(2,1)S(1)}, u32[]{:S(2)}, u32[]{:S(2)}) collective-permute-start(bf16[1,4,2,96,384]{4,3,2,1,0:T(8,128)(2,1)} %shard_map.288), channel_id=1, source_target_pairs={{0,8},{1,9},{2,10},{3,11},{4,12},{5,13},{6,14},{7,15},{8,0},{9,1},... | collective-permute-start | bytes 1769480 | tf_op jit(solution)/shard_map/ppermute | solution.py:747
  502.7 1.4 copy-start.5
  512.7 0.8 copy-start.2
  609.3 6.7 copy-start
  609.3 7.5 %copy-start.4 = (bf16[4,3,48,384]{3,2,1,0:T(8,128)(2,1)S(1)}, bf16[4,3,48,384]{3,2,1,0:T(8,128)(2,1)}, u32[]{:S(2)}) copy-start(bf16[4,3,48,384]{3,2,1,0:T(8,128)(2,1)} %get-tuple-element.188) | copy-start | bytes 1327108
  616.0 1.7 copy-start.1
  616.0 11.3 %collective-permute-start.7 = (bf16[3,4,2,96,384]{4,3,2,1,0:T(8,128)(2,1)}, bf16[3,4,2,96,384]{4,3,2,1,0:T(8,128)(2,1)S(1)}, u32[]{:S(2)}, u32[]{:S(2)}) collective-permute-start(bf16[3,4,2,96,384]{4,3,2,1,0:T(8,128)(2,1)} %shard_map.297), channel_id=1, source_target_pairs={{0,8},{1,9},{2,10},{3,11},{4,12},{5,13},{6,14},{7,15},{8,0},{9,1},... | collective-permute-start | bytes 5308424 | tf_op jit(solution)/shard_map/ppermute | solution.py:747
  627.3 1.2 copy-start.7

commit v14 on v13

--- a/solution.py
+++ b/solution.py
@@ -901,14 +901,18 @@
     pass
 
 
-def spread_vectors(sizes, own_outs, outs):
-    found = outs[0]
+def spread_vectors(found, at, sizes, out_refs):
     for shard in range(CHIPS_Z * CHIPS_X):
         rows = found[shard // CHIPS_X, shard % CHIPS_X, 0].astype(jnp.float32)
-        at = 0
-        for out_ref, size in zip(own_outs[-len(sizes) :], sizes):
-            out_ref[:, shard * size : (shard + 1) * size] = rows[:LAYERS, at : at + size]
-            at += size
+        first = at
+        for out_ref, size in zip(out_refs, sizes):
+            out_ref[:, shard * size : (shard + 1) * size] = rows[:LAYERS, first : first + size]
+            first += size
+
+
+def attend_and_spread(sizes, ins, outs):
+    yield from attend_steps(ins[:3], outs[:4])
+    spread_vectors(ins[3], sizes[0], sizes[1:], outs[4:])
 
 
 def gather(weights, wanted, work, work_args, work_shapes, number, ending=no_ending):
@@ -1272,7 +1276,7 @@
         )
         trees = parent.shape[0]
         sizes = [weights[number].shape[1] for number in VECTORS]
-        slots, bias, *vectors, _, qkv = gather(
+        slots, bias, *vectors, found, qkv = gather(
             shards,
             (("vectors", None, False, 1, 1), (0, 0, True, 1, 1)),
             prep_steps,
@@ -1286,11 +1290,11 @@
                 jax.ShapeDtypeStruct((trees, HEADS, TREE_LEN, LANES), jnp.bfloat16),
                 *[
                     jax.ShapeDtypeStruct((LAYERS, CHIPS_Z * CHIPS_X * size), jnp.float32)
-                    for size in sizes
+                    for size in sizes[:1]
                 ],
             ],
             1,
-            functools.partial(spread_vectors, sizes),
+            lambda own_outs, outs: spread_vectors(outs[0], 0, sizes[:1], own_outs[2:]),
         )
         whole = {(0, 0): qkv}
 
@@ -1301,10 +1305,17 @@
             else:
                 wanted = [(6, layer, True, 1, 1), (8, layer, True, 1, 1)]
                 wanted += [(0, layer + 1, False, 1, 1), (2, layer, False, 1, 1)]
-            results = gather(
-                shards, wanted, attend_steps, (projected, slots, bias), attend_shapes(trees), 2 + layer
-            )
-            for (number, at_layer, *_), array in zip(wanted, results[4:]):
+            work, args, results_of = attend_steps, (projected, slots, bias), attend_shapes(trees)
+            if layer == 0:
+                work, args = functools.partial(attend_and_spread, sizes), (*args, found)
+                results_of += [
+                    jax.ShapeDtypeStruct((LAYERS, CHIPS_Z * CHIPS_X * size), jnp.float32)
+                    for size in sizes[1:]
+                ]
+            results = gather(shards, wanted, work, args, results_of, 2 + layer)
+            if layer == 0:
+                vector.update(zip(VECTORS[1:], results[4:]))
+            for (number, at_layer, *_), array in zip(wanted, results[len(results_of) :]):
                 whole[at_layer, number] = array
             return results[:4]
 

time: 709 us -> 709 us (level)
    pallas_call x3, Pallas kernels: 214 us -> 205 us  [gather(): pl.pallas_call(functools.partial(gather_kernel, plan, len(args), ending,...]
    pallas_call x2, Pallas kernels: 16 us -> 25.4 us  [project(): pl.pallas_call(functools.partial(project_kernel, layer), grid=(count // R...]
where the time goes in v14:
time: 709 us; the launch traced here: 699 us
  Pallas kernels  675 us (95%)
  local copies, waits for them, and re-layouts  16.4 us (2%)
    pallas_call x3, Pallas kernels, reduce_sums(): pl.pallas_call(functools.partial(reduce_kernel, len(flats), len(pairs), l...  219 us
    pallas_call x3, Pallas kernels, gather(): pl.pallas_call(functools.partial(gather_kernel, plan, len(args), ending,...  205 us
    pallas_call x16, Pallas kernels, product(): pl.pallas_call(functools.partial(weight_grad_kernel, split_y), grid_spec=...  104 us
    pallas_call x2, Pallas kernels, feed(): pl.pallas_call(functools.partial(feed_kernel, layer), grid=(count // ROW_...  56.2 us
    pallas_call x2, Pallas kernels, feed_back(): pl.pallas_call(functools.partial(feed_back_kernel, layer, proj is not Non...  50.8 us
    pallas_call x2, Pallas kernels, project(): pl.pallas_call(functools.partial(project_kernel, layer), grid=(count // R...  25.4 us
  transfers between devices with their start and end apart: 8, of which 0 were waited for; matrix products, arithmetic and copies ran while one was open for 0% of the time, Pallas kernels for 15%

profile of v14, /device:TPU:17, one launch (start us, length us, event | category | flops | bytes accessed | tf_op | source)
XLA Modules:
  0.0 699.1 jit_solution(3614140758590760843)
XLA Ops:
  0.7 1.5 transpose_reshape.3.refs_2_
  2.2 0.9 concatenate.3
  3.0 0.6 pad.4.refs_3_
  3.6 40.9 %shard_map.272 = (s32[1,6,2,1024]{3,2,1,0:T(2,128)}, bf16[1,12,1024,128]{3,2,1,0:T(8,128)(2,1)}, f32[2,1536]{1,0:T(2,128)}, bf16[4,2,1,16,1152]{4,3,2,1,0:T(8,128)(2,1)}, bf16[4,2,2,48,2304]{4,3,2,1,0:T(8,128)(2,1)}) custom-call(s32[1,13]{1,0:T(1,128)} %refs_0_.2, s32[1,1,1024]{2,1,0:T(1,128)} %bitcast.65, s32[1,6,2,1024]{3,2,1,0:T(2,128)} %transpose_reshape.3.refs_2_, ...), custom_call_target="tpu_custom_call" | custom-call | bytes 200000000 | tf_op jit(solution)/shard_map/pallas_call | solution.py:944
  44.6 17.1 %shard_map.273.refs_0_ = bf16[1024,2304]{1,0:T(8,128)(2,1)} custom-call(bf16[1024,768]{1,0:T(8,128)(2,1)} %left_ref.3, bf16[768,2304]{1,0:T(8,128)(2,1)} %bitcast.74, f32[2,1536]{1,0:T(2,128)} %get-tuple-element.109.bias_ref), custom_call_target="tpu_custom_call" | custom-call | flops 4348654592 | bytes 5111808 | tf_op jit(solution)/shard_map/pallas_call | solution.py:514
  61.7 84.8 %shard_map.274 = (bf16[1024,768]{1,0:T(8,128)(2,1)}, bf16[1,12,1024,128]{3,2,1,0:T(8,128)(2,1)}, bf16[1,12,1024,128]{3,2,1,0:T(8,128)(2,1)}, bf16[1,12,1024,128]...) custom-call(bf16[1024,2304]{1,0:T(8,128)(2,1)} %shard_map.273.refs_0, ...), custom_call_target="tpu_custom_call" | custom-call | bytes 200000000 | tf_op jit(solution)/shard_map/pallas_call | solution.py:944
  146.6 27.9 %shard_map.275 = (bf16[1024,768]{1,0:T(8,128)(2,1)}, bf16[1024,3072]{1,0:T(8,128)(2,1)}, bf16[1024,3072]{1,0:T(8,128)(2,1)}, f32[1024,768]{1,0:T(8,128)}, f32[10...) custom-call(bf16[1024,768]{1,0:T(8,128)(2,1)} %get-tuple-element.113, ...), custom_call_target="tpu_custom_call" | custom-call | flops 27179089920 | bytes 12189696 | tf_op jit(solution)/shard_map/pallas_call | solution.py:529
  174.5 8.2 %shard_map.276.refs_0_ = bf16[1024,2304]{1,0:T(8,128)(2,1)} custom-call(bf16[1024,768]{1,0:T(8,128)(2,1)} %get-tuple-element.124.rows_ref.left_ref, bf16[768,2304]{1,0:T(8,128)(2,1)} %bitcast.76, f32[2,1536]{1,0:T(2,128)} %get-tuple-element.109.bias_ref), custom_call_target="tpu_custom_call" | custom-call | flops 4348654592 | bytes 5111808 | tf_op jit(solution)/shard_map/pallas_call | solution.py:514
  182.7 79.2 %shard_map.277 = (bf16[1024,768]{1,0:T(8,128)(2,1)}, bf16[1,12,1024,128]{3,2,1,0:T(8,128)(2,1)}, bf16[1,12,1024,128]{3,2,1,0:T(8,128)(2,1)}, bf16[1,12,1024,128]...) custom-call(bf16[1024,2304]{1,0:T(8,128)(2,1)} %shard_map.276.refs_0, ...), custom_call_target="tpu_custom_call" | custom-call | bytes 200000000 | tf_op jit(solution)/shard_map/pallas_call | solution.py:944
  261.9 0.7 pad_add_fusion.at_ref
  262.6 28.4 %shard_map.278 = (bf16[1024,768]{1,0:T(8,128)(2,1)}, bf16[1024,3072]{1,0:T(8,128)(2,1)}, bf16[1024,3072]{1,0:T(8,128)(2,1)}, f32[1024,768]{1,0:T(8,128)}, f32[10...) custom-call(bf16[1024,768]{1,0:T(8,128)(2,1)} %get-tuple-element.126, ...), custom_call_target="tpu_custom_call" | custom-call | flops 27179089920 | bytes 12189696 | tf_op jit(solution)/shard_map/pallas_call | solution.py:529
  290.9 21.7 %shard_map.279 = (bf16[1024,768]{1,0:T(8,128)(2,1)}, bf16[1024,3072]{1,0:T(8,128)(2,1)}, f32[1024,768]{1,0:T(8,128)}, bf16[1024,768]{1,0:T(8,128)(2,1)}, bf16[10...) custom-call(bf16[1024,768]{1,0:T(8,128)(2,1)} %refs_0_.3, f32[1024,768]{1,0:T(8,128)} %get-tuple-element.132.refs_1_, ...), custom_call_target="tpu_custom_call" | custom-call | flops 27179089920 | bytes 12189696 | tf_op jit(solution)/shard_map/pallas_call | solution.py:570
  312.6 6.5 shard_map.284
  319.1 0.1 collective-permute-start.2
  319.2 7.9 %shard_map.281 = bf16[1,4,2,384,384]{4,3,2,1,0:T(8,128)(2,1)} custom-call(s32[4]{0:T(128)} %pad_add_fusion.at_ref, bf16[1024,3072]{1,0:T(8,128)(2,1)} %get-tuple-element.143.left_ref, bf16[1024,768]{1,0:T(8,128)(2,1)} %get-tuple-element.144.right_ref), custom_call_target="tpu_custom_call" | custom-call | flops 4831838208 | bytes 7864320 | tf_op jit(solution)/shard_map/pallas_call | solution.py:712
  327.1 0.4 collective-permute-start.1
  327.5 4.1 shard_map.280
  331.6 0.1 collective-permute-start
  331.7 0.0 collective-permute-done.2.refs_0_
  331.7 7.1 %shard_map.285 = (bf16[2,4,2,48,768]{4,3,2,1,0:T(8,128)(2,1)}, bf16[2,4,2,48,768]{4,3,2,1,0:T(8,128)(2,1)}) custom-call(s32[4]{0:T(128)} %pad_add_fusion.at_ref, bf16[1024,768]{1,0:T(8,128)(2,1)} %get-tuple-element.149.left_ref, bf16[1024,3072]{1,0:T(8,128)(2,1)} %get-tuple-element.150.right_ref, bf16[2,4,2,96,768]{4,3,2,1,0:T(8,128)(2,1)} %collective-permute-done.2.refs_0_), custom_call_target="tpu_custom_call" | custom-call | flops 4831838208 | bytes 7864320 | tf_op jit(solution)/shard_map/pallas_call | solution.py:712
  338.8 1.4 copy-done.6
  340.2 8.5 %shard_map.282 = (bf16[4,480,384]{2,1,0:T(8,128)(2,1)}, bf16[4,480,384]{2,1,0:T(8,128)(2,1)}) custom-call(s32[4]{0:T(128)} %pad_add_fusion.at_ref, bf16[1024,3072]{1,0:T(8,128)(2,1)} %get-tuple-element.143.left_ref, bf16[1024,768]{1,0:T(8,128)(2,1)} %get-tuple-element.144.right_ref, bf16[1,4,2,384,384]{4,3,2,1,0:T(8,128)(2,1)} %copy-done.6), custom_call_target="tpu_custom_call" | custom-call | flops 4831838208 | bytes 7864320 | tf_op jit(solution)/shard_map/pallas_call | solution.py:712
  348.7 0.0 copy-start.3
  348.7 0.8 copy-done.3
  349.5 4.3 shard_map.283
  353.8 79.1 %shard_map.286 = (bf16[3,1024,768]{2,1,0:T(8,128)(2,1)}, f32[1,6,8,128]{3,2,1,0:T(8,128)}, bf16[480,384]{1,0:T(8,128)(2,1)}, bf16[480,384]{1,0:T(8,128)(2,1)}, bf16[4,2,48,768]{3,2,1,0:T(8,128)(2,1)}) custom-call(s32[1,6,2,1024]{3,2,1,0:T(2,128)} %get-tuple-element.110.refs_1_.refs_0_, bf16[1024,768]{1,0:T(8,128)(2,1)} %get-tuple-element.138.refs_1_, ...), custom_call_target="tpu_custom_call" | custom-call | bytes 200000000 | tf_op jit(solution)/shard_map/pallas_call | solution.py:1200
  432.9 6.5 shard_map.294
  439.4 1.2 collective-permute-start.6
  440.7 29.1 %shard_map.287 = (bf16[1024,768]{1,0:T(8,128)(2,1)}, bf16[1024,3072]{1,0:T(8,128)(2,1)}, f32[1024,768]{1,0:T(8,128)}, bf16[1024,768]{1,0:T(8,128)(2,1)}, bf16[10...) custom-call(f32[1024,768]{1,0:T(8,128)} %get-tuple-element.137.refs_0_, ...), custom_call_target="tpu_custom_call" | custom-call | flops 27179089920 | bytes 13762560 | tf_op jit(solution)/shard_map/pallas_call | solution.py:570
  469.8 6.5 shard_map.292
  476.3 0.0 collective-permute-start.5
  476.3 7.9 %shard_map.289 = bf16[1,4,2,384,384]{4,3,2,1,0:T(8,128)(2,1)} custom-call(s32[4]{0:T(128)} %pad_add_fusion.at_ref, bf16[1024,3072]{1,0:T(8,128)(2,1)} %get-tuple-element.164.left_ref, bf16[1024,768]{1,0:T(8,128)(2,1)} %get-tuple-element.165.right_ref), custom_call_target="tpu_custom_call" | custom-call | flops 4831838208 | bytes 7864320 | tf_op jit(solution)/shard_map/pallas_call | solution.py:712
  484.2 0.5 collective-permute-start.4
  484.7 4.1 shard_map.288
  488.8 0.0 collective-permute-start.3
  488.8 0.0 collective-permute-done.6.refs_0_
  488.8 7.0 shard_map.295
  495.8 0.0 collective-permute-done.5.refs_0_
  495.8 7.0 shard_map.293
  502.7 1.4 copy-done.5
  504.1 8.6 %shard_map.290 = (bf16[4,480,384]{2,1,0:T(8,128)(2,1)}, bf16[4,480,384]{2,1,0:T(8,128)(2,1)}) custom-call(s32[4]{0:T(128)} %pad_add_fusion.at_ref, bf16[1024,3072]{1,0:T(8,128)(2,1)} %get-tuple-element.164.left_ref, bf16[1024,768]{1,0:T(8,128)(2,1)} %get-tuple-element.165.right_ref, bf16[1,4,2,384,384]{4,3,2,1,0:T(8,128)(2,1)} %copy-done.5), custom_call_target="tpu_custom_call" | custom-call | flops 4831838208 | bytes 7864320 | tf_op jit(solution)/shard_map/pallas_call | solution.py:712
  512.7 0.0 copy-start.2
  512.7 0.8 copy-done.2
  513.5 4.3 shard_map.291
  517.8 91.4 %shard_map.296 = (bf16[3,1024,768]{2,1,0:T(8,128)(2,1)}, f32[1,6,8,128]{3,2,1,0:T(8,128)}, bf16[480,384]{1,0:T(8,128)(2,1)}, bf16[480,384]{1,0:T(8,128)(2,1)}, b...) custom-call(s32[1,6,2,1024]{3,2,1,0:T(2,128)} %get-tuple-element.110.refs_1_.refs_0_, ...), custom_call_target="tpu_custom_call" | custom-call | bytes 200000000 | tf_op jit(solution)/shard_map/pallas_call | solution.py:1200
  609.3 6.7 shard_map.297
  615.9 0.9 fusion.8
  616.8 0.8 fusion.10
  617.6 0.8 fusion.9
  618.4 8.8 %shard_map.299 = f32[1024,768]{1,0:T(8,128)} custom-call(f32[1024,768]{1,0:T(8,128)} %get-tuple-element.179.above_ref, bf16[3,1024,768]{2,1,0:T(8,128)(2,1)} %get-tuple-element.176.right_ref.proj_ref, bf16[768,2304]{1,0:T(8,128)(2,1)} %bitcast.75), custom_call_target="tpu_custom_call" | custom-call | flops 4348654592 | bytes 6684672 | tf_op jit(solution)/shard_map/pallas_call | solution.py:602
  627.3 1.2 copy-done.7
  628.5 6.9 shard_map.298
  635.4 48.8 %shard_map.300 = (bf16[4,3,48,384]{3,2,1,0:T(8,128)(2,1)}, f32[40,768]{1,0:T(8,128)}) custom-call(bf16[3,4,2,48,384]{4,3,2,1,0:T(8,128)(2,1)} %get-tuple-element.181.refs_0_, bf16[3,4,2,48,384]{4,3,2,1,0:T(8,128)(2,1)} %get-tuple-element.182.refs_1_, f32[8,768]{1,0:T(8,128)} %get-tuple-element.183.refs_2_, f32[1,3072]{1,0:T(1,128)} %get-tuple-element.184.refs_3_, ...), custom_call_target="tpu_custom_call" | custom-call | bytes 200000000 | tf_op jit(solution)/shard_map/pallas_call | solution.py:1200
  684.2 1.1 fusion.12
  685.3 0.8 slice_bitcast_fusion
  686.1 0.8 slice.64
  686.9 0.8 slice.65
  687.7 1.8 fusion.11
  689.5 0.7 fusion
  690.2 0.7 fusion.1
  690.8 0.6 fusion.2
  691.5 0.6 fusion.4
  692.1 0.6 fusion.6
  692.8 6.1 shard_map.301
  (19 shorter events, 0.1 us)
Async XLA Ops:
  319.1 12.6 %collective-permute-start.2 = (bf16[2,4,2,96,768]{4,3,2,1,0:T(8,128)(2,1)}, bf16[2,4,2,96,768]{4,3,2,1,0:T(8,128)(2,1)}, u32[]{:S(2)}, u32[]{:S(2)}) collective-permute-start(bf16[2,4,2,96,768]{4,3,2,1,0:T(8,128)(2,1)} %shard_map.284), channel_id=1, source_target_pairs={{0,8},{1,9},{2,10},{3,11},{4,12},{5,13},{6,14},{7,15},{8,0},{9,1},... | collective-permute-start | bytes 7077896 | tf_op jit(solution)/shard_map/ppermute | solution.py:747
  327.1 11.7 %collective-permute-start.1 = (bf16[1,4,2,384,384]{4,3,2,1,0:T(8,128)(2,1)}, bf16[1,4,2,384,384]{4,3,2,1,0:T(8,128)(2,1)S(1)}, u32[]{:S(2)}, u32[]{:S(2)}) collective-permute-start(bf16[1,4,2,384,384]{4,3,2,1,0:T(8,128)(2,1)} %shard_map.281), channel_id=1, source_target_pairs={{0,8},{1,9},{2,10},{3,11},{4,12},{5,13},{6,14},{7,15},{8,0},{9,1},... | collective-permute-start | bytes 7077896 | tf_op jit(solution)/shard_map/ppermute | solution.py:747
  331.6 17.1 %collective-permute-start = (bf16[1,4,2,96,384]{4,3,2,1,0:T(8,128)(2,1)}, bf16[1,4,2,96,384]{4,3,2,1,0:T(8,128)(2,1)S(1)}, u32[]{:S(2)}, u32[]{:S(2)}) collective-permute-start(bf16[1,4,2,96,384]{4,3,2,1,0:T(8,128)(2,1)} %shard_map.280), channel_id=1, source_target_pairs={{0,8},{1,9},{2,10},{3,11},{4,12},{5,13},{6,14},{7,15},{8,0},{9,1},... | collective-permute-start | bytes 1769480 | tf_op jit(solution)/shard_map/ppermute | solution.py:747
  338.7 1.4 copy-start.6
  348.7 0.8 copy-start.3
  439.4 49.4 %collective-permute-start.6 = (bf16[3,4,2,96,384]{4,3,2,1,0:T(8,128)(2,1)}, bf16[3,4,2,96,384]{4,3,2,1,0:T(8,128)(2,1)}, u32[]{:S(2)}, u32[]{:S(2)}) collective-permute-start(bf16[3,4,2,96,384]{4,3,2,1,0:T(8,128)(2,1)} %shard_map.294), channel_id=1, source_target_pairs={{0,8},{1,9},{2,10},{3,11},{4,12},{5,13},{6,14},{7,15},{8,0},{9,1},... | collective-permute-start | bytes 5308424 | tf_op jit(solution)/shard_map/ppermute | solution.py:747
  476.3 19.5 %collective-permute-start.5 = (bf16[2,4,2,96,768]{4,3,2,1,0:T(8,128)(2,1)}, bf16[2,4,2,96,768]{4,3,2,1,0:T(8,128)(2,1)}, u32[]{:S(2)}, u32[]{:S(2)}) collective-permute-start(bf16[2,4,2,96,768]{4,3,2,1,0:T(8,128)(2,1)} %shard_map.292), channel_id=1, source_target_pairs={{0,8},{1,9},{2,10},{3,11},{4,12},{5,13},{6,14},{7,15},{8,0},{9,1},... | collective-permute-start | bytes 7077896 | tf_op jit(solution)/shard_map/ppermute | solution.py:747
  484.2 18.5 %collective-permute-start.4 = (bf16[1,4,2,384,384]{4,3,2,1,0:T(8,128)(2,1)}, bf16[1,4,2,384,384]{4,3,2,1,0:T(8,128)(2,1)S(1)}, u32[]{:S(2)}, u32[]{:S(2)}) collective-permute-start(bf16[1,4,2,384,384]{4,3,2,1,0:T(8,128)(2,1)} %shard_map.289), channel_id=1, source_target_pairs={{0,8},{1,9},{2,10},{3,11},{4,12},{5,13},{6,14},{7,15},{8,0},{9,1},... | collective-permute-start | bytes 7077896 | tf_op jit(solution)/shard_map/ppermute | solution.py:747
  488.8 23.9 %collective-permute-start.3 = (bf16[1,4,2,96,384]{4,3,2,1,0:T(8,128)(2,1)}, bf16[1,4,2,96,384]{4,3,2,1,0:T(8,128)(2,1)S(1)}, u32[]{:S(2)}, u32[]{:S(2)}) collective-permute-start(bf16[1,4,2,96,384]{4,3,2,1,0:T(8,128)(2,1)} %shard_map.288), channel_id=1, source_target_pairs={{0,8},{1,9},{2,10},{3,11},{4,12},{5,13},{6,14},{7,15},{8,0},{9,1},... | collective-permute-start | bytes 1769480 | tf_op jit(solution)/shard_map/ppermute | solution.py:747
  502.7 1.4 copy-start.5
  512.7 0.8 copy-start.2
  609.2 6.7 copy-start
  609.3 7.5 %copy-start.4 = (bf16[4,3,48,384]{3,2,1,0:T(8,128)(2,1)S(1)}, bf16[4,3,48,384]{3,2,1,0:T(8,128)(2,1)}, u32[]{:S(2)}) copy-start(bf16[4,3,48,384]{3,2,1,0:T(8,128)(2,1)} %get-tuple-element.190) | copy-start | bytes 1327108
  615.9 1.7 copy-start.1
  615.9 11.3 %collective-permute-start.7 = (bf16[3,4,2,96,384]{4,3,2,1,0:T(8,128)(2,1)}, bf16[3,4,2,96,384]{4,3,2,1,0:T(8,128)(2,1)S(1)}, u32[]{:S(2)}, u32[]{:S(2)}) collective-permute-start(bf16[3,4,2,96,384]{4,3,2,1,0:T(8,128)(2,1)} %shard_map.297), channel_id=1, source_target_pairs={{0,8},{1,9},{2,10},{3,11},{4,12},{5,13},{6,14},{7,15},{8,0},{9,1},... | collective-permute-start | bytes 5308424 | tf_op jit(solution)/shard_map/ppermute | solution.py:747
  627.3 1.2 copy-start.7
